TPU v7x, 32 devices: a whole 2x2x4 slice. The times are simulated.
32 devices in a mesh: seq: 8 (over y, x, core), head: 4 (over z).
Axes of the slice: x: 2, y: 2, z: 4, core: 2. Of those that a mesh axis runs over, the one named last changes fastest.
Arguments:
- inputs: bfloat16 [4096, 4096], P('seq', 'head'), may hold values from -6 to 6
- gate: bfloat16 [4096, 4096], P('seq', 'head'), may hold values from -6 to 6
- input_map: bfloat16 [128, 4096], P('head', 'seq'), may hold values from -3 to 3
- output_map: bfloat16 [128, 4096], P('head', 'seq'), may hold values from -3 to 3
- step: float32 [64, 4096], P('head', 'seq'), may hold values from 0.25 to 2
- decay_rate: float32 [64], P('head'), may hold values from 3e-05 to 0.03
- level_mix: float32 [9, 64, 4096], P(None, 'head', 'seq'), may hold values from 0.1 to 1
- skip: float32 [64], P('head'), may hold values from 0.25 to 0.75
- norm_gain: float32 [4096], P('head'), may hold values from 0.5 to 1.5
Outputs:
- normed: bfloat16 [4096, 4096], P('seq', 'head')
All inputs are finite; a program needn't handle non-finite values.
Results may differ from a plain program's by a relative error of at most 0.0075.
Values may be sent and summed in bfloat16 or wider, within the bound.
No kernel may reach another device: no remote copies, remote signals or barrier semaphores. Data moves between devices by JAX's collectives and lax.ppermute only.
A program may use at most 64 MiB of HBM per device.

v0:
```python
import jax
import jax.numpy as jnp
import numpy as np
from jax import lax
from jax.sharding import PartitionSpec as P

HEADS = 64
P_SIZE = 64
N = 128
GROUP = 256
LEVELS = 9


def from_partner(array, axis, distance):
    return lax.ppermute(array, axis, [(i, i ^ 1 << distance) for i in range(lax.axis_size(axis))])


def span_table(groups, group_bits):
    table = np.zeros((groups, max(group_bits, 1), groups), np.float32)
    for later in range(groups):
        if later >> 0 & 1:
            for earlier in range(groups):
                if earlier >> 0 == (later >> 0) - 1:
                    table[later, 0, earlier] = 1.0
    return table


def to_rows(array):
    return jnp.transpose(array, (1, 2, 0))[..., None]


def project_states(out_blocks, states):
    groups, levels, heads_here, width, size = states.shape
    flat = jnp.transpose(states, (0, 3, 1, 2, 4)).reshape(groups, width, levels * heads_here * size)
    high = flat.astype(jnp.bfloat16)
    low = (flat - high.astype(jnp.float32)).astype(jnp.bfloat16)
    paired = jnp.concatenate([high, low], axis=2)
    proj = jnp.einsum("nct,cnk->ctk", out_blocks, paired, preferred_element_type=jnp.float32)
    half = levels * heads_here * size
    proj = proj[:, :, :half] + proj[:, :, half:]
    return proj.reshape(groups, out_blocks.shape[2], levels, heads_here, size)


def on_device(inputs, gate, input_map, output_map, step, decay_rate, level_mix, skip, norm_gain):
    highest = lax.Precision.HIGHEST
    tokens = inputs.shape[0]
    heads_here = inputs.shape[1] // P_SIZE
    groups = tokens // GROUP
    group_bits = groups.bit_length() - 1
    in_map, out_map = (
        lax.all_gather(input_map, "head", axis=0, tiled=True),
        lax.all_gather(output_map, "head", axis=0, tiled=True),
    )
    log_decay = -step * decay_rate[:, None]
    step_blocks = step.reshape(heads_here, groups, GROUP)
    cum = jnp.cumsum(log_decay.reshape(heads_here, groups, GROUP), axis=2)
    in_blocks = in_map.reshape(N, groups, GROUP)
    out_blocks = out_map.reshape(N, groups, GROUP)
    values = inputs.reshape(groups, GROUP, heads_here, P_SIZE)
    scores = jnp.einsum("nct,ncs->cts", out_blocks, in_blocks, preferred_element_type=jnp.float32)
    rows = jnp.arange(GROUP, dtype=jnp.int32)
    causal = (rows[:, None] >= rows[None, :])[None, None]
    spread = cum[:, :, :, None] - cum[:, :, None, :]
    within = jnp.where(causal, jnp.exp(jnp.where(causal, spread, 0.0)), 0.0)
    weights = (scores[None] * within * step_blocks[:, :, None, :]).astype(jnp.bfloat16)
    intra = jnp.einsum("hcts,cshp->cthp", weights, values, preferred_element_type=jnp.float32)
    to_end = jnp.exp(cum[:, :, -1:] - cum) * step_blocks
    loads = (in_blocks[None] * to_end[:, None]).astype(jnp.bfloat16)
    group_states = jnp.einsum("hncs,cshp->chnp", loads, values, preferred_element_type=jnp.float32)
    totals = cum[:, :, -1]
    after = jnp.cumsum(totals, axis=1)
    before = after - totals
    mixed = level_mix.reshape(LEVELS, heads_here, groups, GROUP)
    local_spans = None
    member = jnp.asarray(span_table(groups, group_bits))[None] > 0.5
    gap = before[:, :, None, None] - after[:, None, None, :]
    mixing = jnp.where(member, jnp.exp(jnp.where(member, gap, 0.0)), 0.0)
    local_spans = jnp.einsum("hjbk,khnp->jbhnp", mixing, group_states, precision=highest)
    shard_state = jnp.einsum(
        "hk,khnp->hnp", jnp.exp(after[:, -1:] - after), group_states, precision=highest
    )
    shard_total = after[:, -1]
    rank = lax.axis_index("seq")
    seq_bits = lax.axis_size("seq").bit_length() - 1
    acc_state, acc_total = (shard_state, shard_total)
    got_states = []
    got_totals = []
    for level in range(seq_bits):
        their_state, their_total = from_partner((acc_state, acc_total), "seq", level)
        upper = jnp.right_shift(rank, level) % 2 == 1
        got_states.append(jnp.where(upper, their_state, 0.0))
        got_totals.append(jnp.where(upper, their_total, 0.0))
        acc_state = jnp.where(
            upper,
            jnp.exp(acc_total)[:, None, None] * their_state + acc_state,
            jnp.exp(their_total)[:, None, None] * acc_state + their_state,
        )
        acc_total = acc_total + their_total
    running = jnp.zeros((heads_here,), jnp.float32)
    far_list = []
    for level in range(seq_bits):
        far_list.append(jnp.exp(running)[:, None, None] * got_states[level])
        running = running + got_totals[level]
    far_spans = jnp.stack(far_list, axis=0)
    far_wide = jnp.broadcast_to(far_spans[None], (groups, seq_bits, heads_here, N, P_SIZE))
    all_states = jnp.concatenate([local_spans, far_wide], axis=1)
    proj = project_states(out_blocks, all_states)
    level = 0
    near = to_rows(mixed[1 + level]) * proj[:, :, level]
    far = jnp.zeros((groups, GROUP, heads_here, P_SIZE), jnp.float32)
    for level in range(seq_bits):
        far = far + to_rows(mixed[1 + group_bits + level]) * proj[:, :, group_bits + level]
    total = to_rows(mixed[0]) * intra
    total = total + to_rows(jnp.exp(cum)) * near
    total = total + to_rows(jnp.exp(cum + before[:, :, None])) * far
    total = total + skip[None, None, :, None] * values.astype(jnp.float32)
    gated = total.reshape(tokens, heads_here * P_SIZE) * jax.nn.silu(gate.astype(jnp.float32))
    squares = jnp.sum(gated * gated, axis=1)
    summed = lax.psum(squares, "head")
    scale = lax.rsqrt(summed / (HEADS * P_SIZE) + 1e-05)
    return (gated * scale[:, None] * norm_gain[None, :]).astype(jnp.bfloat16)


def solution(mesh):
    return jax.shard_map(
        on_device,
        mesh=mesh,
        in_specs=(
            P("seq", "head"),
            P("seq", "head"),
            P("head", "seq"),
            P("head", "seq"),
            P("head", "seq"),
            P("head"),
            P(None, "head", "seq"),
            P("head"),
            P("head"),
        ),
        out_specs=P("seq", "head"),
        check_vma=False,
    )
```

profile of v0, /device:TPU:0, one launch (start us, length us, event | category | flops | bytes accessed | tf_op | source)
XLA Modules:
  0.0 109.4 jit_solution(8821593199851248986)
XLA Ops:
  0.0 0.8 negate_multiply_fusion
  0.9 1.2 %reduce-window.6 = f32[16,2,2,128]{3,0,1,2:T(8,128)S(1)} reduce-window(f32[16,2,2,128]{3,0,1,2:T(8,128)S(1)} %copy.125, f32[]{:T(128)} %constant.39.clone.1), window={size=1x1x1x128 pad=0_0x0_0x0_0x127_0}, to_apply=%region_0.0 | reduce-window | flops 1040384 | bytes 65540 | tf_op jit(solution)/shard_map/reduce-window
  3.0 3.0 %reshape.166 = bf16[2,256,16,64]{3,2,1,0:T(8,128)(2,1)S(1)} reshape(bf16[512,1024]{1,0:T(8,128)(2,1)} %param.10) | data formatting | bytes 2097152 | tf_op jit(solution)/shard_map/reshape | solution.py:59
  6.0 1.7 %copy.131 = bf16[2,256,16,64]{1,3,2,0:T(8,128)(2,1)S(1)} copy(bf16[2,256,16,64]{3,2,1,0:T(8,128)(2,1)S(1)} %reshape.166) | data formatting | bytes 2097152 | tf_op jit(solution)/shard_map/reshape | solution.py:59
  7.7 15.1 %all_gather.7 = bf16[128,512]{1,0:T(8,128)(2,1)S(1)} all-gather(bf16[32,512]{1,0:T(8,128)(2,1)S(1)} %copy-done.7), channel_id=1, replica_groups=mesh['seq'=8,'head'=4] {'head'}, dimensions={0}, use_global_device_ids=true | all-gather | bytes 163840 | tf_op jit(solution)/shard_map/all_gather | solution.py:51
  23.0 0.7 exponential_bitcast_fusion.1
  23.7 1.9 %multiply_reduce_fusion.1 = (f32[16,128,64]{1,2,0:T(8,128)S(1)}, f32[2,16,128,64]{2,3,1,0:T(8,128)}) fusion(f32[16,2]{0,1:T(2,128)S(1)} %get-tuple-element.22, bf16[2,256,16,64]{1,3,2,0:T(8,128)(2,1)S(1)} %copy.131, f32[16,2,256]{2,0,1:T(8,128)S(1)} %get-tuple-element.20, f32[128,2,256]{2,0,1:T(8,128)S(1)} %copy.133), kind=kOutput, calls=%fused_computation.47 | convolution fusion | flops 136708096 | bytes 2916480 | tf_op jit(solution)/shard_map/hncs,cshp->chnp/dot_general | solution.py:69
  25.6 0.5 collective-permute-start.1
  26.1 1.4 %collective-permute-done.1 = f32[16]{0:T(128)S(1)} collective-permute-done((f32[16]{0:T(128)S(1)}, f32[16]{0:T(128)S(1)}, u32[]{:S(2)}, u32[]{:S(2)}) %collective-permute-start.1) | collective-permute-done | bytes 96 | tf_op jit(solution)/shard_map/ppermute | solution.py:15
  27.5 1.5 %collective-permute-start.3 = (f32[16]{0:T(128)S(1)}, f32[16]{0:T(128)S(1)}, u32[]{:S(2)}, u32[]{:S(2)}) collective-permute-start(f32[16]{0:T(128)S(1)} %get-tuple-element.8), channel_id=1, source_target_pairs={{0,8},{4,12},{8,0},{12,4},{16,24},{20,28},{24,16},{28,20},{1,9},{5... | collective-permute-start | bytes 200 | tf_op jit(solution)/shard_map/ppermute | solution.py:15
  29.0 2.0 %collective-permute-done.3 = f32[16]{0:T(128)S(1)} collective-permute-done((f32[16]{0:T(128)S(1)}, f32[16]{0:T(128)S(1)}, u32[]{:S(2)}, u32[]{:S(2)}) %collective-permute-start.3) | collective-permute-done | bytes 96 | tf_op jit(solution)/shard_map/ppermute | solution.py:15
  31.2 1.6 %collective-permute-start.2 = (f32[16,128,64]{1,2,0:T(8,128)S(1)}, f32[16,128,64]{1,2,0:T(8,128)}, u32[]{:S(2)}, u32[]{:S(2)}) collective-permute-start(f32[16,128,64]{1,2,0:T(8,128)S(1)} %get-tuple-element.10), channel_id=1, source_target_pairs={{0,8},{4,12},{8,0},{12,4},{16,24},{20,28},{24,16},{28,20},{1,9},{5... | collective-permute-start | bytes 1572872 | tf_op jit(solution)/shard_map/ppermute | solution.py:15
  32.8 0.8 fusion.49
  33.8 4.1 %convolution_bitcast_fusion.1 = f32[2,1,16,128,64]{3,0,4,2,1:T(2,128)S(1)} fusion(f32[2,16,128,64]{2,3,1,0:T(8,128)S(1)} %copy-done.2, pred[2,2]{1,0:T(4,128)(4,1)S(1)} %copy-done.15, f32[16,2]{1,0:T(8,128)S(1)} %copy.137, f32[16,2]{1,0:T(8,128)S(1)} %copy.136), kind=kOutput, calls=%fused_computation.46 | convolution fusion | flops 6291648 | bytes 2097412 | tf_op jit(solution)/shard_map/hjbk,khnp->jbhnp/dot_general | solution.py:78
  37.9 0.6 copy_bitcast_fusion.2
  38.5 5.7 %collective-permute-done.2 = f32[16,128,64]{1,2,0:T(8,128)} collective-permute-done((f32[16,128,64]{1,2,0:T(8,128)S(1)}, f32[16,128,64]{1,2,0:T(8,128)}, u32[]{:S(2)}, u32[]{:S(2)}) %collective-permute-start.2) | collective-permute-done | bytes 524320 | tf_op jit(solution)/shard_map/ppermute | solution.py:15
  44.2 2.0 %multiply_bitcast_fusion.1 = (f32[1,16,128,64]{2,3,1,0:T(8,128)S(1)}, f32[16,128,64]{1,2,0:T(8,128)}) fusion(f32[16,128,64]{1,2,0:T(8,128)} %collective-permute-done.2, f32[16]{0:T(128)S(1)} %get-tuple-element.24, pred[]{:T(512)S(6)} %eq.14, f32[16,128,64]{1,2,0:T(8,128)S(1)} %get-tuple-element.10, f32[16]{0:T(128)S(1)} %get-tuple-element.26, ...), kind=kLoop, calls=%fused_computation.51 | loop fusion | flops 917504 | bytes 2097345 | tf_op jit(solution)/shard_map/stack | solution.py:104
  46.2 1.5 %collective-permute-start.4 = (f32[16,128,64]{1,2,0:T(8,128)}, f32[16,128,64]{1,2,0:T(8,128)}, u32[]{:S(2)}, u32[]{:S(2)}) collective-permute-start(f32[16,128,64]{1,2,0:T(8,128)} %get-tuple-element.12), channel_id=1, source_target_pairs={{0,16},{4,20},{8,24},{12,28},{16,0},{20,4},{24,8},{28,12},{1,17},{... | collective-permute-start | bytes 1572872 | tf_op jit(solution)/shard_map/ppermute | solution.py:15
  47.8 0.6 iota_compare_fusion
  48.4 0.6 copy.186
  49.1 13.6 %all_gather.6 = bf16[128,512]{1,0:T(8,128)(2,1)S(1)} all-gather(bf16[32,512]{1,0:T(8,128)(2,1)S(1)} %copy-done.8), channel_id=1, replica_groups=mesh['seq'=8,'head'=4] {'head'}, dimensions={0}, use_global_device_ids=true | all-gather | bytes 163840 | tf_op jit(solution)/shard_map/all_gather | solution.py:52
  62.9 1.5 %copy.151 = bf16[512,1024]{0,1:T(8,128)(2,1)S(1)} copy(bf16[512,1024]{1,0:T(8,128)(2,1)} %param.11) | data formatting | bytes 2097152 | tf_op args[1]
  65.4 0.4 pad_maximum_fusion
  65.8 0.5 fusion.4
  66.4 8.1 %convolution_bitcast_fusion = f32[2,256,8192]{1,2,0:T(8,128)} fusion(bf16[128,2,256]{0,2,1:T(8,128)(2,1)S(1)} %bitcast.135, bf16[2,128,4096]{1,2,0:T(8,128)(2,1)S(1)} %get-tuple-element.5, bf16[2,128,4096]{1,2,0:T(8,128)(2,1)S(1)} %get-tuple-element.6), kind=kOutput, calls=%fused_computation | convolution fusion | flops 1082130432 | bytes 21102592 | tf_op jit(solution)/shard_map/nct,cnk->ctk/dot_general | solution.py:38
  74.5 10.2 %slice_add_fusion = f32[2,256,4096]{1,2,0:T(8,128)} fusion(f32[2,256,8192]{1,2,0:T(8,128)} %convolution_bitcast_fusion), kind=kLoop, calls=%fused_computation.1 | loop fusion | flops 2097152 | bytes 25165824 | tf_op jit(solution)/shard_map/add | solution.py:40
  84.8 6.1 %fusion.20 = f32[2,256,16,64]{1,3,2,0:T(8,128)S(1)} fusion(f32[2,256,4,16,64]{1,4,3,2,0:T(8,128)} %bitcast.132, bf16[2,256,16,64]{1,3,2,0:T(8,128)(2,1)S(1)} %copy-done.1, f32[16,2,256]{2,0,1:T(8,128)S(1)} %bitcast.140, f32[16,2,256]{2,0,1:T(8,128)S(1)} %copy-done.5, f32[2,256,256]{2,1,0:T(8,128)S(1)} %fusion.51, pred[256,256]{1,0:T(8,128)(4,1)S(1)} %copy-done.6, ...), kind=kOutput, calls=%fused_computation.30 | convolution fusion | flops 288358400 | bytes 13500928 | tf_op jit(solution)/shard_map/hcts,cshp->cthp/dot_general | solution.py:66
  90.9 1.6 %copy.150 = f32[2,256,16,64]{1,0,3,2:T(2,128)S(1)} copy(f32[2,256,16,64]{1,3,2,0:T(8,128)S(1)} %fusion.20) | data formatting | bytes 4194304 | tf_op jit(solution)/shard_map/add | solution.py:116
  92.7 0.7 multiply_reduce_fusion
  93.4 12.1 %psum.7 = f32[512]{0:T(512)S(1)} all-reduce(f32[512]{0:T(512)S(1)} %multiply_reduce_fusion), channel_id=1, replica_groups=mesh['seq'=8,'head'=4] {'head'}, use_global_device_ids=true, to_apply=%region_4.5 | all-reduce | flops 512 | bytes 4096 | tf_op jit(solution)/shard_map/psum | solution.py:119
  105.4 1.7 %multiply_convert_fusion.4 = bf16[512,1024]{0,1:T(8,128)(2,1)} fusion(f32[1024]{0:T(1024)S(1)} %copy-done.14, f32[512]{0:T(512)S(1)} %add_rsqrt_fusion, f32[512,1024]{0,1:T(8,128)S(1)} %bitcast.131, bf16[512,1024]{0,1:T(8,128)(2,1)S(1)} %copy.151), kind=kLoop, calls=%fused_computation.41 | loop fusion | flops 4718592 | bytes 4200448 | tf_op jit(solution)/shard_map/convert_element_type | solution.py:121
  107.1 2.3 %copy.152 = bf16[512,1024]{1,0:T(8,128)(2,1)} copy(bf16[512,1024]{0,1:T(8,128)(2,1)} %multiply_convert_fusion.4) | data formatting | bytes 2097152 | tf_op jit(solution)/shard_map/convert_element_type | solution.py:121
  (73 shorter events, 3.0 us)
Async XLA Ops:
  2.3 0.6 copy-start.4
  5.9 1.7 %copy-start.7 = (bf16[32,512]{1,0:T(8,128)(2,1)S(1)}, bf16[32,512]{1,0:T(8,128)(2,1)}, u32[]{:S(2)}) copy-start(bf16[32,512]{1,0:T(8,128)(2,1)} %param.12) | copy-start | bytes 98308
  5.9 17.0 %copy-start.3 = (f32[16,512]{1,0:T(8,128)S(1)}, f32[16,512]{1,0:T(8,128)}, u32[]{:S(2)}) copy-start(f32[16,512]{1,0:T(8,128)} %param.14) | copy-start | bytes 98308
  7.7 17.9 %copy-start = (bf16[2,256,16,64]{1,3,2,0:T(8,128)(2,1)}, bf16[2,256,16,64]{1,3,2,0:T(8,128)(2,1)S(1)}, u32[]{:S(2)}) copy-start(bf16[2,256,16,64]{1,3,2,0:T(8,128)(2,1)S(1)} %copy.131) | copy-start | bytes 3145732
  25.5 8.3 %copy-start.15 = (pred[2,2]{1,0:T(4,128)(4,1)S(1)}, pred[2,2]{1,0:T(4,128)(4,1)}, u32[]{:S(2)}) copy-start(pred[2,2]{1,0:T(4,128)(4,1)} %constant.51) | copy-start | bytes 16
  25.5 8.3 %copy-start.2 = (f32[2,16,128,64]{2,3,1,0:T(8,128)S(1)}, f32[2,16,128,64]{2,3,1,0:T(8,128)}, u32[]{:S(2)}) copy-start(f32[2,16,128,64]{2,3,1,0:T(8,128)} %get-tuple-element.29) | copy-start | bytes 3145732
  25.5 5.5 %collective-permute-start = (f32[16,128,64]{1,2,0:T(8,128)S(1)}, f32[16,128,64]{1,2,0:T(8,128)S(1)}, u32[]{:S(2)}, u32[]{:S(2)}) collective-permute-start(f32[16,128,64]{1,2,0:T(8,128)S(1)} %get-tuple-element.28), channel_id=1, source_target_pairs={{0,4},{4,0},{8,12},{12,8},{16,20},{20,16},{24,28},{28,24},{1,5},{5... | collective-permute-start | bytes 1572872 | tf_op jit(solution)/shard_map/ppermute | solution.py:15
  25.6 1.9 %collective-permute-start.1 = (f32[16]{0:T(128)S(1)}, f32[16]{0:T(128)S(1)}, u32[]{:S(2)}, u32[]{:S(2)}) collective-permute-start(f32[16]{0:T(128)S(1)} %slice_bitcast_fusion.4), channel_id=1, source_target_pairs={{0,4},{4,0},{8,12},{12,8},{16,20},{20,16},{24,28},{28,24},{1,5},{5... | collective-permute-start | bytes 200 | tf_op jit(solution)/shard_map/ppermute | solution.py:15
  27.5 3.5 %collective-permute-start.3 = (f32[16]{0:T(128)S(1)}, f32[16]{0:T(128)S(1)}, u32[]{:S(2)}, u32[]{:S(2)}) collective-permute-start(f32[16]{0:T(128)S(1)} %get-tuple-element.8), channel_id=1, source_target_pairs={{0,8},{4,12},{8,0},{12,4},{16,24},{20,28},{24,16},{28,20},{1,9},{5... | collective-permute-start | bytes 200 | tf_op jit(solution)/shard_map/ppermute | solution.py:15
  31.2 13.0 %collective-permute-start.2 = (f32[16,128,64]{1,2,0:T(8,128)S(1)}, f32[16,128,64]{1,2,0:T(8,128)}, u32[]{:S(2)}, u32[]{:S(2)}) collective-permute-start(f32[16,128,64]{1,2,0:T(8,128)S(1)} %get-tuple-element.10), channel_id=1, source_target_pairs={{0,8},{4,12},{8,0},{12,4},{16,24},{20,28},{24,16},{28,20},{1,9},{5... | collective-permute-start | bytes 1572872 | tf_op jit(solution)/shard_map/ppermute | solution.py:15
  44.2 4.9 %copy-start.8 = (bf16[32,512]{1,0:T(8,128)(2,1)S(1)}, bf16[32,512]{1,0:T(8,128)(2,1)}, u32[]{:S(2)}) copy-start(bf16[32,512]{1,0:T(8,128)(2,1)} %param.13) | copy-start | bytes 98308
  46.2 18.5 %collective-permute-start.4 = (f32[16,128,64]{1,2,0:T(8,128)}, f32[16,128,64]{1,2,0:T(8,128)}, u32[]{:S(2)}, u32[]{:S(2)}) collective-permute-start(f32[16,128,64]{1,2,0:T(8,128)} %get-tuple-element.12), channel_id=1, source_target_pairs={{0,16},{4,20},{8,24},{12,28},{16,0},{20,4},{24,8},{28,12},{1,17},{... | collective-permute-start | bytes 1572872 | tf_op jit(solution)/shard_map/ppermute | solution.py:15
  74.5 10.2 %copy-start.1 = (bf16[2,256,16,64]{1,3,2,0:T(8,128)(2,1)S(1)}, bf16[2,256,16,64]{1,3,2,0:T(8,128)(2,1)}, u32[]{:S(2)}) copy-start(bf16[2,256,16,64]{1,3,2,0:T(8,128)(2,1)} %copy-done) | copy-start | bytes 3145732
  74.5 10.2 %copy-start.5 = (f32[16,2,256]{2,0,1:T(8,128)S(1)}, f32[16,2,256]{2,0,1:T(8,128)}, u32[]{:S(2)}) copy-start(f32[16,2,256]{2,0,1:T(8,128)} %copy-done.4) | copy-start | bytes 98308
  74.5 10.2 %copy-start.6 = (pred[256,256]{1,0:T(8,128)(4,1)S(1)}, pred[256,256]{1,0:T(8,128)(4,1)}, u32[]{:S(2)}) copy-start(pred[256,256]{1,0:T(8,128)(4,1)} %iota_compare_fusion) | copy-start | bytes 196612
  74.5 10.2 %copy-start.9 = (f32[2,2,8,256]{3,2,0,1:T(8,128)S(1)}, f32[2,2,8,256]{3,2,0,1:T(8,128)}, u32[]{:S(2)}) copy-start(f32[2,2,8,256]{3,2,0,1:T(8,128)} %copy.186) | copy-start | bytes 98308
  74.5 10.2 %copy-start.10 = (f32[2,256,16]{1,2,0:T(8,128)S(1)}, f32[2,256,16]{1,2,0:T(8,128)}, u32[]{:S(2)}) copy-start(f32[2,256,16]{1,2,0:T(8,128)} %get-tuple-element.18) | copy-start | bytes 98308
  74.5 10.2 %copy-start.11 = (f32[2,256,16]{1,2,0:T(8,128)S(1)}, f32[2,256,16]{1,2,0:T(8,128)}, u32[]{:S(2)}) copy-start(f32[2,256,16]{1,2,0:T(8,128)} %get-tuple-element.19) | copy-start | bytes 98308
  74.5 10.2 %copy-start.12 = (f32[2,256,16]{1,2,0:T(8,128)S(1)}, f32[2,256,16]{1,2,0:T(8,128)}, u32[]{:S(2)}) copy-start(f32[2,256,16]{1,2,0:T(8,128)} %get-tuple-element.30) | copy-start | bytes 98308
  74.5 10.2 %copy-start.13 = (f32[2,256,16]{1,2,0:T(8,128)S(1)}, f32[2,256,16]{1,2,0:T(8,128)}, u32[]{:S(2)}) copy-start(f32[2,256,16]{1,2,0:T(8,128)} %get-tuple-element.31) | copy-start | bytes 98308
  74.5 10.2 %copy-start.16 = (f32[16]{0:T(128)S(1)}, f32[16]{0:T(128)}, u32[]{:S(2)}) copy-start(f32[16]{0:T(128)} %param.17) | copy-start | bytes 196
  92.7 12.8 %copy-start.14 = (f32[1024]{0:T(1024)S(1)}, f32[1024]{0:T(1024)}, u32[]{:S(2)}) copy-start(f32[1024]{0:T(1024)} %param.18) | copy-start | bytes 12292
where the time goes:
time: 110 us; the launch traced here: 109 us
  blocking collectives  40.7 us (37%)
  matrix products  20.3 us (18%)
  other arithmetic  19.6 us (18%)
  local copies, waits for them, and re-layouts  14.2 us (13%)
  waiting for transfers between devices  9.11 us (8%)
  starting transfers between devices  5.07 us (5%)
    all_gather x1, blocking collectives, on_device(): lax.all_gather(input_map, 'head', axis=0, tiled=True)  15.1 us
    all_gather x1, blocking collectives, on_device(): lax.all_gather(output_map, 'head', axis=0, tiled=True)  13.6 us
    psum x1, blocking collectives, on_device(): summed = lax.psum(squares, 'head')  12.1 us
    add x1, other arithmetic, project_states(): proj = proj[:, :, :half] + proj[:, :, half:]  10.2 us
    ppermute x5, waiting for transfers between devices, from_partner(): lax.ppermute(array, axis, [(i, i ^ 1 << distance) for i in range(lax.axis...  9.11 us
    dot_general x1, matrix products, project_states(): jnp.einsum('nct,cnk->ctk', out_blocks, paired, preferred_element_type=jnp...  8.08 us
    dot_general x1, matrix products, on_device(): jnp.einsum('hcts,cshp->cthp', weights, values, preferred_element_type=jnp...  6.11 us
    ppermute x5, starting transfers between devices, from_partner(): lax.ppermute(array, axis, [(i, i ^ 1 << distance) for i in range(lax.axis...  5.07 us
  transfers between devices with their start and end apart: 5, of which 3 were waited for; matrix products, arithmetic and copies ran while one was open for 8% of the time, Pallas kernels for 0%

commit v1 on v0

v1 whole, which is shorter than its diff:
```python
import functools

import jax
import jax.numpy as jnp
from jax import lax
from jax.experimental import pallas as pl
from jax.experimental.pallas import tpu as pltpu
from jax.sharding import PartitionSpec as P

P_SIZE = 64
GROUP = 256
DECAY_ROWS = 16
BLOCK = 256
VMEM_LIMIT = 40 * 1024 * 1024

f32, bf16 = jnp.float32, jnp.bfloat16
HIGHEST = lax.Precision.HIGHEST
TRANSPOSED = (((0,), (0,)), ((), ()))


def expander(heads, width, copies):
    row = lax.broadcasted_iota(jnp.int32, (copies * heads, width), 0)
    col = lax.broadcasted_iota(jnp.int32, (copies * heads, width), 1)
    return jnp.where(lax.rem(row, heads) == lax.div(col, P_SIZE), 1.0, 0.0)


def two_parts(factor):
    high = factor.astype(bf16).astype(f32)
    return jnp.concatenate([high, factor - high], axis=0).astype(bf16)


def transposed_dot(left, right):
    return lax.dot_general(left, right, TRANSPOSED, preferred_element_type=f32)


def head_row(heads, width, column):
    return jnp.sum(expander(heads, width, 1) * column, axis=0, keepdims=True)


def group_slice(group):
    return slice(group * GROUP, (group + 1) * GROUP)


def blocks_of(width):
    return [slice(at, at + BLOCK) for at in range(0, width, BLOCK)]


def local_spans(groups):
    spans = []
    for later in range(groups):
        for bit in range(groups.bit_length() - 1):
            if later >> bit & 1:
                start = later >> bit + 1 << bit + 1
                spans.append((later, bit, start, start + 2**bit))
    return spans


def prepare_kernel(inputs_ref, step_ref, rate_ref, scaled_ref, cum_ref):
    heads, tokens = step_ref.shape
    width = inputs_ref.shape[1]
    step = step_ref[...]
    log_decay = -step * rate_ref[...]
    row = lax.broadcasted_iota(jnp.int32, (GROUP, GROUP), 0)
    col = lax.broadcasted_iota(jnp.int32, (GROUP, GROUP), 1)
    until = jnp.where(row <= col, 1.0, 0.0)
    expand = expander(heads, width, 2).astype(bf16)
    for group in range(tokens // GROUP):
        at = group_slice(group)
        cum = jnp.dot(log_decay[:, at], until, precision=HIGHEST, preferred_element_type=f32)
        cum_ref[:, at] = cum
        factor = two_parts(jnp.exp(-cum) * step[:, at])
        for cols in blocks_of(width):
            scale = transposed_dot(factor, expand[:, cols])
            scaled_ref[at, cols] = (inputs_ref[at, cols].astype(f32) * scale).astype(bf16)


def states_kernel(parts, *refs):
    in_refs, (scaled_ref, cum_ref), out_refs = refs[:parts], refs[parts : parts + 2], refs[parts + 2 :]
    shard_ref = out_refs[0]
    heads, tokens = cum_ref.shape
    width = scaled_ref.shape[1]
    in_map = jnp.concatenate([ref[...] for ref in in_refs], axis=0)
    size = in_map.shape[0]
    cum = cum_ref[...]
    states, decays = [], []
    for group in range(tokens // GROUP):
        at = group_slice(group)
        decay = head_row(heads, width, jnp.exp(cum[:, at.stop - 1 : at.stop]))
        raw = jnp.dot(in_map[:, at], scaled_ref[at, :], preferred_element_type=f32)
        states.append(raw * decay)
        decays.append(decay)
    total, decay = states[0], decays[0]
    for group in range(1, len(states)):
        total = total * decays[group] + states[group]
        decay = decay * decays[group]
    shard_ref[:size, :] = total.astype(bf16)
    shard_ref[size:, :] = jnp.broadcast_to(decay, (DECAY_ROWS, width)).astype(bf16)
    for index, (later, _, start, stop) in enumerate(local_spans(len(states))):
        span = states[start]
        for group in range(start + 1, later):
            span = span * decays[group]
            if group < stop:
                span = span + states[group]
        out_refs[1][index * size : (index + 1) * size, :] = span.astype(bf16)


def near_kernel(parts, spans, *refs):
    in_refs, map_refs = refs[:parts], refs[parts : 2 * parts]
    scaled_ref, cum_ref, inputs_ref, gate_ref, mix_ref, skip_ref = refs[2 * parts : 2 * parts + 6]
    span_refs = refs[2 * parts + 6 : -2]
    near_ref, swish_ref = refs[-2:]
    heads, tokens = cum_ref.shape
    width = scaled_ref.shape[1]
    in_map = jnp.concatenate([ref[...] for ref in in_refs], axis=0)
    out_map = jnp.concatenate([ref[...] for ref in map_refs], axis=0)
    size = in_map.shape[0]
    expand = expander(heads, width, 2).astype(bf16)
    skip = head_row(heads, width, skip_ref[...])
    row = lax.broadcasted_iota(jnp.int32, (GROUP, GROUP), 0)
    col = lax.broadcasted_iota(jnp.int32, (GROUP, GROUP), 1)
    for group in range(tokens // GROUP):
        at = group_slice(group)
        scores = transposed_dot(out_map[:, at], in_map[:, at])
        scores = jnp.where(row >= col, scores, 0.0).astype(bf16)
        decay = jnp.exp(cum_ref[:, at])
        mixes = [two_parts(mix_ref[0, :, at] * decay)]
        states = []
        for index, (later, bit, _, _) in enumerate(spans):
            if later == group:
                mixes.append(two_parts(mix_ref[1 + bit, :, at] * decay))
                states.append(slice(index * size, (index + 1) * size))
        for cols in blocks_of(width):
            own = jnp.dot(scores, scaled_ref[at, cols], preferred_element_type=f32)
            total = transposed_dot(mixes[0], expand[:, cols]) * own
            for mix, rows in zip(mixes[1:], states):
                reach = transposed_dot(out_map[:, at], span_refs[0][rows, cols])
                total = total + transposed_dot(mix, expand[:, cols]) * reach
            near_ref[at, cols] = total + skip[:, cols] * inputs_ref[at, cols].astype(f32)
            gate = gate_ref[at, cols].astype(f32)
            swish_ref[at, cols] = gate / (1.0 + jnp.exp(-gate))


def far_body(out_map, cum_ref, mix_ref, near_ref, swish_ref, state_of, levels, gated_ref, squares_ref):
    heads, tokens = cum_ref.shape
    width = near_ref.shape[1]
    groups = tokens // GROUP
    first = groups.bit_length()
    expand = expander(heads, width, 2).astype(bf16)
    mixes = []
    before = jnp.zeros((heads, 1), f32)
    for group in range(groups):
        at = group_slice(group)
        cum = cum_ref[:, at]
        decay = jnp.exp(cum + before)
        before = before + cum[:, GROUP - 1 : GROUP]
        mixes.append([two_parts(mix_ref[first + level, :, at] * decay) for level in range(levels)])
    squares = [jnp.zeros((GROUP, 128), f32) for _ in range(groups)]
    for cols in blocks_of(width):
        states = [state_of(level, cols).astype(bf16) for level in range(levels)]
        for group in range(groups):
            at = group_slice(group)
            total = near_ref[at, cols]
            for level in range(levels):
                reach = transposed_dot(out_map[:, at], states[level])
                total = total + transposed_dot(mixes[group][level], expand[:, cols]) * reach
            gated = total * swish_ref[at, cols]
            gated_ref[at, cols] = gated
            gated = gated * gated
            for part in range(0, BLOCK, 128):
                squares[group] = squares[group] + gated[:, part : part + 128]
    ones = jnp.ones((8, 128), f32)
    for group in range(groups):
        sums = lax.dot_general(
            ones, squares[group], (((1,), (1,)), ((), ())), precision=HIGHEST, preferred_element_type=f32
        )
        squares_ref[:, group_slice(group)] = sums[:1]


def far_kernel(parts, levels, *refs):
    out_map = jnp.concatenate([ref[...] for ref in refs[:parts]], axis=0)
    cum_ref, mix_ref, near_ref, swish_ref = refs[parts : parts + 4]
    state_refs = refs[parts + 4 : -2]
    gated_ref, squares_ref = refs[-2:]

    def state_of(level, cols):
        return state_refs[level][:, cols]

    far_body(out_map, cum_ref, mix_ref, near_ref, swish_ref, state_of, levels, gated_ref, squares_ref)


def far_kernel_of_pairs(parts, *refs):
    out_map = jnp.concatenate([ref[...] for ref in refs[:parts]], axis=0)
    cum_ref, mix_ref, near_ref, swish_ref, core_ref = refs[parts : parts + 5]
    own_refs, other_refs = refs[parts + 5 : parts + 8], refs[parts + 8 : parts + 11]
    gated_ref, squares_ref = refs[-2:]
    size = out_map.shape[0]
    rank = lax.axis_index("seq")
    core = lax.rem(rank, 2)
    along_x = lax.rem(lax.div(rank, 2), 2)
    half = own_refs[0].shape[1]

    def pair_of(index, cols):
        side = cols.start // half
        at = slice(cols.start - side * half, cols.stop - side * half)
        whole = jnp.where(core == side, own_refs[index][:, at], other_refs[index][:, at]).astype(f32)
        return whole[:size], whole[size : size + 1]

    def state_of(level, cols):
        core_state = jnp.where(core == 1, core_ref[:size, cols].astype(f32), 0.0)
        if level == 0:
            return core_state
        running = jnp.where(core == 1, core_ref[size : size + 1, cols].astype(f32), 1.0)
        x_state, x_decay = pair_of(0, cols)
        if level == 1:
            return x_state * running
        running = running * jnp.where(along_x == 1, x_decay, 1.0)
        y_state, y_decay = pair_of(1, cols)
        d_state, d_decay = pair_of(2, cols)
        newer = jnp.where(along_x == 1, y_state, d_state)
        newer_decay = jnp.where(along_x == 1, y_decay, d_decay)
        older = jnp.where(along_x == 1, d_state, y_state)
        return (older * newer_decay + newer) * running

    far_body(out_map, cum_ref, mix_ref, near_ref, swish_ref, state_of, 3, gated_ref, squares_ref)


def norm_kernel(parts, columns, *refs):
    sum_refs = refs[:parts]
    gated_ref, gain_ref, out_ref = refs[parts:]
    total = sum_refs[0][...]
    for ref in sum_refs[1:]:
        total = total + ref[...]
    scale = lax.rsqrt(total / columns + 1e-05)
    scale = jnp.transpose(jnp.broadcast_to(scale, (8, scale.shape[1])))[:, :1]
    out_ref[...] = (gated_ref[...] * scale * gain_ref[...]).astype(bf16)


def call(kernel, out_shape, args, flops=0, bytes_accessed=0):
    return pl.pallas_call(
        kernel,
        out_shape=out_shape,
        in_specs=[pl.BlockSpec(memory_space=pltpu.VMEM)] * len(args),
        out_specs=jax.tree.map(lambda _: pl.BlockSpec(memory_space=pltpu.VMEM), out_shape),
        compiler_params=pltpu.CompilerParams(vmem_limit_bytes=VMEM_LIMIT),
        cost_estimate=pl.CostEstimate(flops=flops, bytes_accessed=bytes_accessed, transcendentals=0),
    )(*args)


def shaped(shape, dtype):
    return jax.ShapeDtypeStruct(shape, dtype)


def around(array, axis):
    size = lax.axis_size(axis)
    return [array] + [
        lax.ppermute(array, axis, [(i, (i + shift) % size) for i in range(size)]) for shift in range(1, size)
    ]


def flip(array, axis, distance):
    return lax.ppermute(array, axis, [(i, i ^ 1 << distance) for i in range(lax.axis_size(axis))])


def merged(older, newer, size):
    older, newer = older.astype(f32), newer.astype(f32)
    decay = newer[size : size + 1]
    return jnp.concatenate([older[:size] * decay + newer[:size], older[size:] * decay], axis=0).astype(bf16)


def far_states(shard, size):
    rank = lax.axis_index("seq")
    levels = lax.axis_size("seq").bit_length() - 1
    states = []
    running = jnp.ones((1, shard.shape[1]), f32)
    for level in range(levels):
        theirs = flip(shard, "seq", level)
        upper = jnp.right_shift(rank, level) % 2 == 1
        states.append(jnp.where(upper, theirs[:size].astype(f32) * running, 0.0).astype(bf16))
        running = jnp.where(upper, running * theirs[size : size + 1].astype(f32), running)
        shard = merged(jnp.where(upper, theirs, shard), jnp.where(upper, shard, theirs), size)
    return states


def pair_states(shard, size):
    rank = lax.axis_index("seq")
    core = rank % 2
    half = shard.shape[1] // 2
    theirs = flip(shard, "seq", 0)
    mine_half, their_half = (lax.dynamic_slice_in_dim(a, core * half, half, 1) for a in (shard, theirs))
    pair = merged(
        jnp.where(core == 1, their_half, mine_half), jnp.where(core == 1, mine_half, their_half), size
    )
    from_x = lax.ppermute(pair, "seq", [(0, 2), (1, 3), (4, 6), (5, 7)])
    from_y = lax.ppermute(pair, "seq", [(i, i + 4) for i in range(4)])
    from_diagonal = lax.ppermute(pair, "seq", [(0, 6), (1, 7), (2, 4), (3, 5)])
    own = [from_x, from_y, from_diagonal]
    return theirs, own, [flip(array, "seq", 0) for array in own]


def on_device(inputs, gate, input_map, output_map, step, decay_rate, level_mix, skip, norm_gain):
    tokens, width = inputs.shape
    heads = step.shape[0]
    parts = lax.axis_size("head")
    size = input_map.shape[0] * parts
    groups = tokens // GROUP
    spans = local_spans(groups)
    in_maps = around(input_map, "head")
    out_maps = around(output_map, "head")
    dense = 2 * tokens * GROUP * width
    scaled, cum = call(
        prepare_kernel,
        (shaped((tokens, width), bf16), shaped((heads, tokens), f32)),
        (inputs, step, decay_rate[:, None]),
        flops=dense,
        bytes_accessed=4 * tokens * width,
    )
    shard_shape = shaped((size + DECAY_ROWS, width), bf16)
    span_shape = [shaped((len(spans) * size, width), bf16)] if spans else []
    shard, *span_states = call(
        functools.partial(states_kernel, parts),
        (shard_shape, *span_shape),
        (*in_maps, scaled, cum),
        flops=dense,
        bytes_accessed=4 * tokens * width,
    )
    pairs = lax.axis_size("seq") == 8 and parts == 4
    if pairs:
        core_state, own, other = pair_states(shard, size)
        far_args, kernel = (core_state, *own, *other), functools.partial(far_kernel_of_pairs, parts)
    else:
        far_args = far_states(shard, size)
        kernel = functools.partial(far_kernel, parts, len(far_args))
    near, swish = call(
        functools.partial(near_kernel, parts, spans),
        (shaped((tokens, width), f32),) * 2,
        (*in_maps, *out_maps, scaled, cum, inputs, gate, level_mix, skip[:, None], *span_states),
        flops=4 * dense,
        bytes_accessed=14 * tokens * width,
    )
    gated, squares = call(
        kernel,
        (shaped((tokens, width), f32), shaped((1, tokens), f32)),
        (*out_maps, cum, level_mix, near, swish, *far_args),
        flops=4 * dense,
        bytes_accessed=14 * tokens * width,
    )
    return call(
        functools.partial(norm_kernel, parts, width * parts),
        shaped((tokens, width), bf16),
        (*around(squares, "head"), gated, norm_gain[None, :]),
        flops=dense,
        bytes_accessed=6 * tokens * width,
    )


def solution(mesh):
    return jax.shard_map(
        on_device,
        mesh=mesh,
        in_specs=(
            P("seq", "head"),
            P("seq", "head"),
            P("head", "seq"),
            P("head", "seq"),
            P("head", "seq"),
            P("head"),
            P(None, "head", "seq"),
            P("head"),
            P("head"),
        ),
        out_specs=P("seq", "head"),
        check_vma=False,
    )
```

time: 110 us -> 55.2 us (0.50)
  blocking collectives: 40.7 us -> 0 us
  matrix products: 20.3 us -> 0 us
  starting transfers between devices: 5.07 us -> 23.7 us
  other arithmetic: 19.6 us -> 1.1 us
  Pallas kernels: 0 us -> 10.5 us
  local copies, waits for them, and re-layouts: 14.2 us -> 6.76 us
  waiting for transfers between devices: 9.11 us -> 12.2 us
    all_gather x2 -> x0, blocking collectives: 28.6 us -> none  [the longest x1 15.1 us: on_device(): lax.all_gather(input_map, 'head', axis=0, tiled=True)]
    dot_general x5 -> x0, matrix products: 20.3 us -> none  [the longest x1 8.08 us: project_states(): jnp.einsum('nct,cnk->ctk', out_blocks, paired, preferred_element_type=jnp...]
    ppermute x5 -> x16, starting transfers between devices: 5.07 us -> 23.7 us  [the longest x9 13.2 us: around(): lax.ppermute(array, axis, [(i, (i + shift) % size) for i in range(size)])]
    psum x1 -> x0, blocking collectives: 12.1 us -> none  [on_device(): summed = lax.psum(squares, 'head')]
    pallas_call x0 -> x5, Pallas kernels: none -> 10.5 us  [call(): pl.pallas_call(kernel, out_shape=out_shape, in_specs=[pl.BlockSpec(memory...]
    add x1 -> x0, other arithmetic: 10.2 us -> none  [project_states(): proj = proj[:, :, :half] + proj[:, :, half:]]
    reshape x4 -> x0, local copies, waits for them, and re-layouts: 4.66 us -> none  [the longest x2 4.64 us: on_device(): values = inputs.reshape(groups, GROUP, heads_here, P_SIZE)]
    unnamed x36 -> x28, local copies, waits for them, and re-layouts: 1.91 us -> 5.93 us
  transfers between devices with their start and end apart: 5 -> 16, of which waited for: 3 -> 9; matrix products, arithmetic and copies ran while one was open for 8% -> 2% of each run, Pallas kernels for 0% -> 7%
where the time goes in v1:
time: 55.2 us; the launch traced here: 54.5 us
  starting transfers between devices  23.7 us (43%)
  waiting for transfers between devices  12.2 us (22%)
  Pallas kernels  10.5 us (19%)
  local copies, waits for them, and re-layouts  6.76 us (12%)
  other arithmetic  1.1 us (2%)
    ppermute x9, starting transfers between devices, around(): lax.ppermute(array, axis, [(i, (i + shift) % size) for i in range(size)])  13.2 us
    pallas_call x5, Pallas kernels, call(): pl.pallas_call(kernel, out_shape=out_shape, in_specs=[pl.BlockSpec(memory...  10.5 us
    ppermute x9, waiting for transfers between devices, around(): lax.ppermute(array, axis, [(i, (i + shift) % size) for i in range(size)])  10.2 us
    unnamed x28, local copies, waits for them, and re-layouts  5.93 us
    ppermute x1, starting transfers between devices, pair_states(): from_diagonal = lax.ppermute(pair, 'seq', [(0, 6), (1, 7), (2, 4), (3, 5)])  5.02 us
    ppermute x1, starting transfers between devices, pair_states(): from_x = lax.ppermute(pair, 'seq', [(0, 2), (1, 3), (4, 6), (5, 7)])  3.08 us
    ppermute x1, starting transfers between devices, pair_states(): from_y = lax.ppermute(pair, 'seq', [(i, i + 4) for i in range(4)])  1.95 us
    ppermute x4, waiting for transfers between devices, flip(): lax.ppermute(array, axis, [(i, i ^ 1 << distance) for i in range(lax.axis...  1.93 us
  transfers between devices with their start and end apart: 16, of which 9 were waited for; matrix products, arithmetic and copies ran while one was open for 2% of the time, Pallas kernels for 7%

profile of v1, /device:TPU:0, one launch (start us, length us, event | category | flops | bytes accessed | tf_op | source)
XLA Modules:
  0.0 54.5 jit_solution(8377332623126116349)
XLA Ops:
  0.0 5.0 %collective-permute-start.5 = (bf16[32,512]{1,0:T(8,128)(2,1)}, bf16[32,512]{1,0:T(8,128)(2,1)S(1)}, u32[]{:S(2)}, u32[]{:S(2)}) collective-permute-start(bf16[32,512]{1,0:T(8,128)(2,1)} %refs_0_.4), channel_id=1, source_target_pairs={{0,3},{1,0},{2,1},{3,2},{4,7},{5,4},{6,5},{7,6},{8,11},{9,8},{10,9... | collective-permute-start | bytes 98312 | tf_op jit(solution)/shard_map/ppermute | solution.py:256
  5.1 1.0 %collective-permute-start.3 = (bf16[32,512]{1,0:T(8,128)(2,1)}, bf16[32,512]{1,0:T(8,128)(2,1)}, u32[]{:S(2)}, u32[]{:S(2)}) collective-permute-start(bf16[32,512]{1,0:T(8,128)(2,1)} %refs_0_.4), channel_id=1, source_target_pairs={{0,1},{1,2},{2,3},{3,0},{4,5},{5,6},{6,7},{7,4},{8,9},{9,10},{10,1... | collective-permute-start | bytes 98312 | tf_op jit(solution)/shard_map/ppermute | solution.py:256
  6.1 0.7 %copy.10.rate_ref = f32[16,1]{1,0:T(8,128)S(1)} copy(f32[16,1]{0,1:T(1,128)} %bitcast.7) | data formatting | bytes 128 | tf_op jit(solution)/shard_map/broadcast_in_dim | solution.py:313
  6.8 1.2 %copy-done = bf16[512,1024]{1,0:T(8,128)(2,1)S(1)} copy-done((bf16[512,1024]{1,0:T(8,128)(2,1)S(1)}, bf16[512,1024]{1,0:T(8,128)(2,1)}, u32[]{:S(2)}) %copy-start) | copy-done | bytes 1048600
  8.0 0.8 %copy-done.11 = f32[16,512]{1,0:T(8,128)S(1)} copy-done((f32[16,512]{1,0:T(8,128)S(1)}, f32[16,512]{1,0:T(8,128)}, u32[]{:S(2)}) %copy-start.11) | copy-done | bytes 32792
  8.8 1.3 %shard_map.91 = (bf16[512,1024]{1,0:T(8,128)(2,1)S(1)}, f32[16,512]{1,0:T(8,128)S(1)}) custom-call(bf16[512,1024]{1,0:T(8,128)(2,1)S(1)} %copy-done, f32[16,512]{1,0:T(8,128)S(1)} %copy-done.11, f32[16,1]{1,0:T(8,128)S(1)} %copy.10.rate_ref), custom_call_target="tpu_custom_call" | custom-call | flops 268435456 | bytes 2097152 | tf_op jit(solution)/shard_map/pallas_call | solution.py:239
  10.2 0.9 %collective-permute-done.3.refs_1_ = bf16[32,512]{1,0:T(8,128)(2,1)} collective-permute-done((bf16[32,512]{1,0:T(8,128)(2,1)}, bf16[32,512]{1,0:T(8,128)(2,1)}, u32[]{:S(2)}, u32[]{:S(2)}) %collective-permute-start.3) | collective-permute-done | bytes 32800 | tf_op jit(solution)/shard_map/ppermute | solution.py:256
  11.1 0.8 %copy-done.7 = bf16[32,512]{1,0:T(8,128)(2,1)S(1)} copy-done((bf16[32,512]{1,0:T(8,128)(2,1)S(1)}, bf16[32,512]{1,0:T(8,128)(2,1)}, u32[]{:S(2)}) %copy-start.7) | copy-done | bytes 32792
  11.8 1.8 %shard_map.92 = (bf16[144,1024]{1,0:T(8,128)(2,1)}, bf16[128,1024]{1,0:T(8,128)(2,1)S(1)}) custom-call(bf16[32,512]{1,0:T(8,128)(2,1)S(1)} %copy-done.7, bf16[32,512]{1,0:T(8,128)(2,1)} %collective-permute-done.3.refs_1_, bf16[32,512]{1,0:T(8,128)(2,1)} %collective-permute-done.4.refs_2_, bf16[32,512]{1,0:T(8,128)(2,1)S(1)} %collective-permute-done.5.refs_3_, ...), custom_call_target="tpu_custom_call" | custom-call | flops 268435456 | bytes 2097152 | tf_op jit(solution)/shard_map/pallas_call | solution.py:239
  13.6 0.7 %copy-done.4 = bf16[128,1024]{1,0:T(8,128)(2,1)} copy-done((bf16[128,1024]{1,0:T(8,128)(2,1)}, bf16[128,1024]{1,0:T(8,128)(2,1)S(1)}, u32[]{:S(2)}) %copy-start.4) | copy-done | bytes 262168
  14.4 1.9 %collective-permute-done.6.refs_8_ = bf16[144,1024]{1,0:T(8,128)(2,1)} collective-permute-done((bf16[144,1024]{1,0:T(8,128)(2,1)}, bf16[144,1024]{1,0:T(8,128)(2,1)}, u32[]{:S(2)}, u32[]{:S(2)}) %collective-permute-start.6) | collective-permute-done | bytes 294944 | tf_op jit(solution)/shard_map/ppermute | solution.py:261
  16.3 1.0 %select_convert_fusion = (f32[144,512]{1,0:T(8,128)S(1)}, f32[144,512]{1,0:T(8,128)S(1)}) fusion(pred[]{:T(512)S(6)} %eq.6, bf16[144,1024]{1,0:T(8,128)(2,1)} %get-tuple-element.18, s32[]{:T(128)S(6)} %select_n.25, bf16[144,1024]{1,0:T(8,128)(2,1)} %collective-permute-done.6.refs_8_), kind=kLoop, calls=%fused_computation.4 | loop fusion | flops 294912 | bytes 884741 | tf_op jit(solution)/shard_map/convert_element_type | solution.py:265
  17.4 5.0 %collective-permute-start.9 = (bf16[144,512]{1,0:T(8,128)(2,1)S(1)}, bf16[144,512]{1,0:T(8,128)(2,1)}, u32[]{:S(2)}, u32[]{:S(2)}) collective-permute-start(bf16[144,512]{1,0:T(8,128)(2,1)S(1)} %pad_maximum_fusion), channel_id=1, source_target_pairs={{0,24},{4,28},{8,16},{12,20},{1,25},{5,29},{9,17},{13,21},{2,26},{... | collective-permute-start | bytes 442376 | tf_op jit(solution)/shard_map/ppermute | solution.py:295
  22.4 1.9 %collective-permute-start.8 = (bf16[144,512]{1,0:T(8,128)(2,1)S(1)}, bf16[144,512]{1,0:T(8,128)(2,1)}, u32[]{:S(2)}, u32[]{:S(2)}) collective-permute-start(bf16[144,512]{1,0:T(8,128)(2,1)S(1)} %pad_maximum_fusion), channel_id=1, source_target_pairs={{0,16},{4,20},{8,24},{12,28},{1,17},{5,21},{9,25},{13,29},{2,18},{... | collective-permute-start | bytes 442376 | tf_op jit(solution)/shard_map/ppermute | solution.py:294
  24.4 3.1 %collective-permute-start.7 = (bf16[144,512]{1,0:T(8,128)(2,1)S(1)}, bf16[144,512]{1,0:T(8,128)(2,1)}, u32[]{:S(2)}, u32[]{:S(2)}) collective-permute-start(bf16[144,512]{1,0:T(8,128)(2,1)S(1)} %pad_maximum_fusion), channel_id=1, source_target_pairs={{0,8},{4,12},{16,24},{20,28},{1,9},{5,13},{17,25},{21,29},{2,10},{... | collective-permute-start | bytes 442376 | tf_op jit(solution)/shard_map/ppermute | solution.py:293
  27.5 1.9 %collective-permute-start.2 = (bf16[32,512]{1,0:T(8,128)(2,1)S(1)}, bf16[32,512]{1,0:T(8,128)(2,1)S(1)}, u32[]{:S(2)}, u32[]{:S(2)}) collective-permute-start(bf16[32,512]{1,0:T(8,128)(2,1)S(1)} %copy-done.6), channel_id=1, source_target_pairs={{0,3},{1,0},{2,1},{3,2},{4,7},{5,4},{6,5},{7,6},{8,11},{9,8},{10,9... | collective-permute-start | bytes 98312 | tf_op jit(solution)/shard_map/ppermute | solution.py:256
  29.4 0.5 collective-permute-start.11
  30.0 1.1 %collective-permute-start.1 = (bf16[32,512]{1,0:T(8,128)(2,1)S(1)}, bf16[32,512]{1,0:T(8,128)(2,1)}, u32[]{:S(2)}, u32[]{:S(2)}) collective-permute-start(bf16[32,512]{1,0:T(8,128)(2,1)S(1)} %copy-done.6), channel_id=1, source_target_pairs={{0,2},{1,3},{2,0},{3,1},{4,6},{5,7},{6,4},{7,5},{8,10},{9,11},{10,... | collective-permute-start | bytes 98312 | tf_op jit(solution)/shard_map/ppermute | solution.py:256
  31.4 1.6 %collective-permute-start = (bf16[32,512]{1,0:T(8,128)(2,1)S(1)}, bf16[32,512]{1,0:T(8,128)(2,1)}, u32[]{:S(2)}, u32[]{:S(2)}) collective-permute-start(bf16[32,512]{1,0:T(8,128)(2,1)S(1)} %copy-done.6), channel_id=1, source_target_pairs={{0,1},{1,2},{2,3},{3,0},{4,5},{5,6},{6,7},{7,4},{8,9},{9,10},{10,1... | collective-permute-start | bytes 98312 | tf_op jit(solution)/shard_map/ppermute | solution.py:256
  33.0 1.8 %collective-permute-done.1.refs_6_.refs_2_ = bf16[32,512]{1,0:T(8,128)(2,1)} collective-permute-done((bf16[32,512]{1,0:T(8,128)(2,1)S(1)}, bf16[32,512]{1,0:T(8,128)(2,1)}, u32[]{:S(2)}, u32[]{:S(2)}) %collective-permute-start.1) | collective-permute-done | bytes 32800 | tf_op jit(solution)/shard_map/ppermute | solution.py:256
  34.9 2.3 %collective-permute-done.refs_5_.refs_1_ = bf16[32,512]{1,0:T(8,128)(2,1)} collective-permute-done((bf16[32,512]{1,0:T(8,128)(2,1)S(1)}, bf16[32,512]{1,0:T(8,128)(2,1)}, u32[]{:S(2)}, u32[]{:S(2)}) %collective-permute-start) | collective-permute-done | bytes 32800 | tf_op jit(solution)/shard_map/ppermute | solution.py:256
  37.2 0.9 %copy-done.5 = bf16[128,1024]{1,0:T(8,128)(2,1)S(1)} copy-done((bf16[128,1024]{1,0:T(8,128)(2,1)S(1)}, bf16[128,1024]{1,0:T(8,128)(2,1)}, u32[]{:S(2)}) %copy-start.5) | copy-done | bytes 262168
  38.2 0.8 %copy-done.8 = bf16[32,512]{1,0:T(8,128)(2,1)S(1)} copy-done((bf16[32,512]{1,0:T(8,128)(2,1)S(1)}, bf16[32,512]{1,0:T(8,128)(2,1)}, u32[]{:S(2)}) %copy-start.8) | copy-done | bytes 32792
  38.9 0.8 %copy-done.10 = bf16[32,512]{1,0:T(8,128)(2,1)S(1)} copy-done((bf16[32,512]{1,0:T(8,128)(2,1)S(1)}, bf16[32,512]{1,0:T(8,128)(2,1)}, u32[]{:S(2)}) %copy-start.10) | copy-done | bytes 32792
  39.7 2.5 %shard_map.93 = (f32[512,1024]{1,0:T(8,128)S(1)}, f32[512,1024]{1,0:T(8,128)S(1)}) custom-call(bf16[32,512]{1,0:T(8,128)(2,1)S(1)} %copy-done.8, bf16[32,512]{1,0:T(8,128)(2,1)} %collective-permute-done.3.refs_1_, bf16[32,512]{1,0:T(8,128)(2,1)} %collective-permute-done.4.refs_2_, bf16[32,512]{1,0:T(8,128)(2,1)S(1)} %copy-done.10, ...), custom_call_target="tpu_custom_call" | custom-call | flops 1073741824 | bytes 7340032 | tf_op jit(solution)/shard_map/pallas_call | solution.py:239
  42.2 3.6 %shard_map.94 = (f32[512,1024]{1,0:T(8,128)S(1)}, f32[1,512]{1,0:T(1,128)S(1)}) custom-call(bf16[32,512]{1,0:T(8,128)(2,1)S(1)} %copy-done.6, bf16[32,512]{1,0:T(8,128)(2,1)} %collective-permute-done.refs_5_.refs_1_, bf16[32,512]{1,0:T(8,128)(2,1)} %collective-permute-done.1.refs_6_.refs_2_, bf16[32,512]{1,0:T(8,128)(2,1)S(1)} %collective-permute-done.2.refs_7_.refs_3_, ...), custom_call_target="tpu_custom_call" | custom-call | flops 1073741824 | bytes 7340032 | tf_op jit(solution)/shard_map/pallas_call | solution.py:239
  45.8 1.9 %collective-permute-start.15 = (f32[1,512]{1,0:T(1,128)S(1)}, f32[1,512]{1,0:T(1,128)S(1)}, u32[]{:S(2)}, u32[]{:S(2)}) collective-permute-start(f32[1,512]{1,0:T(1,128)S(1)} %get-tuple-element.19.refs_0_), channel_id=1, source_target_pairs={{0,3},{1,0},{2,1},{3,2},{4,7},{5,4},{6,5},{7,6},{8,11},{9,8},{10,9... | collective-permute-start | bytes 6152 | tf_op jit(solution)/shard_map/ppermute | solution.py:256
  47.8 0.6 %collective-permute-start.13 = (f32[1,512]{1,0:T(1,128)S(1)}, f32[1,512]{1,0:T(1,128)S(1)}, u32[]{:S(2)}, u32[]{:S(2)}) collective-permute-start(f32[1,512]{1,0:T(1,128)S(1)} %get-tuple-element.19.refs_0_), channel_id=1, source_target_pairs={{0,1},{1,2},{2,3},{3,0},{4,5},{5,6},{6,7},{7,4},{8,9},{9,10},{10,1... | collective-permute-start | bytes 6152 | tf_op jit(solution)/shard_map/ppermute | solution.py:256
  48.4 1.1 %collective-permute-done.15.refs_3_ = f32[1,512]{1,0:T(1,128)S(1)} collective-permute-done((f32[1,512]{1,0:T(1,128)S(1)}, f32[1,512]{1,0:T(1,128)S(1)}, u32[]{:S(2)}, u32[]{:S(2)}) %collective-permute-start.15) | collective-permute-done | bytes 2080 | tf_op jit(solution)/shard_map/ppermute | solution.py:256
  49.4 2.8 %collective-permute-done.14.refs_2_ = f32[1,512]{1,0:T(1,128)S(1)} collective-permute-done((f32[1,512]{1,0:T(1,128)S(1)}, f32[1,512]{1,0:T(1,128)S(1)}, u32[]{:S(2)}, u32[]{:S(2)}) %collective-permute-start.14) | collective-permute-done | bytes 2080 | tf_op jit(solution)/shard_map/ppermute | solution.py:256
  52.2 0.9 %collective-permute-done.13.refs_1_ = f32[1,512]{1,0:T(1,128)S(1)} collective-permute-done((f32[1,512]{1,0:T(1,128)S(1)}, f32[1,512]{1,0:T(1,128)S(1)}, u32[]{:S(2)}, u32[]{:S(2)}) %collective-permute-start.13) | collective-permute-done | bytes 2080 | tf_op jit(solution)/shard_map/ppermute | solution.py:256
  53.1 1.3 %shard_map.95 = bf16[512,1024]{1,0:T(8,128)(2,1)} custom-call(f32[1,512]{1,0:T(1,128)S(1)} %get-tuple-element.19.refs_0_, f32[1,512]{1,0:T(1,128)S(1)} %collective-permute-done.13.refs_1_, f32[1,512]{1,0:T(1,128)S(1)} %collective-permute-done.14.refs_2_, f32[1,512]{1,0:T(1,128)S(1)} %collective-permute-done.15.refs_3_, ...), custom_call_target="tpu_custom_call" | custom-call | flops 268435456 | bytes 3145728 | tf_op jit(solution)/shard_map/pallas_call | solution.py:239
  (40 shorter events, 0.6 us)
Async XLA Ops:
  0.0 10.1 %collective-permute-start.5 = (bf16[32,512]{1,0:T(8,128)(2,1)}, bf16[32,512]{1,0:T(8,128)(2,1)S(1)}, u32[]{:S(2)}, u32[]{:S(2)}) collective-permute-start(bf16[32,512]{1,0:T(8,128)(2,1)} %refs_0_.4), channel_id=1, source_target_pairs={{0,3},{1,0},{2,1},{3,2},{4,7},{5,4},{6,5},{7,6},{8,11},{9,8},{10,9... | collective-permute-start | bytes 98312 | tf_op jit(solution)/shard_map/ppermute | solution.py:256
  5.0 5.1 %collective-permute-start.4 = (bf16[32,512]{1,0:T(8,128)(2,1)}, bf16[32,512]{1,0:T(8,128)(2,1)}, u32[]{:S(2)}, u32[]{:S(2)}) collective-permute-start(bf16[32,512]{1,0:T(8,128)(2,1)} %refs_0_.4), channel_id=1, source_target_pairs={{0,2},{1,3},{2,0},{3,1},{4,6},{5,7},{6,4},{7,5},{8,10},{9,11},{10,... | collective-permute-start | bytes 98312 | tf_op jit(solution)/shard_map/ppermute | solution.py:256
  5.1 6.0 %collective-permute-start.3 = (bf16[32,512]{1,0:T(8,128)(2,1)}, bf16[32,512]{1,0:T(8,128)(2,1)}, u32[]{:S(2)}, u32[]{:S(2)}) collective-permute-start(bf16[32,512]{1,0:T(8,128)(2,1)} %refs_0_.4), channel_id=1, source_target_pairs={{0,1},{1,2},{2,3},{3,0},{4,5},{5,6},{6,7},{7,4},{8,9},{9,10},{10,1... | collective-permute-start | bytes 98312 | tf_op jit(solution)/shard_map/ppermute | solution.py:256
  6.1 26.9 %copy-start.13 = (f32[16]{0:T(128)S(1)}, f32[16]{0:T(128)}, u32[]{:S(2)}) copy-start(f32[16]{0:T(128)} %param.16) | copy-start | bytes 196
  6.8 1.2 %copy-start = (bf16[512,1024]{1,0:T(8,128)(2,1)S(1)}, bf16[512,1024]{1,0:T(8,128)(2,1)}, u32[]{:S(2)}) copy-start(bf16[512,1024]{1,0:T(8,128)(2,1)} %refs_10_.1) | copy-start | bytes 3145732
  8.0 0.8 %copy-start.11 = (f32[16,512]{1,0:T(8,128)S(1)}, f32[16,512]{1,0:T(8,128)}, u32[]{:S(2)}) copy-start(f32[16,512]{1,0:T(8,128)} %step_ref.1) | copy-start | bytes 98308
  8.8 18.7 %copy-start.6 = (bf16[32,512]{1,0:T(8,128)(2,1)S(1)}, bf16[32,512]{1,0:T(8,128)(2,1)}, u32[]{:S(2)}) copy-start(bf16[32,512]{1,0:T(8,128)(2,1)} %refs_0_.5) | copy-start | bytes 98308
  8.8 28.4 %copy-start.1 = (bf16[512,1024]{1,0:T(8,128)(2,1)S(1)}, bf16[512,1024]{1,0:T(8,128)(2,1)}, u32[]{:S(2)}) copy-start(bf16[512,1024]{1,0:T(8,128)(2,1)} %refs_10_.1) | copy-start | bytes 3145732
  8.8 28.4 %copy-start.2 = (f32[9,16,512]{2,1,0:T(8,128)S(1)}, f32[9,16,512]{2,1,0:T(8,128)}, u32[]{:S(2)}) copy-start(f32[9,16,512]{2,1,0:T(8,128)} %refs_5_.1) | copy-start | bytes 884740
  8.8 28.4 %copy-start.3 = (bf16[512,1024]{1,0:T(8,128)(2,1)S(1)}, bf16[512,1024]{1,0:T(8,128)(2,1)}, u32[]{:S(2)}) copy-start(bf16[512,1024]{1,0:T(8,128)(2,1)} %refs_11_.1) | copy-start | bytes 3145732
  10.1 14.3 %copy-start.9 = (bf16[32,512]{1,0:T(8,128)(2,1)}, bf16[32,512]{1,0:T(8,128)(2,1)S(1)}, u32[]{:S(2)}) copy-start(bf16[32,512]{1,0:T(8,128)(2,1)S(1)} %collective-permute-done.5.refs_3_) | copy-start | bytes 98308
  11.1 0.8 %copy-start.7 = (bf16[32,512]{1,0:T(8,128)(2,1)S(1)}, bf16[32,512]{1,0:T(8,128)(2,1)}, u32[]{:S(2)}) copy-start(bf16[32,512]{1,0:T(8,128)(2,1)} %refs_0_.4) | copy-start | bytes 98308
  13.6 0.7 %copy-start.4 = (bf16[128,1024]{1,0:T(8,128)(2,1)}, bf16[128,1024]{1,0:T(8,128)(2,1)S(1)}, u32[]{:S(2)}) copy-start(bf16[128,1024]{1,0:T(8,128)(2,1)S(1)} %get-tuple-element.15.refs_14_) | copy-start | bytes 786436
  14.3 1.9 %collective-permute-start.6 = (bf16[144,1024]{1,0:T(8,128)(2,1)}, bf16[144,1024]{1,0:T(8,128)(2,1)}, u32[]{:S(2)}, u32[]{:S(2)}) collective-permute-start(bf16[144,1024]{1,0:T(8,128)(2,1)} %get-tuple-element.18), channel_id=1, source_target_pairs={{0,4},{4,0},{8,12},{12,8},{16,20},{20,16},{24,28},{28,24},{1,5},{5... | collective-permute-start | bytes 884744 | tf_op jit(solution)/shard_map/ppermute | solution.py:261
  17.4 12.0 %collective-permute-start.9 = (bf16[144,512]{1,0:T(8,128)(2,1)S(1)}, bf16[144,512]{1,0:T(8,128)(2,1)}, u32[]{:S(2)}, u32[]{:S(2)}) collective-permute-start(bf16[144,512]{1,0:T(8,128)(2,1)S(1)} %pad_maximum_fusion), channel_id=1, source_target_pairs={{0,24},{4,28},{8,16},{12,20},{1,25},{5,29},{9,17},{13,21},{2,26},{... | collective-permute-start | bytes 442376 | tf_op jit(solution)/shard_map/ppermute | solution.py:295
  22.4 6.9 %collective-permute-start.8 = (bf16[144,512]{1,0:T(8,128)(2,1)S(1)}, bf16[144,512]{1,0:T(8,128)(2,1)}, u32[]{:S(2)}, u32[]{:S(2)}) collective-permute-start(bf16[144,512]{1,0:T(8,128)(2,1)S(1)} %pad_maximum_fusion), channel_id=1, source_target_pairs={{0,16},{4,20},{8,24},{12,28},{1,17},{5,21},{9,25},{13,29},{2,18},{... | collective-permute-start | bytes 442376 | tf_op jit(solution)/shard_map/ppermute | solution.py:294
  24.4 5.5 %collective-permute-start.7 = (bf16[144,512]{1,0:T(8,128)(2,1)S(1)}, bf16[144,512]{1,0:T(8,128)(2,1)}, u32[]{:S(2)}, u32[]{:S(2)}) collective-permute-start(bf16[144,512]{1,0:T(8,128)(2,1)S(1)} %pad_maximum_fusion), channel_id=1, source_target_pairs={{0,8},{4,12},{16,24},{20,28},{1,9},{5,13},{17,25},{21,29},{2,10},{... | collective-permute-start | bytes 442376 | tf_op jit(solution)/shard_map/ppermute | solution.py:293
  27.5 3.9 %collective-permute-start.2 = (bf16[32,512]{1,0:T(8,128)(2,1)S(1)}, bf16[32,512]{1,0:T(8,128)(2,1)S(1)}, u32[]{:S(2)}, u32[]{:S(2)}) collective-permute-start(bf16[32,512]{1,0:T(8,128)(2,1)S(1)} %copy-done.6), channel_id=1, source_target_pairs={{0,3},{1,0},{2,1},{3,2},{4,7},{5,4},{6,5},{7,6},{8,11},{9,8},{10,9... | collective-permute-start | bytes 98312 | tf_op jit(solution)/shard_map/ppermute | solution.py:256
  29.4 12.8 %collective-permute-start.12 = (bf16[144,512]{1,0:T(8,128)(2,1)}, bf16[144,512]{1,0:T(8,128)(2,1)}, u32[]{:S(2)}, u32[]{:S(2)}) collective-permute-start(bf16[144,512]{1,0:T(8,128)(2,1)} %collective-permute-done.9.refs_11_), channel_id=1, source_target_pairs={{0,4},{4,0},{8,12},{12,8},{16,20},{20,16},{24,28},{28,24},{1,5},{5... | collective-permute-start | bytes 442376 | tf_op jit(solution)/shard_map/ppermute | solution.py:261
  29.4 12.8 %collective-permute-start.11 = (bf16[144,512]{1,0:T(8,128)(2,1)}, bf16[144,512]{1,0:T(8,128)(2,1)}, u32[]{:S(2)}, u32[]{:S(2)}) collective-permute-start(bf16[144,512]{1,0:T(8,128)(2,1)} %collective-permute-done.8.refs_10_), channel_id=1, source_target_pairs={{0,4},{4,0},{8,12},{12,8},{16,20},{20,16},{24,28},{28,24},{1,5},{5... | collective-permute-start | bytes 442376 | tf_op jit(solution)/shard_map/ppermute | solution.py:261
  29.9 12.3 %collective-permute-start.10 = (bf16[144,512]{1,0:T(8,128)(2,1)}, bf16[144,512]{1,0:T(8,128)(2,1)}, u32[]{:S(2)}, u32[]{:S(2)}) collective-permute-start(bf16[144,512]{1,0:T(8,128)(2,1)} %collective-permute-done.7.refs_9_), channel_id=1, source_target_pairs={{0,4},{4,0},{8,12},{12,8},{16,20},{20,16},{24,28},{28,24},{1,5},{5... | collective-permute-start | bytes 442376 | tf_op jit(solution)/shard_map/ppermute | solution.py:261
  30.0 4.9 %collective-permute-start.1 = (bf16[32,512]{1,0:T(8,128)(2,1)S(1)}, bf16[32,512]{1,0:T(8,128)(2,1)}, u32[]{:S(2)}, u32[]{:S(2)}) collective-permute-start(bf16[32,512]{1,0:T(8,128)(2,1)S(1)} %copy-done.6), channel_id=1, source_target_pairs={{0,2},{1,3},{2,0},{3,1},{4,6},{5,7},{6,4},{7,5},{8,10},{9,11},{10,... | collective-permute-start | bytes 98312 | tf_op jit(solution)/shard_map/ppermute | solution.py:256
  31.4 5.8 %collective-permute-start = (bf16[32,512]{1,0:T(8,128)(2,1)S(1)}, bf16[32,512]{1,0:T(8,128)(2,1)}, u32[]{:S(2)}, u32[]{:S(2)}) collective-permute-start(bf16[32,512]{1,0:T(8,128)(2,1)S(1)} %copy-done.6), channel_id=1, source_target_pairs={{0,1},{1,2},{2,3},{3,0},{4,5},{5,6},{6,7},{7,4},{8,9},{9,10},{10,1... | collective-permute-start | bytes 98312 | tf_op jit(solution)/shard_map/ppermute | solution.py:256
  37.2 1.0 %copy-start.5 = (bf16[128,1024]{1,0:T(8,128)(2,1)S(1)}, bf16[128,1024]{1,0:T(8,128)(2,1)}, u32[]{:S(2)}) copy-start(bf16[128,1024]{1,0:T(8,128)(2,1)} %copy-done.4) | copy-start | bytes 786436
  38.2 0.8 %copy-start.8 = (bf16[32,512]{1,0:T(8,128)(2,1)S(1)}, bf16[32,512]{1,0:T(8,128)(2,1)}, u32[]{:S(2)}) copy-start(bf16[32,512]{1,0:T(8,128)(2,1)} %refs_0_.4) | copy-start | bytes 98308
  38.9 0.8 %copy-start.10 = (bf16[32,512]{1,0:T(8,128)(2,1)S(1)}, bf16[32,512]{1,0:T(8,128)(2,1)}, u32[]{:S(2)}) copy-start(bf16[32,512]{1,0:T(8,128)(2,1)} %copy-done.9) | copy-start | bytes 98308
  42.2 10.9 %copy-start.12 = (f32[1024]{0:T(1024)S(1)}, f32[1024]{0:T(1024)}, u32[]{:S(2)}) copy-start(f32[1024]{0:T(1024)} %param.17) | copy-start | bytes 12292
  45.8 3.6 %collective-permute-start.15 = (f32[1,512]{1,0:T(1,128)S(1)}, f32[1,512]{1,0:T(1,128)S(1)}, u32[]{:S(2)}, u32[]{:S(2)}) collective-permute-start(f32[1,512]{1,0:T(1,128)S(1)} %get-tuple-element.19.refs_0_), channel_id=1, source_target_pairs={{0,3},{1,0},{2,1},{3,2},{4,7},{5,4},{6,5},{7,6},{8,11},{9,8},{10,9... | collective-permute-start | bytes 6152 | tf_op jit(solution)/shard_map/ppermute | solution.py:256
  47.7 4.5 %collective-permute-start.14 = (f32[1,512]{1,0:T(1,128)S(1)}, f32[1,512]{1,0:T(1,128)S(1)}, u32[]{:S(2)}, u32[]{:S(2)}) collective-permute-start(f32[1,512]{1,0:T(1,128)S(1)} %get-tuple-element.19.refs_0_), channel_id=1, source_target_pairs={{0,2},{1,3},{2,0},{3,1},{4,6},{5,7},{6,4},{7,5},{8,10},{9,11},{10,... | collective-permute-start | bytes 6152 | tf_op jit(solution)/shard_map/ppermute | solution.py:256
  47.8 5.4 %collective-permute-start.13 = (f32[1,512]{1,0:T(1,128)S(1)}, f32[1,512]{1,0:T(1,128)S(1)}, u32[]{:S(2)}, u32[]{:S(2)}) collective-permute-start(f32[1,512]{1,0:T(1,128)S(1)} %get-tuple-element.19.refs_0_), channel_id=1, source_target_pairs={{0,1},{1,2},{2,3},{3,0},{4,5},{5,6},{6,7},{7,4},{8,9},{9,10},{10,1... | collective-permute-start | bytes 6152 | tf_op jit(solution)/shard_map/ppermute | solution.py:256

commit v2 on v1

v2 whole, which is shorter than its diff:
```python
import functools

import jax
import jax.numpy as jnp
from jax import lax
from jax.experimental import pallas as pl
from jax.experimental.pallas import tpu as pltpu
from jax.sharding import PartitionSpec as P

P_SIZE = 64
GROUP = 256
DECAY_ROWS = 16
BLOCK = 256
VMEM_LIMIT = 40 * 1024 * 1024

f32, bf16 = jnp.float32, jnp.bfloat16
HIGHEST = lax.Precision.HIGHEST
TRANSPOSED = (((0,), (0,)), ((), ()))


def expander(heads, width, copies):
    row = lax.broadcasted_iota(jnp.int32, (copies * heads, width), 0)
    col = lax.broadcasted_iota(jnp.int32, (copies * heads, width), 1)
    return jnp.where(lax.rem(row, heads) == lax.div(col, P_SIZE), 1.0, 0.0)


def two_parts(factor):
    high = factor.astype(bf16).astype(f32)
    return jnp.concatenate([high, factor - high], axis=0).astype(bf16)


def transposed_dot(left, right):
    return lax.dot_general(left, right, TRANSPOSED, preferred_element_type=f32)


def head_row(heads, width, column):
    return jnp.sum(expander(heads, width, 1) * column, axis=0, keepdims=True)


def group_slice(group):
    return slice(group * GROUP, (group + 1) * GROUP)


def blocks_of(width):
    return [slice(at, at + BLOCK) for at in range(0, width, BLOCK)]


def local_spans(groups):
    spans = []
    for later in range(groups):
        for bit in range(groups.bit_length() - 1):
            if later >> bit & 1:
                start = later >> bit + 1 << bit + 1
                spans.append((later, bit, start, start + 2**bit))
    return spans


def column_of(row):
    size = row.shape[1]
    at = lax.broadcasted_iota(jnp.int32, (size, size), 0) == lax.broadcasted_iota(jnp.int32, (size, size), 1)
    return jnp.sum(jnp.where(at, row, 0.0), axis=1, keepdims=True)


def map_rows(maps_ref, parts, which):
    rows = maps_ref.shape[0] // (2 * parts)
    maps = maps_ref[...] if rows % 16 == 0 else maps_ref[...].astype(f32)
    picked = [maps[(2 * part + which) * rows : (2 * part + which + 1) * rows] for part in range(parts)]
    return jnp.concatenate(picked, axis=0).astype(bf16)


def fetch(sources, targets, semaphores):
    copies = [
        pltpu.make_async_copy(source, target, semaphores.at[index])
        for index, (source, target) in enumerate(zip(sources, targets))
    ]
    for copy in copies:
        copy.start()
    return copies


def prepare_kernel(inputs_hbm, step_hbm, rate_hbm, scaled_ref, cum_ref, inputs_ref, step_ref, rate_ref, semaphores):
    copies = fetch((step_hbm, rate_hbm, inputs_hbm), (step_ref, rate_ref, inputs_ref), semaphores)
    heads, tokens = step_ref.shape
    width = inputs_ref.shape[1]
    row = lax.broadcasted_iota(jnp.int32, (GROUP, GROUP), 0)
    col = lax.broadcasted_iota(jnp.int32, (GROUP, GROUP), 1)
    until = jnp.where(row <= col, 1.0, 0.0)
    expand = expander(heads, width, 2).astype(bf16)
    copies[0].wait()
    copies[1].wait()
    step = step_ref[...]
    log_decay = -step * column_of(rate_ref[...])
    factors = []
    for group in range(tokens // GROUP):
        at = group_slice(group)
        cum = jnp.dot(log_decay[:, at], until, precision=HIGHEST, preferred_element_type=f32)
        cum_ref[:, at] = cum
        factors.append(two_parts(jnp.exp(-cum) * step[:, at]))
    factor = jnp.concatenate(factors, axis=1)
    copies[2].wait()
    for cols in blocks_of(width):
        scale = transposed_dot(factor, expand[:, cols])
        scaled_ref[:, cols] = (inputs_ref[:, cols].astype(f32) * scale).astype(bf16)


def states_kernel(parts, maps_ref, scaled_ref, cum_ref, *out_refs):
    shard_ref = out_refs[0]
    heads, tokens = cum_ref.shape
    width = scaled_ref.shape[1]
    in_map = map_rows(maps_ref, parts, 0)
    size = in_map.shape[0]
    cum = cum_ref[...]
    states, decays = [], []
    for group in range(tokens // GROUP):
        at = group_slice(group)
        decay = head_row(heads, width, jnp.exp(cum[:, at.stop - 1 : at.stop]))
        raw = jnp.dot(in_map[:, at], scaled_ref[at, :], preferred_element_type=f32)
        states.append(raw * decay)
        decays.append(decay)
    total, decay = states[0], decays[0]
    for group in range(1, len(states)):
        total = total * decays[group] + states[group]
        decay = decay * decays[group]
    shard_ref[:size, :] = total.astype(bf16)
    shard_ref[size:, :] = jnp.broadcast_to(decay, (DECAY_ROWS, width)).astype(bf16)
    for index, (later, _, start, stop) in enumerate(local_spans(len(states))):
        span = states[start]
        for group in range(start + 1, later):
            span = span * decays[group]
            if group < stop:
                span = span + states[group]
        out_refs[1][index * size : (index + 1) * size, :] = span.astype(bf16)


def merge_kernel(size, mine_ref, theirs_ref, pair_ref):
    core = lax.rem(lax.axis_index("seq"), 2)
    half = pair_ref.shape[1]
    mine = jnp.where(core == 1, mine_ref[:, half:], mine_ref[:, :half])
    theirs = jnp.where(core == 1, theirs_ref[:, half:], theirs_ref[:, :half])
    older = jnp.where(core == 1, theirs, mine).astype(f32)
    newer = jnp.where(core == 1, mine, theirs).astype(f32)
    decay = newer[size : size + 1]
    pair_ref[:size, :] = (older[:size] * decay + newer[:size]).astype(bf16)
    pair_ref[size:, :] = (older[size:] * decay).astype(bf16)


def near_kernel(parts, spans, levels, *refs):
    inputs_hbm, gate_hbm, mix_hbm, skip_hbm = refs[:4]
    maps_ref, scaled_ref, cum_ref, _ = refs[4:8]
    count = 1 if spans else 0
    span_refs = refs[8 : 8 + count]
    near_ref, far_ref, inputs_ref, gate_ref, mix_ref, skip_ref, semaphores = refs[8 + count :]
    copies = fetch(refs[:4], (inputs_ref, gate_ref, mix_ref, skip_ref), semaphores)
    heads, tokens = cum_ref.shape
    width = scaled_ref.shape[1]
    groups = tokens // GROUP
    first = groups.bit_length()
    in_map = map_rows(maps_ref, parts, 0)
    out_map = map_rows(maps_ref, parts, 1)
    size = in_map.shape[0]
    expand = expander(heads, width, 2).astype(bf16)
    row = lax.broadcasted_iota(jnp.int32, (GROUP, GROUP), 0)
    col = lax.broadcasted_iota(jnp.int32, (GROUP, GROUP), 1)
    scores = []
    for group in range(groups):
        at = group_slice(group)
        all_scores = transposed_dot(out_map[:, at], in_map[:, at])
        scores.append(jnp.where(row >= col, all_scores, 0.0).astype(bf16))
    for copy in copies:
        copy.wait()
    skip = head_row(heads, width, column_of(skip_ref[...]))
    before = jnp.zeros((heads, 1), f32)
    for group in range(groups):
        at = group_slice(group)
        cum = cum_ref[:, at]
        decay = jnp.exp(cum)
        mixes = [two_parts(mix_ref[0, :, at] * decay)]
        states = []
        for index, (later, bit, _, _) in enumerate(spans):
            if later == group:
                mixes.append(two_parts(mix_ref[1 + bit, :, at] * decay))
                states.append(slice(index * size, (index + 1) * size))
        decay = jnp.exp(cum + before)
        before = before + cum[:, GROUP - 1 : GROUP]
        far_mixes = [two_parts(mix_ref[first + level, :, at] * decay) for level in range(levels)]
        for cols in blocks_of(width):
            own = jnp.dot(scores[group], scaled_ref[at, cols], preferred_element_type=f32)
            total = transposed_dot(mixes[0], expand[:, cols]) * own
            for mix, rows in zip(mixes[1:], states):
                reach = transposed_dot(out_map[:, at], span_refs[0][rows, cols])
                total = total + transposed_dot(mix, expand[:, cols]) * reach
            total = total + skip[:, cols] * inputs_ref[at, cols].astype(f32)
            gate = gate_ref[at, cols].astype(f32)
            swish = gate / (1.0 + jnp.exp(-gate))
            near_ref[at, cols] = total * swish
            for level in range(levels):
                far_ref[level, at, cols] = (transposed_dot(far_mixes[level], expand[:, cols]) * swish).astype(bf16)


def far_body(out_map, near_ref, far_ref, start, columns, state_of, gated_ref):
    levels, tokens, _ = far_ref.shape
    squares = jnp.zeros((tokens, 128), f32)
    for cols in blocks_of(columns):
        at = pl.ds(pl.multiple_of(start + cols.start, BLOCK), BLOCK)
        total = near_ref[:, at]
        for level in range(levels):
            reach = transposed_dot(out_map, state_of(level, cols, at).astype(bf16))
            total = total + far_ref[level, :, at].astype(f32) * reach
        gated_ref[:, cols] = total
        total = total * total
        for part in range(0, BLOCK, 128):
            squares = squares + total[:, part : part + 128]
    ones = jnp.ones((8, 128), f32)
    sums = lax.dot_general(
        ones, squares, (((1,), (1,)), ((), ())), precision=HIGHEST, preferred_element_type=f32
    )
    return sums[:1]


def far_kernel(parts, maps_ref, near_ref, far_ref, *refs):
    state_refs = refs[:-2]
    gated_ref, squares_ref = refs[-2:]

    def state_of(level, cols, _):
        return state_refs[level][:, cols]

    out_map = map_rows(maps_ref, parts, 1)
    sums = far_body(out_map, near_ref, far_ref, 0, near_ref.shape[1], state_of, gated_ref)
    for part in range(parts):
        squares_ref[part] = sums


def far_kernel_of_half(parts, own, *refs):
    maps_ref, near_ref, far_ref, core_ref, x_ref, y_ref, diagonal_ref = refs[:7]
    gated_ref, squares_ref = refs[-2:]
    out_map = map_rows(maps_ref, parts, 1)
    size = out_map.shape[0]
    rank = lax.axis_index("seq")
    core = lax.rem(rank, 2)
    along_x = lax.rem(lax.div(rank, 2), 2)
    along_y = lax.div(rank, 4)
    half = x_ref.shape[1]
    start = (core if own else 1 - core) * half

    def parts_of(ref, cols):
        whole = ref[:, cols].astype(f32)
        return whole[:size], whole[size : size + 1]

    def state_of(level, cols, at):
        core_state, core_decay = parts_of(core_ref, at)
        if level == 0:
            return jnp.where(core == 1, core_state, 0.0)
        running = jnp.where(core == 1, core_decay, 1.0)
        x_state, x_decay = parts_of(x_ref, cols)
        if level == 1:
            return x_state * jnp.where(along_x == 1, running, 0.0)
        running = running * jnp.where(along_x == 1, x_decay, 1.0)
        running = jnp.where(along_y == 1, running, 0.0)
        y_state, y_decay = parts_of(y_ref, cols)
        d_state, d_decay = parts_of(diagonal_ref, cols)
        newer = jnp.where(along_x == 1, y_state, d_state)
        newer_decay = jnp.where(along_x == 1, y_decay, d_decay)
        older = jnp.where(along_x == 1, d_state, y_state)
        return (older * newer_decay + newer) * running

    sums = far_body(out_map, near_ref, far_ref, start, half, state_of, gated_ref)
    if own:
        squares_ref[...] = sums
    else:
        sums = sums + refs[7][...]
        for part in range(parts):
            squares_ref[part] = sums


def norm_kernel(columns, squares_ref, gain_ref, *refs):
    gated_refs, out_ref = refs[:-1], refs[-1]
    total = jnp.sum(squares_ref[...], axis=0)
    scale = lax.rsqrt(total / columns + 1e-05)
    scale = jnp.transpose(jnp.broadcast_to(scale, (8, scale.shape[1])))[:, :1]
    if len(gated_refs) == 1:
        out_ref[...] = (gated_refs[0][...] * scale * gain_ref[...]).astype(bf16)
        return
    half = gated_refs[0].shape[1]
    core = lax.rem(lax.axis_index("seq"), 2)
    for ref, side in zip(gated_refs, (core, 1 - core)):
        at = pl.ds(pl.multiple_of(side * half, half), half)
        out_ref[:, at] = (ref[...] * scale * gain_ref[:, at]).astype(bf16)


def call(kernel, out_shape, args, flops=0, bytes_accessed=0, hbm=0, fetched=()):
    specs = [pl.BlockSpec(memory_space=pl.ANY)] * hbm + [pl.BlockSpec(memory_space=pltpu.VMEM)] * (len(args) - hbm)
    args = [pltpu.with_memory_space_constraint(arg, pltpu.HBM) for arg in args[:hbm]] + list(args[hbm:])
    scratch = [pltpu.VMEM(arg.shape, arg.dtype) for arg in args[:hbm]]
    return pl.pallas_call(
        kernel,
        out_shape=out_shape,
        in_specs=specs,
        out_specs=jax.tree.map(lambda _: pl.BlockSpec(memory_space=pltpu.VMEM), out_shape),
        scratch_shapes=scratch + ([pltpu.SemaphoreType.DMA((hbm,))] if hbm else []),
        compiler_params=pltpu.CompilerParams(vmem_limit_bytes=VMEM_LIMIT),
        cost_estimate=pl.CostEstimate(flops=flops, bytes_accessed=bytes_accessed, transcendentals=0),
    )(*args)


def shaped(shape, dtype):
    return jax.ShapeDtypeStruct(shape, dtype)


def flip(array, axis, mask):
    return lax.ppermute(array, axis, [(i, i ^ mask) for i in range(lax.axis_size(axis))])


def from_each(array, axis):
    return lax.all_to_all(array, axis, 0, 0)


def merged(older, newer, size):
    older, newer = older.astype(f32), newer.astype(f32)
    decay = newer[size : size + 1]
    return jnp.concatenate([older[:size] * decay + newer[:size], older[size:] * decay], axis=0).astype(bf16)


def far_states(shard, size):
    rank = lax.axis_index("seq")
    levels = lax.axis_size("seq").bit_length() - 1
    states = []
    running = jnp.ones((1, shard.shape[1]), f32)
    for level in range(levels):
        theirs = flip(shard, "seq", 1 << level)
        upper = jnp.right_shift(rank, level) % 2 == 1
        states.append(jnp.where(upper, theirs[:size].astype(f32) * running, 0.0).astype(bf16))
        running = jnp.where(upper, running * theirs[size : size + 1].astype(f32), running)
        shard = merged(jnp.where(upper, theirs, shard), jnp.where(upper, shard, theirs), size)
    return states


def on_device(inputs, gate, input_map, output_map, step, decay_rate, level_mix, skip, norm_gain):
    tokens, width = inputs.shape
    heads = step.shape[0]
    parts = lax.axis_size("head")
    levels = lax.axis_size("seq").bit_length() - 1
    size = input_map.shape[0] * parts
    groups = tokens // GROUP
    spans = local_spans(groups)
    dense = 2 * tokens * GROUP * width
    area = tokens * width
    maps = jnp.concatenate([input_map, output_map], axis=0)
    maps = from_each(jnp.broadcast_to(maps[None], (parts, *maps.shape)), "head")
    maps = maps.reshape(-1, tokens)
    scaled, cum = call(
        prepare_kernel,
        (shaped((tokens, width), bf16), shaped((heads, tokens), f32)),
        (inputs, step, decay_rate[None, :]),
        flops=dense,
        bytes_accessed=4 * area,
        hbm=3,
    )
    shard_shape = shaped((size + DECAY_ROWS, width), bf16)
    span_shape = [shaped((len(spans) * size, width), bf16)] if spans else []
    shard, *span_states = call(
        functools.partial(states_kernel, parts),
        (shard_shape, *span_shape),
        (maps, scaled, cum),
        flops=dense,
        bytes_accessed=4 * area,
    )
    pairs = lax.axis_size("seq") == 8 and parts == 4
    if pairs:
        theirs = flip(shard, "seq", 1)
        message = call(
            functools.partial(merge_kernel, size),
            shaped((size + DECAY_ROWS, width // 2), bf16),
            (shard, theirs),
            bytes_accessed=area,
        )
    else:
        message = shard
    near, far = call(
        functools.partial(near_kernel, parts, spans, levels),
        (shaped((tokens, width), f32), shaped((levels, tokens, width), bf16)),
        (inputs, gate, level_mix, skip[None, :], maps, scaled, cum, message, *span_states),
        flops=8 * dense,
        bytes_accessed=16 * area,
        hbm=4,
    )
    gain = norm_gain[None, :]
    all_squares = shaped((parts, 1, tokens), f32)
    if pairs:
        own = [flip(message, "seq", mask) for mask in (2, 4, 6)]
        other = [flip(array, "seq", 1) for array in own]
        gated_shape = shaped((tokens, width // 2), f32)
        own_gated, own_squares = call(
            functools.partial(far_kernel_of_half, parts, True),
            (gated_shape, shaped((1, tokens), f32)),
            (maps, near, far, theirs, *own),
            flops=2 * dense,
            bytes_accessed=6 * area,
        )
        other_gated, squares = call(
            functools.partial(far_kernel_of_half, parts, False),
            (gated_shape, all_squares),
            (maps, near, far, theirs, *other, own_squares),
            flops=2 * dense,
            bytes_accessed=6 * area,
        )
        gated = (own_gated, other_gated)
    else:
        *gated, squares = call(
            functools.partial(far_kernel, parts),
            (shaped((tokens, width), f32), all_squares),
            (maps, near, far, *far_states(shard, size)),
            flops=4 * dense,
            bytes_accessed=12 * area,
        )
    return call(
        functools.partial(norm_kernel, width * parts),
        shaped((tokens, width), bf16),
        (from_each(squares, "head"), gain, *gated),
        flops=dense,
        bytes_accessed=6 * area,
    )


def solution(mesh):
    return jax.shard_map(
        on_device,
        mesh=mesh,
        in_specs=(
            P("seq", "head"),
            P("seq", "head"),
            P("head", "seq"),
            P("head", "seq"),
            P("head", "seq"),
            P("head"),
            P(None, "head", "seq"),
            P("head"),
            P("head"),
        ),
        out_specs=P("seq", "head"),
        check_vma=False,
    )
```

time: 55.2 us -> 44.9 us (0.81)
  starting transfers between devices: 23.7 us -> 10.4 us
  blocking collectives: 0 us -> 8.1 us
  local copies, waits for them, and re-layouts: 6.76 us -> 0.73 us
  waiting for transfers between devices: 12.2 us -> 15.3 us
  Pallas kernels: 10.5 us -> 9.16 us
    ppermute x16 -> x7, starting transfers between devices: 23.7 us -> 4.05 us  [flip(): lax.ppermute(array, axis, [(i, i ^ mask) for i in range(lax.axis_size(axi...]
    all_to_all x0 -> x1, blocking collectives: none -> 8.1 us  [from_each(): return lax.all_to_all(array, axis, 0, 0)]
    all_to_all x0 -> x1, waiting for transfers between devices: none -> 7.17 us  [from_each(): return lax.all_to_all(array, axis, 0, 0)]
    all_to_all x0 -> x1, starting transfers between devices: none -> 6.32 us  [from_each(): return lax.all_to_all(array, axis, 0, 0)]
    unnamed x28 -> x2, local copies, waits for them, and re-layouts: 5.93 us -> 0.01 us
    ppermute x16 -> x7, waiting for transfers between devices: 12.2 us -> 8.15 us  [flip(): lax.ppermute(array, axis, [(i, i ^ mask) for i in range(lax.axis_size(axi...]
    pallas_call x5 -> x7, Pallas kernels: 10.5 us -> 9.16 us  [call(): pl.pallas_call(kernel, out_shape=out_shape, in_specs=specs, out_specs=jax...]
    convert_element_type x1 -> x0, other arithmetic: 1.04 us -> none  [merged(): older, newer = (older.astype(f32), newer.astype(f32))]
  transfers between devices with their start and end apart: 16 -> 8, of which waited for: 9 -> 5; matrix products, arithmetic and copies ran while one was open for 2% -> 0% of each run, Pallas kernels for 7% -> 14%
where the time goes in v2:
time: 44.9 us; the launch traced here: 44.5 us
  waiting for transfers between devices  15.3 us (34%)
  starting transfers between devices  10.4 us (23%)
  Pallas kernels  9.16 us (20%)
  blocking collectives  8.1 us (18%)
  other arithmetic  0.78 us (2%)
  local copies, waits for them, and re-layouts  0.73 us (2%)
    pallas_call x7, Pallas kernels, call(): pl.pallas_call(kernel, out_shape=out_shape, in_specs=specs, out_specs=jax...  9.16 us
    ppermute x7, waiting for transfers between devices, flip(): lax.ppermute(array, axis, [(i, i ^ mask) for i in range(lax.axis_size(axi...  8.15 us
    all_to_all x1, blocking collectives, from_each(): return lax.all_to_all(array, axis, 0, 0)  8.1 us
    all_to_all x1, waiting for transfers between devices, from_each(): return lax.all_to_all(array, axis, 0, 0)  7.17 us
    all_to_all x1, starting transfers between devices, from_each(): return lax.all_to_all(array, axis, 0, 0)  6.32 us
    ppermute x7, starting transfers between devices, flip(): lax.ppermute(array, axis, [(i, i ^ mask) for i in range(lax.axis_size(axi...  4.05 us
  transfers between devices with their start and end apart: 8, of which 5 were waited for; matrix products, arithmetic and copies ran while one was open for 0% of the time, Pallas kernels for 14%

profile of v2, /device:TPU:0, one launch (start us, length us, event | category | flops | bytes accessed | tf_op | source)
XLA Modules:
  0.0 44.5 jit_solution(10149632350595693550)
XLA Ops:
  0.0 0.8 %pad_maximum_fusion = bf16[64,512]{1,0:T(8,128)(2,1)S(1)} fusion(bf16[32,512]{1,0:T(8,128)(2,1)} %param.12, bf16[32,512]{1,0:T(8,128)(2,1)} %param.11), kind=kLoop, calls=%fused_computation | loop fusion | flops 131072 | bytes 131072 | tf_op jit(solution)/shard_map/concatenate | solution.py:347
  0.8 0.7 %broadcast_in_dim.15 = bf16[4,64,512]{2,1,0:T(8,128)(2,1)} broadcast(bf16[64,512]{1,0:T(8,128)(2,1)S(1)} %pad_maximum_fusion), dimensions={1,2} | broadcast | bytes 327680 | tf_op jit(solution)/shard_map/broadcast_in_dim | solution.py:348
  1.5 6.3 %all-to-all-start = ((bf16[4,64,512]{2,1,0:T(8,128)(2,1)}), bf16[4,64,512]{2,1,0:T(8,128)(2,1)S(1)}, u32[]{:S(2)}, u32[]{:S(2)}) async-start(bf16[4,64,512]{2,1,0:T(8,128)(2,1)} %broadcast_in_dim.15), calls=%async_computation | async-start | bytes 524288 | tf_op jit(solution)/shard_map/all_to_all | solution.py:314
  7.8 1.7 %shard_map.91 = (bf16[512,1024]{1,0:T(8,128)(2,1)S(1)}, f32[16,512]{1,0:T(8,128)S(1)}) custom-call(bf16[512,1024]{1,0:T(8,128)(2,1)} %refs_0_.1, f32[16,512]{1,0:T(8,128)} %step_hbm.1, f32[1,16]{1,0:T(1,128)} %bitcast.9), custom_call_target="tpu_custom_call" | custom-call | flops 268435456 | bytes 2097152 | tf_op jit(solution)/shard_map/pallas_call | solution.py:294
  9.6 7.2 %all-to-all-done = bf16[4,64,512]{2,1,0:T(8,128)(2,1)S(1)} async-done(((bf16[4,64,512]{2,1,0:T(8,128)(2,1)}), bf16[4,64,512]{2,1,0:T(8,128)(2,1)S(1)}, u32[]{:S(2)}, u32[]{:S(2)}) %all-to-all-start) | async-done | bytes 262176 | tf_op jit(solution)/shard_map/all_to_all | solution.py:314
  16.7 0.3 shard_map.92
  17.1 0.1 collective-permute-start
  17.1 1.6 %collective-permute-done.theirs_ref.refs_3_ = bf16[144,1024]{1,0:T(8,128)(2,1)S(1)} collective-permute-done((bf16[144,1024]{1,0:T(8,128)(2,1)S(1)}, bf16[144,1024]{1,0:T(8,128)(2,1)S(1)}, u32[]{:S(2)}, u32[]{:S(2)}) %collective-permute-start) | collective-permute-done | bytes 294944 | tf_op jit(solution)/shard_map/ppermute | solution.py:310
  18.7 0.1 shard_map.93.refs_7_
  18.8 2.5 %collective-permute-start.5 = (bf16[144,512]{1,0:T(8,128)(2,1)S(1)}, bf16[144,512]{1,0:T(8,128)(2,1)S(1)}, u32[]{:S(2)}, u32[]{:S(2)}) collective-permute-start(bf16[144,512]{1,0:T(8,128)(2,1)S(1)} %shard_map.93.refs_7_), channel_id=1, source_target_pairs={{0,24},{4,28},{8,16},{12,20},{16,8},{20,12},{24,0},{28,4},{1,25},{... | collective-permute-start | bytes 442376 | tf_op jit(solution)/shard_map/ppermute | solution.py:310
  21.3 0.5 %collective-permute-start.3 = (bf16[144,512]{1,0:T(8,128)(2,1)S(1)}, bf16[144,512]{1,0:T(8,128)(2,1)S(1)}, u32[]{:S(2)}, u32[]{:S(2)}) collective-permute-start(bf16[144,512]{1,0:T(8,128)(2,1)S(1)} %shard_map.93.refs_7_), channel_id=1, source_target_pairs={{0,16},{4,20},{8,24},{12,28},{16,0},{20,4},{24,8},{28,12},{1,17},{... | collective-permute-start | bytes 442376 | tf_op jit(solution)/shard_map/ppermute | solution.py:310
  21.8 0.5 %collective-permute-start.1 = (bf16[144,512]{1,0:T(8,128)(2,1)S(1)}, bf16[144,512]{1,0:T(8,128)(2,1)S(1)}, u32[]{:S(2)}, u32[]{:S(2)}) collective-permute-start(bf16[144,512]{1,0:T(8,128)(2,1)S(1)} %shard_map.93.refs_7_), channel_id=1, source_target_pairs={{0,8},{4,12},{8,0},{12,4},{16,24},{20,28},{24,16},{28,20},{1,9},{5... | collective-permute-start | bytes 442376 | tf_op jit(solution)/shard_map/ppermute | solution.py:310
  22.3 3.9 %collective-permute-done.5.refs_6_ = bf16[144,512]{1,0:T(8,128)(2,1)S(1)} collective-permute-done((bf16[144,512]{1,0:T(8,128)(2,1)S(1)}, bf16[144,512]{1,0:T(8,128)(2,1)S(1)}, u32[]{:S(2)}, u32[]{:S(2)}) %collective-permute-start.5) | collective-permute-done | bytes 147488 | tf_op jit(solution)/shard_map/ppermute | solution.py:310
  26.3 0.0 collective-permute-start.6
  26.3 2.5 %collective-permute-done.3.refs_5_ = bf16[144,512]{1,0:T(8,128)(2,1)S(1)} collective-permute-done((bf16[144,512]{1,0:T(8,128)(2,1)S(1)}, bf16[144,512]{1,0:T(8,128)(2,1)S(1)}, u32[]{:S(2)}, u32[]{:S(2)}) %collective-permute-start.3) | collective-permute-done | bytes 147488 | tf_op jit(solution)/shard_map/ppermute | solution.py:310
  28.8 0.0 collective-permute-start.4
  28.8 0.1 collective-permute-done.1.refs_4_
  28.9 0.4 collective-permute-start.2
  29.3 3.7 %shard_map.94 = (f32[512,1024]{1,0:T(8,128)S(1)}, bf16[3,512,1024]{2,1,0:T(8,128)(2,1)S(1)}) custom-call(bf16[512,1024]{1,0:T(8,128)(2,1)} %refs_0_.1, bf16[512,1024]{1,0:T(8,128)(2,1)} %refs_1_.1, f32[9,16,512]{2,1,0:T(8,128)} %refs_2_.1, f32[1,16]{1,0:T(1,128)} %bitcast.10, bf16[256,512]{1,0:T(8,128)(2,1)S(1)} %bitcast.5, ...), custom_call_target="tpu_custom_call" | custom-call | flops 2147483648 | bytes 8388608 | tf_op jit(solution)/shard_map/pallas_call | solution.py:294
  33.0 1.0 %shard_map.95 = (f32[512,512]{1,0:T(8,128)S(1)}, f32[1,512]{1,0:T(1,128)S(1)}) custom-call(bf16[256,512]{1,0:T(8,128)(2,1)S(1)} %bitcast.6, f32[512,1024]{1,0:T(8,128)S(1)} %get-tuple-element.19.refs_1_, bf16[3,512,1024]{2,1,0:T(8,128)(2,1)S(1)} %get-tuple-element.20.refs_2_, bf16[144,1024]{1,0:T(8,128)(2,1)S(1)} %collective-permute-done.theirs_ref.refs_3_, ...), custom_call_target="tpu_custom_call" | custom-call | flops 536870912 | bytes 3145728 | tf_op jit(solution)/shard_map/pallas_call | solution.py:294
  34.0 0.0 copy-start
  34.0 0.0 collective-permute-done.6.refs_6_
  34.0 0.0 collective-permute-done.4.refs_5_
  34.0 0.0 collective-permute-done.2.refs_4_
  34.0 1.0 %shard_map.96 = (f32[512,512]{1,0:T(8,128)S(1)}, f32[4,1,512]{2,1,0:T(1,128)S(1)}) custom-call(bf16[256,512]{1,0:T(8,128)(2,1)S(1)} %bitcast.7, f32[512,1024]{1,0:T(8,128)S(1)} %get-tuple-element.19.refs_1_, bf16[3,512,1024]{2,1,0:T(8,128)(2,1)S(1)} %get-tuple-element.20.refs_2_, bf16[144,1024]{1,0:T(8,128)(2,1)S(1)} %collective-permute-done.theirs_ref.refs_3_, ...), custom_call_target="tpu_custom_call" | custom-call | flops 536870912 | bytes 3145728 | tf_op jit(solution)/shard_map/pallas_call | solution.py:294
  35.1 8.1 %all_to_all.10.squares_ref = f32[4,1,512]{2,1,0:T(1,128)S(1)} all-to-all(f32[4,1,512]{2,1,0:T(1,128)S(1)} %get-tuple-element.22), channel_id=1, replica_groups=mesh['seq'=8,'head'=4] {'head'}, dimensions={0} | all-to-all | bytes 16384 | tf_op jit(solution)/shard_map/all_to_all | solution.py:314
  43.2 0.0 copy-done
  43.2 1.3 %shard_map.97 = bf16[512,1024]{1,0:T(8,128)(2,1)} custom-call(f32[4,1,512]{2,1,0:T(1,128)S(1)} %all_to_all.10.squares_ref, f32[1,1024]{1,0:T(1,128)S(1)} %bitcast.8, f32[512,512]{1,0:T(8,128)S(1)} %get-tuple-element.23.refs_0_, f32[512,512]{1,0:T(8,128)S(1)} %get-tuple-element.24.refs_1_), custom_call_target="tpu_custom_call" | custom-call | flops 268435456 | bytes 3145728 | tf_op jit(solution)/shard_map/pallas_call | solution.py:294
Async XLA Ops:
  1.5 15.2 %all-to-all-start = ((bf16[4,64,512]{2,1,0:T(8,128)(2,1)}), bf16[4,64,512]{2,1,0:T(8,128)(2,1)S(1)}, u32[]{:S(2)}, u32[]{:S(2)}) async-start(bf16[4,64,512]{2,1,0:T(8,128)(2,1)} %broadcast_in_dim.15), calls=%async_computation | async-start | bytes 524288 | tf_op jit(solution)/shard_map/all_to_all | solution.py:314
  17.1 1.6 %collective-permute-start = (bf16[144,1024]{1,0:T(8,128)(2,1)S(1)}, bf16[144,1024]{1,0:T(8,128)(2,1)S(1)}, u32[]{:S(2)}, u32[]{:S(2)}) collective-permute-start(bf16[144,1024]{1,0:T(8,128)(2,1)S(1)} %get-tuple-element.17.mine_ref), channel_id=1, source_target_pairs={{0,4},{4,0},{8,12},{12,8},{16,20},{20,16},{24,28},{28,24},{1,5},{5... | collective-permute-start | bytes 884744 | tf_op jit(solution)/shard_map/ppermute | solution.py:310
  18.8 7.5 %collective-permute-start.5 = (bf16[144,512]{1,0:T(8,128)(2,1)S(1)}, bf16[144,512]{1,0:T(8,128)(2,1)S(1)}, u32[]{:S(2)}, u32[]{:S(2)}) collective-permute-start(bf16[144,512]{1,0:T(8,128)(2,1)S(1)} %shard_map.93.refs_7_), channel_id=1, source_target_pairs={{0,24},{4,28},{8,16},{12,20},{16,8},{20,12},{24,0},{28,4},{1,25},{... | collective-permute-start | bytes 442376 | tf_op jit(solution)/shard_map/ppermute | solution.py:310
  21.3 7.5 %collective-permute-start.3 = (bf16[144,512]{1,0:T(8,128)(2,1)S(1)}, bf16[144,512]{1,0:T(8,128)(2,1)S(1)}, u32[]{:S(2)}, u32[]{:S(2)}) collective-permute-start(bf16[144,512]{1,0:T(8,128)(2,1)S(1)} %shard_map.93.refs_7_), channel_id=1, source_target_pairs={{0,16},{4,20},{8,24},{12,28},{16,0},{20,4},{24,8},{28,12},{1,17},{... | collective-permute-start | bytes 442376 | tf_op jit(solution)/shard_map/ppermute | solution.py:310
  21.8 7.1 %collective-permute-start.1 = (bf16[144,512]{1,0:T(8,128)(2,1)S(1)}, bf16[144,512]{1,0:T(8,128)(2,1)S(1)}, u32[]{:S(2)}, u32[]{:S(2)}) collective-permute-start(bf16[144,512]{1,0:T(8,128)(2,1)S(1)} %shard_map.93.refs_7_), channel_id=1, source_target_pairs={{0,8},{4,12},{8,0},{12,4},{16,24},{20,28},{24,16},{28,20},{1,9},{5... | collective-permute-start | bytes 442376 | tf_op jit(solution)/shard_map/ppermute | solution.py:310
  26.3 7.7 %collective-permute-start.6 = (bf16[144,512]{1,0:T(8,128)(2,1)S(1)}, bf16[144,512]{1,0:T(8,128)(2,1)S(1)}, u32[]{:S(2)}, u32[]{:S(2)}) collective-permute-start(bf16[144,512]{1,0:T(8,128)(2,1)S(1)} %collective-permute-done.5.refs_6_), channel_id=1, source_target_pairs={{0,4},{4,0},{8,12},{12,8},{16,20},{20,16},{24,28},{28,24},{1,5},{5... | collective-permute-start | bytes 442376 | tf_op jit(solution)/shard_map/ppermute | solution.py:310
  28.8 5.2 %collective-permute-start.4 = (bf16[144,512]{1,0:T(8,128)(2,1)S(1)}, bf16[144,512]{1,0:T(8,128)(2,1)S(1)}, u32[]{:S(2)}, u32[]{:S(2)}) collective-permute-start(bf16[144,512]{1,0:T(8,128)(2,1)S(1)} %collective-permute-done.3.refs_5_), channel_id=1, source_target_pairs={{0,4},{4,0},{8,12},{12,8},{16,20},{20,16},{24,28},{28,24},{1,5},{5... | collective-permute-start | bytes 442376 | tf_op jit(solution)/shard_map/ppermute | solution.py:310
  28.9 5.1 %collective-permute-start.2 = (bf16[144,512]{1,0:T(8,128)(2,1)S(1)}, bf16[144,512]{1,0:T(8,128)(2,1)S(1)}, u32[]{:S(2)}, u32[]{:S(2)}) collective-permute-start(bf16[144,512]{1,0:T(8,128)(2,1)S(1)} %collective-permute-done.1.refs_4_), channel_id=1, source_target_pairs={{0,4},{4,0},{8,12},{12,8},{16,20},{20,16},{24,28},{28,24},{1,5},{5... | collective-permute-start | bytes 442376 | tf_op jit(solution)/shard_map/ppermute | solution.py:310
  34.0 9.2 %copy-start = (f32[1024]{0:T(1024)S(1)}, f32[1024]{0:T(1024)}, u32[]{:S(2)}) copy-start(f32[1024]{0:T(1024)} %param.17) | copy-start | bytes 12292

commit v3 on v2

--- a/solution.py
+++ b/solution.py
@@ -11,6 +11,7 @@
 GROUP = 256
 DECAY_ROWS = 16
 BLOCK = 256
+NORM_CHUNKS = 4
 VMEM_LIMIT = 40 * 1024 * 1024
 
 f32, bf16 = jnp.float32, jnp.bfloat16
@@ -61,10 +62,12 @@
     return jnp.sum(jnp.where(at, row, 0.0), axis=1, keepdims=True)
 
 
-def map_rows(maps_ref, parts, which):
-    rows = maps_ref.shape[0] // (2 * parts)
-    maps = maps_ref[...] if rows % 16 == 0 else maps_ref[...].astype(f32)
-    picked = [maps[(2 * part + which) * rows : (2 * part + which + 1) * rows] for part in range(parts)]
+def map_rows(map_refs, which):
+    rows = map_refs[0].shape[0] // 2
+    picked = []
+    for ref in map_refs:
+        maps = ref[...] if rows % 16 == 0 else ref[...].astype(f32)
+        picked.append(maps[which * rows : (which + 1) * rows])
     return jnp.concatenate(picked, axis=0).astype(bf16)
 
 
@@ -103,11 +106,18 @@
         scaled_ref[:, cols] = (inputs_ref[:, cols].astype(f32) * scale).astype(bf16)
 
 
-def states_kernel(parts, maps_ref, scaled_ref, cum_ref, *out_refs):
+def pack_kernel(in_hbm, out_hbm, maps_ref, semaphores):
+    rows = in_hbm.shape[0]
+    for copy in fetch((in_hbm, out_hbm), (maps_ref.at[:rows], maps_ref.at[rows:]), semaphores):
+        copy.wait()
+
+
+def states_kernel(parts, *refs):
+    map_refs, (scaled_ref, cum_ref), out_refs = refs[:parts], refs[parts : parts + 2], refs[parts + 2 :]
     shard_ref = out_refs[0]
     heads, tokens = cum_ref.shape
     width = scaled_ref.shape[1]
-    in_map = map_rows(maps_ref, parts, 0)
+    in_map = map_rows(map_refs, 0)
     size = in_map.shape[0]
     cum = cum_ref[...]
     states, decays = [], []
@@ -146,17 +156,18 @@
 
 def near_kernel(parts, spans, levels, *refs):
     inputs_hbm, gate_hbm, mix_hbm, skip_hbm = refs[:4]
-    maps_ref, scaled_ref, cum_ref, _ = refs[4:8]
-    count = 1 if spans else 0
-    span_refs = refs[8 : 8 + count]
-    near_ref, far_ref, inputs_ref, gate_ref, mix_ref, skip_ref, semaphores = refs[8 + count :]
+    scaled_ref, cum_ref, _ = refs[4:7]
+    map_refs = refs[7 : 7 + parts]
+    count = 7 + parts + (1 if spans else 0)
+    span_refs = refs[7 + parts : count]
+    near_ref, far_ref, inputs_ref, gate_ref, mix_ref, skip_ref, semaphores = refs[count:]
     copies = fetch(refs[:4], (inputs_ref, gate_ref, mix_ref, skip_ref), semaphores)
     heads, tokens = cum_ref.shape
     width = scaled_ref.shape[1]
     groups = tokens // GROUP
     first = groups.bit_length()
-    in_map = map_rows(maps_ref, parts, 0)
-    out_map = map_rows(maps_ref, parts, 1)
+    in_map = map_rows(map_refs, 0)
+    out_map = map_rows(map_refs, 1)
     size = in_map.shape[0]
     expand = expander(heads, width, 2).astype(bf16)
     row = lax.broadcasted_iota(jnp.int32, (GROUP, GROUP), 0)
@@ -217,23 +228,23 @@
     return sums[:1]
 
 
-def far_kernel(parts, maps_ref, near_ref, far_ref, *refs):
-    state_refs = refs[:-2]
+def far_kernel(parts, *refs):
+    map_refs, (near_ref, far_ref) = refs[:parts], refs[parts : parts + 2]
+    state_refs = refs[parts + 2 : -2]
     gated_ref, squares_ref = refs[-2:]
 
     def state_of(level, cols, _):
         return state_refs[level][:, cols]
 
-    out_map = map_rows(maps_ref, parts, 1)
-    sums = far_body(out_map, near_ref, far_ref, 0, near_ref.shape[1], state_of, gated_ref)
-    for part in range(parts):
-        squares_ref[part] = sums
+    out_map = map_rows(map_refs, 1)
+    squares_ref[...] = far_body(out_map, near_ref, far_ref, 0, near_ref.shape[1], state_of, gated_ref)
 
 
 def far_kernel_of_half(parts, own, *refs):
-    maps_ref, near_ref, far_ref, core_ref, x_ref, y_ref, diagonal_ref = refs[:7]
+    map_refs = refs[:parts]
+    near_ref, far_ref, core_ref, x_ref, y_ref, diagonal_ref = refs[parts : parts + 6]
     gated_ref, squares_ref = refs[-2:]
-    out_map = map_rows(maps_ref, parts, 1)
+    out_map = map_rows(map_refs, 1)
     size = out_map.shape[0]
     rank = lax.axis_index("seq")
     core = lax.rem(rank, 2)
@@ -264,39 +275,46 @@
         return (older * newer_decay + newer) * running
 
     sums = far_body(out_map, near_ref, far_ref, start, half, state_of, gated_ref)
-    if own:
-        squares_ref[...] = sums
-    else:
-        sums = sums + refs[7][...]
-        for part in range(parts):
-            squares_ref[part] = sums
-
-
-def norm_kernel(columns, squares_ref, gain_ref, *refs):
-    gated_refs, out_ref = refs[:-1], refs[-1]
-    total = jnp.sum(squares_ref[...], axis=0)
+    squares_ref[...] = sums if own else sums + refs[parts + 6][...]
+
+
+def norm_kernel(parts, columns, *refs):
+    gain_ref = refs[parts]
+    gated_refs, (out_hbm, out_ref, semaphores) = refs[parts + 1 : -3], refs[-3:]
+    total = refs[0][...]
+    for ref in refs[1:parts]:
+        total = total + ref[...]
     scale = lax.rsqrt(total / columns + 1e-05)
     scale = jnp.transpose(jnp.broadcast_to(scale, (8, scale.shape[1])))[:, :1]
-    if len(gated_refs) == 1:
-        out_ref[...] = (gated_refs[0][...] * scale * gain_ref[...]).astype(bf16)
-        return
-    half = gated_refs[0].shape[1]
+    tokens = scale.shape[0]
+    width = gated_refs[0].shape[1]
     core = lax.rem(lax.axis_index("seq"), 2)
-    for ref, side in zip(gated_refs, (core, 1 - core)):
-        at = pl.ds(pl.multiple_of(side * half, half), half)
-        out_ref[:, at] = (ref[...] * scale * gain_ref[:, at]).astype(bf16)
-
-
-def call(kernel, out_shape, args, flops=0, bytes_accessed=0, hbm=0, fetched=()):
+    sides = (core, 1 - core) if len(gated_refs) == 2 else (0,)
+    chunk = tokens // NORM_CHUNKS
+    copies = []
+    for index in range(NORM_CHUNKS):
+        rows = slice(index * chunk, (index + 1) * chunk)
+        for ref, side in zip(gated_refs, sides):
+            at = pl.ds(pl.multiple_of(side * width, width), width)
+            out_ref[rows, at] = (ref[rows, :] * scale[rows] * gain_ref[:, at]).astype(bf16)
+        copies.append(pltpu.make_async_copy(out_ref.at[rows], out_hbm.at[rows], semaphores.at[index]))
+        copies[-1].start()
+    for copy in copies:
+        copy.wait()
+
+
+def call(kernel, out_shape, args, flops=0, bytes_accessed=0, hbm=0, scratch=None, out_space=pltpu.VMEM):
     specs = [pl.BlockSpec(memory_space=pl.ANY)] * hbm + [pl.BlockSpec(memory_space=pltpu.VMEM)] * (len(args) - hbm)
     args = [pltpu.with_memory_space_constraint(arg, pltpu.HBM) for arg in args[:hbm]] + list(args[hbm:])
-    scratch = [pltpu.VMEM(arg.shape, arg.dtype) for arg in args[:hbm]]
+    if scratch is None:
+        scratch = [pltpu.VMEM(arg.shape, arg.dtype) for arg in args[:hbm]]
+        scratch += [pltpu.SemaphoreType.DMA((hbm,))] if hbm else []
     return pl.pallas_call(
         kernel,
         out_shape=out_shape,
         in_specs=specs,
-        out_specs=jax.tree.map(lambda _: pl.BlockSpec(memory_space=pltpu.VMEM), out_shape),
-        scratch_shapes=scratch + ([pltpu.SemaphoreType.DMA((hbm,))] if hbm else []),
+        out_specs=jax.tree.map(lambda _: pl.BlockSpec(memory_space=out_space), out_shape),
+        scratch_shapes=scratch,
         compiler_params=pltpu.CompilerParams(vmem_limit_bytes=VMEM_LIMIT),
         cost_estimate=pl.CostEstimate(flops=flops, bytes_accessed=bytes_accessed, transcendentals=0),
     )(*args)
@@ -311,7 +329,7 @@
 
 
 def from_each(array, axis):
-    return lax.all_to_all(array, axis, 0, 0)
+    return [array] + [flip(array, axis, mask) for mask in range(1, lax.axis_size(axis))]
 
 
 def merged(older, newer, size):
@@ -344,9 +362,19 @@
     spans = local_spans(groups)
     dense = 2 * tokens * GROUP * width
     area = tokens * width
-    maps = jnp.concatenate([input_map, output_map], axis=0)
-    maps = from_each(jnp.broadcast_to(maps[None], (parts, *maps.shape)), "head")
-    maps = maps.reshape(-1, tokens)
+    rows = input_map.shape[0]
+    if rows % 16 == 0:
+        maps = call(
+            pack_kernel,
+            shaped((2 * rows, tokens), bf16),
+            (input_map, output_map),
+            bytes_accessed=4 * rows * tokens,
+            hbm=2,
+            scratch=[pltpu.SemaphoreType.DMA((2,))],
+        )
+    else:
+        maps = jnp.concatenate([input_map, output_map], axis=0)
+    maps = from_each(maps, "head")
     scaled, cum = call(
         prepare_kernel,
         (shaped((tokens, width), bf16), shaped((heads, tokens), f32)),
@@ -360,7 +388,7 @@
     shard, *span_states = call(
         functools.partial(states_kernel, parts),
         (shard_shape, *span_shape),
-        (maps, scaled, cum),
+        (*maps, scaled, cum),
         flops=dense,
         bytes_accessed=4 * area,
     )
@@ -378,28 +406,29 @@
     near, far = call(
         functools.partial(near_kernel, parts, spans, levels),
         (shaped((tokens, width), f32), shaped((levels, tokens, width), bf16)),
-        (inputs, gate, level_mix, skip[None, :], maps, scaled, cum, message, *span_states),
+        (inputs, gate, level_mix, skip[None, :], scaled, cum, message, *maps, *span_states),
         flops=8 * dense,
         bytes_accessed=16 * area,
         hbm=4,
     )
     gain = norm_gain[None, :]
-    all_squares = shaped((parts, 1, tokens), f32)
+    sums_shape = shaped((1, tokens), f32)
     if pairs:
         own = [flip(message, "seq", mask) for mask in (2, 4, 6)]
+        *own, near, far = lax.optimization_barrier((*own, near, far))
         other = [flip(array, "seq", 1) for array in own]
         gated_shape = shaped((tokens, width // 2), f32)
         own_gated, own_squares = call(
             functools.partial(far_kernel_of_half, parts, True),
-            (gated_shape, shaped((1, tokens), f32)),
-            (maps, near, far, theirs, *own),
+            (gated_shape, sums_shape),
+            (*maps, near, far, theirs, *own),
             flops=2 * dense,
             bytes_accessed=6 * area,
         )
         other_gated, squares = call(
             functools.partial(far_kernel_of_half, parts, False),
-            (gated_shape, all_squares),
-            (maps, near, far, theirs, *other, own_squares),
+            (gated_shape, sums_shape),
+            (*maps, near, far, theirs, *other, own_squares),
             flops=2 * dense,
             bytes_accessed=6 * area,
         )
@@ -407,17 +436,19 @@
     else:
         *gated, squares = call(
             functools.partial(far_kernel, parts),
-            (shaped((tokens, width), f32), all_squares),
-            (maps, near, far, *far_states(shard, size)),
+            (shaped((tokens, width), f32), sums_shape),
+            (*maps, near, far, *far_states(shard, size)),
             flops=4 * dense,
             bytes_accessed=12 * area,
         )
     return call(
-        functools.partial(norm_kernel, width * parts),
+        functools.partial(norm_kernel, parts, width * parts),
         shaped((tokens, width), bf16),
-        (from_each(squares, "head"), gain, *gated),
+        (*from_each(squares, "head"), gain, *gated),
         flops=dense,
         bytes_accessed=6 * area,
+        scratch=[pltpu.VMEM((tokens, width), bf16), pltpu.SemaphoreType.DMA((NORM_CHUNKS,))],
+        out_space=pl.ANY,
     )
 
 

time: 44.9 us -> 35.3 us (0.79)
  blocking collectives: 8.1 us -> 0 us
  waiting for transfers between devices: 15.3 us -> 10.8 us
  starting transfers between devices: 10.4 us -> 14.3 us
  other arithmetic: 0.78 us -> 0 us
  local copies, waits for them, and re-layouts: 0.73 us -> 0.01 us
  Pallas kernels: 9.16 us -> 9.84 us
    ppermute x7 -> x13, starting transfers between devices: 4.05 us -> 14.3 us  [flip(): lax.ppermute(array, axis, [(i, i ^ mask) for i in range(lax.axis_size(axi...]
    all_to_all x1 -> x0, blocking collectives: 8.1 us -> none  [from_each(): return lax.all_to_all(array, axis, 0, 0)]
    all_to_all x1 -> x0, waiting for transfers between devices: 7.17 us -> none  [from_each(): return lax.all_to_all(array, axis, 0, 0)]
    all_to_all x1 -> x0, starting transfers between devices: 6.32 us -> none  [from_each(): return lax.all_to_all(array, axis, 0, 0)]
    ppermute x7 -> x13, waiting for transfers between devices: 8.15 us -> 10.8 us  [flip(): lax.ppermute(array, axis, [(i, i ^ mask) for i in range(lax.axis_size(axi...]
    concatenate x1 -> x0, other arithmetic: 0.78 us -> none  [on_device(): maps = jnp.concatenate([input_map, output_map], axis=0)]
    broadcast_in_dim x1 -> x0, local copies, waits for them, and re-layouts: 0.72 us -> none  [on_device(): maps = from_each(jnp.broadcast_to(maps[None], (parts, *maps.shape)), 'head')]
    pallas_call x7 -> x8, Pallas kernels: 9.16 us -> 9.84 us  [call(): pl.pallas_call(kernel, out_shape=out_shape, in_specs=specs, out_specs=jax...]
  transfers between devices with their start and end apart: 8 -> 13, of which waited for: 5 -> 10; matrix products, arithmetic and copies ran while one was open for 0% -> 0% of each run, Pallas kernels for 14% -> 18%
where the time goes in v3:
time: 35.3 us; the launch traced here: 35 us
  starting transfers between devices  14.3 us (41%)
  waiting for transfers between devices  10.8 us (31%)
  Pallas kernels  9.84 us (28%)
    ppermute x13, starting transfers between devices, flip(): lax.ppermute(array, axis, [(i, i ^ mask) for i in range(lax.axis_size(axi...  14.3 us
    ppermute x13, waiting for transfers between devices, flip(): lax.ppermute(array, axis, [(i, i ^ mask) for i in range(lax.axis_size(axi...  10.8 us
    pallas_call x8, Pallas kernels, call(): pl.pallas_call(kernel, out_shape=out_shape, in_specs=specs, out_specs=jax...  9.84 us
  transfers between devices with their start and end apart: 13, of which 10 were waited for; matrix products, arithmetic and copies ran while one was open for 0% of the time, Pallas kernels for 18%

profile of v3, /device:TPU:0, one launch (start us, length us, event | category | flops | bytes accessed | tf_op | source)
XLA Modules:
  0.0 35.0 jit_solution(11036208082812301258)
XLA Ops:
  0.0 0.8 %shard_map.91.refs_0_.refs_7_ = bf16[64,512]{1,0:T(8,128)(2,1)S(1)} custom-call(bf16[32,512]{1,0:T(8,128)(2,1)} %in_hbm.1, bf16[32,512]{1,0:T(8,128)(2,1)} %out_hbm.1), custom_call_target="tpu_custom_call" | custom-call | bytes 65536 | tf_op jit(solution)/shard_map/pallas_call | solution.py:312
  0.8 5.1 %collective-permute-start.2 = (bf16[64,512]{1,0:T(8,128)(2,1)S(1)}, bf16[64,512]{1,0:T(8,128)(2,1)S(1)}, u32[]{:S(2)}, u32[]{:S(2)}) collective-permute-start(bf16[64,512]{1,0:T(8,128)(2,1)S(1)} %shard_map.91.refs_0_.refs_7_), channel_id=1, source_target_pairs={{0,3},{1,2},{2,1},{3,0},{4,7},{5,6},{6,5},{7,4},{8,11},{9,10},{10,... | collective-permute-start | bytes 196616 | tf_op jit(solution)/shard_map/ppermute | solution.py:328
  5.9 0.0 collective-permute-start.1
  5.9 0.6 %collective-permute-start = (bf16[64,512]{1,0:T(8,128)(2,1)S(1)}, bf16[64,512]{1,0:T(8,128)(2,1)S(1)}, u32[]{:S(2)}, u32[]{:S(2)}) collective-permute-start(bf16[64,512]{1,0:T(8,128)(2,1)S(1)} %shard_map.91.refs_0_.refs_7_), channel_id=1, source_target_pairs={{0,1},{1,0},{2,3},{3,2},{4,5},{5,4},{6,7},{7,6},{8,9},{9,8},{10,11... | collective-permute-start | bytes 196616 | tf_op jit(solution)/shard_map/ppermute | solution.py:328
  6.6 1.7 %shard_map.92 = (bf16[512,1024]{1,0:T(8,128)(2,1)S(1)}, f32[16,512]{1,0:T(8,128)S(1)}) custom-call(bf16[512,1024]{1,0:T(8,128)(2,1)} %refs_0_.1, f32[16,512]{1,0:T(8,128)} %step_hbm.1, f32[1,16]{1,0:T(1,128)} %bitcast.4), custom_call_target="tpu_custom_call" | custom-call | flops 268435456 | bytes 2097152 | tf_op jit(solution)/shard_map/pallas_call | solution.py:312
  8.3 0.2 collective-permute-done.2.refs_3_.refs_10_
  8.5 3.0 %collective-permute-done.1.refs_2_.refs_9_ = bf16[64,512]{1,0:T(8,128)(2,1)S(1)} collective-permute-done((bf16[64,512]{1,0:T(8,128)(2,1)S(1)}, bf16[64,512]{1,0:T(8,128)(2,1)S(1)}, u32[]{:S(2)}, u32[]{:S(2)}) %collective-permute-start.1) | collective-permute-done | bytes 65568 | tf_op jit(solution)/shard_map/ppermute | solution.py:328
  11.5 0.0 collective-permute-done.refs_1_.refs_8_
  11.5 0.3 shard_map.93
  11.8 0.1 collective-permute-start.3
  11.9 1.6 %collective-permute-done.3.theirs_ref.refs_6_ = bf16[144,1024]{1,0:T(8,128)(2,1)S(1)} collective-permute-done((bf16[144,1024]{1,0:T(8,128)(2,1)S(1)}, bf16[144,1024]{1,0:T(8,128)(2,1)S(1)}, u32[]{:S(2)}, u32[]{:S(2)}) %collective-permute-start.3) | collective-permute-done | bytes 294944 | tf_op jit(solution)/shard_map/ppermute | solution.py:328
  13.5 0.1 shard_map.94.refs_6_
  13.6 2.5 %collective-permute-start.6 = (bf16[144,512]{1,0:T(8,128)(2,1)S(1)}, bf16[144,512]{1,0:T(8,128)(2,1)S(1)}, u32[]{:S(2)}, u32[]{:S(2)}) collective-permute-start(bf16[144,512]{1,0:T(8,128)(2,1)S(1)} %shard_map.94.refs_6_), channel_id=1, source_target_pairs={{0,24},{4,28},{8,16},{12,20},{16,8},{20,12},{24,0},{28,4},{1,25},{... | collective-permute-start | bytes 442376 | tf_op jit(solution)/shard_map/ppermute | solution.py:328
  16.1 0.5 %collective-permute-start.5 = (bf16[144,512]{1,0:T(8,128)(2,1)S(1)}, bf16[144,512]{1,0:T(8,128)(2,1)S(1)}, u32[]{:S(2)}, u32[]{:S(2)}) collective-permute-start(bf16[144,512]{1,0:T(8,128)(2,1)S(1)} %shard_map.94.refs_6_), channel_id=1, source_target_pairs={{0,16},{4,20},{8,24},{12,28},{16,0},{20,4},{24,8},{28,12},{1,17},{... | collective-permute-start | bytes 442376 | tf_op jit(solution)/shard_map/ppermute | solution.py:328
  16.6 0.5 %collective-permute-start.4 = (bf16[144,512]{1,0:T(8,128)(2,1)S(1)}, bf16[144,512]{1,0:T(8,128)(2,1)S(1)}, u32[]{:S(2)}, u32[]{:S(2)}) collective-permute-start(bf16[144,512]{1,0:T(8,128)(2,1)S(1)} %shard_map.94.refs_6_), channel_id=1, source_target_pairs={{0,8},{4,12},{8,0},{12,4},{16,24},{20,28},{24,16},{28,20},{1,9},{5... | collective-permute-start | bytes 442376 | tf_op jit(solution)/shard_map/ppermute | solution.py:328
  17.1 3.7 %shard_map.95 = (f32[512,1024]{1,0:T(8,128)S(1)}, bf16[3,512,1024]{2,1,0:T(8,128)(2,1)S(1)}) custom-call(bf16[512,1024]{1,0:T(8,128)(2,1)} %refs_0_.1, bf16[512,1024]{1,0:T(8,128)(2,1)} %refs_1_.1, f32[9,16,512]{2,1,0:T(8,128)} %refs_2_.1, f32[1,16]{1,0:T(1,128)} %bitcast.5, bf16[512,1024]{1,0:T(8,128)(2,1)S(1)} %get-tuple-element.20.refs_4_, ...), custom_call_target="tpu_custom_call" | custom-call | flops 2147483648 | bytes 8388608 | tf_op jit(solution)/shard_map/pallas_call | solution.py:312
  20.8 0.3 collective-permute-done.6.refs_9_
  21.1 2.5 %collective-permute-done.5.refs_8_ = bf16[144,512]{1,0:T(8,128)(2,1)S(1)} collective-permute-done((bf16[144,512]{1,0:T(8,128)(2,1)S(1)}, bf16[144,512]{1,0:T(8,128)(2,1)S(1)}, u32[]{:S(2)}, u32[]{:S(2)}) %collective-permute-start.5) | collective-permute-done | bytes 147488 | tf_op jit(solution)/shard_map/ppermute | solution.py:328
  23.6 0.1 collective-permute-done.4.refs_7_
  23.7 0.0 collective-permute-start.7
  23.7 0.5 %collective-permute-start.8 = (bf16[144,512]{1,0:T(8,128)(2,1)S(1)}, bf16[144,512]{1,0:T(8,128)(2,1)S(1)}, u32[]{:S(2)}, u32[]{:S(2)}) collective-permute-start(bf16[144,512]{1,0:T(8,128)(2,1)S(1)} %collective-permute-done.5.refs_8_), channel_id=1, source_target_pairs={{0,4},{4,0},{8,12},{12,8},{16,20},{20,16},{24,28},{28,24},{1,5},{5... | collective-permute-start | bytes 442376 | tf_op jit(solution)/shard_map/ppermute | solution.py:328
  24.2 0.0 collective-permute-start.9
  24.2 1.0 %shard_map.96 = (f32[512,512]{1,0:T(8,128)S(1)}, f32[1,512]{1,0:T(1,128)S(1)}) custom-call(bf16[64,512]{1,0:T(8,128)(2,1)S(1)} %shard_map.91.refs_0_.refs_7_, bf16[64,512]{1,0:T(8,128)(2,1)S(1)} %collective-permute-done.refs_1_.refs_8_, bf16[64,512]{1,0:T(8,128)(2,1)S(1)} %collective-permute-done.1.refs_2_.refs_9_, ...), custom_call_target="tpu_custom_call" | custom-call | flops 536870912 | bytes 3145728 | tf_op jit(solution)/shard_map/pallas_call | solution.py:312
  25.2 0.1 collective-permute-done.8.refs_8_
  25.3 0.3 collective-permute-done.9.refs_9_
  25.6 1.0 %shard_map.97 = (f32[512,512]{1,0:T(8,128)S(1)}, f32[1,512]{1,0:T(1,128)S(1)}) custom-call(bf16[64,512]{1,0:T(8,128)(2,1)S(1)} %shard_map.91.refs_0_.refs_7_, bf16[64,512]{1,0:T(8,128)(2,1)S(1)} %collective-permute-done.refs_1_.refs_8_, bf16[64,512]{1,0:T(8,128)(2,1)S(1)} %collective-permute-done.1.refs_2_.refs_9_, ...), custom_call_target="tpu_custom_call" | custom-call | flops 536870912 | bytes 3145728 | tf_op jit(solution)/shard_map/pallas_call | solution.py:312
  26.6 2.7 %collective-permute-start.12 = (f32[1,512]{1,0:T(1,128)S(1)}, f32[1,512]{1,0:T(1,128)S(1)}, u32[]{:S(2)}, u32[]{:S(2)}) collective-permute-start(f32[1,512]{1,0:T(1,128)S(1)} %get-tuple-element.32.refs_0_), channel_id=1, source_target_pairs={{0,3},{1,2},{2,1},{3,0},{4,7},{5,6},{6,5},{7,4},{8,11},{9,10},{10,... | collective-permute-start | bytes 6152 | tf_op jit(solution)/shard_map/ppermute | solution.py:328
  29.3 0.0 collective-permute-start.11
  29.3 1.7 %collective-permute-start.10 = (f32[1,512]{1,0:T(1,128)S(1)}, f32[1,512]{1,0:T(1,128)S(1)}, u32[]{:S(2)}, u32[]{:S(2)}) collective-permute-start(f32[1,512]{1,0:T(1,128)S(1)} %get-tuple-element.32.refs_0_), channel_id=1, source_target_pairs={{0,1},{1,0},{2,3},{3,2},{4,5},{5,4},{6,7},{7,6},{8,9},{9,8},{10,11... | collective-permute-start | bytes 6152 | tf_op jit(solution)/shard_map/ppermute | solution.py:328
  31.0 1.0 %collective-permute-done.12.refs_3_ = f32[1,512]{1,0:T(1,128)S(1)} collective-permute-done((f32[1,512]{1,0:T(1,128)S(1)}, f32[1,512]{1,0:T(1,128)S(1)}, u32[]{:S(2)}, u32[]{:S(2)}) %collective-permute-start.12) | collective-permute-done | bytes 2080 | tf_op jit(solution)/shard_map/ppermute | solution.py:328
  32.0 1.8 %collective-permute-done.11.refs_2_ = f32[1,512]{1,0:T(1,128)S(1)} collective-permute-done((f32[1,512]{1,0:T(1,128)S(1)}, f32[1,512]{1,0:T(1,128)S(1)}, u32[]{:S(2)}, u32[]{:S(2)}) %collective-permute-start.11) | collective-permute-done | bytes 2080 | tf_op jit(solution)/shard_map/ppermute | solution.py:328
  33.8 1.2 %shard_map.98 = bf16[512,1024]{1,0:T(8,128)(2,1)} custom-call(f32[1,512]{1,0:T(1,128)S(1)} %get-tuple-element.32.refs_0_, f32[1,512]{1,0:T(1,128)S(1)} %collective-permute-done.10.refs_1_, f32[1,512]{1,0:T(1,128)S(1)} %collective-permute-done.11.refs_2_, f32[1,512]{1,0:T(1,128)S(1)} %collective-permute-done.12.refs_3_, f32[1,1024]{1,0:T(1,128)S(1)} %bitcast.3, ...), custom_call_target="tpu_custom_call" | custom-call | flops 268435456 | bytes 3145728 | tf_op jit(solution)/shard_map/pallas_call | solution.py:312
  (4 shorter events, 0.0 us)
Async XLA Ops:
  0.8 7.7 %collective-permute-start.2 = (bf16[64,512]{1,0:T(8,128)(2,1)S(1)}, bf16[64,512]{1,0:T(8,128)(2,1)S(1)}, u32[]{:S(2)}, u32[]{:S(2)}) collective-permute-start(bf16[64,512]{1,0:T(8,128)(2,1)S(1)} %shard_map.91.refs_0_.refs_7_), channel_id=1, source_target_pairs={{0,3},{1,2},{2,1},{3,0},{4,7},{5,6},{6,5},{7,4},{8,11},{9,10},{10,... | collective-permute-start | bytes 196616 | tf_op jit(solution)/shard_map/ppermute | solution.py:328
  5.9 5.6 %collective-permute-start.1 = (bf16[64,512]{1,0:T(8,128)(2,1)S(1)}, bf16[64,512]{1,0:T(8,128)(2,1)S(1)}, u32[]{:S(2)}, u32[]{:S(2)}) collective-permute-start(bf16[64,512]{1,0:T(8,128)(2,1)S(1)} %shard_map.91.refs_0_.refs_7_), channel_id=1, source_target_pairs={{0,2},{1,3},{2,0},{3,1},{4,6},{5,7},{6,4},{7,5},{8,10},{9,11},{10,... | collective-permute-start | bytes 196616 | tf_op jit(solution)/shard_map/ppermute | solution.py:328
  5.9 5.6 %collective-permute-start = (bf16[64,512]{1,0:T(8,128)(2,1)S(1)}, bf16[64,512]{1,0:T(8,128)(2,1)S(1)}, u32[]{:S(2)}, u32[]{:S(2)}) collective-permute-start(bf16[64,512]{1,0:T(8,128)(2,1)S(1)} %shard_map.91.refs_0_.refs_7_), channel_id=1, source_target_pairs={{0,1},{1,0},{2,3},{3,2},{4,5},{5,4},{6,7},{7,6},{8,9},{9,8},{10,11... | collective-permute-start | bytes 196616 | tf_op jit(solution)/shard_map/ppermute | solution.py:328
  11.8 1.6 %collective-permute-start.3 = (bf16[144,1024]{1,0:T(8,128)(2,1)S(1)}, bf16[144,1024]{1,0:T(8,128)(2,1)S(1)}, u32[]{:S(2)}, u32[]{:S(2)}) collective-permute-start(bf16[144,1024]{1,0:T(8,128)(2,1)S(1)} %get-tuple-element.22.mine_ref), channel_id=1, source_target_pairs={{0,4},{4,0},{8,12},{12,8},{16,20},{20,16},{24,28},{28,24},{1,5},{5... | collective-permute-start | bytes 884744 | tf_op jit(solution)/shard_map/ppermute | solution.py:328
  13.6 7.5 %collective-permute-start.6 = (bf16[144,512]{1,0:T(8,128)(2,1)S(1)}, bf16[144,512]{1,0:T(8,128)(2,1)S(1)}, u32[]{:S(2)}, u32[]{:S(2)}) collective-permute-start(bf16[144,512]{1,0:T(8,128)(2,1)S(1)} %shard_map.94.refs_6_), channel_id=1, source_target_pairs={{0,24},{4,28},{8,16},{12,20},{16,8},{20,12},{24,0},{28,4},{1,25},{... | collective-permute-start | bytes 442376 | tf_op jit(solution)/shard_map/ppermute | solution.py:328
  16.1 7.5 %collective-permute-start.5 = (bf16[144,512]{1,0:T(8,128)(2,1)S(1)}, bf16[144,512]{1,0:T(8,128)(2,1)S(1)}, u32[]{:S(2)}, u32[]{:S(2)}) collective-permute-start(bf16[144,512]{1,0:T(8,128)(2,1)S(1)} %shard_map.94.refs_6_), channel_id=1, source_target_pairs={{0,16},{4,20},{8,24},{12,28},{16,0},{20,4},{24,8},{28,12},{1,17},{... | collective-permute-start | bytes 442376 | tf_op jit(solution)/shard_map/ppermute | solution.py:328
  16.6 7.1 %collective-permute-start.4 = (bf16[144,512]{1,0:T(8,128)(2,1)S(1)}, bf16[144,512]{1,0:T(8,128)(2,1)S(1)}, u32[]{:S(2)}, u32[]{:S(2)}) collective-permute-start(bf16[144,512]{1,0:T(8,128)(2,1)S(1)} %shard_map.94.refs_6_), channel_id=1, source_target_pairs={{0,8},{4,12},{8,0},{12,4},{16,24},{20,28},{24,16},{28,20},{1,9},{5... | collective-permute-start | bytes 442376 | tf_op jit(solution)/shard_map/ppermute | solution.py:328
  23.7 1.5 %collective-permute-start.7 = (bf16[144,512]{1,0:T(8,128)(2,1)S(1)}, bf16[144,512]{1,0:T(8,128)(2,1)S(1)}, u32[]{:S(2)}, u32[]{:S(2)}) collective-permute-start(bf16[144,512]{1,0:T(8,128)(2,1)S(1)} %collective-permute-done.4.refs_7_), channel_id=1, source_target_pairs={{0,4},{4,0},{8,12},{12,8},{16,20},{20,16},{24,28},{28,24},{1,5},{5... | collective-permute-start | bytes 442376 | tf_op jit(solution)/shard_map/ppermute | solution.py:328
  23.7 1.6 %collective-permute-start.8 = (bf16[144,512]{1,0:T(8,128)(2,1)S(1)}, bf16[144,512]{1,0:T(8,128)(2,1)S(1)}, u32[]{:S(2)}, u32[]{:S(2)}) collective-permute-start(bf16[144,512]{1,0:T(8,128)(2,1)S(1)} %collective-permute-done.5.refs_8_), channel_id=1, source_target_pairs={{0,4},{4,0},{8,12},{12,8},{16,20},{20,16},{24,28},{28,24},{1,5},{5... | collective-permute-start | bytes 442376 | tf_op jit(solution)/shard_map/ppermute | solution.py:328
  24.2 1.4 %collective-permute-start.9 = (bf16[144,512]{1,0:T(8,128)(2,1)S(1)}, bf16[144,512]{1,0:T(8,128)(2,1)S(1)}, u32[]{:S(2)}, u32[]{:S(2)}) collective-permute-start(bf16[144,512]{1,0:T(8,128)(2,1)S(1)} %collective-permute-done.6.refs_9_), channel_id=1, source_target_pairs={{0,4},{4,0},{8,12},{12,8},{16,20},{20,16},{24,28},{28,24},{1,5},{5... | collective-permute-start | bytes 442376 | tf_op jit(solution)/shard_map/ppermute | solution.py:328
  25.2 8.6 %copy-start = (f32[1024]{0:T(1024)S(1)}, f32[1024]{0:T(1024)}, u32[]{:S(2)}) copy-start(f32[1024]{0:T(1024)} %param.17) | copy-start | bytes 12292
  26.6 5.4 %collective-permute-start.12 = (f32[1,512]{1,0:T(1,128)S(1)}, f32[1,512]{1,0:T(1,128)S(1)}, u32[]{:S(2)}, u32[]{:S(2)}) collective-permute-start(f32[1,512]{1,0:T(1,128)S(1)} %get-tuple-element.32.refs_0_), channel_id=1, source_target_pairs={{0,3},{1,2},{2,1},{3,0},{4,7},{5,6},{6,5},{7,4},{8,11},{9,10},{10,... | collective-permute-start | bytes 6152 | tf_op jit(solution)/shard_map/ppermute | solution.py:328
  29.3 4.5 %collective-permute-start.11 = (f32[1,512]{1,0:T(1,128)S(1)}, f32[1,512]{1,0:T(1,128)S(1)}, u32[]{:S(2)}, u32[]{:S(2)}) collective-permute-start(f32[1,512]{1,0:T(1,128)S(1)} %get-tuple-element.32.refs_0_), channel_id=1, source_target_pairs={{0,2},{1,3},{2,0},{3,1},{4,6},{5,7},{6,4},{7,5},{8,10},{9,11},{10,... | collective-permute-start | bytes 6152 | tf_op jit(solution)/shard_map/ppermute | solution.py:328
  29.3 4.5 %collective-permute-start.10 = (f32[1,512]{1,0:T(1,128)S(1)}, f32[1,512]{1,0:T(1,128)S(1)}, u32[]{:S(2)}, u32[]{:S(2)}) collective-permute-start(f32[1,512]{1,0:T(1,128)S(1)} %get-tuple-element.32.refs_0_), channel_id=1, source_target_pairs={{0,1},{1,0},{2,3},{3,2},{4,5},{5,4},{6,7},{7,6},{8,9},{9,8},{10,11... | collective-permute-start | bytes 6152 | tf_op jit(solution)/shard_map/ppermute | solution.py:328

commit v4 on v3

--- a/solution.py
+++ b/solution.py
@@ -154,13 +154,13 @@
     pair_ref[size:, :] = (older[size:] * decay).astype(bf16)
 
 
-def near_kernel(parts, spans, levels, *refs):
+def near_kernel(parts, spans, levels, paired, *refs):
     inputs_hbm, gate_hbm, mix_hbm, skip_hbm = refs[:4]
-    scaled_ref, cum_ref, _ = refs[4:7]
-    map_refs = refs[7 : 7 + parts]
-    count = 7 + parts + (1 if spans else 0)
-    span_refs = refs[7 + parts : count]
-    near_ref, far_ref, inputs_ref, gate_ref, mix_ref, skip_ref, semaphores = refs[count:]
+    scaled_ref, cum_ref, _, core_ref = refs[4:8]
+    map_refs = refs[8 : 8 + parts]
+    count = 8 + parts + (1 if spans else 0)
+    span_refs = refs[8 + parts : count]
+    near_ref, far_ref, turned_ref, inputs_ref, gate_ref, mix_ref, skip_ref, semaphores = refs[count:]
     copies = fetch(refs[:4], (inputs_ref, gate_ref, mix_ref, skip_ref), semaphores)
     heads, tokens = cum_ref.shape
     width = scaled_ref.shape[1]
@@ -169,10 +169,12 @@
     in_map = map_rows(map_refs, 0)
     out_map = map_rows(map_refs, 1)
     size = in_map.shape[0]
+    turned_ref[...] = jnp.transpose(out_map)
     expand = expander(heads, width, 2).astype(bf16)
     row = lax.broadcasted_iota(jnp.int32, (GROUP, GROUP), 0)
     col = lax.broadcasted_iota(jnp.int32, (GROUP, GROUP), 1)
     scores = []
+    has_core = lax.rem(lax.axis_index("seq"), 2) == 1
     for group in range(groups):
         at = group_slice(group)
         all_scores = transposed_dot(out_map[:, at], in_map[:, at])
@@ -194,58 +196,66 @@
         decay = jnp.exp(cum + before)
         before = before + cum[:, GROUP - 1 : GROUP]
         far_mixes = [two_parts(mix_ref[first + level, :, at] * decay) for level in range(levels)]
+        if paired:
+            core_mix, *far_mixes = far_mixes
         for cols in blocks_of(width):
             own = jnp.dot(scores[group], scaled_ref[at, cols], preferred_element_type=f32)
             total = transposed_dot(mixes[0], expand[:, cols]) * own
             for mix, rows in zip(mixes[1:], states):
-                reach = transposed_dot(out_map[:, at], span_refs[0][rows, cols])
+                reach = jnp.dot(turned_ref[at, :], span_refs[0][rows, cols], preferred_element_type=f32)
                 total = total + transposed_dot(mix, expand[:, cols]) * reach
+            if paired:
+                reach = jnp.dot(turned_ref[at, :], core_ref[:size, cols], preferred_element_type=f32)
+                reach = jnp.where(has_core, reach, 0.0)
+                total = total + transposed_dot(core_mix, expand[:, cols]) * reach
             total = total + skip[:, cols] * inputs_ref[at, cols].astype(f32)
             gate = gate_ref[at, cols].astype(f32)
             swish = gate / (1.0 + jnp.exp(-gate))
             near_ref[at, cols] = total * swish
-            for level in range(levels):
-                far_ref[level, at, cols] = (transposed_dot(far_mixes[level], expand[:, cols]) * swish).astype(bf16)
-
-
-def far_body(out_map, near_ref, far_ref, start, columns, state_of, gated_ref):
+            for level, mix in enumerate(far_mixes):
+                far_ref[level, at, cols] = (transposed_dot(mix, expand[:, cols]) * swish).astype(bf16)
+
+
+def far_body(turned_ref, near_ref, far_ref, gain_ref, start, columns, state_of, gated_ref):
     levels, tokens, _ = far_ref.shape
     squares = jnp.zeros((tokens, 128), f32)
     for cols in blocks_of(columns):
         at = pl.ds(pl.multiple_of(start + cols.start, BLOCK), BLOCK)
         total = near_ref[:, at]
         for level in range(levels):
-            reach = transposed_dot(out_map, state_of(level, cols, at).astype(bf16))
+            state = state_of(level, cols, at).astype(bf16)
+            reach = jnp.dot(turned_ref[...], state, preferred_element_type=f32)
             total = total + far_ref[level, :, at].astype(f32) * reach
-        gated_ref[:, cols] = total
+        gated_ref[:, cols] = total * gain_ref[:, at]
         total = total * total
         for part in range(0, BLOCK, 128):
             squares = squares + total[:, part : part + 128]
-    ones = jnp.ones((8, 128), f32)
+    return squares
+
+
+def row_sums(squares):
+    ones = jnp.ones((8, squares.shape[1]), f32)
     sums = lax.dot_general(
         ones, squares, (((1,), (1,)), ((), ())), precision=HIGHEST, preferred_element_type=f32
     )
     return sums[:1]
 
 
-def far_kernel(parts, *refs):
-    map_refs, (near_ref, far_ref) = refs[:parts], refs[parts : parts + 2]
-    state_refs = refs[parts + 2 : -2]
-    gated_ref, squares_ref = refs[-2:]
+def far_kernel(turned_ref, near_ref, far_ref, gain_ref, *refs):
+    state_refs = refs[:-2]
+    gated_ref, sums_ref = refs[-2:]
 
     def state_of(level, cols, _):
         return state_refs[level][:, cols]
 
-    out_map = map_rows(map_refs, 1)
-    squares_ref[...] = far_body(out_map, near_ref, far_ref, 0, near_ref.shape[1], state_of, gated_ref)
-
-
-def far_kernel_of_half(parts, own, *refs):
-    map_refs = refs[:parts]
-    near_ref, far_ref, core_ref, x_ref, y_ref, diagonal_ref = refs[parts : parts + 6]
-    gated_ref, squares_ref = refs[-2:]
-    out_map = map_rows(map_refs, 1)
-    size = out_map.shape[0]
+    width = near_ref.shape[1]
+    sums_ref[...] = row_sums(far_body(turned_ref, near_ref, far_ref, gain_ref, 0, width, state_of, gated_ref))
+
+
+def far_kernel_of_half(own, *refs):
+    turned_ref, near_ref, far_ref, gain_ref, core_ref, x_ref, y_ref, diagonal_ref = refs[:8]
+    gated_ref, sums_ref = refs[-2:]
+    size = turned_ref.shape[1]
     rank = lax.axis_index("seq")
     core = lax.rem(rank, 2)
     along_x = lax.rem(lax.div(rank, 2), 2)
@@ -258,12 +268,10 @@
         return whole[:size], whole[size : size + 1]
 
     def state_of(level, cols, at):
-        core_state, core_decay = parts_of(core_ref, at)
-        if level == 0:
-            return jnp.where(core == 1, core_state, 0.0)
+        core_decay = core_ref[size:, at].astype(f32)[:1]
         running = jnp.where(core == 1, core_decay, 1.0)
         x_state, x_decay = parts_of(x_ref, cols)
-        if level == 1:
+        if level == 0:
             return x_state * jnp.where(along_x == 1, running, 0.0)
         running = running * jnp.where(along_x == 1, x_decay, 1.0)
         running = jnp.where(along_y == 1, running, 0.0)
@@ -274,13 +282,12 @@
         older = jnp.where(along_x == 1, d_state, y_state)
         return (older * newer_decay + newer) * running
 
-    sums = far_body(out_map, near_ref, far_ref, start, half, state_of, gated_ref)
-    squares_ref[...] = sums if own else sums + refs[parts + 6][...]
+    squares = far_body(turned_ref, near_ref, far_ref, gain_ref, start, half, state_of, gated_ref)
+    sums_ref[...] = squares if own else row_sums(squares + refs[8][...])
 
 
 def norm_kernel(parts, columns, *refs):
-    gain_ref = refs[parts]
-    gated_refs, (out_hbm, out_ref, semaphores) = refs[parts + 1 : -3], refs[-3:]
+    gated_refs, (out_hbm, out_ref, semaphores) = refs[parts:-3], refs[-3:]
     total = refs[0][...]
     for ref in refs[1:parts]:
         total = total + ref[...]
@@ -296,7 +303,7 @@
         rows = slice(index * chunk, (index + 1) * chunk)
         for ref, side in zip(gated_refs, sides):
             at = pl.ds(pl.multiple_of(side * width, width), width)
-            out_ref[rows, at] = (ref[rows, :] * scale[rows] * gain_ref[:, at]).astype(bf16)
+            out_ref[rows, at] = (ref[rows, :] * scale[rows]).astype(bf16)
         copies.append(pltpu.make_async_copy(out_ref.at[rows], out_hbm.at[rows], semaphores.at[index]))
         copies[-1].start()
     for copy in copies:
@@ -330,6 +337,21 @@
 
 def from_each(array, axis):
     return [array] + [flip(array, axis, mask) for mask in range(1, lax.axis_size(axis))]
+
+
+def add_kernel(left_ref, right_ref, sum_ref):
+    sum_ref[...] = left_ref[...] + right_ref[...]
+
+
+def sum_to_last(array, axis):
+    size = lax.axis_size(axis)
+    mask = 1
+    theirs = flip(array, axis, mask)
+    while 2 * mask < size:
+        mask = 2 * mask
+        array = call(add_kernel, shaped(array.shape, array.dtype), (array, theirs))
+        theirs = flip(array, axis, mask)
+    return array, theirs
 
 
 def merged(older, newer, size):
@@ -403,10 +425,18 @@
         )
     else:
         message = shard
-    near, far = call(
-        functools.partial(near_kernel, parts, spans, levels),
-        (shaped((tokens, width), f32), shaped((levels, tokens, width), bf16)),
-        (inputs, gate, level_mix, skip[None, :], scaled, cum, message, *maps, *span_states),
+    near_levels = levels - 1 if pairs else levels
+    near, far, turned = call(
+        functools.partial(near_kernel, parts, spans, levels, pairs),
+        (
+            shaped((tokens, width), f32),
+            shaped((near_levels, tokens, width), bf16),
+            shaped((tokens, size), bf16),
+        ),
+        (
+            *(inputs, gate, level_mix, skip[None, :], scaled, cum, message, theirs if pairs else message),
+            *(*maps, *span_states),
+        ),
         flops=8 * dense,
         bytes_accessed=16 * area,
         hbm=4,
@@ -414,37 +444,39 @@
     gain = norm_gain[None, :]
     sums_shape = shaped((1, tokens), f32)
     if pairs:
-        own = [flip(message, "seq", mask) for mask in (2, 4, 6)]
+        own = [flip(message, "seq", mask) for mask in (6, 2, 4)]
         *own, near, far = lax.optimization_barrier((*own, near, far))
+        own = own[1], own[2], own[0]
         other = [flip(array, "seq", 1) for array in own]
         gated_shape = shaped((tokens, width // 2), f32)
         own_gated, own_squares = call(
-            functools.partial(far_kernel_of_half, parts, True),
-            (gated_shape, sums_shape),
-            (*maps, near, far, theirs, *own),
+            functools.partial(far_kernel_of_half, True),
+            (gated_shape, shaped((tokens, 128), f32)),
+            (turned, near, far, gain, theirs, *own),
             flops=2 * dense,
             bytes_accessed=6 * area,
         )
-        other_gated, squares = call(
-            functools.partial(far_kernel_of_half, parts, False),
+        other_gated, sums = call(
+            functools.partial(far_kernel_of_half, False),
             (gated_shape, sums_shape),
-            (*maps, near, far, theirs, *other, own_squares),
+            (turned, near, far, gain, theirs, *other, own_squares),
             flops=2 * dense,
             bytes_accessed=6 * area,
         )
         gated = (own_gated, other_gated)
     else:
-        *gated, squares = call(
-            functools.partial(far_kernel, parts),
+        *gated, sums = call(
+            far_kernel,
             (shaped((tokens, width), f32), sums_shape),
-            (*maps, near, far, *far_states(shard, size)),
+            (turned, near, far, gain, *far_states(shard, size)),
             flops=4 * dense,
             bytes_accessed=12 * area,
         )
+    last = sum_to_last(sums, "head")
     return call(
-        functools.partial(norm_kernel, parts, width * parts),
+        functools.partial(norm_kernel, len(last), width * parts),
         shaped((tokens, width), bf16),
-        (*from_each(squares, "head"), gain, *gated),
+        (*last, *gated),
         flops=dense,
         bytes_accessed=6 * area,
         scratch=[pltpu.VMEM((tokens, width), bf16), pltpu.SemaphoreType.DMA((NORM_CHUNKS,))],

time: 35.3 us -> 36.2 us (1.025)
  waiting for transfers between devices: 10.8 us -> 13.8 us
  starting transfers between devices: 14.3 us -> 12.6 us
  Pallas kernels: 9.84 us -> 9.45 us
    ppermute x13 -> x12, waiting for transfers between devices: 10.8 us -> 13.8 us  [flip(): lax.ppermute(array, axis, [(i, i ^ mask) for i in range(lax.axis_size(axi...]
    ppermute x13 -> x12, starting transfers between devices: 14.3 us -> 12.6 us  [flip(): lax.ppermute(array, axis, [(i, i ^ mask) for i in range(lax.axis_size(axi...]
    pallas_call x8 -> x9, Pallas kernels: 9.84 us -> 9.45 us  [call(): pl.pallas_call(kernel, out_shape=out_shape, in_specs=specs, out_specs=jax...]
  transfers between devices with their start and end apart: 13 -> 12, of which waited for: 10 -> 10; matrix products, arithmetic and copies ran while one was open for 0% -> 0% of each run, Pallas kernels for 18% -> 17%
where the time goes in v4:
time: 36.2 us; the launch traced here: 35.9 us
  waiting for transfers between devices  13.8 us (38%)
  starting transfers between devices  12.6 us (35%)
  Pallas kernels  9.45 us (26%)
    ppermute x12, waiting for transfers between devices, flip(): lax.ppermute(array, axis, [(i, i ^ mask) for i in range(lax.axis_size(axi...  13.8 us
    ppermute x12, starting transfers between devices, flip(): lax.ppermute(array, axis, [(i, i ^ mask) for i in range(lax.axis_size(axi...  12.6 us
    pallas_call x9, Pallas kernels, call(): pl.pallas_call(kernel, out_shape=out_shape, in_specs=specs, out_specs=jax...  9.45 us
  transfers between devices with their start and end apart: 12, of which 10 were waited for; matrix products, arithmetic and copies ran while one was open for 0% of the time, Pallas kernels for 17%

profile of v4, /device:TPU:0, one launch (start us, length us, event | category | flops | bytes accessed | tf_op | source)
XLA Modules:
  0.0 35.9 jit_solution(4771845616389207406)
XLA Ops:
  0.0 0.8 %shard_map.92.refs_0_.refs_8_ = bf16[64,512]{1,0:T(8,128)(2,1)S(1)} custom-call(bf16[32,512]{1,0:T(8,128)(2,1)} %in_hbm.1, bf16[32,512]{1,0:T(8,128)(2,1)} %out_hbm.1), custom_call_target="tpu_custom_call" | custom-call | bytes 65536 | tf_op jit(solution)/shard_map/pallas_call | solution.py:319
  0.8 5.1 %collective-permute-start.2 = (bf16[64,512]{1,0:T(8,128)(2,1)S(1)}, bf16[64,512]{1,0:T(8,128)(2,1)S(1)}, u32[]{:S(2)}, u32[]{:S(2)}) collective-permute-start(bf16[64,512]{1,0:T(8,128)(2,1)S(1)} %shard_map.92.refs_0_.refs_8_), channel_id=1, source_target_pairs={{0,3},{1,2},{2,1},{3,0},{4,7},{5,6},{6,5},{7,4},{8,11},{9,10},{10,... | collective-permute-start | bytes 196616 | tf_op jit(solution)/shard_map/ppermute | solution.py:335
  5.9 0.0 collective-permute-start.1
  5.9 0.6 %collective-permute-start = (bf16[64,512]{1,0:T(8,128)(2,1)S(1)}, bf16[64,512]{1,0:T(8,128)(2,1)S(1)}, u32[]{:S(2)}, u32[]{:S(2)}) collective-permute-start(bf16[64,512]{1,0:T(8,128)(2,1)S(1)} %shard_map.92.refs_0_.refs_8_), channel_id=1, source_target_pairs={{0,1},{1,0},{2,3},{3,2},{4,5},{5,4},{6,7},{7,6},{8,9},{9,8},{10,11... | collective-permute-start | bytes 196616 | tf_op jit(solution)/shard_map/ppermute | solution.py:335
  6.6 1.7 %shard_map.91 = (bf16[512,1024]{1,0:T(8,128)(2,1)S(1)}, f32[16,512]{1,0:T(8,128)S(1)}) custom-call(bf16[512,1024]{1,0:T(8,128)(2,1)} %refs_0_.1, f32[16,512]{1,0:T(8,128)} %step_hbm.1, f32[1,16]{1,0:T(1,128)} %bitcast.5), custom_call_target="tpu_custom_call" | custom-call | flops 268435456 | bytes 2097152 | tf_op jit(solution)/shard_map/pallas_call | solution.py:319
  8.3 0.2 collective-permute-done.2.refs_3_.refs_11_
  8.5 3.0 %collective-permute-done.1.refs_2_.refs_10_ = bf16[64,512]{1,0:T(8,128)(2,1)S(1)} collective-permute-done((bf16[64,512]{1,0:T(8,128)(2,1)S(1)}, bf16[64,512]{1,0:T(8,128)(2,1)S(1)}, u32[]{:S(2)}, u32[]{:S(2)}) %collective-permute-start.1) | collective-permute-done | bytes 65568 | tf_op jit(solution)/shard_map/ppermute | solution.py:335
  11.5 0.0 collective-permute-done.refs_1_.refs_9_
  11.5 0.3 shard_map.93
  11.8 0.1 collective-permute-start.3
  11.9 1.6 %collective-permute-done.3.theirs_ref.refs_7_.refs_4_ = bf16[144,1024]{1,0:T(8,128)(2,1)S(1)} collective-permute-done((bf16[144,1024]{1,0:T(8,128)(2,1)S(1)}, bf16[144,1024]{1,0:T(8,128)(2,1)S(1)}, u32[]{:S(2)}, u32[]{:S(2)}) %collective-permute-start.3) | collective-permute-done | bytes 294944 | tf_op jit(solution)/shard_map/ppermute | solution.py:335
  13.5 0.1 shard_map.94.refs_6_
  13.6 1.6 %collective-permute-start.6 = (bf16[144,512]{1,0:T(8,128)(2,1)S(1)}, bf16[144,512]{1,0:T(8,128)(2,1)S(1)}, u32[]{:S(2)}, u32[]{:S(2)}) collective-permute-start(bf16[144,512]{1,0:T(8,128)(2,1)S(1)} %shard_map.94.refs_6_), channel_id=1, source_target_pairs={{0,16},{4,20},{8,24},{12,28},{16,0},{20,4},{24,8},{28,12},{1,17},{... | collective-permute-start | bytes 442376 | tf_op jit(solution)/shard_map/ppermute | solution.py:335
  15.2 1.5 %collective-permute-start.5 = (bf16[144,512]{1,0:T(8,128)(2,1)S(1)}, bf16[144,512]{1,0:T(8,128)(2,1)S(1)}, u32[]{:S(2)}, u32[]{:S(2)}) collective-permute-start(bf16[144,512]{1,0:T(8,128)(2,1)S(1)} %shard_map.94.refs_6_), channel_id=1, source_target_pairs={{0,8},{4,12},{8,0},{12,4},{16,24},{20,28},{24,16},{28,20},{1,9},{5... | collective-permute-start | bytes 442376 | tf_op jit(solution)/shard_map/ppermute | solution.py:335
  16.6 0.5 %collective-permute-start.4 = (bf16[144,512]{1,0:T(8,128)(2,1)S(1)}, bf16[144,512]{1,0:T(8,128)(2,1)S(1)}, u32[]{:S(2)}, u32[]{:S(2)}) collective-permute-start(bf16[144,512]{1,0:T(8,128)(2,1)S(1)} %shard_map.94.refs_6_), channel_id=1, source_target_pairs={{0,24},{4,28},{8,16},{12,20},{16,8},{20,12},{24,0},{28,4},{1,25},{... | collective-permute-start | bytes 442376 | tf_op jit(solution)/shard_map/ppermute | solution.py:335
  17.1 3.9 %shard_map.95 = (f32[512,1024]{1,0:T(8,128)S(1)}, bf16[2,512,1024]{2,1,0:T(8,128)(2,1)S(1)}, bf16[512,128]{1,0:T(8,128)(2,1)S(1)}) custom-call(bf16[512,1024]{1,0:T(8,128)(2,1)} %refs_0_.1, bf16[512,1024]{1,0:T(8,128)(2,1)} %refs_1_.1, f32[9,16,512]{2,1,0:T(8,128)} %refs_2_.1, f32[1,16]{1,0:T(1,128)} %bitcast.6, ...), custom_call_target="tpu_custom_call" | custom-call | flops 2147483648 | bytes 8388608 | tf_op jit(solution)/shard_map/pallas_call | solution.py:319
  21.1 0.0 collective-permute-done.6.refs_6_
  21.1 0.8 %collective-permute-done.5.refs_5_ = bf16[144,512]{1,0:T(8,128)(2,1)S(1)} collective-permute-done((bf16[144,512]{1,0:T(8,128)(2,1)S(1)}, bf16[144,512]{1,0:T(8,128)(2,1)S(1)}, u32[]{:S(2)}, u32[]{:S(2)}) %collective-permute-start.5) | collective-permute-done | bytes 147488 | tf_op jit(solution)/shard_map/ppermute | solution.py:335
  21.9 2.0 %collective-permute-done.4.refs_7_ = bf16[144,512]{1,0:T(8,128)(2,1)S(1)} collective-permute-done((bf16[144,512]{1,0:T(8,128)(2,1)S(1)}, bf16[144,512]{1,0:T(8,128)(2,1)S(1)}, u32[]{:S(2)}, u32[]{:S(2)}) %collective-permute-start.4) | collective-permute-done | bytes 147488 | tf_op jit(solution)/shard_map/ppermute | solution.py:335
  23.9 0.0 collective-permute-start.7
  23.9 0.5 %collective-permute-start.8 = (bf16[144,512]{1,0:T(8,128)(2,1)S(1)}, bf16[144,512]{1,0:T(8,128)(2,1)S(1)}, u32[]{:S(2)}, u32[]{:S(2)}) collective-permute-start(bf16[144,512]{1,0:T(8,128)(2,1)S(1)} %collective-permute-done.6.refs_6_), channel_id=1, source_target_pairs={{0,4},{4,0},{8,12},{12,8},{16,20},{20,16},{24,28},{28,24},{1,5},{5... | collective-permute-start | bytes 442376 | tf_op jit(solution)/shard_map/ppermute | solution.py:335
  24.4 0.0 collective-permute-start.9
  24.4 0.5 %shard_map.96 = (f32[512,512]{1,0:T(8,128)S(1)}, f32[512,128]{1,0:T(8,128)S(1)}) custom-call(bf16[512,128]{1,0:T(8,128)(2,1)S(1)} %get-tuple-element.25.refs_0_, f32[512,1024]{1,0:T(8,128)S(1)} %get-tuple-element.28.refs_1_, bf16[2,512,1024]{2,1,0:T(8,128)(2,1)S(1)} %get-tuple-element.29.refs_2_, f32[1,1024]{1,0:T(1,128)S(1)} %bitcast.3, ...), custom_call_target="tpu_custom_call" | custom-call | flops 536870912 | bytes 3145728 | tf_op jit(solution)/shard_map/pallas_call | solution.py:319
  24.9 0.3 collective-permute-done.7.refs_5_
  25.2 0.2 collective-permute-done.8.refs_6_
  25.4 0.3 collective-permute-done.9.refs_7_
  25.7 0.9 %shard_map.97 = (f32[512,512]{1,0:T(8,128)S(1)}, f32[1,512]{1,0:T(1,128)S(1)}) custom-call(bf16[512,128]{1,0:T(8,128)(2,1)S(1)} %get-tuple-element.25.refs_0_, f32[512,1024]{1,0:T(8,128)S(1)} %get-tuple-element.28.refs_1_, bf16[2,512,1024]{2,1,0:T(8,128)(2,1)S(1)} %get-tuple-element.29.refs_2_, f32[1,1024]{1,0:T(1,128)S(1)} %bitcast.4, ...), custom_call_target="tpu_custom_call" | custom-call | flops 536870912 | bytes 3145728 | tf_op jit(solution)/shard_map/pallas_call | solution.py:319
  26.6 1.1 %collective-permute-start.10 = (f32[1,512]{1,0:T(1,128)S(1)}, f32[1,512]{1,0:T(1,128)S(1)}, u32[]{:S(2)}, u32[]{:S(2)}) collective-permute-start(f32[1,512]{1,0:T(1,128)S(1)} %get-tuple-element.34.left_ref), channel_id=1, source_target_pairs={{0,1},{1,0},{2,3},{3,2},{4,5},{5,4},{6,7},{7,6},{8,9},{9,8},{10,11... | collective-permute-start | bytes 6152 | tf_op jit(solution)/shard_map/ppermute | solution.py:335
  27.7 2.5 %collective-permute-done.10.right_ref = f32[1,512]{1,0:T(1,128)S(1)} collective-permute-done((f32[1,512]{1,0:T(1,128)S(1)}, f32[1,512]{1,0:T(1,128)S(1)}, u32[]{:S(2)}, u32[]{:S(2)}) %collective-permute-start.10) | collective-permute-done | bytes 2080 | tf_op jit(solution)/shard_map/ppermute | solution.py:335
  30.2 1.6 %collective-permute-start.11 = (f32[1,512]{1,0:T(1,128)S(1)}, f32[1,512]{1,0:T(1,128)S(1)}, u32[]{:S(2)}, u32[]{:S(2)}) collective-permute-start(f32[1,512]{1,0:T(1,128)S(1)} %shard_map.98.refs_0_), channel_id=1, source_target_pairs={{0,2},{1,3},{2,0},{3,1},{4,6},{5,7},{6,4},{7,5},{8,10},{9,11},{10,... | collective-permute-start | bytes 6152 | tf_op jit(solution)/shard_map/ppermute | solution.py:335
  31.8 2.9 %collective-permute-done.11.refs_1_ = f32[1,512]{1,0:T(1,128)S(1)} collective-permute-done((f32[1,512]{1,0:T(1,128)S(1)}, f32[1,512]{1,0:T(1,128)S(1)}, u32[]{:S(2)}, u32[]{:S(2)}) %collective-permute-start.11) | collective-permute-done | bytes 2080 | tf_op jit(solution)/shard_map/ppermute | solution.py:335
  34.7 1.2 %shard_map.99 = bf16[512,1024]{1,0:T(8,128)(2,1)} custom-call(f32[1,512]{1,0:T(1,128)S(1)} %shard_map.98.refs_0_, f32[1,512]{1,0:T(1,128)S(1)} %collective-permute-done.11.refs_1_, f32[512,512]{1,0:T(8,128)S(1)} %get-tuple-element.35.refs_2_, f32[512,512]{1,0:T(8,128)S(1)} %get-tuple-element.36.refs_3_), custom_call_target="tpu_custom_call" | custom-call | flops 268435456 | bytes 3145728 | tf_op jit(solution)/shard_map/pallas_call | solution.py:319
  (3 shorter events, 0.0 us)
Async XLA Ops:
  0.8 7.7 %collective-permute-start.2 = (bf16[64,512]{1,0:T(8,128)(2,1)S(1)}, bf16[64,512]{1,0:T(8,128)(2,1)S(1)}, u32[]{:S(2)}, u32[]{:S(2)}) collective-permute-start(bf16[64,512]{1,0:T(8,128)(2,1)S(1)} %shard_map.92.refs_0_.refs_8_), channel_id=1, source_target_pairs={{0,3},{1,2},{2,1},{3,0},{4,7},{5,6},{6,5},{7,4},{8,11},{9,10},{10,... | collective-permute-start | bytes 196616 | tf_op jit(solution)/shard_map/ppermute | solution.py:335
  5.9 5.6 %collective-permute-start.1 = (bf16[64,512]{1,0:T(8,128)(2,1)S(1)}, bf16[64,512]{1,0:T(8,128)(2,1)S(1)}, u32[]{:S(2)}, u32[]{:S(2)}) collective-permute-start(bf16[64,512]{1,0:T(8,128)(2,1)S(1)} %shard_map.92.refs_0_.refs_8_), channel_id=1, source_target_pairs={{0,2},{1,3},{2,0},{3,1},{4,6},{5,7},{6,4},{7,5},{8,10},{9,11},{10,... | collective-permute-start | bytes 196616 | tf_op jit(solution)/shard_map/ppermute | solution.py:335
  5.9 5.6 %collective-permute-start = (bf16[64,512]{1,0:T(8,128)(2,1)S(1)}, bf16[64,512]{1,0:T(8,128)(2,1)S(1)}, u32[]{:S(2)}, u32[]{:S(2)}) collective-permute-start(bf16[64,512]{1,0:T(8,128)(2,1)S(1)} %shard_map.92.refs_0_.refs_8_), channel_id=1, source_target_pairs={{0,1},{1,0},{2,3},{3,2},{4,5},{5,4},{6,7},{7,6},{8,9},{9,8},{10,11... | collective-permute-start | bytes 196616 | tf_op jit(solution)/shard_map/ppermute | solution.py:335
  11.8 1.6 %collective-permute-start.3 = (bf16[144,1024]{1,0:T(8,128)(2,1)S(1)}, bf16[144,1024]{1,0:T(8,128)(2,1)S(1)}, u32[]{:S(2)}, u32[]{:S(2)}) collective-permute-start(bf16[144,1024]{1,0:T(8,128)(2,1)S(1)} %get-tuple-element.23.mine_ref), channel_id=1, source_target_pairs={{0,4},{4,0},{8,12},{12,8},{16,20},{20,16},{24,28},{28,24},{1,5},{5... | collective-permute-start | bytes 884744 | tf_op jit(solution)/shard_map/ppermute | solution.py:335
  13.6 7.5 %collective-permute-start.6 = (bf16[144,512]{1,0:T(8,128)(2,1)S(1)}, bf16[144,512]{1,0:T(8,128)(2,1)S(1)}, u32[]{:S(2)}, u32[]{:S(2)}) collective-permute-start(bf16[144,512]{1,0:T(8,128)(2,1)S(1)} %shard_map.94.refs_6_), channel_id=1, source_target_pairs={{0,16},{4,20},{8,24},{12,28},{16,0},{20,4},{24,8},{28,12},{1,17},{... | collective-permute-start | bytes 442376 | tf_op jit(solution)/shard_map/ppermute | solution.py:335
  15.2 6.7 %collective-permute-start.5 = (bf16[144,512]{1,0:T(8,128)(2,1)S(1)}, bf16[144,512]{1,0:T(8,128)(2,1)S(1)}, u32[]{:S(2)}, u32[]{:S(2)}) collective-permute-start(bf16[144,512]{1,0:T(8,128)(2,1)S(1)} %shard_map.94.refs_6_), channel_id=1, source_target_pairs={{0,8},{4,12},{8,0},{12,4},{16,24},{20,28},{24,16},{28,20},{1,9},{5... | collective-permute-start | bytes 442376 | tf_op jit(solution)/shard_map/ppermute | solution.py:335
  16.6 7.2 %collective-permute-start.4 = (bf16[144,512]{1,0:T(8,128)(2,1)S(1)}, bf16[144,512]{1,0:T(8,128)(2,1)S(1)}, u32[]{:S(2)}, u32[]{:S(2)}) collective-permute-start(bf16[144,512]{1,0:T(8,128)(2,1)S(1)} %shard_map.94.refs_6_), channel_id=1, source_target_pairs={{0,24},{4,28},{8,16},{12,20},{16,8},{20,12},{24,0},{28,4},{1,25},{... | collective-permute-start | bytes 442376 | tf_op jit(solution)/shard_map/ppermute | solution.py:335
  17.1 7.3 %copy-start = (f32[1024]{0:T(1024)S(1)}, f32[1024]{0:T(1024)}, u32[]{:S(2)}) copy-start(f32[1024]{0:T(1024)} %param.17) | copy-start | bytes 12292
  23.9 1.4 %collective-permute-start.7 = (bf16[144,512]{1,0:T(8,128)(2,1)S(1)}, bf16[144,512]{1,0:T(8,128)(2,1)S(1)}, u32[]{:S(2)}, u32[]{:S(2)}) collective-permute-start(bf16[144,512]{1,0:T(8,128)(2,1)S(1)} %collective-permute-done.5.refs_5_), channel_id=1, source_target_pairs={{0,4},{4,0},{8,12},{12,8},{16,20},{20,16},{24,28},{28,24},{1,5},{5... | collective-permute-start | bytes 442376 | tf_op jit(solution)/shard_map/ppermute | solution.py:335
  23.9 1.6 %collective-permute-start.8 = (bf16[144,512]{1,0:T(8,128)(2,1)S(1)}, bf16[144,512]{1,0:T(8,128)(2,1)S(1)}, u32[]{:S(2)}, u32[]{:S(2)}) collective-permute-start(bf16[144,512]{1,0:T(8,128)(2,1)S(1)} %collective-permute-done.6.refs_6_), channel_id=1, source_target_pairs={{0,4},{4,0},{8,12},{12,8},{16,20},{20,16},{24,28},{28,24},{1,5},{5... | collective-permute-start | bytes 442376 | tf_op jit(solution)/shard_map/ppermute | solution.py:335
  24.4 1.4 %collective-permute-start.9 = (bf16[144,512]{1,0:T(8,128)(2,1)S(1)}, bf16[144,512]{1,0:T(8,128)(2,1)S(1)}, u32[]{:S(2)}, u32[]{:S(2)}) collective-permute-start(bf16[144,512]{1,0:T(8,128)(2,1)S(1)} %collective-permute-done.4.refs_7_), channel_id=1, source_target_pairs={{0,4},{4,0},{8,12},{12,8},{16,20},{20,16},{24,28},{28,24},{1,5},{5... | collective-permute-start | bytes 442376 | tf_op jit(solution)/shard_map/ppermute | solution.py:335
  26.6 3.6 %collective-permute-start.10 = (f32[1,512]{1,0:T(1,128)S(1)}, f32[1,512]{1,0:T(1,128)S(1)}, u32[]{:S(2)}, u32[]{:S(2)}) collective-permute-start(f32[1,512]{1,0:T(1,128)S(1)} %get-tuple-element.34.left_ref), channel_id=1, source_target_pairs={{0,1},{1,0},{2,3},{3,2},{4,5},{5,4},{6,7},{7,6},{8,9},{9,8},{10,11... | collective-permute-start | bytes 6152 | tf_op jit(solution)/shard_map/ppermute | solution.py:335
  30.2 4.5 %collective-permute-start.11 = (f32[1,512]{1,0:T(1,128)S(1)}, f32[1,512]{1,0:T(1,128)S(1)}, u32[]{:S(2)}, u32[]{:S(2)}) collective-permute-start(f32[1,512]{1,0:T(1,128)S(1)} %shard_map.98.refs_0_), channel_id=1, source_target_pairs={{0,2},{1,3},{2,0},{3,1},{4,6},{5,7},{6,4},{7,5},{8,10},{9,11},{10,... | collective-permute-start | bytes 6152 | tf_op jit(solution)/shard_map/ppermute | solution.py:335

commit v5 on v4

--- a/solution.py
+++ b/solution.py
@@ -11,7 +11,7 @@
 GROUP = 256
 DECAY_ROWS = 16
 BLOCK = 256
-NORM_CHUNKS = 4
+NORM_CHUNKS = 8
 VMEM_LIMIT = 40 * 1024 * 1024
 
 f32, bf16 = jnp.float32, jnp.bfloat16
@@ -234,11 +234,11 @@
 
 
 def row_sums(squares):
-    ones = jnp.ones((8, squares.shape[1]), f32)
-    sums = lax.dot_general(
-        ones, squares, (((1,), (1,)), ((), ())), precision=HIGHEST, preferred_element_type=f32
-    )
-    return sums[:1]
+    high = squares.astype(bf16)
+    low = (squares - high.astype(f32)).astype(bf16)
+    parts = jnp.concatenate([high, low], axis=1)
+    ones = jnp.ones((16, parts.shape[1]), bf16)
+    return lax.dot_general(ones, parts, (((1,), (1,)), ((), ())), preferred_element_type=f32)[:1]
 
 
 def far_kernel(turned_ref, near_ref, far_ref, gain_ref, *refs):
@@ -252,38 +252,41 @@
     sums_ref[...] = row_sums(far_body(turned_ref, near_ref, far_ref, gain_ref, 0, width, state_of, gated_ref))
 
 
+def combine_kernel(size, x_ref, y_ref, diagonal_ref, spans_ref):
+    rank = lax.axis_index("seq")
+    along_x = lax.rem(lax.div(rank, 2), 2)
+    along_y = lax.div(rank, 4)
+
+    def parts_of(ref):
+        return ref[:size, :].astype(f32), ref[size:, :].astype(f32)[:1]
+
+    x_state, x_decay = parts_of(x_ref)
+    y_state, y_decay = parts_of(y_ref)
+    d_state, d_decay = parts_of(diagonal_ref)
+    newer = jnp.where(along_x == 1, y_state, d_state)
+    newer_decay = jnp.where(along_x == 1, y_decay, d_decay)
+    older = jnp.where(along_x == 1, d_state, y_state)
+    running = jnp.where(along_x == 1, x_decay, 1.0)
+    running = jnp.where(along_y == 1, running, 0.0)
+    spans_ref[:size, :] = jnp.where(along_x == 1, x_state, 0.0).astype(bf16)
+    spans_ref[size:, :] = ((older * newer_decay + newer) * running).astype(bf16)
+
+
 def far_kernel_of_half(own, *refs):
-    turned_ref, near_ref, far_ref, gain_ref, core_ref, x_ref, y_ref, diagonal_ref = refs[:8]
+    turned_ref, near_ref, far_ref, gain_ref, core_ref, spans_ref = refs[:6]
     gated_ref, sums_ref = refs[-2:]
     size = turned_ref.shape[1]
-    rank = lax.axis_index("seq")
-    core = lax.rem(rank, 2)
-    along_x = lax.rem(lax.div(rank, 2), 2)
-    along_y = lax.div(rank, 4)
-    half = x_ref.shape[1]
+    core = lax.rem(lax.axis_index("seq"), 2)
+    half = spans_ref.shape[1]
     start = (core if own else 1 - core) * half
-
-    def parts_of(ref, cols):
-        whole = ref[:, cols].astype(f32)
-        return whole[:size], whole[size : size + 1]
 
     def state_of(level, cols, at):
         core_decay = core_ref[size:, at].astype(f32)[:1]
         running = jnp.where(core == 1, core_decay, 1.0)
-        x_state, x_decay = parts_of(x_ref, cols)
-        if level == 0:
-            return x_state * jnp.where(along_x == 1, running, 0.0)
-        running = running * jnp.where(along_x == 1, x_decay, 1.0)
-        running = jnp.where(along_y == 1, running, 0.0)
-        y_state, y_decay = parts_of(y_ref, cols)
-        d_state, d_decay = parts_of(diagonal_ref, cols)
-        newer = jnp.where(along_x == 1, y_state, d_state)
-        newer_decay = jnp.where(along_x == 1, y_decay, d_decay)
-        older = jnp.where(along_x == 1, d_state, y_state)
-        return (older * newer_decay + newer) * running
+        return spans_ref[level * size : (level + 1) * size, cols].astype(f32) * running
 
     squares = far_body(turned_ref, near_ref, far_ref, gain_ref, start, half, state_of, gated_ref)
-    sums_ref[...] = squares if own else row_sums(squares + refs[8][...])
+    sums_ref[...] = squares if own else row_sums(squares + refs[6][...])
 
 
 def norm_kernel(parts, columns, *refs):
@@ -292,8 +295,13 @@
     for ref in refs[1:parts]:
         total = total + ref[...]
     scale = lax.rsqrt(total / columns + 1e-05)
-    scale = jnp.transpose(jnp.broadcast_to(scale, (8, scale.shape[1])))[:, :1]
-    tokens = scale.shape[0]
+    pieces, rest = [], scale
+    for _ in range(3):
+        pieces.append(rest.astype(bf16).astype(f32))
+        rest = rest - pieces[-1]
+    tokens = scale.shape[1]
+    pieces.append(jnp.zeros((16 - len(pieces), tokens), f32))
+    scale = transposed_dot(jnp.concatenate(pieces, axis=0).astype(bf16), jnp.ones((16, 128), bf16))
     width = gated_refs[0].shape[1]
     core = lax.rem(lax.axis_index("seq"), 2)
     sides = (core, 1 - core) if len(gated_refs) == 2 else (0,)
@@ -302,8 +310,9 @@
     for index in range(NORM_CHUNKS):
         rows = slice(index * chunk, (index + 1) * chunk)
         for ref, side in zip(gated_refs, sides):
-            at = pl.ds(pl.multiple_of(side * width, width), width)
-            out_ref[rows, at] = (ref[rows, :] * scale[rows]).astype(bf16)
+            for col in range(0, width, 128):
+                at = pl.ds(pl.multiple_of(side * width + col, 128), 128)
+                out_ref[rows, at] = (ref[rows, col : col + 128] * scale[rows]).astype(bf16)
         copies.append(pltpu.make_async_copy(out_ref.at[rows], out_hbm.at[rows], semaphores.at[index]))
         copies[-1].start()
     for copy in copies:
@@ -337,21 +346,6 @@
 
 def from_each(array, axis):
     return [array] + [flip(array, axis, mask) for mask in range(1, lax.axis_size(axis))]
-
-
-def add_kernel(left_ref, right_ref, sum_ref):
-    sum_ref[...] = left_ref[...] + right_ref[...]
-
-
-def sum_to_last(array, axis):
-    size = lax.axis_size(axis)
-    mask = 1
-    theirs = flip(array, axis, mask)
-    while 2 * mask < size:
-        mask = 2 * mask
-        array = call(add_kernel, shaped(array.shape, array.dtype), (array, theirs))
-        theirs = flip(array, axis, mask)
-    return array, theirs
 
 
 def merged(older, newer, size):
@@ -444,22 +438,27 @@
     gain = norm_gain[None, :]
     sums_shape = shaped((1, tokens), f32)
     if pairs:
-        own = [flip(message, "seq", mask) for mask in (6, 2, 4)]
-        *own, near, far = lax.optimization_barrier((*own, near, far))
-        own = own[1], own[2], own[0]
-        other = [flip(array, "seq", 1) for array in own]
+        received = [flip(message, "seq", mask) for mask in (2, 4, 6)]
+        *received, near, far = lax.optimization_barrier((*received, near, far))
+        own = call(
+            functools.partial(combine_kernel, size),
+            shaped((2 * size, width // 2), bf16),
+            received,
+            bytes_accessed=area,
+        )
+        other = flip(own, "seq", 1)
         gated_shape = shaped((tokens, width // 2), f32)
         own_gated, own_squares = call(
             functools.partial(far_kernel_of_half, True),
             (gated_shape, shaped((tokens, 128), f32)),
-            (turned, near, far, gain, theirs, *own),
+            (turned, near, far, gain, theirs, own),
             flops=2 * dense,
             bytes_accessed=6 * area,
         )
         other_gated, sums = call(
             functools.partial(far_kernel_of_half, False),
             (gated_shape, sums_shape),
-            (turned, near, far, gain, theirs, *other, own_squares),
+            (turned, near, far, gain, theirs, other, own_squares),
             flops=2 * dense,
             bytes_accessed=6 * area,
         )
@@ -472,7 +471,7 @@
             flops=4 * dense,
             bytes_accessed=12 * area,
         )
-    last = sum_to_last(sums, "head")
+    last = from_each(sums, "head")
     return call(
         functools.partial(norm_kernel, len(last), width * parts),
         shaped((tokens, width), bf16),

time: 36.2 us -> 34.8 us (0.961)
  waiting for transfers between devices: 13.8 us -> 11.2 us
  starting transfers between devices: 12.6 us -> 13.9 us
    ppermute x12 -> x11, waiting for transfers between devices: 13.8 us -> 11.2 us  [flip(): lax.ppermute(array, axis, [(i, i ^ mask) for i in range(lax.axis_size(axi...]
    ppermute x12 -> x11, starting transfers between devices: 12.6 us -> 13.9 us  [flip(): lax.ppermute(array, axis, [(i, i ^ mask) for i in range(lax.axis_size(axi...]
  transfers between devices with their start and end apart: 12 -> 11, of which waited for: 10 -> 8; matrix products, arithmetic and copies ran while one was open for 0% -> 0% of each run, Pallas kernels for 17% -> 18%
where the time goes in v5:
time: 34.8 us; the launch traced here: 34.6 us
  starting transfers between devices  13.9 us (40%)
  waiting for transfers between devices  11.2 us (32%)
  Pallas kernels  9.46 us (27%)
    ppermute x11, starting transfers between devices, flip(): lax.ppermute(array, axis, [(i, i ^ mask) for i in range(lax.axis_size(axi...  13.9 us
    ppermute x11, waiting for transfers between devices, flip(): lax.ppermute(array, axis, [(i, i ^ mask) for i in range(lax.axis_size(axi...  11.2 us
    pallas_call x9, Pallas kernels, call(): pl.pallas_call(kernel, out_shape=out_shape, in_specs=specs, out_specs=jax...  9.46 us
  transfers between devices with their start and end apart: 11, of which 8 were waited for; matrix products, arithmetic and copies ran while one was open for 0% of the time, Pallas kernels for 18%

profile of v5, /device:TPU:0, one launch (start us, length us, event | category | flops | bytes accessed | tf_op | source)
XLA Modules:
  0.0 34.6 jit_solution(14834732289109063656)
XLA Ops:
  0.0 0.8 %shard_map.92.refs_0_.refs_8_ = bf16[64,512]{1,0:T(8,128)(2,1)S(1)} custom-call(bf16[32,512]{1,0:T(8,128)(2,1)} %in_hbm.1, bf16[32,512]{1,0:T(8,128)(2,1)} %out_hbm.1), custom_call_target="tpu_custom_call" | custom-call | bytes 65536 | tf_op jit(solution)/shard_map/pallas_call | solution.py:328
  0.8 5.1 %collective-permute-start.2 = (bf16[64,512]{1,0:T(8,128)(2,1)S(1)}, bf16[64,512]{1,0:T(8,128)(2,1)S(1)}, u32[]{:S(2)}, u32[]{:S(2)}) collective-permute-start(bf16[64,512]{1,0:T(8,128)(2,1)S(1)} %shard_map.92.refs_0_.refs_8_), channel_id=1, source_target_pairs={{0,3},{1,2},{2,1},{3,0},{4,7},{5,6},{6,5},{7,4},{8,11},{9,10},{10,... | collective-permute-start | bytes 196616 | tf_op jit(solution)/shard_map/ppermute | solution.py:344
  5.9 0.0 collective-permute-start.1
  5.9 0.6 %collective-permute-start = (bf16[64,512]{1,0:T(8,128)(2,1)S(1)}, bf16[64,512]{1,0:T(8,128)(2,1)S(1)}, u32[]{:S(2)}, u32[]{:S(2)}) collective-permute-start(bf16[64,512]{1,0:T(8,128)(2,1)S(1)} %shard_map.92.refs_0_.refs_8_), channel_id=1, source_target_pairs={{0,1},{1,0},{2,3},{3,2},{4,5},{5,4},{6,7},{7,6},{8,9},{9,8},{10,11... | collective-permute-start | bytes 196616 | tf_op jit(solution)/shard_map/ppermute | solution.py:344
  6.6 1.7 %shard_map.91 = (bf16[512,1024]{1,0:T(8,128)(2,1)S(1)}, f32[16,512]{1,0:T(8,128)S(1)}) custom-call(bf16[512,1024]{1,0:T(8,128)(2,1)} %refs_0_.1, f32[16,512]{1,0:T(8,128)} %step_hbm.1, f32[1,16]{1,0:T(1,128)} %bitcast.5), custom_call_target="tpu_custom_call" | custom-call | flops 268435456 | bytes 2097152 | tf_op jit(solution)/shard_map/pallas_call | solution.py:328
  8.3 0.2 collective-permute-done.2.refs_3_.refs_11_
  8.5 3.0 %collective-permute-done.1.refs_2_.refs_10_ = bf16[64,512]{1,0:T(8,128)(2,1)S(1)} collective-permute-done((bf16[64,512]{1,0:T(8,128)(2,1)S(1)}, bf16[64,512]{1,0:T(8,128)(2,1)S(1)}, u32[]{:S(2)}, u32[]{:S(2)}) %collective-permute-start.1) | collective-permute-done | bytes 65568 | tf_op jit(solution)/shard_map/ppermute | solution.py:344
  11.5 0.0 collective-permute-done.refs_1_.refs_9_
  11.5 0.3 shard_map.93
  11.8 0.1 collective-permute-start.3
  11.9 1.6 %collective-permute-done.3.theirs_ref.refs_7_.refs_4_ = bf16[144,1024]{1,0:T(8,128)(2,1)S(1)} collective-permute-done((bf16[144,1024]{1,0:T(8,128)(2,1)S(1)}, bf16[144,1024]{1,0:T(8,128)(2,1)S(1)}, u32[]{:S(2)}, u32[]{:S(2)}) %collective-permute-start.3) | collective-permute-done | bytes 294944 | tf_op jit(solution)/shard_map/ppermute | solution.py:344
  13.5 0.1 shard_map.94.refs_6_
  13.6 2.5 %collective-permute-start.6 = (bf16[144,512]{1,0:T(8,128)(2,1)S(1)}, bf16[144,512]{1,0:T(8,128)(2,1)S(1)}, u32[]{:S(2)}, u32[]{:S(2)}) collective-permute-start(bf16[144,512]{1,0:T(8,128)(2,1)S(1)} %shard_map.94.refs_6_), channel_id=1, source_target_pairs={{0,24},{4,28},{8,16},{12,20},{16,8},{20,12},{24,0},{28,4},{1,25},{... | collective-permute-start | bytes 442376 | tf_op jit(solution)/shard_map/ppermute | solution.py:344
  16.1 0.5 %collective-permute-start.5 = (bf16[144,512]{1,0:T(8,128)(2,1)S(1)}, bf16[144,512]{1,0:T(8,128)(2,1)S(1)}, u32[]{:S(2)}, u32[]{:S(2)}) collective-permute-start(bf16[144,512]{1,0:T(8,128)(2,1)S(1)} %shard_map.94.refs_6_), channel_id=1, source_target_pairs={{0,16},{4,20},{8,24},{12,28},{16,0},{20,4},{24,8},{28,12},{1,17},{... | collective-permute-start | bytes 442376 | tf_op jit(solution)/shard_map/ppermute | solution.py:344
  16.6 0.5 %collective-permute-start.4 = (bf16[144,512]{1,0:T(8,128)(2,1)S(1)}, bf16[144,512]{1,0:T(8,128)(2,1)S(1)}, u32[]{:S(2)}, u32[]{:S(2)}) collective-permute-start(bf16[144,512]{1,0:T(8,128)(2,1)S(1)} %shard_map.94.refs_6_), channel_id=1, source_target_pairs={{0,8},{4,12},{8,0},{12,4},{16,24},{20,28},{24,16},{28,20},{1,9},{5... | collective-permute-start | bytes 442376 | tf_op jit(solution)/shard_map/ppermute | solution.py:344
  17.1 3.9 %shard_map.95 = (f32[512,1024]{1,0:T(8,128)S(1)}, bf16[2,512,1024]{2,1,0:T(8,128)(2,1)S(1)}, bf16[512,128]{1,0:T(8,128)(2,1)S(1)}) custom-call(bf16[512,1024]{1,0:T(8,128)(2,1)} %refs_0_.1, bf16[512,1024]{1,0:T(8,128)(2,1)} %refs_1_.1, f32[9,16,512]{2,1,0:T(8,128)} %refs_2_.1, f32[1,16]{1,0:T(1,128)} %bitcast.6, ...), custom_call_target="tpu_custom_call" | custom-call | flops 2147483648 | bytes 8388608 | tf_op jit(solution)/shard_map/pallas_call | solution.py:328
  21.1 0.0 collective-permute-done.6.diagonal_ref
  21.1 2.5 %collective-permute-done.5.y_ref = bf16[144,512]{1,0:T(8,128)(2,1)S(1)} collective-permute-done((bf16[144,512]{1,0:T(8,128)(2,1)S(1)}, bf16[144,512]{1,0:T(8,128)(2,1)S(1)}, u32[]{:S(2)}, u32[]{:S(2)}) %collective-permute-start.5) | collective-permute-done | bytes 147488 | tf_op jit(solution)/shard_map/ppermute | solution.py:344
  23.6 0.1 collective-permute-done.4.x_ref
  23.7 0.1 shard_map.96.refs_5_
  23.8 0.1 collective-permute-start.7
  23.9 0.0 copy-done
  23.9 0.5 %shard_map.97 = (f32[512,512]{1,0:T(8,128)S(1)}, f32[512,128]{1,0:T(8,128)S(1)}) custom-call(bf16[512,128]{1,0:T(8,128)(2,1)S(1)} %get-tuple-element.25.refs_0_, f32[512,1024]{1,0:T(8,128)S(1)} %get-tuple-element.28.refs_1_, bf16[2,512,1024]{2,1,0:T(8,128)(2,1)S(1)} %get-tuple-element.29.refs_2_, f32[1,1024]{1,0:T(1,128)S(1)} %bitcast.3, ...), custom_call_target="tpu_custom_call" | custom-call | flops 536870912 | bytes 3145728 | tf_op jit(solution)/shard_map/pallas_call | solution.py:328
  24.4 1.0 %collective-permute-done.7.refs_5_ = bf16[256,512]{1,0:T(8,128)(2,1)S(1)} collective-permute-done((bf16[256,512]{1,0:T(8,128)(2,1)S(1)}, bf16[256,512]{1,0:T(8,128)(2,1)S(1)}, u32[]{:S(2)}, u32[]{:S(2)}) %collective-permute-start.7) | collective-permute-done | bytes 262176 | tf_op jit(solution)/shard_map/ppermute | solution.py:344
  25.4 0.7 %shard_map.98 = (f32[512,512]{1,0:T(8,128)S(1)}, f32[1,512]{1,0:T(1,128)S(1)}) custom-call(bf16[512,128]{1,0:T(8,128)(2,1)S(1)} %get-tuple-element.25.refs_0_, f32[512,1024]{1,0:T(8,128)S(1)} %get-tuple-element.28.refs_1_, bf16[2,512,1024]{2,1,0:T(8,128)(2,1)S(1)} %get-tuple-element.29.refs_2_, f32[1,1024]{1,0:T(1,128)S(1)} %bitcast.4, ...), custom_call_target="tpu_custom_call" | custom-call | flops 536870912 | bytes 3145728 | tf_op jit(solution)/shard_map/pallas_call | solution.py:328
  26.1 2.7 %collective-permute-start.10 = (f32[1,512]{1,0:T(1,128)S(1)}, f32[1,512]{1,0:T(1,128)S(1)}, u32[]{:S(2)}, u32[]{:S(2)}) collective-permute-start(f32[1,512]{1,0:T(1,128)S(1)} %get-tuple-element.34.refs_0_), channel_id=1, source_target_pairs={{0,3},{1,2},{2,1},{3,0},{4,7},{5,6},{6,5},{7,4},{8,11},{9,10},{10,... | collective-permute-start | bytes 6152 | tf_op jit(solution)/shard_map/ppermute | solution.py:344
  28.8 0.0 collective-permute-start.9
  28.8 1.7 %collective-permute-start.8 = (f32[1,512]{1,0:T(1,128)S(1)}, f32[1,512]{1,0:T(1,128)S(1)}, u32[]{:S(2)}, u32[]{:S(2)}) collective-permute-start(f32[1,512]{1,0:T(1,128)S(1)} %get-tuple-element.34.refs_0_), channel_id=1, source_target_pairs={{0,1},{1,0},{2,3},{3,2},{4,5},{5,4},{6,7},{7,6},{8,9},{9,8},{10,11... | collective-permute-start | bytes 6152 | tf_op jit(solution)/shard_map/ppermute | solution.py:344
  30.5 1.0 %collective-permute-done.10.refs_3_ = f32[1,512]{1,0:T(1,128)S(1)} collective-permute-done((f32[1,512]{1,0:T(1,128)S(1)}, f32[1,512]{1,0:T(1,128)S(1)}, u32[]{:S(2)}, u32[]{:S(2)}) %collective-permute-start.10) | collective-permute-done | bytes 2080 | tf_op jit(solution)/shard_map/ppermute | solution.py:344
  31.5 1.8 %collective-permute-done.9.refs_2_ = f32[1,512]{1,0:T(1,128)S(1)} collective-permute-done((f32[1,512]{1,0:T(1,128)S(1)}, f32[1,512]{1,0:T(1,128)S(1)}, u32[]{:S(2)}, u32[]{:S(2)}) %collective-permute-start.9) | collective-permute-done | bytes 2080 | tf_op jit(solution)/shard_map/ppermute | solution.py:344
  33.3 0.0 collective-permute-done.8.refs_1_
  33.3 1.3 %shard_map.99 = bf16[512,1024]{1,0:T(8,128)(2,1)} custom-call(f32[1,512]{1,0:T(1,128)S(1)} %get-tuple-element.34.refs_0_, f32[1,512]{1,0:T(1,128)S(1)} %collective-permute-done.8.refs_1_, f32[1,512]{1,0:T(1,128)S(1)} %collective-permute-done.9.refs_2_, f32[1,512]{1,0:T(1,128)S(1)} %collective-permute-done.10.refs_3_, ...), custom_call_target="tpu_custom_call" | custom-call | flops 268435456 | bytes 3145728 | tf_op jit(solution)/shard_map/pallas_call | solution.py:328
  (1 shorter events, 0.0 us)
Async XLA Ops:
  0.8 7.7 %collective-permute-start.2 = (bf16[64,512]{1,0:T(8,128)(2,1)S(1)}, bf16[64,512]{1,0:T(8,128)(2,1)S(1)}, u32[]{:S(2)}, u32[]{:S(2)}) collective-permute-start(bf16[64,512]{1,0:T(8,128)(2,1)S(1)} %shard_map.92.refs_0_.refs_8_), channel_id=1, source_target_pairs={{0,3},{1,2},{2,1},{3,0},{4,7},{5,6},{6,5},{7,4},{8,11},{9,10},{10,... | collective-permute-start | bytes 196616 | tf_op jit(solution)/shard_map/ppermute | solution.py:344
  5.9 5.6 %collective-permute-start.1 = (bf16[64,512]{1,0:T(8,128)(2,1)S(1)}, bf16[64,512]{1,0:T(8,128)(2,1)S(1)}, u32[]{:S(2)}, u32[]{:S(2)}) collective-permute-start(bf16[64,512]{1,0:T(8,128)(2,1)S(1)} %shard_map.92.refs_0_.refs_8_), channel_id=1, source_target_pairs={{0,2},{1,3},{2,0},{3,1},{4,6},{5,7},{6,4},{7,5},{8,10},{9,11},{10,... | collective-permute-start | bytes 196616 | tf_op jit(solution)/shard_map/ppermute | solution.py:344
  5.9 5.6 %collective-permute-start = (bf16[64,512]{1,0:T(8,128)(2,1)S(1)}, bf16[64,512]{1,0:T(8,128)(2,1)S(1)}, u32[]{:S(2)}, u32[]{:S(2)}) collective-permute-start(bf16[64,512]{1,0:T(8,128)(2,1)S(1)} %shard_map.92.refs_0_.refs_8_), channel_id=1, source_target_pairs={{0,1},{1,0},{2,3},{3,2},{4,5},{5,4},{6,7},{7,6},{8,9},{9,8},{10,11... | collective-permute-start | bytes 196616 | tf_op jit(solution)/shard_map/ppermute | solution.py:344
  11.8 1.6 %collective-permute-start.3 = (bf16[144,1024]{1,0:T(8,128)(2,1)S(1)}, bf16[144,1024]{1,0:T(8,128)(2,1)S(1)}, u32[]{:S(2)}, u32[]{:S(2)}) collective-permute-start(bf16[144,1024]{1,0:T(8,128)(2,1)S(1)} %get-tuple-element.23.mine_ref), channel_id=1, source_target_pairs={{0,4},{4,0},{8,12},{12,8},{16,20},{20,16},{24,28},{28,24},{1,5},{5... | collective-permute-start | bytes 884744 | tf_op jit(solution)/shard_map/ppermute | solution.py:344
  13.6 7.5 %collective-permute-start.6 = (bf16[144,512]{1,0:T(8,128)(2,1)S(1)}, bf16[144,512]{1,0:T(8,128)(2,1)S(1)}, u32[]{:S(2)}, u32[]{:S(2)}) collective-permute-start(bf16[144,512]{1,0:T(8,128)(2,1)S(1)} %shard_map.94.refs_6_), channel_id=1, source_target_pairs={{0,24},{4,28},{8,16},{12,20},{16,8},{20,12},{24,0},{28,4},{1,25},{... | collective-permute-start | bytes 442376 | tf_op jit(solution)/shard_map/ppermute | solution.py:344
  16.1 7.5 %collective-permute-start.5 = (bf16[144,512]{1,0:T(8,128)(2,1)S(1)}, bf16[144,512]{1,0:T(8,128)(2,1)S(1)}, u32[]{:S(2)}, u32[]{:S(2)}) collective-permute-start(bf16[144,512]{1,0:T(8,128)(2,1)S(1)} %shard_map.94.refs_6_), channel_id=1, source_target_pairs={{0,16},{4,20},{8,24},{12,28},{16,0},{20,4},{24,8},{28,12},{1,17},{... | collective-permute-start | bytes 442376 | tf_op jit(solution)/shard_map/ppermute | solution.py:344
  16.6 7.1 %collective-permute-start.4 = (bf16[144,512]{1,0:T(8,128)(2,1)S(1)}, bf16[144,512]{1,0:T(8,128)(2,1)S(1)}, u32[]{:S(2)}, u32[]{:S(2)}) collective-permute-start(bf16[144,512]{1,0:T(8,128)(2,1)S(1)} %shard_map.94.refs_6_), channel_id=1, source_target_pairs={{0,8},{4,12},{8,0},{12,4},{16,24},{20,28},{24,16},{28,20},{1,9},{5... | collective-permute-start | bytes 442376 | tf_op jit(solution)/shard_map/ppermute | solution.py:344
  17.1 6.8 %copy-start = (f32[1024]{0:T(1024)S(1)}, f32[1024]{0:T(1024)}, u32[]{:S(2)}) copy-start(f32[1024]{0:T(1024)} %param.17) | copy-start | bytes 12292
  23.8 1.6 %collective-permute-start.7 = (bf16[256,512]{1,0:T(8,128)(2,1)S(1)}, bf16[256,512]{1,0:T(8,128)(2,1)S(1)}, u32[]{:S(2)}, u32[]{:S(2)}) collective-permute-start(bf16[256,512]{1,0:T(8,128)(2,1)S(1)} %shard_map.96.refs_5_), channel_id=1, source_target_pairs={{0,4},{4,0},{8,12},{12,8},{16,20},{20,16},{24,28},{28,24},{1,5},{5... | collective-permute-start | bytes 786440 | tf_op jit(solution)/shard_map/ppermute | solution.py:344
  26.1 5.4 %collective-permute-start.10 = (f32[1,512]{1,0:T(1,128)S(1)}, f32[1,512]{1,0:T(1,128)S(1)}, u32[]{:S(2)}, u32[]{:S(2)}) collective-permute-start(f32[1,512]{1,0:T(1,128)S(1)} %get-tuple-element.34.refs_0_), channel_id=1, source_target_pairs={{0,3},{1,2},{2,1},{3,0},{4,7},{5,6},{6,5},{7,4},{8,11},{9,10},{10,... | collective-permute-start | bytes 6152 | tf_op jit(solution)/shard_map/ppermute | solution.py:344
  28.8 4.5 %collective-permute-start.9 = (f32[1,512]{1,0:T(1,128)S(1)}, f32[1,512]{1,0:T(1,128)S(1)}, u32[]{:S(2)}, u32[]{:S(2)}) collective-permute-start(f32[1,512]{1,0:T(1,128)S(1)} %get-tuple-element.34.refs_0_), channel_id=1, source_target_pairs={{0,2},{1,3},{2,0},{3,1},{4,6},{5,7},{6,4},{7,5},{8,10},{9,11},{10,... | collective-permute-start | bytes 6152 | tf_op jit(solution)/shard_map/ppermute | solution.py:344
  28.8 4.5 %collective-permute-start.8 = (f32[1,512]{1,0:T(1,128)S(1)}, f32[1,512]{1,0:T(1,128)S(1)}, u32[]{:S(2)}, u32[]{:S(2)}) collective-permute-start(f32[1,512]{1,0:T(1,128)S(1)} %get-tuple-element.34.refs_0_), channel_id=1, source_target_pairs={{0,1},{1,0},{2,3},{3,2},{4,5},{5,4},{6,7},{7,6},{8,9},{9,8},{10,11... | collective-permute-start | bytes 6152 | tf_op jit(solution)/shard_map/ppermute | solution.py:344

commit v6 on v5

--- a/solution.py
+++ b/solution.py
@@ -62,13 +62,18 @@
     return jnp.sum(jnp.where(at, row, 0.0), axis=1, keepdims=True)
 
 
-def map_rows(map_refs, which):
+def map_rows(maps):
+    if all(rows.shape[0] % 16 == 0 for rows in maps):
+        return jnp.concatenate([rows[...] for rows in maps], axis=0)
+    return jnp.concatenate([rows[...].astype(f32) for rows in maps], axis=0).astype(bf16)
+
+
+def in_map_rows(map_refs):
     rows = map_refs[0].shape[0] // 2
-    picked = []
-    for ref in map_refs:
-        maps = ref[...] if rows % 16 == 0 else ref[...].astype(f32)
-        picked.append(maps[which * rows : (which + 1) * rows])
-    return jnp.concatenate(picked, axis=0).astype(bf16)
+    others = map_refs[:1:-1]
+    if rows % 16 == 0:
+        return map_rows([map_refs[0].at[:rows], map_refs[1].at[:rows], *others])
+    return map_rows([map_refs[0][...].astype(f32)[:rows], map_refs[1][...].astype(f32)[:rows], *others])
 
 
 def fetch(sources, targets, semaphores):
@@ -112,12 +117,18 @@
         copy.wait()
 
 
+def join_kernel(mine_ref, theirs_ref, _, both_ref):
+    rows = mine_ref.shape[0] // 2
+    both_ref[:rows, :] = mine_ref[rows:, :]
+    both_ref[rows:, :] = theirs_ref[rows:, :]
+
+
 def states_kernel(parts, *refs):
     map_refs, (scaled_ref, cum_ref), out_refs = refs[:parts], refs[parts : parts + 2], refs[parts + 2 :]
     shard_ref = out_refs[0]
     heads, tokens = cum_ref.shape
     width = scaled_ref.shape[1]
-    in_map = map_rows(map_refs, 0)
+    in_map = in_map_rows(map_refs)
     size = in_map.shape[0]
     cum = cum_ref[...]
     states, decays = [], []
@@ -154,31 +165,17 @@
     pair_ref[size:, :] = (older[size:] * decay).astype(bf16)
 
 
-def near_kernel(parts, spans, levels, paired, *refs):
-    inputs_hbm, gate_hbm, mix_hbm, skip_hbm = refs[:4]
-    scaled_ref, cum_ref, _, core_ref = refs[4:8]
-    map_refs = refs[8 : 8 + parts]
-    count = 8 + parts + (1 if spans else 0)
-    span_refs = refs[8 + parts : count]
-    near_ref, far_ref, turned_ref, inputs_ref, gate_ref, mix_ref, skip_ref, semaphores = refs[count:]
+def factor_kernel(spans, levels, *refs):
+    inputs_hbm, gate_hbm, mix_hbm, skip_hbm, cum_ref, _ = refs[:6]
+    base_ref, own_ref, far_ref = refs[6:9]
+    span_refs = refs[9:-5]
+    inputs_ref, gate_ref, mix_ref, skip_ref, semaphores = refs[-5:]
     copies = fetch(refs[:4], (inputs_ref, gate_ref, mix_ref, skip_ref), semaphores)
     heads, tokens = cum_ref.shape
-    width = scaled_ref.shape[1]
+    width = inputs_ref.shape[1]
     groups = tokens // GROUP
     first = groups.bit_length()
-    in_map = map_rows(map_refs, 0)
-    out_map = map_rows(map_refs, 1)
-    size = in_map.shape[0]
-    turned_ref[...] = jnp.transpose(out_map)
     expand = expander(heads, width, 2).astype(bf16)
-    row = lax.broadcasted_iota(jnp.int32, (GROUP, GROUP), 0)
-    col = lax.broadcasted_iota(jnp.int32, (GROUP, GROUP), 1)
-    scores = []
-    has_core = lax.rem(lax.axis_index("seq"), 2) == 1
-    for group in range(groups):
-        at = group_slice(group)
-        all_scores = transposed_dot(out_map[:, at], in_map[:, at])
-        scores.append(jnp.where(row >= col, all_scores, 0.0).astype(bf16))
     for copy in copies:
         copy.wait()
     skip = head_row(heads, width, column_of(skip_ref[...]))
@@ -187,42 +184,66 @@
         at = group_slice(group)
         cum = cum_ref[:, at]
         decay = jnp.exp(cum)
-        mixes = [two_parts(mix_ref[0, :, at] * decay)]
-        states = []
-        for index, (later, bit, _, _) in enumerate(spans):
-            if later == group:
-                mixes.append(two_parts(mix_ref[1 + bit, :, at] * decay))
-                states.append(slice(index * size, (index + 1) * size))
+        own_mix = two_parts(mix_ref[0, :, at] * decay)
+        span_mixes = [
+            (index, two_parts(mix_ref[1 + bit, :, at] * decay))
+            for index, (later, bit, _, _) in enumerate(spans)
+            if later == group
+        ]
         decay = jnp.exp(cum + before)
         before = before + cum[:, GROUP - 1 : GROUP]
         far_mixes = [two_parts(mix_ref[first + level, :, at] * decay) for level in range(levels)]
-        if paired:
-            core_mix, *far_mixes = far_mixes
         for cols in blocks_of(width):
-            own = jnp.dot(scores[group], scaled_ref[at, cols], preferred_element_type=f32)
-            total = transposed_dot(mixes[0], expand[:, cols]) * own
-            for mix, rows in zip(mixes[1:], states):
-                reach = jnp.dot(turned_ref[at, :], span_refs[0][rows, cols], preferred_element_type=f32)
-                total = total + transposed_dot(mix, expand[:, cols]) * reach
-            if paired:
-                reach = jnp.dot(turned_ref[at, :], core_ref[:size, cols], preferred_element_type=f32)
-                reach = jnp.where(has_core, reach, 0.0)
-                total = total + transposed_dot(core_mix, expand[:, cols]) * reach
-            total = total + skip[:, cols] * inputs_ref[at, cols].astype(f32)
             gate = gate_ref[at, cols].astype(f32)
             swish = gate / (1.0 + jnp.exp(-gate))
-            near_ref[at, cols] = total * swish
+            base_ref[at, cols] = skip[:, cols] * inputs_ref[at, cols].astype(f32) * swish
+            own_ref[at, cols] = transposed_dot(own_mix, expand[:, cols]) * swish
             for level, mix in enumerate(far_mixes):
                 far_ref[level, at, cols] = (transposed_dot(mix, expand[:, cols]) * swish).astype(bf16)
-
-
-def far_body(turned_ref, near_ref, far_ref, gain_ref, start, columns, state_of, gated_ref):
-    levels, tokens, _ = far_ref.shape
+            for index, mix in span_mixes:
+                span_refs[0][index, :, cols] = (transposed_dot(mix, expand[:, cols]) * swish).astype(bf16)
+
+
+def near_kernel(parts, spans, paired, *refs):
+    base_ref, own_ref, far_ref, core_ref, scaled_ref = refs[:5]
+    count = 5 + parts + parts // 2
+    in_refs, out_refs = refs[5 : 5 + parts], refs[5 + parts : count]
+    span_refs = refs[count:-2]
+    near_ref, turned_ref = refs[-2:]
+    tokens, width = base_ref.shape
+    in_map = in_map_rows(in_refs)
+    turned = jnp.transpose(map_rows([out_refs[0], *out_refs[:0:-1]]))
+    turned_ref[...] = turned
+    size = in_map.shape[0]
+    row = lax.broadcasted_iota(jnp.int32, (GROUP, GROUP), 0)
+    col = lax.broadcasted_iota(jnp.int32, (GROUP, GROUP), 1)
+    has_core = lax.rem(lax.axis_index("seq"), 2) == 1
+    for group in range(tokens // GROUP):
+        at = group_slice(group)
+        scores = jnp.dot(turned[at], in_map[:, at], preferred_element_type=f32)
+        scores = jnp.where(row >= col, scores, 0.0).astype(bf16)
+        for cols in blocks_of(width):
+            own = jnp.dot(scores, scaled_ref[at, cols], preferred_element_type=f32)
+            total = base_ref[at, cols] + own_ref[at, cols] * own
+            for index, (later, _, _, _) in enumerate(spans):
+                if later == group:
+                    rows = slice(index * size, (index + 1) * size)
+                    reach = jnp.dot(turned[at], span_refs[0][rows, cols], preferred_element_type=f32)
+                    total = total + span_refs[1][index, :, cols].astype(f32) * reach
+            if paired:
+                reach = jnp.dot(turned[at], core_ref[:size, cols], preferred_element_type=f32)
+                reach = jnp.where(has_core, reach, 0.0)
+                total = total + far_ref[0, at, cols].astype(f32) * reach
+            near_ref[at, cols] = total
+
+
+def far_body(turned_ref, near_ref, far_ref, gain_ref, start, columns, levels, state_of, gated_ref):
+    tokens = far_ref.shape[1]
     squares = jnp.zeros((tokens, 128), f32)
     for cols in blocks_of(columns):
         at = pl.ds(pl.multiple_of(start + cols.start, BLOCK), BLOCK)
         total = near_ref[:, at]
-        for level in range(levels):
+        for level in levels:
             state = state_of(level, cols, at).astype(bf16)
             reach = jnp.dot(turned_ref[...], state, preferred_element_type=f32)
             total = total + far_ref[level, :, at].astype(f32) * reach
@@ -249,7 +270,9 @@
         return state_refs[level][:, cols]
 
     width = near_ref.shape[1]
-    sums_ref[...] = row_sums(far_body(turned_ref, near_ref, far_ref, gain_ref, 0, width, state_of, gated_ref))
+    levels = range(far_ref.shape[0])
+    squares = far_body(turned_ref, near_ref, far_ref, gain_ref, 0, width, levels, state_of, gated_ref)
+    sums_ref[...] = row_sums(squares)
 
 
 def combine_kernel(size, x_ref, y_ref, diagonal_ref, spans_ref):
@@ -283,9 +306,9 @@
     def state_of(level, cols, at):
         core_decay = core_ref[size:, at].astype(f32)[:1]
         running = jnp.where(core == 1, core_decay, 1.0)
-        return spans_ref[level * size : (level + 1) * size, cols].astype(f32) * running
-
-    squares = far_body(turned_ref, near_ref, far_ref, gain_ref, start, half, state_of, gated_ref)
+        return spans_ref[(level - 1) * size : level * size, cols].astype(f32) * running
+
+    squares = far_body(turned_ref, near_ref, far_ref, gain_ref, start, half, (1, 2), state_of, gated_ref)
     sums_ref[...] = squares if own else row_sums(squares + refs[6][...])
 
 
@@ -344,8 +367,9 @@
     return lax.ppermute(array, axis, [(i, i ^ mask) for i in range(lax.axis_size(axis))])
 
 
-def from_each(array, axis):
-    return [array] + [flip(array, axis, mask) for mask in range(1, lax.axis_size(axis))]
+def from_each(array, axis, first=1, stride=1):
+    masks = range(first, lax.axis_size(axis), stride)
+    return [flip(array, axis, mask) for mask in reversed(masks)]
 
 
 def merged(older, newer, size):
@@ -378,6 +402,7 @@
     spans = local_spans(groups)
     dense = 2 * tokens * GROUP * width
     area = tokens * width
+    others = from_each(input_map, "head", first=2)
     rows = input_map.shape[0]
     if rows % 16 == 0:
         maps = call(
@@ -390,12 +415,13 @@
         )
     else:
         maps = jnp.concatenate([input_map, output_map], axis=0)
-    maps = from_each(maps, "head")
+    near_maps = flip(maps, "head", 1)
+    in_maps = [maps, near_maps, *others]
     scaled, cum = call(
         prepare_kernel,
         (shaped((tokens, width), bf16), shaped((heads, tokens), f32)),
         (inputs, step, decay_rate[None, :]),
-        flops=dense,
+        flops=16 * dense,
         bytes_accessed=4 * area,
         hbm=3,
     )
@@ -404,7 +430,7 @@
     shard, *span_states = call(
         functools.partial(states_kernel, parts),
         (shard_shape, *span_shape),
-        (*maps, scaled, cum),
+        (*in_maps, scaled, cum),
         flops=dense,
         bytes_accessed=4 * area,
     )
@@ -419,31 +445,44 @@
         )
     else:
         message = shard
-    near_levels = levels - 1 if pairs else levels
-    near, far, turned = call(
-        functools.partial(near_kernel, parts, spans, levels, pairs),
+    if rows % 16 == 0:
+        both = call(
+            join_kernel, shaped((2 * rows, tokens), bf16), (maps, near_maps, shard), bytes_accessed=8 * rows * tokens
+        )
+    else:
+        both = jnp.concatenate([maps[rows:], near_maps[rows:]], axis=0)
+    out_maps = [both, *from_each(both, "head", first=2, stride=2)]
+    factor_shape = [shaped((len(spans), GROUP, width), bf16)] if spans else []
+    base, own_factor, far, *span_factors = call(
+        functools.partial(factor_kernel, spans, levels),
         (
-            shaped((tokens, width), f32),
-            shaped((near_levels, tokens, width), bf16),
-            shaped((tokens, size), bf16),
+            *(shaped((tokens, width), f32), shaped((tokens, width), f32)),
+            *(shaped((levels, tokens, width), bf16), *factor_shape),
         ),
-        (
-            *(inputs, gate, level_mix, skip[None, :], scaled, cum, message, theirs if pairs else message),
-            *(*maps, *span_states),
-        ),
+        (inputs, gate, level_mix, skip[None, :], cum, message),
         flops=8 * dense,
         bytes_accessed=16 * area,
         hbm=4,
     )
+    near, turned = call(
+        functools.partial(near_kernel, parts, spans, pairs),
+        (shaped((tokens, width), f32), shaped((tokens, size), bf16)),
+        (
+            *(base, own_factor, far, theirs if pairs else message, scaled),
+            *(*in_maps, *out_maps, *span_states, *span_factors),
+        ),
+        flops=4 * dense,
+        bytes_accessed=16 * area,
+    )
     gain = norm_gain[None, :]
     sums_shape = shaped((1, tokens), f32)
     if pairs:
-        received = [flip(message, "seq", mask) for mask in (2, 4, 6)]
+        received = [flip(message, "seq", mask) for mask in (6, 4, 2)]
         *received, near, far = lax.optimization_barrier((*received, near, far))
         own = call(
             functools.partial(combine_kernel, size),
             shaped((2 * size, width // 2), bf16),
-            received,
+            received[::-1],
             bytes_accessed=area,
         )
         other = flip(own, "seq", 1)
@@ -471,7 +510,8 @@
             flops=4 * dense,
             bytes_accessed=12 * area,
         )
-    last = from_each(sums, "head")
+    *last, nearest = [sums, *from_each(sums, "head")]
+    last = [nearest, *last]
     return call(
         functools.partial(norm_kernel, len(last), width * parts),
         shaped((tokens, width), bf16),

time: 34.8 us -> 33.7 us (0.968)
  waiting for transfers between devices: 11.2 us -> 6.87 us
  starting transfers between devices: 13.9 us -> 16.4 us
  Pallas kernels: 9.46 us -> 10.1 us
    ppermute x11 -> x12, waiting for transfers between devices: 11.2 us -> 6.87 us  [flip(): lax.ppermute(array, axis, [(i, i ^ mask) for i in range(lax.axis_size(axi...]
    ppermute x11 -> x12, starting transfers between devices: 13.9 us -> 16.4 us  [flip(): lax.ppermute(array, axis, [(i, i ^ mask) for i in range(lax.axis_size(axi...]
    pallas_call x9 -> x11, Pallas kernels: 9.46 us -> 10.1 us  [call(): pl.pallas_call(kernel, out_shape=out_shape, in_specs=specs, out_specs=jax...]
  transfers between devices with their start and end apart: 11 -> 12, of which waited for: 8 -> 7; matrix products, arithmetic and copies ran while one was open for 0% -> 0% of each run, Pallas kernels for 18% -> 23%
where the time goes in v6:
time: 33.7 us; the launch traced here: 33.5 us
  starting transfers between devices  16.4 us (49%)
  Pallas kernels  10.1 us (30%)
  waiting for transfers between devices  6.87 us (20%)
    ppermute x12, starting transfers between devices, flip(): lax.ppermute(array, axis, [(i, i ^ mask) for i in range(lax.axis_size(axi...  16.4 us
    pallas_call x11, Pallas kernels, call(): pl.pallas_call(kernel, out_shape=out_shape, in_specs=specs, out_specs=jax...  10.1 us
    ppermute x12, waiting for transfers between devices, flip(): lax.ppermute(array, axis, [(i, i ^ mask) for i in range(lax.axis_size(axi...  6.87 us
  transfers between devices with their start and end apart: 12, of which 7 were waited for; matrix products, arithmetic and copies ran while one was open for 0% of the time, Pallas kernels for 23%

profile of v6, /device:TPU:0, one launch (start us, length us, event | category | flops | bytes accessed | tf_op | source)
XLA Modules:
  0.0 33.5 jit_solution(7706788887249304489)
XLA Ops:
  0.0 5.0 %collective-permute-start.1 = (bf16[32,512]{1,0:T(8,128)(2,1)}, bf16[32,512]{1,0:T(8,128)(2,1)S(1)}, u32[]{:S(2)}, u32[]{:S(2)}) collective-permute-start(bf16[32,512]{1,0:T(8,128)(2,1)} %in_hbm.1), channel_id=1, source_target_pairs={{0,3},{1,2},{2,1},{3,0},{4,7},{5,6},{6,5},{7,4},{8,11},{9,10},{10,... | collective-permute-start | bytes 98312 | tf_op jit(solution)/shard_map/ppermute | solution.py:367
  5.0 0.0 collective-permute-start.2
  5.1 0.8 %shard_map.92.refs_0_.mine_ref.refs_5_ = bf16[64,512]{1,0:T(8,128)(2,1)S(1)} custom-call(bf16[32,512]{1,0:T(8,128)(2,1)} %in_hbm.1, bf16[32,512]{1,0:T(8,128)(2,1)} %out_hbm.1), custom_call_target="tpu_custom_call" | custom-call | bytes 65536 | tf_op jit(solution)/shard_map/pallas_call | solution.py:351
  5.9 0.6 %collective-permute-start = (bf16[64,512]{1,0:T(8,128)(2,1)S(1)}, bf16[64,512]{1,0:T(8,128)(2,1)S(1)}, u32[]{:S(2)}, u32[]{:S(2)}) collective-permute-start(bf16[64,512]{1,0:T(8,128)(2,1)S(1)} %shard_map.92.refs_0_.mine_ref.refs_5_), channel_id=1, source_target_pairs={{0,1},{1,0},{2,3},{3,2},{4,5},{5,4},{6,7},{7,6},{8,9},{9,8},{10,11... | collective-permute-start | bytes 196616 | tf_op jit(solution)/shard_map/ppermute | solution.py:367
  6.5 1.7 %shard_map.91 = (bf16[512,1024]{1,0:T(8,128)(2,1)S(1)}, f32[16,512]{1,0:T(8,128)S(1)}) custom-call(bf16[512,1024]{1,0:T(8,128)(2,1)} %refs_0_.1, f32[16,512]{1,0:T(8,128)} %step_hbm.1, f32[1,16]{1,0:T(1,128)} %bitcast.5), custom_call_target="tpu_custom_call" | custom-call | flops 4294967296 | bytes 2097152 | tf_op jit(solution)/shard_map/pallas_call | solution.py:351
  8.2 0.0 collective-permute-done.1.refs_2_.refs_7_
  8.3 1.9 %collective-permute-done.2.refs_3_.refs_8_ = bf16[32,512]{1,0:T(8,128)(2,1)S(1)} collective-permute-done((bf16[32,512]{1,0:T(8,128)(2,1)}, bf16[32,512]{1,0:T(8,128)(2,1)S(1)}, u32[]{:S(2)}, u32[]{:S(2)}) %collective-permute-start.2) | collective-permute-done | bytes 32800 | tf_op jit(solution)/shard_map/ppermute | solution.py:367
  10.2 0.4 %collective-permute-done.refs_1_.theirs_ref.refs_6_ = bf16[64,512]{1,0:T(8,128)(2,1)S(1)} collective-permute-done((bf16[64,512]{1,0:T(8,128)(2,1)S(1)}, bf16[64,512]{1,0:T(8,128)(2,1)S(1)}, u32[]{:S(2)}, u32[]{:S(2)}) %collective-permute-start) | collective-permute-done | bytes 65568 | tf_op jit(solution)/shard_map/ppermute | solution.py:367
  10.6 0.3 shard_map.93
  10.9 0.1 collective-permute-start.3
  11.0 2.6 %collective-permute-start.4 = (bf16[64,512]{1,0:T(8,128)(2,1)S(1)}, bf16[64,512]{1,0:T(8,128)(2,1)S(1)}, u32[]{:S(2)}, u32[]{:S(2)}) collective-permute-start(bf16[64,512]{1,0:T(8,128)(2,1)S(1)} %shard_map.96.refs_9_), channel_id=1, source_target_pairs={{0,2},{1,3},{2,0},{3,1},{4,6},{5,7},{6,4},{7,5},{8,10},{9,11},{10,... | collective-permute-start | bytes 196616 | tf_op jit(solution)/shard_map/ppermute | solution.py:367
  13.6 0.1 shard_map.94.refs_5_
  13.7 2.5 %collective-permute-start.5 = (bf16[144,512]{1,0:T(8,128)(2,1)S(1)}, bf16[144,512]{1,0:T(8,128)(2,1)S(1)}, u32[]{:S(2)}, u32[]{:S(2)}) collective-permute-start(bf16[144,512]{1,0:T(8,128)(2,1)S(1)} %shard_map.94.refs_5_), channel_id=1, source_target_pairs={{0,24},{4,28},{8,16},{12,20},{16,8},{20,12},{24,0},{28,4},{1,25},{... | collective-permute-start | bytes 442376 | tf_op jit(solution)/shard_map/ppermute | solution.py:367
  16.2 0.5 %collective-permute-start.6 = (bf16[144,512]{1,0:T(8,128)(2,1)S(1)}, bf16[144,512]{1,0:T(8,128)(2,1)S(1)}, u32[]{:S(2)}, u32[]{:S(2)}) collective-permute-start(bf16[144,512]{1,0:T(8,128)(2,1)S(1)} %shard_map.94.refs_5_), channel_id=1, source_target_pairs={{0,16},{4,20},{8,24},{12,28},{16,0},{20,4},{24,8},{28,12},{1,17},{... | collective-permute-start | bytes 442376 | tf_op jit(solution)/shard_map/ppermute | solution.py:367
  16.7 0.5 %collective-permute-start.7 = (bf16[144,512]{1,0:T(8,128)(2,1)S(1)}, bf16[144,512]{1,0:T(8,128)(2,1)S(1)}, u32[]{:S(2)}, u32[]{:S(2)}) collective-permute-start(bf16[144,512]{1,0:T(8,128)(2,1)S(1)} %shard_map.94.refs_5_), channel_id=1, source_target_pairs={{0,8},{4,12},{8,0},{12,4},{16,24},{20,28},{24,16},{28,20},{1,9},{5... | collective-permute-start | bytes 442376 | tf_op jit(solution)/shard_map/ppermute | solution.py:367
  17.2 3.4 %shard_map.95 = (f32[512,1024]{1,0:T(8,128)S(1)}, f32[512,1024]{1,0:T(8,128)S(1)}, bf16[3,512,1024]{2,1,0:T(8,128)(2,1)S(1)}, bf16[1,256,1024]{2,1,0:T(8,128)(2,1)S(1)}) custom-call(bf16[512,1024]{1,0:T(8,128)(2,1)} %refs_0_.1, bf16[512,1024]{1,0:T(8,128)(2,1)} %refs_1_.1, f32[9,16,512]{2,1,0:T(8,128)} %refs_2_.1, f32[1,16]{1,0:T(1,128)} %bitcast.6, ...), custom_call_target="tpu_custom_call" | custom-call | flops 2147483648 | bytes 8388608 | tf_op jit(solution)/shard_map/pallas_call | solution.py:351
  20.7 0.0 copy-start
  20.7 1.1 %shard_map.97 = (f32[512,1024]{1,0:T(8,128)S(1)}, bf16[512,128]{1,0:T(8,128)(2,1)S(1)}) custom-call(f32[512,1024]{1,0:T(8,128)S(1)} %get-tuple-element.27.refs_0_, f32[512,1024]{1,0:T(8,128)S(1)} %get-tuple-element.28.refs_1_, bf16[3,512,1024]{2,1,0:T(8,128)(2,1)S(1)} %get-tuple-element.35.refs_2_, ...), custom_call_target="tpu_custom_call" | custom-call | flops 1073741824 | bytes 8388608 | tf_op jit(solution)/shard_map/pallas_call | solution.py:351
  21.8 1.9 %collective-permute-done.6.y_ref = bf16[144,512]{1,0:T(8,128)(2,1)S(1)} collective-permute-done((bf16[144,512]{1,0:T(8,128)(2,1)S(1)}, bf16[144,512]{1,0:T(8,128)(2,1)S(1)}, u32[]{:S(2)}, u32[]{:S(2)}) %collective-permute-start.6) | collective-permute-done | bytes 147488 | tf_op jit(solution)/shard_map/ppermute | solution.py:367
  23.7 0.1 collective-permute-done.7.x_ref
  23.8 0.1 shard_map.98.refs_5_
  23.9 0.1 collective-permute-start.8
  24.0 0.5 %shard_map.99 = (f32[512,512]{1,0:T(8,128)S(1)}, f32[512,128]{1,0:T(8,128)S(1)}) custom-call(bf16[512,128]{1,0:T(8,128)(2,1)S(1)} %get-tuple-element.32.refs_0_, f32[512,1024]{1,0:T(8,128)S(1)} %get-tuple-element.34.refs_1_, bf16[3,512,1024]{2,1,0:T(8,128)(2,1)S(1)} %get-tuple-element.35.refs_2_, f32[1,1024]{1,0:T(1,128)S(1)} %bitcast.3, ...), custom_call_target="tpu_custom_call" | custom-call | flops 536870912 | bytes 3145728 | tf_op jit(solution)/shard_map/pallas_call | solution.py:351
  24.6 1.0 %collective-permute-done.8.refs_5_ = bf16[256,512]{1,0:T(8,128)(2,1)S(1)} collective-permute-done((bf16[256,512]{1,0:T(8,128)(2,1)S(1)}, bf16[256,512]{1,0:T(8,128)(2,1)S(1)}, u32[]{:S(2)}, u32[]{:S(2)}) %collective-permute-start.8) | collective-permute-done | bytes 262176 | tf_op jit(solution)/shard_map/ppermute | solution.py:367
  25.5 0.7 %shard_map.100 = (f32[512,512]{1,0:T(8,128)S(1)}, f32[1,512]{1,0:T(1,128)S(1)}) custom-call(bf16[512,128]{1,0:T(8,128)(2,1)S(1)} %get-tuple-element.32.refs_0_, f32[512,1024]{1,0:T(8,128)S(1)} %get-tuple-element.34.refs_1_, bf16[3,512,1024]{2,1,0:T(8,128)(2,1)S(1)} %get-tuple-element.35.refs_2_, f32[1,1024]{1,0:T(1,128)S(1)} %bitcast.4, ...), custom_call_target="tpu_custom_call" | custom-call | flops 536870912 | bytes 3145728 | tf_op jit(solution)/shard_map/pallas_call | solution.py:351
  26.2 0.9 %collective-permute-start.10 = (f32[1,512]{1,0:T(1,128)S(1)}, f32[1,512]{1,0:T(1,128)S(1)}, u32[]{:S(2)}, u32[]{:S(2)}) collective-permute-start(f32[1,512]{1,0:T(1,128)S(1)} %get-tuple-element.40.refs_1_), channel_id=1, source_target_pairs={{0,3},{1,2},{2,1},{3,0},{4,7},{5,6},{6,5},{7,4},{8,11},{9,10},{10,... | collective-permute-start | bytes 6152 | tf_op jit(solution)/shard_map/ppermute | solution.py:367
  27.2 0.6 %collective-permute-start.11 = (f32[1,512]{1,0:T(1,128)S(1)}, f32[1,512]{1,0:T(1,128)S(1)}, u32[]{:S(2)}, u32[]{:S(2)}) collective-permute-start(f32[1,512]{1,0:T(1,128)S(1)} %get-tuple-element.40.refs_1_), channel_id=1, source_target_pairs={{0,2},{1,3},{2,0},{3,1},{4,6},{5,7},{6,4},{7,5},{8,10},{9,11},{10,... | collective-permute-start | bytes 6152 | tf_op jit(solution)/shard_map/ppermute | solution.py:367
  27.8 2.9 %collective-permute-start.9 = (f32[1,512]{1,0:T(1,128)S(1)}, f32[1,512]{1,0:T(1,128)S(1)}, u32[]{:S(2)}, u32[]{:S(2)}) collective-permute-start(f32[1,512]{1,0:T(1,128)S(1)} %get-tuple-element.40.refs_1_), channel_id=1, source_target_pairs={{0,1},{1,0},{2,3},{3,2},{4,5},{5,4},{6,7},{7,6},{8,9},{9,8},{10,11... | collective-permute-start | bytes 6152 | tf_op jit(solution)/shard_map/ppermute | solution.py:367
  30.6 1.0 %collective-permute-done.10.refs_2_ = f32[1,512]{1,0:T(1,128)S(1)} collective-permute-done((f32[1,512]{1,0:T(1,128)S(1)}, f32[1,512]{1,0:T(1,128)S(1)}, u32[]{:S(2)}, u32[]{:S(2)}) %collective-permute-start.10) | collective-permute-done | bytes 2080 | tf_op jit(solution)/shard_map/ppermute | solution.py:367
  31.6 0.0 collective-permute-done.11.refs_3_
  31.7 0.5 %collective-permute-done.9.refs_0_ = f32[1,512]{1,0:T(1,128)S(1)} collective-permute-done((f32[1,512]{1,0:T(1,128)S(1)}, f32[1,512]{1,0:T(1,128)S(1)}, u32[]{:S(2)}, u32[]{:S(2)}) %collective-permute-start.9) | collective-permute-done | bytes 2080 | tf_op jit(solution)/shard_map/ppermute | solution.py:367
  32.2 1.3 %shard_map.101 = bf16[512,1024]{1,0:T(8,128)(2,1)} custom-call(f32[1,512]{1,0:T(1,128)S(1)} %collective-permute-done.9.refs_0_, f32[1,512]{1,0:T(1,128)S(1)} %get-tuple-element.40.refs_1_, f32[1,512]{1,0:T(1,128)S(1)} %collective-permute-done.10.refs_2_, f32[1,512]{1,0:T(1,128)S(1)} %collective-permute-done.11.refs_3_, ...), custom_call_target="tpu_custom_call" | custom-call | flops 268435456 | bytes 3145728 | tf_op jit(solution)/shard_map/pallas_call | solution.py:351
  (5 shorter events, 0.0 us)
Async XLA Ops:
  0.0 8.2 %collective-permute-start.1 = (bf16[32,512]{1,0:T(8,128)(2,1)}, bf16[32,512]{1,0:T(8,128)(2,1)S(1)}, u32[]{:S(2)}, u32[]{:S(2)}) collective-permute-start(bf16[32,512]{1,0:T(8,128)(2,1)} %in_hbm.1), channel_id=1, source_target_pairs={{0,3},{1,2},{2,1},{3,0},{4,7},{5,6},{6,5},{7,4},{8,11},{9,10},{10,... | collective-permute-start | bytes 98312 | tf_op jit(solution)/shard_map/ppermute | solution.py:367
  5.0 5.1 %collective-permute-start.2 = (bf16[32,512]{1,0:T(8,128)(2,1)}, bf16[32,512]{1,0:T(8,128)(2,1)S(1)}, u32[]{:S(2)}, u32[]{:S(2)}) collective-permute-start(bf16[32,512]{1,0:T(8,128)(2,1)} %in_hbm.1), channel_id=1, source_target_pairs={{0,2},{1,3},{2,0},{3,1},{4,6},{5,7},{6,4},{7,5},{8,10},{9,11},{10,... | collective-permute-start | bytes 98312 | tf_op jit(solution)/shard_map/ppermute | solution.py:367
  5.9 4.7 %collective-permute-start = (bf16[64,512]{1,0:T(8,128)(2,1)S(1)}, bf16[64,512]{1,0:T(8,128)(2,1)S(1)}, u32[]{:S(2)}, u32[]{:S(2)}) collective-permute-start(bf16[64,512]{1,0:T(8,128)(2,1)S(1)} %shard_map.92.refs_0_.mine_ref.refs_5_), channel_id=1, source_target_pairs={{0,1},{1,0},{2,3},{3,2},{4,5},{5,4},{6,7},{7,6},{8,9},{9,8},{10,11... | collective-permute-start | bytes 196616 | tf_op jit(solution)/shard_map/ppermute | solution.py:367
  10.9 2.7 %collective-permute-start.3 = (bf16[144,1024]{1,0:T(8,128)(2,1)S(1)}, bf16[144,1024]{1,0:T(8,128)(2,1)S(1)}, u32[]{:S(2)}, u32[]{:S(2)}) collective-permute-start(bf16[144,1024]{1,0:T(8,128)(2,1)S(1)} %get-tuple-element.26.mine_ref._), channel_id=1, source_target_pairs={{0,4},{4,0},{8,12},{12,8},{16,20},{20,16},{24,28},{28,24},{1,5},{5... | collective-permute-start | bytes 884744 | tf_op jit(solution)/shard_map/ppermute | solution.py:367
  11.0 9.7 %collective-permute-start.4 = (bf16[64,512]{1,0:T(8,128)(2,1)S(1)}, bf16[64,512]{1,0:T(8,128)(2,1)S(1)}, u32[]{:S(2)}, u32[]{:S(2)}) collective-permute-start(bf16[64,512]{1,0:T(8,128)(2,1)S(1)} %shard_map.96.refs_9_), channel_id=1, source_target_pairs={{0,2},{1,3},{2,0},{3,1},{4,6},{5,7},{6,4},{7,5},{8,10},{9,11},{10,... | collective-permute-start | bytes 196616 | tf_op jit(solution)/shard_map/ppermute | solution.py:367
  13.7 8.1 %collective-permute-start.5 = (bf16[144,512]{1,0:T(8,128)(2,1)S(1)}, bf16[144,512]{1,0:T(8,128)(2,1)S(1)}, u32[]{:S(2)}, u32[]{:S(2)}) collective-permute-start(bf16[144,512]{1,0:T(8,128)(2,1)S(1)} %shard_map.94.refs_5_), channel_id=1, source_target_pairs={{0,24},{4,28},{8,16},{12,20},{16,8},{20,12},{24,0},{28,4},{1,25},{... | collective-permute-start | bytes 442376 | tf_op jit(solution)/shard_map/ppermute | solution.py:367
  16.2 7.5 %collective-permute-start.6 = (bf16[144,512]{1,0:T(8,128)(2,1)S(1)}, bf16[144,512]{1,0:T(8,128)(2,1)S(1)}, u32[]{:S(2)}, u32[]{:S(2)}) collective-permute-start(bf16[144,512]{1,0:T(8,128)(2,1)S(1)} %shard_map.94.refs_5_), channel_id=1, source_target_pairs={{0,16},{4,20},{8,24},{12,28},{16,0},{20,4},{24,8},{28,12},{1,17},{... | collective-permute-start | bytes 442376 | tf_op jit(solution)/shard_map/ppermute | solution.py:367
  16.7 7.1 %collective-permute-start.7 = (bf16[144,512]{1,0:T(8,128)(2,1)S(1)}, bf16[144,512]{1,0:T(8,128)(2,1)S(1)}, u32[]{:S(2)}, u32[]{:S(2)}) collective-permute-start(bf16[144,512]{1,0:T(8,128)(2,1)S(1)} %shard_map.94.refs_5_), channel_id=1, source_target_pairs={{0,8},{4,12},{8,0},{12,4},{16,24},{20,28},{24,16},{28,20},{1,9},{5... | collective-permute-start | bytes 442376 | tf_op jit(solution)/shard_map/ppermute | solution.py:367
  20.7 3.3 %copy-start = (f32[1024]{0:T(1024)S(1)}, f32[1024]{0:T(1024)}, u32[]{:S(2)}) copy-start(f32[1024]{0:T(1024)} %param.17) | copy-start | bytes 12292
  23.9 1.6 %collective-permute-start.8 = (bf16[256,512]{1,0:T(8,128)(2,1)S(1)}, bf16[256,512]{1,0:T(8,128)(2,1)S(1)}, u32[]{:S(2)}, u32[]{:S(2)}) collective-permute-start(bf16[256,512]{1,0:T(8,128)(2,1)S(1)} %shard_map.98.refs_5_), channel_id=1, source_target_pairs={{0,4},{4,0},{8,12},{12,8},{16,20},{20,16},{24,28},{28,24},{1,5},{5... | collective-permute-start | bytes 786440 | tf_op jit(solution)/shard_map/ppermute | solution.py:367
  26.2 5.4 %collective-permute-start.10 = (f32[1,512]{1,0:T(1,128)S(1)}, f32[1,512]{1,0:T(1,128)S(1)}, u32[]{:S(2)}, u32[]{:S(2)}) collective-permute-start(f32[1,512]{1,0:T(1,128)S(1)} %get-tuple-element.40.refs_1_), channel_id=1, source_target_pairs={{0,3},{1,2},{2,1},{3,0},{4,7},{5,6},{6,5},{7,4},{8,11},{9,10},{10,... | collective-permute-start | bytes 6152 | tf_op jit(solution)/shard_map/ppermute | solution.py:367
  27.2 4.5 %collective-permute-start.11 = (f32[1,512]{1,0:T(1,128)S(1)}, f32[1,512]{1,0:T(1,128)S(1)}, u32[]{:S(2)}, u32[]{:S(2)}) collective-permute-start(f32[1,512]{1,0:T(1,128)S(1)} %get-tuple-element.40.refs_1_), channel_id=1, source_target_pairs={{0,2},{1,3},{2,0},{3,1},{4,6},{5,7},{6,4},{7,5},{8,10},{9,11},{10,... | collective-permute-start | bytes 6152 | tf_op jit(solution)/shard_map/ppermute | solution.py:367
  27.8 4.4 %collective-permute-start.9 = (f32[1,512]{1,0:T(1,128)S(1)}, f32[1,512]{1,0:T(1,128)S(1)}, u32[]{:S(2)}, u32[]{:S(2)}) collective-permute-start(f32[1,512]{1,0:T(1,128)S(1)} %get-tuple-element.40.refs_1_), channel_id=1, source_target_pairs={{0,1},{1,0},{2,3},{3,2},{4,5},{5,4},{6,7},{7,6},{8,9},{9,8},{10,11... | collective-permute-start | bytes 6152 | tf_op jit(solution)/shard_map/ppermute | solution.py:367

commit v7 on v6

--- a/solution.py
+++ b/solution.py
@@ -68,12 +68,12 @@
     return jnp.concatenate([rows[...].astype(f32) for rows in maps], axis=0).astype(bf16)
 
 
-def in_map_rows(map_refs):
+def out_map_rows(map_refs):
     rows = map_refs[0].shape[0] // 2
-    others = map_refs[:1:-1]
     if rows % 16 == 0:
-        return map_rows([map_refs[0].at[:rows], map_refs[1].at[:rows], *others])
-    return map_rows([map_refs[0][...].astype(f32)[:rows], map_refs[1][...].astype(f32)[:rows], *others])
+        return map_rows([map_refs[0].at[:rows], *map_refs[1:], map_refs[0].at[rows:]])
+    pair = map_refs[0][...].astype(f32)
+    return map_rows([pair[:rows], *map_refs[1:], pair[rows:]])
 
 
 def fetch(sources, targets, semaphores):
@@ -86,8 +86,11 @@
     return copies
 
 
-def prepare_kernel(inputs_hbm, step_hbm, rate_hbm, scaled_ref, cum_ref, inputs_ref, step_ref, rate_ref, semaphores):
-    copies = fetch((step_hbm, rate_hbm, inputs_hbm), (step_ref, rate_ref, inputs_ref), semaphores)
+def prepare_kernel(*refs):
+    sources, (scaled_ref, cum_ref), kept_refs = refs[:8], refs[8:10], refs[10:16]
+    step_ref, rate_ref, semaphores = refs[16:]
+    inputs_ref = kept_refs[0]
+    copies = fetch(sources, (step_ref, rate_ref, *kept_refs), semaphores)
     heads, tokens = step_ref.shape
     width = inputs_ref.shape[1]
     row = lax.broadcasted_iota(jnp.int32, (GROUP, GROUP), 0)
@@ -109,26 +112,22 @@
     for cols in blocks_of(width):
         scale = transposed_dot(factor, expand[:, cols])
         scaled_ref[:, cols] = (inputs_ref[:, cols].astype(f32) * scale).astype(bf16)
-
-
-def pack_kernel(in_hbm, out_hbm, maps_ref, semaphores):
-    rows = in_hbm.shape[0]
-    for copy in fetch((in_hbm, out_hbm), (maps_ref.at[:rows], maps_ref.at[rows:]), semaphores):
+    for copy in copies[3:]:
         copy.wait()
 
 
 def join_kernel(mine_ref, theirs_ref, _, both_ref):
-    rows = mine_ref.shape[0] // 2
-    both_ref[:rows, :] = mine_ref[rows:, :]
-    both_ref[rows:, :] = theirs_ref[rows:, :]
+    rows = mine_ref.shape[0]
+    both_ref[:rows, :] = mine_ref[...]
+    both_ref[rows:, :] = theirs_ref[...]
 
 
 def states_kernel(parts, *refs):
-    map_refs, (scaled_ref, cum_ref), out_refs = refs[:parts], refs[parts : parts + 2], refs[parts + 2 :]
+    map_refs, (scaled_ref, cum_ref), out_refs = refs[:parts], refs[parts : parts + 2], refs[parts + 3 :]
     shard_ref = out_refs[0]
     heads, tokens = cum_ref.shape
     width = scaled_ref.shape[1]
-    in_map = in_map_rows(map_refs)
+    in_map = map_rows(map_refs)
     size = in_map.shape[0]
     cum = cum_ref[...]
     states, decays = [], []
@@ -166,18 +165,14 @@
 
 
 def factor_kernel(spans, levels, *refs):
-    inputs_hbm, gate_hbm, mix_hbm, skip_hbm, cum_ref, _ = refs[:6]
+    inputs_ref, gate_ref, mix_ref, skip_ref, cum_ref, _ = refs[:6]
     base_ref, own_ref, far_ref = refs[6:9]
-    span_refs = refs[9:-5]
-    inputs_ref, gate_ref, mix_ref, skip_ref, semaphores = refs[-5:]
-    copies = fetch(refs[:4], (inputs_ref, gate_ref, mix_ref, skip_ref), semaphores)
+    span_refs = refs[9:]
     heads, tokens = cum_ref.shape
     width = inputs_ref.shape[1]
     groups = tokens // GROUP
     first = groups.bit_length()
     expand = expander(heads, width, 2).astype(bf16)
-    for copy in copies:
-        copy.wait()
     skip = head_row(heads, width, column_of(skip_ref[...]))
     before = jnp.zeros((heads, 1), f32)
     for group in range(groups):
@@ -211,8 +206,8 @@
     span_refs = refs[count:-2]
     near_ref, turned_ref = refs[-2:]
     tokens, width = base_ref.shape
-    in_map = in_map_rows(in_refs)
-    turned = jnp.transpose(map_rows([out_refs[0], *out_refs[:0:-1]]))
+    in_map = map_rows(in_refs)
+    turned = jnp.transpose(out_map_rows(out_refs))
     turned_ref[...] = turned
     size = in_map.shape[0]
     row = lax.broadcasted_iota(jnp.int32, (GROUP, GROUP), 0)
@@ -368,8 +363,8 @@
 
 
 def from_each(array, axis, first=1, stride=1):
-    masks = range(first, lax.axis_size(axis), stride)
-    return [flip(array, axis, mask) for mask in reversed(masks)]
+    masks = sorted(range(first, lax.axis_size(axis), stride), key=lambda mask: (mask == 1, mask))
+    return [flip(array, axis, mask) for mask in masks]
 
 
 def merged(older, newer, size):
@@ -402,35 +397,29 @@
     spans = local_spans(groups)
     dense = 2 * tokens * GROUP * width
     area = tokens * width
-    others = from_each(input_map, "head", first=2)
-    rows = input_map.shape[0]
-    if rows % 16 == 0:
-        maps = call(
-            pack_kernel,
-            shaped((2 * rows, tokens), bf16),
-            (input_map, output_map),
-            bytes_accessed=4 * rows * tokens,
-            hbm=2,
-            scratch=[pltpu.SemaphoreType.DMA((2,))],
-        )
-    else:
-        maps = jnp.concatenate([input_map, output_map], axis=0)
-    near_maps = flip(maps, "head", 1)
-    in_maps = [maps, near_maps, *others]
-    scaled, cum = call(
+    others = from_each(input_map, "head")
+    beside = flip(output_map, "head", 1)
+    kept = inputs, gate, level_mix, skip[None, :], input_map, output_map
+    scaled, cum, *kept = call(
         prepare_kernel,
-        (shaped((tokens, width), bf16), shaped((heads, tokens), f32)),
-        (inputs, step, decay_rate[None, :]),
+        (
+            *(shaped((tokens, width), bf16), shaped((heads, tokens), f32)),
+            *(shaped(array.shape, array.dtype) for array in kept),
+        ),
+        (step, decay_rate[None, :], *kept),
         flops=16 * dense,
         bytes_accessed=4 * area,
-        hbm=3,
+        hbm=8,
+        scratch=[pltpu.VMEM(step.shape, f32), pltpu.VMEM((1, heads), f32), pltpu.SemaphoreType.DMA((8,))],
     )
+    inputs, gate, level_mix, skip, input_map, output_map = kept
+    in_maps = [input_map, *others]
     shard_shape = shaped((size + DECAY_ROWS, width), bf16)
     span_shape = [shaped((len(spans) * size, width), bf16)] if spans else []
     shard, *span_states = call(
         functools.partial(states_kernel, parts),
         (shard_shape, *span_shape),
-        (*in_maps, scaled, cum),
+        (*in_maps, scaled, cum, beside),
         flops=dense,
         bytes_accessed=4 * area,
     )
@@ -445,12 +434,16 @@
         )
     else:
         message = shard
+    rows = output_map.shape[0]
     if rows % 16 == 0:
         both = call(
-            join_kernel, shaped((2 * rows, tokens), bf16), (maps, near_maps, shard), bytes_accessed=8 * rows * tokens
+            join_kernel,
+            shaped((2 * rows, tokens), bf16),
+            (output_map, beside, shard),
+            bytes_accessed=8 * rows * tokens,
         )
     else:
-        both = jnp.concatenate([maps[rows:], near_maps[rows:]], axis=0)
+        both = jnp.concatenate([output_map, beside], axis=0)
     out_maps = [both, *from_each(both, "head", first=2, stride=2)]
     factor_shape = [shaped((len(spans), GROUP, width), bf16)] if spans else []
     base, own_factor, far, *span_factors = call(
@@ -459,10 +452,9 @@
             *(shaped((tokens, width), f32), shaped((tokens, width), f32)),
             *(shaped((levels, tokens, width), bf16), *factor_shape),
         ),
-        (inputs, gate, level_mix, skip[None, :], cum, message),
+        (inputs, gate, level_mix, skip, cum, message),
         flops=8 * dense,
         bytes_accessed=16 * area,
-        hbm=4,
     )
     near, turned = call(
         functools.partial(near_kernel, parts, spans, pairs),
@@ -510,8 +502,7 @@
             flops=4 * dense,
             bytes_accessed=12 * area,
         )
-    *last, nearest = [sums, *from_each(sums, "head")]
-    last = [nearest, *last]
+    last = [sums, *from_each(sums, "head")]
     return call(
         functools.partial(norm_kernel, len(last), width * parts),
         shaped((tokens, width), bf16),

time: 33.7 us -> 34 us (level)
  Pallas kernels: 10.1 us -> 7.85 us
  waiting for transfers between devices: 6.87 us -> 8.88 us
  starting transfers between devices: 16.4 us -> 17 us
    pallas_call x11 -> x10, Pallas kernels: 10.1 us -> 7.85 us  [call(): pl.pallas_call(kernel, out_shape=out_shape, in_specs=specs, out_specs=jax...]
    ppermute x12 -> x13, waiting for transfers between devices: 6.87 us -> 8.88 us  [flip(): lax.ppermute(array, axis, [(i, i ^ mask) for i in range(lax.axis_size(axi...]
    ppermute x12 -> x13, starting transfers between devices: 16.4 us -> 17 us  [flip(): lax.ppermute(array, axis, [(i, i ^ mask) for i in range(lax.axis_size(axi...]
  transfers between devices with their start and end apart: 12 -> 13, of which waited for: 7 -> 7; matrix products, arithmetic and copies ran while one was open for 0% -> 0% of each run, Pallas kernels for 23% -> 16%
where the time goes in v7:
time: 34 us; the launch traced here: 33.8 us
  starting transfers between devices  17 us (50%)
  waiting for transfers between devices  8.88 us (26%)
  Pallas kernels  7.85 us (23%)
    ppermute x13, starting transfers between devices, flip(): lax.ppermute(array, axis, [(i, i ^ mask) for i in range(lax.axis_size(axi...  17 us
    ppermute x13, waiting for transfers between devices, flip(): lax.ppermute(array, axis, [(i, i ^ mask) for i in range(lax.axis_size(axi...  8.88 us
    pallas_call x10, Pallas kernels, call(): pl.pallas_call(kernel, out_shape=out_shape, in_specs=specs, out_specs=jax...  7.85 us
  transfers between devices with their start and end apart: 13, of which 7 were waited for; matrix products, arithmetic and copies ran while one was open for 0% of the time, Pallas kernels for 16%

profile of v7, /device:TPU:0, one launch (start us, length us, event | category | flops | bytes accessed | tf_op | source)
XLA Modules:
  0.0 33.8 jit_solution(3409323263646263894)
XLA Ops:
  0.0 4.0 %collective-permute-start = (bf16[32,512]{1,0:T(8,128)(2,1)}, bf16[32,512]{1,0:T(8,128)(2,1)S(1)}, u32[]{:S(2)}, u32[]{:S(2)}) collective-permute-start(bf16[32,512]{1,0:T(8,128)(2,1)} %refs_6_.1), channel_id=1, source_target_pairs={{0,2},{1,3},{2,0},{3,1},{4,6},{5,7},{6,4},{7,5},{8,10},{9,11},{10,... | collective-permute-start | bytes 98312 | tf_op jit(solution)/shard_map/ppermute | solution.py:362
  4.0 1.3 %collective-permute-start.1 = (bf16[32,512]{1,0:T(8,128)(2,1)}, bf16[32,512]{1,0:T(8,128)(2,1)S(1)}, u32[]{:S(2)}, u32[]{:S(2)}) collective-permute-start(bf16[32,512]{1,0:T(8,128)(2,1)} %refs_6_.1), channel_id=1, source_target_pairs={{0,3},{1,2},{2,1},{3,0},{4,7},{5,6},{6,5},{7,4},{8,11},{9,10},{10,... | collective-permute-start | bytes 98312 | tf_op jit(solution)/shard_map/ppermute | solution.py:362
  5.4 0.2 collective-permute-start.2
  5.6 1.8 %collective-permute-start.3 = (bf16[32,512]{1,0:T(8,128)(2,1)}, bf16[32,512]{1,0:T(8,128)(2,1)S(1)}, u32[]{:S(2)}, u32[]{:S(2)}) collective-permute-start(bf16[32,512]{1,0:T(8,128)(2,1)} %refs_7_.1), channel_id=1, source_target_pairs={{0,1},{1,0},{2,3},{3,2},{4,5},{5,4},{6,7},{7,6},{8,9},{9,8},{10,11... | collective-permute-start | bytes 98312 | tf_op jit(solution)/shard_map/ppermute | solution.py:362
  7.4 1.8 %shard_map.91 = (bf16[512,1024]{1,0:T(8,128)(2,1)S(1)}, f32[16,512]{1,0:T(8,128)S(1)}, bf16[512,1024]{1,0:T(8,128)(2,1)S(1)}, bf16[512,1024]{1,0:T(8,128)(2,1)S(...) custom-call(f32[16,512]{1,0:T(8,128)} %refs_0_.1, ...), custom_call_target="tpu_custom_call" | custom-call | flops 4294967296 | bytes 2097152 | tf_op jit(solution)/shard_map/pallas_call | solution.py:346
  9.2 1.0 %collective-permute-done.1.refs_2_.refs_7_ = bf16[32,512]{1,0:T(8,128)(2,1)S(1)} collective-permute-done((bf16[32,512]{1,0:T(8,128)(2,1)}, bf16[32,512]{1,0:T(8,128)(2,1)S(1)}, u32[]{:S(2)}, u32[]{:S(2)}) %collective-permute-start.1) | collective-permute-done | bytes 32800 | tf_op jit(solution)/shard_map/ppermute | solution.py:362
  10.3 0.0 collective-permute-done.2.refs_3_.refs_8_
  10.3 0.0 collective-permute-done.3.refs_6_.theirs_ref
  10.3 0.3 shard_map.92
  10.6 0.1 collective-permute-start.4
  10.7 2.4 %collective-permute-start.5 = (bf16[64,512]{1,0:T(8,128)(2,1)S(1)}, bf16[64,512]{1,0:T(8,128)(2,1)S(1)}, u32[]{:S(2)}, u32[]{:S(2)}) collective-permute-start(bf16[64,512]{1,0:T(8,128)(2,1)S(1)} %shard_map.95.refs_9_), channel_id=1, source_target_pairs={{0,2},{1,3},{2,0},{3,1},{4,6},{5,7},{6,4},{7,5},{8,10},{9,11},{10,... | collective-permute-start | bytes 196616 | tf_op jit(solution)/shard_map/ppermute | solution.py:362
  13.0 0.1 shard_map.93.refs_5_
  13.1 2.5 %collective-permute-start.6 = (bf16[144,512]{1,0:T(8,128)(2,1)S(1)}, bf16[144,512]{1,0:T(8,128)(2,1)S(1)}, u32[]{:S(2)}, u32[]{:S(2)}) collective-permute-start(bf16[144,512]{1,0:T(8,128)(2,1)S(1)} %shard_map.93.refs_5_), channel_id=1, source_target_pairs={{0,24},{4,28},{8,16},{12,20},{16,8},{20,12},{24,0},{28,4},{1,25},{... | collective-permute-start | bytes 442376 | tf_op jit(solution)/shard_map/ppermute | solution.py:362
  15.6 0.5 %collective-permute-start.7 = (bf16[144,512]{1,0:T(8,128)(2,1)S(1)}, bf16[144,512]{1,0:T(8,128)(2,1)S(1)}, u32[]{:S(2)}, u32[]{:S(2)}) collective-permute-start(bf16[144,512]{1,0:T(8,128)(2,1)S(1)} %shard_map.93.refs_5_), channel_id=1, source_target_pairs={{0,16},{4,20},{8,24},{12,28},{16,0},{20,4},{24,8},{28,12},{1,17},{... | collective-permute-start | bytes 442376 | tf_op jit(solution)/shard_map/ppermute | solution.py:362
  16.1 0.5 %collective-permute-start.8 = (bf16[144,512]{1,0:T(8,128)(2,1)S(1)}, bf16[144,512]{1,0:T(8,128)(2,1)S(1)}, u32[]{:S(2)}, u32[]{:S(2)}) collective-permute-start(bf16[144,512]{1,0:T(8,128)(2,1)S(1)} %shard_map.93.refs_5_), channel_id=1, source_target_pairs={{0,8},{4,12},{8,0},{12,4},{16,24},{20,28},{24,16},{28,20},{1,9},{5... | collective-permute-start | bytes 442376 | tf_op jit(solution)/shard_map/ppermute | solution.py:362
  16.7 1.8 %shard_map.94 = (f32[512,1024]{1,0:T(8,128)S(1)}, f32[512,1024]{1,0:T(8,128)S(1)}, bf16[3,512,1024]{2,1,0:T(8,128)(2,1)S(1)}, bf16[1,256,1024]{2,1,0:T(8,128)(2,1)S(1)}) custom-call(bf16[512,1024]{1,0:T(8,128)(2,1)S(1)} %get-tuple-element.30.refs_0_, bf16[512,1024]{1,0:T(8,128)(2,1)S(1)} %get-tuple-element.31.refs_1_, ...), custom_call_target="tpu_custom_call" | custom-call | flops 2147483648 | bytes 8388608 | tf_op jit(solution)/shard_map/pallas_call | solution.py:346
  18.5 0.0 copy-start
  18.5 1.3 %shard_map.96 = (f32[512,1024]{1,0:T(8,128)S(1)}, bf16[512,128]{1,0:T(8,128)(2,1)S(1)}) custom-call(f32[512,1024]{1,0:T(8,128)S(1)} %get-tuple-element.38.refs_0_, f32[512,1024]{1,0:T(8,128)S(1)} %get-tuple-element.39.refs_1_, bf16[3,512,1024]{2,1,0:T(8,128)(2,1)S(1)} %get-tuple-element.47.refs_2_, ...), custom_call_target="tpu_custom_call" | custom-call | flops 1073741824 | bytes 8388608 | tf_op jit(solution)/shard_map/pallas_call | solution.py:346
  19.8 0.9 %collective-permute-done.6.diagonal_ref = bf16[144,512]{1,0:T(8,128)(2,1)S(1)} collective-permute-done((bf16[144,512]{1,0:T(8,128)(2,1)S(1)}, bf16[144,512]{1,0:T(8,128)(2,1)S(1)}, u32[]{:S(2)}, u32[]{:S(2)}) %collective-permute-start.6) | collective-permute-done | bytes 147488 | tf_op jit(solution)/shard_map/ppermute | solution.py:362
  20.6 2.5 %collective-permute-done.7.y_ref = bf16[144,512]{1,0:T(8,128)(2,1)S(1)} collective-permute-done((bf16[144,512]{1,0:T(8,128)(2,1)S(1)}, bf16[144,512]{1,0:T(8,128)(2,1)S(1)}, u32[]{:S(2)}, u32[]{:S(2)}) %collective-permute-start.7) | collective-permute-done | bytes 147488 | tf_op jit(solution)/shard_map/ppermute | solution.py:362
  23.2 0.1 collective-permute-done.8.x_ref
  23.3 0.1 shard_map.97.refs_5_
  23.4 0.1 collective-permute-start.9
  23.5 0.5 %shard_map.98 = (f32[512,512]{1,0:T(8,128)S(1)}, f32[512,128]{1,0:T(8,128)S(1)}) custom-call(bf16[512,128]{1,0:T(8,128)(2,1)S(1)} %get-tuple-element.44.refs_0_, f32[512,1024]{1,0:T(8,128)S(1)} %get-tuple-element.46.refs_1_, bf16[3,512,1024]{2,1,0:T(8,128)(2,1)S(1)} %get-tuple-element.47.refs_2_, f32[1,1024]{1,0:T(1,128)S(1)} %bitcast.3, ...), custom_call_target="tpu_custom_call" | custom-call | flops 536870912 | bytes 3145728 | tf_op jit(solution)/shard_map/pallas_call | solution.py:346
  24.0 1.0 %collective-permute-done.9.refs_5_ = bf16[256,512]{1,0:T(8,128)(2,1)S(1)} collective-permute-done((bf16[256,512]{1,0:T(8,128)(2,1)S(1)}, bf16[256,512]{1,0:T(8,128)(2,1)S(1)}, u32[]{:S(2)}, u32[]{:S(2)}) %collective-permute-start.9) | collective-permute-done | bytes 262176 | tf_op jit(solution)/shard_map/ppermute | solution.py:362
  25.0 0.7 %shard_map.99 = (f32[512,512]{1,0:T(8,128)S(1)}, f32[1,512]{1,0:T(1,128)S(1)}) custom-call(bf16[512,128]{1,0:T(8,128)(2,1)S(1)} %get-tuple-element.44.refs_0_, f32[512,1024]{1,0:T(8,128)S(1)} %get-tuple-element.46.refs_1_, bf16[3,512,1024]{2,1,0:T(8,128)(2,1)S(1)} %get-tuple-element.47.refs_2_, f32[1,1024]{1,0:T(1,128)S(1)} %bitcast.4, ...), custom_call_target="tpu_custom_call" | custom-call | flops 536870912 | bytes 3145728 | tf_op jit(solution)/shard_map/pallas_call | solution.py:346
  25.7 1.5 %collective-permute-start.10 = (f32[1,512]{1,0:T(1,128)S(1)}, f32[1,512]{1,0:T(1,128)S(1)}, u32[]{:S(2)}, u32[]{:S(2)}) collective-permute-start(f32[1,512]{1,0:T(1,128)S(1)} %get-tuple-element.52.refs_0_), channel_id=1, source_target_pairs={{0,2},{1,3},{2,0},{3,1},{4,6},{5,7},{6,4},{7,5},{8,10},{9,11},{10,... | collective-permute-start | bytes 6152 | tf_op jit(solution)/shard_map/ppermute | solution.py:362
  27.2 1.6 %collective-permute-start.11 = (f32[1,512]{1,0:T(1,128)S(1)}, f32[1,512]{1,0:T(1,128)S(1)}, u32[]{:S(2)}, u32[]{:S(2)}) collective-permute-start(f32[1,512]{1,0:T(1,128)S(1)} %get-tuple-element.52.refs_0_), channel_id=1, source_target_pairs={{0,3},{1,2},{2,1},{3,0},{4,7},{5,6},{6,5},{7,4},{8,11},{9,10},{10,... | collective-permute-start | bytes 6152 | tf_op jit(solution)/shard_map/ppermute | solution.py:362
  28.7 0.5 %collective-permute-start.12 = (f32[1,512]{1,0:T(1,128)S(1)}, f32[1,512]{1,0:T(1,128)S(1)}, u32[]{:S(2)}, u32[]{:S(2)}) collective-permute-start(f32[1,512]{1,0:T(1,128)S(1)} %get-tuple-element.52.refs_0_), channel_id=1, source_target_pairs={{0,1},{1,0},{2,3},{3,2},{4,5},{5,4},{6,7},{7,6},{8,9},{9,8},{10,11... | collective-permute-start | bytes 6152 | tf_op jit(solution)/shard_map/ppermute | solution.py:362
  29.2 1.0 %collective-permute-done.10.refs_1_ = f32[1,512]{1,0:T(1,128)S(1)} collective-permute-done((f32[1,512]{1,0:T(1,128)S(1)}, f32[1,512]{1,0:T(1,128)S(1)}, u32[]{:S(2)}, u32[]{:S(2)}) %collective-permute-start.10) | collective-permute-done | bytes 2080 | tf_op jit(solution)/shard_map/ppermute | solution.py:362
  30.2 2.4 %collective-permute-done.11.refs_2_ = f32[1,512]{1,0:T(1,128)S(1)} collective-permute-done((f32[1,512]{1,0:T(1,128)S(1)}, f32[1,512]{1,0:T(1,128)S(1)}, u32[]{:S(2)}, u32[]{:S(2)}) %collective-permute-start.11) | collective-permute-done | bytes 2080 | tf_op jit(solution)/shard_map/ppermute | solution.py:362
  32.5 1.3 %shard_map.100 = bf16[512,1024]{1,0:T(8,128)(2,1)} custom-call(f32[1,512]{1,0:T(1,128)S(1)} %get-tuple-element.52.refs_0_, f32[1,512]{1,0:T(1,128)S(1)} %collective-permute-done.10.refs_1_, f32[1,512]{1,0:T(1,128)S(1)} %collective-permute-done.11.refs_2_, f32[1,512]{1,0:T(1,128)S(1)} %collective-permute-done.12.refs_3_, ...), custom_call_target="tpu_custom_call" | custom-call | flops 268435456 | bytes 3145728 | tf_op jit(solution)/shard_map/pallas_call | solution.py:346
  (6 shorter events, 0.0 us)
Async XLA Ops:
  0.0 9.2 %collective-permute-start = (bf16[32,512]{1,0:T(8,128)(2,1)}, bf16[32,512]{1,0:T(8,128)(2,1)S(1)}, u32[]{:S(2)}, u32[]{:S(2)}) collective-permute-start(bf16[32,512]{1,0:T(8,128)(2,1)} %refs_6_.1), channel_id=1, source_target_pairs={{0,2},{1,3},{2,0},{3,1},{4,6},{5,7},{6,4},{7,5},{8,10},{9,11},{10,... | collective-permute-start | bytes 98312 | tf_op jit(solution)/shard_map/ppermute | solution.py:362
  4.0 6.2 %collective-permute-start.1 = (bf16[32,512]{1,0:T(8,128)(2,1)}, bf16[32,512]{1,0:T(8,128)(2,1)S(1)}, u32[]{:S(2)}, u32[]{:S(2)}) collective-permute-start(bf16[32,512]{1,0:T(8,128)(2,1)} %refs_6_.1), channel_id=1, source_target_pairs={{0,3},{1,2},{2,1},{3,0},{4,7},{5,6},{6,5},{7,4},{8,11},{9,10},{10,... | collective-permute-start | bytes 98312 | tf_op jit(solution)/shard_map/ppermute | solution.py:362
  5.4 4.9 %collective-permute-start.2 = (bf16[32,512]{1,0:T(8,128)(2,1)}, bf16[32,512]{1,0:T(8,128)(2,1)S(1)}, u32[]{:S(2)}, u32[]{:S(2)}) collective-permute-start(bf16[32,512]{1,0:T(8,128)(2,1)} %refs_6_.1), channel_id=1, source_target_pairs={{0,1},{1,0},{2,3},{3,2},{4,5},{5,4},{6,7},{7,6},{8,9},{9,8},{10,11... | collective-permute-start | bytes 98312 | tf_op jit(solution)/shard_map/ppermute | solution.py:362
  5.6 4.6 %collective-permute-start.3 = (bf16[32,512]{1,0:T(8,128)(2,1)}, bf16[32,512]{1,0:T(8,128)(2,1)S(1)}, u32[]{:S(2)}, u32[]{:S(2)}) collective-permute-start(bf16[32,512]{1,0:T(8,128)(2,1)} %refs_7_.1), channel_id=1, source_target_pairs={{0,1},{1,0},{2,3},{3,2},{4,5},{5,4},{6,7},{7,6},{8,9},{9,8},{10,11... | collective-permute-start | bytes 98312 | tf_op jit(solution)/shard_map/ppermute | solution.py:362
  10.6 2.4 %collective-permute-start.4 = (bf16[144,1024]{1,0:T(8,128)(2,1)S(1)}, bf16[144,1024]{1,0:T(8,128)(2,1)S(1)}, u32[]{:S(2)}, u32[]{:S(2)}) collective-permute-start(bf16[144,1024]{1,0:T(8,128)(2,1)S(1)} %get-tuple-element.37.mine_ref._), channel_id=1, source_target_pairs={{0,4},{4,0},{8,12},{12,8},{16,20},{20,16},{24,28},{28,24},{1,5},{5... | collective-permute-start | bytes 884744 | tf_op jit(solution)/shard_map/ppermute | solution.py:362
  10.7 7.8 %collective-permute-start.5 = (bf16[64,512]{1,0:T(8,128)(2,1)S(1)}, bf16[64,512]{1,0:T(8,128)(2,1)S(1)}, u32[]{:S(2)}, u32[]{:S(2)}) collective-permute-start(bf16[64,512]{1,0:T(8,128)(2,1)S(1)} %shard_map.95.refs_9_), channel_id=1, source_target_pairs={{0,2},{1,3},{2,0},{3,1},{4,6},{5,7},{6,4},{7,5},{8,10},{9,11},{10,... | collective-permute-start | bytes 196616 | tf_op jit(solution)/shard_map/ppermute | solution.py:362
  13.1 7.5 %collective-permute-start.6 = (bf16[144,512]{1,0:T(8,128)(2,1)S(1)}, bf16[144,512]{1,0:T(8,128)(2,1)S(1)}, u32[]{:S(2)}, u32[]{:S(2)}) collective-permute-start(bf16[144,512]{1,0:T(8,128)(2,1)S(1)} %shard_map.93.refs_5_), channel_id=1, source_target_pairs={{0,24},{4,28},{8,16},{12,20},{16,8},{20,12},{24,0},{28,4},{1,25},{... | collective-permute-start | bytes 442376 | tf_op jit(solution)/shard_map/ppermute | solution.py:362
  15.6 7.5 %collective-permute-start.7 = (bf16[144,512]{1,0:T(8,128)(2,1)S(1)}, bf16[144,512]{1,0:T(8,128)(2,1)S(1)}, u32[]{:S(2)}, u32[]{:S(2)}) collective-permute-start(bf16[144,512]{1,0:T(8,128)(2,1)S(1)} %shard_map.93.refs_5_), channel_id=1, source_target_pairs={{0,16},{4,20},{8,24},{12,28},{16,0},{20,4},{24,8},{28,12},{1,17},{... | collective-permute-start | bytes 442376 | tf_op jit(solution)/shard_map/ppermute | solution.py:362
  16.1 7.1 %collective-permute-start.8 = (bf16[144,512]{1,0:T(8,128)(2,1)S(1)}, bf16[144,512]{1,0:T(8,128)(2,1)S(1)}, u32[]{:S(2)}, u32[]{:S(2)}) collective-permute-start(bf16[144,512]{1,0:T(8,128)(2,1)S(1)} %shard_map.93.refs_5_), channel_id=1, source_target_pairs={{0,8},{4,12},{8,0},{12,4},{16,24},{20,28},{24,16},{28,20},{1,9},{5... | collective-permute-start | bytes 442376 | tf_op jit(solution)/shard_map/ppermute | solution.py:362
  18.5 5.0 %copy-start = (f32[1024]{0:T(1024)S(1)}, f32[1024]{0:T(1024)}, u32[]{:S(2)}) copy-start(f32[1024]{0:T(1024)} %param.17) | copy-start | bytes 12292
  23.4 1.6 %collective-permute-start.9 = (bf16[256,512]{1,0:T(8,128)(2,1)S(1)}, bf16[256,512]{1,0:T(8,128)(2,1)S(1)}, u32[]{:S(2)}, u32[]{:S(2)}) collective-permute-start(bf16[256,512]{1,0:T(8,128)(2,1)S(1)} %shard_map.97.refs_5_), channel_id=1, source_target_pairs={{0,4},{4,0},{8,12},{12,8},{16,20},{20,16},{24,28},{28,24},{1,5},{5... | collective-permute-start | bytes 786440 | tf_op jit(solution)/shard_map/ppermute | solution.py:362
  25.7 4.5 %collective-permute-start.10 = (f32[1,512]{1,0:T(1,128)S(1)}, f32[1,512]{1,0:T(1,128)S(1)}, u32[]{:S(2)}, u32[]{:S(2)}) collective-permute-start(f32[1,512]{1,0:T(1,128)S(1)} %get-tuple-element.52.refs_0_), channel_id=1, source_target_pairs={{0,2},{1,3},{2,0},{3,1},{4,6},{5,7},{6,4},{7,5},{8,10},{9,11},{10,... | collective-permute-start | bytes 6152 | tf_op jit(solution)/shard_map/ppermute | solution.py:362
  27.2 5.4 %collective-permute-start.11 = (f32[1,512]{1,0:T(1,128)S(1)}, f32[1,512]{1,0:T(1,128)S(1)}, u32[]{:S(2)}, u32[]{:S(2)}) collective-permute-start(f32[1,512]{1,0:T(1,128)S(1)} %get-tuple-element.52.refs_0_), channel_id=1, source_target_pairs={{0,3},{1,2},{2,1},{3,0},{4,7},{5,6},{6,5},{7,4},{8,11},{9,10},{10,... | collective-permute-start | bytes 6152 | tf_op jit(solution)/shard_map/ppermute | solution.py:362
  28.7 3.8 %collective-permute-start.12 = (f32[1,512]{1,0:T(1,128)S(1)}, f32[1,512]{1,0:T(1,128)S(1)}, u32[]{:S(2)}, u32[]{:S(2)}) collective-permute-start(f32[1,512]{1,0:T(1,128)S(1)} %get-tuple-element.52.refs_0_), channel_id=1, source_target_pairs={{0,1},{1,0},{2,3},{3,2},{4,5},{5,4},{6,7},{7,6},{8,9},{9,8},{10,11... | collective-permute-start | bytes 6152 | tf_op jit(solution)/shard_map/ppermute | solution.py:362

commit v8 on v7

--- a/solution.py
+++ b/solution.py
@@ -116,14 +116,14 @@
         copy.wait()
 
 
-def join_kernel(mine_ref, theirs_ref, _, both_ref):
+def join_kernel(mine_ref, theirs_ref, both_ref):
     rows = mine_ref.shape[0]
     both_ref[:rows, :] = mine_ref[...]
     both_ref[rows:, :] = theirs_ref[...]
 
 
 def states_kernel(parts, *refs):
-    map_refs, (scaled_ref, cum_ref), out_refs = refs[:parts], refs[parts : parts + 2], refs[parts + 3 :]
+    map_refs, (scaled_ref, cum_ref), out_refs = refs[:parts], refs[parts : parts + 2], refs[parts + 2 :]
     shard_ref = out_refs[0]
     heads, tokens = cum_ref.shape
     width = scaled_ref.shape[1]
@@ -398,7 +398,6 @@
     dense = 2 * tokens * GROUP * width
     area = tokens * width
     others = from_each(input_map, "head")
-    beside = flip(output_map, "head", 1)
     kept = inputs, gate, level_mix, skip[None, :], input_map, output_map
     scaled, cum, *kept = call(
         prepare_kernel,
@@ -419,7 +418,7 @@
     shard, *span_states = call(
         functools.partial(states_kernel, parts),
         (shard_shape, *span_shape),
-        (*in_maps, scaled, cum, beside),
+        (*in_maps, scaled, cum),
         flops=dense,
         bytes_accessed=4 * area,
     )
@@ -430,16 +429,19 @@
             functools.partial(merge_kernel, size),
             shaped((size + DECAY_ROWS, width // 2), bf16),
             (shard, theirs),
+            flops=0,
             bytes_accessed=area,
         )
     else:
         message = shard
+    output_map, _ = lax.optimization_barrier((output_map, shard))
+    beside = flip(output_map, "head", 1)
     rows = output_map.shape[0]
     if rows % 16 == 0:
         both = call(
             join_kernel,
             shaped((2 * rows, tokens), bf16),
-            (output_map, beside, shard),
+            (output_map, beside),
             bytes_accessed=8 * rows * tokens,
         )
     else:
@@ -453,8 +455,8 @@
             *(shaped((levels, tokens, width), bf16), *factor_shape),
         ),
         (inputs, gate, level_mix, skip, cum, message),
-        flops=8 * dense,
-        bytes_accessed=16 * area,
+        flops=21 * dense // 4,
+        bytes_accessed=0,
     )
     near, turned = call(
         functools.partial(near_kernel, parts, spans, pairs),
@@ -463,8 +465,8 @@
             *(base, own_factor, far, theirs if pairs else message, scaled),
             *(*in_maps, *out_maps, *span_states, *span_factors),
         ),
-        flops=4 * dense,
-        bytes_accessed=16 * area,
+        flops=0,
+        bytes_accessed=0,
     )
     gain = norm_gain[None, :]
     sums_shape = shaped((1, tokens), f32)

time: 34 us -> 32.7 us (0.962)
  starting transfers between devices: 17 us -> 14.2 us
  waiting for transfers between devices: 8.88 us -> 10.4 us
    ppermute x13, starting transfers between devices: 17 us -> 14.2 us  [flip(): lax.ppermute(array, axis, [(i, i ^ mask) for i in range(lax.axis_size(axi...]
    ppermute x13, waiting for transfers between devices: 8.88 us -> 10.4 us  [flip(): lax.ppermute(array, axis, [(i, i ^ mask) for i in range(lax.axis_size(axi...]
  transfers between devices with their start and end apart: 13 -> 13, of which waited for: 7 -> 6; matrix products, arithmetic and copies ran while one was open for 0% -> 0% of each run, Pallas kernels for 16% -> 17%
where the time goes in v8:
time: 32.7 us; the launch traced here: 32.6 us
  starting transfers between devices  14.2 us (43%)
  waiting for transfers between devices  10.4 us (32%)
  Pallas kernels  7.83 us (24%)
    ppermute x13, starting transfers between devices, flip(): lax.ppermute(array, axis, [(i, i ^ mask) for i in range(lax.axis_size(axi...  14.2 us
    ppermute x13, waiting for transfers between devices, flip(): lax.ppermute(array, axis, [(i, i ^ mask) for i in range(lax.axis_size(axi...  10.4 us
    pallas_call x10, Pallas kernels, call(): pl.pallas_call(kernel, out_shape=out_shape, in_specs=specs, out_specs=jax...  7.83 us
  transfers between devices with their start and end apart: 13, of which 6 were waited for; matrix products, arithmetic and copies ran while one was open for 0% of the time, Pallas kernels for 17%

profile of v8, /device:TPU:0, one launch (start us, length us, event | category | flops | bytes accessed | tf_op | source)
XLA Modules:
  0.0 32.6 jit_solution(13536385797806339331)
XLA Ops:
  0.0 4.0 %collective-permute-start = (bf16[32,512]{1,0:T(8,128)(2,1)}, bf16[32,512]{1,0:T(8,128)(2,1)S(1)}, u32[]{:S(2)}, u32[]{:S(2)}) collective-permute-start(bf16[32,512]{1,0:T(8,128)(2,1)} %refs_6_.1), channel_id=1, source_target_pairs={{0,2},{1,3},{2,0},{3,1},{4,6},{5,7},{6,4},{7,5},{8,10},{9,11},{10,... | collective-permute-start | bytes 98312 | tf_op jit(solution)/shard_map/ppermute | solution.py:362
  4.0 1.3 %collective-permute-start.1 = (bf16[32,512]{1,0:T(8,128)(2,1)}, bf16[32,512]{1,0:T(8,128)(2,1)S(1)}, u32[]{:S(2)}, u32[]{:S(2)}) collective-permute-start(bf16[32,512]{1,0:T(8,128)(2,1)} %refs_6_.1), channel_id=1, source_target_pairs={{0,3},{1,2},{2,1},{3,0},{4,7},{5,6},{6,5},{7,4},{8,11},{9,10},{10,... | collective-permute-start | bytes 98312 | tf_op jit(solution)/shard_map/ppermute | solution.py:362
  5.4 0.2 collective-permute-start.2
  5.6 1.8 %shard_map.91 = (bf16[512,1024]{1,0:T(8,128)(2,1)S(1)}, f32[16,512]{1,0:T(8,128)S(1)}, bf16[512,1024]{1,0:T(8,128)(2,1)S(1)}, bf16[512,1024]{1,0:T(8,128)(2,1)S(...) custom-call(f32[16,512]{1,0:T(8,128)} %refs_0_.1, ...), custom_call_target="tpu_custom_call" | custom-call | flops 4294967296 | bytes 2097152 | tf_op jit(solution)/shard_map/pallas_call | solution.py:346
  7.4 2.5 %collective-permute-done.1.refs_2_.refs_7_ = bf16[32,512]{1,0:T(8,128)(2,1)S(1)} collective-permute-done((bf16[32,512]{1,0:T(8,128)(2,1)}, bf16[32,512]{1,0:T(8,128)(2,1)S(1)}, u32[]{:S(2)}, u32[]{:S(2)}) %collective-permute-start.1) | collective-permute-done | bytes 32800 | tf_op jit(solution)/shard_map/ppermute | solution.py:362
  10.0 0.0 collective-permute-done.2.refs_3_.refs_8_
  10.0 0.3 shard_map.92
  10.3 0.1 collective-permute-start.3
  10.4 0.1 collective-permute-start.4
  10.5 1.5 %collective-permute-done.3.theirs_ref.refs_3_.refs_4_ = bf16[144,1024]{1,0:T(8,128)(2,1)S(1)} collective-permute-done((bf16[144,1024]{1,0:T(8,128)(2,1)S(1)}, bf16[144,1024]{1,0:T(8,128)(2,1)S(1)}, u32[]{:S(2)}, u32[]{:S(2)}) %collective-permute-start.3) | collective-permute-done | bytes 294944 | tf_op jit(solution)/shard_map/ppermute | solution.py:362
  11.9 0.1 shard_map.93.refs_5_
  12.0 2.5 %collective-permute-start.6 = (bf16[144,512]{1,0:T(8,128)(2,1)S(1)}, bf16[144,512]{1,0:T(8,128)(2,1)S(1)}, u32[]{:S(2)}, u32[]{:S(2)}) collective-permute-start(bf16[144,512]{1,0:T(8,128)(2,1)S(1)} %shard_map.93.refs_5_), channel_id=1, source_target_pairs={{0,24},{4,28},{8,16},{12,20},{16,8},{20,12},{24,0},{28,4},{1,25},{... | collective-permute-start | bytes 442376 | tf_op jit(solution)/shard_map/ppermute | solution.py:362
  14.5 0.5 %collective-permute-start.7 = (bf16[144,512]{1,0:T(8,128)(2,1)S(1)}, bf16[144,512]{1,0:T(8,128)(2,1)S(1)}, u32[]{:S(2)}, u32[]{:S(2)}) collective-permute-start(bf16[144,512]{1,0:T(8,128)(2,1)S(1)} %shard_map.93.refs_5_), channel_id=1, source_target_pairs={{0,16},{4,20},{8,24},{12,28},{16,0},{20,4},{24,8},{28,12},{1,17},{... | collective-permute-start | bytes 442376 | tf_op jit(solution)/shard_map/ppermute | solution.py:362
  15.0 0.5 %collective-permute-start.8 = (bf16[144,512]{1,0:T(8,128)(2,1)S(1)}, bf16[144,512]{1,0:T(8,128)(2,1)S(1)}, u32[]{:S(2)}, u32[]{:S(2)}) collective-permute-start(bf16[144,512]{1,0:T(8,128)(2,1)S(1)} %shard_map.93.refs_5_), channel_id=1, source_target_pairs={{0,8},{4,12},{8,0},{12,4},{16,24},{20,28},{24,16},{28,20},{1,9},{5... | collective-permute-start | bytes 442376 | tf_op jit(solution)/shard_map/ppermute | solution.py:362
  15.6 0.0 collective-permute-done.4.theirs_ref
  15.6 1.3 %collective-permute-start.5 = (bf16[64,512]{1,0:T(8,128)(2,1)S(1)}, bf16[64,512]{1,0:T(8,128)(2,1)S(1)}, u32[]{:S(2)}, u32[]{:S(2)}) collective-permute-start(bf16[64,512]{1,0:T(8,128)(2,1)S(1)} %shard_map.95.refs_9_), channel_id=1, source_target_pairs={{0,2},{1,3},{2,0},{3,1},{4,6},{5,7},{6,4},{7,5},{8,10},{9,11},{10,... | collective-permute-start | bytes 196616 | tf_op jit(solution)/shard_map/ppermute | solution.py:362
  16.9 1.8 %shard_map.94 = (f32[512,1024]{1,0:T(8,128)S(1)}, f32[512,1024]{1,0:T(8,128)S(1)}, bf16[3,512,1024]{2,1,0:T(8,128)(2,1)S(1)}, bf16[1,256,1024]{2,1,0:T(8,128)(2,1)S(1)}) custom-call(bf16[512,1024]{1,0:T(8,128)(2,1)S(1)} %get-tuple-element.31.refs_0_, bf16[512,1024]{1,0:T(8,128)(2,1)S(1)} %get-tuple-element.32.refs_1_, ...), custom_call_target="tpu_custom_call" | custom-call | flops 1409286144 | tf_op jit(solution)/shard_map/pallas_call | solution.py:346
  18.7 2.8 %collective-permute-done.5.refs_10_ = bf16[64,512]{1,0:T(8,128)(2,1)S(1)} collective-permute-done((bf16[64,512]{1,0:T(8,128)(2,1)S(1)}, bf16[64,512]{1,0:T(8,128)(2,1)S(1)}, u32[]{:S(2)}, u32[]{:S(2)}) %collective-permute-start.5) | collective-permute-done | bytes 65568 | tf_op jit(solution)/shard_map/ppermute | solution.py:362
  21.5 1.3 %shard_map.96 = (f32[512,1024]{1,0:T(8,128)S(1)}, bf16[512,128]{1,0:T(8,128)(2,1)S(1)}) custom-call(f32[512,1024]{1,0:T(8,128)S(1)} %get-tuple-element.39.refs_0_, f32[512,1024]{1,0:T(8,128)S(1)} %get-tuple-element.40.refs_1_, bf16[3,512,1024]{2,1,0:T(8,128)(2,1)S(1)} %get-tuple-element.49.refs_2_, ...), custom_call_target="tpu_custom_call" | custom-call | tf_op jit(solution)/shard_map/pallas_call | solution.py:346
  22.8 0.0 collective-permute-done.7.y_ref
  22.8 0.0 collective-permute-done.8.x_ref
  22.8 0.1 shard_map.97.refs_5_
  22.9 0.1 collective-permute-start.9
  23.0 0.5 %shard_map.98 = (f32[512,512]{1,0:T(8,128)S(1)}, f32[512,128]{1,0:T(8,128)S(1)}) custom-call(bf16[512,128]{1,0:T(8,128)(2,1)S(1)} %get-tuple-element.46.refs_0_, f32[512,1024]{1,0:T(8,128)S(1)} %get-tuple-element.48.refs_1_, bf16[3,512,1024]{2,1,0:T(8,128)(2,1)S(1)} %get-tuple-element.49.refs_2_, f32[1,1024]{1,0:T(1,128)S(1)} %bitcast.3, ...), custom_call_target="tpu_custom_call" | custom-call | flops 536870912 | bytes 3145728 | tf_op jit(solution)/shard_map/pallas_call | solution.py:346
  23.5 1.0 %collective-permute-done.9.refs_5_ = bf16[256,512]{1,0:T(8,128)(2,1)S(1)} collective-permute-done((bf16[256,512]{1,0:T(8,128)(2,1)S(1)}, bf16[256,512]{1,0:T(8,128)(2,1)S(1)}, u32[]{:S(2)}, u32[]{:S(2)}) %collective-permute-start.9) | collective-permute-done | bytes 262176 | tf_op jit(solution)/shard_map/ppermute | solution.py:362
  24.5 0.7 %shard_map.99 = (f32[512,512]{1,0:T(8,128)S(1)}, f32[1,512]{1,0:T(1,128)S(1)}) custom-call(bf16[512,128]{1,0:T(8,128)(2,1)S(1)} %get-tuple-element.46.refs_0_, f32[512,1024]{1,0:T(8,128)S(1)} %get-tuple-element.48.refs_1_, bf16[3,512,1024]{2,1,0:T(8,128)(2,1)S(1)} %get-tuple-element.49.refs_2_, f32[1,1024]{1,0:T(1,128)S(1)} %bitcast.4, ...), custom_call_target="tpu_custom_call" | custom-call | flops 536870912 | bytes 3145728 | tf_op jit(solution)/shard_map/pallas_call | solution.py:346
  25.2 0.7 %collective-permute-start.10 = (f32[1,512]{1,0:T(1,128)S(1)}, f32[1,512]{1,0:T(1,128)S(1)}, u32[]{:S(2)}, u32[]{:S(2)}) collective-permute-start(f32[1,512]{1,0:T(1,128)S(1)} %get-tuple-element.54.refs_0_), channel_id=1, source_target_pairs={{0,2},{1,3},{2,0},{3,1},{4,6},{5,7},{6,4},{7,5},{8,10},{9,11},{10,... | collective-permute-start | bytes 6152 | tf_op jit(solution)/shard_map/ppermute | solution.py:362
  25.9 1.6 %collective-permute-start.11 = (f32[1,512]{1,0:T(1,128)S(1)}, f32[1,512]{1,0:T(1,128)S(1)}, u32[]{:S(2)}, u32[]{:S(2)}) collective-permute-start(f32[1,512]{1,0:T(1,128)S(1)} %get-tuple-element.54.refs_0_), channel_id=1, source_target_pairs={{0,3},{1,2},{2,1},{3,0},{4,7},{5,6},{6,5},{7,4},{8,11},{9,10},{10,... | collective-permute-start | bytes 6152 | tf_op jit(solution)/shard_map/ppermute | solution.py:362
  27.5 1.2 %collective-permute-start.12 = (f32[1,512]{1,0:T(1,128)S(1)}, f32[1,512]{1,0:T(1,128)S(1)}, u32[]{:S(2)}, u32[]{:S(2)}) collective-permute-start(f32[1,512]{1,0:T(1,128)S(1)} %get-tuple-element.54.refs_0_), channel_id=1, source_target_pairs={{0,1},{1,0},{2,3},{3,2},{4,5},{5,4},{6,7},{7,6},{8,9},{9,8},{10,11... | collective-permute-start | bytes 6152 | tf_op jit(solution)/shard_map/ppermute | solution.py:362
  28.7 1.0 %collective-permute-done.10.refs_1_ = f32[1,512]{1,0:T(1,128)S(1)} collective-permute-done((f32[1,512]{1,0:T(1,128)S(1)}, f32[1,512]{1,0:T(1,128)S(1)}, u32[]{:S(2)}, u32[]{:S(2)}) %collective-permute-start.10) | collective-permute-done | bytes 2080 | tf_op jit(solution)/shard_map/ppermute | solution.py:362
  29.7 1.6 %collective-permute-done.11.refs_2_ = f32[1,512]{1,0:T(1,128)S(1)} collective-permute-done((f32[1,512]{1,0:T(1,128)S(1)}, f32[1,512]{1,0:T(1,128)S(1)}, u32[]{:S(2)}, u32[]{:S(2)}) %collective-permute-start.11) | collective-permute-done | bytes 2080 | tf_op jit(solution)/shard_map/ppermute | solution.py:362
  31.3 1.3 %shard_map.100 = bf16[512,1024]{1,0:T(8,128)(2,1)} custom-call(f32[1,512]{1,0:T(1,128)S(1)} %get-tuple-element.54.refs_0_, f32[1,512]{1,0:T(1,128)S(1)} %collective-permute-done.10.refs_1_, f32[1,512]{1,0:T(1,128)S(1)} %collective-permute-done.11.refs_2_, f32[1,512]{1,0:T(1,128)S(1)} %collective-permute-done.12.refs_3_, ...), custom_call_target="tpu_custom_call" | custom-call | flops 268435456 | bytes 3145728 | tf_op jit(solution)/shard_map/pallas_call | solution.py:346
  (6 shorter events, 0.0 us)
Async XLA Ops:
  0.0 7.4 %collective-permute-start = (bf16[32,512]{1,0:T(8,128)(2,1)}, bf16[32,512]{1,0:T(8,128)(2,1)S(1)}, u32[]{:S(2)}, u32[]{:S(2)}) collective-permute-start(bf16[32,512]{1,0:T(8,128)(2,1)} %refs_6_.1), channel_id=1, source_target_pairs={{0,2},{1,3},{2,0},{3,1},{4,6},{5,7},{6,4},{7,5},{8,10},{9,11},{10,... | collective-permute-start | bytes 98312 | tf_op jit(solution)/shard_map/ppermute | solution.py:362
  4.0 5.9 %collective-permute-start.1 = (bf16[32,512]{1,0:T(8,128)(2,1)}, bf16[32,512]{1,0:T(8,128)(2,1)S(1)}, u32[]{:S(2)}, u32[]{:S(2)}) collective-permute-start(bf16[32,512]{1,0:T(8,128)(2,1)} %refs_6_.1), channel_id=1, source_target_pairs={{0,3},{1,2},{2,1},{3,0},{4,7},{5,6},{6,5},{7,4},{8,11},{9,10},{10,... | collective-permute-start | bytes 98312 | tf_op jit(solution)/shard_map/ppermute | solution.py:362
  5.4 4.6 %collective-permute-start.2 = (bf16[32,512]{1,0:T(8,128)(2,1)}, bf16[32,512]{1,0:T(8,128)(2,1)S(1)}, u32[]{:S(2)}, u32[]{:S(2)}) collective-permute-start(bf16[32,512]{1,0:T(8,128)(2,1)} %refs_6_.1), channel_id=1, source_target_pairs={{0,1},{1,0},{2,3},{3,2},{4,5},{5,4},{6,7},{7,6},{8,9},{9,8},{10,11... | collective-permute-start | bytes 98312 | tf_op jit(solution)/shard_map/ppermute | solution.py:362
  10.3 1.6 %collective-permute-start.3 = (bf16[144,1024]{1,0:T(8,128)(2,1)S(1)}, bf16[144,1024]{1,0:T(8,128)(2,1)S(1)}, u32[]{:S(2)}, u32[]{:S(2)}) collective-permute-start(bf16[144,1024]{1,0:T(8,128)(2,1)S(1)} %get-tuple-element.38.mine_ref), channel_id=1, source_target_pairs={{0,4},{4,0},{8,12},{12,8},{16,20},{20,16},{24,28},{28,24},{1,5},{5... | collective-permute-start | bytes 884744 | tf_op jit(solution)/shard_map/ppermute | solution.py:362
  10.4 5.2 %collective-permute-start.4 = (bf16[32,512]{1,0:T(8,128)(2,1)S(1)}, bf16[32,512]{1,0:T(8,128)(2,1)S(1)}, u32[]{:S(2)}, u32[]{:S(2)}) collective-permute-start(bf16[32,512]{1,0:T(8,128)(2,1)S(1)} %get-tuple-element.43.mine_ref), channel_id=1, source_target_pairs={{0,1},{1,0},{2,3},{3,2},{4,5},{5,4},{6,7},{7,6},{8,9},{9,8},{10,11... | collective-permute-start | bytes 98312 | tf_op jit(solution)/shard_map/ppermute | solution.py:362
  12.0 10.7 %collective-permute-start.6 = (bf16[144,512]{1,0:T(8,128)(2,1)S(1)}, bf16[144,512]{1,0:T(8,128)(2,1)S(1)}, u32[]{:S(2)}, u32[]{:S(2)}) collective-permute-start(bf16[144,512]{1,0:T(8,128)(2,1)S(1)} %shard_map.93.refs_5_), channel_id=1, source_target_pairs={{0,24},{4,28},{8,16},{12,20},{16,8},{20,12},{24,0},{28,4},{1,25},{... | collective-permute-start | bytes 442376 | tf_op jit(solution)/shard_map/ppermute | solution.py:362
  14.5 8.2 %collective-permute-start.7 = (bf16[144,512]{1,0:T(8,128)(2,1)S(1)}, bf16[144,512]{1,0:T(8,128)(2,1)S(1)}, u32[]{:S(2)}, u32[]{:S(2)}) collective-permute-start(bf16[144,512]{1,0:T(8,128)(2,1)S(1)} %shard_map.93.refs_5_), channel_id=1, source_target_pairs={{0,16},{4,20},{8,24},{12,28},{16,0},{20,4},{24,8},{28,12},{1,17},{... | collective-permute-start | bytes 442376 | tf_op jit(solution)/shard_map/ppermute | solution.py:362
  15.0 7.7 %collective-permute-start.8 = (bf16[144,512]{1,0:T(8,128)(2,1)S(1)}, bf16[144,512]{1,0:T(8,128)(2,1)S(1)}, u32[]{:S(2)}, u32[]{:S(2)}) collective-permute-start(bf16[144,512]{1,0:T(8,128)(2,1)S(1)} %shard_map.93.refs_5_), channel_id=1, source_target_pairs={{0,8},{4,12},{8,0},{12,4},{16,24},{20,28},{24,16},{28,20},{1,9},{5... | collective-permute-start | bytes 442376 | tf_op jit(solution)/shard_map/ppermute | solution.py:362
  15.6 5.9 %collective-permute-start.5 = (bf16[64,512]{1,0:T(8,128)(2,1)S(1)}, bf16[64,512]{1,0:T(8,128)(2,1)S(1)}, u32[]{:S(2)}, u32[]{:S(2)}) collective-permute-start(bf16[64,512]{1,0:T(8,128)(2,1)S(1)} %shard_map.95.refs_9_), channel_id=1, source_target_pairs={{0,2},{1,3},{2,0},{3,1},{4,6},{5,7},{6,4},{7,5},{8,10},{9,11},{10,... | collective-permute-start | bytes 196616 | tf_op jit(solution)/shard_map/ppermute | solution.py:362
  21.5 1.5 %copy-start = (f32[1024]{0:T(1024)S(1)}, f32[1024]{0:T(1024)}, u32[]{:S(2)}) copy-start(f32[1024]{0:T(1024)} %param.17) | copy-start | bytes 12292
  22.9 1.6 %collective-permute-start.9 = (bf16[256,512]{1,0:T(8,128)(2,1)S(1)}, bf16[256,512]{1,0:T(8,128)(2,1)S(1)}, u32[]{:S(2)}, u32[]{:S(2)}) collective-permute-start(bf16[256,512]{1,0:T(8,128)(2,1)S(1)} %shard_map.97.refs_5_), channel_id=1, source_target_pairs={{0,4},{4,0},{8,12},{12,8},{16,20},{20,16},{24,28},{28,24},{1,5},{5... | collective-permute-start | bytes 786440 | tf_op jit(solution)/shard_map/ppermute | solution.py:362
  25.2 4.5 %collective-permute-start.10 = (f32[1,512]{1,0:T(1,128)S(1)}, f32[1,512]{1,0:T(1,128)S(1)}, u32[]{:S(2)}, u32[]{:S(2)}) collective-permute-start(f32[1,512]{1,0:T(1,128)S(1)} %get-tuple-element.54.refs_0_), channel_id=1, source_target_pairs={{0,2},{1,3},{2,0},{3,1},{4,6},{5,7},{6,4},{7,5},{8,10},{9,11},{10,... | collective-permute-start | bytes 6152 | tf_op jit(solution)/shard_map/ppermute | solution.py:362
  25.9 5.4 %collective-permute-start.11 = (f32[1,512]{1,0:T(1,128)S(1)}, f32[1,512]{1,0:T(1,128)S(1)}, u32[]{:S(2)}, u32[]{:S(2)}) collective-permute-start(f32[1,512]{1,0:T(1,128)S(1)} %get-tuple-element.54.refs_0_), channel_id=1, source_target_pairs={{0,3},{1,2},{2,1},{3,0},{4,7},{5,6},{6,5},{7,4},{8,11},{9,10},{10,... | collective-permute-start | bytes 6152 | tf_op jit(solution)/shard_map/ppermute | solution.py:362
  27.5 3.8 %collective-permute-start.12 = (f32[1,512]{1,0:T(1,128)S(1)}, f32[1,512]{1,0:T(1,128)S(1)}, u32[]{:S(2)}, u32[]{:S(2)}) collective-permute-start(f32[1,512]{1,0:T(1,128)S(1)} %get-tuple-element.54.refs_0_), channel_id=1, source_target_pairs={{0,1},{1,0},{2,3},{3,2},{4,5},{5,4},{6,7},{7,6},{8,9},{9,8},{10,11... | collective-permute-start | bytes 6152 | tf_op jit(solution)/shard_map/ppermute | solution.py:362

commit v9 on v8

--- a/solution.py
+++ b/solution.py
@@ -199,37 +199,50 @@
                 span_refs[0][index, :, cols] = (transposed_dot(mix, expand[:, cols]) * swish).astype(bf16)
 
 
+def near_body(spans, paired, start, scores_ref, turned_ref, refs, near_ref):
+    base_ref, own_ref, far_ref, core_ref, scaled_ref = refs[:5]
+    span_refs = refs[5:]
+    tokens, size = turned_ref.shape
+    has_core = lax.rem(lax.axis_index("seq"), 2) == 1
+    for group in range(tokens // GROUP):
+        at = group_slice(group)
+        for cols in blocks_of(near_ref.shape[1]):
+            of = pl.ds(pl.multiple_of(start + cols.start, BLOCK), BLOCK)
+            own = jnp.dot(scores_ref[at, :], scaled_ref[at, of], preferred_element_type=f32)
+            total = base_ref[at, of] + own_ref[at, of] * own
+            for index, (later, _, _, _) in enumerate(spans):
+                if later == group:
+                    rows = slice(index * size, (index + 1) * size)
+                    reach = jnp.dot(turned_ref[at, :], span_refs[0][rows, of], preferred_element_type=f32)
+                    total = total + span_refs[1][index, :, of].astype(f32) * reach
+            if paired:
+                reach = jnp.dot(turned_ref[at, :], core_ref[:size, of], preferred_element_type=f32)
+                reach = jnp.where(has_core, reach, 0.0)
+                total = total + far_ref[0, at, of].astype(f32) * reach
+            near_ref[at, cols] = total
+
+
 def near_kernel(parts, spans, paired, *refs):
-    base_ref, own_ref, far_ref, core_ref, scaled_ref = refs[:5]
-    count = 5 + parts + parts // 2
-    in_refs, out_refs = refs[5 : 5 + parts], refs[5 + parts : count]
-    span_refs = refs[count:-2]
-    near_ref, turned_ref = refs[-2:]
-    tokens, width = base_ref.shape
+    count = parts + parts // 2
+    in_refs, out_refs, rest = refs[:parts], refs[parts:count], refs[count:-3]
+    near_ref, turned_ref, scores_ref = refs[-3:]
     in_map = map_rows(in_refs)
     turned = jnp.transpose(out_map_rows(out_refs))
     turned_ref[...] = turned
-    size = in_map.shape[0]
     row = lax.broadcasted_iota(jnp.int32, (GROUP, GROUP), 0)
     col = lax.broadcasted_iota(jnp.int32, (GROUP, GROUP), 1)
-    has_core = lax.rem(lax.axis_index("seq"), 2) == 1
-    for group in range(tokens // GROUP):
+    for group in range(turned.shape[0] // GROUP):
         at = group_slice(group)
         scores = jnp.dot(turned[at], in_map[:, at], preferred_element_type=f32)
-        scores = jnp.where(row >= col, scores, 0.0).astype(bf16)
-        for cols in blocks_of(width):
-            own = jnp.dot(scores, scaled_ref[at, cols], preferred_element_type=f32)
-            total = base_ref[at, cols] + own_ref[at, cols] * own
-            for index, (later, _, _, _) in enumerate(spans):
-                if later == group:
-                    rows = slice(index * size, (index + 1) * size)
-                    reach = jnp.dot(turned[at], span_refs[0][rows, cols], preferred_element_type=f32)
-                    total = total + span_refs[1][index, :, cols].astype(f32) * reach
-            if paired:
-                reach = jnp.dot(turned[at], core_ref[:size, cols], preferred_element_type=f32)
-                reach = jnp.where(has_core, reach, 0.0)
-                total = total + far_ref[0, at, cols].astype(f32) * reach
-            near_ref[at, cols] = total
+        scores_ref[at, :] = jnp.where(row >= col, scores, 0.0).astype(bf16)
+    start = lax.rem(lax.axis_index("seq"), 2) * near_ref.shape[1] if paired else 0
+    near_body(spans, paired, start, scores_ref, turned_ref, rest, near_ref)
+
+
+def other_near_kernel(spans, scores_ref, turned_ref, _, *refs):
+    near_ref = refs[-1]
+    start = (1 - lax.rem(lax.axis_index("seq"), 2)) * near_ref.shape[1]
+    near_body(spans, True, start, scores_ref, turned_ref, refs[:-1], near_ref)
 
 
 def far_body(turned_ref, near_ref, far_ref, gain_ref, start, columns, levels, state_of, gated_ref):
@@ -237,7 +250,7 @@
     squares = jnp.zeros((tokens, 128), f32)
     for cols in blocks_of(columns):
         at = pl.ds(pl.multiple_of(start + cols.start, BLOCK), BLOCK)
-        total = near_ref[:, at]
+        total = near_ref[:, cols]
         for level in levels:
             state = state_of(level, cols, at).astype(bf16)
             reach = jnp.dot(turned_ref[...], state, preferred_element_type=f32)
@@ -458,15 +471,12 @@
         flops=21 * dense // 4,
         bytes_accessed=0,
     )
-    near, turned = call(
+    near_args = base, own_factor, far, theirs if pairs else message, scaled, *span_states, *span_factors
+    near_shape = shaped((tokens, width // 2 if pairs else width), f32)
+    near, turned, scores = call(
         functools.partial(near_kernel, parts, spans, pairs),
-        (shaped((tokens, width), f32), shaped((tokens, size), bf16)),
-        (
-            *(base, own_factor, far, theirs if pairs else message, scaled),
-            *(*in_maps, *out_maps, *span_states, *span_factors),
-        ),
-        flops=0,
-        bytes_accessed=0,
+        (near_shape, shaped((tokens, size), bf16), shaped((tokens, GROUP), bf16)),
+        (*in_maps, *out_maps, *near_args),
     )
     gain = norm_gain[None, :]
     sums_shape = shaped((1, tokens), f32)
@@ -480,6 +490,9 @@
             bytes_accessed=area,
         )
         other = flip(own, "seq", 1)
+        other_near = call(
+            functools.partial(other_near_kernel, spans), near_shape, (scores, turned, own, *near_args), flops=dense
+        )
         gated_shape = shaped((tokens, width // 2), f32)
         own_gated, own_squares = call(
             functools.partial(far_kernel_of_half, True),
@@ -491,7 +504,7 @@
         other_gated, sums = call(
             functools.partial(far_kernel_of_half, False),
             (gated_shape, sums_shape),
-            (turned, near, far, gain, theirs, other, own_squares),
+            (turned, other_near, far, gain, theirs, other, own_squares),
             flops=2 * dense,
             bytes_accessed=6 * area,
         )

time: 32.7 us -> 32.6 us (level)
    pallas_call x10 -> x11, Pallas kernels: 7.83 us -> 7.81 us  [call(): pl.pallas_call(kernel, out_shape=out_shape, in_specs=specs, out_specs=jax...]
where the time goes in v9:
time: 32.6 us; the launch traced here: 32.4 us
  starting transfers between devices  14.2 us (44%)
  waiting for transfers between devices  10.2 us (31%)
  Pallas kernels  7.81 us (24%)
    ppermute x13, starting transfers between devices, flip(): lax.ppermute(array, axis, [(i, i ^ mask) for i in range(lax.axis_size(axi...  14.2 us
    ppermute x13, waiting for transfers between devices, flip(): lax.ppermute(array, axis, [(i, i ^ mask) for i in range(lax.axis_size(axi...  10.2 us
    pallas_call x11, Pallas kernels, call(): pl.pallas_call(kernel, out_shape=out_shape, in_specs=specs, out_specs=jax...  7.81 us
  transfers between devices with their start and end apart: 13, of which 6 were waited for; matrix products, arithmetic and copies ran while one was open for 0% of the time, Pallas kernels for 17%

profile of v9, /device:TPU:0, one launch (start us, length us, event | category | flops | bytes accessed | tf_op | source)
XLA Modules:
  0.0 32.4 jit_solution(14420929744957458175)
XLA Ops:
  0.0 4.0 %collective-permute-start = (bf16[32,512]{1,0:T(8,128)(2,1)}, bf16[32,512]{1,0:T(8,128)(2,1)S(1)}, u32[]{:S(2)}, u32[]{:S(2)}) collective-permute-start(bf16[32,512]{1,0:T(8,128)(2,1)} %refs_6_.1), channel_id=1, source_target_pairs={{0,2},{1,3},{2,0},{3,1},{4,6},{5,7},{6,4},{7,5},{8,10},{9,11},{10,... | collective-permute-start | bytes 98312 | tf_op jit(solution)/shard_map/ppermute | solution.py:375
  4.0 1.3 %collective-permute-start.1 = (bf16[32,512]{1,0:T(8,128)(2,1)}, bf16[32,512]{1,0:T(8,128)(2,1)S(1)}, u32[]{:S(2)}, u32[]{:S(2)}) collective-permute-start(bf16[32,512]{1,0:T(8,128)(2,1)} %refs_6_.1), channel_id=1, source_target_pairs={{0,3},{1,2},{2,1},{3,0},{4,7},{5,6},{6,5},{7,4},{8,11},{9,10},{10,... | collective-permute-start | bytes 98312 | tf_op jit(solution)/shard_map/ppermute | solution.py:375
  5.4 0.2 collective-permute-start.2
  5.6 1.8 %shard_map.91 = (bf16[512,1024]{1,0:T(8,128)(2,1)S(1)}, f32[16,512]{1,0:T(8,128)S(1)}, bf16[512,1024]{1,0:T(8,128)(2,1)S(1)}, bf16[512,1024]{1,0:T(8,128)(2,1)S(...) custom-call(f32[16,512]{1,0:T(8,128)} %refs_0_.1, ...), custom_call_target="tpu_custom_call" | custom-call | flops 4294967296 | bytes 2097152 | tf_op jit(solution)/shard_map/pallas_call | solution.py:359
  7.4 2.5 %collective-permute-done.1.refs_2_ = bf16[32,512]{1,0:T(8,128)(2,1)S(1)} collective-permute-done((bf16[32,512]{1,0:T(8,128)(2,1)}, bf16[32,512]{1,0:T(8,128)(2,1)S(1)}, u32[]{:S(2)}, u32[]{:S(2)}) %collective-permute-start.1) | collective-permute-done | bytes 32800 | tf_op jit(solution)/shard_map/ppermute | solution.py:375
  10.0 0.0 collective-permute-done.2.refs_3_
  10.0 0.3 shard_map.92
  10.3 0.1 collective-permute-start.5
  10.4 0.1 collective-permute-start.3
  10.5 1.5 %collective-permute-done.5.theirs_ref.refs_9_.refs_3_.refs_4_ = bf16[144,1024]{1,0:T(8,128)(2,1)S(1)} collective-permute-done((bf16[144,1024]{1,0:T(8,128)(2,1)S(1)}, bf16[144,1024]{1,0:T(8,128)(2,1)S(1)}, u32[]{:S(2)}, u32[]{:S(2)}) %collective-permute-start.5) | collective-permute-done | bytes 294944 | tf_op jit(solution)/shard_map/ppermute | solution.py:375
  11.9 0.1 shard_map.94.refs_5_
  12.0 2.5 %collective-permute-start.6 = (bf16[144,512]{1,0:T(8,128)(2,1)S(1)}, bf16[144,512]{1,0:T(8,128)(2,1)S(1)}, u32[]{:S(2)}, u32[]{:S(2)}) collective-permute-start(bf16[144,512]{1,0:T(8,128)(2,1)S(1)} %shard_map.94.refs_5_), channel_id=1, source_target_pairs={{0,24},{4,28},{8,16},{12,20},{16,8},{20,12},{24,0},{28,4},{1,25},{... | collective-permute-start | bytes 442376 | tf_op jit(solution)/shard_map/ppermute | solution.py:375
  14.5 0.5 %collective-permute-start.7 = (bf16[144,512]{1,0:T(8,128)(2,1)S(1)}, bf16[144,512]{1,0:T(8,128)(2,1)S(1)}, u32[]{:S(2)}, u32[]{:S(2)}) collective-permute-start(bf16[144,512]{1,0:T(8,128)(2,1)S(1)} %shard_map.94.refs_5_), channel_id=1, source_target_pairs={{0,16},{4,20},{8,24},{12,28},{16,0},{20,4},{24,8},{28,12},{1,17},{... | collective-permute-start | bytes 442376 | tf_op jit(solution)/shard_map/ppermute | solution.py:375
  15.0 0.5 %collective-permute-start.8 = (bf16[144,512]{1,0:T(8,128)(2,1)S(1)}, bf16[144,512]{1,0:T(8,128)(2,1)S(1)}, u32[]{:S(2)}, u32[]{:S(2)}) collective-permute-start(bf16[144,512]{1,0:T(8,128)(2,1)S(1)} %shard_map.94.refs_5_), channel_id=1, source_target_pairs={{0,8},{4,12},{8,0},{12,4},{16,24},{20,28},{24,16},{28,20},{1,9},{5... | collective-permute-start | bytes 442376 | tf_op jit(solution)/shard_map/ppermute | solution.py:375
  15.6 1.3 %collective-permute-start.4 = (bf16[64,512]{1,0:T(8,128)(2,1)S(1)}, bf16[64,512]{1,0:T(8,128)(2,1)S(1)}, u32[]{:S(2)}, u32[]{:S(2)}) collective-permute-start(bf16[64,512]{1,0:T(8,128)(2,1)S(1)} %shard_map.93.refs_4_), channel_id=1, source_target_pairs={{0,2},{1,3},{2,0},{3,1},{4,6},{5,7},{6,4},{7,5},{8,10},{9,11},{10,... | collective-permute-start | bytes 196616 | tf_op jit(solution)/shard_map/ppermute | solution.py:375
  16.9 1.8 %shard_map.95 = (f32[512,1024]{1,0:T(8,128)S(1)}, f32[512,1024]{1,0:T(8,128)S(1)}, bf16[3,512,1024]{2,1,0:T(8,128)(2,1)S(1)}, bf16[1,256,1024]{2,1,0:T(8,128)(2,1)S(1)}) custom-call(bf16[512,1024]{1,0:T(8,128)(2,1)S(1)} %get-tuple-element.38.refs_0_, bf16[512,1024]{1,0:T(8,128)(2,1)S(1)} %get-tuple-element.39.refs_1_, ...), custom_call_target="tpu_custom_call" | custom-call | flops 1409286144 | tf_op jit(solution)/shard_map/pallas_call | solution.py:359
  18.7 2.8 %collective-permute-done.4.refs_5_ = bf16[64,512]{1,0:T(8,128)(2,1)S(1)} collective-permute-done((bf16[64,512]{1,0:T(8,128)(2,1)S(1)}, bf16[64,512]{1,0:T(8,128)(2,1)S(1)}, u32[]{:S(2)}, u32[]{:S(2)}) %collective-permute-start.4) | collective-permute-done | bytes 65568 | tf_op jit(solution)/shard_map/ppermute | solution.py:375
  21.5 0.7 %shard_map.96 = (f32[512,512]{1,0:T(8,128)S(1)}, bf16[512,128]{1,0:T(8,128)(2,1)S(1)}, bf16[512,256]{1,0:T(8,128)(2,1)S(1)}) custom-call(bf16[32,512]{1,0:T(8,128)(2,1)S(1)} %get-tuple-element.32.refs_0_, bf16[32,512]{1,0:T(8,128)(2,1)S(1)} %collective-permute-done.refs_1_, bf16[32,512]{1,0:T(8,128)(2,1)S(1)} %collective-permute-done.1.refs_2_, ...), custom_call_target="tpu_custom_call" | custom-call | tf_op jit(solution)/shard_map/pallas_call | solution.py:359
  22.2 0.1 shard_map.97._.refs_5_
  22.4 0.1 collective-permute-start.9
  22.4 0.0 copy-start
  22.4 0.6 %shard_map.98.refs_1_ = f32[512,512]{1,0:T(8,128)S(1)} custom-call(bf16[512,256]{1,0:T(8,128)(2,1)S(1)} %get-tuple-element.48.scores_ref, bf16[512,128]{1,0:T(8,128)(2,1)S(1)} %get-tuple-element.47.turned_ref.refs_0_, bf16[256,512]{1,0:T(8,128)(2,1)S(1)} %shard_map.97._.refs_5_, f32[512,1024]{1,0:T(8,128)S(1)} %get-tuple-element.42.refs_6_.refs_0_, ...), custom_call_target="tpu_custom_call" | custom-call | flops 268435456 | tf_op jit(solution)/shard_map/pallas_call | solution.py:359
  23.0 0.1 copy-done
  23.1 0.5 %shard_map.99 = (f32[512,512]{1,0:T(8,128)S(1)}, f32[512,128]{1,0:T(8,128)S(1)}) custom-call(bf16[512,128]{1,0:T(8,128)(2,1)S(1)} %get-tuple-element.47.turned_ref.refs_0_, f32[512,512]{1,0:T(8,128)S(1)} %get-tuple-element.54.refs_1_, bf16[3,512,1024]{2,1,0:T(8,128)(2,1)S(1)} %get-tuple-element.53.refs_8_.refs_2_, f32[1,1024]{1,0:T(1,128)S(1)} %bitcast.3, ...), custom_call_target="tpu_custom_call" | custom-call | flops 536870912 | bytes 3145728 | tf_op jit(solution)/shard_map/pallas_call | solution.py:359
  23.6 0.3 collective-permute-done.9.refs_5_
  24.0 0.7 %shard_map.100 = (f32[512,512]{1,0:T(8,128)S(1)}, f32[1,512]{1,0:T(1,128)S(1)}) custom-call(bf16[512,128]{1,0:T(8,128)(2,1)S(1)} %get-tuple-element.47.turned_ref.refs_0_, f32[512,512]{1,0:T(8,128)S(1)} %shard_map.98.refs_1_, bf16[3,512,1024]{2,1,0:T(8,128)(2,1)S(1)} %get-tuple-element.53.refs_8_.refs_2_, f32[1,1024]{1,0:T(1,128)S(1)} %bitcast.4, ...), custom_call_target="tpu_custom_call" | custom-call | flops 536870912 | bytes 3145728 | tf_op jit(solution)/shard_map/pallas_call | solution.py:359
  24.6 1.2 %collective-permute-start.10 = (f32[1,512]{1,0:T(1,128)S(1)}, f32[1,512]{1,0:T(1,128)S(1)}, u32[]{:S(2)}, u32[]{:S(2)}) collective-permute-start(f32[1,512]{1,0:T(1,128)S(1)} %get-tuple-element.56.refs_0_), channel_id=1, source_target_pairs={{0,2},{1,3},{2,0},{3,1},{4,6},{5,7},{6,4},{7,5},{8,10},{9,11},{10,... | collective-permute-start | bytes 6152 | tf_op jit(solution)/shard_map/ppermute | solution.py:375
  25.8 1.7 %collective-permute-start.11 = (f32[1,512]{1,0:T(1,128)S(1)}, f32[1,512]{1,0:T(1,128)S(1)}, u32[]{:S(2)}, u32[]{:S(2)}) collective-permute-start(f32[1,512]{1,0:T(1,128)S(1)} %get-tuple-element.56.refs_0_), channel_id=1, source_target_pairs={{0,3},{1,2},{2,1},{3,0},{4,7},{5,6},{6,5},{7,4},{8,11},{9,10},{10,... | collective-permute-start | bytes 6152 | tf_op jit(solution)/shard_map/ppermute | solution.py:375
  27.5 0.7 %collective-permute-start.12 = (f32[1,512]{1,0:T(1,128)S(1)}, f32[1,512]{1,0:T(1,128)S(1)}, u32[]{:S(2)}, u32[]{:S(2)}) collective-permute-start(f32[1,512]{1,0:T(1,128)S(1)} %get-tuple-element.56.refs_0_), channel_id=1, source_target_pairs={{0,1},{1,0},{2,3},{3,2},{4,5},{5,4},{6,7},{7,6},{8,9},{9,8},{10,11... | collective-permute-start | bytes 6152 | tf_op jit(solution)/shard_map/ppermute | solution.py:375
  28.1 1.0 %collective-permute-done.10.refs_1_ = f32[1,512]{1,0:T(1,128)S(1)} collective-permute-done((f32[1,512]{1,0:T(1,128)S(1)}, f32[1,512]{1,0:T(1,128)S(1)}, u32[]{:S(2)}, u32[]{:S(2)}) %collective-permute-start.10) | collective-permute-done | bytes 2080 | tf_op jit(solution)/shard_map/ppermute | solution.py:375
  29.1 2.0 %collective-permute-done.11.refs_2_ = f32[1,512]{1,0:T(1,128)S(1)} collective-permute-done((f32[1,512]{1,0:T(1,128)S(1)}, f32[1,512]{1,0:T(1,128)S(1)}, u32[]{:S(2)}, u32[]{:S(2)}) %collective-permute-start.11) | collective-permute-done | bytes 2080 | tf_op jit(solution)/shard_map/ppermute | solution.py:375
  31.2 1.3 %shard_map.101 = bf16[512,1024]{1,0:T(8,128)(2,1)} custom-call(f32[1,512]{1,0:T(1,128)S(1)} %get-tuple-element.56.refs_0_, f32[1,512]{1,0:T(1,128)S(1)} %collective-permute-done.10.refs_1_, f32[1,512]{1,0:T(1,128)S(1)} %collective-permute-done.11.refs_2_, f32[1,512]{1,0:T(1,128)S(1)} %collective-permute-done.12.refs_3_, ...), custom_call_target="tpu_custom_call" | custom-call | flops 268435456 | bytes 3145728 | tf_op jit(solution)/shard_map/pallas_call | solution.py:359
  (7 shorter events, 0.0 us)
Async XLA Ops:
  0.0 7.4 %collective-permute-start = (bf16[32,512]{1,0:T(8,128)(2,1)}, bf16[32,512]{1,0:T(8,128)(2,1)S(1)}, u32[]{:S(2)}, u32[]{:S(2)}) collective-permute-start(bf16[32,512]{1,0:T(8,128)(2,1)} %refs_6_.1), channel_id=1, source_target_pairs={{0,2},{1,3},{2,0},{3,1},{4,6},{5,7},{6,4},{7,5},{8,10},{9,11},{10,... | collective-permute-start | bytes 98312 | tf_op jit(solution)/shard_map/ppermute | solution.py:375
  4.0 5.9 %collective-permute-start.1 = (bf16[32,512]{1,0:T(8,128)(2,1)}, bf16[32,512]{1,0:T(8,128)(2,1)S(1)}, u32[]{:S(2)}, u32[]{:S(2)}) collective-permute-start(bf16[32,512]{1,0:T(8,128)(2,1)} %refs_6_.1), channel_id=1, source_target_pairs={{0,3},{1,2},{2,1},{3,0},{4,7},{5,6},{6,5},{7,4},{8,11},{9,10},{10,... | collective-permute-start | bytes 98312 | tf_op jit(solution)/shard_map/ppermute | solution.py:375
  5.4 4.6 %collective-permute-start.2 = (bf16[32,512]{1,0:T(8,128)(2,1)}, bf16[32,512]{1,0:T(8,128)(2,1)S(1)}, u32[]{:S(2)}, u32[]{:S(2)}) collective-permute-start(bf16[32,512]{1,0:T(8,128)(2,1)} %refs_6_.1), channel_id=1, source_target_pairs={{0,1},{1,0},{2,3},{3,2},{4,5},{5,4},{6,7},{7,6},{8,9},{9,8},{10,11... | collective-permute-start | bytes 98312 | tf_op jit(solution)/shard_map/ppermute | solution.py:375
  10.3 1.6 %collective-permute-start.5 = (bf16[144,1024]{1,0:T(8,128)(2,1)S(1)}, bf16[144,1024]{1,0:T(8,128)(2,1)S(1)}, u32[]{:S(2)}, u32[]{:S(2)}) collective-permute-start(bf16[144,1024]{1,0:T(8,128)(2,1)S(1)} %get-tuple-element.36.mine_ref), channel_id=1, source_target_pairs={{0,4},{4,0},{8,12},{12,8},{16,20},{20,16},{24,28},{28,24},{1,5},{5... | collective-permute-start | bytes 884744 | tf_op jit(solution)/shard_map/ppermute | solution.py:375
  10.4 5.2 %collective-permute-start.3 = (bf16[32,512]{1,0:T(8,128)(2,1)S(1)}, bf16[32,512]{1,0:T(8,128)(2,1)S(1)}, u32[]{:S(2)}, u32[]{:S(2)}) collective-permute-start(bf16[32,512]{1,0:T(8,128)(2,1)S(1)} %get-tuple-element.37.mine_ref), channel_id=1, source_target_pairs={{0,1},{1,0},{2,3},{3,2},{4,5},{5,4},{6,7},{7,6},{8,9},{9,8},{10,11... | collective-permute-start | bytes 98312 | tf_op jit(solution)/shard_map/ppermute | solution.py:375
  12.0 10.2 %collective-permute-start.6 = (bf16[144,512]{1,0:T(8,128)(2,1)S(1)}, bf16[144,512]{1,0:T(8,128)(2,1)S(1)}, u32[]{:S(2)}, u32[]{:S(2)}) collective-permute-start(bf16[144,512]{1,0:T(8,128)(2,1)S(1)} %shard_map.94.refs_5_), channel_id=1, source_target_pairs={{0,24},{4,28},{8,16},{12,20},{16,8},{20,12},{24,0},{28,4},{1,25},{... | collective-permute-start | bytes 442376 | tf_op jit(solution)/shard_map/ppermute | solution.py:375
  14.5 7.7 %collective-permute-start.7 = (bf16[144,512]{1,0:T(8,128)(2,1)S(1)}, bf16[144,512]{1,0:T(8,128)(2,1)S(1)}, u32[]{:S(2)}, u32[]{:S(2)}) collective-permute-start(bf16[144,512]{1,0:T(8,128)(2,1)S(1)} %shard_map.94.refs_5_), channel_id=1, source_target_pairs={{0,16},{4,20},{8,24},{12,28},{16,0},{20,4},{24,8},{28,12},{1,17},{... | collective-permute-start | bytes 442376 | tf_op jit(solution)/shard_map/ppermute | solution.py:375
  15.0 7.2 %collective-permute-start.8 = (bf16[144,512]{1,0:T(8,128)(2,1)S(1)}, bf16[144,512]{1,0:T(8,128)(2,1)S(1)}, u32[]{:S(2)}, u32[]{:S(2)}) collective-permute-start(bf16[144,512]{1,0:T(8,128)(2,1)S(1)} %shard_map.94.refs_5_), channel_id=1, source_target_pairs={{0,8},{4,12},{8,0},{12,4},{16,24},{20,28},{24,16},{28,20},{1,9},{5... | collective-permute-start | bytes 442376 | tf_op jit(solution)/shard_map/ppermute | solution.py:375
  15.6 5.9 %collective-permute-start.4 = (bf16[64,512]{1,0:T(8,128)(2,1)S(1)}, bf16[64,512]{1,0:T(8,128)(2,1)S(1)}, u32[]{:S(2)}, u32[]{:S(2)}) collective-permute-start(bf16[64,512]{1,0:T(8,128)(2,1)S(1)} %shard_map.93.refs_4_), channel_id=1, source_target_pairs={{0,2},{1,3},{2,0},{3,1},{4,6},{5,7},{6,4},{7,5},{8,10},{9,11},{10,... | collective-permute-start | bytes 196616 | tf_op jit(solution)/shard_map/ppermute | solution.py:375
  22.4 1.6 %collective-permute-start.9 = (bf16[256,512]{1,0:T(8,128)(2,1)S(1)}, bf16[256,512]{1,0:T(8,128)(2,1)S(1)}, u32[]{:S(2)}, u32[]{:S(2)}) collective-permute-start(bf16[256,512]{1,0:T(8,128)(2,1)S(1)} %shard_map.97._.refs_5_), channel_id=1, source_target_pairs={{0,4},{4,0},{8,12},{12,8},{16,20},{20,16},{24,28},{28,24},{1,5},{5... | collective-permute-start | bytes 786440 | tf_op jit(solution)/shard_map/ppermute | solution.py:375
  22.4 0.7 %copy-start = (f32[1024]{0:T(1024)S(1)}, f32[1024]{0:T(1024)}, u32[]{:S(2)}) copy-start(f32[1024]{0:T(1024)} %param.17) | copy-start | bytes 12292
  24.6 4.5 %collective-permute-start.10 = (f32[1,512]{1,0:T(1,128)S(1)}, f32[1,512]{1,0:T(1,128)S(1)}, u32[]{:S(2)}, u32[]{:S(2)}) collective-permute-start(f32[1,512]{1,0:T(1,128)S(1)} %get-tuple-element.56.refs_0_), channel_id=1, source_target_pairs={{0,2},{1,3},{2,0},{3,1},{4,6},{5,7},{6,4},{7,5},{8,10},{9,11},{10,... | collective-permute-start | bytes 6152 | tf_op jit(solution)/shard_map/ppermute | solution.py:375
  25.8 5.4 %collective-permute-start.11 = (f32[1,512]{1,0:T(1,128)S(1)}, f32[1,512]{1,0:T(1,128)S(1)}, u32[]{:S(2)}, u32[]{:S(2)}) collective-permute-start(f32[1,512]{1,0:T(1,128)S(1)} %get-tuple-element.56.refs_0_), channel_id=1, source_target_pairs={{0,3},{1,2},{2,1},{3,0},{4,7},{5,6},{6,5},{7,4},{8,11},{9,10},{10,... | collective-permute-start | bytes 6152 | tf_op jit(solution)/shard_map/ppermute | solution.py:375
  27.5 3.7 %collective-permute-start.12 = (f32[1,512]{1,0:T(1,128)S(1)}, f32[1,512]{1,0:T(1,128)S(1)}, u32[]{:S(2)}, u32[]{:S(2)}) collective-permute-start(f32[1,512]{1,0:T(1,128)S(1)} %get-tuple-element.56.refs_0_), channel_id=1, source_target_pairs={{0,1},{1,0},{2,3},{3,2},{4,5},{5,4},{6,7},{7,6},{8,9},{9,8},{10,11... | collective-permute-start | bytes 6152 | tf_op jit(solution)/shard_map/ppermute | solution.py:375

commit v10 on v9

--- a/solution.py
+++ b/solution.py
@@ -222,7 +222,7 @@
             near_ref[at, cols] = total
 
 
-def near_kernel(parts, spans, paired, *refs):
+def near_kernel(parts, spans, paired, _, *refs):
     count = parts + parts // 2
     in_refs, out_refs, rest = refs[:parts], refs[parts:count], refs[count:-3]
     near_ref, turned_ref, scores_ref = refs[-3:]
@@ -473,15 +473,16 @@
     )
     near_args = base, own_factor, far, theirs if pairs else message, scaled, *span_states, *span_factors
     near_shape = shaped((tokens, width // 2 if pairs else width), f32)
+    received = [flip(message, "seq", mask) for mask in (6, 4, 2)] if pairs else [message]
     near, turned, scores = call(
         functools.partial(near_kernel, parts, spans, pairs),
         (near_shape, shaped((tokens, size), bf16), shaped((tokens, GROUP), bf16)),
-        (*in_maps, *out_maps, *near_args),
+        (received[0], *in_maps, *out_maps, *near_args),
+        flops=4 * dense,
     )
     gain = norm_gain[None, :]
     sums_shape = shaped((1, tokens), f32)
     if pairs:
-        received = [flip(message, "seq", mask) for mask in (6, 4, 2)]
         *received, near, far = lax.optimization_barrier((*received, near, far))
         own = call(
             functools.partial(combine_kernel, size),

time: 32.6 us -> 33.4 us (1.025)
  starting transfers between devices: 14.2 us -> 16.1 us
  waiting for transfers between devices: 10.2 us -> 9.09 us
    ppermute x13, starting transfers between devices: 14.2 us -> 16.1 us  [flip(): lax.ppermute(array, axis, [(i, i ^ mask) for i in range(lax.axis_size(axi...]
    ppermute x13, waiting for transfers between devices: 10.2 us -> 9.09 us  [flip(): lax.ppermute(array, axis, [(i, i ^ mask) for i in range(lax.axis_size(axi...]
  transfers between devices with their start and end apart: 13 -> 13, of which waited for: 6 -> 9; matrix products, arithmetic and copies ran while one was open for 0% -> 0% of each run, Pallas kernels for 17% -> 16%
where the time goes in v10:
time: 33.4 us; the launch traced here: 33.2 us
  starting transfers between devices  16.1 us (48%)
  waiting for transfers between devices  9.09 us (27%)
  Pallas kernels  7.81 us (23%)
    ppermute x13, starting transfers between devices, flip(): lax.ppermute(array, axis, [(i, i ^ mask) for i in range(lax.axis_size(axi...  16.1 us
    ppermute x13, waiting for transfers between devices, flip(): lax.ppermute(array, axis, [(i, i ^ mask) for i in range(lax.axis_size(axi...  9.09 us
    pallas_call x11, Pallas kernels, call(): pl.pallas_call(kernel, out_shape=out_shape, in_specs=specs, out_specs=jax...  7.81 us
  transfers between devices with their start and end apart: 13, of which 9 were waited for; matrix products, arithmetic and copies ran while one was open for 0% of the time, Pallas kernels for 16%

profile of v10, /device:TPU:0, one launch (start us, length us, event | category | flops | bytes accessed | tf_op | source)
XLA Modules:
  0.0 33.2 jit_solution(1311961993226578452)
XLA Ops:
  0.0 4.0 %collective-permute-start = (bf16[32,512]{1,0:T(8,128)(2,1)}, bf16[32,512]{1,0:T(8,128)(2,1)S(1)}, u32[]{:S(2)}, u32[]{:S(2)}) collective-permute-start(bf16[32,512]{1,0:T(8,128)(2,1)} %refs_6_.1), channel_id=1, source_target_pairs={{0,2},{1,3},{2,0},{3,1},{4,6},{5,7},{6,4},{7,5},{8,10},{9,11},{10,... | collective-permute-start | bytes 98312 | tf_op jit(solution)/shard_map/ppermute | solution.py:375
  4.0 1.3 %collective-permute-start.1 = (bf16[32,512]{1,0:T(8,128)(2,1)}, bf16[32,512]{1,0:T(8,128)(2,1)S(1)}, u32[]{:S(2)}, u32[]{:S(2)}) collective-permute-start(bf16[32,512]{1,0:T(8,128)(2,1)} %refs_6_.1), channel_id=1, source_target_pairs={{0,3},{1,2},{2,1},{3,0},{4,7},{5,6},{6,5},{7,4},{8,11},{9,10},{10,... | collective-permute-start | bytes 98312 | tf_op jit(solution)/shard_map/ppermute | solution.py:375
  5.4 0.2 collective-permute-start.2
  5.6 1.8 %shard_map.91 = (bf16[512,1024]{1,0:T(8,128)(2,1)S(1)}, f32[16,512]{1,0:T(8,128)S(1)}, bf16[512,1024]{1,0:T(8,128)(2,1)S(1)}, bf16[512,1024]{1,0:T(8,128)(2,1)S(...) custom-call(f32[16,512]{1,0:T(8,128)} %refs_0_.1, ...), custom_call_target="tpu_custom_call" | custom-call | flops 4294967296 | bytes 2097152 | tf_op jit(solution)/shard_map/pallas_call | solution.py:359
  7.4 2.5 %collective-permute-done.1.refs_2_ = bf16[32,512]{1,0:T(8,128)(2,1)S(1)} collective-permute-done((bf16[32,512]{1,0:T(8,128)(2,1)}, bf16[32,512]{1,0:T(8,128)(2,1)S(1)}, u32[]{:S(2)}, u32[]{:S(2)}) %collective-permute-start.1) | collective-permute-done | bytes 32800 | tf_op jit(solution)/shard_map/ppermute | solution.py:375
  10.0 0.3 shard_map.92
  10.3 0.1 collective-permute-start.3
  10.4 0.1 collective-permute-start.5
  10.5 1.5 %collective-permute-done.3.theirs_ref.refs_9_.refs_3_.refs_4_ = bf16[144,1024]{1,0:T(8,128)(2,1)S(1)} collective-permute-done((bf16[144,1024]{1,0:T(8,128)(2,1)S(1)}, bf16[144,1024]{1,0:T(8,128)(2,1)S(1)}, u32[]{:S(2)}, u32[]{:S(2)}) %collective-permute-start.3) | collective-permute-done | bytes 294944 | tf_op jit(solution)/shard_map/ppermute | solution.py:375
  11.9 0.1 shard_map.93.refs_5_
  12.0 2.5 %collective-permute-start.4 = (bf16[144,512]{1,0:T(8,128)(2,1)S(1)}, bf16[144,512]{1,0:T(8,128)(2,1)S(1)}, u32[]{:S(2)}, u32[]{:S(2)}) collective-permute-start(bf16[144,512]{1,0:T(8,128)(2,1)S(1)} %shard_map.93.refs_5_), channel_id=1, source_target_pairs={{0,24},{4,28},{8,16},{12,20},{16,8},{20,12},{24,0},{28,4},{1,25},{... | collective-permute-start | bytes 442376 | tf_op jit(solution)/shard_map/ppermute | solution.py:375
  14.6 1.3 %collective-permute-start.6 = (bf16[64,512]{1,0:T(8,128)(2,1)S(1)}, bf16[64,512]{1,0:T(8,128)(2,1)S(1)}, u32[]{:S(2)}, u32[]{:S(2)}) collective-permute-start(bf16[64,512]{1,0:T(8,128)(2,1)S(1)} %shard_map.94.refs_4_), channel_id=1, source_target_pairs={{0,2},{1,3},{2,0},{3,1},{4,6},{5,7},{6,4},{7,5},{8,10},{9,11},{10,... | collective-permute-start | bytes 196616 | tf_op jit(solution)/shard_map/ppermute | solution.py:375
  15.9 1.3 %collective-permute-start.7 = (bf16[144,512]{1,0:T(8,128)(2,1)S(1)}, bf16[144,512]{1,0:T(8,128)(2,1)S(1)}, u32[]{:S(2)}, u32[]{:S(2)}) collective-permute-start(bf16[144,512]{1,0:T(8,128)(2,1)S(1)} %shard_map.93.refs_5_), channel_id=1, source_target_pairs={{0,16},{4,20},{8,24},{12,28},{16,0},{20,4},{24,8},{28,12},{1,17},{... | collective-permute-start | bytes 442376 | tf_op jit(solution)/shard_map/ppermute | solution.py:375
  17.1 1.5 %collective-permute-start.8 = (bf16[144,512]{1,0:T(8,128)(2,1)S(1)}, bf16[144,512]{1,0:T(8,128)(2,1)S(1)}, u32[]{:S(2)}, u32[]{:S(2)}) collective-permute-start(bf16[144,512]{1,0:T(8,128)(2,1)S(1)} %shard_map.93.refs_5_), channel_id=1, source_target_pairs={{0,8},{4,12},{8,0},{12,4},{16,24},{20,28},{24,16},{28,20},{1,9},{5... | collective-permute-start | bytes 442376 | tf_op jit(solution)/shard_map/ppermute | solution.py:375
  18.6 1.8 %shard_map.95 = (f32[512,1024]{1,0:T(8,128)S(1)}, f32[512,1024]{1,0:T(8,128)S(1)}, bf16[3,512,1024]{2,1,0:T(8,128)(2,1)S(1)}, bf16[1,256,1024]{2,1,0:T(8,128)(2,1)S(1)}) custom-call(bf16[512,1024]{1,0:T(8,128)(2,1)S(1)} %get-tuple-element.38.refs_0_, bf16[512,1024]{1,0:T(8,128)(2,1)S(1)} %get-tuple-element.39.refs_1_, ...), custom_call_target="tpu_custom_call" | custom-call | flops 1409286144 | tf_op jit(solution)/shard_map/pallas_call | solution.py:359
  20.4 0.4 %collective-permute-done.6.refs_5_ = bf16[64,512]{1,0:T(8,128)(2,1)S(1)} collective-permute-done((bf16[64,512]{1,0:T(8,128)(2,1)S(1)}, bf16[64,512]{1,0:T(8,128)(2,1)S(1)}, u32[]{:S(2)}, u32[]{:S(2)}) %collective-permute-start.6) | collective-permute-done | bytes 65568 | tf_op jit(solution)/shard_map/ppermute | solution.py:375
  20.8 0.7 %shard_map.96 = (f32[512,512]{1,0:T(8,128)S(1)}, bf16[512,128]{1,0:T(8,128)(2,1)S(1)}, bf16[512,256]{1,0:T(8,128)(2,1)S(1)}) custom-call(bf16[144,512]{1,0:T(8,128)(2,1)S(1)} %collective-permute-done.4._.diagonal_ref, bf16[32,512]{1,0:T(8,128)(2,1)S(1)} %get-tuple-element.32.refs_0_, bf16[32,512]{1,0:T(8,128)(2,1)S(1)} %collective-permute-done.refs_1_, ...), custom_call_target="tpu_custom_call" | custom-call | flops 1073741824 | tf_op jit(solution)/shard_map/pallas_call | solution.py:359
  21.5 0.6 %collective-permute-done.7.y_ref = bf16[144,512]{1,0:T(8,128)(2,1)S(1)} collective-permute-done((bf16[144,512]{1,0:T(8,128)(2,1)S(1)}, bf16[144,512]{1,0:T(8,128)(2,1)S(1)}, u32[]{:S(2)}, u32[]{:S(2)}) %collective-permute-start.7) | collective-permute-done | bytes 147488 | tf_op jit(solution)/shard_map/ppermute | solution.py:375
  22.0 0.2 collective-permute-done.8.x_ref
  22.3 0.1 shard_map.97._.refs_5_
  22.4 0.1 collective-permute-start.9
  22.5 0.6 %shard_map.98.refs_1_ = f32[512,512]{1,0:T(8,128)S(1)} custom-call(bf16[512,256]{1,0:T(8,128)(2,1)S(1)} %get-tuple-element.48.scores_ref, bf16[512,128]{1,0:T(8,128)(2,1)S(1)} %get-tuple-element.47.turned_ref.refs_0_, bf16[256,512]{1,0:T(8,128)(2,1)S(1)} %shard_map.97._.refs_5_, f32[512,1024]{1,0:T(8,128)S(1)} %get-tuple-element.42.refs_6_.refs_0_, ...), custom_call_target="tpu_custom_call" | custom-call | flops 268435456 | tf_op jit(solution)/shard_map/pallas_call | solution.py:359
  23.1 0.1 copy-done
  23.2 0.5 %shard_map.99 = (f32[512,512]{1,0:T(8,128)S(1)}, f32[512,128]{1,0:T(8,128)S(1)}) custom-call(bf16[512,128]{1,0:T(8,128)(2,1)S(1)} %get-tuple-element.47.turned_ref.refs_0_, f32[512,512]{1,0:T(8,128)S(1)} %get-tuple-element.54.refs_1_, bf16[3,512,1024]{2,1,0:T(8,128)(2,1)S(1)} %get-tuple-element.53.refs_8_.refs_2_, f32[1,1024]{1,0:T(1,128)S(1)} %bitcast.3, ...), custom_call_target="tpu_custom_call" | custom-call | flops 536870912 | bytes 3145728 | tf_op jit(solution)/shard_map/pallas_call | solution.py:359
  23.7 0.3 collective-permute-done.9.refs_5_
  24.0 0.7 %shard_map.100 = (f32[512,512]{1,0:T(8,128)S(1)}, f32[1,512]{1,0:T(1,128)S(1)}) custom-call(bf16[512,128]{1,0:T(8,128)(2,1)S(1)} %get-tuple-element.47.turned_ref.refs_0_, f32[512,512]{1,0:T(8,128)S(1)} %shard_map.98.refs_1_, bf16[3,512,1024]{2,1,0:T(8,128)(2,1)S(1)} %get-tuple-element.53.refs_8_.refs_2_, f32[1,1024]{1,0:T(1,128)S(1)} %bitcast.4, ...), custom_call_target="tpu_custom_call" | custom-call | flops 536870912 | bytes 3145728 | tf_op jit(solution)/shard_map/pallas_call | solution.py:359
  24.7 1.7 %collective-permute-start.10 = (f32[1,512]{1,0:T(1,128)S(1)}, f32[1,512]{1,0:T(1,128)S(1)}, u32[]{:S(2)}, u32[]{:S(2)}) collective-permute-start(f32[1,512]{1,0:T(1,128)S(1)} %get-tuple-element.56.refs_0_), channel_id=1, source_target_pairs={{0,2},{1,3},{2,0},{3,1},{4,6},{5,7},{6,4},{7,5},{8,10},{9,11},{10,... | collective-permute-start | bytes 6152 | tf_op jit(solution)/shard_map/ppermute | solution.py:375
  26.4 2.0 %collective-permute-start.11 = (f32[1,512]{1,0:T(1,128)S(1)}, f32[1,512]{1,0:T(1,128)S(1)}, u32[]{:S(2)}, u32[]{:S(2)}) collective-permute-start(f32[1,512]{1,0:T(1,128)S(1)} %get-tuple-element.56.refs_0_), channel_id=1, source_target_pairs={{0,3},{1,2},{2,1},{3,0},{4,7},{5,6},{6,5},{7,4},{8,11},{9,10},{10,... | collective-permute-start | bytes 6152 | tf_op jit(solution)/shard_map/ppermute | solution.py:375
  28.4 0.8 %collective-permute-done.10.refs_1_ = f32[1,512]{1,0:T(1,128)S(1)} collective-permute-done((f32[1,512]{1,0:T(1,128)S(1)}, f32[1,512]{1,0:T(1,128)S(1)}, u32[]{:S(2)}, u32[]{:S(2)}) %collective-permute-start.10) | collective-permute-done | bytes 2080 | tf_op jit(solution)/shard_map/ppermute | solution.py:375
  29.2 2.6 %collective-permute-done.11.refs_2_ = f32[1,512]{1,0:T(1,128)S(1)} collective-permute-done((f32[1,512]{1,0:T(1,128)S(1)}, f32[1,512]{1,0:T(1,128)S(1)}, u32[]{:S(2)}, u32[]{:S(2)}) %collective-permute-start.11) | collective-permute-done | bytes 2080 | tf_op jit(solution)/shard_map/ppermute | solution.py:375
  31.7 0.2 collective-permute-done.12.refs_3_
  32.0 1.3 %shard_map.101 = bf16[512,1024]{1,0:T(8,128)(2,1)} custom-call(f32[1,512]{1,0:T(1,128)S(1)} %get-tuple-element.56.refs_0_, f32[1,512]{1,0:T(1,128)S(1)} %collective-permute-done.10.refs_1_, f32[1,512]{1,0:T(1,128)S(1)} %collective-permute-done.11.refs_2_, f32[1,512]{1,0:T(1,128)S(1)} %collective-permute-done.12.refs_3_, ...), custom_call_target="tpu_custom_call" | custom-call | flops 268435456 | bytes 3145728 | tf_op jit(solution)/shard_map/pallas_call | solution.py:359
  (7 shorter events, 0.0 us)
Async XLA Ops:
  0.0 7.4 %collective-permute-start = (bf16[32,512]{1,0:T(8,128)(2,1)}, bf16[32,512]{1,0:T(8,128)(2,1)S(1)}, u32[]{:S(2)}, u32[]{:S(2)}) collective-permute-start(bf16[32,512]{1,0:T(8,128)(2,1)} %refs_6_.1), channel_id=1, source_target_pairs={{0,2},{1,3},{2,0},{3,1},{4,6},{5,7},{6,4},{7,5},{8,10},{9,11},{10,... | collective-permute-start | bytes 98312 | tf_op jit(solution)/shard_map/ppermute | solution.py:375
  4.0 5.9 %collective-permute-start.1 = (bf16[32,512]{1,0:T(8,128)(2,1)}, bf16[32,512]{1,0:T(8,128)(2,1)S(1)}, u32[]{:S(2)}, u32[]{:S(2)}) collective-permute-start(bf16[32,512]{1,0:T(8,128)(2,1)} %refs_6_.1), channel_id=1, source_target_pairs={{0,3},{1,2},{2,1},{3,0},{4,7},{5,6},{6,5},{7,4},{8,11},{9,10},{10,... | collective-permute-start | bytes 98312 | tf_op jit(solution)/shard_map/ppermute | solution.py:375
  5.4 4.6 %collective-permute-start.2 = (bf16[32,512]{1,0:T(8,128)(2,1)}, bf16[32,512]{1,0:T(8,128)(2,1)S(1)}, u32[]{:S(2)}, u32[]{:S(2)}) collective-permute-start(bf16[32,512]{1,0:T(8,128)(2,1)} %refs_6_.1), channel_id=1, source_target_pairs={{0,1},{1,0},{2,3},{3,2},{4,5},{5,4},{6,7},{7,6},{8,9},{9,8},{10,11... | collective-permute-start | bytes 98312 | tf_op jit(solution)/shard_map/ppermute | solution.py:375
  10.3 1.6 %collective-permute-start.3 = (bf16[144,1024]{1,0:T(8,128)(2,1)S(1)}, bf16[144,1024]{1,0:T(8,128)(2,1)S(1)}, u32[]{:S(2)}, u32[]{:S(2)}) collective-permute-start(bf16[144,1024]{1,0:T(8,128)(2,1)S(1)} %get-tuple-element.35.mine_ref), channel_id=1, source_target_pairs={{0,4},{4,0},{8,12},{12,8},{16,20},{20,16},{24,28},{28,24},{1,5},{5... | collective-permute-start | bytes 884744 | tf_op jit(solution)/shard_map/ppermute | solution.py:375
  10.4 4.2 %collective-permute-start.5 = (bf16[32,512]{1,0:T(8,128)(2,1)S(1)}, bf16[32,512]{1,0:T(8,128)(2,1)S(1)}, u32[]{:S(2)}, u32[]{:S(2)}) collective-permute-start(bf16[32,512]{1,0:T(8,128)(2,1)S(1)} %get-tuple-element.37.mine_ref), channel_id=1, source_target_pairs={{0,1},{1,0},{2,3},{3,2},{4,5},{5,4},{6,7},{7,6},{8,9},{9,8},{10,11... | collective-permute-start | bytes 98312 | tf_op jit(solution)/shard_map/ppermute | solution.py:375
  12.0 8.7 %collective-permute-start.4 = (bf16[144,512]{1,0:T(8,128)(2,1)S(1)}, bf16[144,512]{1,0:T(8,128)(2,1)S(1)}, u32[]{:S(2)}, u32[]{:S(2)}) collective-permute-start(bf16[144,512]{1,0:T(8,128)(2,1)S(1)} %shard_map.93.refs_5_), channel_id=1, source_target_pairs={{0,24},{4,28},{8,16},{12,20},{16,8},{20,12},{24,0},{28,4},{1,25},{... | collective-permute-start | bytes 442376 | tf_op jit(solution)/shard_map/ppermute | solution.py:375
  14.6 6.2 %collective-permute-start.6 = (bf16[64,512]{1,0:T(8,128)(2,1)S(1)}, bf16[64,512]{1,0:T(8,128)(2,1)S(1)}, u32[]{:S(2)}, u32[]{:S(2)}) collective-permute-start(bf16[64,512]{1,0:T(8,128)(2,1)S(1)} %shard_map.94.refs_4_), channel_id=1, source_target_pairs={{0,2},{1,3},{2,0},{3,1},{4,6},{5,7},{6,4},{7,5},{8,10},{9,11},{10,... | collective-permute-start | bytes 196616 | tf_op jit(solution)/shard_map/ppermute | solution.py:375
  15.9 6.2 %collective-permute-start.7 = (bf16[144,512]{1,0:T(8,128)(2,1)S(1)}, bf16[144,512]{1,0:T(8,128)(2,1)S(1)}, u32[]{:S(2)}, u32[]{:S(2)}) collective-permute-start(bf16[144,512]{1,0:T(8,128)(2,1)S(1)} %shard_map.93.refs_5_), channel_id=1, source_target_pairs={{0,16},{4,20},{8,24},{12,28},{16,0},{20,4},{24,8},{28,12},{1,17},{... | collective-permute-start | bytes 442376 | tf_op jit(solution)/shard_map/ppermute | solution.py:375
  17.1 5.1 %collective-permute-start.8 = (bf16[144,512]{1,0:T(8,128)(2,1)S(1)}, bf16[144,512]{1,0:T(8,128)(2,1)S(1)}, u32[]{:S(2)}, u32[]{:S(2)}) collective-permute-start(bf16[144,512]{1,0:T(8,128)(2,1)S(1)} %shard_map.93.refs_5_), channel_id=1, source_target_pairs={{0,8},{4,12},{8,0},{12,4},{16,24},{20,28},{24,16},{28,20},{1,9},{5... | collective-permute-start | bytes 442376 | tf_op jit(solution)/shard_map/ppermute | solution.py:375
  22.4 1.6 %collective-permute-start.9 = (bf16[256,512]{1,0:T(8,128)(2,1)S(1)}, bf16[256,512]{1,0:T(8,128)(2,1)S(1)}, u32[]{:S(2)}, u32[]{:S(2)}) collective-permute-start(bf16[256,512]{1,0:T(8,128)(2,1)S(1)} %shard_map.97._.refs_5_), channel_id=1, source_target_pairs={{0,4},{4,0},{8,12},{12,8},{16,20},{20,16},{24,28},{28,24},{1,5},{5... | collective-permute-start | bytes 786440 | tf_op jit(solution)/shard_map/ppermute | solution.py:375
  22.5 0.7 %copy-start = (f32[1024]{0:T(1024)S(1)}, f32[1024]{0:T(1024)}, u32[]{:S(2)}) copy-start(f32[1024]{0:T(1024)} %param.17) | copy-start | bytes 12292
  24.7 4.5 %collective-permute-start.10 = (f32[1,512]{1,0:T(1,128)S(1)}, f32[1,512]{1,0:T(1,128)S(1)}, u32[]{:S(2)}, u32[]{:S(2)}) collective-permute-start(f32[1,512]{1,0:T(1,128)S(1)} %get-tuple-element.56.refs_0_), channel_id=1, source_target_pairs={{0,2},{1,3},{2,0},{3,1},{4,6},{5,7},{6,4},{7,5},{8,10},{9,11},{10,... | collective-permute-start | bytes 6152 | tf_op jit(solution)/shard_map/ppermute | solution.py:375
  26.4 5.4 %collective-permute-start.11 = (f32[1,512]{1,0:T(1,128)S(1)}, f32[1,512]{1,0:T(1,128)S(1)}, u32[]{:S(2)}, u32[]{:S(2)}) collective-permute-start(f32[1,512]{1,0:T(1,128)S(1)} %get-tuple-element.56.refs_0_), channel_id=1, source_target_pairs={{0,3},{1,2},{2,1},{3,0},{4,7},{5,6},{6,5},{7,4},{8,11},{9,10},{10,... | collective-permute-start | bytes 6152 | tf_op jit(solution)/shard_map/ppermute | solution.py:375
  28.4 3.6 %collective-permute-start.12 = (f32[1,512]{1,0:T(1,128)S(1)}, f32[1,512]{1,0:T(1,128)S(1)}, u32[]{:S(2)}, u32[]{:S(2)}) collective-permute-start(f32[1,512]{1,0:T(1,128)S(1)} %get-tuple-element.56.refs_0_), channel_id=1, source_target_pairs={{0,1},{1,0},{2,3},{3,2},{4,5},{5,4},{6,7},{7,6},{8,9},{9,8},{10,11... | collective-permute-start | bytes 6152 | tf_op jit(solution)/shard_map/ppermute | solution.py:375

commit v11 on v9

--- a/solution.py
+++ b/solution.py
@@ -12,6 +12,7 @@
 DECAY_ROWS = 16
 BLOCK = 256
 NORM_CHUNKS = 8
+FIRST_HOP = 2
 VMEM_LIMIT = 40 * 1024 * 1024
 
 f32, bf16 = jnp.float32, jnp.bfloat16
@@ -23,6 +24,14 @@
     row = lax.broadcasted_iota(jnp.int32, (copies * heads, width), 0)
     col = lax.broadcasted_iota(jnp.int32, (copies * heads, width), 1)
     return jnp.where(lax.rem(row, heads) == lax.div(col, P_SIZE), 1.0, 0.0)
+
+
+def far_first_masks(size):
+    return (*range(2, size), 1)
+
+
+def pair_masks(size):
+    return tuple(mask for mask in range(1, size) if not mask & FIRST_HOP)
 
 
 def two_parts(factor):
@@ -68,12 +77,16 @@
     return jnp.concatenate([rows[...].astype(f32) for rows in maps], axis=0).astype(bf16)
 
 
-def out_map_rows(map_refs):
+def out_map_rows(map_refs, parts):
     rows = map_refs[0].shape[0] // 2
-    if rows % 16 == 0:
-        return map_rows([map_refs[0].at[:rows], *map_refs[1:], map_refs[0].at[rows:]])
-    pair = map_refs[0][...].astype(f32)
-    return map_rows([pair[:rows], *map_refs[1:], pair[rows:]])
+    pairs = [ref if rows % 16 == 0 else ref[...].astype(f32) for ref in map_refs]
+    sent = (0, *pair_masks(parts))
+    picked = []
+    for mask in (0, *far_first_masks(parts)):
+        pair = pairs[sent.index(mask & ~FIRST_HOP)]
+        at = slice(rows, 2 * rows) if mask & FIRST_HOP else slice(0, rows)
+        picked.append(pair.at[at] if rows % 16 == 0 else pair[at])
+    return map_rows(picked)
 
 
 def fetch(sources, targets, semaphores):
@@ -227,7 +240,7 @@
     in_refs, out_refs, rest = refs[:parts], refs[parts:count], refs[count:-3]
     near_ref, turned_ref, scores_ref = refs[-3:]
     in_map = map_rows(in_refs)
-    turned = jnp.transpose(out_map_rows(out_refs))
+    turned = jnp.transpose(out_map_rows(out_refs, parts))
     turned_ref[...] = turned
     row = lax.broadcasted_iota(jnp.int32, (GROUP, GROUP), 0)
     col = lax.broadcasted_iota(jnp.int32, (GROUP, GROUP), 1)
@@ -375,8 +388,7 @@
     return lax.ppermute(array, axis, [(i, i ^ mask) for i in range(lax.axis_size(axis))])
 
 
-def from_each(array, axis, first=1, stride=1):
-    masks = sorted(range(first, lax.axis_size(axis), stride), key=lambda mask: (mask == 1, mask))
+def from_each(array, axis, masks):
     return [flip(array, axis, mask) for mask in masks]
 
 
@@ -410,7 +422,7 @@
     spans = local_spans(groups)
     dense = 2 * tokens * GROUP * width
     area = tokens * width
-    others = from_each(input_map, "head")
+    others = from_each(input_map, "head", far_first_masks(parts))
     kept = inputs, gate, level_mix, skip[None, :], input_map, output_map
     scaled, cum, *kept = call(
         prepare_kernel,
@@ -448,7 +460,7 @@
     else:
         message = shard
     output_map, _ = lax.optimization_barrier((output_map, shard))
-    beside = flip(output_map, "head", 1)
+    beside = flip(output_map, "head", FIRST_HOP)
     rows = output_map.shape[0]
     if rows % 16 == 0:
         both = call(
@@ -459,7 +471,7 @@
         )
     else:
         both = jnp.concatenate([output_map, beside], axis=0)
-    out_maps = [both, *from_each(both, "head", first=2, stride=2)]
+    out_maps = [both, *from_each(both, "head", pair_masks(parts))]
     factor_shape = [shaped((len(spans), GROUP, width), bf16)] if spans else []
     base, own_factor, far, *span_factors = call(
         functools.partial(factor_kernel, spans, levels),
@@ -517,7 +529,7 @@
             flops=4 * dense,
             bytes_accessed=12 * area,
         )
-    last = [sums, *from_each(sums, "head")]
+    last = [sums, *from_each(sums, "head", far_first_masks(parts))]
     return call(
         functools.partial(norm_kernel, len(last), width * parts),
         shaped((tokens, width), bf16),

time: 32.6 us -> 33.1 us (1.015)
  starting transfers between devices: 14.2 us -> 15.3 us
  waiting for transfers between devices: 10.2 us -> 9.6 us
    ppermute x13, starting transfers between devices: 14.2 us -> 15.3 us  [flip(): lax.ppermute(array, axis, [(i, i ^ mask) for i in range(lax.axis_size(axi...]
    ppermute x13, waiting for transfers between devices: 10.2 us -> 9.6 us  [flip(): lax.ppermute(array, axis, [(i, i ^ mask) for i in range(lax.axis_size(axi...]
  transfers between devices with their start and end apart: 13 -> 13, of which waited for: 6 -> 9; matrix products, arithmetic and copies ran while one was open for 0% -> 0% of each run, Pallas kernels for 17% -> 16%
where the time goes in v11:
time: 33.1 us; the launch traced here: 32.9 us
  starting transfers between devices  15.3 us (46%)
  waiting for transfers between devices  9.6 us (29%)
  Pallas kernels  7.8 us (24%)
    ppermute x13, starting transfers between devices, flip(): lax.ppermute(array, axis, [(i, i ^ mask) for i in range(lax.axis_size(axi...  15.3 us
    ppermute x13, waiting for transfers between devices, flip(): lax.ppermute(array, axis, [(i, i ^ mask) for i in range(lax.axis_size(axi...  9.6 us
    pallas_call x11, Pallas kernels, call(): pl.pallas_call(kernel, out_shape=out_shape, in_specs=specs, out_specs=jax...  7.8 us
  transfers between devices with their start and end apart: 13, of which 9 were waited for; matrix products, arithmetic and copies ran while one was open for 0% of the time, Pallas kernels for 16%

profile of v11, /device:TPU:0, one launch (start us, length us, event | category | flops | bytes accessed | tf_op | source)
XLA Modules:
  0.0 32.9 jit_solution(506340564933254345)
XLA Ops:
  0.0 4.0 %collective-permute-start = (bf16[32,512]{1,0:T(8,128)(2,1)}, bf16[32,512]{1,0:T(8,128)(2,1)S(1)}, u32[]{:S(2)}, u32[]{:S(2)}) collective-permute-start(bf16[32,512]{1,0:T(8,128)(2,1)} %refs_6_.1), channel_id=1, source_target_pairs={{0,2},{1,3},{2,0},{3,1},{4,6},{5,7},{6,4},{7,5},{8,10},{9,11},{10,... | collective-permute-start | bytes 98312 | tf_op jit(solution)/shard_map/ppermute | solution.py:388
  4.0 1.3 %collective-permute-start.1 = (bf16[32,512]{1,0:T(8,128)(2,1)}, bf16[32,512]{1,0:T(8,128)(2,1)S(1)}, u32[]{:S(2)}, u32[]{:S(2)}) collective-permute-start(bf16[32,512]{1,0:T(8,128)(2,1)} %refs_6_.1), channel_id=1, source_target_pairs={{0,3},{1,2},{2,1},{3,0},{4,7},{5,6},{6,5},{7,4},{8,11},{9,10},{10,... | collective-permute-start | bytes 98312 | tf_op jit(solution)/shard_map/ppermute | solution.py:388
  5.4 0.2 collective-permute-start.2
  5.6 1.8 %shard_map.91 = (bf16[512,1024]{1,0:T(8,128)(2,1)S(1)}, f32[16,512]{1,0:T(8,128)S(1)}, bf16[512,1024]{1,0:T(8,128)(2,1)S(1)}, bf16[512,1024]{1,0:T(8,128)(2,1)S(...) custom-call(f32[16,512]{1,0:T(8,128)} %refs_0_.1, ...), custom_call_target="tpu_custom_call" | custom-call | flops 4294967296 | bytes 2097152 | tf_op jit(solution)/shard_map/pallas_call | solution.py:372
  7.4 2.5 %collective-permute-done.1.refs_2_ = bf16[32,512]{1,0:T(8,128)(2,1)S(1)} collective-permute-done((bf16[32,512]{1,0:T(8,128)(2,1)}, bf16[32,512]{1,0:T(8,128)(2,1)S(1)}, u32[]{:S(2)}, u32[]{:S(2)}) %collective-permute-start.1) | collective-permute-done | bytes 32800 | tf_op jit(solution)/shard_map/ppermute | solution.py:388
  10.0 0.3 shard_map.92
  10.3 0.1 collective-permute-start.5
  10.4 1.3 %collective-permute-start.3 = (bf16[32,512]{1,0:T(8,128)(2,1)S(1)}, bf16[32,512]{1,0:T(8,128)(2,1)S(1)}, u32[]{:S(2)}, u32[]{:S(2)}) collective-permute-start(bf16[32,512]{1,0:T(8,128)(2,1)S(1)} %get-tuple-element.37.mine_ref), channel_id=1, source_target_pairs={{0,2},{1,3},{2,0},{3,1},{4,6},{5,7},{6,4},{7,5},{8,10},{9,11},{10,... | collective-permute-start | bytes 98312 | tf_op jit(solution)/shard_map/ppermute | solution.py:388
  11.7 0.3 collective-permute-done.5.theirs_ref.refs_9_.refs_3_.refs_4_
  11.9 0.1 shard_map.94.refs_5_
  12.0 2.5 %collective-permute-start.6 = (bf16[144,512]{1,0:T(8,128)(2,1)S(1)}, bf16[144,512]{1,0:T(8,128)(2,1)S(1)}, u32[]{:S(2)}, u32[]{:S(2)}) collective-permute-start(bf16[144,512]{1,0:T(8,128)(2,1)S(1)} %shard_map.94.refs_5_), channel_id=1, source_target_pairs={{0,24},{4,28},{8,16},{12,20},{16,8},{20,12},{24,0},{28,4},{1,25},{... | collective-permute-start | bytes 442376 | tf_op jit(solution)/shard_map/ppermute | solution.py:388
  14.5 0.5 %collective-permute-start.7 = (bf16[144,512]{1,0:T(8,128)(2,1)S(1)}, bf16[144,512]{1,0:T(8,128)(2,1)S(1)}, u32[]{:S(2)}, u32[]{:S(2)}) collective-permute-start(bf16[144,512]{1,0:T(8,128)(2,1)S(1)} %shard_map.94.refs_5_), channel_id=1, source_target_pairs={{0,16},{4,20},{8,24},{12,28},{16,0},{20,4},{24,8},{28,12},{1,17},{... | collective-permute-start | bytes 442376 | tf_op jit(solution)/shard_map/ppermute | solution.py:388
  15.0 0.5 %collective-permute-start.8 = (bf16[144,512]{1,0:T(8,128)(2,1)S(1)}, bf16[144,512]{1,0:T(8,128)(2,1)S(1)}, u32[]{:S(2)}, u32[]{:S(2)}) collective-permute-start(bf16[144,512]{1,0:T(8,128)(2,1)S(1)} %shard_map.94.refs_5_), channel_id=1, source_target_pairs={{0,8},{4,12},{8,0},{12,4},{16,24},{20,28},{24,16},{28,20},{1,9},{5... | collective-permute-start | bytes 442376 | tf_op jit(solution)/shard_map/ppermute | solution.py:388
  15.6 1.2 %collective-permute-start.4 = (bf16[64,512]{1,0:T(8,128)(2,1)S(1)}, bf16[64,512]{1,0:T(8,128)(2,1)S(1)}, u32[]{:S(2)}, u32[]{:S(2)}) collective-permute-start(bf16[64,512]{1,0:T(8,128)(2,1)S(1)} %shard_map.93.refs_4_), channel_id=1, source_target_pairs={{0,1},{1,0},{2,3},{3,2},{4,5},{5,4},{6,7},{7,6},{8,9},{9,8},{10,11... | collective-permute-start | bytes 196616 | tf_op jit(solution)/shard_map/ppermute | solution.py:388
  16.7 1.8 %shard_map.95 = (f32[512,1024]{1,0:T(8,128)S(1)}, f32[512,1024]{1,0:T(8,128)S(1)}, bf16[3,512,1024]{2,1,0:T(8,128)(2,1)S(1)}, bf16[1,256,1024]{2,1,0:T(8,128)(2,1)S(1)}) custom-call(bf16[512,1024]{1,0:T(8,128)(2,1)S(1)} %get-tuple-element.38.refs_0_, bf16[512,1024]{1,0:T(8,128)(2,1)S(1)} %get-tuple-element.39.refs_1_, ...), custom_call_target="tpu_custom_call" | custom-call | flops 1409286144 | tf_op jit(solution)/shard_map/pallas_call | solution.py:372
  18.5 1.4 %collective-permute-done.4.refs_5_ = bf16[64,512]{1,0:T(8,128)(2,1)S(1)} collective-permute-done((bf16[64,512]{1,0:T(8,128)(2,1)S(1)}, bf16[64,512]{1,0:T(8,128)(2,1)S(1)}, u32[]{:S(2)}, u32[]{:S(2)}) %collective-permute-start.4) | collective-permute-done | bytes 65568 | tf_op jit(solution)/shard_map/ppermute | solution.py:388
  19.9 0.7 %shard_map.96 = (f32[512,512]{1,0:T(8,128)S(1)}, bf16[512,128]{1,0:T(8,128)(2,1)S(1)}, bf16[512,256]{1,0:T(8,128)(2,1)S(1)}) custom-call(bf16[32,512]{1,0:T(8,128)(2,1)S(1)} %get-tuple-element.32.refs_0_, bf16[32,512]{1,0:T(8,128)(2,1)S(1)} %collective-permute-done.refs_1_, bf16[32,512]{1,0:T(8,128)(2,1)S(1)} %collective-permute-done.1.refs_2_, ...), custom_call_target="tpu_custom_call" | custom-call | tf_op jit(solution)/shard_map/pallas_call | solution.py:372
  20.6 1.4 %collective-permute-done.7.y_ref = bf16[144,512]{1,0:T(8,128)(2,1)S(1)} collective-permute-done((bf16[144,512]{1,0:T(8,128)(2,1)S(1)}, bf16[144,512]{1,0:T(8,128)(2,1)S(1)}, u32[]{:S(2)}, u32[]{:S(2)}) %collective-permute-start.7) | collective-permute-done | bytes 147488 | tf_op jit(solution)/shard_map/ppermute | solution.py:388
  22.0 0.1 collective-permute-done.8.x_ref
  22.1 0.1 shard_map.97._.refs_5_
  22.3 0.1 collective-permute-start.9
  22.3 0.6 %shard_map.98.refs_1_ = f32[512,512]{1,0:T(8,128)S(1)} custom-call(bf16[512,256]{1,0:T(8,128)(2,1)S(1)} %get-tuple-element.48.scores_ref, bf16[512,128]{1,0:T(8,128)(2,1)S(1)} %get-tuple-element.47.turned_ref.refs_0_, bf16[256,512]{1,0:T(8,128)(2,1)S(1)} %shard_map.97._.refs_5_, f32[512,1024]{1,0:T(8,128)S(1)} %get-tuple-element.42.refs_6_.refs_0_, ...), custom_call_target="tpu_custom_call" | custom-call | flops 268435456 | tf_op jit(solution)/shard_map/pallas_call | solution.py:372
  22.9 0.1 copy-done
  23.0 0.5 %shard_map.99 = (f32[512,512]{1,0:T(8,128)S(1)}, f32[512,128]{1,0:T(8,128)S(1)}) custom-call(bf16[512,128]{1,0:T(8,128)(2,1)S(1)} %get-tuple-element.47.turned_ref.refs_0_, f32[512,512]{1,0:T(8,128)S(1)} %get-tuple-element.54.refs_1_, bf16[3,512,1024]{2,1,0:T(8,128)(2,1)S(1)} %get-tuple-element.53.refs_8_.refs_2_, f32[1,1024]{1,0:T(1,128)S(1)} %bitcast.3, ...), custom_call_target="tpu_custom_call" | custom-call | flops 536870912 | bytes 3145728 | tf_op jit(solution)/shard_map/pallas_call | solution.py:372
  23.5 0.3 collective-permute-done.9.refs_5_
  23.9 0.7 %shard_map.100 = (f32[512,512]{1,0:T(8,128)S(1)}, f32[1,512]{1,0:T(1,128)S(1)}) custom-call(bf16[512,128]{1,0:T(8,128)(2,1)S(1)} %get-tuple-element.47.turned_ref.refs_0_, f32[512,512]{1,0:T(8,128)S(1)} %shard_map.98.refs_1_, bf16[3,512,1024]{2,1,0:T(8,128)(2,1)S(1)} %get-tuple-element.53.refs_8_.refs_2_, f32[1,1024]{1,0:T(1,128)S(1)} %bitcast.4, ...), custom_call_target="tpu_custom_call" | custom-call | flops 536870912 | bytes 3145728 | tf_op jit(solution)/shard_map/pallas_call | solution.py:372
  24.5 1.5 %collective-permute-start.10 = (f32[1,512]{1,0:T(1,128)S(1)}, f32[1,512]{1,0:T(1,128)S(1)}, u32[]{:S(2)}, u32[]{:S(2)}) collective-permute-start(f32[1,512]{1,0:T(1,128)S(1)} %get-tuple-element.56.refs_0_), channel_id=1, source_target_pairs={{0,2},{1,3},{2,0},{3,1},{4,6},{5,7},{6,4},{7,5},{8,10},{9,11},{10,... | collective-permute-start | bytes 6152 | tf_op jit(solution)/shard_map/ppermute | solution.py:388
  26.0 2.0 %collective-permute-start.11 = (f32[1,512]{1,0:T(1,128)S(1)}, f32[1,512]{1,0:T(1,128)S(1)}, u32[]{:S(2)}, u32[]{:S(2)}) collective-permute-start(f32[1,512]{1,0:T(1,128)S(1)} %get-tuple-element.56.refs_0_), channel_id=1, source_target_pairs={{0,3},{1,2},{2,1},{3,0},{4,7},{5,6},{6,5},{7,4},{8,11},{9,10},{10,... | collective-permute-start | bytes 6152 | tf_op jit(solution)/shard_map/ppermute | solution.py:388
  28.0 1.0 %collective-permute-done.10.refs_1_ = f32[1,512]{1,0:T(1,128)S(1)} collective-permute-done((f32[1,512]{1,0:T(1,128)S(1)}, f32[1,512]{1,0:T(1,128)S(1)}, u32[]{:S(2)}, u32[]{:S(2)}) %collective-permute-start.10) | collective-permute-done | bytes 2080 | tf_op jit(solution)/shard_map/ppermute | solution.py:388
  29.0 2.4 %collective-permute-done.11.refs_2_ = f32[1,512]{1,0:T(1,128)S(1)} collective-permute-done((f32[1,512]{1,0:T(1,128)S(1)}, f32[1,512]{1,0:T(1,128)S(1)}, u32[]{:S(2)}, u32[]{:S(2)}) %collective-permute-start.11) | collective-permute-done | bytes 2080 | tf_op jit(solution)/shard_map/ppermute | solution.py:388
  31.4 0.2 collective-permute-done.12.refs_3_
  31.6 1.3 %shard_map.101 = bf16[512,1024]{1,0:T(8,128)(2,1)} custom-call(f32[1,512]{1,0:T(1,128)S(1)} %get-tuple-element.56.refs_0_, f32[1,512]{1,0:T(1,128)S(1)} %collective-permute-done.10.refs_1_, f32[1,512]{1,0:T(1,128)S(1)} %collective-permute-done.11.refs_2_, f32[1,512]{1,0:T(1,128)S(1)} %collective-permute-done.12.refs_3_, ...), custom_call_target="tpu_custom_call" | custom-call | flops 268435456 | bytes 3145728 | tf_op jit(solution)/shard_map/pallas_call | solution.py:372
  (7 shorter events, 0.0 us)
Async XLA Ops:
  0.0 7.4 %collective-permute-start = (bf16[32,512]{1,0:T(8,128)(2,1)}, bf16[32,512]{1,0:T(8,128)(2,1)S(1)}, u32[]{:S(2)}, u32[]{:S(2)}) collective-permute-start(bf16[32,512]{1,0:T(8,128)(2,1)} %refs_6_.1), channel_id=1, source_target_pairs={{0,2},{1,3},{2,0},{3,1},{4,6},{5,7},{6,4},{7,5},{8,10},{9,11},{10,... | collective-permute-start | bytes 98312 | tf_op jit(solution)/shard_map/ppermute | solution.py:388
  4.0 5.9 %collective-permute-start.1 = (bf16[32,512]{1,0:T(8,128)(2,1)}, bf16[32,512]{1,0:T(8,128)(2,1)S(1)}, u32[]{:S(2)}, u32[]{:S(2)}) collective-permute-start(bf16[32,512]{1,0:T(8,128)(2,1)} %refs_6_.1), channel_id=1, source_target_pairs={{0,3},{1,2},{2,1},{3,0},{4,7},{5,6},{6,5},{7,4},{8,11},{9,10},{10,... | collective-permute-start | bytes 98312 | tf_op jit(solution)/shard_map/ppermute | solution.py:388
  5.4 4.6 %collective-permute-start.2 = (bf16[32,512]{1,0:T(8,128)(2,1)}, bf16[32,512]{1,0:T(8,128)(2,1)S(1)}, u32[]{:S(2)}, u32[]{:S(2)}) collective-permute-start(bf16[32,512]{1,0:T(8,128)(2,1)} %refs_6_.1), channel_id=1, source_target_pairs={{0,1},{1,0},{2,3},{3,2},{4,5},{5,4},{6,7},{7,6},{8,9},{9,8},{10,11... | collective-permute-start | bytes 98312 | tf_op jit(solution)/shard_map/ppermute | solution.py:388
  10.3 1.6 %collective-permute-start.5 = (bf16[144,1024]{1,0:T(8,128)(2,1)S(1)}, bf16[144,1024]{1,0:T(8,128)(2,1)S(1)}, u32[]{:S(2)}, u32[]{:S(2)}) collective-permute-start(bf16[144,1024]{1,0:T(8,128)(2,1)S(1)} %get-tuple-element.36.mine_ref), channel_id=1, source_target_pairs={{0,4},{4,0},{8,12},{12,8},{16,20},{20,16},{24,28},{28,24},{1,5},{5... | collective-permute-start | bytes 884744 | tf_op jit(solution)/shard_map/ppermute | solution.py:388
  10.4 5.2 %collective-permute-start.3 = (bf16[32,512]{1,0:T(8,128)(2,1)S(1)}, bf16[32,512]{1,0:T(8,128)(2,1)S(1)}, u32[]{:S(2)}, u32[]{:S(2)}) collective-permute-start(bf16[32,512]{1,0:T(8,128)(2,1)S(1)} %get-tuple-element.37.mine_ref), channel_id=1, source_target_pairs={{0,2},{1,3},{2,0},{3,1},{4,6},{5,7},{6,4},{7,5},{8,10},{9,11},{10,... | collective-permute-start | bytes 98312 | tf_op jit(solution)/shard_map/ppermute | solution.py:388
  12.0 8.6 %collective-permute-start.6 = (bf16[144,512]{1,0:T(8,128)(2,1)S(1)}, bf16[144,512]{1,0:T(8,128)(2,1)S(1)}, u32[]{:S(2)}, u32[]{:S(2)}) collective-permute-start(bf16[144,512]{1,0:T(8,128)(2,1)S(1)} %shard_map.94.refs_5_), channel_id=1, source_target_pairs={{0,24},{4,28},{8,16},{12,20},{16,8},{20,12},{24,0},{28,4},{1,25},{... | collective-permute-start | bytes 442376 | tf_op jit(solution)/shard_map/ppermute | solution.py:388
  14.5 7.5 %collective-permute-start.7 = (bf16[144,512]{1,0:T(8,128)(2,1)S(1)}, bf16[144,512]{1,0:T(8,128)(2,1)S(1)}, u32[]{:S(2)}, u32[]{:S(2)}) collective-permute-start(bf16[144,512]{1,0:T(8,128)(2,1)S(1)} %shard_map.94.refs_5_), channel_id=1, source_target_pairs={{0,16},{4,20},{8,24},{12,28},{16,0},{20,4},{24,8},{28,12},{1,17},{... | collective-permute-start | bytes 442376 | tf_op jit(solution)/shard_map/ppermute | solution.py:388
  15.0 7.1 %collective-permute-start.8 = (bf16[144,512]{1,0:T(8,128)(2,1)S(1)}, bf16[144,512]{1,0:T(8,128)(2,1)S(1)}, u32[]{:S(2)}, u32[]{:S(2)}) collective-permute-start(bf16[144,512]{1,0:T(8,128)(2,1)S(1)} %shard_map.94.refs_5_), channel_id=1, source_target_pairs={{0,8},{4,12},{8,0},{12,4},{16,24},{20,28},{24,16},{28,20},{1,9},{5... | collective-permute-start | bytes 442376 | tf_op jit(solution)/shard_map/ppermute | solution.py:388
  15.6 4.3 %collective-permute-start.4 = (bf16[64,512]{1,0:T(8,128)(2,1)S(1)}, bf16[64,512]{1,0:T(8,128)(2,1)S(1)}, u32[]{:S(2)}, u32[]{:S(2)}) collective-permute-start(bf16[64,512]{1,0:T(8,128)(2,1)S(1)} %shard_map.93.refs_4_), channel_id=1, source_target_pairs={{0,1},{1,0},{2,3},{3,2},{4,5},{5,4},{6,7},{7,6},{8,9},{9,8},{10,11... | collective-permute-start | bytes 196616 | tf_op jit(solution)/shard_map/ppermute | solution.py:388
  22.3 1.6 %collective-permute-start.9 = (bf16[256,512]{1,0:T(8,128)(2,1)S(1)}, bf16[256,512]{1,0:T(8,128)(2,1)S(1)}, u32[]{:S(2)}, u32[]{:S(2)}) collective-permute-start(bf16[256,512]{1,0:T(8,128)(2,1)S(1)} %shard_map.97._.refs_5_), channel_id=1, source_target_pairs={{0,4},{4,0},{8,12},{12,8},{16,20},{20,16},{24,28},{28,24},{1,5},{5... | collective-permute-start | bytes 786440 | tf_op jit(solution)/shard_map/ppermute | solution.py:388
  22.3 0.7 %copy-start = (f32[1024]{0:T(1024)S(1)}, f32[1024]{0:T(1024)}, u32[]{:S(2)}) copy-start(f32[1024]{0:T(1024)} %param.17) | copy-start | bytes 12292
  24.5 4.5 %collective-permute-start.10 = (f32[1,512]{1,0:T(1,128)S(1)}, f32[1,512]{1,0:T(1,128)S(1)}, u32[]{:S(2)}, u32[]{:S(2)}) collective-permute-start(f32[1,512]{1,0:T(1,128)S(1)} %get-tuple-element.56.refs_0_), channel_id=1, source_target_pairs={{0,2},{1,3},{2,0},{3,1},{4,6},{5,7},{6,4},{7,5},{8,10},{9,11},{10,... | collective-permute-start | bytes 6152 | tf_op jit(solution)/shard_map/ppermute | solution.py:388
  26.0 5.4 %collective-permute-start.11 = (f32[1,512]{1,0:T(1,128)S(1)}, f32[1,512]{1,0:T(1,128)S(1)}, u32[]{:S(2)}, u32[]{:S(2)}) collective-permute-start(f32[1,512]{1,0:T(1,128)S(1)} %get-tuple-element.56.refs_0_), channel_id=1, source_target_pairs={{0,3},{1,2},{2,1},{3,0},{4,7},{5,6},{6,5},{7,4},{8,11},{9,10},{10,... | collective-permute-start | bytes 6152 | tf_op jit(solution)/shard_map/ppermute | solution.py:388
  28.0 3.6 %collective-permute-start.12 = (f32[1,512]{1,0:T(1,128)S(1)}, f32[1,512]{1,0:T(1,128)S(1)}, u32[]{:S(2)}, u32[]{:S(2)}) collective-permute-start(f32[1,512]{1,0:T(1,128)S(1)} %get-tuple-element.56.refs_0_), channel_id=1, source_target_pairs={{0,1},{1,0},{2,3},{3,2},{4,5},{5,4},{6,7},{7,6},{8,9},{9,8},{10,11... | collective-permute-start | bytes 6152 | tf_op jit(solution)/shard_map/ppermute | solution.py:388

commit v12 on v11

--- a/solution.py
+++ b/solution.py
@@ -9,9 +9,9 @@
 
 P_SIZE = 64
 GROUP = 256
-DECAY_ROWS = 16
+DECAY_ROWS = 8
 BLOCK = 256
-NORM_CHUNKS = 8
+NORM_CHUNKS = 4
 FIRST_HOP = 2
 VMEM_LIMIT = 40 * 1024 * 1024
 
@@ -135,9 +135,9 @@
     both_ref[rows:, :] = theirs_ref[...]
 
 
-def states_kernel(parts, *refs):
+def states_kernel(parts, sides, *refs):
     map_refs, (scaled_ref, cum_ref), out_refs = refs[:parts], refs[parts : parts + 2], refs[parts + 2 :]
-    shard_ref = out_refs[0]
+    shard_refs = out_refs[:sides]
     heads, tokens = cum_ref.shape
     width = scaled_ref.shape[1]
     in_map = map_rows(map_refs)
@@ -154,22 +154,25 @@
     for group in range(1, len(states)):
         total = total * decays[group] + states[group]
         decay = decay * decays[group]
-    shard_ref[:size, :] = total.astype(bf16)
-    shard_ref[size:, :] = jnp.broadcast_to(decay, (DECAY_ROWS, width)).astype(bf16)
+    columns = width // sides
+    core = lax.rem(lax.axis_index("seq"), 2)
+    for ref, first in zip(shard_refs, (core == 0, core == 1)):
+        at = slice(0, columns)
+        ref[:size, :] = jnp.where(first, total[:, at], total[:, width - columns :]).astype(bf16)
+        row = jnp.where(first, decay[:, at], decay[:, width - columns :])
+        ref[size:, :] = jnp.broadcast_to(row, (DECAY_ROWS, columns)).astype(bf16)
     for index, (later, _, start, stop) in enumerate(local_spans(len(states))):
         span = states[start]
         for group in range(start + 1, later):
             span = span * decays[group]
             if group < stop:
                 span = span + states[group]
-        out_refs[1][index * size : (index + 1) * size, :] = span.astype(bf16)
+        out_refs[sides][index * size : (index + 1) * size, :] = span.astype(bf16)
 
 
 def merge_kernel(size, mine_ref, theirs_ref, pair_ref):
     core = lax.rem(lax.axis_index("seq"), 2)
-    half = pair_ref.shape[1]
-    mine = jnp.where(core == 1, mine_ref[:, half:], mine_ref[:, :half])
-    theirs = jnp.where(core == 1, theirs_ref[:, half:], theirs_ref[:, :half])
+    mine, theirs = mine_ref[...], theirs_ref[...]
     older = jnp.where(core == 1, theirs, mine).astype(f32)
     newer = jnp.where(core == 1, mine, theirs).astype(f32)
     decay = newer[size : size + 1]
@@ -229,13 +232,13 @@
                     reach = jnp.dot(turned_ref[at, :], span_refs[0][rows, of], preferred_element_type=f32)
                     total = total + span_refs[1][index, :, of].astype(f32) * reach
             if paired:
-                reach = jnp.dot(turned_ref[at, :], core_ref[:size, of], preferred_element_type=f32)
+                reach = jnp.dot(turned_ref[at, :], core_ref[:size, cols], preferred_element_type=f32)
                 reach = jnp.where(has_core, reach, 0.0)
                 total = total + far_ref[0, at, of].astype(f32) * reach
             near_ref[at, cols] = total
 
 
-def near_kernel(parts, spans, paired, *refs):
+def near_kernel(parts, spans, paired, _, *refs):
     count = parts + parts // 2
     in_refs, out_refs, rest = refs[:parts], refs[parts:count], refs[count:-3]
     near_ref, turned_ref, scores_ref = refs[-3:]
@@ -325,7 +328,7 @@
     start = (core if own else 1 - core) * half
 
     def state_of(level, cols, at):
-        core_decay = core_ref[size:, at].astype(f32)[:1]
+        core_decay = core_ref[size:, cols].astype(f32)[:1]
         running = jnp.where(core == 1, core_decay, 1.0)
         return spans_ref[(level - 1) * size : level * size, cols].astype(f32) * running
 
@@ -438,27 +441,26 @@
     )
     inputs, gate, level_mix, skip, input_map, output_map = kept
     in_maps = [input_map, *others]
-    shard_shape = shaped((size + DECAY_ROWS, width), bf16)
+    pairs = lax.axis_size("seq") == 8 and parts == 4
+    sides = 2 if pairs else 1
+    shard_shape = shaped((size + DECAY_ROWS, width // sides), bf16)
     span_shape = [shaped((len(spans) * size, width), bf16)] if spans else []
-    shard, *span_states = call(
-        functools.partial(states_kernel, parts),
-        (shard_shape, *span_shape),
+    shard, *rest = call(
+        functools.partial(states_kernel, parts, sides),
+        (*[shard_shape] * sides, *span_shape),
         (*in_maps, scaled, cum),
         flops=dense,
         bytes_accessed=4 * area,
     )
-    pairs = lax.axis_size("seq") == 8 and parts == 4
+    span_states = rest[sides - 1 :]
     if pairs:
-        theirs = flip(shard, "seq", 1)
+        theirs = flip(rest[0], "seq", 1)
         message = call(
-            functools.partial(merge_kernel, size),
-            shaped((size + DECAY_ROWS, width // 2), bf16),
-            (shard, theirs),
-            flops=0,
-            bytes_accessed=area,
-        )
+            functools.partial(merge_kernel, size), shard_shape, (shard, theirs), bytes_accessed=area
+        )
+        other_theirs = flip(lax.optimization_barrier((shard, message))[0], "seq", 1)
     else:
-        message = shard
+        other_theirs = theirs = message = shard
     output_map, _ = lax.optimization_barrier((output_map, shard))
     beside = flip(output_map, "head", FIRST_HOP)
     rows = output_map.shape[0]
@@ -480,15 +482,15 @@
             *(shaped((levels, tokens, width), bf16), *factor_shape),
         ),
         (inputs, gate, level_mix, skip, cum, message),
-        flops=21 * dense // 4,
+        flops=5 * dense,
         bytes_accessed=0,
     )
-    near_args = base, own_factor, far, theirs if pairs else message, scaled, *span_states, *span_factors
+    near_args = base, own_factor, far, theirs, scaled, *span_states, *span_factors
     near_shape = shaped((tokens, width // 2 if pairs else width), f32)
     near, turned, scores = call(
         functools.partial(near_kernel, parts, spans, pairs),
         (near_shape, shaped((tokens, size), bf16), shaped((tokens, GROUP), bf16)),
-        (*in_maps, *out_maps, *near_args),
+        (other_theirs, *in_maps, *out_maps, *near_args),
     )
     gain = norm_gain[None, :]
     sums_shape = shaped((1, tokens), f32)
@@ -502,6 +504,7 @@
             bytes_accessed=area,
         )
         other = flip(own, "seq", 1)
+        near_args = base, own_factor, far, other_theirs, scaled, *span_states, *span_factors
         other_near = call(
             functools.partial(other_near_kernel, spans), near_shape, (scores, turned, own, *near_args), flops=dense
         )
@@ -516,7 +519,7 @@
         other_gated, sums = call(
             functools.partial(far_kernel_of_half, False),
             (gated_shape, sums_shape),
-            (turned, other_near, far, gain, theirs, other, own_squares),
+            (turned, other_near, far, gain, other_theirs, other, own_squares),
             flops=2 * dense,
             bytes_accessed=6 * area,
         )

time: 33.1 us -> 33 us (level)
  waiting for transfers between devices: 9.6 us -> 9.03 us
  starting transfers between devices: 15.3 us -> 15.8 us
    ppermute x13 -> x14, waiting for transfers between devices: 9.6 us -> 9.03 us  [flip(): lax.ppermute(array, axis, [(i, i ^ mask) for i in range(lax.axis_size(axi...]
    ppermute x13 -> x14, starting transfers between devices: 15.3 us -> 15.8 us  [flip(): lax.ppermute(array, axis, [(i, i ^ mask) for i in range(lax.axis_size(axi...]
  transfers between devices with their start and end apart: 13 -> 14, of which waited for: 9 -> 8; matrix products, arithmetic and copies ran while one was open for 0% -> 0% of each run, Pallas kernels for 16% -> 16%
where the time goes in v12:
time: 33 us; the launch traced here: 32.9 us
  starting transfers between devices  15.8 us (48%)
  waiting for transfers between devices  9.03 us (27%)
  Pallas kernels  7.82 us (24%)
    ppermute x14, starting transfers between devices, flip(): lax.ppermute(array, axis, [(i, i ^ mask) for i in range(lax.axis_size(axi...  15.8 us
    ppermute x14, waiting for transfers between devices, flip(): lax.ppermute(array, axis, [(i, i ^ mask) for i in range(lax.axis_size(axi...  9.03 us
    pallas_call x11, Pallas kernels, call(): pl.pallas_call(kernel, out_shape=out_shape, in_specs=specs, out_specs=jax...  7.82 us
  transfers between devices with their start and end apart: 14, of which 8 were waited for; matrix products, arithmetic and copies ran while one was open for 0% of the time, Pallas kernels for 16%

profile of v12, /device:TPU:0, one launch (start us, length us, event | category | flops | bytes accessed | tf_op | source)
XLA Modules:
  0.0 32.9 jit_solution(16709637881939059892)
XLA Ops:
  0.0 4.0 %collective-permute-start = (bf16[32,512]{1,0:T(8,128)(2,1)}, bf16[32,512]{1,0:T(8,128)(2,1)S(1)}, u32[]{:S(2)}, u32[]{:S(2)}) collective-permute-start(bf16[32,512]{1,0:T(8,128)(2,1)} %refs_6_.1), channel_id=1, source_target_pairs={{0,2},{1,3},{2,0},{3,1},{4,6},{5,7},{6,4},{7,5},{8,10},{9,11},{10,... | collective-permute-start | bytes 98312 | tf_op jit(solution)/shard_map/ppermute | solution.py:391
  4.0 1.3 %collective-permute-start.1 = (bf16[32,512]{1,0:T(8,128)(2,1)}, bf16[32,512]{1,0:T(8,128)(2,1)S(1)}, u32[]{:S(2)}, u32[]{:S(2)}) collective-permute-start(bf16[32,512]{1,0:T(8,128)(2,1)} %refs_6_.1), channel_id=1, source_target_pairs={{0,3},{1,2},{2,1},{3,0},{4,7},{5,6},{6,5},{7,4},{8,11},{9,10},{10,... | collective-permute-start | bytes 98312 | tf_op jit(solution)/shard_map/ppermute | solution.py:391
  5.4 0.2 collective-permute-start.2
  5.6 1.8 %shard_map.91 = (bf16[512,1024]{1,0:T(8,128)(2,1)S(1)}, f32[16,512]{1,0:T(8,128)S(1)}, bf16[512,1024]{1,0:T(8,128)(2,1)S(1)}, bf16[512,1024]{1,0:T(8,128)(2,1)S(...) custom-call(f32[16,512]{1,0:T(8,128)} %refs_0_.1, ...), custom_call_target="tpu_custom_call" | custom-call | flops 4294967296 | bytes 2097152 | tf_op jit(solution)/shard_map/pallas_call | solution.py:375
  7.4 2.5 %collective-permute-done.1.refs_2_ = bf16[32,512]{1,0:T(8,128)(2,1)S(1)} collective-permute-done((bf16[32,512]{1,0:T(8,128)(2,1)}, bf16[32,512]{1,0:T(8,128)(2,1)S(1)}, u32[]{:S(2)}, u32[]{:S(2)}) %collective-permute-start.1) | collective-permute-done | bytes 32800 | tf_op jit(solution)/shard_map/ppermute | solution.py:391
  10.0 0.3 %shard_map.92 = (bf16[136,512]{1,0:T(8,128)(2,1)S(1)}, bf16[136,512]{1,0:T(8,128)(2,1)S(1)}, bf16[128,1024]{1,0:T(8,128)(2,1)S(1)}) custom-call(bf16[32,512]{1,0:T(8,128)(2,1)S(1)} %get-tuple-element.34.refs_0_, bf16[32,512]{1,0:T(8,128)(2,1)S(1)} %collective-permute-done.refs_1_, bf16[32,512]{1,0:T(8,128)(2,1)S(1)} %collective-permute-done.1.refs_2_, ...), custom_call_target="tpu_custom_call" | custom-call | flops 268435456 | bytes 2097152 | tf_op jit(solution)/shard_map/pallas_call | solution.py:375
  10.3 0.1 collective-permute-start.3
  10.4 1.3 %collective-permute-start.5 = (bf16[32,512]{1,0:T(8,128)(2,1)S(1)}, bf16[32,512]{1,0:T(8,128)(2,1)S(1)}, u32[]{:S(2)}, u32[]{:S(2)}) collective-permute-start(bf16[32,512]{1,0:T(8,128)(2,1)S(1)} %get-tuple-element.41.mine_ref), channel_id=1, source_target_pairs={{0,2},{1,3},{2,0},{3,1},{4,6},{5,7},{6,4},{7,5},{8,10},{9,11},{10,... | collective-permute-start | bytes 98312 | tf_op jit(solution)/shard_map/ppermute | solution.py:391
  11.7 0.1 shard_map.93.refs_5_
  11.8 0.2 collective-permute-start.4
  12.0 2.5 %collective-permute-start.7 = (bf16[136,512]{1,0:T(8,128)(2,1)S(1)}, bf16[136,512]{1,0:T(8,128)(2,1)S(1)}, u32[]{:S(2)}, u32[]{:S(2)}) collective-permute-start(bf16[136,512]{1,0:T(8,128)(2,1)S(1)} %shard_map.93.refs_5_), channel_id=1, source_target_pairs={{0,24},{4,28},{8,16},{12,20},{16,8},{20,12},{24,0},{28,4},{1,25},{... | collective-permute-start | bytes 417800 | tf_op jit(solution)/shard_map/ppermute | solution.py:391
  14.5 0.5 %collective-permute-start.8 = (bf16[136,512]{1,0:T(8,128)(2,1)S(1)}, bf16[136,512]{1,0:T(8,128)(2,1)S(1)}, u32[]{:S(2)}, u32[]{:S(2)}) collective-permute-start(bf16[136,512]{1,0:T(8,128)(2,1)S(1)} %shard_map.93.refs_5_), channel_id=1, source_target_pairs={{0,16},{4,20},{8,24},{12,28},{16,0},{20,4},{24,8},{28,12},{1,17},{... | collective-permute-start | bytes 417800 | tf_op jit(solution)/shard_map/ppermute | solution.py:391
  15.0 0.5 %collective-permute-start.9 = (bf16[136,512]{1,0:T(8,128)(2,1)S(1)}, bf16[136,512]{1,0:T(8,128)(2,1)S(1)}, u32[]{:S(2)}, u32[]{:S(2)}) collective-permute-start(bf16[136,512]{1,0:T(8,128)(2,1)S(1)} %shard_map.93.refs_5_), channel_id=1, source_target_pairs={{0,8},{4,12},{8,0},{12,4},{16,24},{20,28},{24,16},{28,20},{1,9},{5... | collective-permute-start | bytes 417800 | tf_op jit(solution)/shard_map/ppermute | solution.py:391
  15.5 1.4 %collective-permute-start.6 = (bf16[64,512]{1,0:T(8,128)(2,1)S(1)}, bf16[64,512]{1,0:T(8,128)(2,1)S(1)}, u32[]{:S(2)}, u32[]{:S(2)}) collective-permute-start(bf16[64,512]{1,0:T(8,128)(2,1)S(1)} %shard_map.94.refs_4_), channel_id=1, source_target_pairs={{0,1},{1,0},{2,3},{3,2},{4,5},{5,4},{6,7},{7,6},{8,9},{9,8},{10,11... | collective-permute-start | bytes 196616 | tf_op jit(solution)/shard_map/ppermute | solution.py:391
  16.9 1.8 %shard_map.95 = (f32[512,1024]{1,0:T(8,128)S(1)}, f32[512,1024]{1,0:T(8,128)S(1)}, bf16[3,512,1024]{2,1,0:T(8,128)(2,1)S(1)}, bf16[1,256,1024]{2,1,0:T(8,128)(2,1)S(1)}) custom-call(bf16[512,1024]{1,0:T(8,128)(2,1)S(1)} %get-tuple-element.42.refs_0_, bf16[512,1024]{1,0:T(8,128)(2,1)S(1)} %get-tuple-element.43.refs_1_, ...), custom_call_target="tpu_custom_call" | custom-call | flops 1342177280 | tf_op jit(solution)/shard_map/pallas_call | solution.py:375
  18.7 1.2 %collective-permute-done.6.refs_5_ = bf16[64,512]{1,0:T(8,128)(2,1)S(1)} collective-permute-done((bf16[64,512]{1,0:T(8,128)(2,1)S(1)}, bf16[64,512]{1,0:T(8,128)(2,1)S(1)}, u32[]{:S(2)}, u32[]{:S(2)}) %collective-permute-start.6) | collective-permute-done | bytes 65568 | tf_op jit(solution)/shard_map/ppermute | solution.py:391
  19.9 0.7 %shard_map.96 = (f32[512,512]{1,0:T(8,128)S(1)}, bf16[512,128]{1,0:T(8,128)(2,1)S(1)}, bf16[512,256]{1,0:T(8,128)(2,1)S(1)}) custom-call(bf16[136,512]{1,0:T(8,128)(2,1)S(1)} %collective-permute-done.4._.refs_3_.refs_4_, bf16[32,512]{1,0:T(8,128)(2,1)S(1)} %get-tuple-element.34.refs_0_, bf16[32,512]{1,0:T(8,128)(2,1)S(1)} %collective-permute-done.refs_1_, ...), custom_call_target="tpu_custom_call" | custom-call | tf_op jit(solution)/shard_map/pallas_call | solution.py:375
  20.6 1.3 %collective-permute-done.8.y_ref = bf16[136,512]{1,0:T(8,128)(2,1)S(1)} collective-permute-done((bf16[136,512]{1,0:T(8,128)(2,1)S(1)}, bf16[136,512]{1,0:T(8,128)(2,1)S(1)}, u32[]{:S(2)}, u32[]{:S(2)}) %collective-permute-start.8) | collective-permute-done | bytes 139296 | tf_op jit(solution)/shard_map/ppermute | solution.py:391
  21.8 0.1 collective-permute-done.9.x_ref
  21.9 0.1 shard_map.97._.refs_5_
  22.1 0.1 collective-permute-start.10
  22.1 0.6 %shard_map.98.refs_1_ = f32[512,512]{1,0:T(8,128)S(1)} custom-call(bf16[512,256]{1,0:T(8,128)(2,1)S(1)} %get-tuple-element.52.scores_ref, bf16[512,128]{1,0:T(8,128)(2,1)S(1)} %get-tuple-element.51.turned_ref.refs_0_, bf16[256,512]{1,0:T(8,128)(2,1)S(1)} %shard_map.97._.refs_5_, f32[512,1024]{1,0:T(8,128)S(1)} %get-tuple-element.46.refs_6_.refs_0_, ...), custom_call_target="tpu_custom_call" | custom-call | flops 268435456 | tf_op jit(solution)/shard_map/pallas_call | solution.py:375
  22.7 0.1 copy-done
  22.8 0.5 %shard_map.99 = (f32[512,512]{1,0:T(8,128)S(1)}, f32[512,128]{1,0:T(8,128)S(1)}) custom-call(bf16[512,128]{1,0:T(8,128)(2,1)S(1)} %get-tuple-element.51.turned_ref.refs_0_, f32[512,512]{1,0:T(8,128)S(1)} %get-tuple-element.58.refs_1_, bf16[3,512,1024]{2,1,0:T(8,128)(2,1)S(1)} %get-tuple-element.57.refs_8_.refs_2_, f32[1,1024]{1,0:T(1,128)S(1)} %bitcast.3, ...), custom_call_target="tpu_custom_call" | custom-call | flops 536870912 | bytes 3145728 | tf_op jit(solution)/shard_map/pallas_call | solution.py:375
  23.4 0.3 collective-permute-done.10.refs_5_
  23.7 0.7 %shard_map.100 = (f32[512,512]{1,0:T(8,128)S(1)}, f32[1,512]{1,0:T(1,128)S(1)}) custom-call(bf16[512,128]{1,0:T(8,128)(2,1)S(1)} %get-tuple-element.51.turned_ref.refs_0_, f32[512,512]{1,0:T(8,128)S(1)} %shard_map.98.refs_1_, bf16[3,512,1024]{2,1,0:T(8,128)(2,1)S(1)} %get-tuple-element.57.refs_8_.refs_2_, f32[1,1024]{1,0:T(1,128)S(1)} %bitcast.4, ...), custom_call_target="tpu_custom_call" | custom-call | flops 536870912 | bytes 3145728 | tf_op jit(solution)/shard_map/pallas_call | solution.py:375
  24.3 1.7 %collective-permute-start.11 = (f32[1,512]{1,0:T(1,128)S(1)}, f32[1,512]{1,0:T(1,128)S(1)}, u32[]{:S(2)}, u32[]{:S(2)}) collective-permute-start(f32[1,512]{1,0:T(1,128)S(1)} %get-tuple-element.60.refs_0_), channel_id=1, source_target_pairs={{0,2},{1,3},{2,0},{3,1},{4,6},{5,7},{6,4},{7,5},{8,10},{9,11},{10,... | collective-permute-start | bytes 6152 | tf_op jit(solution)/shard_map/ppermute | solution.py:391
  26.0 2.0 %collective-permute-start.12 = (f32[1,512]{1,0:T(1,128)S(1)}, f32[1,512]{1,0:T(1,128)S(1)}, u32[]{:S(2)}, u32[]{:S(2)}) collective-permute-start(f32[1,512]{1,0:T(1,128)S(1)} %get-tuple-element.60.refs_0_), channel_id=1, source_target_pairs={{0,3},{1,2},{2,1},{3,0},{4,7},{5,6},{6,5},{7,4},{8,11},{9,10},{10,... | collective-permute-start | bytes 6152 | tf_op jit(solution)/shard_map/ppermute | solution.py:391
  28.0 0.8 %collective-permute-done.11.refs_1_ = f32[1,512]{1,0:T(1,128)S(1)} collective-permute-done((f32[1,512]{1,0:T(1,128)S(1)}, f32[1,512]{1,0:T(1,128)S(1)}, u32[]{:S(2)}, u32[]{:S(2)}) %collective-permute-start.11) | collective-permute-done | bytes 2080 | tf_op jit(solution)/shard_map/ppermute | solution.py:391
  28.8 2.5 %collective-permute-done.12.refs_2_ = f32[1,512]{1,0:T(1,128)S(1)} collective-permute-done((f32[1,512]{1,0:T(1,128)S(1)}, f32[1,512]{1,0:T(1,128)S(1)}, u32[]{:S(2)}, u32[]{:S(2)}) %collective-permute-start.12) | collective-permute-done | bytes 2080 | tf_op jit(solution)/shard_map/ppermute | solution.py:391
  31.4 0.2 collective-permute-done.13.refs_3_
  31.6 1.3 %shard_map.101 = bf16[512,1024]{1,0:T(8,128)(2,1)} custom-call(f32[1,512]{1,0:T(1,128)S(1)} %get-tuple-element.60.refs_0_, f32[1,512]{1,0:T(1,128)S(1)} %collective-permute-done.11.refs_1_, f32[1,512]{1,0:T(1,128)S(1)} %collective-permute-done.12.refs_2_, f32[1,512]{1,0:T(1,128)S(1)} %collective-permute-done.13.refs_3_, ...), custom_call_target="tpu_custom_call" | custom-call | flops 268435456 | bytes 3145728 | tf_op jit(solution)/shard_map/pallas_call | solution.py:375
  (9 shorter events, 0.1 us)
Async XLA Ops:
  0.0 7.4 %collective-permute-start = (bf16[32,512]{1,0:T(8,128)(2,1)}, bf16[32,512]{1,0:T(8,128)(2,1)S(1)}, u32[]{:S(2)}, u32[]{:S(2)}) collective-permute-start(bf16[32,512]{1,0:T(8,128)(2,1)} %refs_6_.1), channel_id=1, source_target_pairs={{0,2},{1,3},{2,0},{3,1},{4,6},{5,7},{6,4},{7,5},{8,10},{9,11},{10,... | collective-permute-start | bytes 98312 | tf_op jit(solution)/shard_map/ppermute | solution.py:391
  4.0 5.9 %collective-permute-start.1 = (bf16[32,512]{1,0:T(8,128)(2,1)}, bf16[32,512]{1,0:T(8,128)(2,1)S(1)}, u32[]{:S(2)}, u32[]{:S(2)}) collective-permute-start(bf16[32,512]{1,0:T(8,128)(2,1)} %refs_6_.1), channel_id=1, source_target_pairs={{0,3},{1,2},{2,1},{3,0},{4,7},{5,6},{6,5},{7,4},{8,11},{9,10},{10,... | collective-permute-start | bytes 98312 | tf_op jit(solution)/shard_map/ppermute | solution.py:391
  5.4 4.6 %collective-permute-start.2 = (bf16[32,512]{1,0:T(8,128)(2,1)}, bf16[32,512]{1,0:T(8,128)(2,1)S(1)}, u32[]{:S(2)}, u32[]{:S(2)}) collective-permute-start(bf16[32,512]{1,0:T(8,128)(2,1)} %refs_6_.1), channel_id=1, source_target_pairs={{0,1},{1,0},{2,3},{3,2},{4,5},{5,4},{6,7},{7,6},{8,9},{9,8},{10,11... | collective-permute-start | bytes 98312 | tf_op jit(solution)/shard_map/ppermute | solution.py:391
  10.3 1.4 %collective-permute-start.3 = (bf16[136,512]{1,0:T(8,128)(2,1)S(1)}, bf16[136,512]{1,0:T(8,128)(2,1)S(1)}, u32[]{:S(2)}, u32[]{:S(2)}) collective-permute-start(bf16[136,512]{1,0:T(8,128)(2,1)S(1)} %get-tuple-element.38), channel_id=1, source_target_pairs={{0,4},{4,0},{8,12},{12,8},{16,20},{20,16},{24,28},{28,24},{1,5},{5... | collective-permute-start | bytes 417800 | tf_op jit(solution)/shard_map/ppermute | solution.py:391
  10.4 5.1 %collective-permute-start.5 = (bf16[32,512]{1,0:T(8,128)(2,1)S(1)}, bf16[32,512]{1,0:T(8,128)(2,1)S(1)}, u32[]{:S(2)}, u32[]{:S(2)}) collective-permute-start(bf16[32,512]{1,0:T(8,128)(2,1)S(1)} %get-tuple-element.41.mine_ref), channel_id=1, source_target_pairs={{0,2},{1,3},{2,0},{3,1},{4,6},{5,7},{6,4},{7,5},{8,10},{9,11},{10,... | collective-permute-start | bytes 98312 | tf_op jit(solution)/shard_map/ppermute | solution.py:391
  11.8 8.1 %collective-permute-start.4 = (bf16[136,512]{1,0:T(8,128)(2,1)S(1)}, bf16[136,512]{1,0:T(8,128)(2,1)S(1)}, u32[]{:S(2)}, u32[]{:S(2)}) collective-permute-start(bf16[136,512]{1,0:T(8,128)(2,1)S(1)} %get-tuple-element.39.mine_ref), channel_id=1, source_target_pairs={{0,4},{4,0},{8,12},{12,8},{16,20},{20,16},{24,28},{28,24},{1,5},{5... | collective-permute-start | bytes 417800 | tf_op jit(solution)/shard_map/ppermute | solution.py:391
  12.0 8.5 %collective-permute-start.7 = (bf16[136,512]{1,0:T(8,128)(2,1)S(1)}, bf16[136,512]{1,0:T(8,128)(2,1)S(1)}, u32[]{:S(2)}, u32[]{:S(2)}) collective-permute-start(bf16[136,512]{1,0:T(8,128)(2,1)S(1)} %shard_map.93.refs_5_), channel_id=1, source_target_pairs={{0,24},{4,28},{8,16},{12,20},{16,8},{20,12},{24,0},{28,4},{1,25},{... | collective-permute-start | bytes 417800 | tf_op jit(solution)/shard_map/ppermute | solution.py:391
  14.5 7.4 %collective-permute-start.8 = (bf16[136,512]{1,0:T(8,128)(2,1)S(1)}, bf16[136,512]{1,0:T(8,128)(2,1)S(1)}, u32[]{:S(2)}, u32[]{:S(2)}) collective-permute-start(bf16[136,512]{1,0:T(8,128)(2,1)S(1)} %shard_map.93.refs_5_), channel_id=1, source_target_pairs={{0,16},{4,20},{8,24},{12,28},{16,0},{20,4},{24,8},{28,12},{1,17},{... | collective-permute-start | bytes 417800 | tf_op jit(solution)/shard_map/ppermute | solution.py:391
  15.0 7.0 %collective-permute-start.9 = (bf16[136,512]{1,0:T(8,128)(2,1)S(1)}, bf16[136,512]{1,0:T(8,128)(2,1)S(1)}, u32[]{:S(2)}, u32[]{:S(2)}) collective-permute-start(bf16[136,512]{1,0:T(8,128)(2,1)S(1)} %shard_map.93.refs_5_), channel_id=1, source_target_pairs={{0,8},{4,12},{8,0},{12,4},{16,24},{20,28},{24,16},{28,20},{1,9},{5... | collective-permute-start | bytes 417800 | tf_op jit(solution)/shard_map/ppermute | solution.py:391
  15.5 4.3 %collective-permute-start.6 = (bf16[64,512]{1,0:T(8,128)(2,1)S(1)}, bf16[64,512]{1,0:T(8,128)(2,1)S(1)}, u32[]{:S(2)}, u32[]{:S(2)}) collective-permute-start(bf16[64,512]{1,0:T(8,128)(2,1)S(1)} %shard_map.94.refs_4_), channel_id=1, source_target_pairs={{0,1},{1,0},{2,3},{3,2},{4,5},{5,4},{6,7},{7,6},{8,9},{9,8},{10,11... | collective-permute-start | bytes 196616 | tf_op jit(solution)/shard_map/ppermute | solution.py:391
  22.1 1.6 %collective-permute-start.10 = (bf16[256,512]{1,0:T(8,128)(2,1)S(1)}, bf16[256,512]{1,0:T(8,128)(2,1)S(1)}, u32[]{:S(2)}, u32[]{:S(2)}) collective-permute-start(bf16[256,512]{1,0:T(8,128)(2,1)S(1)} %shard_map.97._.refs_5_), channel_id=1, source_target_pairs={{0,4},{4,0},{8,12},{12,8},{16,20},{20,16},{24,28},{28,24},{1,5},{5... | collective-permute-start | bytes 786440 | tf_op jit(solution)/shard_map/ppermute | solution.py:391
  22.1 0.7 %copy-start = (f32[1024]{0:T(1024)S(1)}, f32[1024]{0:T(1024)}, u32[]{:S(2)}) copy-start(f32[1024]{0:T(1024)} %param.17) | copy-start | bytes 12292
  24.3 4.5 %collective-permute-start.11 = (f32[1,512]{1,0:T(1,128)S(1)}, f32[1,512]{1,0:T(1,128)S(1)}, u32[]{:S(2)}, u32[]{:S(2)}) collective-permute-start(f32[1,512]{1,0:T(1,128)S(1)} %get-tuple-element.60.refs_0_), channel_id=1, source_target_pairs={{0,2},{1,3},{2,0},{3,1},{4,6},{5,7},{6,4},{7,5},{8,10},{9,11},{10,... | collective-permute-start | bytes 6152 | tf_op jit(solution)/shard_map/ppermute | solution.py:391
  26.0 5.4 %collective-permute-start.12 = (f32[1,512]{1,0:T(1,128)S(1)}, f32[1,512]{1,0:T(1,128)S(1)}, u32[]{:S(2)}, u32[]{:S(2)}) collective-permute-start(f32[1,512]{1,0:T(1,128)S(1)} %get-tuple-element.60.refs_0_), channel_id=1, source_target_pairs={{0,3},{1,2},{2,1},{3,0},{4,7},{5,6},{6,5},{7,4},{8,11},{9,10},{10,... | collective-permute-start | bytes 6152 | tf_op jit(solution)/shard_map/ppermute | solution.py:391
  28.0 3.6 %collective-permute-start.13 = (f32[1,512]{1,0:T(1,128)S(1)}, f32[1,512]{1,0:T(1,128)S(1)}, u32[]{:S(2)}, u32[]{:S(2)}) collective-permute-start(f32[1,512]{1,0:T(1,128)S(1)} %get-tuple-element.60.refs_0_), channel_id=1, source_target_pairs={{0,1},{1,0},{2,3},{3,2},{4,5},{5,4},{6,7},{7,6},{8,9},{9,8},{10,11... | collective-permute-start | bytes 6152 | tf_op jit(solution)/shard_map/ppermute | solution.py:391

commit v13 on v12

--- a/solution.py
+++ b/solution.py
@@ -12,7 +12,7 @@
 DECAY_ROWS = 8
 BLOCK = 256
 NORM_CHUNKS = 4
-FIRST_HOP = 2
+FIRST_HOP = 1
 VMEM_LIMIT = 40 * 1024 * 1024
 
 f32, bf16 = jnp.float32, jnp.bfloat16
@@ -129,7 +129,7 @@
         copy.wait()
 
 
-def join_kernel(mine_ref, theirs_ref, both_ref):
+def join_kernel(mine_ref, theirs_ref, _, both_ref):
     rows = mine_ref.shape[0]
     both_ref[:rows, :] = mine_ref[...]
     both_ref[rows:, :] = theirs_ref[...]
@@ -170,7 +170,7 @@
         out_refs[sides][index * size : (index + 1) * size, :] = span.astype(bf16)
 
 
-def merge_kernel(size, mine_ref, theirs_ref, pair_ref):
+def merge_kernel(size, mine_ref, theirs_ref, _, pair_ref):
     core = lax.rem(lax.axis_index("seq"), 2)
     mine, theirs = mine_ref[...], theirs_ref[...]
     older = jnp.where(core == 1, theirs, mine).astype(f32)
@@ -427,6 +427,7 @@
     area = tokens * width
     others = from_each(input_map, "head", far_first_masks(parts))
     kept = inputs, gate, level_mix, skip[None, :], input_map, output_map
+    beside = flip(output_map, "head", FIRST_HOP)
     scaled, cum, *kept = call(
         prepare_kernel,
         (
@@ -450,29 +451,26 @@
         (*[shard_shape] * sides, *span_shape),
         (*in_maps, scaled, cum),
         flops=dense,
-        bytes_accessed=4 * area,
     )
     span_states = rest[sides - 1 :]
-    if pairs:
-        theirs = flip(rest[0], "seq", 1)
-        message = call(
-            functools.partial(merge_kernel, size), shard_shape, (shard, theirs), bytes_accessed=area
-        )
-        other_theirs = flip(lax.optimization_barrier((shard, message))[0], "seq", 1)
-    else:
-        other_theirs = theirs = message = shard
-    output_map, _ = lax.optimization_barrier((output_map, shard))
-    beside = flip(output_map, "head", FIRST_HOP)
     rows = output_map.shape[0]
     if rows % 16 == 0:
         both = call(
             join_kernel,
             shaped((2 * rows, tokens), bf16),
-            (output_map, beside),
-            bytes_accessed=8 * rows * tokens,
+            (output_map, beside, shard),
+            flops=8 * dense,
         )
     else:
         both = jnp.concatenate([output_map, beside], axis=0)
+    if pairs:
+        theirs = flip(rest[0], "seq", 1)
+        message = call(
+            functools.partial(merge_kernel, size), shard_shape, (shard, theirs, both), flops=0
+        )
+        other_theirs = flip(lax.optimization_barrier((shard, message))[0], "seq", 1)
+    else:
+        other_theirs = theirs = message = shard
     out_maps = [both, *from_each(both, "head", pair_masks(parts))]
     factor_shape = [shaped((len(spans), GROUP, width), bf16)] if spans else []
     base, own_factor, far, *span_factors = call(

time: 33 us -> 32.5 us (0.985)
  waiting for transfers between devices: 9.03 us -> 8.5 us
    ppermute x14, waiting for transfers between devices: 9.03 us -> 8.5 us  [flip(): lax.ppermute(array, axis, [(i, i ^ mask) for i in range(lax.axis_size(axi...]
  transfers between devices with their start and end apart: 14 -> 14, of which waited for: 8 -> 8; matrix products, arithmetic and copies ran while one was open for 0% -> 0% of each run, Pallas kernels for 16% -> 18%
where the time goes in v13:
time: 32.5 us; the launch traced here: 32.3 us
  starting transfers between devices  15.7 us (48%)
  waiting for transfers between devices  8.5 us (26%)
  Pallas kernels  7.84 us (24%)
    ppermute x14, starting transfers between devices, flip(): lax.ppermute(array, axis, [(i, i ^ mask) for i in range(lax.axis_size(axi...  15.7 us
    ppermute x14, waiting for transfers between devices, flip(): lax.ppermute(array, axis, [(i, i ^ mask) for i in range(lax.axis_size(axi...  8.5 us
    pallas_call x11, Pallas kernels, call(): pl.pallas_call(kernel, out_shape=out_shape, in_specs=specs, out_specs=jax...  7.84 us
  transfers between devices with their start and end apart: 14, of which 8 were waited for; matrix products, arithmetic and copies ran while one was open for 0% of the time, Pallas kernels for 18%

profile of v13, /device:TPU:0, one launch (start us, length us, event | category | flops | bytes accessed | tf_op | source)
XLA Modules:
  0.0 32.3 jit_solution(10412378039193061826)
XLA Ops:
  0.0 4.0 %collective-permute-start = (bf16[32,512]{1,0:T(8,128)(2,1)}, bf16[32,512]{1,0:T(8,128)(2,1)S(1)}, u32[]{:S(2)}, u32[]{:S(2)}) collective-permute-start(bf16[32,512]{1,0:T(8,128)(2,1)} %refs_6_.1), channel_id=1, source_target_pairs={{0,2},{1,3},{2,0},{3,1},{4,6},{5,7},{6,4},{7,5},{8,10},{9,11},{10,... | collective-permute-start | bytes 98312 | tf_op jit(solution)/shard_map/ppermute | solution.py:391
  4.0 1.3 %collective-permute-start.1 = (bf16[32,512]{1,0:T(8,128)(2,1)}, bf16[32,512]{1,0:T(8,128)(2,1)S(1)}, u32[]{:S(2)}, u32[]{:S(2)}) collective-permute-start(bf16[32,512]{1,0:T(8,128)(2,1)} %refs_6_.1), channel_id=1, source_target_pairs={{0,3},{1,2},{2,1},{3,0},{4,7},{5,6},{6,5},{7,4},{8,11},{9,10},{10,... | collective-permute-start | bytes 98312 | tf_op jit(solution)/shard_map/ppermute | solution.py:391
  5.4 0.2 collective-permute-start.2
  5.6 1.8 %collective-permute-start.4 = (bf16[32,512]{1,0:T(8,128)(2,1)}, bf16[32,512]{1,0:T(8,128)(2,1)S(1)}, u32[]{:S(2)}, u32[]{:S(2)}) collective-permute-start(bf16[32,512]{1,0:T(8,128)(2,1)} %refs_7_.1), channel_id=1, source_target_pairs={{0,1},{1,0},{2,3},{3,2},{4,5},{5,4},{6,7},{7,6},{8,9},{9,8},{10,11... | collective-permute-start | bytes 98312 | tf_op jit(solution)/shard_map/ppermute | solution.py:391
  7.4 1.8 %shard_map.91 = (bf16[512,1024]{1,0:T(8,128)(2,1)S(1)}, f32[16,512]{1,0:T(8,128)S(1)}, bf16[512,1024]{1,0:T(8,128)(2,1)S(1)}, bf16[512,1024]{1,0:T(8,128)(2,1)S(...) custom-call(f32[16,512]{1,0:T(8,128)} %refs_0_.1, ...), custom_call_target="tpu_custom_call" | custom-call | flops 4294967296 | bytes 2097152 | tf_op jit(solution)/shard_map/pallas_call | solution.py:375
  9.2 1.0 %collective-permute-done.1.refs_2_ = bf16[32,512]{1,0:T(8,128)(2,1)S(1)} collective-permute-done((bf16[32,512]{1,0:T(8,128)(2,1)}, bf16[32,512]{1,0:T(8,128)(2,1)S(1)}, u32[]{:S(2)}, u32[]{:S(2)}) %collective-permute-start.1) | collective-permute-done | bytes 32800 | tf_op jit(solution)/shard_map/ppermute | solution.py:391
  10.3 0.3 %shard_map.92 = (bf16[136,512]{1,0:T(8,128)(2,1)S(1)}, bf16[136,512]{1,0:T(8,128)(2,1)S(1)}, bf16[128,1024]{1,0:T(8,128)(2,1)S(1)}) custom-call(bf16[32,512]{1,0:T(8,128)(2,1)S(1)} %get-tuple-element.33.refs_0_, bf16[32,512]{1,0:T(8,128)(2,1)S(1)} %collective-permute-done.refs_1_, bf16[32,512]{1,0:T(8,128)(2,1)S(1)} %collective-permute-done.1.refs_2_, ...), custom_call_target="tpu_custom_call" | custom-call | flops 268435456 | tf_op jit(solution)/shard_map/pallas_call | solution.py:375
  10.6 0.1 collective-permute-start.3
  10.7 1.3 %collective-permute-done.3.theirs_ref.refs_9_.refs_4_ = bf16[136,512]{1,0:T(8,128)(2,1)S(1)} collective-permute-done((bf16[136,512]{1,0:T(8,128)(2,1)S(1)}, bf16[136,512]{1,0:T(8,128)(2,1)S(1)}, u32[]{:S(2)}, u32[]{:S(2)}) %collective-permute-start.3) | collective-permute-done | bytes 139296 | tf_op jit(solution)/shard_map/ppermute | solution.py:391
  12.1 0.2 collective-permute-start.5
  12.3 2.5 %collective-permute-start.7 = (bf16[136,512]{1,0:T(8,128)(2,1)S(1)}, bf16[136,512]{1,0:T(8,128)(2,1)S(1)}, u32[]{:S(2)}, u32[]{:S(2)}) collective-permute-start(bf16[136,512]{1,0:T(8,128)(2,1)S(1)} %shard_map.94.refs_5_), channel_id=1, source_target_pairs={{0,24},{4,28},{8,16},{12,20},{16,8},{20,12},{24,0},{28,4},{1,25},{... | collective-permute-start | bytes 417800 | tf_op jit(solution)/shard_map/ppermute | solution.py:391
  14.8 0.5 %collective-permute-start.8 = (bf16[136,512]{1,0:T(8,128)(2,1)S(1)}, bf16[136,512]{1,0:T(8,128)(2,1)S(1)}, u32[]{:S(2)}, u32[]{:S(2)}) collective-permute-start(bf16[136,512]{1,0:T(8,128)(2,1)S(1)} %shard_map.94.refs_5_), channel_id=1, source_target_pairs={{0,16},{4,20},{8,24},{12,28},{16,0},{20,4},{24,8},{28,12},{1,17},{... | collective-permute-start | bytes 417800 | tf_op jit(solution)/shard_map/ppermute | solution.py:391
  15.3 0.5 %collective-permute-start.9 = (bf16[136,512]{1,0:T(8,128)(2,1)S(1)}, bf16[136,512]{1,0:T(8,128)(2,1)S(1)}, u32[]{:S(2)}, u32[]{:S(2)}) collective-permute-start(bf16[136,512]{1,0:T(8,128)(2,1)S(1)} %shard_map.94.refs_5_), channel_id=1, source_target_pairs={{0,8},{4,12},{8,0},{12,4},{16,24},{20,28},{24,16},{28,20},{1,9},{5... | collective-permute-start | bytes 417800 | tf_op jit(solution)/shard_map/ppermute | solution.py:391
  15.8 1.0 %collective-permute-start.6 = (bf16[64,512]{1,0:T(8,128)(2,1)S(1)}, bf16[64,512]{1,0:T(8,128)(2,1)S(1)}, u32[]{:S(2)}, u32[]{:S(2)}) collective-permute-start(bf16[64,512]{1,0:T(8,128)(2,1)S(1)} %shard_map.93._.refs_4_), channel_id=1, source_target_pairs={{0,2},{1,3},{2,0},{3,1},{4,6},{5,7},{6,4},{7,5},{8,10},{9,11},{10,... | collective-permute-start | bytes 196616 | tf_op jit(solution)/shard_map/ppermute | solution.py:391
  16.8 1.8 %shard_map.95 = (f32[512,1024]{1,0:T(8,128)S(1)}, f32[512,1024]{1,0:T(8,128)S(1)}, bf16[3,512,1024]{2,1,0:T(8,128)(2,1)S(1)}, bf16[1,256,1024]{2,1,0:T(8,128)(2,1)S(1)}) custom-call(bf16[512,1024]{1,0:T(8,128)(2,1)S(1)} %get-tuple-element.40.refs_0_, bf16[512,1024]{1,0:T(8,128)(2,1)S(1)} %get-tuple-element.41.refs_1_, ...), custom_call_target="tpu_custom_call" | custom-call | flops 1342177280 | tf_op jit(solution)/shard_map/pallas_call | solution.py:375
  18.6 2.5 %collective-permute-done.6.refs_5_ = bf16[64,512]{1,0:T(8,128)(2,1)S(1)} collective-permute-done((bf16[64,512]{1,0:T(8,128)(2,1)S(1)}, bf16[64,512]{1,0:T(8,128)(2,1)S(1)}, u32[]{:S(2)}, u32[]{:S(2)}) %collective-permute-start.6) | collective-permute-done | bytes 65568 | tf_op jit(solution)/shard_map/ppermute | solution.py:391
  21.1 0.7 %shard_map.96 = (f32[512,512]{1,0:T(8,128)S(1)}, bf16[512,128]{1,0:T(8,128)(2,1)S(1)}, bf16[512,256]{1,0:T(8,128)(2,1)S(1)}) custom-call(bf16[136,512]{1,0:T(8,128)(2,1)S(1)} %collective-permute-done.5._.refs_3_.refs_4_, bf16[32,512]{1,0:T(8,128)(2,1)S(1)} %get-tuple-element.33.refs_0_, bf16[32,512]{1,0:T(8,128)(2,1)S(1)} %collective-permute-done.refs_1_, ...), custom_call_target="tpu_custom_call" | custom-call | tf_op jit(solution)/shard_map/pallas_call | solution.py:375
  21.8 0.4 %collective-permute-done.8.y_ref = bf16[136,512]{1,0:T(8,128)(2,1)S(1)} collective-permute-done((bf16[136,512]{1,0:T(8,128)(2,1)S(1)}, bf16[136,512]{1,0:T(8,128)(2,1)S(1)}, u32[]{:S(2)}, u32[]{:S(2)}) %collective-permute-start.8) | collective-permute-done | bytes 139296 | tf_op jit(solution)/shard_map/ppermute | solution.py:391
  22.1 0.1 collective-permute-done.9.x_ref
  22.2 0.1 shard_map.97._.refs_5_
  22.4 0.1 collective-permute-start.10
  22.4 0.6 %shard_map.98.refs_1_ = f32[512,512]{1,0:T(8,128)S(1)} custom-call(bf16[512,256]{1,0:T(8,128)(2,1)S(1)} %get-tuple-element.50.scores_ref, bf16[512,128]{1,0:T(8,128)(2,1)S(1)} %get-tuple-element.49.turned_ref.refs_0_, bf16[256,512]{1,0:T(8,128)(2,1)S(1)} %shard_map.97._.refs_5_, f32[512,1024]{1,0:T(8,128)S(1)} %get-tuple-element.44.refs_6_.refs_0_, ...), custom_call_target="tpu_custom_call" | custom-call | flops 268435456 | tf_op jit(solution)/shard_map/pallas_call | solution.py:375
  23.0 0.1 copy-done
  23.1 0.5 %shard_map.99 = (f32[512,512]{1,0:T(8,128)S(1)}, f32[512,128]{1,0:T(8,128)S(1)}) custom-call(bf16[512,128]{1,0:T(8,128)(2,1)S(1)} %get-tuple-element.49.turned_ref.refs_0_, f32[512,512]{1,0:T(8,128)S(1)} %get-tuple-element.56.refs_1_, bf16[3,512,1024]{2,1,0:T(8,128)(2,1)S(1)} %get-tuple-element.55.refs_8_.refs_2_, f32[1,1024]{1,0:T(1,128)S(1)} %bitcast.3, ...), custom_call_target="tpu_custom_call" | custom-call | flops 536870912 | bytes 3145728 | tf_op jit(solution)/shard_map/pallas_call | solution.py:375
  23.7 0.3 collective-permute-done.10.refs_5_
  24.0 0.7 %shard_map.100 = (f32[512,512]{1,0:T(8,128)S(1)}, f32[1,512]{1,0:T(1,128)S(1)}) custom-call(bf16[512,128]{1,0:T(8,128)(2,1)S(1)} %get-tuple-element.49.turned_ref.refs_0_, f32[512,512]{1,0:T(8,128)S(1)} %shard_map.98.refs_1_, bf16[3,512,1024]{2,1,0:T(8,128)(2,1)S(1)} %get-tuple-element.55.refs_8_.refs_2_, f32[1,1024]{1,0:T(1,128)S(1)} %bitcast.4, ...), custom_call_target="tpu_custom_call" | custom-call | flops 536870912 | bytes 3145728 | tf_op jit(solution)/shard_map/pallas_call | solution.py:375
  24.6 1.0 %collective-permute-start.11 = (f32[1,512]{1,0:T(1,128)S(1)}, f32[1,512]{1,0:T(1,128)S(1)}, u32[]{:S(2)}, u32[]{:S(2)}) collective-permute-start(f32[1,512]{1,0:T(1,128)S(1)} %get-tuple-element.58.refs_0_), channel_id=1, source_target_pairs={{0,2},{1,3},{2,0},{3,1},{4,6},{5,7},{6,4},{7,5},{8,10},{9,11},{10,... | collective-permute-start | bytes 6152 | tf_op jit(solution)/shard_map/ppermute | solution.py:391
  25.6 1.3 %collective-permute-start.12 = (f32[1,512]{1,0:T(1,128)S(1)}, f32[1,512]{1,0:T(1,128)S(1)}, u32[]{:S(2)}, u32[]{:S(2)}) collective-permute-start(f32[1,512]{1,0:T(1,128)S(1)} %get-tuple-element.58.refs_0_), channel_id=1, source_target_pairs={{0,3},{1,2},{2,1},{3,0},{4,7},{5,6},{6,5},{7,4},{8,11},{9,10},{10,... | collective-permute-start | bytes 6152 | tf_op jit(solution)/shard_map/ppermute | solution.py:391
  26.9 1.2 %collective-permute-start.13 = (f32[1,512]{1,0:T(1,128)S(1)}, f32[1,512]{1,0:T(1,128)S(1)}, u32[]{:S(2)}, u32[]{:S(2)}) collective-permute-start(f32[1,512]{1,0:T(1,128)S(1)} %get-tuple-element.58.refs_0_), channel_id=1, source_target_pairs={{0,1},{1,0},{2,3},{3,2},{4,5},{5,4},{6,7},{7,6},{8,9},{9,8},{10,11... | collective-permute-start | bytes 6152 | tf_op jit(solution)/shard_map/ppermute | solution.py:391
  28.1 1.0 %collective-permute-done.11.refs_1_ = f32[1,512]{1,0:T(1,128)S(1)} collective-permute-done((f32[1,512]{1,0:T(1,128)S(1)}, f32[1,512]{1,0:T(1,128)S(1)}, u32[]{:S(2)}, u32[]{:S(2)}) %collective-permute-start.11) | collective-permute-done | bytes 2080 | tf_op jit(solution)/shard_map/ppermute | solution.py:391
  29.1 1.9 %collective-permute-done.12.refs_2_ = f32[1,512]{1,0:T(1,128)S(1)} collective-permute-done((f32[1,512]{1,0:T(1,128)S(1)}, f32[1,512]{1,0:T(1,128)S(1)}, u32[]{:S(2)}, u32[]{:S(2)}) %collective-permute-start.12) | collective-permute-done | bytes 2080 | tf_op jit(solution)/shard_map/ppermute | solution.py:391
  31.0 1.3 %shard_map.101 = bf16[512,1024]{1,0:T(8,128)(2,1)} custom-call(f32[1,512]{1,0:T(1,128)S(1)} %get-tuple-element.58.refs_0_, f32[1,512]{1,0:T(1,128)S(1)} %collective-permute-done.11.refs_1_, f32[1,512]{1,0:T(1,128)S(1)} %collective-permute-done.12.refs_2_, f32[1,512]{1,0:T(1,128)S(1)} %collective-permute-done.13.refs_3_, ...), custom_call_target="tpu_custom_call" | custom-call | flops 268435456 | bytes 3145728 | tf_op jit(solution)/shard_map/pallas_call | solution.py:375
  (9 shorter events, 0.1 us)
Async XLA Ops:
  0.0 9.2 %collective-permute-start = (bf16[32,512]{1,0:T(8,128)(2,1)}, bf16[32,512]{1,0:T(8,128)(2,1)S(1)}, u32[]{:S(2)}, u32[]{:S(2)}) collective-permute-start(bf16[32,512]{1,0:T(8,128)(2,1)} %refs_6_.1), channel_id=1, source_target_pairs={{0,2},{1,3},{2,0},{3,1},{4,6},{5,7},{6,4},{7,5},{8,10},{9,11},{10,... | collective-permute-start | bytes 98312 | tf_op jit(solution)/shard_map/ppermute | solution.py:391
  4.0 6.2 %collective-permute-start.1 = (bf16[32,512]{1,0:T(8,128)(2,1)}, bf16[32,512]{1,0:T(8,128)(2,1)S(1)}, u32[]{:S(2)}, u32[]{:S(2)}) collective-permute-start(bf16[32,512]{1,0:T(8,128)(2,1)} %refs_6_.1), channel_id=1, source_target_pairs={{0,3},{1,2},{2,1},{3,0},{4,7},{5,6},{6,5},{7,4},{8,11},{9,10},{10,... | collective-permute-start | bytes 98312 | tf_op jit(solution)/shard_map/ppermute | solution.py:391
  5.4 4.9 %collective-permute-start.2 = (bf16[32,512]{1,0:T(8,128)(2,1)}, bf16[32,512]{1,0:T(8,128)(2,1)S(1)}, u32[]{:S(2)}, u32[]{:S(2)}) collective-permute-start(bf16[32,512]{1,0:T(8,128)(2,1)} %refs_6_.1), channel_id=1, source_target_pairs={{0,1},{1,0},{2,3},{3,2},{4,5},{5,4},{6,7},{7,6},{8,9},{9,8},{10,11... | collective-permute-start | bytes 98312 | tf_op jit(solution)/shard_map/ppermute | solution.py:391
  5.6 5.1 %collective-permute-start.4 = (bf16[32,512]{1,0:T(8,128)(2,1)}, bf16[32,512]{1,0:T(8,128)(2,1)S(1)}, u32[]{:S(2)}, u32[]{:S(2)}) collective-permute-start(bf16[32,512]{1,0:T(8,128)(2,1)} %refs_7_.1), channel_id=1, source_target_pairs={{0,1},{1,0},{2,3},{3,2},{4,5},{5,4},{6,7},{7,6},{8,9},{9,8},{10,11... | collective-permute-start | bytes 98312 | tf_op jit(solution)/shard_map/ppermute | solution.py:391
  10.6 1.4 %collective-permute-start.3 = (bf16[136,512]{1,0:T(8,128)(2,1)S(1)}, bf16[136,512]{1,0:T(8,128)(2,1)S(1)}, u32[]{:S(2)}, u32[]{:S(2)}) collective-permute-start(bf16[136,512]{1,0:T(8,128)(2,1)S(1)} %get-tuple-element.37), channel_id=1, source_target_pairs={{0,4},{4,0},{8,12},{12,8},{16,20},{20,16},{24,28},{28,24},{1,5},{5... | collective-permute-start | bytes 417800 | tf_op jit(solution)/shard_map/ppermute | solution.py:391
  12.1 9.0 %collective-permute-start.5 = (bf16[136,512]{1,0:T(8,128)(2,1)S(1)}, bf16[136,512]{1,0:T(8,128)(2,1)S(1)}, u32[]{:S(2)}, u32[]{:S(2)}) collective-permute-start(bf16[136,512]{1,0:T(8,128)(2,1)S(1)} %get-tuple-element.39._.mine_ref), channel_id=1, source_target_pairs={{0,4},{4,0},{8,12},{12,8},{16,20},{20,16},{24,28},{28,24},{1,5},{5... | collective-permute-start | bytes 417800 | tf_op jit(solution)/shard_map/ppermute | solution.py:391
  12.3 9.5 %collective-permute-start.7 = (bf16[136,512]{1,0:T(8,128)(2,1)S(1)}, bf16[136,512]{1,0:T(8,128)(2,1)S(1)}, u32[]{:S(2)}, u32[]{:S(2)}) collective-permute-start(bf16[136,512]{1,0:T(8,128)(2,1)S(1)} %shard_map.94.refs_5_), channel_id=1, source_target_pairs={{0,24},{4,28},{8,16},{12,20},{16,8},{20,12},{24,0},{28,4},{1,25},{... | collective-permute-start | bytes 417800 | tf_op jit(solution)/shard_map/ppermute | solution.py:391
  14.8 7.4 %collective-permute-start.8 = (bf16[136,512]{1,0:T(8,128)(2,1)S(1)}, bf16[136,512]{1,0:T(8,128)(2,1)S(1)}, u32[]{:S(2)}, u32[]{:S(2)}) collective-permute-start(bf16[136,512]{1,0:T(8,128)(2,1)S(1)} %shard_map.94.refs_5_), channel_id=1, source_target_pairs={{0,16},{4,20},{8,24},{12,28},{16,0},{20,4},{24,8},{28,12},{1,17},{... | collective-permute-start | bytes 417800 | tf_op jit(solution)/shard_map/ppermute | solution.py:391
  15.3 7.0 %collective-permute-start.9 = (bf16[136,512]{1,0:T(8,128)(2,1)S(1)}, bf16[136,512]{1,0:T(8,128)(2,1)S(1)}, u32[]{:S(2)}, u32[]{:S(2)}) collective-permute-start(bf16[136,512]{1,0:T(8,128)(2,1)S(1)} %shard_map.94.refs_5_), channel_id=1, source_target_pairs={{0,8},{4,12},{8,0},{12,4},{16,24},{20,28},{24,16},{28,20},{1,9},{5... | collective-permute-start | bytes 417800 | tf_op jit(solution)/shard_map/ppermute | solution.py:391
  15.8 5.3 %collective-permute-start.6 = (bf16[64,512]{1,0:T(8,128)(2,1)S(1)}, bf16[64,512]{1,0:T(8,128)(2,1)S(1)}, u32[]{:S(2)}, u32[]{:S(2)}) collective-permute-start(bf16[64,512]{1,0:T(8,128)(2,1)S(1)} %shard_map.93._.refs_4_), channel_id=1, source_target_pairs={{0,2},{1,3},{2,0},{3,1},{4,6},{5,7},{6,4},{7,5},{8,10},{9,11},{10,... | collective-permute-start | bytes 196616 | tf_op jit(solution)/shard_map/ppermute | solution.py:391
  22.4 1.6 %collective-permute-start.10 = (bf16[256,512]{1,0:T(8,128)(2,1)S(1)}, bf16[256,512]{1,0:T(8,128)(2,1)S(1)}, u32[]{:S(2)}, u32[]{:S(2)}) collective-permute-start(bf16[256,512]{1,0:T(8,128)(2,1)S(1)} %shard_map.97._.refs_5_), channel_id=1, source_target_pairs={{0,4},{4,0},{8,12},{12,8},{16,20},{20,16},{24,28},{28,24},{1,5},{5... | collective-permute-start | bytes 786440 | tf_op jit(solution)/shard_map/ppermute | solution.py:391
  22.4 0.7 %copy-start = (f32[1024]{0:T(1024)S(1)}, f32[1024]{0:T(1024)}, u32[]{:S(2)}) copy-start(f32[1024]{0:T(1024)} %param.17) | copy-start | bytes 12292
  24.6 4.5 %collective-permute-start.11 = (f32[1,512]{1,0:T(1,128)S(1)}, f32[1,512]{1,0:T(1,128)S(1)}, u32[]{:S(2)}, u32[]{:S(2)}) collective-permute-start(f32[1,512]{1,0:T(1,128)S(1)} %get-tuple-element.58.refs_0_), channel_id=1, source_target_pairs={{0,2},{1,3},{2,0},{3,1},{4,6},{5,7},{6,4},{7,5},{8,10},{9,11},{10,... | collective-permute-start | bytes 6152 | tf_op jit(solution)/shard_map/ppermute | solution.py:391
  25.6 5.4 %collective-permute-start.12 = (f32[1,512]{1,0:T(1,128)S(1)}, f32[1,512]{1,0:T(1,128)S(1)}, u32[]{:S(2)}, u32[]{:S(2)}) collective-permute-start(f32[1,512]{1,0:T(1,128)S(1)} %get-tuple-element.58.refs_0_), channel_id=1, source_target_pairs={{0,3},{1,2},{2,1},{3,0},{4,7},{5,6},{6,5},{7,4},{8,11},{9,10},{10,... | collective-permute-start | bytes 6152 | tf_op jit(solution)/shard_map/ppermute | solution.py:391
  26.9 4.0 %collective-permute-start.13 = (f32[1,512]{1,0:T(1,128)S(1)}, f32[1,512]{1,0:T(1,128)S(1)}, u32[]{:S(2)}, u32[]{:S(2)}) collective-permute-start(f32[1,512]{1,0:T(1,128)S(1)} %get-tuple-element.58.refs_0_), channel_id=1, source_target_pairs={{0,1},{1,0},{2,3},{3,2},{4,5},{5,4},{6,7},{7,6},{8,9},{9,8},{10,11... | collective-permute-start | bytes 6152 | tf_op jit(solution)/shard_map/ppermute | solution.py:391

commit v14 on v13

--- a/solution.py
+++ b/solution.py
@@ -12,7 +12,7 @@
 DECAY_ROWS = 8
 BLOCK = 256
 NORM_CHUNKS = 4
-FIRST_HOP = 1
+FIRST_HOP = 2
 VMEM_LIMIT = 40 * 1024 * 1024
 
 f32, bf16 = jnp.float32, jnp.bfloat16
@@ -100,8 +100,8 @@
 
 
 def prepare_kernel(*refs):
-    sources, (scaled_ref, cum_ref), kept_refs = refs[:8], refs[8:10], refs[10:16]
-    step_ref, rate_ref, semaphores = refs[16:]
+    sources, (scaled_ref, cum_ref), kept_refs = refs[:9], refs[9:11], refs[11:18]
+    step_ref, rate_ref, semaphores = refs[18:]
     inputs_ref = kept_refs[0]
     copies = fetch(sources, (step_ref, rate_ref, *kept_refs), semaphores)
     heads, tokens = step_ref.shape
@@ -395,6 +395,11 @@
     return [flip(array, axis, mask) for mask in masks]
 
 
+def around(array, axis):
+    size = lax.axis_size(axis)
+    return [lax.ppermute(array, axis, [(i, (i + shift) % size) for i in range(size)]) for shift in range(1, size)]
+
+
 def merged(older, newer, size):
     older, newer = older.astype(f32), newer.astype(f32)
     decay = newer[size : size + 1]
@@ -426,7 +431,7 @@
     dense = 2 * tokens * GROUP * width
     area = tokens * width
     others = from_each(input_map, "head", far_first_masks(parts))
-    kept = inputs, gate, level_mix, skip[None, :], input_map, output_map
+    kept = inputs, gate, level_mix, skip[None, :], input_map, output_map, norm_gain[None, :]
     beside = flip(output_map, "head", FIRST_HOP)
     scaled, cum, *kept = call(
         prepare_kernel,
@@ -437,10 +442,10 @@
         (step, decay_rate[None, :], *kept),
         flops=16 * dense,
         bytes_accessed=4 * area,
-        hbm=8,
-        scratch=[pltpu.VMEM(step.shape, f32), pltpu.VMEM((1, heads), f32), pltpu.SemaphoreType.DMA((8,))],
+        hbm=9,
+        scratch=[pltpu.VMEM(step.shape, f32), pltpu.VMEM((1, heads), f32), pltpu.SemaphoreType.DMA((9,))],
     )
-    inputs, gate, level_mix, skip, input_map, output_map = kept
+    inputs, gate, level_mix, skip, input_map, output_map, gain = kept
     in_maps = [input_map, *others]
     pairs = lax.axis_size("seq") == 8 and parts == 4
     sides = 2 if pairs else 1
@@ -490,7 +495,6 @@
         (near_shape, shaped((tokens, size), bf16), shaped((tokens, GROUP), bf16)),
         (other_theirs, *in_maps, *out_maps, *near_args),
     )
-    gain = norm_gain[None, :]
     sums_shape = shaped((1, tokens), f32)
     if pairs:
         received = [flip(message, "seq", mask) for mask in (6, 4, 2)]
@@ -530,7 +534,7 @@
             flops=4 * dense,
             bytes_accessed=12 * area,
         )
-    last = [sums, *from_each(sums, "head", far_first_masks(parts))]
+    last = [sums, *around(sums, "head")]
     return call(
         functools.partial(norm_kernel, len(last), width * parts),
         shaped((tokens, width), bf16),

time: 32.5 us -> 32 us (0.985)
  waiting for transfers between devices: 8.5 us -> 6.57 us
  starting transfers between devices: 15.7 us -> 17.4 us
    ppermute x0 -> x3, starting transfers between devices: none -> 4.39 us  [around(): lax.ppermute(array, axis, [(i, (i + shift) % size) for i in range(size)])]
    ppermute x14 -> x11, waiting for transfers between devices: 8.5 us -> 5 us  [flip(): lax.ppermute(array, axis, [(i, i ^ mask) for i in range(lax.axis_size(axi...]
    ppermute x14 -> x11, starting transfers between devices: 15.7 us -> 13 us  [flip(): lax.ppermute(array, axis, [(i, i ^ mask) for i in range(lax.axis_size(axi...]
    ppermute x0 -> x3, waiting for transfers between devices: none -> 1.57 us  [around(): lax.ppermute(array, axis, [(i, (i + shift) % size) for i in range(size)])]
  transfers between devices with their start and end apart: 14 -> 14, of which waited for: 8 -> 7; matrix products, arithmetic and copies ran while one was open for 0% -> 0% of each run, Pallas kernels for 18% -> 18%
where the time goes in v14:
time: 32 us; the launch traced here: 31.9 us
  starting transfers between devices  17.4 us (54%)
  Pallas kernels  7.83 us (24%)
  waiting for transfers between devices  6.57 us (21%)
    ppermute x11, starting transfers between devices, flip(): lax.ppermute(array, axis, [(i, i ^ mask) for i in range(lax.axis_size(axi...  13 us
    pallas_call x11, Pallas kernels, call(): pl.pallas_call(kernel, out_shape=out_shape, in_specs=specs, out_specs=jax...  7.83 us
    ppermute x11, waiting for transfers between devices, flip(): lax.ppermute(array, axis, [(i, i ^ mask) for i in range(lax.axis_size(axi...  5 us
    ppermute x3, starting transfers between devices, around(): lax.ppermute(array, axis, [(i, (i + shift) % size) for i in range(size)])  4.39 us
    ppermute x3, waiting for transfers between devices, around(): lax.ppermute(array, axis, [(i, (i + shift) % size) for i in range(size)])  1.57 us
  transfers between devices with their start and end apart: 14, of which 7 were waited for; matrix products, arithmetic and copies ran while one was open for 0% of the time, Pallas kernels for 18%

profile of v14, /device:TPU:0, one launch (start us, length us, event | category | flops | bytes accessed | tf_op | source)
XLA Modules:
  0.0 31.9 jit_solution(13724790750272956256)
XLA Ops:
  0.0 4.0 %collective-permute-start = (bf16[32,512]{1,0:T(8,128)(2,1)}, bf16[32,512]{1,0:T(8,128)(2,1)S(1)}, u32[]{:S(2)}, u32[]{:S(2)}) collective-permute-start(bf16[32,512]{1,0:T(8,128)(2,1)} %refs_6_.1), channel_id=1, source_target_pairs={{0,2},{1,3},{2,0},{3,1},{4,6},{5,7},{6,4},{7,5},{8,10},{9,11},{10,... | collective-permute-start | bytes 98312 | tf_op jit(solution)/shard_map/ppermute | solution.py:391
  4.0 1.3 %collective-permute-start.1 = (bf16[32,512]{1,0:T(8,128)(2,1)}, bf16[32,512]{1,0:T(8,128)(2,1)S(1)}, u32[]{:S(2)}, u32[]{:S(2)}) collective-permute-start(bf16[32,512]{1,0:T(8,128)(2,1)} %refs_6_.1), channel_id=1, source_target_pairs={{0,3},{1,2},{2,1},{3,0},{4,7},{5,6},{6,5},{7,4},{8,11},{9,10},{10,... | collective-permute-start | bytes 98312 | tf_op jit(solution)/shard_map/ppermute | solution.py:391
  5.4 0.2 collective-permute-start.2
  5.6 2.8 %collective-permute-start.4 = (bf16[32,512]{1,0:T(8,128)(2,1)}, bf16[32,512]{1,0:T(8,128)(2,1)S(1)}, u32[]{:S(2)}, u32[]{:S(2)}) collective-permute-start(bf16[32,512]{1,0:T(8,128)(2,1)} %refs_7_.1), channel_id=1, source_target_pairs={{0,2},{1,3},{2,0},{3,1},{4,6},{5,7},{6,4},{7,5},{8,10},{9,11},{10,... | collective-permute-start | bytes 98312 | tf_op jit(solution)/shard_map/ppermute | solution.py:391
  8.4 1.8 %shard_map.91 = (bf16[512,1024]{1,0:T(8,128)(2,1)S(1)}, f32[16,512]{1,0:T(8,128)S(1)}, bf16[512,1024]{1,0:T(8,128)(2,1)S(1)}, bf16[512,1024]{1,0:T(8,128)(2,1)S(...) custom-call(f32[16,512]{1,0:T(8,128)} %refs_0_.1, ...), custom_call_target="tpu_custom_call" | custom-call | flops 4294967296 | bytes 2097152 | tf_op jit(solution)/shard_map/pallas_call | solution.py:375
  10.2 0.0 collective-permute-done.refs_1_
  10.3 0.3 %shard_map.92 = (bf16[136,512]{1,0:T(8,128)(2,1)S(1)}, bf16[136,512]{1,0:T(8,128)(2,1)S(1)}, bf16[128,1024]{1,0:T(8,128)(2,1)S(1)}) custom-call(bf16[32,512]{1,0:T(8,128)(2,1)S(1)} %get-tuple-element.34.refs_0_, bf16[32,512]{1,0:T(8,128)(2,1)S(1)} %collective-permute-done.refs_1_, bf16[32,512]{1,0:T(8,128)(2,1)S(1)} %collective-permute-done.1.refs_2_, ...), custom_call_target="tpu_custom_call" | custom-call | flops 268435456 | tf_op jit(solution)/shard_map/pallas_call | solution.py:375
  10.6 0.1 collective-permute-start.3
  10.7 1.3 %collective-permute-done.3.theirs_ref.refs_9_.refs_4_ = bf16[136,512]{1,0:T(8,128)(2,1)S(1)} collective-permute-done((bf16[136,512]{1,0:T(8,128)(2,1)S(1)}, bf16[136,512]{1,0:T(8,128)(2,1)S(1)}, u32[]{:S(2)}, u32[]{:S(2)}) %collective-permute-start.3) | collective-permute-done | bytes 139296 | tf_op jit(solution)/shard_map/ppermute | solution.py:391
  12.0 0.1 shard_map.94.refs_5_
  12.1 0.2 collective-permute-start.5
  12.3 2.5 %collective-permute-start.7 = (bf16[136,512]{1,0:T(8,128)(2,1)S(1)}, bf16[136,512]{1,0:T(8,128)(2,1)S(1)}, u32[]{:S(2)}, u32[]{:S(2)}) collective-permute-start(bf16[136,512]{1,0:T(8,128)(2,1)S(1)} %shard_map.94.refs_5_), channel_id=1, source_target_pairs={{0,24},{4,28},{8,16},{12,20},{16,8},{20,12},{24,0},{28,4},{1,25},{... | collective-permute-start | bytes 417800 | tf_op jit(solution)/shard_map/ppermute | solution.py:391
  14.8 0.5 %collective-permute-start.8 = (bf16[136,512]{1,0:T(8,128)(2,1)S(1)}, bf16[136,512]{1,0:T(8,128)(2,1)S(1)}, u32[]{:S(2)}, u32[]{:S(2)}) collective-permute-start(bf16[136,512]{1,0:T(8,128)(2,1)S(1)} %shard_map.94.refs_5_), channel_id=1, source_target_pairs={{0,16},{4,20},{8,24},{12,28},{16,0},{20,4},{24,8},{28,12},{1,17},{... | collective-permute-start | bytes 417800 | tf_op jit(solution)/shard_map/ppermute | solution.py:391
  15.3 0.5 %collective-permute-start.9 = (bf16[136,512]{1,0:T(8,128)(2,1)S(1)}, bf16[136,512]{1,0:T(8,128)(2,1)S(1)}, u32[]{:S(2)}, u32[]{:S(2)}) collective-permute-start(bf16[136,512]{1,0:T(8,128)(2,1)S(1)} %shard_map.94.refs_5_), channel_id=1, source_target_pairs={{0,8},{4,12},{8,0},{12,4},{16,24},{20,28},{24,16},{28,20},{1,9},{5... | collective-permute-start | bytes 417800 | tf_op jit(solution)/shard_map/ppermute | solution.py:391
  15.8 0.7 %collective-permute-start.6 = (bf16[64,512]{1,0:T(8,128)(2,1)S(1)}, bf16[64,512]{1,0:T(8,128)(2,1)S(1)}, u32[]{:S(2)}, u32[]{:S(2)}) collective-permute-start(bf16[64,512]{1,0:T(8,128)(2,1)S(1)} %shard_map.93._.refs_4_), channel_id=1, source_target_pairs={{0,1},{1,0},{2,3},{3,2},{4,5},{5,4},{6,7},{7,6},{8,9},{9,8},{10,11... | collective-permute-start | bytes 196616 | tf_op jit(solution)/shard_map/ppermute | solution.py:391
  16.5 1.8 %shard_map.95 = (f32[512,1024]{1,0:T(8,128)S(1)}, f32[512,1024]{1,0:T(8,128)S(1)}, bf16[3,512,1024]{2,1,0:T(8,128)(2,1)S(1)}, bf16[1,256,1024]{2,1,0:T(8,128)(2,1)S(1)}) custom-call(bf16[512,1024]{1,0:T(8,128)(2,1)S(1)} %get-tuple-element.41.refs_0_, bf16[512,1024]{1,0:T(8,128)(2,1)S(1)} %get-tuple-element.42.refs_1_, ...), custom_call_target="tpu_custom_call" | custom-call | flops 1342177280 | tf_op jit(solution)/shard_map/pallas_call | solution.py:375
  18.3 1.8 %collective-permute-done.6.refs_5_ = bf16[64,512]{1,0:T(8,128)(2,1)S(1)} collective-permute-done((bf16[64,512]{1,0:T(8,128)(2,1)S(1)}, bf16[64,512]{1,0:T(8,128)(2,1)S(1)}, u32[]{:S(2)}, u32[]{:S(2)}) %collective-permute-start.6) | collective-permute-done | bytes 65568 | tf_op jit(solution)/shard_map/ppermute | solution.py:391
  20.1 0.7 %shard_map.96 = (f32[512,512]{1,0:T(8,128)S(1)}, bf16[512,128]{1,0:T(8,128)(2,1)S(1)}, bf16[512,256]{1,0:T(8,128)(2,1)S(1)}) custom-call(bf16[136,512]{1,0:T(8,128)(2,1)S(1)} %collective-permute-done.5._.refs_3_.refs_4_, bf16[32,512]{1,0:T(8,128)(2,1)S(1)} %get-tuple-element.34.refs_0_, bf16[32,512]{1,0:T(8,128)(2,1)S(1)} %collective-permute-done.refs_1_, ...), custom_call_target="tpu_custom_call" | custom-call | tf_op jit(solution)/shard_map/pallas_call | solution.py:375
  20.8 1.3 %collective-permute-done.8.y_ref = bf16[136,512]{1,0:T(8,128)(2,1)S(1)} collective-permute-done((bf16[136,512]{1,0:T(8,128)(2,1)S(1)}, bf16[136,512]{1,0:T(8,128)(2,1)S(1)}, u32[]{:S(2)}, u32[]{:S(2)}) %collective-permute-start.8) | collective-permute-done | bytes 139296 | tf_op jit(solution)/shard_map/ppermute | solution.py:391
  22.1 0.1 collective-permute-done.9.x_ref
  22.2 0.1 shard_map.97._.refs_5_
  22.4 0.1 collective-permute-start.10
  22.4 0.6 %shard_map.98.refs_1_ = f32[512,512]{1,0:T(8,128)S(1)} custom-call(bf16[512,256]{1,0:T(8,128)(2,1)S(1)} %get-tuple-element.51.scores_ref, bf16[512,128]{1,0:T(8,128)(2,1)S(1)} %get-tuple-element.50.turned_ref.refs_0_, bf16[256,512]{1,0:T(8,128)(2,1)S(1)} %shard_map.97._.refs_5_, f32[512,1024]{1,0:T(8,128)S(1)} %get-tuple-element.45.refs_6_.refs_0_, ...), custom_call_target="tpu_custom_call" | custom-call | flops 268435456 | tf_op jit(solution)/shard_map/pallas_call | solution.py:375
  23.0 0.5 %shard_map.99 = (f32[512,512]{1,0:T(8,128)S(1)}, f32[512,128]{1,0:T(8,128)S(1)}) custom-call(bf16[512,128]{1,0:T(8,128)(2,1)S(1)} %get-tuple-element.50.turned_ref.refs_0_, f32[512,512]{1,0:T(8,128)S(1)} %get-tuple-element.58.refs_1_, bf16[3,512,1024]{2,1,0:T(8,128)(2,1)S(1)} %get-tuple-element.56.refs_8_.refs_2_, f32[1,1024]{1,0:T(1,128)S(1)} %get-tuple-element.57.refs_3_, ...), custom_call_target="tpu_custom_call" | custom-call | flops 536870912 | bytes 3145728 | tf_op jit(solution)/shard_map/pallas_call | solution.py:375
  23.6 0.4 %collective-permute-done.10.refs_5_ = bf16[256,512]{1,0:T(8,128)(2,1)S(1)} collective-permute-done((bf16[256,512]{1,0:T(8,128)(2,1)S(1)}, bf16[256,512]{1,0:T(8,128)(2,1)S(1)}, u32[]{:S(2)}, u32[]{:S(2)}) %collective-permute-start.10) | collective-permute-done | bytes 262176 | tf_op jit(solution)/shard_map/ppermute | solution.py:391
  24.0 0.7 %shard_map.100 = (f32[512,512]{1,0:T(8,128)S(1)}, f32[1,512]{1,0:T(1,128)S(1)}) custom-call(bf16[512,128]{1,0:T(8,128)(2,1)S(1)} %get-tuple-element.50.turned_ref.refs_0_, f32[512,512]{1,0:T(8,128)S(1)} %shard_map.98.refs_1_, bf16[3,512,1024]{2,1,0:T(8,128)(2,1)S(1)} %get-tuple-element.56.refs_8_.refs_2_, f32[1,1024]{1,0:T(1,128)S(1)} %get-tuple-element.57.refs_3_, ...), custom_call_target="tpu_custom_call" | custom-call | flops 536870912 | bytes 3145728 | tf_op jit(solution)/shard_map/pallas_call | solution.py:375
  24.6 0.7 %collective-permute-start.11 = (f32[1,512]{1,0:T(1,128)S(1)}, f32[1,512]{1,0:T(1,128)S(1)}, u32[]{:S(2)}, u32[]{:S(2)}) collective-permute-start(f32[1,512]{1,0:T(1,128)S(1)} %get-tuple-element.60.refs_0_), channel_id=1, source_target_pairs={{0,1},{1,2},{2,3},{3,0},{4,5},{5,6},{6,7},{7,4},{8,9},{9,10},{10,1... | collective-permute-start | bytes 6152 | tf_op jit(solution)/shard_map/ppermute | solution.py:400
  25.3 1.6 %collective-permute-start.12 = (f32[1,512]{1,0:T(1,128)S(1)}, f32[1,512]{1,0:T(1,128)S(1)}, u32[]{:S(2)}, u32[]{:S(2)}) collective-permute-start(f32[1,512]{1,0:T(1,128)S(1)} %get-tuple-element.60.refs_0_), channel_id=1, source_target_pairs={{0,2},{1,3},{2,0},{3,1},{4,6},{5,7},{6,4},{7,5},{8,10},{9,11},{10,... | collective-permute-start | bytes 6152 | tf_op jit(solution)/shard_map/ppermute | solution.py:400
  27.0 2.1 %collective-permute-start.13 = (f32[1,512]{1,0:T(1,128)S(1)}, f32[1,512]{1,0:T(1,128)S(1)}, u32[]{:S(2)}, u32[]{:S(2)}) collective-permute-start(f32[1,512]{1,0:T(1,128)S(1)} %get-tuple-element.60.refs_0_), channel_id=1, source_target_pairs={{0,3},{1,0},{2,1},{3,2},{4,7},{5,4},{6,5},{7,6},{8,11},{9,8},{10,9... | collective-permute-start | bytes 6152 | tf_op jit(solution)/shard_map/ppermute | solution.py:400
  29.0 1.0 %collective-permute-done.11.refs_1_ = f32[1,512]{1,0:T(1,128)S(1)} collective-permute-done((f32[1,512]{1,0:T(1,128)S(1)}, f32[1,512]{1,0:T(1,128)S(1)}, u32[]{:S(2)}, u32[]{:S(2)}) %collective-permute-start.11) | collective-permute-done | bytes 2080 | tf_op jit(solution)/shard_map/ppermute | solution.py:400
  30.0 0.6 %collective-permute-done.13.refs_3_ = f32[1,512]{1,0:T(1,128)S(1)} collective-permute-done((f32[1,512]{1,0:T(1,128)S(1)}, f32[1,512]{1,0:T(1,128)S(1)}, u32[]{:S(2)}, u32[]{:S(2)}) %collective-permute-start.13) | collective-permute-done | bytes 2080 | tf_op jit(solution)/shard_map/ppermute | solution.py:400
  30.6 1.3 %shard_map.101 = bf16[512,1024]{1,0:T(8,128)(2,1)} custom-call(f32[1,512]{1,0:T(1,128)S(1)} %get-tuple-element.60.refs_0_, f32[1,512]{1,0:T(1,128)S(1)} %collective-permute-done.11.refs_1_, f32[1,512]{1,0:T(1,128)S(1)} %collective-permute-done.12.refs_2_, f32[1,512]{1,0:T(1,128)S(1)} %collective-permute-done.13.refs_3_, ...), custom_call_target="tpu_custom_call" | custom-call | flops 268435456 | bytes 3145728 | tf_op jit(solution)/shard_map/pallas_call | solution.py:375
  (7 shorter events, 0.0 us)
Async XLA Ops:
  0.0 10.2 %collective-permute-start = (bf16[32,512]{1,0:T(8,128)(2,1)}, bf16[32,512]{1,0:T(8,128)(2,1)S(1)}, u32[]{:S(2)}, u32[]{:S(2)}) collective-permute-start(bf16[32,512]{1,0:T(8,128)(2,1)} %refs_6_.1), channel_id=1, source_target_pairs={{0,2},{1,3},{2,0},{3,1},{4,6},{5,7},{6,4},{7,5},{8,10},{9,11},{10,... | collective-permute-start | bytes 98312 | tf_op jit(solution)/shard_map/ppermute | solution.py:391
  4.0 6.2 %collective-permute-start.1 = (bf16[32,512]{1,0:T(8,128)(2,1)}, bf16[32,512]{1,0:T(8,128)(2,1)S(1)}, u32[]{:S(2)}, u32[]{:S(2)}) collective-permute-start(bf16[32,512]{1,0:T(8,128)(2,1)} %refs_6_.1), channel_id=1, source_target_pairs={{0,3},{1,2},{2,1},{3,0},{4,7},{5,6},{6,5},{7,4},{8,11},{9,10},{10,... | collective-permute-start | bytes 98312 | tf_op jit(solution)/shard_map/ppermute | solution.py:391
  5.4 4.9 %collective-permute-start.2 = (bf16[32,512]{1,0:T(8,128)(2,1)}, bf16[32,512]{1,0:T(8,128)(2,1)S(1)}, u32[]{:S(2)}, u32[]{:S(2)}) collective-permute-start(bf16[32,512]{1,0:T(8,128)(2,1)} %refs_6_.1), channel_id=1, source_target_pairs={{0,1},{1,0},{2,3},{3,2},{4,5},{5,4},{6,7},{7,6},{8,9},{9,8},{10,11... | collective-permute-start | bytes 98312 | tf_op jit(solution)/shard_map/ppermute | solution.py:391
  5.6 5.1 %collective-permute-start.4 = (bf16[32,512]{1,0:T(8,128)(2,1)}, bf16[32,512]{1,0:T(8,128)(2,1)S(1)}, u32[]{:S(2)}, u32[]{:S(2)}) collective-permute-start(bf16[32,512]{1,0:T(8,128)(2,1)} %refs_7_.1), channel_id=1, source_target_pairs={{0,2},{1,3},{2,0},{3,1},{4,6},{5,7},{6,4},{7,5},{8,10},{9,11},{10,... | collective-permute-start | bytes 98312 | tf_op jit(solution)/shard_map/ppermute | solution.py:391
  10.6 1.4 %collective-permute-start.3 = (bf16[136,512]{1,0:T(8,128)(2,1)S(1)}, bf16[136,512]{1,0:T(8,128)(2,1)S(1)}, u32[]{:S(2)}, u32[]{:S(2)}) collective-permute-start(bf16[136,512]{1,0:T(8,128)(2,1)S(1)} %get-tuple-element.38), channel_id=1, source_target_pairs={{0,4},{4,0},{8,12},{12,8},{16,20},{20,16},{24,28},{28,24},{1,5},{5... | collective-permute-start | bytes 417800 | tf_op jit(solution)/shard_map/ppermute | solution.py:391
  12.1 8.0 %collective-permute-start.5 = (bf16[136,512]{1,0:T(8,128)(2,1)S(1)}, bf16[136,512]{1,0:T(8,128)(2,1)S(1)}, u32[]{:S(2)}, u32[]{:S(2)}) collective-permute-start(bf16[136,512]{1,0:T(8,128)(2,1)S(1)} %get-tuple-element.40._.mine_ref), channel_id=1, source_target_pairs={{0,4},{4,0},{8,12},{12,8},{16,20},{20,16},{24,28},{28,24},{1,5},{5... | collective-permute-start | bytes 417800 | tf_op jit(solution)/shard_map/ppermute | solution.py:391
  12.3 8.5 %collective-permute-start.7 = (bf16[136,512]{1,0:T(8,128)(2,1)S(1)}, bf16[136,512]{1,0:T(8,128)(2,1)S(1)}, u32[]{:S(2)}, u32[]{:S(2)}) collective-permute-start(bf16[136,512]{1,0:T(8,128)(2,1)S(1)} %shard_map.94.refs_5_), channel_id=1, source_target_pairs={{0,24},{4,28},{8,16},{12,20},{16,8},{20,12},{24,0},{28,4},{1,25},{... | collective-permute-start | bytes 417800 | tf_op jit(solution)/shard_map/ppermute | solution.py:391
  14.8 7.4 %collective-permute-start.8 = (bf16[136,512]{1,0:T(8,128)(2,1)S(1)}, bf16[136,512]{1,0:T(8,128)(2,1)S(1)}, u32[]{:S(2)}, u32[]{:S(2)}) collective-permute-start(bf16[136,512]{1,0:T(8,128)(2,1)S(1)} %shard_map.94.refs_5_), channel_id=1, source_target_pairs={{0,16},{4,20},{8,24},{12,28},{16,0},{20,4},{24,8},{28,12},{1,17},{... | collective-permute-start | bytes 417800 | tf_op jit(solution)/shard_map/ppermute | solution.py:391
  15.3 6.9 %collective-permute-start.9 = (bf16[136,512]{1,0:T(8,128)(2,1)S(1)}, bf16[136,512]{1,0:T(8,128)(2,1)S(1)}, u32[]{:S(2)}, u32[]{:S(2)}) collective-permute-start(bf16[136,512]{1,0:T(8,128)(2,1)S(1)} %shard_map.94.refs_5_), channel_id=1, source_target_pairs={{0,8},{4,12},{8,0},{12,4},{16,24},{20,28},{24,16},{28,20},{1,9},{5... | collective-permute-start | bytes 417800 | tf_op jit(solution)/shard_map/ppermute | solution.py:391
  15.8 4.3 %collective-permute-start.6 = (bf16[64,512]{1,0:T(8,128)(2,1)S(1)}, bf16[64,512]{1,0:T(8,128)(2,1)S(1)}, u32[]{:S(2)}, u32[]{:S(2)}) collective-permute-start(bf16[64,512]{1,0:T(8,128)(2,1)S(1)} %shard_map.93._.refs_4_), channel_id=1, source_target_pairs={{0,1},{1,0},{2,3},{3,2},{4,5},{5,4},{6,7},{7,6},{8,9},{9,8},{10,11... | collective-permute-start | bytes 196616 | tf_op jit(solution)/shard_map/ppermute | solution.py:391
  22.4 1.6 %collective-permute-start.10 = (bf16[256,512]{1,0:T(8,128)(2,1)S(1)}, bf16[256,512]{1,0:T(8,128)(2,1)S(1)}, u32[]{:S(2)}, u32[]{:S(2)}) collective-permute-start(bf16[256,512]{1,0:T(8,128)(2,1)S(1)} %shard_map.97._.refs_5_), channel_id=1, source_target_pairs={{0,4},{4,0},{8,12},{12,8},{16,20},{20,16},{24,28},{28,24},{1,5},{5... | collective-permute-start | bytes 786440 | tf_op jit(solution)/shard_map/ppermute | solution.py:391
  24.6 5.4 %collective-permute-start.11 = (f32[1,512]{1,0:T(1,128)S(1)}, f32[1,512]{1,0:T(1,128)S(1)}, u32[]{:S(2)}, u32[]{:S(2)}) collective-permute-start(f32[1,512]{1,0:T(1,128)S(1)} %get-tuple-element.60.refs_0_), channel_id=1, source_target_pairs={{0,1},{1,2},{2,3},{3,0},{4,5},{5,6},{6,7},{7,4},{8,9},{9,10},{10,1... | collective-permute-start | bytes 6152 | tf_op jit(solution)/shard_map/ppermute | solution.py:400
  25.3 4.7 %collective-permute-start.12 = (f32[1,512]{1,0:T(1,128)S(1)}, f32[1,512]{1,0:T(1,128)S(1)}, u32[]{:S(2)}, u32[]{:S(2)}) collective-permute-start(f32[1,512]{1,0:T(1,128)S(1)} %get-tuple-element.60.refs_0_), channel_id=1, source_target_pairs={{0,2},{1,3},{2,0},{3,1},{4,6},{5,7},{6,4},{7,5},{8,10},{9,11},{10,... | collective-permute-start | bytes 6152 | tf_op jit(solution)/shard_map/ppermute | solution.py:400
  27.0 3.6 %collective-permute-start.13 = (f32[1,512]{1,0:T(1,128)S(1)}, f32[1,512]{1,0:T(1,128)S(1)}, u32[]{:S(2)}, u32[]{:S(2)}) collective-permute-start(f32[1,512]{1,0:T(1,128)S(1)} %get-tuple-element.60.refs_0_), channel_id=1, source_target_pairs={{0,3},{1,0},{2,1},{3,2},{4,7},{5,4},{6,5},{7,6},{8,11},{9,8},{10,9... | collective-permute-start | bytes 6152 | tf_op jit(solution)/shard_map/ppermute | solution.py:400

commit v15 on v14

--- a/solution.py
+++ b/solution.py
@@ -238,7 +238,7 @@
             near_ref[at, cols] = total
 
 
-def near_kernel(parts, spans, paired, _, *refs):
+def near_kernel(parts, spans, paired, *refs):
     count = parts + parts // 2
     in_refs, out_refs, rest = refs[:parts], refs[parts:count], refs[count:-3]
     near_ref, turned_ref, scores_ref = refs[-3:]
@@ -493,12 +493,12 @@
     near, turned, scores = call(
         functools.partial(near_kernel, parts, spans, pairs),
         (near_shape, shaped((tokens, size), bf16), shaped((tokens, GROUP), bf16)),
-        (other_theirs, *in_maps, *out_maps, *near_args),
+        (*in_maps, *out_maps, *near_args),
     )
     sums_shape = shaped((1, tokens), f32)
     if pairs:
         received = [flip(message, "seq", mask) for mask in (6, 4, 2)]
-        *received, near, far = lax.optimization_barrier((*received, near, far))
+        *received, other_theirs, near, far = lax.optimization_barrier((*received, other_theirs, near, far))
         own = call(
             functools.partial(combine_kernel, size),
             shaped((2 * size, width // 2), bf16),

time: 32 us -> 31.7 us (level)
  starting transfers between devices: 17.4 us -> 16.6 us
  waiting for transfers between devices: 6.57 us -> 6.91 us
    ppermute x3, starting transfers between devices: 4.39 us -> 3.84 us  [around(): lax.ppermute(array, axis, [(i, (i + shift) % size) for i in range(size)])]
    ppermute x3, waiting for transfers between devices: 1.57 us -> 2.12 us  [around(): lax.ppermute(array, axis, [(i, (i + shift) % size) for i in range(size)])]
where the time goes in v15:
time: 31.7 us; the launch traced here: 31.5 us
  starting transfers between devices  16.6 us (52%)
  Pallas kernels  7.86 us (25%)
  waiting for transfers between devices  6.91 us (22%)
    ppermute x11, starting transfers between devices, flip(): lax.ppermute(array, axis, [(i, i ^ mask) for i in range(lax.axis_size(axi...  12.8 us
    pallas_call x11, Pallas kernels, call(): pl.pallas_call(kernel, out_shape=out_shape, in_specs=specs, out_specs=jax...  7.86 us
    ppermute x11, waiting for transfers between devices, flip(): lax.ppermute(array, axis, [(i, i ^ mask) for i in range(lax.axis_size(axi...  4.79 us
    ppermute x3, starting transfers between devices, around(): lax.ppermute(array, axis, [(i, (i + shift) % size) for i in range(size)])  3.84 us
    ppermute x3, waiting for transfers between devices, around(): lax.ppermute(array, axis, [(i, (i + shift) % size) for i in range(size)])  2.12 us
  transfers between devices with their start and end apart: 14, of which 7 were waited for; matrix products, arithmetic and copies ran while one was open for 0% of the time, Pallas kernels for 18%

profile of v15, /device:TPU:0, one launch (start us, length us, event | category | flops | bytes accessed | tf_op | source)
XLA Modules:
  0.0 31.5 jit_solution(8662284904870195460)
XLA Ops:
  0.0 4.0 %collective-permute-start = (bf16[32,512]{1,0:T(8,128)(2,1)}, bf16[32,512]{1,0:T(8,128)(2,1)S(1)}, u32[]{:S(2)}, u32[]{:S(2)}) collective-permute-start(bf16[32,512]{1,0:T(8,128)(2,1)} %refs_6_.1), channel_id=1, source_target_pairs={{0,2},{1,3},{2,0},{3,1},{4,6},{5,7},{6,4},{7,5},{8,10},{9,11},{10,... | collective-permute-start | bytes 98312 | tf_op jit(solution)/shard_map/ppermute | solution.py:391
  4.0 1.3 %collective-permute-start.1 = (bf16[32,512]{1,0:T(8,128)(2,1)}, bf16[32,512]{1,0:T(8,128)(2,1)S(1)}, u32[]{:S(2)}, u32[]{:S(2)}) collective-permute-start(bf16[32,512]{1,0:T(8,128)(2,1)} %refs_6_.1), channel_id=1, source_target_pairs={{0,3},{1,2},{2,1},{3,0},{4,7},{5,6},{6,5},{7,4},{8,11},{9,10},{10,... | collective-permute-start | bytes 98312 | tf_op jit(solution)/shard_map/ppermute | solution.py:391
  5.4 0.2 collective-permute-start.2
  5.6 2.8 %collective-permute-start.3 = (bf16[32,512]{1,0:T(8,128)(2,1)}, bf16[32,512]{1,0:T(8,128)(2,1)S(1)}, u32[]{:S(2)}, u32[]{:S(2)}) collective-permute-start(bf16[32,512]{1,0:T(8,128)(2,1)} %refs_7_.1), channel_id=1, source_target_pairs={{0,2},{1,3},{2,0},{3,1},{4,6},{5,7},{6,4},{7,5},{8,10},{9,11},{10,... | collective-permute-start | bytes 98312 | tf_op jit(solution)/shard_map/ppermute | solution.py:391
  8.4 1.8 %shard_map.91 = (bf16[512,1024]{1,0:T(8,128)(2,1)S(1)}, f32[16,512]{1,0:T(8,128)S(1)}, bf16[512,1024]{1,0:T(8,128)(2,1)S(1)}, bf16[512,1024]{1,0:T(8,128)(2,1)S(...) custom-call(f32[16,512]{1,0:T(8,128)} %refs_0_.1, ...), custom_call_target="tpu_custom_call" | custom-call | flops 4294967296 | bytes 2097152 | tf_op jit(solution)/shard_map/pallas_call | solution.py:375
  10.2 0.0 collective-permute-done.1.refs_2_
  10.3 0.0 collective-permute-done.2.refs_3_
  10.3 0.3 %shard_map.92 = (bf16[136,512]{1,0:T(8,128)(2,1)S(1)}, bf16[136,512]{1,0:T(8,128)(2,1)S(1)}, bf16[128,1024]{1,0:T(8,128)(2,1)S(1)}) custom-call(bf16[32,512]{1,0:T(8,128)(2,1)S(1)} %get-tuple-element.35.refs_0_, bf16[32,512]{1,0:T(8,128)(2,1)S(1)} %collective-permute-done.refs_1_, bf16[32,512]{1,0:T(8,128)(2,1)S(1)} %collective-permute-done.1.refs_2_, ...), custom_call_target="tpu_custom_call" | custom-call | flops 268435456 | tf_op jit(solution)/shard_map/pallas_call | solution.py:375
  10.6 0.1 collective-permute-start.5
  10.7 1.3 %collective-permute-done.5.theirs_ref.refs_9_.refs_4_ = bf16[136,512]{1,0:T(8,128)(2,1)S(1)} collective-permute-done((bf16[136,512]{1,0:T(8,128)(2,1)S(1)}, bf16[136,512]{1,0:T(8,128)(2,1)S(1)}, u32[]{:S(2)}, u32[]{:S(2)}) %collective-permute-start.5) | collective-permute-done | bytes 139296 | tf_op jit(solution)/shard_map/ppermute | solution.py:391
  12.0 0.1 shard_map.94.refs_5_
  12.1 2.5 %collective-permute-start.6 = (bf16[136,512]{1,0:T(8,128)(2,1)S(1)}, bf16[136,512]{1,0:T(8,128)(2,1)S(1)}, u32[]{:S(2)}, u32[]{:S(2)}) collective-permute-start(bf16[136,512]{1,0:T(8,128)(2,1)S(1)} %shard_map.94.refs_5_), channel_id=1, source_target_pairs={{0,24},{4,28},{8,16},{12,20},{16,8},{20,12},{24,0},{28,4},{1,25},{... | collective-permute-start | bytes 417800 | tf_op jit(solution)/shard_map/ppermute | solution.py:391
  14.6 0.5 %collective-permute-start.7 = (bf16[136,512]{1,0:T(8,128)(2,1)S(1)}, bf16[136,512]{1,0:T(8,128)(2,1)S(1)}, u32[]{:S(2)}, u32[]{:S(2)}) collective-permute-start(bf16[136,512]{1,0:T(8,128)(2,1)S(1)} %shard_map.94.refs_5_), channel_id=1, source_target_pairs={{0,16},{4,20},{8,24},{12,28},{16,0},{20,4},{24,8},{28,12},{1,17},{... | collective-permute-start | bytes 417800 | tf_op jit(solution)/shard_map/ppermute | solution.py:391
  15.1 0.5 %collective-permute-start.8 = (bf16[136,512]{1,0:T(8,128)(2,1)S(1)}, bf16[136,512]{1,0:T(8,128)(2,1)S(1)}, u32[]{:S(2)}, u32[]{:S(2)}) collective-permute-start(bf16[136,512]{1,0:T(8,128)(2,1)S(1)} %shard_map.94.refs_5_), channel_id=1, source_target_pairs={{0,8},{4,12},{8,0},{12,4},{16,24},{20,28},{24,16},{28,20},{1,9},{5... | collective-permute-start | bytes 417800 | tf_op jit(solution)/shard_map/ppermute | solution.py:391
  15.7 0.7 %collective-permute-start.4 = (bf16[64,512]{1,0:T(8,128)(2,1)S(1)}, bf16[64,512]{1,0:T(8,128)(2,1)S(1)}, u32[]{:S(2)}, u32[]{:S(2)}) collective-permute-start(bf16[64,512]{1,0:T(8,128)(2,1)S(1)} %shard_map.93._.refs_4_), channel_id=1, source_target_pairs={{0,1},{1,0},{2,3},{3,2},{4,5},{5,4},{6,7},{7,6},{8,9},{9,8},{10,11... | collective-permute-start | bytes 196616 | tf_op jit(solution)/shard_map/ppermute | solution.py:391
  16.3 1.8 %shard_map.95 = (f32[512,1024]{1,0:T(8,128)S(1)}, f32[512,1024]{1,0:T(8,128)S(1)}, bf16[3,512,1024]{2,1,0:T(8,128)(2,1)S(1)}, bf16[1,256,1024]{2,1,0:T(8,128)(2,1)S(1)}) custom-call(bf16[512,1024]{1,0:T(8,128)(2,1)S(1)} %get-tuple-element.40.refs_0_, bf16[512,1024]{1,0:T(8,128)(2,1)S(1)} %get-tuple-element.41.refs_1_, ...), custom_call_target="tpu_custom_call" | custom-call | flops 1342177280 | tf_op jit(solution)/shard_map/pallas_call | solution.py:375
  18.1 2.0 %collective-permute-done.4.refs_5_ = bf16[64,512]{1,0:T(8,128)(2,1)S(1)} collective-permute-done((bf16[64,512]{1,0:T(8,128)(2,1)S(1)}, bf16[64,512]{1,0:T(8,128)(2,1)S(1)}, u32[]{:S(2)}, u32[]{:S(2)}) %collective-permute-start.4) | collective-permute-done | bytes 65568 | tf_op jit(solution)/shard_map/ppermute | solution.py:391
  20.2 0.7 %shard_map.96 = (f32[512,512]{1,0:T(8,128)S(1)}, bf16[512,128]{1,0:T(8,128)(2,1)S(1)}, bf16[512,256]{1,0:T(8,128)(2,1)S(1)}) custom-call(bf16[32,512]{1,0:T(8,128)(2,1)S(1)} %get-tuple-element.35.refs_0_, bf16[32,512]{1,0:T(8,128)(2,1)S(1)} %collective-permute-done.refs_1_, bf16[32,512]{1,0:T(8,128)(2,1)S(1)} %collective-permute-done.1.refs_2_, ...), custom_call_target="tpu_custom_call" | custom-call | tf_op jit(solution)/shard_map/pallas_call | solution.py:375
  20.9 0.9 %collective-permute-done.7.y_ref = bf16[136,512]{1,0:T(8,128)(2,1)S(1)} collective-permute-done((bf16[136,512]{1,0:T(8,128)(2,1)S(1)}, bf16[136,512]{1,0:T(8,128)(2,1)S(1)}, u32[]{:S(2)}, u32[]{:S(2)}) %collective-permute-start.7) | collective-permute-done | bytes 139296 | tf_op jit(solution)/shard_map/ppermute | solution.py:391
  21.8 0.1 collective-permute-done.8.x_ref
  21.9 0.1 shard_map.97._.refs_5_
  22.0 0.1 collective-permute-start.10
  22.1 0.6 %shard_map.98.refs_1_ = f32[512,512]{1,0:T(8,128)S(1)} custom-call(bf16[512,256]{1,0:T(8,128)(2,1)S(1)} %get-tuple-element.51.scores_ref, bf16[512,128]{1,0:T(8,128)(2,1)S(1)} %get-tuple-element.50.turned_ref.refs_0_, bf16[256,512]{1,0:T(8,128)(2,1)S(1)} %shard_map.97._.refs_5_, f32[512,1024]{1,0:T(8,128)S(1)} %get-tuple-element.45.refs_6_.refs_0_, ...), custom_call_target="tpu_custom_call" | custom-call | flops 268435456 | tf_op jit(solution)/shard_map/pallas_call | solution.py:375
  22.7 0.5 %shard_map.99 = (f32[512,512]{1,0:T(8,128)S(1)}, f32[512,128]{1,0:T(8,128)S(1)}) custom-call(bf16[512,128]{1,0:T(8,128)(2,1)S(1)} %get-tuple-element.50.turned_ref.refs_0_, f32[512,512]{1,0:T(8,128)S(1)} %get-tuple-element.60.refs_1_, bf16[3,512,1024]{2,1,0:T(8,128)(2,1)S(1)} %get-tuple-element.57.refs_8_.refs_2_, f32[1,1024]{1,0:T(1,128)S(1)} %get-tuple-element.59.refs_3_, ...), custom_call_target="tpu_custom_call" | custom-call | flops 536870912 | bytes 3145728 | tf_op jit(solution)/shard_map/pallas_call | solution.py:375
  23.2 0.4 %collective-permute-done.10.refs_5_ = bf16[256,512]{1,0:T(8,128)(2,1)S(1)} collective-permute-done((bf16[256,512]{1,0:T(8,128)(2,1)S(1)}, bf16[256,512]{1,0:T(8,128)(2,1)S(1)}, u32[]{:S(2)}, u32[]{:S(2)}) %collective-permute-start.10) | collective-permute-done | bytes 262176 | tf_op jit(solution)/shard_map/ppermute | solution.py:391
  23.6 0.7 %shard_map.100 = (f32[512,512]{1,0:T(8,128)S(1)}, f32[1,512]{1,0:T(1,128)S(1)}) custom-call(bf16[512,128]{1,0:T(8,128)(2,1)S(1)} %get-tuple-element.50.turned_ref.refs_0_, f32[512,512]{1,0:T(8,128)S(1)} %shard_map.98.refs_1_, bf16[3,512,1024]{2,1,0:T(8,128)(2,1)S(1)} %get-tuple-element.57.refs_8_.refs_2_, f32[1,1024]{1,0:T(1,128)S(1)} %get-tuple-element.59.refs_3_, ...), custom_call_target="tpu_custom_call" | custom-call | flops 536870912 | bytes 3145728 | tf_op jit(solution)/shard_map/pallas_call | solution.py:375
  24.3 0.7 %collective-permute-start.11 = (f32[1,512]{1,0:T(1,128)S(1)}, f32[1,512]{1,0:T(1,128)S(1)}, u32[]{:S(2)}, u32[]{:S(2)}) collective-permute-start(f32[1,512]{1,0:T(1,128)S(1)} %get-tuple-element.62.refs_0_), channel_id=1, source_target_pairs={{0,1},{1,2},{2,3},{3,0},{4,5},{5,6},{6,7},{7,4},{8,9},{9,10},{10,1... | collective-permute-start | bytes 6152 | tf_op jit(solution)/shard_map/ppermute | solution.py:400
  25.0 1.6 %collective-permute-start.12 = (f32[1,512]{1,0:T(1,128)S(1)}, f32[1,512]{1,0:T(1,128)S(1)}, u32[]{:S(2)}, u32[]{:S(2)}) collective-permute-start(f32[1,512]{1,0:T(1,128)S(1)} %get-tuple-element.62.refs_0_), channel_id=1, source_target_pairs={{0,2},{1,3},{2,0},{3,1},{4,6},{5,7},{6,4},{7,5},{8,10},{9,11},{10,... | collective-permute-start | bytes 6152 | tf_op jit(solution)/shard_map/ppermute | solution.py:400
  26.6 1.5 %collective-permute-start.13 = (f32[1,512]{1,0:T(1,128)S(1)}, f32[1,512]{1,0:T(1,128)S(1)}, u32[]{:S(2)}, u32[]{:S(2)}) collective-permute-start(f32[1,512]{1,0:T(1,128)S(1)} %get-tuple-element.62.refs_0_), channel_id=1, source_target_pairs={{0,3},{1,0},{2,1},{3,2},{4,7},{5,4},{6,5},{7,6},{8,11},{9,8},{10,9... | collective-permute-start | bytes 6152 | tf_op jit(solution)/shard_map/ppermute | solution.py:400
  28.1 1.6 %collective-permute-done.11.refs_1_ = f32[1,512]{1,0:T(1,128)S(1)} collective-permute-done((f32[1,512]{1,0:T(1,128)S(1)}, f32[1,512]{1,0:T(1,128)S(1)}, u32[]{:S(2)}, u32[]{:S(2)}) %collective-permute-start.11) | collective-permute-done | bytes 2080 | tf_op jit(solution)/shard_map/ppermute | solution.py:400
  29.7 0.6 %collective-permute-done.13.refs_3_ = f32[1,512]{1,0:T(1,128)S(1)} collective-permute-done((f32[1,512]{1,0:T(1,128)S(1)}, f32[1,512]{1,0:T(1,128)S(1)}, u32[]{:S(2)}, u32[]{:S(2)}) %collective-permute-start.13) | collective-permute-done | bytes 2080 | tf_op jit(solution)/shard_map/ppermute | solution.py:400
  30.2 1.3 %shard_map.101 = bf16[512,1024]{1,0:T(8,128)(2,1)} custom-call(f32[1,512]{1,0:T(1,128)S(1)} %get-tuple-element.62.refs_0_, f32[1,512]{1,0:T(1,128)S(1)} %collective-permute-done.11.refs_1_, f32[1,512]{1,0:T(1,128)S(1)} %collective-permute-done.12.refs_2_, f32[1,512]{1,0:T(1,128)S(1)} %collective-permute-done.13.refs_3_, ...), custom_call_target="tpu_custom_call" | custom-call | flops 268435456 | bytes 3145728 | tf_op jit(solution)/shard_map/pallas_call | solution.py:375
  (7 shorter events, 0.0 us)
Async XLA Ops:
  0.0 10.2 %collective-permute-start = (bf16[32,512]{1,0:T(8,128)(2,1)}, bf16[32,512]{1,0:T(8,128)(2,1)S(1)}, u32[]{:S(2)}, u32[]{:S(2)}) collective-permute-start(bf16[32,512]{1,0:T(8,128)(2,1)} %refs_6_.1), channel_id=1, source_target_pairs={{0,2},{1,3},{2,0},{3,1},{4,6},{5,7},{6,4},{7,5},{8,10},{9,11},{10,... | collective-permute-start | bytes 98312 | tf_op jit(solution)/shard_map/ppermute | solution.py:391
  4.0 6.2 %collective-permute-start.1 = (bf16[32,512]{1,0:T(8,128)(2,1)}, bf16[32,512]{1,0:T(8,128)(2,1)S(1)}, u32[]{:S(2)}, u32[]{:S(2)}) collective-permute-start(bf16[32,512]{1,0:T(8,128)(2,1)} %refs_6_.1), channel_id=1, source_target_pairs={{0,3},{1,2},{2,1},{3,0},{4,7},{5,6},{6,5},{7,4},{8,11},{9,10},{10,... | collective-permute-start | bytes 98312 | tf_op jit(solution)/shard_map/ppermute | solution.py:391
  5.4 4.9 %collective-permute-start.2 = (bf16[32,512]{1,0:T(8,128)(2,1)}, bf16[32,512]{1,0:T(8,128)(2,1)S(1)}, u32[]{:S(2)}, u32[]{:S(2)}) collective-permute-start(bf16[32,512]{1,0:T(8,128)(2,1)} %refs_6_.1), channel_id=1, source_target_pairs={{0,1},{1,0},{2,3},{3,2},{4,5},{5,4},{6,7},{7,6},{8,9},{9,8},{10,11... | collective-permute-start | bytes 98312 | tf_op jit(solution)/shard_map/ppermute | solution.py:391
  5.6 5.1 %collective-permute-start.3 = (bf16[32,512]{1,0:T(8,128)(2,1)}, bf16[32,512]{1,0:T(8,128)(2,1)S(1)}, u32[]{:S(2)}, u32[]{:S(2)}) collective-permute-start(bf16[32,512]{1,0:T(8,128)(2,1)} %refs_7_.1), channel_id=1, source_target_pairs={{0,2},{1,3},{2,0},{3,1},{4,6},{5,7},{6,4},{7,5},{8,10},{9,11},{10,... | collective-permute-start | bytes 98312 | tf_op jit(solution)/shard_map/ppermute | solution.py:391
  10.6 1.4 %collective-permute-start.5 = (bf16[136,512]{1,0:T(8,128)(2,1)S(1)}, bf16[136,512]{1,0:T(8,128)(2,1)S(1)}, u32[]{:S(2)}, u32[]{:S(2)}) collective-permute-start(bf16[136,512]{1,0:T(8,128)(2,1)S(1)} %get-tuple-element.44), channel_id=1, source_target_pairs={{0,4},{4,0},{8,12},{12,8},{16,20},{20,16},{24,28},{28,24},{1,5},{5... | collective-permute-start | bytes 417800 | tf_op jit(solution)/shard_map/ppermute | solution.py:391
  12.1 8.8 %collective-permute-start.6 = (bf16[136,512]{1,0:T(8,128)(2,1)S(1)}, bf16[136,512]{1,0:T(8,128)(2,1)S(1)}, u32[]{:S(2)}, u32[]{:S(2)}) collective-permute-start(bf16[136,512]{1,0:T(8,128)(2,1)S(1)} %shard_map.94.refs_5_), channel_id=1, source_target_pairs={{0,24},{4,28},{8,16},{12,20},{16,8},{20,12},{24,0},{28,4},{1,25},{... | collective-permute-start | bytes 417800 | tf_op jit(solution)/shard_map/ppermute | solution.py:391
  14.6 7.2 %collective-permute-start.7 = (bf16[136,512]{1,0:T(8,128)(2,1)S(1)}, bf16[136,512]{1,0:T(8,128)(2,1)S(1)}, u32[]{:S(2)}, u32[]{:S(2)}) collective-permute-start(bf16[136,512]{1,0:T(8,128)(2,1)S(1)} %shard_map.94.refs_5_), channel_id=1, source_target_pairs={{0,16},{4,20},{8,24},{12,28},{16,0},{20,4},{24,8},{28,12},{1,17},{... | collective-permute-start | bytes 417800 | tf_op jit(solution)/shard_map/ppermute | solution.py:391
  15.1 6.7 %collective-permute-start.8 = (bf16[136,512]{1,0:T(8,128)(2,1)S(1)}, bf16[136,512]{1,0:T(8,128)(2,1)S(1)}, u32[]{:S(2)}, u32[]{:S(2)}) collective-permute-start(bf16[136,512]{1,0:T(8,128)(2,1)S(1)} %shard_map.94.refs_5_), channel_id=1, source_target_pairs={{0,8},{4,12},{8,0},{12,4},{16,24},{20,28},{24,16},{28,20},{1,9},{5... | collective-permute-start | bytes 417800 | tf_op jit(solution)/shard_map/ppermute | solution.py:391
  15.7 6.2 %collective-permute-start.9 = (bf16[136,512]{1,0:T(8,128)(2,1)S(1)}, bf16[136,512]{1,0:T(8,128)(2,1)S(1)}, u32[]{:S(2)}, u32[]{:S(2)}) collective-permute-start(bf16[136,512]{1,0:T(8,128)(2,1)S(1)} %get-tuple-element.52._.mine_ref), channel_id=1, source_target_pairs={{0,4},{4,0},{8,12},{12,8},{16,20},{20,16},{24,28},{28,24},{1,5},{5... | collective-permute-start | bytes 417800 | tf_op jit(solution)/shard_map/ppermute | solution.py:391
  15.7 4.5 %collective-permute-start.4 = (bf16[64,512]{1,0:T(8,128)(2,1)S(1)}, bf16[64,512]{1,0:T(8,128)(2,1)S(1)}, u32[]{:S(2)}, u32[]{:S(2)}) collective-permute-start(bf16[64,512]{1,0:T(8,128)(2,1)S(1)} %shard_map.93._.refs_4_), channel_id=1, source_target_pairs={{0,1},{1,0},{2,3},{3,2},{4,5},{5,4},{6,7},{7,6},{8,9},{9,8},{10,11... | collective-permute-start | bytes 196616 | tf_op jit(solution)/shard_map/ppermute | solution.py:391
  22.0 1.6 %collective-permute-start.10 = (bf16[256,512]{1,0:T(8,128)(2,1)S(1)}, bf16[256,512]{1,0:T(8,128)(2,1)S(1)}, u32[]{:S(2)}, u32[]{:S(2)}) collective-permute-start(bf16[256,512]{1,0:T(8,128)(2,1)S(1)} %shard_map.97._.refs_5_), channel_id=1, source_target_pairs={{0,4},{4,0},{8,12},{12,8},{16,20},{20,16},{24,28},{28,24},{1,5},{5... | collective-permute-start | bytes 786440 | tf_op jit(solution)/shard_map/ppermute | solution.py:391
  24.3 5.4 %collective-permute-start.11 = (f32[1,512]{1,0:T(1,128)S(1)}, f32[1,512]{1,0:T(1,128)S(1)}, u32[]{:S(2)}, u32[]{:S(2)}) collective-permute-start(f32[1,512]{1,0:T(1,128)S(1)} %get-tuple-element.62.refs_0_), channel_id=1, source_target_pairs={{0,1},{1,2},{2,3},{3,0},{4,5},{5,6},{6,7},{7,4},{8,9},{9,10},{10,1... | collective-permute-start | bytes 6152 | tf_op jit(solution)/shard_map/ppermute | solution.py:400
  25.0 4.7 %collective-permute-start.12 = (f32[1,512]{1,0:T(1,128)S(1)}, f32[1,512]{1,0:T(1,128)S(1)}, u32[]{:S(2)}, u32[]{:S(2)}) collective-permute-start(f32[1,512]{1,0:T(1,128)S(1)} %get-tuple-element.62.refs_0_), channel_id=1, source_target_pairs={{0,2},{1,3},{2,0},{3,1},{4,6},{5,7},{6,4},{7,5},{8,10},{9,11},{10,... | collective-permute-start | bytes 6152 | tf_op jit(solution)/shard_map/ppermute | solution.py:400
  26.6 3.6 %collective-permute-start.13 = (f32[1,512]{1,0:T(1,128)S(1)}, f32[1,512]{1,0:T(1,128)S(1)}, u32[]{:S(2)}, u32[]{:S(2)}) collective-permute-start(f32[1,512]{1,0:T(1,128)S(1)} %get-tuple-element.62.refs_0_), channel_id=1, source_target_pairs={{0,3},{1,0},{2,1},{3,2},{4,7},{5,4},{6,5},{7,6},{8,11},{9,8},{10,9... | collective-permute-start | bytes 6152 | tf_op jit(solution)/shard_map/ppermute | solution.py:400

commit v16 on v15

--- a/solution.py
+++ b/solution.py
@@ -505,7 +505,7 @@
             received[::-1],
             bytes_accessed=area,
         )
-        other = flip(own, "seq", 1)
+        other = lax.ppermute(own, "seq", [(i, i ^ 1) for i in range(2, lax.axis_size("seq"))])
         near_args = base, own_factor, far, other_theirs, scaled, *span_states, *span_factors
         other_near = call(
             functools.partial(other_near_kernel, spans), near_shape, (scores, turned, own, *near_args), flops=dense

time: 31.7 us -> 32.5 us (1.025)
  the two profiles are of different devices: /device:TPU:0 before, /device:TPU:10 now
where the time goes in v16:
time: 32.5 us; the launch traced here: 32.4 us
  starting transfers between devices  16.7 us (51%)
  Pallas kernels  7.86 us (24%)
  waiting for transfers between devices  7.69 us (24%)
    ppermute x10, starting transfers between devices, flip(): lax.ppermute(array, axis, [(i, i ^ mask) for i in range(lax.axis_size(axi...  11.1 us
    pallas_call x11, Pallas kernels, call(): pl.pallas_call(kernel, out_shape=out_shape, in_specs=specs, out_specs=jax...  7.86 us
    ppermute x10, waiting for transfers between devices, flip(): lax.ppermute(array, axis, [(i, i ^ mask) for i in range(lax.axis_size(axi...  3.74 us
    ppermute x3, starting transfers between devices, around(): lax.ppermute(array, axis, [(i, (i + shift) % size) for i in range(size)])  3.73 us
    ppermute x3, waiting for transfers between devices, around(): lax.ppermute(array, axis, [(i, (i + shift) % size) for i in range(size)])  3.58 us
    ppermute x1, starting transfers between devices, on_device(): lax.ppermute(own, 'seq', [(i, i ^ 1) for i in range(2, lax.axis_size('seq...  1.92 us
  transfers between devices with their start and end apart: 14, of which 8 were waited for; matrix products, arithmetic and copies ran while one was open for 0% of the time, Pallas kernels for 18%

profile of v16, /device:TPU:10, one launch (start us, length us, event | category | flops | bytes accessed | tf_op | source)
XLA Modules:
  0.0 32.4 jit_solution(3369517004947731250)
XLA Ops:
  0.0 2.6 %collective-permute-start = (bf16[32,512]{1,0:T(8,128)(2,1)}, bf16[32,512]{1,0:T(8,128)(2,1)S(1)}, u32[]{:S(2)}, u32[]{:S(2)}) collective-permute-start(bf16[32,512]{1,0:T(8,128)(2,1)} %refs_6_.1), channel_id=1, source_target_pairs={{0,2},{1,3},{2,0},{3,1},{4,6},{5,7},{6,4},{7,5},{8,10},{9,11},{10,... | collective-permute-start | bytes 98312 | tf_op jit(solution)/shard_map/ppermute | solution.py:391
  2.6 0.0 collective-permute-start.1
  2.6 1.8 %collective-permute-start.2 = (bf16[32,512]{1,0:T(8,128)(2,1)}, bf16[32,512]{1,0:T(8,128)(2,1)S(1)}, u32[]{:S(2)}, u32[]{:S(2)}) collective-permute-start(bf16[32,512]{1,0:T(8,128)(2,1)} %refs_6_.1), channel_id=1, source_target_pairs={{0,1},{1,0},{2,3},{3,2},{4,5},{5,4},{6,7},{7,6},{8,9},{9,8},{10,11... | collective-permute-start | bytes 98312 | tf_op jit(solution)/shard_map/ppermute | solution.py:391
  4.4 1.7 %collective-permute-start.3 = (bf16[32,512]{1,0:T(8,128)(2,1)}, bf16[32,512]{1,0:T(8,128)(2,1)S(1)}, u32[]{:S(2)}, u32[]{:S(2)}) collective-permute-start(bf16[32,512]{1,0:T(8,128)(2,1)} %refs_7_.1), channel_id=1, source_target_pairs={{0,2},{1,3},{2,0},{3,1},{4,6},{5,7},{6,4},{7,5},{8,10},{9,11},{10,... | collective-permute-start | bytes 98312 | tf_op jit(solution)/shard_map/ppermute | solution.py:391
  6.1 1.8 %shard_map.91 = (bf16[512,1024]{1,0:T(8,128)(2,1)S(1)}, f32[16,512]{1,0:T(8,128)S(1)}, bf16[512,1024]{1,0:T(8,128)(2,1)S(1)}, bf16[512,1024]{1,0:T(8,128)(2,1)S(...) custom-call(f32[16,512]{1,0:T(8,128)} %refs_0_.1, ...), custom_call_target="tpu_custom_call" | custom-call | flops 4294967296 | bytes 2097152 | tf_op jit(solution)/shard_map/pallas_call | solution.py:375
  7.9 0.0 collective-permute-done.1.refs_2_
  7.9 0.0 collective-permute-done.2.refs_3_
  7.9 0.3 %shard_map.92 = (bf16[136,512]{1,0:T(8,128)(2,1)S(1)}, bf16[136,512]{1,0:T(8,128)(2,1)S(1)}, bf16[128,1024]{1,0:T(8,128)(2,1)S(1)}) custom-call(bf16[32,512]{1,0:T(8,128)(2,1)S(1)} %get-tuple-element.35.refs_0_, bf16[32,512]{1,0:T(8,128)(2,1)S(1)} %collective-permute-done.refs_1_, bf16[32,512]{1,0:T(8,128)(2,1)S(1)} %collective-permute-done.1.refs_2_, ...), custom_call_target="tpu_custom_call" | custom-call | flops 268435456 | tf_op jit(solution)/shard_map/pallas_call | solution.py:375
  8.3 0.1 collective-permute-start.5
  8.4 1.1 %collective-permute-done.3.theirs_ref = bf16[32,512]{1,0:T(8,128)(2,1)S(1)} collective-permute-done((bf16[32,512]{1,0:T(8,128)(2,1)}, bf16[32,512]{1,0:T(8,128)(2,1)S(1)}, u32[]{:S(2)}, u32[]{:S(2)}) %collective-permute-start.3) | collective-permute-done | bytes 32800 | tf_op jit(solution)/shard_map/ppermute | solution.py:391
  9.4 0.3 collective-permute-done.5.theirs_ref.refs_9_.refs_4_
  9.7 0.1 shard_map.94.refs_5_
  9.8 1.6 %collective-permute-start.6 = (bf16[136,512]{1,0:T(8,128)(2,1)S(1)}, bf16[136,512]{1,0:T(8,128)(2,1)S(1)}, u32[]{:S(2)}, u32[]{:S(2)}) collective-permute-start(bf16[136,512]{1,0:T(8,128)(2,1)S(1)} %shard_map.94.refs_5_), channel_id=1, source_target_pairs={{0,24},{4,28},{8,16},{12,20},{16,8},{20,12},{24,0},{28,4},{1,25},{... | collective-permute-start | bytes 417800 | tf_op jit(solution)/shard_map/ppermute | solution.py:391
  11.3 0.5 %collective-permute-start.7 = (bf16[136,512]{1,0:T(8,128)(2,1)S(1)}, bf16[136,512]{1,0:T(8,128)(2,1)S(1)}, u32[]{:S(2)}, u32[]{:S(2)}) collective-permute-start(bf16[136,512]{1,0:T(8,128)(2,1)S(1)} %shard_map.94.refs_5_), channel_id=1, source_target_pairs={{0,16},{4,20},{8,24},{12,28},{16,0},{20,4},{24,8},{28,12},{1,17},{... | collective-permute-start | bytes 417800 | tf_op jit(solution)/shard_map/ppermute | solution.py:391
  11.8 1.5 %collective-permute-start.8 = (bf16[136,512]{1,0:T(8,128)(2,1)S(1)}, bf16[136,512]{1,0:T(8,128)(2,1)S(1)}, u32[]{:S(2)}, u32[]{:S(2)}) collective-permute-start(bf16[136,512]{1,0:T(8,128)(2,1)S(1)} %shard_map.94.refs_5_), channel_id=1, source_target_pairs={{0,8},{4,12},{8,0},{12,4},{16,24},{20,28},{24,16},{28,20},{1,9},{5... | collective-permute-start | bytes 417800 | tf_op jit(solution)/shard_map/ppermute | solution.py:391
  13.3 1.3 %collective-permute-start.4 = (bf16[64,512]{1,0:T(8,128)(2,1)S(1)}, bf16[64,512]{1,0:T(8,128)(2,1)S(1)}, u32[]{:S(2)}, u32[]{:S(2)}) collective-permute-start(bf16[64,512]{1,0:T(8,128)(2,1)S(1)} %shard_map.93._.refs_4_), channel_id=1, source_target_pairs={{0,1},{1,0},{2,3},{3,2},{4,5},{5,4},{6,7},{7,6},{8,9},{9,8},{10,11... | collective-permute-start | bytes 196616 | tf_op jit(solution)/shard_map/ppermute | solution.py:391
  14.7 1.8 %shard_map.95 = (f32[512,1024]{1,0:T(8,128)S(1)}, f32[512,1024]{1,0:T(8,128)S(1)}, bf16[3,512,1024]{2,1,0:T(8,128)(2,1)S(1)}, bf16[1,256,1024]{2,1,0:T(8,128)(2,1)S(1)}) custom-call(bf16[512,1024]{1,0:T(8,128)(2,1)S(1)} %get-tuple-element.40.refs_0_, bf16[512,1024]{1,0:T(8,128)(2,1)S(1)} %get-tuple-element.41.refs_1_, ...), custom_call_target="tpu_custom_call" | custom-call | flops 1342177280 | tf_op jit(solution)/shard_map/pallas_call | solution.py:375
  16.5 1.4 %collective-permute-done.4.refs_5_ = bf16[64,512]{1,0:T(8,128)(2,1)S(1)} collective-permute-done((bf16[64,512]{1,0:T(8,128)(2,1)S(1)}, bf16[64,512]{1,0:T(8,128)(2,1)S(1)}, u32[]{:S(2)}, u32[]{:S(2)}) %collective-permute-start.4) | collective-permute-done | bytes 65568 | tf_op jit(solution)/shard_map/ppermute | solution.py:391
  17.8 0.7 %shard_map.96 = (f32[512,512]{1,0:T(8,128)S(1)}, bf16[512,128]{1,0:T(8,128)(2,1)S(1)}, bf16[512,256]{1,0:T(8,128)(2,1)S(1)}) custom-call(bf16[32,512]{1,0:T(8,128)(2,1)S(1)} %get-tuple-element.35.refs_0_, bf16[32,512]{1,0:T(8,128)(2,1)S(1)} %collective-permute-done.refs_1_, bf16[32,512]{1,0:T(8,128)(2,1)S(1)} %collective-permute-done.1.refs_2_, ...), custom_call_target="tpu_custom_call" | custom-call | tf_op jit(solution)/shard_map/pallas_call | solution.py:375
  18.5 0.9 %collective-permute-done.7.y_ref = bf16[136,512]{1,0:T(8,128)(2,1)S(1)} collective-permute-done((bf16[136,512]{1,0:T(8,128)(2,1)S(1)}, bf16[136,512]{1,0:T(8,128)(2,1)S(1)}, u32[]{:S(2)}, u32[]{:S(2)}) %collective-permute-start.7) | collective-permute-done | bytes 139296 | tf_op jit(solution)/shard_map/ppermute | solution.py:391
  19.4 0.1 collective-permute-done.8.x_ref
  19.5 0.1 shard_map.97._.refs_5_
  19.7 1.9 %collective-permute-start.10 = (bf16[256,512]{1,0:T(8,128)(2,1)S(1)}, bf16[256,512]{1,0:T(8,128)(2,1)S(1)}, u32[]{:S(2)}, u32[]{:S(2)}) collective-permute-start(bf16[256,512]{1,0:T(8,128)(2,1)S(1)} %shard_map.97._.refs_5_), channel_id=1, source_target_pairs={{8,12},{12,8},{16,20},{20,16},{24,28},{28,24},{9,13},{13,9},{17,21... | collective-permute-start | bytes 786440 | tf_op jit(solution)/shard_map/ppermute | solution.py:508
  21.6 0.6 %shard_map.98.refs_1_ = f32[512,512]{1,0:T(8,128)S(1)} custom-call(bf16[512,256]{1,0:T(8,128)(2,1)S(1)} %get-tuple-element.51.scores_ref, bf16[512,128]{1,0:T(8,128)(2,1)S(1)} %get-tuple-element.50.turned_ref.refs_0_, bf16[256,512]{1,0:T(8,128)(2,1)S(1)} %shard_map.97._.refs_5_, f32[512,1024]{1,0:T(8,128)S(1)} %get-tuple-element.45.refs_6_.refs_0_, ...), custom_call_target="tpu_custom_call" | custom-call | flops 268435456 | tf_op jit(solution)/shard_map/pallas_call | solution.py:375
  22.2 0.5 %shard_map.99 = (f32[512,512]{1,0:T(8,128)S(1)}, f32[512,128]{1,0:T(8,128)S(1)}) custom-call(bf16[512,128]{1,0:T(8,128)(2,1)S(1)} %get-tuple-element.50.turned_ref.refs_0_, f32[512,512]{1,0:T(8,128)S(1)} %get-tuple-element.60.refs_1_, bf16[3,512,1024]{2,1,0:T(8,128)(2,1)S(1)} %get-tuple-element.57.refs_8_.refs_2_, f32[1,1024]{1,0:T(1,128)S(1)} %get-tuple-element.59.refs_3_, ...), custom_call_target="tpu_custom_call" | custom-call | flops 536870912 | bytes 3145728 | tf_op jit(solution)/shard_map/pallas_call | solution.py:375
  22.7 0.4 %collective-permute-done.10.refs_5_ = bf16[256,512]{1,0:T(8,128)(2,1)S(1)} collective-permute-done((bf16[256,512]{1,0:T(8,128)(2,1)S(1)}, bf16[256,512]{1,0:T(8,128)(2,1)S(1)}, u32[]{:S(2)}, u32[]{:S(2)}) %collective-permute-start.10) | collective-permute-done | bytes 262176 | tf_op jit(solution)/shard_map/ppermute | solution.py:508
  23.1 0.7 %shard_map.100 = (f32[512,512]{1,0:T(8,128)S(1)}, f32[1,512]{1,0:T(1,128)S(1)}) custom-call(bf16[512,128]{1,0:T(8,128)(2,1)S(1)} %get-tuple-element.50.turned_ref.refs_0_, f32[512,512]{1,0:T(8,128)S(1)} %shard_map.98.refs_1_, bf16[3,512,1024]{2,1,0:T(8,128)(2,1)S(1)} %get-tuple-element.57.refs_8_.refs_2_, f32[1,1024]{1,0:T(1,128)S(1)} %get-tuple-element.59.refs_3_, ...), custom_call_target="tpu_custom_call" | custom-call | flops 536870912 | bytes 3145728 | tf_op jit(solution)/shard_map/pallas_call | solution.py:375
  23.8 0.8 %collective-permute-start.11 = (f32[1,512]{1,0:T(1,128)S(1)}, f32[1,512]{1,0:T(1,128)S(1)}, u32[]{:S(2)}, u32[]{:S(2)}) collective-permute-start(f32[1,512]{1,0:T(1,128)S(1)} %get-tuple-element.62.refs_0_), channel_id=1, source_target_pairs={{0,1},{1,2},{2,3},{3,0},{4,5},{5,6},{6,7},{7,4},{8,9},{9,10},{10,1... | collective-permute-start | bytes 6152 | tf_op jit(solution)/shard_map/ppermute | solution.py:400
  24.6 2.9 %collective-permute-start.12 = (f32[1,512]{1,0:T(1,128)S(1)}, f32[1,512]{1,0:T(1,128)S(1)}, u32[]{:S(2)}, u32[]{:S(2)}) collective-permute-start(f32[1,512]{1,0:T(1,128)S(1)} %get-tuple-element.62.refs_0_), channel_id=1, source_target_pairs={{0,2},{1,3},{2,0},{3,1},{4,6},{5,7},{6,4},{7,5},{8,10},{9,11},{10,... | collective-permute-start | bytes 6152 | tf_op jit(solution)/shard_map/ppermute | solution.py:400
  27.5 1.6 %collective-permute-done.12.refs_2_ = f32[1,512]{1,0:T(1,128)S(1)} collective-permute-done((f32[1,512]{1,0:T(1,128)S(1)}, f32[1,512]{1,0:T(1,128)S(1)}, u32[]{:S(2)}, u32[]{:S(2)}) %collective-permute-start.12) | collective-permute-done | bytes 2080 | tf_op jit(solution)/shard_map/ppermute | solution.py:400
  29.1 2.0 %collective-permute-done.13.refs_3_ = f32[1,512]{1,0:T(1,128)S(1)} collective-permute-done((f32[1,512]{1,0:T(1,128)S(1)}, f32[1,512]{1,0:T(1,128)S(1)}, u32[]{:S(2)}, u32[]{:S(2)}) %collective-permute-start.13) | collective-permute-done | bytes 2080 | tf_op jit(solution)/shard_map/ppermute | solution.py:400
  31.1 1.3 %shard_map.101 = bf16[512,1024]{1,0:T(8,128)(2,1)} custom-call(f32[1,512]{1,0:T(1,128)S(1)} %get-tuple-element.62.refs_0_, f32[1,512]{1,0:T(1,128)S(1)} %collective-permute-done.11.refs_1_, f32[1,512]{1,0:T(1,128)S(1)} %collective-permute-done.12.refs_2_, f32[1,512]{1,0:T(1,128)S(1)} %collective-permute-done.13.refs_3_, ...), custom_call_target="tpu_custom_call" | custom-call | flops 268435456 | bytes 3145728 | tf_op jit(solution)/shard_map/pallas_call | solution.py:375
  (7 shorter events, 0.0 us)
Async XLA Ops:
  0.0 7.9 %collective-permute-start = (bf16[32,512]{1,0:T(8,128)(2,1)}, bf16[32,512]{1,0:T(8,128)(2,1)S(1)}, u32[]{:S(2)}, u32[]{:S(2)}) collective-permute-start(bf16[32,512]{1,0:T(8,128)(2,1)} %refs_6_.1), channel_id=1, source_target_pairs={{0,2},{1,3},{2,0},{3,1},{4,6},{5,7},{6,4},{7,5},{8,10},{9,11},{10,... | collective-permute-start | bytes 98312 | tf_op jit(solution)/shard_map/ppermute | solution.py:391
  2.6 5.3 %collective-permute-start.1 = (bf16[32,512]{1,0:T(8,128)(2,1)}, bf16[32,512]{1,0:T(8,128)(2,1)S(1)}, u32[]{:S(2)}, u32[]{:S(2)}) collective-permute-start(bf16[32,512]{1,0:T(8,128)(2,1)} %refs_6_.1), channel_id=1, source_target_pairs={{0,3},{1,2},{2,1},{3,0},{4,7},{5,6},{6,5},{7,4},{8,11},{9,10},{10,... | collective-permute-start | bytes 98312 | tf_op jit(solution)/shard_map/ppermute | solution.py:391
  2.6 5.3 %collective-permute-start.2 = (bf16[32,512]{1,0:T(8,128)(2,1)}, bf16[32,512]{1,0:T(8,128)(2,1)S(1)}, u32[]{:S(2)}, u32[]{:S(2)}) collective-permute-start(bf16[32,512]{1,0:T(8,128)(2,1)} %refs_6_.1), channel_id=1, source_target_pairs={{0,1},{1,0},{2,3},{3,2},{4,5},{5,4},{6,7},{7,6},{8,9},{9,8},{10,11... | collective-permute-start | bytes 98312 | tf_op jit(solution)/shard_map/ppermute | solution.py:391
  4.4 5.0 %collective-permute-start.3 = (bf16[32,512]{1,0:T(8,128)(2,1)}, bf16[32,512]{1,0:T(8,128)(2,1)S(1)}, u32[]{:S(2)}, u32[]{:S(2)}) collective-permute-start(bf16[32,512]{1,0:T(8,128)(2,1)} %refs_7_.1), channel_id=1, source_target_pairs={{0,2},{1,3},{2,0},{3,1},{4,6},{5,7},{6,4},{7,5},{8,10},{9,11},{10,... | collective-permute-start | bytes 98312 | tf_op jit(solution)/shard_map/ppermute | solution.py:391
  8.3 1.4 %collective-permute-start.5 = (bf16[136,512]{1,0:T(8,128)(2,1)S(1)}, bf16[136,512]{1,0:T(8,128)(2,1)S(1)}, u32[]{:S(2)}, u32[]{:S(2)}) collective-permute-start(bf16[136,512]{1,0:T(8,128)(2,1)S(1)} %get-tuple-element.44), channel_id=1, source_target_pairs={{0,4},{4,0},{8,12},{12,8},{16,20},{20,16},{24,28},{28,24},{1,5},{5... | collective-permute-start | bytes 417800 | tf_op jit(solution)/shard_map/ppermute | solution.py:391
  9.8 8.8 %collective-permute-start.6 = (bf16[136,512]{1,0:T(8,128)(2,1)S(1)}, bf16[136,512]{1,0:T(8,128)(2,1)S(1)}, u32[]{:S(2)}, u32[]{:S(2)}) collective-permute-start(bf16[136,512]{1,0:T(8,128)(2,1)S(1)} %shard_map.94.refs_5_), channel_id=1, source_target_pairs={{0,24},{4,28},{8,16},{12,20},{16,8},{20,12},{24,0},{28,4},{1,25},{... | collective-permute-start | bytes 417800 | tf_op jit(solution)/shard_map/ppermute | solution.py:391
  11.3 8.1 %collective-permute-start.7 = (bf16[136,512]{1,0:T(8,128)(2,1)S(1)}, bf16[136,512]{1,0:T(8,128)(2,1)S(1)}, u32[]{:S(2)}, u32[]{:S(2)}) collective-permute-start(bf16[136,512]{1,0:T(8,128)(2,1)S(1)} %shard_map.94.refs_5_), channel_id=1, source_target_pairs={{0,16},{4,20},{8,24},{12,28},{16,0},{20,4},{24,8},{28,12},{1,17},{... | collective-permute-start | bytes 417800 | tf_op jit(solution)/shard_map/ppermute | solution.py:391
  11.8 7.7 %collective-permute-start.8 = (bf16[136,512]{1,0:T(8,128)(2,1)S(1)}, bf16[136,512]{1,0:T(8,128)(2,1)S(1)}, u32[]{:S(2)}, u32[]{:S(2)}) collective-permute-start(bf16[136,512]{1,0:T(8,128)(2,1)S(1)} %shard_map.94.refs_5_), channel_id=1, source_target_pairs={{0,8},{4,12},{8,0},{12,4},{16,24},{20,28},{24,16},{28,20},{1,9},{5... | collective-permute-start | bytes 417800 | tf_op jit(solution)/shard_map/ppermute | solution.py:391
  13.3 6.2 %collective-permute-start.9 = (bf16[136,512]{1,0:T(8,128)(2,1)S(1)}, bf16[136,512]{1,0:T(8,128)(2,1)S(1)}, u32[]{:S(2)}, u32[]{:S(2)}) collective-permute-start(bf16[136,512]{1,0:T(8,128)(2,1)S(1)} %get-tuple-element.52._.mine_ref), channel_id=1, source_target_pairs={{0,4},{4,0},{8,12},{12,8},{16,20},{20,16},{24,28},{28,24},{1,5},{5... | collective-permute-start | bytes 417800 | tf_op jit(solution)/shard_map/ppermute | solution.py:391
  13.3 4.5 %collective-permute-start.4 = (bf16[64,512]{1,0:T(8,128)(2,1)S(1)}, bf16[64,512]{1,0:T(8,128)(2,1)S(1)}, u32[]{:S(2)}, u32[]{:S(2)}) collective-permute-start(bf16[64,512]{1,0:T(8,128)(2,1)S(1)} %shard_map.93._.refs_4_), channel_id=1, source_target_pairs={{0,1},{1,0},{2,3},{3,2},{4,5},{5,4},{6,7},{7,6},{8,9},{9,8},{10,11... | collective-permute-start | bytes 196616 | tf_op jit(solution)/shard_map/ppermute | solution.py:391
  19.7 3.4 %collective-permute-start.10 = (bf16[256,512]{1,0:T(8,128)(2,1)S(1)}, bf16[256,512]{1,0:T(8,128)(2,1)S(1)}, u32[]{:S(2)}, u32[]{:S(2)}) collective-permute-start(bf16[256,512]{1,0:T(8,128)(2,1)S(1)} %shard_map.97._.refs_5_), channel_id=1, source_target_pairs={{8,12},{12,8},{16,20},{20,16},{24,28},{28,24},{9,13},{13,9},{17,21... | collective-permute-start | bytes 786440 | tf_op jit(solution)/shard_map/ppermute | solution.py:508
  23.8 3.7 %collective-permute-start.11 = (f32[1,512]{1,0:T(1,128)S(1)}, f32[1,512]{1,0:T(1,128)S(1)}, u32[]{:S(2)}, u32[]{:S(2)}) collective-permute-start(f32[1,512]{1,0:T(1,128)S(1)} %get-tuple-element.62.refs_0_), channel_id=1, source_target_pairs={{0,1},{1,2},{2,3},{3,0},{4,5},{5,6},{6,7},{7,4},{8,9},{9,10},{10,1... | collective-permute-start | bytes 6152 | tf_op jit(solution)/shard_map/ppermute | solution.py:400
  24.6 4.5 %collective-permute-start.12 = (f32[1,512]{1,0:T(1,128)S(1)}, f32[1,512]{1,0:T(1,128)S(1)}, u32[]{:S(2)}, u32[]{:S(2)}) collective-permute-start(f32[1,512]{1,0:T(1,128)S(1)} %get-tuple-element.62.refs_0_), channel_id=1, source_target_pairs={{0,2},{1,3},{2,0},{3,1},{4,6},{5,7},{6,4},{7,5},{8,10},{9,11},{10,... | collective-permute-start | bytes 6152 | tf_op jit(solution)/shard_map/ppermute | solution.py:400
  27.5 3.6 %collective-permute-start.13 = (f32[1,512]{1,0:T(1,128)S(1)}, f32[1,512]{1,0:T(1,128)S(1)}, u32[]{:S(2)}, u32[]{:S(2)}) collective-permute-start(f32[1,512]{1,0:T(1,128)S(1)} %get-tuple-element.62.refs_0_), channel_id=1, source_target_pairs={{0,3},{1,0},{2,1},{3,2},{4,7},{5,4},{6,5},{7,6},{8,11},{9,8},{10,9... | collective-permute-start | bytes 6152 | tf_op jit(solution)/shard_map/ppermute | solution.py:400

commit v17 on v16

--- a/solution.py
+++ b/solution.py
@@ -255,7 +255,7 @@
     near_body(spans, paired, start, scores_ref, turned_ref, rest, near_ref)
 
 
-def other_near_kernel(spans, scores_ref, turned_ref, _, *refs):
+def other_near_kernel(spans, scores_ref, turned_ref, *refs):
     near_ref = refs[-1]
     start = (1 - lax.rem(lax.axis_index("seq"), 2)) * near_ref.shape[1]
     near_body(spans, True, start, scores_ref, turned_ref, refs[:-1], near_ref)
@@ -498,18 +498,19 @@
     sums_shape = shaped((1, tokens), f32)
     if pairs:
         received = [flip(message, "seq", mask) for mask in (6, 4, 2)]
-        *received, other_theirs, near, far = lax.optimization_barrier((*received, other_theirs, near, far))
+        near_args = base, own_factor, far, other_theirs, scaled, *span_states, *span_factors
+        other_near = call(
+            functools.partial(other_near_kernel, spans), near_shape, (scores, turned, *near_args), flops=0
+        )
+        *received, near, far, other_near = lax.optimization_barrier((*received, near, far, other_near))
         own = call(
             functools.partial(combine_kernel, size),
             shaped((2 * size, width // 2), bf16),
             received[::-1],
             bytes_accessed=area,
         )
-        other = lax.ppermute(own, "seq", [(i, i ^ 1) for i in range(2, lax.axis_size("seq"))])
+        other = lax.ppermute(own, "seq", [(i, i ^ 1 if i >= 2 else i) for i in range(lax.axis_size("seq"))])
         near_args = base, own_factor, far, other_theirs, scaled, *span_states, *span_factors
-        other_near = call(
-            functools.partial(other_near_kernel, spans), near_shape, (scores, turned, own, *near_args), flops=dense
-        )
         gated_shape = shaped((tokens, width // 2), f32)
         own_gated, own_squares = call(
             functools.partial(far_kernel_of_half, True),

time: 32.5 us -> 32.9 us (1.012)
    ppermute x1, waiting for transfers between devices: 0.37 us -> 0.98 us  [on_device(): lax.ppermute(own, 'seq', [(i, i ^ 1 if i >= 2 else i) for i in range(lax....]
    ppermute x10, waiting for transfers between devices: 3.74 us -> 3.35 us  [flip(): lax.ppermute(array, axis, [(i, i ^ mask) for i in range(lax.axis_size(axi...]
  transfers between devices with their start and end apart: 14 -> 14, of which waited for: 8 -> 8; matrix products, arithmetic and copies ran while one was open for 0% -> 0% of each run, Pallas kernels for 18% -> 17%
where the time goes in v17:
time: 32.9 us; the launch traced here: 32.7 us
  starting transfers between devices  16.9 us (51%)
  waiting for transfers between devices  7.91 us (24%)
  Pallas kernels  7.84 us (24%)
    ppermute x10, starting transfers between devices, flip(): lax.ppermute(array, axis, [(i, i ^ mask) for i in range(lax.axis_size(axi...  11.2 us
    pallas_call x11, Pallas kernels, call(): pl.pallas_call(kernel, out_shape=out_shape, in_specs=specs, out_specs=jax...  7.84 us
    ppermute x3, starting transfers between devices, around(): lax.ppermute(array, axis, [(i, (i + shift) % size) for i in range(size)])  3.73 us
    ppermute x3, waiting for transfers between devices, around(): lax.ppermute(array, axis, [(i, (i + shift) % size) for i in range(size)])  3.58 us
    ppermute x10, waiting for transfers between devices, flip(): lax.ppermute(array, axis, [(i, i ^ mask) for i in range(lax.axis_size(axi...  3.35 us
    ppermute x1, starting transfers between devices, on_device(): lax.ppermute(own, 'seq', [(i, i ^ 1 if i >= 2 else i) for i in range(lax....  1.92 us
    ppermute x1, waiting for transfers between devices, on_device(): lax.ppermute(own, 'seq', [(i, i ^ 1 if i >= 2 else i) for i in range(lax....  0.98 us
  transfers between devices with their start and end apart: 14, of which 8 were waited for; matrix products, arithmetic and copies ran while one was open for 0% of the time, Pallas kernels for 17%

profile of v17, /device:TPU:10, one launch (start us, length us, event | category | flops | bytes accessed | tf_op | source)
XLA Modules:
  0.0 32.7 jit_solution(11495364601419968712)
XLA Ops:
  0.0 2.6 %collective-permute-start = (bf16[32,512]{1,0:T(8,128)(2,1)}, bf16[32,512]{1,0:T(8,128)(2,1)S(1)}, u32[]{:S(2)}, u32[]{:S(2)}) collective-permute-start(bf16[32,512]{1,0:T(8,128)(2,1)} %refs_6_.1), channel_id=1, source_target_pairs={{0,2},{1,3},{2,0},{3,1},{4,6},{5,7},{6,4},{7,5},{8,10},{9,11},{10,... | collective-permute-start | bytes 98312 | tf_op jit(solution)/shard_map/ppermute | solution.py:391
  2.6 0.0 collective-permute-start.1
  2.6 1.8 %collective-permute-start.2 = (bf16[32,512]{1,0:T(8,128)(2,1)}, bf16[32,512]{1,0:T(8,128)(2,1)S(1)}, u32[]{:S(2)}, u32[]{:S(2)}) collective-permute-start(bf16[32,512]{1,0:T(8,128)(2,1)} %refs_6_.1), channel_id=1, source_target_pairs={{0,1},{1,0},{2,3},{3,2},{4,5},{5,4},{6,7},{7,6},{8,9},{9,8},{10,11... | collective-permute-start | bytes 98312 | tf_op jit(solution)/shard_map/ppermute | solution.py:391
  4.4 1.7 %collective-permute-start.3 = (bf16[32,512]{1,0:T(8,128)(2,1)}, bf16[32,512]{1,0:T(8,128)(2,1)S(1)}, u32[]{:S(2)}, u32[]{:S(2)}) collective-permute-start(bf16[32,512]{1,0:T(8,128)(2,1)} %refs_7_.1), channel_id=1, source_target_pairs={{0,2},{1,3},{2,0},{3,1},{4,6},{5,7},{6,4},{7,5},{8,10},{9,11},{10,... | collective-permute-start | bytes 98312 | tf_op jit(solution)/shard_map/ppermute | solution.py:391
  6.1 1.8 %shard_map.91 = (bf16[512,1024]{1,0:T(8,128)(2,1)S(1)}, f32[16,512]{1,0:T(8,128)S(1)}, bf16[512,1024]{1,0:T(8,128)(2,1)S(1)}, bf16[512,1024]{1,0:T(8,128)(2,1)S(...) custom-call(f32[16,512]{1,0:T(8,128)} %refs_0_.1, ...), custom_call_target="tpu_custom_call" | custom-call | flops 4294967296 | bytes 2097152 | tf_op jit(solution)/shard_map/pallas_call | solution.py:375
  7.9 0.0 collective-permute-done.1.refs_2_
  7.9 0.3 %shard_map.92 = (bf16[136,512]{1,0:T(8,128)(2,1)S(1)}, bf16[136,512]{1,0:T(8,128)(2,1)S(1)}, bf16[128,1024]{1,0:T(8,128)(2,1)S(1)}) custom-call(bf16[32,512]{1,0:T(8,128)(2,1)S(1)} %get-tuple-element.35.refs_0_, bf16[32,512]{1,0:T(8,128)(2,1)S(1)} %collective-permute-done.refs_1_, bf16[32,512]{1,0:T(8,128)(2,1)S(1)} %collective-permute-done.1.refs_2_, ...), custom_call_target="tpu_custom_call" | custom-call | flops 268435456 | tf_op jit(solution)/shard_map/pallas_call | solution.py:375
  8.3 0.1 collective-permute-start.5
  8.4 1.1 %collective-permute-done.3.theirs_ref = bf16[32,512]{1,0:T(8,128)(2,1)S(1)} collective-permute-done((bf16[32,512]{1,0:T(8,128)(2,1)}, bf16[32,512]{1,0:T(8,128)(2,1)S(1)}, u32[]{:S(2)}, u32[]{:S(2)}) %collective-permute-start.3) | collective-permute-done | bytes 32800 | tf_op jit(solution)/shard_map/ppermute | solution.py:391
  9.4 0.3 collective-permute-done.5.theirs_ref.refs_9_.refs_4_
  9.7 0.1 shard_map.94.refs_5_
  9.8 0.2 collective-permute-start.9
  10.0 1.5 %collective-permute-start.6 = (bf16[136,512]{1,0:T(8,128)(2,1)S(1)}, bf16[136,512]{1,0:T(8,128)(2,1)S(1)}, u32[]{:S(2)}, u32[]{:S(2)}) collective-permute-start(bf16[136,512]{1,0:T(8,128)(2,1)S(1)} %shard_map.94.refs_5_), channel_id=1, source_target_pairs={{0,24},{4,28},{8,16},{12,20},{16,8},{20,12},{24,0},{28,4},{1,25},{... | collective-permute-start | bytes 417800 | tf_op jit(solution)/shard_map/ppermute | solution.py:391
  11.5 0.5 %collective-permute-start.7 = (bf16[136,512]{1,0:T(8,128)(2,1)S(1)}, bf16[136,512]{1,0:T(8,128)(2,1)S(1)}, u32[]{:S(2)}, u32[]{:S(2)}) collective-permute-start(bf16[136,512]{1,0:T(8,128)(2,1)S(1)} %shard_map.94.refs_5_), channel_id=1, source_target_pairs={{0,16},{4,20},{8,24},{12,28},{16,0},{20,4},{24,8},{28,12},{1,17},{... | collective-permute-start | bytes 417800 | tf_op jit(solution)/shard_map/ppermute | solution.py:391
  12.0 1.5 %collective-permute-start.8 = (bf16[136,512]{1,0:T(8,128)(2,1)S(1)}, bf16[136,512]{1,0:T(8,128)(2,1)S(1)}, u32[]{:S(2)}, u32[]{:S(2)}) collective-permute-start(bf16[136,512]{1,0:T(8,128)(2,1)S(1)} %shard_map.94.refs_5_), channel_id=1, source_target_pairs={{0,8},{4,12},{8,0},{12,4},{16,24},{20,28},{24,16},{28,20},{1,9},{5... | collective-permute-start | bytes 417800 | tf_op jit(solution)/shard_map/ppermute | solution.py:391
  13.5 1.4 %collective-permute-start.4 = (bf16[64,512]{1,0:T(8,128)(2,1)S(1)}, bf16[64,512]{1,0:T(8,128)(2,1)S(1)}, u32[]{:S(2)}, u32[]{:S(2)}) collective-permute-start(bf16[64,512]{1,0:T(8,128)(2,1)S(1)} %shard_map.93._.refs_4_), channel_id=1, source_target_pairs={{0,1},{1,0},{2,3},{3,2},{4,5},{5,4},{6,7},{7,6},{8,9},{9,8},{10,11... | collective-permute-start | bytes 196616 | tf_op jit(solution)/shard_map/ppermute | solution.py:391
  14.8 1.8 %shard_map.95 = (f32[512,1024]{1,0:T(8,128)S(1)}, f32[512,1024]{1,0:T(8,128)S(1)}, bf16[3,512,1024]{2,1,0:T(8,128)(2,1)S(1)}, bf16[1,256,1024]{2,1,0:T(8,128)(2,1)S(1)}) custom-call(bf16[512,1024]{1,0:T(8,128)(2,1)S(1)} %get-tuple-element.40.refs_0_, bf16[512,1024]{1,0:T(8,128)(2,1)S(1)} %get-tuple-element.41.refs_1_, ...), custom_call_target="tpu_custom_call" | custom-call | flops 1342177280 | tf_op jit(solution)/shard_map/pallas_call | solution.py:375
  16.6 1.1 %collective-permute-done.4.refs_5_ = bf16[64,512]{1,0:T(8,128)(2,1)S(1)} collective-permute-done((bf16[64,512]{1,0:T(8,128)(2,1)S(1)}, bf16[64,512]{1,0:T(8,128)(2,1)S(1)}, u32[]{:S(2)}, u32[]{:S(2)}) %collective-permute-start.4) | collective-permute-done | bytes 65568 | tf_op jit(solution)/shard_map/ppermute | solution.py:391
  17.7 0.7 %shard_map.96 = (f32[512,512]{1,0:T(8,128)S(1)}, bf16[512,128]{1,0:T(8,128)(2,1)S(1)}, bf16[512,256]{1,0:T(8,128)(2,1)S(1)}) custom-call(bf16[32,512]{1,0:T(8,128)(2,1)S(1)} %get-tuple-element.35.refs_0_, bf16[32,512]{1,0:T(8,128)(2,1)S(1)} %collective-permute-done.refs_1_, bf16[32,512]{1,0:T(8,128)(2,1)S(1)} %collective-permute-done.1.refs_2_, ...), custom_call_target="tpu_custom_call" | custom-call | tf_op jit(solution)/shard_map/pallas_call | solution.py:375
  18.4 0.6 %shard_map.97.refs_1_ = f32[512,512]{1,0:T(8,128)S(1)} custom-call(bf16[512,256]{1,0:T(8,128)(2,1)S(1)} %get-tuple-element.52.scores_ref, bf16[512,128]{1,0:T(8,128)(2,1)S(1)} %get-tuple-element.50.turned_ref.refs_0_, f32[512,1024]{1,0:T(8,128)S(1)} %get-tuple-element.45.refs_6_.refs_0_, f32[512,1024]{1,0:T(8,128)S(1)} %get-tuple-element.46.refs_7_.refs_1_, ...), custom_call_target="tpu_custom_call" | custom-call | tf_op jit(solution)/shard_map/pallas_call | solution.py:375
  19.0 0.8 %collective-permute-done.7.y_ref = bf16[136,512]{1,0:T(8,128)(2,1)S(1)} collective-permute-done((bf16[136,512]{1,0:T(8,128)(2,1)S(1)}, bf16[136,512]{1,0:T(8,128)(2,1)S(1)}, u32[]{:S(2)}, u32[]{:S(2)}) %collective-permute-start.7) | collective-permute-done | bytes 139296 | tf_op jit(solution)/shard_map/ppermute | solution.py:391
  19.8 0.1 collective-permute-done.8.x_ref
  19.9 0.1 shard_map.98.refs_5_
  20.0 1.9 %collective-permute-start.10 = (bf16[256,512]{1,0:T(8,128)(2,1)S(1)}, bf16[256,512]{1,0:T(8,128)(2,1)S(1)}, u32[]{:S(2)}, u32[]{:S(2)}) collective-permute-start(bf16[256,512]{1,0:T(8,128)(2,1)S(1)} %shard_map.98.refs_5_), channel_id=1, source_target_pairs={{0,0},{4,4},{8,12},{12,8},{16,20},{20,16},{24,28},{28,24},{1,1},{5... | collective-permute-start | bytes 786440 | tf_op jit(solution)/shard_map/ppermute | solution.py:512
  22.0 0.5 %shard_map.99 = (f32[512,512]{1,0:T(8,128)S(1)}, f32[512,128]{1,0:T(8,128)S(1)}) custom-call(bf16[512,128]{1,0:T(8,128)(2,1)S(1)} %get-tuple-element.50.turned_ref.refs_0_, f32[512,512]{1,0:T(8,128)S(1)} %get-tuple-element.60.refs_1_, bf16[3,512,1024]{2,1,0:T(8,128)(2,1)S(1)} %get-tuple-element.55.refs_8_.refs_2_, f32[1,1024]{1,0:T(1,128)S(1)} %get-tuple-element.56.refs_3_, ...), custom_call_target="tpu_custom_call" | custom-call | flops 536870912 | bytes 3145728 | tf_op jit(solution)/shard_map/pallas_call | solution.py:375
  22.5 1.0 %collective-permute-done.10.refs_5_ = bf16[256,512]{1,0:T(8,128)(2,1)S(1)} collective-permute-done((bf16[256,512]{1,0:T(8,128)(2,1)S(1)}, bf16[256,512]{1,0:T(8,128)(2,1)S(1)}, u32[]{:S(2)}, u32[]{:S(2)}) %collective-permute-start.10) | collective-permute-done | bytes 262176 | tf_op jit(solution)/shard_map/ppermute | solution.py:512
  23.5 0.7 %shard_map.100 = (f32[512,512]{1,0:T(8,128)S(1)}, f32[1,512]{1,0:T(1,128)S(1)}) custom-call(bf16[512,128]{1,0:T(8,128)(2,1)S(1)} %get-tuple-element.50.turned_ref.refs_0_, f32[512,512]{1,0:T(8,128)S(1)} %shard_map.97.refs_1_, bf16[3,512,1024]{2,1,0:T(8,128)(2,1)S(1)} %get-tuple-element.55.refs_8_.refs_2_, f32[1,1024]{1,0:T(1,128)S(1)} %get-tuple-element.56.refs_3_, ...), custom_call_target="tpu_custom_call" | custom-call | flops 536870912 | bytes 3145728 | tf_op jit(solution)/shard_map/pallas_call | solution.py:375
  24.1 1.3 %collective-permute-start.11 = (f32[1,512]{1,0:T(1,128)S(1)}, f32[1,512]{1,0:T(1,128)S(1)}, u32[]{:S(2)}, u32[]{:S(2)}) collective-permute-start(f32[1,512]{1,0:T(1,128)S(1)} %get-tuple-element.62.refs_0_), channel_id=1, source_target_pairs={{0,1},{1,2},{2,3},{3,0},{4,5},{5,6},{6,7},{7,4},{8,9},{9,10},{10,1... | collective-permute-start | bytes 6152 | tf_op jit(solution)/shard_map/ppermute | solution.py:400
  25.5 2.4 %collective-permute-start.12 = (f32[1,512]{1,0:T(1,128)S(1)}, f32[1,512]{1,0:T(1,128)S(1)}, u32[]{:S(2)}, u32[]{:S(2)}) collective-permute-start(f32[1,512]{1,0:T(1,128)S(1)} %get-tuple-element.62.refs_0_), channel_id=1, source_target_pairs={{0,2},{1,3},{2,0},{3,1},{4,6},{5,7},{6,4},{7,5},{8,10},{9,11},{10,... | collective-permute-start | bytes 6152 | tf_op jit(solution)/shard_map/ppermute | solution.py:400
  27.9 2.1 %collective-permute-done.12.refs_2_ = f32[1,512]{1,0:T(1,128)S(1)} collective-permute-done((f32[1,512]{1,0:T(1,128)S(1)}, f32[1,512]{1,0:T(1,128)S(1)}, u32[]{:S(2)}, u32[]{:S(2)}) %collective-permute-start.12) | collective-permute-done | bytes 2080 | tf_op jit(solution)/shard_map/ppermute | solution.py:400
  30.0 1.5 %collective-permute-done.13.refs_3_ = f32[1,512]{1,0:T(1,128)S(1)} collective-permute-done((f32[1,512]{1,0:T(1,128)S(1)}, f32[1,512]{1,0:T(1,128)S(1)}, u32[]{:S(2)}, u32[]{:S(2)}) %collective-permute-start.13) | collective-permute-done | bytes 2080 | tf_op jit(solution)/shard_map/ppermute | solution.py:400
  31.4 1.3 %shard_map.101 = bf16[512,1024]{1,0:T(8,128)(2,1)} custom-call(f32[1,512]{1,0:T(1,128)S(1)} %get-tuple-element.62.refs_0_, f32[1,512]{1,0:T(1,128)S(1)} %collective-permute-done.11.refs_1_, f32[1,512]{1,0:T(1,128)S(1)} %collective-permute-done.12.refs_2_, f32[1,512]{1,0:T(1,128)S(1)} %collective-permute-done.13.refs_3_, ...), custom_call_target="tpu_custom_call" | custom-call | flops 268435456 | bytes 3145728 | tf_op jit(solution)/shard_map/pallas_call | solution.py:375
  (7 shorter events, 0.0 us)
Async XLA Ops:
  0.0 7.9 %collective-permute-start = (bf16[32,512]{1,0:T(8,128)(2,1)}, bf16[32,512]{1,0:T(8,128)(2,1)S(1)}, u32[]{:S(2)}, u32[]{:S(2)}) collective-permute-start(bf16[32,512]{1,0:T(8,128)(2,1)} %refs_6_.1), channel_id=1, source_target_pairs={{0,2},{1,3},{2,0},{3,1},{4,6},{5,7},{6,4},{7,5},{8,10},{9,11},{10,... | collective-permute-start | bytes 98312 | tf_op jit(solution)/shard_map/ppermute | solution.py:391
  2.6 5.3 %collective-permute-start.1 = (bf16[32,512]{1,0:T(8,128)(2,1)}, bf16[32,512]{1,0:T(8,128)(2,1)S(1)}, u32[]{:S(2)}, u32[]{:S(2)}) collective-permute-start(bf16[32,512]{1,0:T(8,128)(2,1)} %refs_6_.1), channel_id=1, source_target_pairs={{0,3},{1,2},{2,1},{3,0},{4,7},{5,6},{6,5},{7,4},{8,11},{9,10},{10,... | collective-permute-start | bytes 98312 | tf_op jit(solution)/shard_map/ppermute | solution.py:391
  2.6 5.3 %collective-permute-start.2 = (bf16[32,512]{1,0:T(8,128)(2,1)}, bf16[32,512]{1,0:T(8,128)(2,1)S(1)}, u32[]{:S(2)}, u32[]{:S(2)}) collective-permute-start(bf16[32,512]{1,0:T(8,128)(2,1)} %refs_6_.1), channel_id=1, source_target_pairs={{0,1},{1,0},{2,3},{3,2},{4,5},{5,4},{6,7},{7,6},{8,9},{9,8},{10,11... | collective-permute-start | bytes 98312 | tf_op jit(solution)/shard_map/ppermute | solution.py:391
  4.4 5.0 %collective-permute-start.3 = (bf16[32,512]{1,0:T(8,128)(2,1)}, bf16[32,512]{1,0:T(8,128)(2,1)S(1)}, u32[]{:S(2)}, u32[]{:S(2)}) collective-permute-start(bf16[32,512]{1,0:T(8,128)(2,1)} %refs_7_.1), channel_id=1, source_target_pairs={{0,2},{1,3},{2,0},{3,1},{4,6},{5,7},{6,4},{7,5},{8,10},{9,11},{10,... | collective-permute-start | bytes 98312 | tf_op jit(solution)/shard_map/ppermute | solution.py:391
  8.3 1.4 %collective-permute-start.5 = (bf16[136,512]{1,0:T(8,128)(2,1)S(1)}, bf16[136,512]{1,0:T(8,128)(2,1)S(1)}, u32[]{:S(2)}, u32[]{:S(2)}) collective-permute-start(bf16[136,512]{1,0:T(8,128)(2,1)S(1)} %get-tuple-element.44), channel_id=1, source_target_pairs={{0,4},{4,0},{8,12},{12,8},{16,20},{20,16},{24,28},{28,24},{1,5},{5... | collective-permute-start | bytes 417800 | tf_op jit(solution)/shard_map/ppermute | solution.py:391
  9.8 8.7 %collective-permute-start.9 = (bf16[136,512]{1,0:T(8,128)(2,1)S(1)}, bf16[136,512]{1,0:T(8,128)(2,1)S(1)}, u32[]{:S(2)}, u32[]{:S(2)}) collective-permute-start(bf16[136,512]{1,0:T(8,128)(2,1)S(1)} %get-tuple-element.53._.mine_ref), channel_id=1, source_target_pairs={{0,4},{4,0},{8,12},{12,8},{16,20},{20,16},{24,28},{28,24},{1,5},{5... | collective-permute-start | bytes 417800 | tf_op jit(solution)/shard_map/ppermute | solution.py:391
  10.0 9.0 %collective-permute-start.6 = (bf16[136,512]{1,0:T(8,128)(2,1)S(1)}, bf16[136,512]{1,0:T(8,128)(2,1)S(1)}, u32[]{:S(2)}, u32[]{:S(2)}) collective-permute-start(bf16[136,512]{1,0:T(8,128)(2,1)S(1)} %shard_map.94.refs_5_), channel_id=1, source_target_pairs={{0,24},{4,28},{8,16},{12,20},{16,8},{20,12},{24,0},{28,4},{1,25},{... | collective-permute-start | bytes 417800 | tf_op jit(solution)/shard_map/ppermute | solution.py:391
  11.5 8.3 %collective-permute-start.7 = (bf16[136,512]{1,0:T(8,128)(2,1)S(1)}, bf16[136,512]{1,0:T(8,128)(2,1)S(1)}, u32[]{:S(2)}, u32[]{:S(2)}) collective-permute-start(bf16[136,512]{1,0:T(8,128)(2,1)S(1)} %shard_map.94.refs_5_), channel_id=1, source_target_pairs={{0,16},{4,20},{8,24},{12,28},{16,0},{20,4},{24,8},{28,12},{1,17},{... | collective-permute-start | bytes 417800 | tf_op jit(solution)/shard_map/ppermute | solution.py:391
  12.0 7.9 %collective-permute-start.8 = (bf16[136,512]{1,0:T(8,128)(2,1)S(1)}, bf16[136,512]{1,0:T(8,128)(2,1)S(1)}, u32[]{:S(2)}, u32[]{:S(2)}) collective-permute-start(bf16[136,512]{1,0:T(8,128)(2,1)S(1)} %shard_map.94.refs_5_), channel_id=1, source_target_pairs={{0,8},{4,12},{8,0},{12,4},{16,24},{20,28},{24,16},{28,20},{1,9},{5... | collective-permute-start | bytes 417800 | tf_op jit(solution)/shard_map/ppermute | solution.py:391
  13.5 4.3 %collective-permute-start.4 = (bf16[64,512]{1,0:T(8,128)(2,1)S(1)}, bf16[64,512]{1,0:T(8,128)(2,1)S(1)}, u32[]{:S(2)}, u32[]{:S(2)}) collective-permute-start(bf16[64,512]{1,0:T(8,128)(2,1)S(1)} %shard_map.93._.refs_4_), channel_id=1, source_target_pairs={{0,1},{1,0},{2,3},{3,2},{4,5},{5,4},{6,7},{7,6},{8,9},{9,8},{10,11... | collective-permute-start | bytes 196616 | tf_op jit(solution)/shard_map/ppermute | solution.py:391
  20.0 3.4 %collective-permute-start.10 = (bf16[256,512]{1,0:T(8,128)(2,1)S(1)}, bf16[256,512]{1,0:T(8,128)(2,1)S(1)}, u32[]{:S(2)}, u32[]{:S(2)}) collective-permute-start(bf16[256,512]{1,0:T(8,128)(2,1)S(1)} %shard_map.98.refs_5_), channel_id=1, source_target_pairs={{0,0},{4,4},{8,12},{12,8},{16,20},{20,16},{24,28},{28,24},{1,1},{5... | collective-permute-start | bytes 786440 | tf_op jit(solution)/shard_map/ppermute | solution.py:512
  24.1 3.7 %collective-permute-start.11 = (f32[1,512]{1,0:T(1,128)S(1)}, f32[1,512]{1,0:T(1,128)S(1)}, u32[]{:S(2)}, u32[]{:S(2)}) collective-permute-start(f32[1,512]{1,0:T(1,128)S(1)} %get-tuple-element.62.refs_0_), channel_id=1, source_target_pairs={{0,1},{1,2},{2,3},{3,0},{4,5},{5,6},{6,7},{7,4},{8,9},{9,10},{10,1... | collective-permute-start | bytes 6152 | tf_op jit(solution)/shard_map/ppermute | solution.py:400
  25.5 4.5 %collective-permute-start.12 = (f32[1,512]{1,0:T(1,128)S(1)}, f32[1,512]{1,0:T(1,128)S(1)}, u32[]{:S(2)}, u32[]{:S(2)}) collective-permute-start(f32[1,512]{1,0:T(1,128)S(1)} %get-tuple-element.62.refs_0_), channel_id=1, source_target_pairs={{0,2},{1,3},{2,0},{3,1},{4,6},{5,7},{6,4},{7,5},{8,10},{9,11},{10,... | collective-permute-start | bytes 6152 | tf_op jit(solution)/shard_map/ppermute | solution.py:400
  27.9 3.6 %collective-permute-start.13 = (f32[1,512]{1,0:T(1,128)S(1)}, f32[1,512]{1,0:T(1,128)S(1)}, u32[]{:S(2)}, u32[]{:S(2)}) collective-permute-start(f32[1,512]{1,0:T(1,128)S(1)} %get-tuple-element.62.refs_0_), channel_id=1, source_target_pairs={{0,3},{1,0},{2,1},{3,2},{4,7},{5,4},{6,5},{7,6},{8,11},{9,8},{10,9... | collective-permute-start | bytes 6152 | tf_op jit(solution)/shard_map/ppermute | solution.py:400

commit v18 on v15

--- a/solution.py
+++ b/solution.py
@@ -13,6 +13,7 @@
 BLOCK = 256
 NORM_CHUNKS = 4
 FIRST_HOP = 2
+CYCLE = [(2 * chip + core, 2 * target + core) for chip, target in ((0, 3), (3, 1), (1, 2), (2, 0)) for core in (0, 1)]
 VMEM_LIMIT = 40 * 1024 * 1024
 
 f32, bf16 = jnp.float32, jnp.bfloat16
@@ -497,12 +498,12 @@
     )
     sums_shape = shaped((1, tokens), f32)
     if pairs:
-        received = [flip(message, "seq", mask) for mask in (6, 4, 2)]
+        received = [flip(message, "seq", 4), flip(message, "seq", 2), lax.ppermute(message, "seq", CYCLE)]
         *received, other_theirs, near, far = lax.optimization_barrier((*received, other_theirs, near, far))
         own = call(
             functools.partial(combine_kernel, size),
             shaped((2 * size, width // 2), bf16),
-            received[::-1],
+            (received[1], received[0], received[2]),
             bytes_accessed=area,
         )
         other = flip(own, "seq", 1)

time: 31.7 us -> 30.9 us (0.975)
  waiting for transfers between devices: 6.91 us -> 5.87 us
    ppermute x11 -> x10, waiting for transfers between devices: 4.79 us -> 3.78 us  [flip(): lax.ppermute(array, axis, [(i, i ^ mask) for i in range(lax.axis_size(axi...]
    ppermute x11 -> x10, starting transfers between devices: 12.8 us -> 12.3 us  [flip(): lax.ppermute(array, axis, [(i, i ^ mask) for i in range(lax.axis_size(axi...]
    ppermute x0 -> x1, starting transfers between devices: none -> 0.47 us  [on_device(): lax.ppermute(message, 'seq', CYCLE)]
  transfers between devices with their start and end apart: 14 -> 14, of which waited for: 7 -> 6; matrix products, arithmetic and copies ran while one was open for 0% -> 0% of each run, Pallas kernels for 18% -> 19%
where the time goes in v18:
time: 30.9 us; the launch traced here: 30.8 us
  starting transfers between devices  16.9 us (55%)
  Pallas kernels  7.86 us (25%)
  waiting for transfers between devices  5.87 us (19%)
    ppermute x10, starting transfers between devices, flip(): lax.ppermute(array, axis, [(i, i ^ mask) for i in range(lax.axis_size(axi...  12.3 us
    pallas_call x11, Pallas kernels, call(): pl.pallas_call(kernel, out_shape=out_shape, in_specs=specs, out_specs=jax...  7.86 us
    ppermute x3, starting transfers between devices, around(): lax.ppermute(array, axis, [(i, (i + shift) % size) for i in range(size)])  4.13 us
    ppermute x10, waiting for transfers between devices, flip(): lax.ppermute(array, axis, [(i, i ^ mask) for i in range(lax.axis_size(axi...  3.78 us
    ppermute x3, waiting for transfers between devices, around(): lax.ppermute(array, axis, [(i, (i + shift) % size) for i in range(size)])  1.83 us
  transfers between devices with their start and end apart: 14, of which 6 were waited for; matrix products, arithmetic and copies ran while one was open for 0% of the time, Pallas kernels for 19%

profile of v18, /device:TPU:0, one launch (start us, length us, event | category | flops | bytes accessed | tf_op | source)
XLA Modules:
  0.0 30.8 jit_solution(11773110673434068032)
XLA Ops:
  0.0 4.0 %collective-permute-start = (bf16[32,512]{1,0:T(8,128)(2,1)}, bf16[32,512]{1,0:T(8,128)(2,1)S(1)}, u32[]{:S(2)}, u32[]{:S(2)}) collective-permute-start(bf16[32,512]{1,0:T(8,128)(2,1)} %refs_6_.1), channel_id=1, source_target_pairs={{0,2},{1,3},{2,0},{3,1},{4,6},{5,7},{6,4},{7,5},{8,10},{9,11},{10,... | collective-permute-start | bytes 98312 | tf_op jit(solution)/shard_map/ppermute | solution.py:392
  4.0 1.3 %collective-permute-start.1 = (bf16[32,512]{1,0:T(8,128)(2,1)}, bf16[32,512]{1,0:T(8,128)(2,1)S(1)}, u32[]{:S(2)}, u32[]{:S(2)}) collective-permute-start(bf16[32,512]{1,0:T(8,128)(2,1)} %refs_6_.1), channel_id=1, source_target_pairs={{0,3},{1,2},{2,1},{3,0},{4,7},{5,6},{6,5},{7,4},{8,11},{9,10},{10,... | collective-permute-start | bytes 98312 | tf_op jit(solution)/shard_map/ppermute | solution.py:392
  5.4 0.2 collective-permute-start.2
  5.6 2.8 %collective-permute-start.3 = (bf16[32,512]{1,0:T(8,128)(2,1)}, bf16[32,512]{1,0:T(8,128)(2,1)S(1)}, u32[]{:S(2)}, u32[]{:S(2)}) collective-permute-start(bf16[32,512]{1,0:T(8,128)(2,1)} %refs_7_.1), channel_id=1, source_target_pairs={{0,2},{1,3},{2,0},{3,1},{4,6},{5,7},{6,4},{7,5},{8,10},{9,11},{10,... | collective-permute-start | bytes 98312 | tf_op jit(solution)/shard_map/ppermute | solution.py:392
  8.4 1.8 %shard_map.91 = (bf16[512,1024]{1,0:T(8,128)(2,1)S(1)}, f32[16,512]{1,0:T(8,128)S(1)}, bf16[512,1024]{1,0:T(8,128)(2,1)S(1)}, bf16[512,1024]{1,0:T(8,128)(2,1)S(...) custom-call(f32[16,512]{1,0:T(8,128)} %refs_0_.1, ...), custom_call_target="tpu_custom_call" | custom-call | flops 4294967296 | bytes 2097152 | tf_op jit(solution)/shard_map/pallas_call | solution.py:376
  10.2 0.0 collective-permute-done.refs_1_
  10.2 0.0 collective-permute-done.1.refs_2_
  10.3 0.3 %shard_map.92 = (bf16[136,512]{1,0:T(8,128)(2,1)S(1)}, bf16[136,512]{1,0:T(8,128)(2,1)S(1)}, bf16[128,1024]{1,0:T(8,128)(2,1)S(1)}) custom-call(bf16[32,512]{1,0:T(8,128)(2,1)S(1)} %get-tuple-element.35.refs_0_, bf16[32,512]{1,0:T(8,128)(2,1)S(1)} %collective-permute-done.refs_1_, bf16[32,512]{1,0:T(8,128)(2,1)S(1)} %collective-permute-done.1.refs_2_, ...), custom_call_target="tpu_custom_call" | custom-call | flops 268435456 | tf_op jit(solution)/shard_map/pallas_call | solution.py:376
  10.6 0.1 collective-permute-start.5
  10.7 1.3 %collective-permute-done.5.theirs_ref.refs_9_.refs_4_ = bf16[136,512]{1,0:T(8,128)(2,1)S(1)} collective-permute-done((bf16[136,512]{1,0:T(8,128)(2,1)S(1)}, bf16[136,512]{1,0:T(8,128)(2,1)S(1)}, u32[]{:S(2)}, u32[]{:S(2)}) %collective-permute-start.5) | collective-permute-done | bytes 139296 | tf_op jit(solution)/shard_map/ppermute | solution.py:392
  12.0 0.1 shard_map.94.refs_5_
  12.1 1.6 %collective-permute-start.6 = (bf16[136,512]{1,0:T(8,128)(2,1)S(1)}, bf16[136,512]{1,0:T(8,128)(2,1)S(1)}, u32[]{:S(2)}, u32[]{:S(2)}) collective-permute-start(bf16[136,512]{1,0:T(8,128)(2,1)S(1)} %shard_map.94.refs_5_), channel_id=1, source_target_pairs={{0,16},{4,20},{8,24},{12,28},{16,0},{20,4},{24,8},{28,12},{1,17},{... | collective-permute-start | bytes 417800 | tf_op jit(solution)/shard_map/ppermute | solution.py:392
  13.7 1.5 %collective-permute-start.7 = (bf16[136,512]{1,0:T(8,128)(2,1)S(1)}, bf16[136,512]{1,0:T(8,128)(2,1)S(1)}, u32[]{:S(2)}, u32[]{:S(2)}) collective-permute-start(bf16[136,512]{1,0:T(8,128)(2,1)S(1)} %shard_map.94.refs_5_), channel_id=1, source_target_pairs={{0,8},{4,12},{8,0},{12,4},{16,24},{20,28},{24,16},{28,20},{1,9},{5... | collective-permute-start | bytes 417800 | tf_op jit(solution)/shard_map/ppermute | solution.py:392
  15.2 0.5 %collective-permute-start.8 = (bf16[136,512]{1,0:T(8,128)(2,1)S(1)}, bf16[136,512]{1,0:T(8,128)(2,1)S(1)}, u32[]{:S(2)}, u32[]{:S(2)}) collective-permute-start(bf16[136,512]{1,0:T(8,128)(2,1)S(1)} %shard_map.94.refs_5_), channel_id=1, source_target_pairs={{0,24},{4,28},{24,8},{28,12},{8,16},{12,20},{16,0},{20,4},{1,25},{... | collective-permute-start | bytes 417800 | tf_op jit(solution)/shard_map/ppermute | solution.py:501
  15.7 0.7 %collective-permute-start.4 = (bf16[64,512]{1,0:T(8,128)(2,1)S(1)}, bf16[64,512]{1,0:T(8,128)(2,1)S(1)}, u32[]{:S(2)}, u32[]{:S(2)}) collective-permute-start(bf16[64,512]{1,0:T(8,128)(2,1)S(1)} %shard_map.93._.refs_4_), channel_id=1, source_target_pairs={{0,1},{1,0},{2,3},{3,2},{4,5},{5,4},{6,7},{7,6},{8,9},{9,8},{10,11... | collective-permute-start | bytes 196616 | tf_op jit(solution)/shard_map/ppermute | solution.py:392
  16.3 1.8 %shard_map.95 = (f32[512,1024]{1,0:T(8,128)S(1)}, f32[512,1024]{1,0:T(8,128)S(1)}, bf16[3,512,1024]{2,1,0:T(8,128)(2,1)S(1)}, bf16[1,256,1024]{2,1,0:T(8,128)(2,1)S(1)}) custom-call(bf16[512,1024]{1,0:T(8,128)(2,1)S(1)} %get-tuple-element.40.refs_0_, bf16[512,1024]{1,0:T(8,128)(2,1)S(1)} %get-tuple-element.41.refs_1_, ...), custom_call_target="tpu_custom_call" | custom-call | flops 1342177280 | tf_op jit(solution)/shard_map/pallas_call | solution.py:376
  18.1 2.0 %collective-permute-done.4.refs_5_ = bf16[64,512]{1,0:T(8,128)(2,1)S(1)} collective-permute-done((bf16[64,512]{1,0:T(8,128)(2,1)S(1)}, bf16[64,512]{1,0:T(8,128)(2,1)S(1)}, u32[]{:S(2)}, u32[]{:S(2)}) %collective-permute-start.4) | collective-permute-done | bytes 65568 | tf_op jit(solution)/shard_map/ppermute | solution.py:392
  20.2 0.7 %shard_map.96 = (f32[512,512]{1,0:T(8,128)S(1)}, bf16[512,128]{1,0:T(8,128)(2,1)S(1)}, bf16[512,256]{1,0:T(8,128)(2,1)S(1)}) custom-call(bf16[32,512]{1,0:T(8,128)(2,1)S(1)} %get-tuple-element.35.refs_0_, bf16[32,512]{1,0:T(8,128)(2,1)S(1)} %collective-permute-done.refs_1_, bf16[32,512]{1,0:T(8,128)(2,1)S(1)} %collective-permute-done.1.refs_2_, ...), custom_call_target="tpu_custom_call" | custom-call | tf_op jit(solution)/shard_map/pallas_call | solution.py:376
  20.9 0.0 collective-permute-done.6.y_ref
  20.9 0.3 collective-permute-done.8.diagonal_ref
  21.1 0.1 shard_map.97._.refs_5_
  21.3 0.1 collective-permute-start.10
  21.3 0.6 %shard_map.98.refs_1_ = f32[512,512]{1,0:T(8,128)S(1)} custom-call(bf16[512,256]{1,0:T(8,128)(2,1)S(1)} %get-tuple-element.51.scores_ref, bf16[512,128]{1,0:T(8,128)(2,1)S(1)} %get-tuple-element.50.turned_ref.refs_0_, bf16[256,512]{1,0:T(8,128)(2,1)S(1)} %shard_map.97._.refs_5_, f32[512,1024]{1,0:T(8,128)S(1)} %get-tuple-element.45.refs_6_.refs_0_, ...), custom_call_target="tpu_custom_call" | custom-call | flops 268435456 | tf_op jit(solution)/shard_map/pallas_call | solution.py:376
  21.9 0.5 %shard_map.99 = (f32[512,512]{1,0:T(8,128)S(1)}, f32[512,128]{1,0:T(8,128)S(1)}) custom-call(bf16[512,128]{1,0:T(8,128)(2,1)S(1)} %get-tuple-element.50.turned_ref.refs_0_, f32[512,512]{1,0:T(8,128)S(1)} %get-tuple-element.60.refs_1_, bf16[3,512,1024]{2,1,0:T(8,128)(2,1)S(1)} %get-tuple-element.57.refs_8_.refs_2_, f32[1,1024]{1,0:T(1,128)S(1)} %get-tuple-element.59.refs_3_, ...), custom_call_target="tpu_custom_call" | custom-call | flops 536870912 | bytes 3145728 | tf_op jit(solution)/shard_map/pallas_call | solution.py:376
  22.5 0.4 %collective-permute-done.10.refs_5_ = bf16[256,512]{1,0:T(8,128)(2,1)S(1)} collective-permute-done((bf16[256,512]{1,0:T(8,128)(2,1)S(1)}, bf16[256,512]{1,0:T(8,128)(2,1)S(1)}, u32[]{:S(2)}, u32[]{:S(2)}) %collective-permute-start.10) | collective-permute-done | bytes 262176 | tf_op jit(solution)/shard_map/ppermute | solution.py:392
  22.9 0.7 %shard_map.100 = (f32[512,512]{1,0:T(8,128)S(1)}, f32[1,512]{1,0:T(1,128)S(1)}) custom-call(bf16[512,128]{1,0:T(8,128)(2,1)S(1)} %get-tuple-element.50.turned_ref.refs_0_, f32[512,512]{1,0:T(8,128)S(1)} %shard_map.98.refs_1_, bf16[3,512,1024]{2,1,0:T(8,128)(2,1)S(1)} %get-tuple-element.57.refs_8_.refs_2_, f32[1,1024]{1,0:T(1,128)S(1)} %get-tuple-element.59.refs_3_, ...), custom_call_target="tpu_custom_call" | custom-call | flops 536870912 | bytes 3145728 | tf_op jit(solution)/shard_map/pallas_call | solution.py:376
  23.5 0.7 %collective-permute-start.11 = (f32[1,512]{1,0:T(1,128)S(1)}, f32[1,512]{1,0:T(1,128)S(1)}, u32[]{:S(2)}, u32[]{:S(2)}) collective-permute-start(f32[1,512]{1,0:T(1,128)S(1)} %get-tuple-element.62.refs_0_), channel_id=1, source_target_pairs={{0,1},{1,2},{2,3},{3,0},{4,5},{5,6},{6,7},{7,4},{8,9},{9,10},{10,1... | collective-permute-start | bytes 6152 | tf_op jit(solution)/shard_map/ppermute | solution.py:401
  24.2 1.6 %collective-permute-start.12 = (f32[1,512]{1,0:T(1,128)S(1)}, f32[1,512]{1,0:T(1,128)S(1)}, u32[]{:S(2)}, u32[]{:S(2)}) collective-permute-start(f32[1,512]{1,0:T(1,128)S(1)} %get-tuple-element.62.refs_0_), channel_id=1, source_target_pairs={{0,2},{1,3},{2,0},{3,1},{4,6},{5,7},{6,4},{7,5},{8,10},{9,11},{10,... | collective-permute-start | bytes 6152 | tf_op jit(solution)/shard_map/ppermute | solution.py:401
  25.9 1.8 %collective-permute-start.13 = (f32[1,512]{1,0:T(1,128)S(1)}, f32[1,512]{1,0:T(1,128)S(1)}, u32[]{:S(2)}, u32[]{:S(2)}) collective-permute-start(f32[1,512]{1,0:T(1,128)S(1)} %get-tuple-element.62.refs_0_), channel_id=1, source_target_pairs={{0,3},{1,0},{2,1},{3,2},{4,7},{5,4},{6,5},{7,6},{8,11},{9,8},{10,9... | collective-permute-start | bytes 6152 | tf_op jit(solution)/shard_map/ppermute | solution.py:401
  27.7 1.3 %collective-permute-done.11.refs_1_ = f32[1,512]{1,0:T(1,128)S(1)} collective-permute-done((f32[1,512]{1,0:T(1,128)S(1)}, f32[1,512]{1,0:T(1,128)S(1)}, u32[]{:S(2)}, u32[]{:S(2)}) %collective-permute-start.11) | collective-permute-done | bytes 2080 | tf_op jit(solution)/shard_map/ppermute | solution.py:401
  28.9 0.6 %collective-permute-done.13.refs_3_ = f32[1,512]{1,0:T(1,128)S(1)} collective-permute-done((f32[1,512]{1,0:T(1,128)S(1)}, f32[1,512]{1,0:T(1,128)S(1)}, u32[]{:S(2)}, u32[]{:S(2)}) %collective-permute-start.13) | collective-permute-done | bytes 2080 | tf_op jit(solution)/shard_map/ppermute | solution.py:401
  29.5 1.3 %shard_map.101 = bf16[512,1024]{1,0:T(8,128)(2,1)} custom-call(f32[1,512]{1,0:T(1,128)S(1)} %get-tuple-element.62.refs_0_, f32[1,512]{1,0:T(1,128)S(1)} %collective-permute-done.11.refs_1_, f32[1,512]{1,0:T(1,128)S(1)} %collective-permute-done.12.refs_2_, f32[1,512]{1,0:T(1,128)S(1)} %collective-permute-done.13.refs_3_, ...), custom_call_target="tpu_custom_call" | custom-call | flops 268435456 | bytes 3145728 | tf_op jit(solution)/shard_map/pallas_call | solution.py:376
  (7 shorter events, 0.0 us)
Async XLA Ops:
  0.0 10.2 %collective-permute-start = (bf16[32,512]{1,0:T(8,128)(2,1)}, bf16[32,512]{1,0:T(8,128)(2,1)S(1)}, u32[]{:S(2)}, u32[]{:S(2)}) collective-permute-start(bf16[32,512]{1,0:T(8,128)(2,1)} %refs_6_.1), channel_id=1, source_target_pairs={{0,2},{1,3},{2,0},{3,1},{4,6},{5,7},{6,4},{7,5},{8,10},{9,11},{10,... | collective-permute-start | bytes 98312 | tf_op jit(solution)/shard_map/ppermute | solution.py:392
  4.0 6.2 %collective-permute-start.1 = (bf16[32,512]{1,0:T(8,128)(2,1)}, bf16[32,512]{1,0:T(8,128)(2,1)S(1)}, u32[]{:S(2)}, u32[]{:S(2)}) collective-permute-start(bf16[32,512]{1,0:T(8,128)(2,1)} %refs_6_.1), channel_id=1, source_target_pairs={{0,3},{1,2},{2,1},{3,0},{4,7},{5,6},{6,5},{7,4},{8,11},{9,10},{10,... | collective-permute-start | bytes 98312 | tf_op jit(solution)/shard_map/ppermute | solution.py:392
  5.4 4.9 %collective-permute-start.2 = (bf16[32,512]{1,0:T(8,128)(2,1)}, bf16[32,512]{1,0:T(8,128)(2,1)S(1)}, u32[]{:S(2)}, u32[]{:S(2)}) collective-permute-start(bf16[32,512]{1,0:T(8,128)(2,1)} %refs_6_.1), channel_id=1, source_target_pairs={{0,1},{1,0},{2,3},{3,2},{4,5},{5,4},{6,7},{7,6},{8,9},{9,8},{10,11... | collective-permute-start | bytes 98312 | tf_op jit(solution)/shard_map/ppermute | solution.py:392
  5.6 5.1 %collective-permute-start.3 = (bf16[32,512]{1,0:T(8,128)(2,1)}, bf16[32,512]{1,0:T(8,128)(2,1)S(1)}, u32[]{:S(2)}, u32[]{:S(2)}) collective-permute-start(bf16[32,512]{1,0:T(8,128)(2,1)} %refs_7_.1), channel_id=1, source_target_pairs={{0,2},{1,3},{2,0},{3,1},{4,6},{5,7},{6,4},{7,5},{8,10},{9,11},{10,... | collective-permute-start | bytes 98312 | tf_op jit(solution)/shard_map/ppermute | solution.py:392
  10.6 1.4 %collective-permute-start.5 = (bf16[136,512]{1,0:T(8,128)(2,1)S(1)}, bf16[136,512]{1,0:T(8,128)(2,1)S(1)}, u32[]{:S(2)}, u32[]{:S(2)}) collective-permute-start(bf16[136,512]{1,0:T(8,128)(2,1)S(1)} %get-tuple-element.44), channel_id=1, source_target_pairs={{0,4},{4,0},{8,12},{12,8},{16,20},{20,16},{24,28},{28,24},{1,5},{5... | collective-permute-start | bytes 417800 | tf_op jit(solution)/shard_map/ppermute | solution.py:392
  12.1 8.8 %collective-permute-start.6 = (bf16[136,512]{1,0:T(8,128)(2,1)S(1)}, bf16[136,512]{1,0:T(8,128)(2,1)S(1)}, u32[]{:S(2)}, u32[]{:S(2)}) collective-permute-start(bf16[136,512]{1,0:T(8,128)(2,1)S(1)} %shard_map.94.refs_5_), channel_id=1, source_target_pairs={{0,16},{4,20},{8,24},{12,28},{16,0},{20,4},{24,8},{28,12},{1,17},{... | collective-permute-start | bytes 417800 | tf_op jit(solution)/shard_map/ppermute | solution.py:392
  13.7 7.2 %collective-permute-start.7 = (bf16[136,512]{1,0:T(8,128)(2,1)S(1)}, bf16[136,512]{1,0:T(8,128)(2,1)S(1)}, u32[]{:S(2)}, u32[]{:S(2)}) collective-permute-start(bf16[136,512]{1,0:T(8,128)(2,1)S(1)} %shard_map.94.refs_5_), channel_id=1, source_target_pairs={{0,8},{4,12},{8,0},{12,4},{16,24},{20,28},{24,16},{28,20},{1,9},{5... | collective-permute-start | bytes 417800 | tf_op jit(solution)/shard_map/ppermute | solution.py:392
  15.2 5.9 %collective-permute-start.8 = (bf16[136,512]{1,0:T(8,128)(2,1)S(1)}, bf16[136,512]{1,0:T(8,128)(2,1)S(1)}, u32[]{:S(2)}, u32[]{:S(2)}) collective-permute-start(bf16[136,512]{1,0:T(8,128)(2,1)S(1)} %shard_map.94.refs_5_), channel_id=1, source_target_pairs={{0,24},{4,28},{24,8},{28,12},{8,16},{12,20},{16,0},{20,4},{1,25},{... | collective-permute-start | bytes 417800 | tf_op jit(solution)/shard_map/ppermute | solution.py:501
  15.7 5.5 %collective-permute-start.9 = (bf16[136,512]{1,0:T(8,128)(2,1)S(1)}, bf16[136,512]{1,0:T(8,128)(2,1)S(1)}, u32[]{:S(2)}, u32[]{:S(2)}) collective-permute-start(bf16[136,512]{1,0:T(8,128)(2,1)S(1)} %get-tuple-element.52._.mine_ref), channel_id=1, source_target_pairs={{0,4},{4,0},{8,12},{12,8},{16,20},{20,16},{24,28},{28,24},{1,5},{5... | collective-permute-start | bytes 417800 | tf_op jit(solution)/shard_map/ppermute | solution.py:392
  15.7 4.5 %collective-permute-start.4 = (bf16[64,512]{1,0:T(8,128)(2,1)S(1)}, bf16[64,512]{1,0:T(8,128)(2,1)S(1)}, u32[]{:S(2)}, u32[]{:S(2)}) collective-permute-start(bf16[64,512]{1,0:T(8,128)(2,1)S(1)} %shard_map.93._.refs_4_), channel_id=1, source_target_pairs={{0,1},{1,0},{2,3},{3,2},{4,5},{5,4},{6,7},{7,6},{8,9},{9,8},{10,11... | collective-permute-start | bytes 196616 | tf_op jit(solution)/shard_map/ppermute | solution.py:392
  21.3 1.6 %collective-permute-start.10 = (bf16[256,512]{1,0:T(8,128)(2,1)S(1)}, bf16[256,512]{1,0:T(8,128)(2,1)S(1)}, u32[]{:S(2)}, u32[]{:S(2)}) collective-permute-start(bf16[256,512]{1,0:T(8,128)(2,1)S(1)} %shard_map.97._.refs_5_), channel_id=1, source_target_pairs={{0,4},{4,0},{8,12},{12,8},{16,20},{20,16},{24,28},{28,24},{1,5},{5... | collective-permute-start | bytes 786440 | tf_op jit(solution)/shard_map/ppermute | solution.py:392
  23.5 5.4 %collective-permute-start.11 = (f32[1,512]{1,0:T(1,128)S(1)}, f32[1,512]{1,0:T(1,128)S(1)}, u32[]{:S(2)}, u32[]{:S(2)}) collective-permute-start(f32[1,512]{1,0:T(1,128)S(1)} %get-tuple-element.62.refs_0_), channel_id=1, source_target_pairs={{0,1},{1,2},{2,3},{3,0},{4,5},{5,6},{6,7},{7,4},{8,9},{9,10},{10,1... | collective-permute-start | bytes 6152 | tf_op jit(solution)/shard_map/ppermute | solution.py:401
  24.2 4.7 %collective-permute-start.12 = (f32[1,512]{1,0:T(1,128)S(1)}, f32[1,512]{1,0:T(1,128)S(1)}, u32[]{:S(2)}, u32[]{:S(2)}) collective-permute-start(f32[1,512]{1,0:T(1,128)S(1)} %get-tuple-element.62.refs_0_), channel_id=1, source_target_pairs={{0,2},{1,3},{2,0},{3,1},{4,6},{5,7},{6,4},{7,5},{8,10},{9,11},{10,... | collective-permute-start | bytes 6152 | tf_op jit(solution)/shard_map/ppermute | solution.py:401
  25.9 3.7 %collective-permute-start.13 = (f32[1,512]{1,0:T(1,128)S(1)}, f32[1,512]{1,0:T(1,128)S(1)}, u32[]{:S(2)}, u32[]{:S(2)}) collective-permute-start(f32[1,512]{1,0:T(1,128)S(1)} %get-tuple-element.62.refs_0_), channel_id=1, source_target_pairs={{0,3},{1,0},{2,1},{3,2},{4,7},{5,4},{6,5},{7,6},{8,11},{9,8},{10,9... | collective-permute-start | bytes 6152 | tf_op jit(solution)/shard_map/ppermute | solution.py:401

commit v19 on v15

--- a/solution.py
+++ b/solution.py
@@ -13,6 +13,7 @@
 BLOCK = 256
 NORM_CHUNKS = 4
 FIRST_HOP = 2
+CYCLE = [(2 * chip + core, 2 * target + core) for chip, target in ((0, 3), (3, 1), (1, 2), (2, 0)) for core in (0, 1)]
 VMEM_LIMIT = 40 * 1024 * 1024
 
 f32, bf16 = jnp.float32, jnp.bfloat16
@@ -282,8 +283,14 @@
     high = squares.astype(bf16)
     low = (squares - high.astype(f32)).astype(bf16)
     parts = jnp.concatenate([high, low], axis=1)
-    ones = jnp.ones((16, parts.shape[1]), bf16)
-    return lax.dot_general(ones, parts, (((1,), (1,)), ((), ())), preferred_element_type=f32)[:1]
+    sums = jnp.dot(parts, jnp.ones((parts.shape[1], 128), bf16), preferred_element_type=f32)
+    row = lax.broadcasted_iota(jnp.int32, (128, 128), 0)
+    col = lax.broadcasted_iota(jnp.int32, (128, 128), 1)
+    blocks = [
+        jnp.sum(jnp.where(row == col, sums[at : at + 128], 0.0), axis=0, keepdims=True)
+        for at in range(0, sums.shape[0], 128)
+    ]
+    return jnp.concatenate(blocks, axis=1)
 
 
 def far_kernel(turned_ref, near_ref, far_ref, gain_ref, *refs):
@@ -342,13 +349,8 @@
     for ref in refs[1:parts]:
         total = total + ref[...]
     scale = lax.rsqrt(total / columns + 1e-05)
-    pieces, rest = [], scale
-    for _ in range(3):
-        pieces.append(rest.astype(bf16).astype(f32))
-        rest = rest - pieces[-1]
     tokens = scale.shape[1]
-    pieces.append(jnp.zeros((16 - len(pieces), tokens), f32))
-    scale = transposed_dot(jnp.concatenate(pieces, axis=0).astype(bf16), jnp.ones((16, 128), bf16))
+    scale = jnp.broadcast_to(scale, (8, tokens))
     width = gated_refs[0].shape[1]
     core = lax.rem(lax.axis_index("seq"), 2)
     sides = (core, 1 - core) if len(gated_refs) == 2 else (0,)
@@ -356,10 +358,10 @@
     copies = []
     for index in range(NORM_CHUNKS):
         rows = slice(index * chunk, (index + 1) * chunk)
+        column = jnp.transpose(scale[:, rows])[:, :1]
         for ref, side in zip(gated_refs, sides):
-            for col in range(0, width, 128):
-                at = pl.ds(pl.multiple_of(side * width + col, 128), 128)
-                out_ref[rows, at] = (ref[rows, col : col + 128] * scale[rows]).astype(bf16)
+            at = pl.ds(pl.multiple_of(side * width, width), width)
+            out_ref[rows, at] = (ref[rows, :] * column).astype(bf16)
         copies.append(pltpu.make_async_copy(out_ref.at[rows], out_hbm.at[rows], semaphores.at[index]))
         copies[-1].start()
     for copy in copies:
@@ -497,7 +499,7 @@
     )
     sums_shape = shaped((1, tokens), f32)
     if pairs:
-        received = [flip(message, "seq", mask) for mask in (6, 4, 2)]
+        received = [lax.ppermute(message, "seq", CYCLE), flip(message, "seq", 4), flip(message, "seq", 2)]
         *received, other_theirs, near, far = lax.optimization_barrier((*received, other_theirs, near, far))
         own = call(
             functools.partial(combine_kernel, size),

time: 31.7 us -> 31.7 us (level)
    ppermute x0 -> x1, starting transfers between devices: none -> 2.51 us  [on_device(): lax.ppermute(message, 'seq', CYCLE)]
    ppermute x11 -> x10, starting transfers between devices: 12.8 us -> 10.3 us  [flip(): lax.ppermute(array, axis, [(i, i ^ mask) for i in range(lax.axis_size(axi...]
    ppermute x11 -> x10, waiting for transfers between devices: 4.79 us -> 4.75 us  [flip(): lax.ppermute(array, axis, [(i, i ^ mask) for i in range(lax.axis_size(axi...]
  transfers between devices with their start and end apart: 14 -> 14, of which waited for: 7 -> 6; matrix products, arithmetic and copies ran while one was open for 0% -> 0% of each run, Pallas kernels for 18% -> 18%
where the time goes in v19:
time: 31.7 us; the launch traced here: 31.6 us
  starting transfers between devices  16.7 us (53%)
  Pallas kernels  7.88 us (25%)
  waiting for transfers between devices  6.87 us (22%)
    ppermute x10, starting transfers between devices, flip(): lax.ppermute(array, axis, [(i, i ^ mask) for i in range(lax.axis_size(axi...  10.3 us
    pallas_call x11, Pallas kernels, call(): pl.pallas_call(kernel, out_shape=out_shape, in_specs=specs, out_specs=jax...  7.88 us
    ppermute x10, waiting for transfers between devices, flip(): lax.ppermute(array, axis, [(i, i ^ mask) for i in range(lax.axis_size(axi...  4.75 us
    ppermute x3, starting transfers between devices, around(): lax.ppermute(array, axis, [(i, (i + shift) % size) for i in range(size)])  3.88 us
    ppermute x1, starting transfers between devices, on_device(): lax.ppermute(message, 'seq', CYCLE)  2.51 us
    ppermute x3, waiting for transfers between devices, around(): lax.ppermute(array, axis, [(i, (i + shift) % size) for i in range(size)])  2.12 us
  transfers between devices with their start and end apart: 14, of which 6 were waited for; matrix products, arithmetic and copies ran while one was open for 0% of the time, Pallas kernels for 18%

profile of v19, /device:TPU:0, one launch (start us, length us, event | category | flops | bytes accessed | tf_op | source)
XLA Modules:
  0.0 31.6 jit_solution(11883403142135930749)
XLA Ops:
  0.0 4.0 %collective-permute-start = (bf16[32,512]{1,0:T(8,128)(2,1)}, bf16[32,512]{1,0:T(8,128)(2,1)S(1)}, u32[]{:S(2)}, u32[]{:S(2)}) collective-permute-start(bf16[32,512]{1,0:T(8,128)(2,1)} %refs_6_.1), channel_id=1, source_target_pairs={{0,2},{1,3},{2,0},{3,1},{4,6},{5,7},{6,4},{7,5},{8,10},{9,11},{10,... | collective-permute-start | bytes 98312 | tf_op jit(solution)/shard_map/ppermute | solution.py:393
  4.0 1.3 %collective-permute-start.1 = (bf16[32,512]{1,0:T(8,128)(2,1)}, bf16[32,512]{1,0:T(8,128)(2,1)S(1)}, u32[]{:S(2)}, u32[]{:S(2)}) collective-permute-start(bf16[32,512]{1,0:T(8,128)(2,1)} %refs_6_.1), channel_id=1, source_target_pairs={{0,3},{1,2},{2,1},{3,0},{4,7},{5,6},{6,5},{7,4},{8,11},{9,10},{10,... | collective-permute-start | bytes 98312 | tf_op jit(solution)/shard_map/ppermute | solution.py:393
  5.4 0.2 collective-permute-start.2
  5.6 2.8 %collective-permute-start.3 = (bf16[32,512]{1,0:T(8,128)(2,1)}, bf16[32,512]{1,0:T(8,128)(2,1)S(1)}, u32[]{:S(2)}, u32[]{:S(2)}) collective-permute-start(bf16[32,512]{1,0:T(8,128)(2,1)} %refs_7_.1), channel_id=1, source_target_pairs={{0,2},{1,3},{2,0},{3,1},{4,6},{5,7},{6,4},{7,5},{8,10},{9,11},{10,... | collective-permute-start | bytes 98312 | tf_op jit(solution)/shard_map/ppermute | solution.py:393
  8.4 1.8 %shard_map.91 = (bf16[512,1024]{1,0:T(8,128)(2,1)S(1)}, f32[16,512]{1,0:T(8,128)S(1)}, bf16[512,1024]{1,0:T(8,128)(2,1)S(1)}, bf16[512,1024]{1,0:T(8,128)(2,1)S(...) custom-call(f32[16,512]{1,0:T(8,128)} %refs_0_.1, ...), custom_call_target="tpu_custom_call" | custom-call | flops 4294967296 | bytes 2097152 | tf_op jit(solution)/shard_map/pallas_call | solution.py:377
  10.2 0.0 collective-permute-done.1.refs_2_
  10.3 0.0 collective-permute-done.2.refs_3_
  10.3 0.3 %shard_map.92 = (bf16[136,512]{1,0:T(8,128)(2,1)S(1)}, bf16[136,512]{1,0:T(8,128)(2,1)S(1)}, bf16[128,1024]{1,0:T(8,128)(2,1)S(1)}) custom-call(bf16[32,512]{1,0:T(8,128)(2,1)S(1)} %get-tuple-element.35.refs_0_, bf16[32,512]{1,0:T(8,128)(2,1)S(1)} %collective-permute-done.refs_1_, bf16[32,512]{1,0:T(8,128)(2,1)S(1)} %collective-permute-done.1.refs_2_, ...), custom_call_target="tpu_custom_call" | custom-call | flops 268435456 | tf_op jit(solution)/shard_map/pallas_call | solution.py:377
  10.6 0.1 collective-permute-start.5
  10.7 0.0 collective-permute-done.3.theirs_ref
  10.7 1.3 %collective-permute-done.5.theirs_ref.refs_9_.refs_4_ = bf16[136,512]{1,0:T(8,128)(2,1)S(1)} collective-permute-done((bf16[136,512]{1,0:T(8,128)(2,1)S(1)}, bf16[136,512]{1,0:T(8,128)(2,1)S(1)}, u32[]{:S(2)}, u32[]{:S(2)}) %collective-permute-start.5) | collective-permute-done | bytes 139296 | tf_op jit(solution)/shard_map/ppermute | solution.py:393
  12.0 0.1 shard_map.94.refs_5_
  12.1 2.5 %collective-permute-start.6 = (bf16[136,512]{1,0:T(8,128)(2,1)S(1)}, bf16[136,512]{1,0:T(8,128)(2,1)S(1)}, u32[]{:S(2)}, u32[]{:S(2)}) collective-permute-start(bf16[136,512]{1,0:T(8,128)(2,1)S(1)} %shard_map.94.refs_5_), channel_id=1, source_target_pairs={{0,24},{4,28},{24,8},{28,12},{8,16},{12,20},{16,0},{20,4},{1,25},{... | collective-permute-start | bytes 417800 | tf_op jit(solution)/shard_map/ppermute | solution.py:502
  14.6 0.0 collective-permute-start.7
  14.6 1.1 %collective-permute-start.8 = (bf16[136,512]{1,0:T(8,128)(2,1)S(1)}, bf16[136,512]{1,0:T(8,128)(2,1)S(1)}, u32[]{:S(2)}, u32[]{:S(2)}) collective-permute-start(bf16[136,512]{1,0:T(8,128)(2,1)S(1)} %shard_map.94.refs_5_), channel_id=1, source_target_pairs={{0,8},{4,12},{8,0},{12,4},{16,24},{20,28},{24,16},{28,20},{1,9},{5... | collective-permute-start | bytes 417800 | tf_op jit(solution)/shard_map/ppermute | solution.py:393
  15.7 0.7 %collective-permute-start.4 = (bf16[64,512]{1,0:T(8,128)(2,1)S(1)}, bf16[64,512]{1,0:T(8,128)(2,1)S(1)}, u32[]{:S(2)}, u32[]{:S(2)}) collective-permute-start(bf16[64,512]{1,0:T(8,128)(2,1)S(1)} %shard_map.93._.refs_4_), channel_id=1, source_target_pairs={{0,1},{1,0},{2,3},{3,2},{4,5},{5,4},{6,7},{7,6},{8,9},{9,8},{10,11... | collective-permute-start | bytes 196616 | tf_op jit(solution)/shard_map/ppermute | solution.py:393
  16.4 1.8 %shard_map.95 = (f32[512,1024]{1,0:T(8,128)S(1)}, f32[512,1024]{1,0:T(8,128)S(1)}, bf16[3,512,1024]{2,1,0:T(8,128)(2,1)S(1)}, bf16[1,256,1024]{2,1,0:T(8,128)(2,1)S(1)}) custom-call(bf16[512,1024]{1,0:T(8,128)(2,1)S(1)} %get-tuple-element.40.refs_0_, bf16[512,1024]{1,0:T(8,128)(2,1)S(1)} %get-tuple-element.41.refs_1_, ...), custom_call_target="tpu_custom_call" | custom-call | flops 1342177280 | tf_op jit(solution)/shard_map/pallas_call | solution.py:377
  18.1 2.0 %collective-permute-done.4.refs_5_ = bf16[64,512]{1,0:T(8,128)(2,1)S(1)} collective-permute-done((bf16[64,512]{1,0:T(8,128)(2,1)S(1)}, bf16[64,512]{1,0:T(8,128)(2,1)S(1)}, u32[]{:S(2)}, u32[]{:S(2)}) %collective-permute-start.4) | collective-permute-done | bytes 65568 | tf_op jit(solution)/shard_map/ppermute | solution.py:393
  20.2 0.7 %shard_map.96 = (f32[512,512]{1,0:T(8,128)S(1)}, bf16[512,128]{1,0:T(8,128)(2,1)S(1)}, bf16[512,256]{1,0:T(8,128)(2,1)S(1)}) custom-call(bf16[32,512]{1,0:T(8,128)(2,1)S(1)} %get-tuple-element.35.refs_0_, bf16[32,512]{1,0:T(8,128)(2,1)S(1)} %collective-permute-done.refs_1_, bf16[32,512]{1,0:T(8,128)(2,1)S(1)} %collective-permute-done.1.refs_2_, ...), custom_call_target="tpu_custom_call" | custom-call | tf_op jit(solution)/shard_map/pallas_call | solution.py:377
  20.9 1.0 %collective-permute-done.8.x_ref = bf16[136,512]{1,0:T(8,128)(2,1)S(1)} collective-permute-done((bf16[136,512]{1,0:T(8,128)(2,1)S(1)}, bf16[136,512]{1,0:T(8,128)(2,1)S(1)}, u32[]{:S(2)}, u32[]{:S(2)}) %collective-permute-start.8) | collective-permute-done | bytes 139296 | tf_op jit(solution)/shard_map/ppermute | solution.py:393
  21.9 0.1 shard_map.97._.refs_5_
  22.0 0.1 collective-permute-start.10
  22.1 0.6 %shard_map.98.refs_1_ = f32[512,512]{1,0:T(8,128)S(1)} custom-call(bf16[512,256]{1,0:T(8,128)(2,1)S(1)} %get-tuple-element.51.scores_ref, bf16[512,128]{1,0:T(8,128)(2,1)S(1)} %get-tuple-element.50.turned_ref.refs_0_, bf16[256,512]{1,0:T(8,128)(2,1)S(1)} %shard_map.97._.refs_5_, f32[512,1024]{1,0:T(8,128)S(1)} %get-tuple-element.45.refs_6_.refs_0_, ...), custom_call_target="tpu_custom_call" | custom-call | flops 268435456 | tf_op jit(solution)/shard_map/pallas_call | solution.py:377
  22.7 0.5 %shard_map.99 = (f32[512,512]{1,0:T(8,128)S(1)}, f32[512,128]{1,0:T(8,128)S(1)}) custom-call(bf16[512,128]{1,0:T(8,128)(2,1)S(1)} %get-tuple-element.50.turned_ref.refs_0_, f32[512,512]{1,0:T(8,128)S(1)} %get-tuple-element.60.refs_1_, bf16[3,512,1024]{2,1,0:T(8,128)(2,1)S(1)} %get-tuple-element.57.refs_8_.refs_2_, f32[1,1024]{1,0:T(1,128)S(1)} %get-tuple-element.59.refs_3_, ...), custom_call_target="tpu_custom_call" | custom-call | flops 536870912 | bytes 3145728 | tf_op jit(solution)/shard_map/pallas_call | solution.py:377
  23.2 0.4 %collective-permute-done.10.refs_5_ = bf16[256,512]{1,0:T(8,128)(2,1)S(1)} collective-permute-done((bf16[256,512]{1,0:T(8,128)(2,1)S(1)}, bf16[256,512]{1,0:T(8,128)(2,1)S(1)}, u32[]{:S(2)}, u32[]{:S(2)}) %collective-permute-start.10) | collective-permute-done | bytes 262176 | tf_op jit(solution)/shard_map/ppermute | solution.py:393
  23.6 0.7 %shard_map.100 = (f32[512,512]{1,0:T(8,128)S(1)}, f32[1,512]{1,0:T(1,128)S(1)}) custom-call(bf16[512,128]{1,0:T(8,128)(2,1)S(1)} %get-tuple-element.50.turned_ref.refs_0_, f32[512,512]{1,0:T(8,128)S(1)} %shard_map.98.refs_1_, bf16[3,512,1024]{2,1,0:T(8,128)(2,1)S(1)} %get-tuple-element.57.refs_8_.refs_2_, f32[1,1024]{1,0:T(1,128)S(1)} %get-tuple-element.59.refs_3_, ...), custom_call_target="tpu_custom_call" | custom-call | flops 536870912 | bytes 3145728 | tf_op jit(solution)/shard_map/pallas_call | solution.py:377
  24.3 0.7 %collective-permute-start.11 = (f32[1,512]{1,0:T(1,128)S(1)}, f32[1,512]{1,0:T(1,128)S(1)}, u32[]{:S(2)}, u32[]{:S(2)}) collective-permute-start(f32[1,512]{1,0:T(1,128)S(1)} %get-tuple-element.62.refs_0_), channel_id=1, source_target_pairs={{0,1},{1,2},{2,3},{3,0},{4,5},{5,6},{6,7},{7,4},{8,9},{9,10},{10,1... | collective-permute-start | bytes 6152 | tf_op jit(solution)/shard_map/ppermute | solution.py:402
  25.1 1.6 %collective-permute-start.12 = (f32[1,512]{1,0:T(1,128)S(1)}, f32[1,512]{1,0:T(1,128)S(1)}, u32[]{:S(2)}, u32[]{:S(2)}) collective-permute-start(f32[1,512]{1,0:T(1,128)S(1)} %get-tuple-element.62.refs_0_), channel_id=1, source_target_pairs={{0,2},{1,3},{2,0},{3,1},{4,6},{5,7},{6,4},{7,5},{8,10},{9,11},{10,... | collective-permute-start | bytes 6152 | tf_op jit(solution)/shard_map/ppermute | solution.py:402
  26.7 1.5 %collective-permute-start.13 = (f32[1,512]{1,0:T(1,128)S(1)}, f32[1,512]{1,0:T(1,128)S(1)}, u32[]{:S(2)}, u32[]{:S(2)}) collective-permute-start(f32[1,512]{1,0:T(1,128)S(1)} %get-tuple-element.62.refs_0_), channel_id=1, source_target_pairs={{0,3},{1,0},{2,1},{3,2},{4,7},{5,4},{6,5},{7,6},{8,11},{9,8},{10,9... | collective-permute-start | bytes 6152 | tf_op jit(solution)/shard_map/ppermute | solution.py:402
  28.2 1.6 %collective-permute-done.11.refs_1_ = f32[1,512]{1,0:T(1,128)S(1)} collective-permute-done((f32[1,512]{1,0:T(1,128)S(1)}, f32[1,512]{1,0:T(1,128)S(1)}, u32[]{:S(2)}, u32[]{:S(2)}) %collective-permute-start.11) | collective-permute-done | bytes 2080 | tf_op jit(solution)/shard_map/ppermute | solution.py:402
  29.8 0.6 %collective-permute-done.13.refs_3_ = f32[1,512]{1,0:T(1,128)S(1)} collective-permute-done((f32[1,512]{1,0:T(1,128)S(1)}, f32[1,512]{1,0:T(1,128)S(1)}, u32[]{:S(2)}, u32[]{:S(2)}) %collective-permute-start.13) | collective-permute-done | bytes 2080 | tf_op jit(solution)/shard_map/ppermute | solution.py:402
  30.3 1.2 %shard_map.101 = bf16[512,1024]{1,0:T(8,128)(2,1)} custom-call(f32[1,512]{1,0:T(1,128)S(1)} %get-tuple-element.62.refs_0_, f32[1,512]{1,0:T(1,128)S(1)} %collective-permute-done.11.refs_1_, f32[1,512]{1,0:T(1,128)S(1)} %collective-permute-done.12.refs_2_, f32[1,512]{1,0:T(1,128)S(1)} %collective-permute-done.13.refs_3_, ...), custom_call_target="tpu_custom_call" | custom-call | flops 268435456 | bytes 3145728 | tf_op jit(solution)/shard_map/pallas_call | solution.py:377
  (7 shorter events, 0.0 us)
Async XLA Ops:
  0.0 10.2 %collective-permute-start = (bf16[32,512]{1,0:T(8,128)(2,1)}, bf16[32,512]{1,0:T(8,128)(2,1)S(1)}, u32[]{:S(2)}, u32[]{:S(2)}) collective-permute-start(bf16[32,512]{1,0:T(8,128)(2,1)} %refs_6_.1), channel_id=1, source_target_pairs={{0,2},{1,3},{2,0},{3,1},{4,6},{5,7},{6,4},{7,5},{8,10},{9,11},{10,... | collective-permute-start | bytes 98312 | tf_op jit(solution)/shard_map/ppermute | solution.py:393
  4.0 6.2 %collective-permute-start.1 = (bf16[32,512]{1,0:T(8,128)(2,1)}, bf16[32,512]{1,0:T(8,128)(2,1)S(1)}, u32[]{:S(2)}, u32[]{:S(2)}) collective-permute-start(bf16[32,512]{1,0:T(8,128)(2,1)} %refs_6_.1), channel_id=1, source_target_pairs={{0,3},{1,2},{2,1},{3,0},{4,7},{5,6},{6,5},{7,4},{8,11},{9,10},{10,... | collective-permute-start | bytes 98312 | tf_op jit(solution)/shard_map/ppermute | solution.py:393
  5.4 4.9 %collective-permute-start.2 = (bf16[32,512]{1,0:T(8,128)(2,1)}, bf16[32,512]{1,0:T(8,128)(2,1)S(1)}, u32[]{:S(2)}, u32[]{:S(2)}) collective-permute-start(bf16[32,512]{1,0:T(8,128)(2,1)} %refs_6_.1), channel_id=1, source_target_pairs={{0,1},{1,0},{2,3},{3,2},{4,5},{5,4},{6,7},{7,6},{8,9},{9,8},{10,11... | collective-permute-start | bytes 98312 | tf_op jit(solution)/shard_map/ppermute | solution.py:393
  5.6 5.1 %collective-permute-start.3 = (bf16[32,512]{1,0:T(8,128)(2,1)}, bf16[32,512]{1,0:T(8,128)(2,1)S(1)}, u32[]{:S(2)}, u32[]{:S(2)}) collective-permute-start(bf16[32,512]{1,0:T(8,128)(2,1)} %refs_7_.1), channel_id=1, source_target_pairs={{0,2},{1,3},{2,0},{3,1},{4,6},{5,7},{6,4},{7,5},{8,10},{9,11},{10,... | collective-permute-start | bytes 98312 | tf_op jit(solution)/shard_map/ppermute | solution.py:393
  10.6 1.4 %collective-permute-start.5 = (bf16[136,512]{1,0:T(8,128)(2,1)S(1)}, bf16[136,512]{1,0:T(8,128)(2,1)S(1)}, u32[]{:S(2)}, u32[]{:S(2)}) collective-permute-start(bf16[136,512]{1,0:T(8,128)(2,1)S(1)} %get-tuple-element.44), channel_id=1, source_target_pairs={{0,4},{4,0},{8,12},{12,8},{16,20},{20,16},{24,28},{28,24},{1,5},{5... | collective-permute-start | bytes 417800 | tf_op jit(solution)/shard_map/ppermute | solution.py:393
  12.1 8.8 %collective-permute-start.6 = (bf16[136,512]{1,0:T(8,128)(2,1)S(1)}, bf16[136,512]{1,0:T(8,128)(2,1)S(1)}, u32[]{:S(2)}, u32[]{:S(2)}) collective-permute-start(bf16[136,512]{1,0:T(8,128)(2,1)S(1)} %shard_map.94.refs_5_), channel_id=1, source_target_pairs={{0,24},{4,28},{24,8},{28,12},{8,16},{12,20},{16,0},{20,4},{1,25},{... | collective-permute-start | bytes 417800 | tf_op jit(solution)/shard_map/ppermute | solution.py:502
  14.6 6.3 %collective-permute-start.7 = (bf16[136,512]{1,0:T(8,128)(2,1)S(1)}, bf16[136,512]{1,0:T(8,128)(2,1)S(1)}, u32[]{:S(2)}, u32[]{:S(2)}) collective-permute-start(bf16[136,512]{1,0:T(8,128)(2,1)S(1)} %shard_map.94.refs_5_), channel_id=1, source_target_pairs={{0,16},{4,20},{8,24},{12,28},{16,0},{20,4},{24,8},{28,12},{1,17},{... | collective-permute-start | bytes 417800 | tf_op jit(solution)/shard_map/ppermute | solution.py:393
  14.6 7.3 %collective-permute-start.8 = (bf16[136,512]{1,0:T(8,128)(2,1)S(1)}, bf16[136,512]{1,0:T(8,128)(2,1)S(1)}, u32[]{:S(2)}, u32[]{:S(2)}) collective-permute-start(bf16[136,512]{1,0:T(8,128)(2,1)S(1)} %shard_map.94.refs_5_), channel_id=1, source_target_pairs={{0,8},{4,12},{8,0},{12,4},{16,24},{20,28},{24,16},{28,20},{1,9},{5... | collective-permute-start | bytes 417800 | tf_op jit(solution)/shard_map/ppermute | solution.py:393
  15.7 6.2 %collective-permute-start.9 = (bf16[136,512]{1,0:T(8,128)(2,1)S(1)}, bf16[136,512]{1,0:T(8,128)(2,1)S(1)}, u32[]{:S(2)}, u32[]{:S(2)}) collective-permute-start(bf16[136,512]{1,0:T(8,128)(2,1)S(1)} %get-tuple-element.52._.mine_ref), channel_id=1, source_target_pairs={{0,4},{4,0},{8,12},{12,8},{16,20},{20,16},{24,28},{28,24},{1,5},{5... | collective-permute-start | bytes 417800 | tf_op jit(solution)/shard_map/ppermute | solution.py:393
  15.7 4.5 %collective-permute-start.4 = (bf16[64,512]{1,0:T(8,128)(2,1)S(1)}, bf16[64,512]{1,0:T(8,128)(2,1)S(1)}, u32[]{:S(2)}, u32[]{:S(2)}) collective-permute-start(bf16[64,512]{1,0:T(8,128)(2,1)S(1)} %shard_map.93._.refs_4_), channel_id=1, source_target_pairs={{0,1},{1,0},{2,3},{3,2},{4,5},{5,4},{6,7},{7,6},{8,9},{9,8},{10,11... | collective-permute-start | bytes 196616 | tf_op jit(solution)/shard_map/ppermute | solution.py:393
  22.0 1.6 %collective-permute-start.10 = (bf16[256,512]{1,0:T(8,128)(2,1)S(1)}, bf16[256,512]{1,0:T(8,128)(2,1)S(1)}, u32[]{:S(2)}, u32[]{:S(2)}) collective-permute-start(bf16[256,512]{1,0:T(8,128)(2,1)S(1)} %shard_map.97._.refs_5_), channel_id=1, source_target_pairs={{0,4},{4,0},{8,12},{12,8},{16,20},{20,16},{24,28},{28,24},{1,5},{5... | collective-permute-start | bytes 786440 | tf_op jit(solution)/shard_map/ppermute | solution.py:393
  24.3 5.4 %collective-permute-start.11 = (f32[1,512]{1,0:T(1,128)S(1)}, f32[1,512]{1,0:T(1,128)S(1)}, u32[]{:S(2)}, u32[]{:S(2)}) collective-permute-start(f32[1,512]{1,0:T(1,128)S(1)} %get-tuple-element.62.refs_0_), channel_id=1, source_target_pairs={{0,1},{1,2},{2,3},{3,0},{4,5},{5,6},{6,7},{7,4},{8,9},{9,10},{10,1... | collective-permute-start | bytes 6152 | tf_op jit(solution)/shard_map/ppermute | solution.py:402
  25.1 4.7 %collective-permute-start.12 = (f32[1,512]{1,0:T(1,128)S(1)}, f32[1,512]{1,0:T(1,128)S(1)}, u32[]{:S(2)}, u32[]{:S(2)}) collective-permute-start(f32[1,512]{1,0:T(1,128)S(1)} %get-tuple-element.62.refs_0_), channel_id=1, source_target_pairs={{0,2},{1,3},{2,0},{3,1},{4,6},{5,7},{6,4},{7,5},{8,10},{9,11},{10,... | collective-permute-start | bytes 6152 | tf_op jit(solution)/shard_map/ppermute | solution.py:402
  26.7 3.6 %collective-permute-start.13 = (f32[1,512]{1,0:T(1,128)S(1)}, f32[1,512]{1,0:T(1,128)S(1)}, u32[]{:S(2)}, u32[]{:S(2)}) collective-permute-start(f32[1,512]{1,0:T(1,128)S(1)} %get-tuple-element.62.refs_0_), channel_id=1, source_target_pairs={{0,3},{1,0},{2,1},{3,2},{4,7},{5,4},{6,5},{7,6},{8,11},{9,8},{10,9... | collective-permute-start | bytes 6152 | tf_op jit(solution)/shard_map/ppermute | solution.py:402

commit v20 on v19

--- a/solution.py
+++ b/solution.py
@@ -283,14 +283,8 @@
     high = squares.astype(bf16)
     low = (squares - high.astype(f32)).astype(bf16)
     parts = jnp.concatenate([high, low], axis=1)
-    sums = jnp.dot(parts, jnp.ones((parts.shape[1], 128), bf16), preferred_element_type=f32)
-    row = lax.broadcasted_iota(jnp.int32, (128, 128), 0)
-    col = lax.broadcasted_iota(jnp.int32, (128, 128), 1)
-    blocks = [
-        jnp.sum(jnp.where(row == col, sums[at : at + 128], 0.0), axis=0, keepdims=True)
-        for at in range(0, sums.shape[0], 128)
-    ]
-    return jnp.concatenate(blocks, axis=1)
+    ones = jnp.ones((16, parts.shape[1]), bf16)
+    return lax.dot_general(ones, parts, (((1,), (1,)), ((), ())), preferred_element_type=f32)[:1]
 
 
 def far_kernel(turned_ref, near_ref, far_ref, gain_ref, *refs):
@@ -314,7 +308,7 @@
     def parts_of(ref):
         return ref[:size, :].astype(f32), ref[size:, :].astype(f32)[:1]
 
-    x_state, x_decay = parts_of(x_ref)
+    _, x_decay = parts_of(x_ref)
     y_state, y_decay = parts_of(y_ref)
     d_state, d_decay = parts_of(diagonal_ref)
     newer = jnp.where(along_x == 1, y_state, d_state)
@@ -322,25 +316,28 @@
     older = jnp.where(along_x == 1, d_state, y_state)
     running = jnp.where(along_x == 1, x_decay, 1.0)
     running = jnp.where(along_y == 1, running, 0.0)
-    spans_ref[:size, :] = jnp.where(along_x == 1, x_state, 0.0).astype(bf16)
-    spans_ref[size:, :] = ((older * newer_decay + newer) * running).astype(bf16)
+    spans_ref[...] = ((older * newer_decay + newer) * running).astype(bf16)
 
 
 def far_kernel_of_half(own, *refs):
-    turned_ref, near_ref, far_ref, gain_ref, core_ref, spans_ref = refs[:6]
+    turned_ref, near_ref, far_ref, gain_ref, core_ref, x_ref, span_ref = refs[:7]
     gated_ref, sums_ref = refs[-2:]
     size = turned_ref.shape[1]
-    core = lax.rem(lax.axis_index("seq"), 2)
-    half = spans_ref.shape[1]
+    rank = lax.axis_index("seq")
+    core = lax.rem(rank, 2)
+    along_x = lax.rem(lax.div(rank, 2), 2)
+    half = span_ref.shape[1]
     start = (core if own else 1 - core) * half
 
     def state_of(level, cols, at):
         core_decay = core_ref[size:, cols].astype(f32)[:1]
         running = jnp.where(core == 1, core_decay, 1.0)
-        return spans_ref[(level - 1) * size : level * size, cols].astype(f32) * running
+        if level == 1:
+            return x_ref[:size, cols].astype(f32) * jnp.where(along_x == 1, running, 0.0)
+        return span_ref[:, cols].astype(f32) * running
 
     squares = far_body(turned_ref, near_ref, far_ref, gain_ref, start, half, (1, 2), state_of, gated_ref)
-    sums_ref[...] = squares if own else row_sums(squares + refs[6][...])
+    sums_ref[...] = squares if own else row_sums(squares + refs[7][...])
 
 
 def norm_kernel(parts, columns, *refs):
@@ -499,15 +496,18 @@
     )
     sums_shape = shaped((1, tokens), f32)
     if pairs:
-        received = [lax.ppermute(message, "seq", CYCLE), flip(message, "seq", 4), flip(message, "seq", 2)]
-        *received, other_theirs, near, far = lax.optimization_barrier((*received, other_theirs, near, far))
+        received = [flip(message, "seq", 4), flip(message, "seq", 2), lax.ppermute(message, "seq", CYCLE)]
+        from_y, from_x, from_cycle = received
+        from_y, from_x, near, far = lax.optimization_barrier((from_y, from_x, near, far))
+        from_cycle, other_theirs, near = lax.optimization_barrier((from_cycle, other_theirs, near))
         own = call(
             functools.partial(combine_kernel, size),
-            shaped((2 * size, width // 2), bf16),
-            received[::-1],
+            shaped((size, width // 2), bf16),
+            (from_x, from_y, from_cycle),
             bytes_accessed=area,
         )
         other = flip(own, "seq", 1)
+        other_x = flip(from_x, "seq", 1)
         near_args = base, own_factor, far, other_theirs, scaled, *span_states, *span_factors
         other_near = call(
             functools.partial(other_near_kernel, spans), near_shape, (scores, turned, own, *near_args), flops=dense
@@ -516,14 +516,14 @@
         own_gated, own_squares = call(
             functools.partial(far_kernel_of_half, True),
             (gated_shape, shaped((tokens, 128), f32)),
-            (turned, near, far, gain, theirs, own),
+            (turned, near, far, gain, theirs, from_x, own),
             flops=2 * dense,
             bytes_accessed=6 * area,
         )
         other_gated, sums = call(
             functools.partial(far_kernel_of_half, False),
             (gated_shape, sums_shape),
-            (turned, other_near, far, gain, other_theirs, other, own_squares),
+            (turned, other_near, far, gain, other_theirs, other_x, other, own_squares),
             flops=2 * dense,
             bytes_accessed=6 * area,
         )

time: 31.7 us -> 30.8 us (0.972)
  waiting for transfers between devices: 6.87 us -> 5.16 us
  starting transfers between devices: 16.7 us -> 17.6 us
    ppermute x10 -> x11, starting transfers between devices: 10.3 us -> 12.7 us  [flip(): lax.ppermute(array, axis, [(i, i ^ mask) for i in range(lax.axis_size(axi...]
    ppermute x1, starting transfers between devices: 2.51 us -> 0.47 us  [on_device(): lax.ppermute(message, 'seq', CYCLE)]
    ppermute x10 -> x11, waiting for transfers between devices: 4.75 us -> 3.38 us  [flip(): lax.ppermute(array, axis, [(i, i ^ mask) for i in range(lax.axis_size(axi...]
    ppermute x3, waiting for transfers between devices: 2.12 us -> 1.59 us  [around(): lax.ppermute(array, axis, [(i, (i + shift) % size) for i in range(size)])]
    ppermute x3, starting transfers between devices: 3.88 us -> 4.37 us  [around(): lax.ppermute(array, axis, [(i, (i + shift) % size) for i in range(size)])]
  transfers between devices with their start and end apart: 14 -> 15, of which waited for: 6 -> 5; matrix products, arithmetic and copies ran while one was open for 0% -> 0% of each run, Pallas kernels for 18% -> 19%
where the time goes in v20:
time: 30.8 us; the launch traced here: 30.7 us
  starting transfers between devices  17.6 us (57%)
  Pallas kernels  7.82 us (25%)
  waiting for transfers between devices  5.16 us (17%)
    ppermute x11, starting transfers between devices, flip(): lax.ppermute(array, axis, [(i, i ^ mask) for i in range(lax.axis_size(axi...  12.7 us
    pallas_call x11, Pallas kernels, call(): pl.pallas_call(kernel, out_shape=out_shape, in_specs=specs, out_specs=jax...  7.82 us
    ppermute x3, starting transfers between devices, around(): lax.ppermute(array, axis, [(i, (i + shift) % size) for i in range(size)])  4.37 us
    ppermute x11, waiting for transfers between devices, flip(): lax.ppermute(array, axis, [(i, i ^ mask) for i in range(lax.axis_size(axi...  3.38 us
    ppermute x3, waiting for transfers between devices, around(): lax.ppermute(array, axis, [(i, (i + shift) % size) for i in range(size)])  1.59 us
  transfers between devices with their start and end apart: 15, of which 5 were waited for; matrix products, arithmetic and copies ran while one was open for 0% of the time, Pallas kernels for 19%

profile of v20, /device:TPU:0, one launch (start us, length us, event | category | flops | bytes accessed | tf_op | source)
XLA Modules:
  0.0 30.7 jit_solution(13352531019953516391)
XLA Ops:
  0.0 4.0 %collective-permute-start = (bf16[32,512]{1,0:T(8,128)(2,1)}, bf16[32,512]{1,0:T(8,128)(2,1)S(1)}, u32[]{:S(2)}, u32[]{:S(2)}) collective-permute-start(bf16[32,512]{1,0:T(8,128)(2,1)} %refs_6_.1), channel_id=1, source_target_pairs={{0,2},{1,3},{2,0},{3,1},{4,6},{5,7},{6,4},{7,5},{8,10},{9,11},{10,... | collective-permute-start | bytes 98312 | tf_op jit(solution)/shard_map/ppermute | solution.py:390
  4.0 1.3 %collective-permute-start.1 = (bf16[32,512]{1,0:T(8,128)(2,1)}, bf16[32,512]{1,0:T(8,128)(2,1)S(1)}, u32[]{:S(2)}, u32[]{:S(2)}) collective-permute-start(bf16[32,512]{1,0:T(8,128)(2,1)} %refs_6_.1), channel_id=1, source_target_pairs={{0,3},{1,2},{2,1},{3,0},{4,7},{5,6},{6,5},{7,4},{8,11},{9,10},{10,... | collective-permute-start | bytes 98312 | tf_op jit(solution)/shard_map/ppermute | solution.py:390
  5.4 0.2 collective-permute-start.2
  5.6 2.8 %collective-permute-start.3 = (bf16[32,512]{1,0:T(8,128)(2,1)}, bf16[32,512]{1,0:T(8,128)(2,1)S(1)}, u32[]{:S(2)}, u32[]{:S(2)}) collective-permute-start(bf16[32,512]{1,0:T(8,128)(2,1)} %refs_7_.1), channel_id=1, source_target_pairs={{0,2},{1,3},{2,0},{3,1},{4,6},{5,7},{6,4},{7,5},{8,10},{9,11},{10,... | collective-permute-start | bytes 98312 | tf_op jit(solution)/shard_map/ppermute | solution.py:390
  8.4 1.8 %shard_map.91 = (bf16[512,1024]{1,0:T(8,128)(2,1)S(1)}, f32[16,512]{1,0:T(8,128)S(1)}, bf16[512,1024]{1,0:T(8,128)(2,1)S(1)}, bf16[512,1024]{1,0:T(8,128)(2,1)S(...) custom-call(f32[16,512]{1,0:T(8,128)} %refs_0_.1, ...), custom_call_target="tpu_custom_call" | custom-call | flops 4294967296 | bytes 2097152 | tf_op jit(solution)/shard_map/pallas_call | solution.py:374
  10.2 0.0 collective-permute-done.1.refs_2_
  10.3 0.0 collective-permute-done.2.refs_3_
  10.3 0.3 %shard_map.92 = (bf16[136,512]{1,0:T(8,128)(2,1)S(1)}, bf16[136,512]{1,0:T(8,128)(2,1)S(1)}, bf16[128,1024]{1,0:T(8,128)(2,1)S(1)}) custom-call(bf16[32,512]{1,0:T(8,128)(2,1)S(1)} %get-tuple-element.36.refs_0_, bf16[32,512]{1,0:T(8,128)(2,1)S(1)} %collective-permute-done.refs_1_, bf16[32,512]{1,0:T(8,128)(2,1)S(1)} %collective-permute-done.1.refs_2_, ...), custom_call_target="tpu_custom_call" | custom-call | flops 268435456 | tf_op jit(solution)/shard_map/pallas_call | solution.py:374
  10.6 0.1 collective-permute-start.5
  10.7 0.0 collective-permute-done.3.theirs_ref
  10.7 1.3 %collective-permute-done.5.theirs_ref.refs_9_.refs_4_ = bf16[136,512]{1,0:T(8,128)(2,1)S(1)} collective-permute-done((bf16[136,512]{1,0:T(8,128)(2,1)S(1)}, bf16[136,512]{1,0:T(8,128)(2,1)S(1)}, u32[]{:S(2)}, u32[]{:S(2)}) %collective-permute-start.5) | collective-permute-done | bytes 139296 | tf_op jit(solution)/shard_map/ppermute | solution.py:390
  12.0 0.1 shard_map.94.refs_5_
  12.1 1.6 %collective-permute-start.6 = (bf16[136,512]{1,0:T(8,128)(2,1)S(1)}, bf16[136,512]{1,0:T(8,128)(2,1)S(1)}, u32[]{:S(2)}, u32[]{:S(2)}) collective-permute-start(bf16[136,512]{1,0:T(8,128)(2,1)S(1)} %shard_map.94.refs_5_), channel_id=1, source_target_pairs={{0,16},{4,20},{8,24},{12,28},{16,0},{20,4},{24,8},{28,12},{1,17},{... | collective-permute-start | bytes 417800 | tf_op jit(solution)/shard_map/ppermute | solution.py:390
  13.7 1.5 %collective-permute-start.7 = (bf16[136,512]{1,0:T(8,128)(2,1)S(1)}, bf16[136,512]{1,0:T(8,128)(2,1)S(1)}, u32[]{:S(2)}, u32[]{:S(2)}) collective-permute-start(bf16[136,512]{1,0:T(8,128)(2,1)S(1)} %shard_map.94.refs_5_), channel_id=1, source_target_pairs={{0,8},{4,12},{8,0},{12,4},{16,24},{20,28},{24,16},{28,20},{1,9},{5... | collective-permute-start | bytes 417800 | tf_op jit(solution)/shard_map/ppermute | solution.py:390
  15.2 0.5 %collective-permute-start.8 = (bf16[136,512]{1,0:T(8,128)(2,1)S(1)}, bf16[136,512]{1,0:T(8,128)(2,1)S(1)}, u32[]{:S(2)}, u32[]{:S(2)}) collective-permute-start(bf16[136,512]{1,0:T(8,128)(2,1)S(1)} %shard_map.94.refs_5_), channel_id=1, source_target_pairs={{0,24},{4,28},{24,8},{28,12},{8,16},{12,20},{16,0},{20,4},{1,25},{... | collective-permute-start | bytes 417800 | tf_op jit(solution)/shard_map/ppermute | solution.py:499
  15.7 0.7 %collective-permute-start.4 = (bf16[64,512]{1,0:T(8,128)(2,1)S(1)}, bf16[64,512]{1,0:T(8,128)(2,1)S(1)}, u32[]{:S(2)}, u32[]{:S(2)}) collective-permute-start(bf16[64,512]{1,0:T(8,128)(2,1)S(1)} %shard_map.93._.refs_4_), channel_id=1, source_target_pairs={{0,1},{1,0},{2,3},{3,2},{4,5},{5,4},{6,7},{7,6},{8,9},{9,8},{10,11... | collective-permute-start | bytes 196616 | tf_op jit(solution)/shard_map/ppermute | solution.py:390
  16.3 1.8 %shard_map.95 = (f32[512,1024]{1,0:T(8,128)S(1)}, f32[512,1024]{1,0:T(8,128)S(1)}, bf16[3,512,1024]{2,1,0:T(8,128)(2,1)S(1)}, bf16[1,256,1024]{2,1,0:T(8,128)(2,1)S(1)}) custom-call(bf16[512,1024]{1,0:T(8,128)(2,1)S(1)} %get-tuple-element.41.refs_0_, bf16[512,1024]{1,0:T(8,128)(2,1)S(1)} %get-tuple-element.42.refs_1_, ...), custom_call_target="tpu_custom_call" | custom-call | flops 1342177280 | tf_op jit(solution)/shard_map/pallas_call | solution.py:374
  18.1 2.0 %collective-permute-done.4.refs_5_ = bf16[64,512]{1,0:T(8,128)(2,1)S(1)} collective-permute-done((bf16[64,512]{1,0:T(8,128)(2,1)S(1)}, bf16[64,512]{1,0:T(8,128)(2,1)S(1)}, u32[]{:S(2)}, u32[]{:S(2)}) %collective-permute-start.4) | collective-permute-done | bytes 65568 | tf_op jit(solution)/shard_map/ppermute | solution.py:390
  20.2 0.7 %shard_map.96 = (f32[512,512]{1,0:T(8,128)S(1)}, bf16[512,128]{1,0:T(8,128)(2,1)S(1)}, bf16[512,256]{1,0:T(8,128)(2,1)S(1)}) custom-call(bf16[32,512]{1,0:T(8,128)(2,1)S(1)} %get-tuple-element.36.refs_0_, bf16[32,512]{1,0:T(8,128)(2,1)S(1)} %collective-permute-done.refs_1_, bf16[32,512]{1,0:T(8,128)(2,1)S(1)} %collective-permute-done.1.refs_2_, ...), custom_call_target="tpu_custom_call" | custom-call | tf_op jit(solution)/shard_map/pallas_call | solution.py:374
  20.9 0.1 collective-permute-start.10
  20.9 0.2 collective-permute-done.8.diagonal_ref
  21.1 0.1 shard_map.97._.refs_6_
  21.3 0.4 %collective-permute-start.11 = (bf16[128,512]{1,0:T(8,128)(2,1)S(1)}, bf16[128,512]{1,0:T(8,128)(2,1)S(1)}, u32[]{:S(2)}, u32[]{:S(2)}) collective-permute-start(bf16[128,512]{1,0:T(8,128)(2,1)S(1)} %shard_map.97._.refs_6_), channel_id=1, source_target_pairs={{0,4},{4,0},{8,12},{12,8},{16,20},{20,16},{24,28},{28,24},{1,5},{5... | collective-permute-start | bytes 393224 | tf_op jit(solution)/shard_map/ppermute | solution.py:390
  21.6 0.6 %shard_map.98.refs_1_ = f32[512,512]{1,0:T(8,128)S(1)} custom-call(bf16[512,256]{1,0:T(8,128)(2,1)S(1)} %get-tuple-element.52.scores_ref, bf16[512,128]{1,0:T(8,128)(2,1)S(1)} %get-tuple-element.51.turned_ref.refs_0_, bf16[128,512]{1,0:T(8,128)(2,1)S(1)} %shard_map.97._.refs_6_, f32[512,1024]{1,0:T(8,128)S(1)} %get-tuple-element.46.refs_6_.refs_0_, ...), custom_call_target="tpu_custom_call" | custom-call | flops 268435456 | tf_op jit(solution)/shard_map/pallas_call | solution.py:374
  22.2 0.5 %shard_map.99 = (f32[512,512]{1,0:T(8,128)S(1)}, f32[512,128]{1,0:T(8,128)S(1)}) custom-call(bf16[512,128]{1,0:T(8,128)(2,1)S(1)} %get-tuple-element.51.turned_ref.refs_0_, f32[512,512]{1,0:T(8,128)S(1)} %get-tuple-element.62.refs_1_, bf16[3,512,1024]{2,1,0:T(8,128)(2,1)S(1)} %get-tuple-element.59.refs_8_.refs_2_, f32[1,1024]{1,0:T(1,128)S(1)} %get-tuple-element.61.refs_3_, ...), custom_call_target="tpu_custom_call" | custom-call | flops 536870912 | bytes 3145728 | tf_op jit(solution)/shard_map/pallas_call | solution.py:374
  22.8 0.7 %shard_map.100 = (f32[512,512]{1,0:T(8,128)S(1)}, f32[1,512]{1,0:T(1,128)S(1)}) custom-call(bf16[512,128]{1,0:T(8,128)(2,1)S(1)} %get-tuple-element.51.turned_ref.refs_0_, f32[512,512]{1,0:T(8,128)S(1)} %shard_map.98.refs_1_, bf16[3,512,1024]{2,1,0:T(8,128)(2,1)S(1)} %get-tuple-element.59.refs_8_.refs_2_, f32[1,1024]{1,0:T(1,128)S(1)} %get-tuple-element.61.refs_3_, ...), custom_call_target="tpu_custom_call" | custom-call | flops 536870912 | bytes 3145728 | tf_op jit(solution)/shard_map/pallas_call | solution.py:374
  23.5 0.7 %collective-permute-start.12 = (f32[1,512]{1,0:T(1,128)S(1)}, f32[1,512]{1,0:T(1,128)S(1)}, u32[]{:S(2)}, u32[]{:S(2)}) collective-permute-start(f32[1,512]{1,0:T(1,128)S(1)} %get-tuple-element.64.refs_0_), channel_id=1, source_target_pairs={{0,1},{1,2},{2,3},{3,0},{4,5},{5,6},{6,7},{7,4},{8,9},{9,10},{10,1... | collective-permute-start | bytes 6152 | tf_op jit(solution)/shard_map/ppermute | solution.py:399
  24.2 1.6 %collective-permute-start.13 = (f32[1,512]{1,0:T(1,128)S(1)}, f32[1,512]{1,0:T(1,128)S(1)}, u32[]{:S(2)}, u32[]{:S(2)}) collective-permute-start(f32[1,512]{1,0:T(1,128)S(1)} %get-tuple-element.64.refs_0_), channel_id=1, source_target_pairs={{0,2},{1,3},{2,0},{3,1},{4,6},{5,7},{6,4},{7,5},{8,10},{9,11},{10,... | collective-permute-start | bytes 6152 | tf_op jit(solution)/shard_map/ppermute | solution.py:399
  25.8 2.1 %collective-permute-start.14 = (f32[1,512]{1,0:T(1,128)S(1)}, f32[1,512]{1,0:T(1,128)S(1)}, u32[]{:S(2)}, u32[]{:S(2)}) collective-permute-start(f32[1,512]{1,0:T(1,128)S(1)} %get-tuple-element.64.refs_0_), channel_id=1, source_target_pairs={{0,3},{1,0},{2,1},{3,2},{4,7},{5,4},{6,5},{7,6},{8,11},{9,8},{10,9... | collective-permute-start | bytes 6152 | tf_op jit(solution)/shard_map/ppermute | solution.py:399
  27.9 1.0 %collective-permute-done.12.refs_1_ = f32[1,512]{1,0:T(1,128)S(1)} collective-permute-done((f32[1,512]{1,0:T(1,128)S(1)}, f32[1,512]{1,0:T(1,128)S(1)}, u32[]{:S(2)}, u32[]{:S(2)}) %collective-permute-start.12) | collective-permute-done | bytes 2080 | tf_op jit(solution)/shard_map/ppermute | solution.py:399
  28.9 0.6 %collective-permute-done.14.refs_3_ = f32[1,512]{1,0:T(1,128)S(1)} collective-permute-done((f32[1,512]{1,0:T(1,128)S(1)}, f32[1,512]{1,0:T(1,128)S(1)}, u32[]{:S(2)}, u32[]{:S(2)}) %collective-permute-start.14) | collective-permute-done | bytes 2080 | tf_op jit(solution)/shard_map/ppermute | solution.py:399
  29.4 1.2 %shard_map.101 = bf16[512,1024]{1,0:T(8,128)(2,1)} custom-call(f32[1,512]{1,0:T(1,128)S(1)} %get-tuple-element.64.refs_0_, f32[1,512]{1,0:T(1,128)S(1)} %collective-permute-done.12.refs_1_, f32[1,512]{1,0:T(1,128)S(1)} %collective-permute-done.13.refs_2_, f32[1,512]{1,0:T(1,128)S(1)} %collective-permute-done.14.refs_3_, ...), custom_call_target="tpu_custom_call" | custom-call | flops 268435456 | bytes 3145728 | tf_op jit(solution)/shard_map/pallas_call | solution.py:374
  (9 shorter events, 0.0 us)
Async XLA Ops:
  0.0 10.2 %collective-permute-start = (bf16[32,512]{1,0:T(8,128)(2,1)}, bf16[32,512]{1,0:T(8,128)(2,1)S(1)}, u32[]{:S(2)}, u32[]{:S(2)}) collective-permute-start(bf16[32,512]{1,0:T(8,128)(2,1)} %refs_6_.1), channel_id=1, source_target_pairs={{0,2},{1,3},{2,0},{3,1},{4,6},{5,7},{6,4},{7,5},{8,10},{9,11},{10,... | collective-permute-start | bytes 98312 | tf_op jit(solution)/shard_map/ppermute | solution.py:390
  4.0 6.2 %collective-permute-start.1 = (bf16[32,512]{1,0:T(8,128)(2,1)}, bf16[32,512]{1,0:T(8,128)(2,1)S(1)}, u32[]{:S(2)}, u32[]{:S(2)}) collective-permute-start(bf16[32,512]{1,0:T(8,128)(2,1)} %refs_6_.1), channel_id=1, source_target_pairs={{0,3},{1,2},{2,1},{3,0},{4,7},{5,6},{6,5},{7,4},{8,11},{9,10},{10,... | collective-permute-start | bytes 98312 | tf_op jit(solution)/shard_map/ppermute | solution.py:390
  5.4 4.9 %collective-permute-start.2 = (bf16[32,512]{1,0:T(8,128)(2,1)}, bf16[32,512]{1,0:T(8,128)(2,1)S(1)}, u32[]{:S(2)}, u32[]{:S(2)}) collective-permute-start(bf16[32,512]{1,0:T(8,128)(2,1)} %refs_6_.1), channel_id=1, source_target_pairs={{0,1},{1,0},{2,3},{3,2},{4,5},{5,4},{6,7},{7,6},{8,9},{9,8},{10,11... | collective-permute-start | bytes 98312 | tf_op jit(solution)/shard_map/ppermute | solution.py:390
  5.6 5.1 %collective-permute-start.3 = (bf16[32,512]{1,0:T(8,128)(2,1)}, bf16[32,512]{1,0:T(8,128)(2,1)S(1)}, u32[]{:S(2)}, u32[]{:S(2)}) collective-permute-start(bf16[32,512]{1,0:T(8,128)(2,1)} %refs_7_.1), channel_id=1, source_target_pairs={{0,2},{1,3},{2,0},{3,1},{4,6},{5,7},{6,4},{7,5},{8,10},{9,11},{10,... | collective-permute-start | bytes 98312 | tf_op jit(solution)/shard_map/ppermute | solution.py:390
  10.6 1.4 %collective-permute-start.5 = (bf16[136,512]{1,0:T(8,128)(2,1)S(1)}, bf16[136,512]{1,0:T(8,128)(2,1)S(1)}, u32[]{:S(2)}, u32[]{:S(2)}) collective-permute-start(bf16[136,512]{1,0:T(8,128)(2,1)S(1)} %get-tuple-element.45), channel_id=1, source_target_pairs={{0,4},{4,0},{8,12},{12,8},{16,20},{20,16},{24,28},{28,24},{1,5},{5... | collective-permute-start | bytes 417800 | tf_op jit(solution)/shard_map/ppermute | solution.py:390
  12.1 8.7 %collective-permute-start.6 = (bf16[136,512]{1,0:T(8,128)(2,1)S(1)}, bf16[136,512]{1,0:T(8,128)(2,1)S(1)}, u32[]{:S(2)}, u32[]{:S(2)}) collective-permute-start(bf16[136,512]{1,0:T(8,128)(2,1)S(1)} %shard_map.94.refs_5_), channel_id=1, source_target_pairs={{0,16},{4,20},{8,24},{12,28},{16,0},{20,4},{24,8},{28,12},{1,17},{... | collective-permute-start | bytes 417800 | tf_op jit(solution)/shard_map/ppermute | solution.py:390
  13.7 7.2 %collective-permute-start.7 = (bf16[136,512]{1,0:T(8,128)(2,1)S(1)}, bf16[136,512]{1,0:T(8,128)(2,1)S(1)}, u32[]{:S(2)}, u32[]{:S(2)}) collective-permute-start(bf16[136,512]{1,0:T(8,128)(2,1)S(1)} %shard_map.94.refs_5_), channel_id=1, source_target_pairs={{0,8},{4,12},{8,0},{12,4},{16,24},{20,28},{24,16},{28,20},{1,9},{5... | collective-permute-start | bytes 417800 | tf_op jit(solution)/shard_map/ppermute | solution.py:390
  15.2 5.9 %collective-permute-start.8 = (bf16[136,512]{1,0:T(8,128)(2,1)S(1)}, bf16[136,512]{1,0:T(8,128)(2,1)S(1)}, u32[]{:S(2)}, u32[]{:S(2)}) collective-permute-start(bf16[136,512]{1,0:T(8,128)(2,1)S(1)} %shard_map.94.refs_5_), channel_id=1, source_target_pairs={{0,24},{4,28},{24,8},{28,12},{8,16},{12,20},{16,0},{20,4},{1,25},{... | collective-permute-start | bytes 417800 | tf_op jit(solution)/shard_map/ppermute | solution.py:499
  15.7 5.5 %collective-permute-start.9 = (bf16[136,512]{1,0:T(8,128)(2,1)S(1)}, bf16[136,512]{1,0:T(8,128)(2,1)S(1)}, u32[]{:S(2)}, u32[]{:S(2)}) collective-permute-start(bf16[136,512]{1,0:T(8,128)(2,1)S(1)} %get-tuple-element.56._.mine_ref), channel_id=1, source_target_pairs={{0,4},{4,0},{8,12},{12,8},{16,20},{20,16},{24,28},{28,24},{1,5},{5... | collective-permute-start | bytes 417800 | tf_op jit(solution)/shard_map/ppermute | solution.py:390
  15.7 4.5 %collective-permute-start.4 = (bf16[64,512]{1,0:T(8,128)(2,1)S(1)}, bf16[64,512]{1,0:T(8,128)(2,1)S(1)}, u32[]{:S(2)}, u32[]{:S(2)}) collective-permute-start(bf16[64,512]{1,0:T(8,128)(2,1)S(1)} %shard_map.93._.refs_4_), channel_id=1, source_target_pairs={{0,1},{1,0},{2,3},{3,2},{4,5},{5,4},{6,7},{7,6},{8,9},{9,8},{10,11... | collective-permute-start | bytes 196616 | tf_op jit(solution)/shard_map/ppermute | solution.py:390
  20.9 1.9 %collective-permute-start.10 = (bf16[136,512]{1,0:T(8,128)(2,1)S(1)}, bf16[136,512]{1,0:T(8,128)(2,1)S(1)}, u32[]{:S(2)}, u32[]{:S(2)}) collective-permute-start(bf16[136,512]{1,0:T(8,128)(2,1)S(1)} %collective-permute-done.7.x_ref.refs_5_), channel_id=1, source_target_pairs={{0,4},{4,0},{8,12},{12,8},{16,20},{20,16},{24,28},{28,24},{1,5},{5... | collective-permute-start | bytes 417800 | tf_op jit(solution)/shard_map/ppermute | solution.py:390
  21.3 1.5 %collective-permute-start.11 = (bf16[128,512]{1,0:T(8,128)(2,1)S(1)}, bf16[128,512]{1,0:T(8,128)(2,1)S(1)}, u32[]{:S(2)}, u32[]{:S(2)}) collective-permute-start(bf16[128,512]{1,0:T(8,128)(2,1)S(1)} %shard_map.97._.refs_6_), channel_id=1, source_target_pairs={{0,4},{4,0},{8,12},{12,8},{16,20},{20,16},{24,28},{28,24},{1,5},{5... | collective-permute-start | bytes 393224 | tf_op jit(solution)/shard_map/ppermute | solution.py:390
  23.5 5.4 %collective-permute-start.12 = (f32[1,512]{1,0:T(1,128)S(1)}, f32[1,512]{1,0:T(1,128)S(1)}, u32[]{:S(2)}, u32[]{:S(2)}) collective-permute-start(f32[1,512]{1,0:T(1,128)S(1)} %get-tuple-element.64.refs_0_), channel_id=1, source_target_pairs={{0,1},{1,2},{2,3},{3,0},{4,5},{5,6},{6,7},{7,4},{8,9},{9,10},{10,1... | collective-permute-start | bytes 6152 | tf_op jit(solution)/shard_map/ppermute | solution.py:399
  24.2 4.7 %collective-permute-start.13 = (f32[1,512]{1,0:T(1,128)S(1)}, f32[1,512]{1,0:T(1,128)S(1)}, u32[]{:S(2)}, u32[]{:S(2)}) collective-permute-start(f32[1,512]{1,0:T(1,128)S(1)} %get-tuple-element.64.refs_0_), channel_id=1, source_target_pairs={{0,2},{1,3},{2,0},{3,1},{4,6},{5,7},{6,4},{7,5},{8,10},{9,11},{10,... | collective-permute-start | bytes 6152 | tf_op jit(solution)/shard_map/ppermute | solution.py:399
  25.8 3.6 %collective-permute-start.14 = (f32[1,512]{1,0:T(1,128)S(1)}, f32[1,512]{1,0:T(1,128)S(1)}, u32[]{:S(2)}, u32[]{:S(2)}) collective-permute-start(f32[1,512]{1,0:T(1,128)S(1)} %get-tuple-element.64.refs_0_), channel_id=1, source_target_pairs={{0,3},{1,0},{2,1},{3,2},{4,7},{5,4},{6,5},{7,6},{8,11},{9,8},{10,9... | collective-permute-start | bytes 6152 | tf_op jit(solution)/shard_map/ppermute | solution.py:399

commit v21 on v20

--- a/solution.py
+++ b/solution.py
@@ -216,11 +216,10 @@
                 span_refs[0][index, :, cols] = (transposed_dot(mix, expand[:, cols]) * swish).astype(bf16)
 
 
-def near_body(spans, paired, start, scores_ref, turned_ref, refs, near_ref):
+def near_body(spans, has_core, start, scores_ref, turned_ref, refs, near_ref):
     base_ref, own_ref, far_ref, core_ref, scaled_ref = refs[:5]
     span_refs = refs[5:]
     tokens, size = turned_ref.shape
-    has_core = lax.rem(lax.axis_index("seq"), 2) == 1
     for group in range(tokens // GROUP):
         at = group_slice(group)
         for cols in blocks_of(near_ref.shape[1]):
@@ -232,11 +231,20 @@
                     rows = slice(index * size, (index + 1) * size)
                     reach = jnp.dot(turned_ref[at, :], span_refs[0][rows, of], preferred_element_type=f32)
                     total = total + span_refs[1][index, :, of].astype(f32) * reach
-            if paired:
+            if has_core:
                 reach = jnp.dot(turned_ref[at, :], core_ref[:size, cols], preferred_element_type=f32)
-                reach = jnp.where(has_core, reach, 0.0)
                 total = total + far_ref[0, at, of].astype(f32) * reach
             near_ref[at, cols] = total
+
+
+def near_of_core(spans, own, scores_ref, turned_ref, refs, near_ref):
+    core = lax.rem(lax.axis_index("seq"), 2)
+    for has_core in (0, 1):
+
+        @pl.when(core == has_core)
+        def _():
+            start = (has_core if own else 1 - has_core) * near_ref.shape[1]
+            near_body(spans, has_core, start, scores_ref, turned_ref, refs, near_ref)
 
 
 def near_kernel(parts, spans, paired, *refs):
@@ -252,14 +260,14 @@
         at = group_slice(group)
         scores = jnp.dot(turned[at], in_map[:, at], preferred_element_type=f32)
         scores_ref[at, :] = jnp.where(row >= col, scores, 0.0).astype(bf16)
-    start = lax.rem(lax.axis_index("seq"), 2) * near_ref.shape[1] if paired else 0
-    near_body(spans, paired, start, scores_ref, turned_ref, rest, near_ref)
+    if paired:
+        near_of_core(spans, True, scores_ref, turned_ref, rest, near_ref)
+    else:
+        near_body(spans, False, 0, scores_ref, turned_ref, rest, near_ref)
 
 
 def other_near_kernel(spans, scores_ref, turned_ref, _, *refs):
-    near_ref = refs[-1]
-    start = (1 - lax.rem(lax.axis_index("seq"), 2)) * near_ref.shape[1]
-    near_body(spans, True, start, scores_ref, turned_ref, refs[:-1], near_ref)
+    near_of_core(spans, False, scores_ref, turned_ref, refs[:-1], refs[-1])
 
 
 def far_body(turned_ref, near_ref, far_ref, gain_ref, start, columns, levels, state_of, gated_ref):
@@ -326,6 +334,7 @@
     rank = lax.axis_index("seq")
     core = lax.rem(rank, 2)
     along_x = lax.rem(lax.div(rank, 2), 2)
+    along_y = lax.div(rank, 4)
     half = span_ref.shape[1]
     start = (core if own else 1 - core) * half
 
@@ -333,11 +342,16 @@
         core_decay = core_ref[size:, cols].astype(f32)[:1]
         running = jnp.where(core == 1, core_decay, 1.0)
         if level == 1:
-            return x_ref[:size, cols].astype(f32) * jnp.where(along_x == 1, running, 0.0)
+            return x_ref[:size, cols].astype(f32) * running
         return span_ref[:, cols].astype(f32) * running
 
-    squares = far_body(turned_ref, near_ref, far_ref, gain_ref, start, half, (1, 2), state_of, gated_ref)
-    sums_ref[...] = squares if own else row_sums(squares + refs[7][...])
+    for has_x, has_y in ((0, 0), (0, 1), (1, 0), (1, 1)):
+
+        @pl.when((along_x == has_x) & (along_y == has_y))
+        def _():
+            levels = (1,) * has_x + (2,) * has_y
+            squares = far_body(turned_ref, near_ref, far_ref, gain_ref, start, half, levels, state_of, gated_ref)
+            sums_ref[...] = squares if own else row_sums(squares + refs[7][...])
 
 
 def norm_kernel(parts, columns, *refs):

time: 30.8 us -> 30.6 us (level); the launches traced: 30.7 us -> 30.1 us
  Pallas kernels: 7.82 us -> 6.82 us
  waiting for transfers between devices: 5.16 us -> 5.73 us
    pallas_call x11, Pallas kernels: 7.82 us -> 6.82 us  [call(): pl.pallas_call(kernel, out_shape=out_shape, in_specs=specs, out_specs=jax...]
    ppermute x11, waiting for transfers between devices: 3.38 us -> 3.85 us  [flip(): lax.ppermute(array, axis, [(i, i ^ mask) for i in range(lax.axis_size(axi...]
  transfers between devices with their start and end apart: 15 -> 15, of which waited for: 5 -> 6; matrix products, arithmetic and copies ran while one was open for 0% -> 0% of each run, Pallas kernels for 19% -> 17%
where the time goes in v21:
time: 30.6 us; the launch traced here: 30.1 us
  starting transfers between devices  17.4 us (57%)
  Pallas kernels  6.82 us (22%)
  waiting for transfers between devices  5.73 us (19%)
    ppermute x11, starting transfers between devices, flip(): lax.ppermute(array, axis, [(i, i ^ mask) for i in range(lax.axis_size(axi...  12.7 us
    pallas_call x11, Pallas kernels, call(): pl.pallas_call(kernel, out_shape=out_shape, in_specs=specs, out_specs=jax...  6.82 us
    ppermute x3, starting transfers between devices, around(): lax.ppermute(array, axis, [(i, (i + shift) % size) for i in range(size)])  4.3 us
    ppermute x11, waiting for transfers between devices, flip(): lax.ppermute(array, axis, [(i, i ^ mask) for i in range(lax.axis_size(axi...  3.85 us
    ppermute x3, waiting for transfers between devices, around(): lax.ppermute(array, axis, [(i, (i + shift) % size) for i in range(size)])  1.66 us
  transfers between devices with their start and end apart: 15, of which 6 were waited for; matrix products, arithmetic and copies ran while one was open for 0% of the time, Pallas kernels for 17%

profile of v21, /device:TPU:0, one launch (start us, length us, event | category | flops | bytes accessed | tf_op | source)
XLA Modules:
  0.0 30.1 jit_solution(5545061060949701955)
XLA Ops:
  0.0 4.0 %collective-permute-start = (bf16[32,512]{1,0:T(8,128)(2,1)}, bf16[32,512]{1,0:T(8,128)(2,1)S(1)}, u32[]{:S(2)}, u32[]{:S(2)}) collective-permute-start(bf16[32,512]{1,0:T(8,128)(2,1)} %refs_6_.1), channel_id=1, source_target_pairs={{0,2},{1,3},{2,0},{3,1},{4,6},{5,7},{6,4},{7,5},{8,10},{9,11},{10,... | collective-permute-start | bytes 98312 | tf_op jit(solution)/shard_map/ppermute | solution.py:404
  4.0 1.3 %collective-permute-start.1 = (bf16[32,512]{1,0:T(8,128)(2,1)}, bf16[32,512]{1,0:T(8,128)(2,1)S(1)}, u32[]{:S(2)}, u32[]{:S(2)}) collective-permute-start(bf16[32,512]{1,0:T(8,128)(2,1)} %refs_6_.1), channel_id=1, source_target_pairs={{0,3},{1,2},{2,1},{3,0},{4,7},{5,6},{6,5},{7,4},{8,11},{9,10},{10,... | collective-permute-start | bytes 98312 | tf_op jit(solution)/shard_map/ppermute | solution.py:404
  5.4 0.2 collective-permute-start.2
  5.6 2.8 %collective-permute-start.3 = (bf16[32,512]{1,0:T(8,128)(2,1)}, bf16[32,512]{1,0:T(8,128)(2,1)S(1)}, u32[]{:S(2)}, u32[]{:S(2)}) collective-permute-start(bf16[32,512]{1,0:T(8,128)(2,1)} %refs_7_.1), channel_id=1, source_target_pairs={{0,2},{1,3},{2,0},{3,1},{4,6},{5,7},{6,4},{7,5},{8,10},{9,11},{10,... | collective-permute-start | bytes 98312 | tf_op jit(solution)/shard_map/ppermute | solution.py:404
  8.4 1.8 %shard_map.91 = (bf16[512,1024]{1,0:T(8,128)(2,1)S(1)}, f32[16,512]{1,0:T(8,128)S(1)}, bf16[512,1024]{1,0:T(8,128)(2,1)S(1)}, bf16[512,1024]{1,0:T(8,128)(2,1)S(...) custom-call(f32[16,512]{1,0:T(8,128)} %refs_0_.1, ...), custom_call_target="tpu_custom_call" | custom-call | flops 4294967296 | bytes 2097152 | tf_op jit(solution)/shard_map/pallas_call | solution.py:388
  10.2 0.0 collective-permute-done.1.refs_2_
  10.3 0.0 collective-permute-done.2.refs_3_
  10.3 0.3 %shard_map.92 = (bf16[136,512]{1,0:T(8,128)(2,1)S(1)}, bf16[136,512]{1,0:T(8,128)(2,1)S(1)}, bf16[128,1024]{1,0:T(8,128)(2,1)S(1)}) custom-call(bf16[32,512]{1,0:T(8,128)(2,1)S(1)} %get-tuple-element.36.refs_0_, bf16[32,512]{1,0:T(8,128)(2,1)S(1)} %collective-permute-done.refs_1_, bf16[32,512]{1,0:T(8,128)(2,1)S(1)} %collective-permute-done.1.refs_2_, ...), custom_call_target="tpu_custom_call" | custom-call | flops 268435456 | tf_op jit(solution)/shard_map/pallas_call | solution.py:388
  10.6 0.1 collective-permute-start.5
  10.7 1.3 %collective-permute-done.5.theirs_ref.refs_9_.refs_4_ = bf16[136,512]{1,0:T(8,128)(2,1)S(1)} collective-permute-done((bf16[136,512]{1,0:T(8,128)(2,1)S(1)}, bf16[136,512]{1,0:T(8,128)(2,1)S(1)}, u32[]{:S(2)}, u32[]{:S(2)}) %collective-permute-start.5) | collective-permute-done | bytes 139296 | tf_op jit(solution)/shard_map/ppermute | solution.py:404
  12.0 0.1 shard_map.94.refs_5_
  12.1 1.6 %collective-permute-start.6 = (bf16[136,512]{1,0:T(8,128)(2,1)S(1)}, bf16[136,512]{1,0:T(8,128)(2,1)S(1)}, u32[]{:S(2)}, u32[]{:S(2)}) collective-permute-start(bf16[136,512]{1,0:T(8,128)(2,1)S(1)} %shard_map.94.refs_5_), channel_id=1, source_target_pairs={{0,16},{4,20},{8,24},{12,28},{16,0},{20,4},{24,8},{28,12},{1,17},{... | collective-permute-start | bytes 417800 | tf_op jit(solution)/shard_map/ppermute | solution.py:404
  13.7 1.5 %collective-permute-start.7 = (bf16[136,512]{1,0:T(8,128)(2,1)S(1)}, bf16[136,512]{1,0:T(8,128)(2,1)S(1)}, u32[]{:S(2)}, u32[]{:S(2)}) collective-permute-start(bf16[136,512]{1,0:T(8,128)(2,1)S(1)} %shard_map.94.refs_5_), channel_id=1, source_target_pairs={{0,8},{4,12},{8,0},{12,4},{16,24},{20,28},{24,16},{28,20},{1,9},{5... | collective-permute-start | bytes 417800 | tf_op jit(solution)/shard_map/ppermute | solution.py:404
  15.2 0.5 %collective-permute-start.8 = (bf16[136,512]{1,0:T(8,128)(2,1)S(1)}, bf16[136,512]{1,0:T(8,128)(2,1)S(1)}, u32[]{:S(2)}, u32[]{:S(2)}) collective-permute-start(bf16[136,512]{1,0:T(8,128)(2,1)S(1)} %shard_map.94.refs_5_), channel_id=1, source_target_pairs={{0,24},{4,28},{24,8},{28,12},{8,16},{12,20},{16,0},{20,4},{1,25},{... | collective-permute-start | bytes 417800 | tf_op jit(solution)/shard_map/ppermute | solution.py:513
  15.7 0.7 %collective-permute-start.4 = (bf16[64,512]{1,0:T(8,128)(2,1)S(1)}, bf16[64,512]{1,0:T(8,128)(2,1)S(1)}, u32[]{:S(2)}, u32[]{:S(2)}) collective-permute-start(bf16[64,512]{1,0:T(8,128)(2,1)S(1)} %shard_map.93._.refs_4_), channel_id=1, source_target_pairs={{0,1},{1,0},{2,3},{3,2},{4,5},{5,4},{6,7},{7,6},{8,9},{9,8},{10,11... | collective-permute-start | bytes 196616 | tf_op jit(solution)/shard_map/ppermute | solution.py:404
  16.3 1.8 %shard_map.95 = (f32[512,1024]{1,0:T(8,128)S(1)}, f32[512,1024]{1,0:T(8,128)S(1)}, bf16[3,512,1024]{2,1,0:T(8,128)(2,1)S(1)}, bf16[1,256,1024]{2,1,0:T(8,128)(2,1)S(1)}) custom-call(bf16[512,1024]{1,0:T(8,128)(2,1)S(1)} %get-tuple-element.41.refs_0_, bf16[512,1024]{1,0:T(8,128)(2,1)S(1)} %get-tuple-element.42.refs_1_, ...), custom_call_target="tpu_custom_call" | custom-call | flops 1342177280 | tf_op jit(solution)/shard_map/pallas_call | solution.py:388
  18.1 2.0 %collective-permute-done.4.refs_5_ = bf16[64,512]{1,0:T(8,128)(2,1)S(1)} collective-permute-done((bf16[64,512]{1,0:T(8,128)(2,1)S(1)}, bf16[64,512]{1,0:T(8,128)(2,1)S(1)}, u32[]{:S(2)}, u32[]{:S(2)}) %collective-permute-start.4) | collective-permute-done | bytes 65568 | tf_op jit(solution)/shard_map/ppermute | solution.py:404
  20.2 0.6 %shard_map.96 = (f32[512,512]{1,0:T(8,128)S(1)}, bf16[512,128]{1,0:T(8,128)(2,1)S(1)}, bf16[512,256]{1,0:T(8,128)(2,1)S(1)}) custom-call(bf16[32,512]{1,0:T(8,128)(2,1)S(1)} %get-tuple-element.36.refs_0_, bf16[32,512]{1,0:T(8,128)(2,1)S(1)} %collective-permute-done.refs_1_, bf16[32,512]{1,0:T(8,128)(2,1)S(1)} %collective-permute-done.1.refs_2_, ...), custom_call_target="tpu_custom_call" | custom-call | tf_op jit(solution)/shard_map/pallas_call | solution.py:388
  20.8 0.1 collective-permute-start.10
  20.9 0.2 collective-permute-done.8.diagonal_ref
  21.1 0.1 shard_map.97._.refs_6_
  21.3 0.3 %collective-permute-start.11 = (bf16[128,512]{1,0:T(8,128)(2,1)S(1)}, bf16[128,512]{1,0:T(8,128)(2,1)S(1)}, u32[]{:S(2)}, u32[]{:S(2)}) collective-permute-start(bf16[128,512]{1,0:T(8,128)(2,1)S(1)} %shard_map.97._.refs_6_), channel_id=1, source_target_pairs={{0,4},{4,0},{8,12},{12,8},{16,20},{20,16},{24,28},{28,24},{1,5},{5... | collective-permute-start | bytes 393224 | tf_op jit(solution)/shard_map/ppermute | solution.py:404
  21.6 0.4 %shard_map.98.refs_1_ = f32[512,512]{1,0:T(8,128)S(1)} custom-call(bf16[512,256]{1,0:T(8,128)(2,1)S(1)} %get-tuple-element.52.scores_ref, bf16[512,128]{1,0:T(8,128)(2,1)S(1)} %get-tuple-element.51.turned_ref.refs_0_, bf16[128,512]{1,0:T(8,128)(2,1)S(1)} %shard_map.97._.refs_6_, f32[512,1024]{1,0:T(8,128)S(1)} %get-tuple-element.46.refs_6_.refs_0_, ...), custom_call_target="tpu_custom_call" | custom-call | flops 268435456 | tf_op jit(solution)/shard_map/pallas_call | solution.py:388
  22.0 0.2 shard_map.99
  22.2 0.5 %collective-permute-done.11.refs_6_ = bf16[128,512]{1,0:T(8,128)(2,1)S(1)} collective-permute-done((bf16[128,512]{1,0:T(8,128)(2,1)S(1)}, bf16[128,512]{1,0:T(8,128)(2,1)S(1)}, u32[]{:S(2)}, u32[]{:S(2)}) %collective-permute-start.11) | collective-permute-done | bytes 131104 | tf_op jit(solution)/shard_map/ppermute | solution.py:404
  22.7 0.3 shard_map.100
  22.9 0.7 %collective-permute-start.12 = (f32[1,512]{1,0:T(1,128)S(1)}, f32[1,512]{1,0:T(1,128)S(1)}, u32[]{:S(2)}, u32[]{:S(2)}) collective-permute-start(f32[1,512]{1,0:T(1,128)S(1)} %get-tuple-element.64.refs_0_), channel_id=1, source_target_pairs={{0,1},{1,2},{2,3},{3,0},{4,5},{5,6},{6,7},{7,4},{8,9},{9,10},{10,1... | collective-permute-start | bytes 6152 | tf_op jit(solution)/shard_map/ppermute | solution.py:413
  23.6 1.6 %collective-permute-start.13 = (f32[1,512]{1,0:T(1,128)S(1)}, f32[1,512]{1,0:T(1,128)S(1)}, u32[]{:S(2)}, u32[]{:S(2)}) collective-permute-start(f32[1,512]{1,0:T(1,128)S(1)} %get-tuple-element.64.refs_0_), channel_id=1, source_target_pairs={{0,2},{1,3},{2,0},{3,1},{4,6},{5,7},{6,4},{7,5},{8,10},{9,11},{10,... | collective-permute-start | bytes 6152 | tf_op jit(solution)/shard_map/ppermute | solution.py:413
  25.2 2.0 %collective-permute-start.14 = (f32[1,512]{1,0:T(1,128)S(1)}, f32[1,512]{1,0:T(1,128)S(1)}, u32[]{:S(2)}, u32[]{:S(2)}) collective-permute-start(f32[1,512]{1,0:T(1,128)S(1)} %get-tuple-element.64.refs_0_), channel_id=1, source_target_pairs={{0,3},{1,0},{2,1},{3,2},{4,7},{5,4},{6,5},{7,6},{8,11},{9,8},{10,9... | collective-permute-start | bytes 6152 | tf_op jit(solution)/shard_map/ppermute | solution.py:413
  27.2 1.1 %collective-permute-done.12.refs_1_ = f32[1,512]{1,0:T(1,128)S(1)} collective-permute-done((f32[1,512]{1,0:T(1,128)S(1)}, f32[1,512]{1,0:T(1,128)S(1)}, u32[]{:S(2)}, u32[]{:S(2)}) %collective-permute-start.12) | collective-permute-done | bytes 2080 | tf_op jit(solution)/shard_map/ppermute | solution.py:413
  28.3 0.6 %collective-permute-done.14.refs_3_ = f32[1,512]{1,0:T(1,128)S(1)} collective-permute-done((f32[1,512]{1,0:T(1,128)S(1)}, f32[1,512]{1,0:T(1,128)S(1)}, u32[]{:S(2)}, u32[]{:S(2)}) %collective-permute-start.14) | collective-permute-done | bytes 2080 | tf_op jit(solution)/shard_map/ppermute | solution.py:413
  28.9 1.2 %shard_map.101 = bf16[512,1024]{1,0:T(8,128)(2,1)} custom-call(f32[1,512]{1,0:T(1,128)S(1)} %get-tuple-element.64.refs_0_, f32[1,512]{1,0:T(1,128)S(1)} %collective-permute-done.12.refs_1_, f32[1,512]{1,0:T(1,128)S(1)} %collective-permute-done.13.refs_2_, f32[1,512]{1,0:T(1,128)S(1)} %collective-permute-done.14.refs_3_, ...), custom_call_target="tpu_custom_call" | custom-call | flops 268435456 | bytes 3145728 | tf_op jit(solution)/shard_map/pallas_call | solution.py:388
  (9 shorter events, 0.0 us)
Async XLA Ops:
  0.0 10.2 %collective-permute-start = (bf16[32,512]{1,0:T(8,128)(2,1)}, bf16[32,512]{1,0:T(8,128)(2,1)S(1)}, u32[]{:S(2)}, u32[]{:S(2)}) collective-permute-start(bf16[32,512]{1,0:T(8,128)(2,1)} %refs_6_.1), channel_id=1, source_target_pairs={{0,2},{1,3},{2,0},{3,1},{4,6},{5,7},{6,4},{7,5},{8,10},{9,11},{10,... | collective-permute-start | bytes 98312 | tf_op jit(solution)/shard_map/ppermute | solution.py:404
  4.0 6.2 %collective-permute-start.1 = (bf16[32,512]{1,0:T(8,128)(2,1)}, bf16[32,512]{1,0:T(8,128)(2,1)S(1)}, u32[]{:S(2)}, u32[]{:S(2)}) collective-permute-start(bf16[32,512]{1,0:T(8,128)(2,1)} %refs_6_.1), channel_id=1, source_target_pairs={{0,3},{1,2},{2,1},{3,0},{4,7},{5,6},{6,5},{7,4},{8,11},{9,10},{10,... | collective-permute-start | bytes 98312 | tf_op jit(solution)/shard_map/ppermute | solution.py:404
  5.4 4.9 %collective-permute-start.2 = (bf16[32,512]{1,0:T(8,128)(2,1)}, bf16[32,512]{1,0:T(8,128)(2,1)S(1)}, u32[]{:S(2)}, u32[]{:S(2)}) collective-permute-start(bf16[32,512]{1,0:T(8,128)(2,1)} %refs_6_.1), channel_id=1, source_target_pairs={{0,1},{1,0},{2,3},{3,2},{4,5},{5,4},{6,7},{7,6},{8,9},{9,8},{10,11... | collective-permute-start | bytes 98312 | tf_op jit(solution)/shard_map/ppermute | solution.py:404
  5.6 5.1 %collective-permute-start.3 = (bf16[32,512]{1,0:T(8,128)(2,1)}, bf16[32,512]{1,0:T(8,128)(2,1)S(1)}, u32[]{:S(2)}, u32[]{:S(2)}) collective-permute-start(bf16[32,512]{1,0:T(8,128)(2,1)} %refs_7_.1), channel_id=1, source_target_pairs={{0,2},{1,3},{2,0},{3,1},{4,6},{5,7},{6,4},{7,5},{8,10},{9,11},{10,... | collective-permute-start | bytes 98312 | tf_op jit(solution)/shard_map/ppermute | solution.py:404
  10.6 1.4 %collective-permute-start.5 = (bf16[136,512]{1,0:T(8,128)(2,1)S(1)}, bf16[136,512]{1,0:T(8,128)(2,1)S(1)}, u32[]{:S(2)}, u32[]{:S(2)}) collective-permute-start(bf16[136,512]{1,0:T(8,128)(2,1)S(1)} %get-tuple-element.45), channel_id=1, source_target_pairs={{0,4},{4,0},{8,12},{12,8},{16,20},{20,16},{24,28},{28,24},{1,5},{5... | collective-permute-start | bytes 417800 | tf_op jit(solution)/shard_map/ppermute | solution.py:404
  12.1 8.7 %collective-permute-start.6 = (bf16[136,512]{1,0:T(8,128)(2,1)S(1)}, bf16[136,512]{1,0:T(8,128)(2,1)S(1)}, u32[]{:S(2)}, u32[]{:S(2)}) collective-permute-start(bf16[136,512]{1,0:T(8,128)(2,1)S(1)} %shard_map.94.refs_5_), channel_id=1, source_target_pairs={{0,16},{4,20},{8,24},{12,28},{16,0},{20,4},{24,8},{28,12},{1,17},{... | collective-permute-start | bytes 417800 | tf_op jit(solution)/shard_map/ppermute | solution.py:404
  13.7 7.1 %collective-permute-start.7 = (bf16[136,512]{1,0:T(8,128)(2,1)S(1)}, bf16[136,512]{1,0:T(8,128)(2,1)S(1)}, u32[]{:S(2)}, u32[]{:S(2)}) collective-permute-start(bf16[136,512]{1,0:T(8,128)(2,1)S(1)} %shard_map.94.refs_5_), channel_id=1, source_target_pairs={{0,8},{4,12},{8,0},{12,4},{16,24},{20,28},{24,16},{28,20},{1,9},{5... | collective-permute-start | bytes 417800 | tf_op jit(solution)/shard_map/ppermute | solution.py:404
  15.2 5.9 %collective-permute-start.8 = (bf16[136,512]{1,0:T(8,128)(2,1)S(1)}, bf16[136,512]{1,0:T(8,128)(2,1)S(1)}, u32[]{:S(2)}, u32[]{:S(2)}) collective-permute-start(bf16[136,512]{1,0:T(8,128)(2,1)S(1)} %shard_map.94.refs_5_), channel_id=1, source_target_pairs={{0,24},{4,28},{24,8},{28,12},{8,16},{12,20},{16,0},{20,4},{1,25},{... | collective-permute-start | bytes 417800 | tf_op jit(solution)/shard_map/ppermute | solution.py:513
  15.7 5.5 %collective-permute-start.9 = (bf16[136,512]{1,0:T(8,128)(2,1)S(1)}, bf16[136,512]{1,0:T(8,128)(2,1)S(1)}, u32[]{:S(2)}, u32[]{:S(2)}) collective-permute-start(bf16[136,512]{1,0:T(8,128)(2,1)S(1)} %get-tuple-element.56._.mine_ref), channel_id=1, source_target_pairs={{0,4},{4,0},{8,12},{12,8},{16,20},{20,16},{24,28},{28,24},{1,5},{5... | collective-permute-start | bytes 417800 | tf_op jit(solution)/shard_map/ppermute | solution.py:404
  15.7 4.5 %collective-permute-start.4 = (bf16[64,512]{1,0:T(8,128)(2,1)S(1)}, bf16[64,512]{1,0:T(8,128)(2,1)S(1)}, u32[]{:S(2)}, u32[]{:S(2)}) collective-permute-start(bf16[64,512]{1,0:T(8,128)(2,1)S(1)} %shard_map.93._.refs_4_), channel_id=1, source_target_pairs={{0,1},{1,0},{2,3},{3,2},{4,5},{5,4},{6,7},{7,6},{8,9},{9,8},{10,11... | collective-permute-start | bytes 196616 | tf_op jit(solution)/shard_map/ppermute | solution.py:404
  20.8 1.8 %collective-permute-start.10 = (bf16[136,512]{1,0:T(8,128)(2,1)S(1)}, bf16[136,512]{1,0:T(8,128)(2,1)S(1)}, u32[]{:S(2)}, u32[]{:S(2)}) collective-permute-start(bf16[136,512]{1,0:T(8,128)(2,1)S(1)} %collective-permute-done.7.x_ref.refs_5_), channel_id=1, source_target_pairs={{0,4},{4,0},{8,12},{12,8},{16,20},{20,16},{24,28},{28,24},{1,5},{5... | collective-permute-start | bytes 417800 | tf_op jit(solution)/shard_map/ppermute | solution.py:404
  21.3 1.4 %collective-permute-start.11 = (bf16[128,512]{1,0:T(8,128)(2,1)S(1)}, bf16[128,512]{1,0:T(8,128)(2,1)S(1)}, u32[]{:S(2)}, u32[]{:S(2)}) collective-permute-start(bf16[128,512]{1,0:T(8,128)(2,1)S(1)} %shard_map.97._.refs_6_), channel_id=1, source_target_pairs={{0,4},{4,0},{8,12},{12,8},{16,20},{20,16},{24,28},{28,24},{1,5},{5... | collective-permute-start | bytes 393224 | tf_op jit(solution)/shard_map/ppermute | solution.py:404
  22.9 5.4 %collective-permute-start.12 = (f32[1,512]{1,0:T(1,128)S(1)}, f32[1,512]{1,0:T(1,128)S(1)}, u32[]{:S(2)}, u32[]{:S(2)}) collective-permute-start(f32[1,512]{1,0:T(1,128)S(1)} %get-tuple-element.64.refs_0_), channel_id=1, source_target_pairs={{0,1},{1,2},{2,3},{3,0},{4,5},{5,6},{6,7},{7,4},{8,9},{9,10},{10,1... | collective-permute-start | bytes 6152 | tf_op jit(solution)/shard_map/ppermute | solution.py:413
  23.6 4.7 %collective-permute-start.13 = (f32[1,512]{1,0:T(1,128)S(1)}, f32[1,512]{1,0:T(1,128)S(1)}, u32[]{:S(2)}, u32[]{:S(2)}) collective-permute-start(f32[1,512]{1,0:T(1,128)S(1)} %get-tuple-element.64.refs_0_), channel_id=1, source_target_pairs={{0,2},{1,3},{2,0},{3,1},{4,6},{5,7},{6,4},{7,5},{8,10},{9,11},{10,... | collective-permute-start | bytes 6152 | tf_op jit(solution)/shard_map/ppermute | solution.py:413
  25.2 3.6 %collective-permute-start.14 = (f32[1,512]{1,0:T(1,128)S(1)}, f32[1,512]{1,0:T(1,128)S(1)}, u32[]{:S(2)}, u32[]{:S(2)}) collective-permute-start(f32[1,512]{1,0:T(1,128)S(1)} %get-tuple-element.64.refs_0_), channel_id=1, source_target_pairs={{0,3},{1,0},{2,1},{3,2},{4,7},{5,4},{6,5},{7,6},{8,11},{9,8},{10,9... | collective-permute-start | bytes 6152 | tf_op jit(solution)/shard_map/ppermute | solution.py:413

commit v22 on v21

--- a/solution.py
+++ b/solution.py
@@ -13,6 +13,7 @@
 BLOCK = 256
 NORM_CHUNKS = 4
 FIRST_HOP = 2
+LATER_SHIFTS = (2, 1, 3)
 CYCLE = [(2 * chip + core, 2 * target + core) for chip, target in ((0, 3), (3, 1), (1, 2), (2, 0)) for core in (0, 1)]
 VMEM_LIMIT = 40 * 1024 * 1024
 
@@ -408,9 +409,16 @@
     return [flip(array, axis, mask) for mask in masks]
 
 
-def around(array, axis):
-    size = lax.axis_size(axis)
-    return [lax.ppermute(array, axis, [(i, (i + shift) % size) for i in range(size)]) for shift in range(1, size)]
+def around(array, paired):
+    shards, size = lax.axis_size("seq"), lax.axis_size("head")
+    received = []
+    for step in range(1, size):
+        pairs = []
+        for shard in range(shards):
+            shift = LATER_SHIFTS[step - 1] if paired and shard >= shards // 2 else step
+            pairs += [(shard * size + i, shard * size + (i + shift) % size) for i in range(size)]
+        received.append(lax.ppermute(array, ("seq", "head"), pairs))
+    return received
 
 
 def merged(older, newer, size):
@@ -550,7 +558,7 @@
             flops=4 * dense,
             bytes_accessed=12 * area,
         )
-    last = [sums, *around(sums, "head")]
+    last = [sums, *around(sums, pairs)]
     return call(
         functools.partial(norm_kernel, len(last), width * parts),
         shaped((tokens, width), bf16),

time: 30.6 us -> 30.7 us (level)
  no operation moved by 1% of the time
where the time goes in v22:
time: 30.7 us; the launch traced here: 30.1 us
  starting transfers between devices  17.4 us (57%)
  Pallas kernels  6.82 us (22%)
  waiting for transfers between devices  5.73 us (19%)
    ppermute x11, starting transfers between devices, flip(): lax.ppermute(array, axis, [(i, i ^ mask) for i in range(lax.axis_size(axi...  12.7 us
    pallas_call x11, Pallas kernels, call(): pl.pallas_call(kernel, out_shape=out_shape, in_specs=specs, out_specs=jax...  6.82 us
    ppermute x3, starting transfers between devices, around(): received.append(lax.ppermute(array, ('seq', 'head'), pairs))  4.3 us
    ppermute x11, waiting for transfers between devices, flip(): lax.ppermute(array, axis, [(i, i ^ mask) for i in range(lax.axis_size(axi...  3.85 us
    ppermute x3, waiting for transfers between devices, around(): received.append(lax.ppermute(array, ('seq', 'head'), pairs))  1.66 us
  transfers between devices with their start and end apart: 15, of which 6 were waited for; matrix products, arithmetic and copies ran while one was open for 0% of the time, Pallas kernels for 17%

profile of v22, /device:TPU:0, one launch (start us, length us, event | category | flops | bytes accessed | tf_op | source)
XLA Modules:
  0.0 30.1 jit_solution(4265257111155105047)
XLA Ops:
  0.0 4.0 %collective-permute-start = (bf16[32,512]{1,0:T(8,128)(2,1)}, bf16[32,512]{1,0:T(8,128)(2,1)S(1)}, u32[]{:S(2)}, u32[]{:S(2)}) collective-permute-start(bf16[32,512]{1,0:T(8,128)(2,1)} %refs_6_.1), channel_id=1, source_target_pairs={{0,2},{1,3},{2,0},{3,1},{4,6},{5,7},{6,4},{7,5},{8,10},{9,11},{10,... | collective-permute-start | bytes 98312 | tf_op jit(solution)/shard_map/ppermute | solution.py:405
  4.0 1.3 %collective-permute-start.1 = (bf16[32,512]{1,0:T(8,128)(2,1)}, bf16[32,512]{1,0:T(8,128)(2,1)S(1)}, u32[]{:S(2)}, u32[]{:S(2)}) collective-permute-start(bf16[32,512]{1,0:T(8,128)(2,1)} %refs_6_.1), channel_id=1, source_target_pairs={{0,3},{1,2},{2,1},{3,0},{4,7},{5,6},{6,5},{7,4},{8,11},{9,10},{10,... | collective-permute-start | bytes 98312 | tf_op jit(solution)/shard_map/ppermute | solution.py:405
  5.4 0.2 collective-permute-start.2
  5.6 2.8 %collective-permute-start.3 = (bf16[32,512]{1,0:T(8,128)(2,1)}, bf16[32,512]{1,0:T(8,128)(2,1)S(1)}, u32[]{:S(2)}, u32[]{:S(2)}) collective-permute-start(bf16[32,512]{1,0:T(8,128)(2,1)} %refs_7_.1), channel_id=1, source_target_pairs={{0,2},{1,3},{2,0},{3,1},{4,6},{5,7},{6,4},{7,5},{8,10},{9,11},{10,... | collective-permute-start | bytes 98312 | tf_op jit(solution)/shard_map/ppermute | solution.py:405
  8.4 1.8 %shard_map.91 = (bf16[512,1024]{1,0:T(8,128)(2,1)S(1)}, f32[16,512]{1,0:T(8,128)S(1)}, bf16[512,1024]{1,0:T(8,128)(2,1)S(1)}, bf16[512,1024]{1,0:T(8,128)(2,1)S(...) custom-call(f32[16,512]{1,0:T(8,128)} %refs_0_.1, ...), custom_call_target="tpu_custom_call" | custom-call | flops 4294967296 | bytes 2097152 | tf_op jit(solution)/shard_map/pallas_call | solution.py:389
  10.2 0.0 collective-permute-done.refs_1_
  10.2 0.0 collective-permute-done.1.refs_2_
  10.3 0.3 %shard_map.92 = (bf16[136,512]{1,0:T(8,128)(2,1)S(1)}, bf16[136,512]{1,0:T(8,128)(2,1)S(1)}, bf16[128,1024]{1,0:T(8,128)(2,1)S(1)}) custom-call(bf16[32,512]{1,0:T(8,128)(2,1)S(1)} %get-tuple-element.36.refs_0_, bf16[32,512]{1,0:T(8,128)(2,1)S(1)} %collective-permute-done.refs_1_, bf16[32,512]{1,0:T(8,128)(2,1)S(1)} %collective-permute-done.1.refs_2_, ...), custom_call_target="tpu_custom_call" | custom-call | flops 268435456 | tf_op jit(solution)/shard_map/pallas_call | solution.py:389
  10.6 0.1 collective-permute-start.5
  10.7 1.3 %collective-permute-done.5.theirs_ref.refs_9_.refs_4_ = bf16[136,512]{1,0:T(8,128)(2,1)S(1)} collective-permute-done((bf16[136,512]{1,0:T(8,128)(2,1)S(1)}, bf16[136,512]{1,0:T(8,128)(2,1)S(1)}, u32[]{:S(2)}, u32[]{:S(2)}) %collective-permute-start.5) | collective-permute-done | bytes 139296 | tf_op jit(solution)/shard_map/ppermute | solution.py:405
  12.0 0.1 shard_map.94.refs_5_
  12.1 1.6 %collective-permute-start.6 = (bf16[136,512]{1,0:T(8,128)(2,1)S(1)}, bf16[136,512]{1,0:T(8,128)(2,1)S(1)}, u32[]{:S(2)}, u32[]{:S(2)}) collective-permute-start(bf16[136,512]{1,0:T(8,128)(2,1)S(1)} %shard_map.94.refs_5_), channel_id=1, source_target_pairs={{0,16},{4,20},{8,24},{12,28},{16,0},{20,4},{24,8},{28,12},{1,17},{... | collective-permute-start | bytes 417800 | tf_op jit(solution)/shard_map/ppermute | solution.py:405
  13.7 1.5 %collective-permute-start.7 = (bf16[136,512]{1,0:T(8,128)(2,1)S(1)}, bf16[136,512]{1,0:T(8,128)(2,1)S(1)}, u32[]{:S(2)}, u32[]{:S(2)}) collective-permute-start(bf16[136,512]{1,0:T(8,128)(2,1)S(1)} %shard_map.94.refs_5_), channel_id=1, source_target_pairs={{0,8},{4,12},{8,0},{12,4},{16,24},{20,28},{24,16},{28,20},{1,9},{5... | collective-permute-start | bytes 417800 | tf_op jit(solution)/shard_map/ppermute | solution.py:405
  15.2 0.5 %collective-permute-start.8 = (bf16[136,512]{1,0:T(8,128)(2,1)S(1)}, bf16[136,512]{1,0:T(8,128)(2,1)S(1)}, u32[]{:S(2)}, u32[]{:S(2)}) collective-permute-start(bf16[136,512]{1,0:T(8,128)(2,1)S(1)} %shard_map.94.refs_5_), channel_id=1, source_target_pairs={{0,24},{4,28},{24,8},{28,12},{8,16},{12,20},{16,0},{20,4},{1,25},{... | collective-permute-start | bytes 417800 | tf_op jit(solution)/shard_map/ppermute | solution.py:521
  15.7 0.7 %collective-permute-start.4 = (bf16[64,512]{1,0:T(8,128)(2,1)S(1)}, bf16[64,512]{1,0:T(8,128)(2,1)S(1)}, u32[]{:S(2)}, u32[]{:S(2)}) collective-permute-start(bf16[64,512]{1,0:T(8,128)(2,1)S(1)} %shard_map.93._.refs_4_), channel_id=1, source_target_pairs={{0,1},{1,0},{2,3},{3,2},{4,5},{5,4},{6,7},{7,6},{8,9},{9,8},{10,11... | collective-permute-start | bytes 196616 | tf_op jit(solution)/shard_map/ppermute | solution.py:405
  16.3 1.8 %shard_map.95 = (f32[512,1024]{1,0:T(8,128)S(1)}, f32[512,1024]{1,0:T(8,128)S(1)}, bf16[3,512,1024]{2,1,0:T(8,128)(2,1)S(1)}, bf16[1,256,1024]{2,1,0:T(8,128)(2,1)S(1)}) custom-call(bf16[512,1024]{1,0:T(8,128)(2,1)S(1)} %get-tuple-element.41.refs_0_, bf16[512,1024]{1,0:T(8,128)(2,1)S(1)} %get-tuple-element.42.refs_1_, ...), custom_call_target="tpu_custom_call" | custom-call | flops 1342177280 | tf_op jit(solution)/shard_map/pallas_call | solution.py:389
  18.1 2.0 %collective-permute-done.4.refs_5_ = bf16[64,512]{1,0:T(8,128)(2,1)S(1)} collective-permute-done((bf16[64,512]{1,0:T(8,128)(2,1)S(1)}, bf16[64,512]{1,0:T(8,128)(2,1)S(1)}, u32[]{:S(2)}, u32[]{:S(2)}) %collective-permute-start.4) | collective-permute-done | bytes 65568 | tf_op jit(solution)/shard_map/ppermute | solution.py:405
  20.2 0.6 %shard_map.96 = (f32[512,512]{1,0:T(8,128)S(1)}, bf16[512,128]{1,0:T(8,128)(2,1)S(1)}, bf16[512,256]{1,0:T(8,128)(2,1)S(1)}) custom-call(bf16[32,512]{1,0:T(8,128)(2,1)S(1)} %get-tuple-element.36.refs_0_, bf16[32,512]{1,0:T(8,128)(2,1)S(1)} %collective-permute-done.refs_1_, bf16[32,512]{1,0:T(8,128)(2,1)S(1)} %collective-permute-done.1.refs_2_, ...), custom_call_target="tpu_custom_call" | custom-call | tf_op jit(solution)/shard_map/pallas_call | solution.py:389
  20.8 0.1 collective-permute-start.10
  20.9 0.2 collective-permute-done.8.diagonal_ref
  21.1 0.1 shard_map.97._.refs_6_
  21.3 0.3 %collective-permute-start.11 = (bf16[128,512]{1,0:T(8,128)(2,1)S(1)}, bf16[128,512]{1,0:T(8,128)(2,1)S(1)}, u32[]{:S(2)}, u32[]{:S(2)}) collective-permute-start(bf16[128,512]{1,0:T(8,128)(2,1)S(1)} %shard_map.97._.refs_6_), channel_id=1, source_target_pairs={{0,4},{4,0},{8,12},{12,8},{16,20},{20,16},{24,28},{28,24},{1,5},{5... | collective-permute-start | bytes 393224 | tf_op jit(solution)/shard_map/ppermute | solution.py:405
  21.6 0.4 %shard_map.98.refs_1_ = f32[512,512]{1,0:T(8,128)S(1)} custom-call(bf16[512,256]{1,0:T(8,128)(2,1)S(1)} %get-tuple-element.52.scores_ref, bf16[512,128]{1,0:T(8,128)(2,1)S(1)} %get-tuple-element.51.turned_ref.refs_0_, bf16[128,512]{1,0:T(8,128)(2,1)S(1)} %shard_map.97._.refs_6_, f32[512,1024]{1,0:T(8,128)S(1)} %get-tuple-element.46.refs_6_.refs_0_, ...), custom_call_target="tpu_custom_call" | custom-call | flops 268435456 | tf_op jit(solution)/shard_map/pallas_call | solution.py:389
  22.0 0.2 shard_map.99
  22.2 0.5 %collective-permute-done.11.refs_6_ = bf16[128,512]{1,0:T(8,128)(2,1)S(1)} collective-permute-done((bf16[128,512]{1,0:T(8,128)(2,1)S(1)}, bf16[128,512]{1,0:T(8,128)(2,1)S(1)}, u32[]{:S(2)}, u32[]{:S(2)}) %collective-permute-start.11) | collective-permute-done | bytes 131104 | tf_op jit(solution)/shard_map/ppermute | solution.py:405
  22.7 0.3 shard_map.100
  22.9 0.7 %collective-permute-start.12 = (f32[1,512]{1,0:T(1,128)S(1)}, f32[1,512]{1,0:T(1,128)S(1)}, u32[]{:S(2)}, u32[]{:S(2)}) collective-permute-start(f32[1,512]{1,0:T(1,128)S(1)} %get-tuple-element.64.refs_0_), channel_id=1, source_target_pairs={{0,1},{1,2},{2,3},{3,0},{4,5},{5,6},{6,7},{7,4},{8,9},{9,10},{10,1... | collective-permute-start | bytes 6152 | tf_op jit(solution)/shard_map/ppermute | solution.py:420
  23.6 1.6 %collective-permute-start.13 = (f32[1,512]{1,0:T(1,128)S(1)}, f32[1,512]{1,0:T(1,128)S(1)}, u32[]{:S(2)}, u32[]{:S(2)}) collective-permute-start(f32[1,512]{1,0:T(1,128)S(1)} %get-tuple-element.64.refs_0_), channel_id=1, source_target_pairs={{0,2},{1,3},{2,0},{3,1},{4,6},{5,7},{6,4},{7,5},{8,10},{9,11},{10,... | collective-permute-start | bytes 6152 | tf_op jit(solution)/shard_map/ppermute | solution.py:420
  25.2 2.0 %collective-permute-start.14 = (f32[1,512]{1,0:T(1,128)S(1)}, f32[1,512]{1,0:T(1,128)S(1)}, u32[]{:S(2)}, u32[]{:S(2)}) collective-permute-start(f32[1,512]{1,0:T(1,128)S(1)} %get-tuple-element.64.refs_0_), channel_id=1, source_target_pairs={{0,3},{1,0},{2,1},{3,2},{4,7},{5,4},{6,5},{7,6},{8,11},{9,8},{10,9... | collective-permute-start | bytes 6152 | tf_op jit(solution)/shard_map/ppermute | solution.py:420
  27.2 1.1 %collective-permute-done.12.refs_1_ = f32[1,512]{1,0:T(1,128)S(1)} collective-permute-done((f32[1,512]{1,0:T(1,128)S(1)}, f32[1,512]{1,0:T(1,128)S(1)}, u32[]{:S(2)}, u32[]{:S(2)}) %collective-permute-start.12) | collective-permute-done | bytes 2080 | tf_op jit(solution)/shard_map/ppermute | solution.py:420
  28.3 0.6 %collective-permute-done.14.refs_3_ = f32[1,512]{1,0:T(1,128)S(1)} collective-permute-done((f32[1,512]{1,0:T(1,128)S(1)}, f32[1,512]{1,0:T(1,128)S(1)}, u32[]{:S(2)}, u32[]{:S(2)}) %collective-permute-start.14) | collective-permute-done | bytes 2080 | tf_op jit(solution)/shard_map/ppermute | solution.py:420
  28.9 1.2 %shard_map.101 = bf16[512,1024]{1,0:T(8,128)(2,1)} custom-call(f32[1,512]{1,0:T(1,128)S(1)} %get-tuple-element.64.refs_0_, f32[1,512]{1,0:T(1,128)S(1)} %collective-permute-done.12.refs_1_, f32[1,512]{1,0:T(1,128)S(1)} %collective-permute-done.13.refs_2_, f32[1,512]{1,0:T(1,128)S(1)} %collective-permute-done.14.refs_3_, ...), custom_call_target="tpu_custom_call" | custom-call | flops 268435456 | bytes 3145728 | tf_op jit(solution)/shard_map/pallas_call | solution.py:389
  (9 shorter events, 0.0 us)
Async XLA Ops:
  0.0 10.2 %collective-permute-start = (bf16[32,512]{1,0:T(8,128)(2,1)}, bf16[32,512]{1,0:T(8,128)(2,1)S(1)}, u32[]{:S(2)}, u32[]{:S(2)}) collective-permute-start(bf16[32,512]{1,0:T(8,128)(2,1)} %refs_6_.1), channel_id=1, source_target_pairs={{0,2},{1,3},{2,0},{3,1},{4,6},{5,7},{6,4},{7,5},{8,10},{9,11},{10,... | collective-permute-start | bytes 98312 | tf_op jit(solution)/shard_map/ppermute | solution.py:405
  4.0 6.2 %collective-permute-start.1 = (bf16[32,512]{1,0:T(8,128)(2,1)}, bf16[32,512]{1,0:T(8,128)(2,1)S(1)}, u32[]{:S(2)}, u32[]{:S(2)}) collective-permute-start(bf16[32,512]{1,0:T(8,128)(2,1)} %refs_6_.1), channel_id=1, source_target_pairs={{0,3},{1,2},{2,1},{3,0},{4,7},{5,6},{6,5},{7,4},{8,11},{9,10},{10,... | collective-permute-start | bytes 98312 | tf_op jit(solution)/shard_map/ppermute | solution.py:405
  5.4 4.9 %collective-permute-start.2 = (bf16[32,512]{1,0:T(8,128)(2,1)}, bf16[32,512]{1,0:T(8,128)(2,1)S(1)}, u32[]{:S(2)}, u32[]{:S(2)}) collective-permute-start(bf16[32,512]{1,0:T(8,128)(2,1)} %refs_6_.1), channel_id=1, source_target_pairs={{0,1},{1,0},{2,3},{3,2},{4,5},{5,4},{6,7},{7,6},{8,9},{9,8},{10,11... | collective-permute-start | bytes 98312 | tf_op jit(solution)/shard_map/ppermute | solution.py:405
  5.6 5.1 %collective-permute-start.3 = (bf16[32,512]{1,0:T(8,128)(2,1)}, bf16[32,512]{1,0:T(8,128)(2,1)S(1)}, u32[]{:S(2)}, u32[]{:S(2)}) collective-permute-start(bf16[32,512]{1,0:T(8,128)(2,1)} %refs_7_.1), channel_id=1, source_target_pairs={{0,2},{1,3},{2,0},{3,1},{4,6},{5,7},{6,4},{7,5},{8,10},{9,11},{10,... | collective-permute-start | bytes 98312 | tf_op jit(solution)/shard_map/ppermute | solution.py:405
  10.6 1.4 %collective-permute-start.5 = (bf16[136,512]{1,0:T(8,128)(2,1)S(1)}, bf16[136,512]{1,0:T(8,128)(2,1)S(1)}, u32[]{:S(2)}, u32[]{:S(2)}) collective-permute-start(bf16[136,512]{1,0:T(8,128)(2,1)S(1)} %get-tuple-element.45), channel_id=1, source_target_pairs={{0,4},{4,0},{8,12},{12,8},{16,20},{20,16},{24,28},{28,24},{1,5},{5... | collective-permute-start | bytes 417800 | tf_op jit(solution)/shard_map/ppermute | solution.py:405
  12.1 8.7 %collective-permute-start.6 = (bf16[136,512]{1,0:T(8,128)(2,1)S(1)}, bf16[136,512]{1,0:T(8,128)(2,1)S(1)}, u32[]{:S(2)}, u32[]{:S(2)}) collective-permute-start(bf16[136,512]{1,0:T(8,128)(2,1)S(1)} %shard_map.94.refs_5_), channel_id=1, source_target_pairs={{0,16},{4,20},{8,24},{12,28},{16,0},{20,4},{24,8},{28,12},{1,17},{... | collective-permute-start | bytes 417800 | tf_op jit(solution)/shard_map/ppermute | solution.py:405
  13.7 7.1 %collective-permute-start.7 = (bf16[136,512]{1,0:T(8,128)(2,1)S(1)}, bf16[136,512]{1,0:T(8,128)(2,1)S(1)}, u32[]{:S(2)}, u32[]{:S(2)}) collective-permute-start(bf16[136,512]{1,0:T(8,128)(2,1)S(1)} %shard_map.94.refs_5_), channel_id=1, source_target_pairs={{0,8},{4,12},{8,0},{12,4},{16,24},{20,28},{24,16},{28,20},{1,9},{5... | collective-permute-start | bytes 417800 | tf_op jit(solution)/shard_map/ppermute | solution.py:405
  15.2 5.9 %collective-permute-start.8 = (bf16[136,512]{1,0:T(8,128)(2,1)S(1)}, bf16[136,512]{1,0:T(8,128)(2,1)S(1)}, u32[]{:S(2)}, u32[]{:S(2)}) collective-permute-start(bf16[136,512]{1,0:T(8,128)(2,1)S(1)} %shard_map.94.refs_5_), channel_id=1, source_target_pairs={{0,24},{4,28},{24,8},{28,12},{8,16},{12,20},{16,0},{20,4},{1,25},{... | collective-permute-start | bytes 417800 | tf_op jit(solution)/shard_map/ppermute | solution.py:521
  15.7 5.5 %collective-permute-start.9 = (bf16[136,512]{1,0:T(8,128)(2,1)S(1)}, bf16[136,512]{1,0:T(8,128)(2,1)S(1)}, u32[]{:S(2)}, u32[]{:S(2)}) collective-permute-start(bf16[136,512]{1,0:T(8,128)(2,1)S(1)} %get-tuple-element.56._.mine_ref), channel_id=1, source_target_pairs={{0,4},{4,0},{8,12},{12,8},{16,20},{20,16},{24,28},{28,24},{1,5},{5... | collective-permute-start | bytes 417800 | tf_op jit(solution)/shard_map/ppermute | solution.py:405
  15.7 4.5 %collective-permute-start.4 = (bf16[64,512]{1,0:T(8,128)(2,1)S(1)}, bf16[64,512]{1,0:T(8,128)(2,1)S(1)}, u32[]{:S(2)}, u32[]{:S(2)}) collective-permute-start(bf16[64,512]{1,0:T(8,128)(2,1)S(1)} %shard_map.93._.refs_4_), channel_id=1, source_target_pairs={{0,1},{1,0},{2,3},{3,2},{4,5},{5,4},{6,7},{7,6},{8,9},{9,8},{10,11... | collective-permute-start | bytes 196616 | tf_op jit(solution)/shard_map/ppermute | solution.py:405
  20.8 1.8 %collective-permute-start.10 = (bf16[136,512]{1,0:T(8,128)(2,1)S(1)}, bf16[136,512]{1,0:T(8,128)(2,1)S(1)}, u32[]{:S(2)}, u32[]{:S(2)}) collective-permute-start(bf16[136,512]{1,0:T(8,128)(2,1)S(1)} %collective-permute-done.7.x_ref.refs_5_), channel_id=1, source_target_pairs={{0,4},{4,0},{8,12},{12,8},{16,20},{20,16},{24,28},{28,24},{1,5},{5... | collective-permute-start | bytes 417800 | tf_op jit(solution)/shard_map/ppermute | solution.py:405
  21.3 1.4 %collective-permute-start.11 = (bf16[128,512]{1,0:T(8,128)(2,1)S(1)}, bf16[128,512]{1,0:T(8,128)(2,1)S(1)}, u32[]{:S(2)}, u32[]{:S(2)}) collective-permute-start(bf16[128,512]{1,0:T(8,128)(2,1)S(1)} %shard_map.97._.refs_6_), channel_id=1, source_target_pairs={{0,4},{4,0},{8,12},{12,8},{16,20},{20,16},{24,28},{28,24},{1,5},{5... | collective-permute-start | bytes 393224 | tf_op jit(solution)/shard_map/ppermute | solution.py:405
  22.9 5.4 %collective-permute-start.12 = (f32[1,512]{1,0:T(1,128)S(1)}, f32[1,512]{1,0:T(1,128)S(1)}, u32[]{:S(2)}, u32[]{:S(2)}) collective-permute-start(f32[1,512]{1,0:T(1,128)S(1)} %get-tuple-element.64.refs_0_), channel_id=1, source_target_pairs={{0,1},{1,2},{2,3},{3,0},{4,5},{5,6},{6,7},{7,4},{8,9},{9,10},{10,1... | collective-permute-start | bytes 6152 | tf_op jit(solution)/shard_map/ppermute | solution.py:420
  23.6 4.7 %collective-permute-start.13 = (f32[1,512]{1,0:T(1,128)S(1)}, f32[1,512]{1,0:T(1,128)S(1)}, u32[]{:S(2)}, u32[]{:S(2)}) collective-permute-start(f32[1,512]{1,0:T(1,128)S(1)} %get-tuple-element.64.refs_0_), channel_id=1, source_target_pairs={{0,2},{1,3},{2,0},{3,1},{4,6},{5,7},{6,4},{7,5},{8,10},{9,11},{10,... | collective-permute-start | bytes 6152 | tf_op jit(solution)/shard_map/ppermute | solution.py:420
  25.2 3.6 %collective-permute-start.14 = (f32[1,512]{1,0:T(1,128)S(1)}, f32[1,512]{1,0:T(1,128)S(1)}, u32[]{:S(2)}, u32[]{:S(2)}) collective-permute-start(f32[1,512]{1,0:T(1,128)S(1)} %get-tuple-element.64.refs_0_), channel_id=1, source_target_pairs={{0,3},{1,0},{2,1},{3,2},{4,7},{5,4},{6,5},{7,6},{8,11},{9,8},{10,9... | collective-permute-start | bytes 6152 | tf_op jit(solution)/shard_map/ppermute | solution.py:420

commit v23 on v22

--- a/solution.py
+++ b/solution.py
@@ -9,7 +9,7 @@
 
 P_SIZE = 64
 GROUP = 256
-DECAY_ROWS = 8
+DECAY_ROWS = 16
 BLOCK = 256
 NORM_CHUNKS = 4
 FIRST_HOP = 2

time: 30.7 us -> 31.1 us (1.013)
  waiting for transfers between devices: 5.73 us -> 6.71 us
  starting transfers between devices: 17.4 us -> 16.8 us
    ppermute x3, starting transfers between devices: 4.3 us -> 3.94 us  [around(): received.append(lax.ppermute(array, ('seq', 'head'), pairs))]
    ppermute x3, waiting for transfers between devices: 1.66 us -> 2.02 us  [around(): received.append(lax.ppermute(array, ('seq', 'head'), pairs))]
    ppermute x1, waiting for transfers between devices: 0.22 us -> 0.57 us  [on_device(): lax.ppermute(message, 'seq', CYCLE)]
where the time goes in v23:
time: 31.1 us; the launch traced here: 30.5 us
  starting transfers between devices  16.8 us (54%)
  Pallas kernels  6.81 us (22%)
  waiting for transfers between devices  6.71 us (22%)
    ppermute x11, starting transfers between devices, flip(): lax.ppermute(array, axis, [(i, i ^ mask) for i in range(lax.axis_size(axi...  12.4 us
    pallas_call x11, Pallas kernels, call(): pl.pallas_call(kernel, out_shape=out_shape, in_specs=specs, out_specs=jax...  6.81 us
    ppermute x11, waiting for transfers between devices, flip(): lax.ppermute(array, axis, [(i, i ^ mask) for i in range(lax.axis_size(axi...  4.12 us
    ppermute x3, starting transfers between devices, around(): received.append(lax.ppermute(array, ('seq', 'head'), pairs))  3.94 us
    ppermute x3, waiting for transfers between devices, around(): received.append(lax.ppermute(array, ('seq', 'head'), pairs))  2.02 us
  transfers between devices with their start and end apart: 15, of which 6 were waited for; matrix products, arithmetic and copies ran while one was open for 0% of the time, Pallas kernels for 17%

profile of v23, /device:TPU:0, one launch (start us, length us, event | category | flops | bytes accessed | tf_op | source)
XLA Modules:
  0.0 30.5 jit_solution(4112333164400919174)
XLA Ops:
  0.0 4.0 %collective-permute-start = (bf16[32,512]{1,0:T(8,128)(2,1)}, bf16[32,512]{1,0:T(8,128)(2,1)S(1)}, u32[]{:S(2)}, u32[]{:S(2)}) collective-permute-start(bf16[32,512]{1,0:T(8,128)(2,1)} %refs_6_.1), channel_id=1, source_target_pairs={{0,2},{1,3},{2,0},{3,1},{4,6},{5,7},{6,4},{7,5},{8,10},{9,11},{10,... | collective-permute-start | bytes 98312 | tf_op jit(solution)/shard_map/ppermute | solution.py:405
  4.0 1.3 %collective-permute-start.1 = (bf16[32,512]{1,0:T(8,128)(2,1)}, bf16[32,512]{1,0:T(8,128)(2,1)S(1)}, u32[]{:S(2)}, u32[]{:S(2)}) collective-permute-start(bf16[32,512]{1,0:T(8,128)(2,1)} %refs_6_.1), channel_id=1, source_target_pairs={{0,3},{1,2},{2,1},{3,0},{4,7},{5,6},{6,5},{7,4},{8,11},{9,10},{10,... | collective-permute-start | bytes 98312 | tf_op jit(solution)/shard_map/ppermute | solution.py:405
  5.4 0.2 collective-permute-start.2
  5.6 2.8 %collective-permute-start.3 = (bf16[32,512]{1,0:T(8,128)(2,1)}, bf16[32,512]{1,0:T(8,128)(2,1)S(1)}, u32[]{:S(2)}, u32[]{:S(2)}) collective-permute-start(bf16[32,512]{1,0:T(8,128)(2,1)} %refs_7_.1), channel_id=1, source_target_pairs={{0,2},{1,3},{2,0},{3,1},{4,6},{5,7},{6,4},{7,5},{8,10},{9,11},{10,... | collective-permute-start | bytes 98312 | tf_op jit(solution)/shard_map/ppermute | solution.py:405
  8.4 1.8 %shard_map.91 = (bf16[512,1024]{1,0:T(8,128)(2,1)S(1)}, f32[16,512]{1,0:T(8,128)S(1)}, bf16[512,1024]{1,0:T(8,128)(2,1)S(1)}, bf16[512,1024]{1,0:T(8,128)(2,1)S(...) custom-call(f32[16,512]{1,0:T(8,128)} %refs_0_.1, ...), custom_call_target="tpu_custom_call" | custom-call | flops 4294967296 | bytes 2097152 | tf_op jit(solution)/shard_map/pallas_call | solution.py:389
  10.2 0.0 collective-permute-done.refs_1_
  10.2 0.0 collective-permute-done.1.refs_2_
  10.3 0.3 %shard_map.92 = (bf16[144,512]{1,0:T(8,128)(2,1)S(1)}, bf16[144,512]{1,0:T(8,128)(2,1)S(1)}, bf16[128,1024]{1,0:T(8,128)(2,1)S(1)}) custom-call(bf16[32,512]{1,0:T(8,128)(2,1)S(1)} %get-tuple-element.36.refs_0_, bf16[32,512]{1,0:T(8,128)(2,1)S(1)} %collective-permute-done.refs_1_, bf16[32,512]{1,0:T(8,128)(2,1)S(1)} %collective-permute-done.1.refs_2_, ...), custom_call_target="tpu_custom_call" | custom-call | flops 268435456 | tf_op jit(solution)/shard_map/pallas_call | solution.py:389
  10.6 0.1 collective-permute-start.5
  10.7 1.3 %collective-permute-done.5.theirs_ref.refs_9_.refs_4_ = bf16[144,512]{1,0:T(8,128)(2,1)S(1)} collective-permute-done((bf16[144,512]{1,0:T(8,128)(2,1)S(1)}, bf16[144,512]{1,0:T(8,128)(2,1)S(1)}, u32[]{:S(2)}, u32[]{:S(2)}) %collective-permute-start.5) | collective-permute-done | bytes 147488 | tf_op jit(solution)/shard_map/ppermute | solution.py:405
  12.1 0.1 shard_map.94.refs_5_
  12.1 1.6 %collective-permute-start.6 = (bf16[144,512]{1,0:T(8,128)(2,1)S(1)}, bf16[144,512]{1,0:T(8,128)(2,1)S(1)}, u32[]{:S(2)}, u32[]{:S(2)}) collective-permute-start(bf16[144,512]{1,0:T(8,128)(2,1)S(1)} %shard_map.94.refs_5_), channel_id=1, source_target_pairs={{0,16},{4,20},{8,24},{12,28},{16,0},{20,4},{24,8},{28,12},{1,17},{... | collective-permute-start | bytes 442376 | tf_op jit(solution)/shard_map/ppermute | solution.py:405
  13.7 1.5 %collective-permute-start.7 = (bf16[144,512]{1,0:T(8,128)(2,1)S(1)}, bf16[144,512]{1,0:T(8,128)(2,1)S(1)}, u32[]{:S(2)}, u32[]{:S(2)}) collective-permute-start(bf16[144,512]{1,0:T(8,128)(2,1)S(1)} %shard_map.94.refs_5_), channel_id=1, source_target_pairs={{0,8},{4,12},{8,0},{12,4},{16,24},{20,28},{24,16},{28,20},{1,9},{5... | collective-permute-start | bytes 442376 | tf_op jit(solution)/shard_map/ppermute | solution.py:405
  15.2 0.5 %collective-permute-start.8 = (bf16[144,512]{1,0:T(8,128)(2,1)S(1)}, bf16[144,512]{1,0:T(8,128)(2,1)S(1)}, u32[]{:S(2)}, u32[]{:S(2)}) collective-permute-start(bf16[144,512]{1,0:T(8,128)(2,1)S(1)} %shard_map.94.refs_5_), channel_id=1, source_target_pairs={{0,24},{4,28},{24,8},{28,12},{8,16},{12,20},{16,0},{20,4},{1,25},{... | collective-permute-start | bytes 442376 | tf_op jit(solution)/shard_map/ppermute | solution.py:521
  15.7 0.7 %collective-permute-start.4 = (bf16[64,512]{1,0:T(8,128)(2,1)S(1)}, bf16[64,512]{1,0:T(8,128)(2,1)S(1)}, u32[]{:S(2)}, u32[]{:S(2)}) collective-permute-start(bf16[64,512]{1,0:T(8,128)(2,1)S(1)} %shard_map.93._.refs_4_), channel_id=1, source_target_pairs={{0,1},{1,0},{2,3},{3,2},{4,5},{5,4},{6,7},{7,6},{8,9},{9,8},{10,11... | collective-permute-start | bytes 196616 | tf_op jit(solution)/shard_map/ppermute | solution.py:405
  16.4 1.8 %shard_map.95 = (f32[512,1024]{1,0:T(8,128)S(1)}, f32[512,1024]{1,0:T(8,128)S(1)}, bf16[3,512,1024]{2,1,0:T(8,128)(2,1)S(1)}, bf16[1,256,1024]{2,1,0:T(8,128)(2,1)S(1)}) custom-call(bf16[512,1024]{1,0:T(8,128)(2,1)S(1)} %get-tuple-element.41.refs_0_, bf16[512,1024]{1,0:T(8,128)(2,1)S(1)} %get-tuple-element.42.refs_1_, ...), custom_call_target="tpu_custom_call" | custom-call | flops 1342177280 | tf_op jit(solution)/shard_map/pallas_call | solution.py:389
  18.1 2.1 %collective-permute-done.4.refs_5_ = bf16[64,512]{1,0:T(8,128)(2,1)S(1)} collective-permute-done((bf16[64,512]{1,0:T(8,128)(2,1)S(1)}, bf16[64,512]{1,0:T(8,128)(2,1)S(1)}, u32[]{:S(2)}, u32[]{:S(2)}) %collective-permute-start.4) | collective-permute-done | bytes 65568 | tf_op jit(solution)/shard_map/ppermute | solution.py:405
  20.2 0.6 %shard_map.96 = (f32[512,512]{1,0:T(8,128)S(1)}, bf16[512,128]{1,0:T(8,128)(2,1)S(1)}, bf16[512,256]{1,0:T(8,128)(2,1)S(1)}) custom-call(bf16[32,512]{1,0:T(8,128)(2,1)S(1)} %get-tuple-element.36.refs_0_, bf16[32,512]{1,0:T(8,128)(2,1)S(1)} %collective-permute-done.refs_1_, bf16[32,512]{1,0:T(8,128)(2,1)S(1)} %collective-permute-done.1.refs_2_, ...), custom_call_target="tpu_custom_call" | custom-call | tf_op jit(solution)/shard_map/pallas_call | solution.py:389
  20.8 0.1 collective-permute-start.10
  20.9 0.6 %collective-permute-done.8.diagonal_ref = bf16[144,512]{1,0:T(8,128)(2,1)S(1)} collective-permute-done((bf16[144,512]{1,0:T(8,128)(2,1)S(1)}, bf16[144,512]{1,0:T(8,128)(2,1)S(1)}, u32[]{:S(2)}, u32[]{:S(2)}) %collective-permute-start.8) | collective-permute-done | bytes 147488 | tf_op jit(solution)/shard_map/ppermute | solution.py:521
  21.5 0.1 shard_map.97._.refs_6_
  21.6 0.1 collective-permute-start.11
  21.7 0.4 %shard_map.98.refs_1_ = f32[512,512]{1,0:T(8,128)S(1)} custom-call(bf16[512,256]{1,0:T(8,128)(2,1)S(1)} %get-tuple-element.52.scores_ref, bf16[512,128]{1,0:T(8,128)(2,1)S(1)} %get-tuple-element.51.turned_ref.refs_0_, bf16[128,512]{1,0:T(8,128)(2,1)S(1)} %shard_map.97._.refs_6_, f32[512,1024]{1,0:T(8,128)S(1)} %get-tuple-element.46.refs_6_.refs_0_, ...), custom_call_target="tpu_custom_call" | custom-call | flops 268435456 | tf_op jit(solution)/shard_map/pallas_call | solution.py:389
  22.1 0.2 shard_map.99
  22.3 0.7 %collective-permute-done.11.refs_6_ = bf16[128,512]{1,0:T(8,128)(2,1)S(1)} collective-permute-done((bf16[128,512]{1,0:T(8,128)(2,1)S(1)}, bf16[128,512]{1,0:T(8,128)(2,1)S(1)}, u32[]{:S(2)}, u32[]{:S(2)}) %collective-permute-start.11) | collective-permute-done | bytes 131104 | tf_op jit(solution)/shard_map/ppermute | solution.py:405
  23.0 0.3 shard_map.100
  23.3 0.7 %collective-permute-start.12 = (f32[1,512]{1,0:T(1,128)S(1)}, f32[1,512]{1,0:T(1,128)S(1)}, u32[]{:S(2)}, u32[]{:S(2)}) collective-permute-start(f32[1,512]{1,0:T(1,128)S(1)} %get-tuple-element.64.refs_0_), channel_id=1, source_target_pairs={{0,1},{1,2},{2,3},{3,0},{4,5},{5,6},{6,7},{7,4},{8,9},{9,10},{10,1... | collective-permute-start | bytes 6152 | tf_op jit(solution)/shard_map/ppermute | solution.py:420
  24.0 1.6 %collective-permute-start.13 = (f32[1,512]{1,0:T(1,128)S(1)}, f32[1,512]{1,0:T(1,128)S(1)}, u32[]{:S(2)}, u32[]{:S(2)}) collective-permute-start(f32[1,512]{1,0:T(1,128)S(1)} %get-tuple-element.64.refs_0_), channel_id=1, source_target_pairs={{0,2},{1,3},{2,0},{3,1},{4,6},{5,7},{6,4},{7,5},{8,10},{9,11},{10,... | collective-permute-start | bytes 6152 | tf_op jit(solution)/shard_map/ppermute | solution.py:420
  25.6 1.6 %collective-permute-start.14 = (f32[1,512]{1,0:T(1,128)S(1)}, f32[1,512]{1,0:T(1,128)S(1)}, u32[]{:S(2)}, u32[]{:S(2)}) collective-permute-start(f32[1,512]{1,0:T(1,128)S(1)} %get-tuple-element.64.refs_0_), channel_id=1, source_target_pairs={{0,3},{1,0},{2,1},{3,2},{4,7},{5,4},{6,5},{7,6},{8,11},{9,8},{10,9... | collective-permute-start | bytes 6152 | tf_op jit(solution)/shard_map/ppermute | solution.py:420
  27.2 1.5 %collective-permute-done.12.refs_1_ = f32[1,512]{1,0:T(1,128)S(1)} collective-permute-done((f32[1,512]{1,0:T(1,128)S(1)}, f32[1,512]{1,0:T(1,128)S(1)}, u32[]{:S(2)}, u32[]{:S(2)}) %collective-permute-start.12) | collective-permute-done | bytes 2080 | tf_op jit(solution)/shard_map/ppermute | solution.py:420
  28.7 0.6 %collective-permute-done.14.refs_3_ = f32[1,512]{1,0:T(1,128)S(1)} collective-permute-done((f32[1,512]{1,0:T(1,128)S(1)}, f32[1,512]{1,0:T(1,128)S(1)}, u32[]{:S(2)}, u32[]{:S(2)}) %collective-permute-start.14) | collective-permute-done | bytes 2080 | tf_op jit(solution)/shard_map/ppermute | solution.py:420
  29.2 1.2 %shard_map.101 = bf16[512,1024]{1,0:T(8,128)(2,1)} custom-call(f32[1,512]{1,0:T(1,128)S(1)} %get-tuple-element.64.refs_0_, f32[1,512]{1,0:T(1,128)S(1)} %collective-permute-done.12.refs_1_, f32[1,512]{1,0:T(1,128)S(1)} %collective-permute-done.13.refs_2_, f32[1,512]{1,0:T(1,128)S(1)} %collective-permute-done.14.refs_3_, ...), custom_call_target="tpu_custom_call" | custom-call | flops 268435456 | bytes 3145728 | tf_op jit(solution)/shard_map/pallas_call | solution.py:389
  (9 shorter events, 0.0 us)
Async XLA Ops:
  0.0 10.2 %collective-permute-start = (bf16[32,512]{1,0:T(8,128)(2,1)}, bf16[32,512]{1,0:T(8,128)(2,1)S(1)}, u32[]{:S(2)}, u32[]{:S(2)}) collective-permute-start(bf16[32,512]{1,0:T(8,128)(2,1)} %refs_6_.1), channel_id=1, source_target_pairs={{0,2},{1,3},{2,0},{3,1},{4,6},{5,7},{6,4},{7,5},{8,10},{9,11},{10,... | collective-permute-start | bytes 98312 | tf_op jit(solution)/shard_map/ppermute | solution.py:405
  4.0 6.2 %collective-permute-start.1 = (bf16[32,512]{1,0:T(8,128)(2,1)}, bf16[32,512]{1,0:T(8,128)(2,1)S(1)}, u32[]{:S(2)}, u32[]{:S(2)}) collective-permute-start(bf16[32,512]{1,0:T(8,128)(2,1)} %refs_6_.1), channel_id=1, source_target_pairs={{0,3},{1,2},{2,1},{3,0},{4,7},{5,6},{6,5},{7,4},{8,11},{9,10},{10,... | collective-permute-start | bytes 98312 | tf_op jit(solution)/shard_map/ppermute | solution.py:405
  5.4 4.9 %collective-permute-start.2 = (bf16[32,512]{1,0:T(8,128)(2,1)}, bf16[32,512]{1,0:T(8,128)(2,1)S(1)}, u32[]{:S(2)}, u32[]{:S(2)}) collective-permute-start(bf16[32,512]{1,0:T(8,128)(2,1)} %refs_6_.1), channel_id=1, source_target_pairs={{0,1},{1,0},{2,3},{3,2},{4,5},{5,4},{6,7},{7,6},{8,9},{9,8},{10,11... | collective-permute-start | bytes 98312 | tf_op jit(solution)/shard_map/ppermute | solution.py:405
  5.6 5.1 %collective-permute-start.3 = (bf16[32,512]{1,0:T(8,128)(2,1)}, bf16[32,512]{1,0:T(8,128)(2,1)S(1)}, u32[]{:S(2)}, u32[]{:S(2)}) collective-permute-start(bf16[32,512]{1,0:T(8,128)(2,1)} %refs_7_.1), channel_id=1, source_target_pairs={{0,2},{1,3},{2,0},{3,1},{4,6},{5,7},{6,4},{7,5},{8,10},{9,11},{10,... | collective-permute-start | bytes 98312 | tf_op jit(solution)/shard_map/ppermute | solution.py:405
  10.6 1.4 %collective-permute-start.5 = (bf16[144,512]{1,0:T(8,128)(2,1)S(1)}, bf16[144,512]{1,0:T(8,128)(2,1)S(1)}, u32[]{:S(2)}, u32[]{:S(2)}) collective-permute-start(bf16[144,512]{1,0:T(8,128)(2,1)S(1)} %get-tuple-element.45), channel_id=1, source_target_pairs={{0,4},{4,0},{8,12},{12,8},{16,20},{20,16},{24,28},{28,24},{1,5},{5... | collective-permute-start | bytes 442376 | tf_op jit(solution)/shard_map/ppermute | solution.py:405
  12.1 8.7 %collective-permute-start.6 = (bf16[144,512]{1,0:T(8,128)(2,1)S(1)}, bf16[144,512]{1,0:T(8,128)(2,1)S(1)}, u32[]{:S(2)}, u32[]{:S(2)}) collective-permute-start(bf16[144,512]{1,0:T(8,128)(2,1)S(1)} %shard_map.94.refs_5_), channel_id=1, source_target_pairs={{0,16},{4,20},{8,24},{12,28},{16,0},{20,4},{24,8},{28,12},{1,17},{... | collective-permute-start | bytes 442376 | tf_op jit(solution)/shard_map/ppermute | solution.py:405
  13.7 7.1 %collective-permute-start.7 = (bf16[144,512]{1,0:T(8,128)(2,1)S(1)}, bf16[144,512]{1,0:T(8,128)(2,1)S(1)}, u32[]{:S(2)}, u32[]{:S(2)}) collective-permute-start(bf16[144,512]{1,0:T(8,128)(2,1)S(1)} %shard_map.94.refs_5_), channel_id=1, source_target_pairs={{0,8},{4,12},{8,0},{12,4},{16,24},{20,28},{24,16},{28,20},{1,9},{5... | collective-permute-start | bytes 442376 | tf_op jit(solution)/shard_map/ppermute | solution.py:405
  15.2 6.3 %collective-permute-start.8 = (bf16[144,512]{1,0:T(8,128)(2,1)S(1)}, bf16[144,512]{1,0:T(8,128)(2,1)S(1)}, u32[]{:S(2)}, u32[]{:S(2)}) collective-permute-start(bf16[144,512]{1,0:T(8,128)(2,1)S(1)} %shard_map.94.refs_5_), channel_id=1, source_target_pairs={{0,24},{4,28},{24,8},{28,12},{8,16},{12,20},{16,0},{20,4},{1,25},{... | collective-permute-start | bytes 442376 | tf_op jit(solution)/shard_map/ppermute | solution.py:521
  15.7 5.8 %collective-permute-start.9 = (bf16[144,512]{1,0:T(8,128)(2,1)S(1)}, bf16[144,512]{1,0:T(8,128)(2,1)S(1)}, u32[]{:S(2)}, u32[]{:S(2)}) collective-permute-start(bf16[144,512]{1,0:T(8,128)(2,1)S(1)} %get-tuple-element.56._.mine_ref), channel_id=1, source_target_pairs={{0,4},{4,0},{8,12},{12,8},{16,20},{20,16},{24,28},{28,24},{1,5},{5... | collective-permute-start | bytes 442376 | tf_op jit(solution)/shard_map/ppermute | solution.py:405
  15.7 4.5 %collective-permute-start.4 = (bf16[64,512]{1,0:T(8,128)(2,1)S(1)}, bf16[64,512]{1,0:T(8,128)(2,1)S(1)}, u32[]{:S(2)}, u32[]{:S(2)}) collective-permute-start(bf16[64,512]{1,0:T(8,128)(2,1)S(1)} %shard_map.93._.refs_4_), channel_id=1, source_target_pairs={{0,1},{1,0},{2,3},{3,2},{4,5},{5,4},{6,7},{7,6},{8,9},{9,8},{10,11... | collective-permute-start | bytes 196616 | tf_op jit(solution)/shard_map/ppermute | solution.py:405
  20.8 2.2 %collective-permute-start.10 = (bf16[144,512]{1,0:T(8,128)(2,1)S(1)}, bf16[144,512]{1,0:T(8,128)(2,1)S(1)}, u32[]{:S(2)}, u32[]{:S(2)}) collective-permute-start(bf16[144,512]{1,0:T(8,128)(2,1)S(1)} %collective-permute-done.7.x_ref.refs_5_), channel_id=1, source_target_pairs={{0,4},{4,0},{8,12},{12,8},{16,20},{20,16},{24,28},{28,24},{1,5},{5... | collective-permute-start | bytes 442376 | tf_op jit(solution)/shard_map/ppermute | solution.py:405
  21.6 1.4 %collective-permute-start.11 = (bf16[128,512]{1,0:T(8,128)(2,1)S(1)}, bf16[128,512]{1,0:T(8,128)(2,1)S(1)}, u32[]{:S(2)}, u32[]{:S(2)}) collective-permute-start(bf16[128,512]{1,0:T(8,128)(2,1)S(1)} %shard_map.97._.refs_6_), channel_id=1, source_target_pairs={{0,4},{4,0},{8,12},{12,8},{16,20},{20,16},{24,28},{28,24},{1,5},{5... | collective-permute-start | bytes 393224 | tf_op jit(solution)/shard_map/ppermute | solution.py:405
  23.3 5.4 %collective-permute-start.12 = (f32[1,512]{1,0:T(1,128)S(1)}, f32[1,512]{1,0:T(1,128)S(1)}, u32[]{:S(2)}, u32[]{:S(2)}) collective-permute-start(f32[1,512]{1,0:T(1,128)S(1)} %get-tuple-element.64.refs_0_), channel_id=1, source_target_pairs={{0,1},{1,2},{2,3},{3,0},{4,5},{5,6},{6,7},{7,4},{8,9},{9,10},{10,1... | collective-permute-start | bytes 6152 | tf_op jit(solution)/shard_map/ppermute | solution.py:420
  24.0 4.7 %collective-permute-start.13 = (f32[1,512]{1,0:T(1,128)S(1)}, f32[1,512]{1,0:T(1,128)S(1)}, u32[]{:S(2)}, u32[]{:S(2)}) collective-permute-start(f32[1,512]{1,0:T(1,128)S(1)} %get-tuple-element.64.refs_0_), channel_id=1, source_target_pairs={{0,2},{1,3},{2,0},{3,1},{4,6},{5,7},{6,4},{7,5},{8,10},{9,11},{10,... | collective-permute-start | bytes 6152 | tf_op jit(solution)/shard_map/ppermute | solution.py:420
  25.6 3.7 %collective-permute-start.14 = (f32[1,512]{1,0:T(1,128)S(1)}, f32[1,512]{1,0:T(1,128)S(1)}, u32[]{:S(2)}, u32[]{:S(2)}) collective-permute-start(f32[1,512]{1,0:T(1,128)S(1)} %get-tuple-element.64.refs_0_), channel_id=1, source_target_pairs={{0,3},{1,0},{2,1},{3,2},{4,7},{5,4},{6,5},{7,6},{8,11},{9,8},{10,9... | collective-permute-start | bytes 6152 | tf_op jit(solution)/shard_map/ppermute | solution.py:420

commit v24 on v22

--- a/solution.py
+++ b/solution.py
@@ -217,7 +217,7 @@
                 span_refs[0][index, :, cols] = (transposed_dot(mix, expand[:, cols]) * swish).astype(bf16)
 
 
-def near_body(spans, has_core, start, scores_ref, turned_ref, refs, near_ref):
+def near_body(spans, has_core, start, scores_ref, turned_ref, refs, near_ref, x_ref=None):
     base_ref, own_ref, far_ref, core_ref, scaled_ref = refs[:5]
     span_refs = refs[5:]
     tokens, size = turned_ref.shape
@@ -235,17 +235,27 @@
             if has_core:
                 reach = jnp.dot(turned_ref[at, :], core_ref[:size, cols], preferred_element_type=f32)
                 total = total + far_ref[0, at, of].astype(f32) * reach
+            if x_ref is not None:
+                state = x_ref[:size, cols]
+                if has_core:
+                    state = (state.astype(f32) * core_ref[size:, cols].astype(f32)[:1]).astype(bf16)
+                reach = jnp.dot(turned_ref[at, :], state, preferred_element_type=f32)
+                total = total + far_ref[1, at, of].astype(f32) * reach
             near_ref[at, cols] = total
 
 
-def near_of_core(spans, own, scores_ref, turned_ref, refs, near_ref):
-    core = lax.rem(lax.axis_index("seq"), 2)
+def near_of_core(spans, scores_ref, turned_ref, refs, near_ref, x_ref=None):
+    rank = lax.axis_index("seq")
+    core = lax.rem(rank, 2)
+    along_x = lax.rem(lax.div(rank, 2), 2)
     for has_core in (0, 1):
-
-        @pl.when(core == has_core)
-        def _():
-            start = (has_core if own else 1 - has_core) * near_ref.shape[1]
-            near_body(spans, has_core, start, scores_ref, turned_ref, refs, near_ref)
+        for has_x in (0,) if x_ref is None else (0, 1):
+
+            @pl.when((core == has_core) if x_ref is None else (core == has_core) & (along_x == has_x))
+            def _():
+                start = (has_core if x_ref is None else 1 - has_core) * near_ref.shape[1]
+                x_state = x_ref if has_x else None
+                near_body(spans, has_core, start, scores_ref, turned_ref, refs, near_ref, x_state)
 
 
 def near_kernel(parts, spans, paired, *refs):
@@ -262,13 +272,13 @@
         scores = jnp.dot(turned[at], in_map[:, at], preferred_element_type=f32)
         scores_ref[at, :] = jnp.where(row >= col, scores, 0.0).astype(bf16)
     if paired:
-        near_of_core(spans, True, scores_ref, turned_ref, rest, near_ref)
+        near_of_core(spans, scores_ref, turned_ref, rest, near_ref)
     else:
         near_body(spans, False, 0, scores_ref, turned_ref, rest, near_ref)
 
 
-def other_near_kernel(spans, scores_ref, turned_ref, _, *refs):
-    near_of_core(spans, False, scores_ref, turned_ref, refs[:-1], refs[-1])
+def other_near_kernel(spans, scores_ref, turned_ref, x_ref, _, *refs):
+    near_of_core(spans, scores_ref, turned_ref, refs[:-1], refs[-1], x_ref)
 
 
 def far_body(turned_ref, near_ref, far_ref, gain_ref, start, columns, levels, state_of, gated_ref):
@@ -350,7 +360,7 @@
 
         @pl.when((along_x == has_x) & (along_y == has_y))
         def _():
-            levels = (1,) * has_x + (2,) * has_y
+            levels = ((1,) * has_x if own else ()) + (2,) * has_y
             squares = far_body(turned_ref, near_ref, far_ref, gain_ref, start, half, levels, state_of, gated_ref)
             sums_ref[...] = squares if own else row_sums(squares + refs[7][...])
 
@@ -530,10 +540,6 @@
         )
         other = flip(own, "seq", 1)
         other_x = flip(from_x, "seq", 1)
-        near_args = base, own_factor, far, other_theirs, scaled, *span_states, *span_factors
-        other_near = call(
-            functools.partial(other_near_kernel, spans), near_shape, (scores, turned, own, *near_args), flops=dense
-        )
         gated_shape = shaped((tokens, width // 2), f32)
         own_gated, own_squares = call(
             functools.partial(far_kernel_of_half, True),
@@ -541,6 +547,10 @@
             (turned, near, far, gain, theirs, from_x, own),
             flops=2 * dense,
             bytes_accessed=6 * area,
+        )
+        near_args = base, own_factor, far, other_theirs, scaled, *span_states, *span_factors
+        other_near = call(
+            functools.partial(other_near_kernel, spans), near_shape, (scores, turned, other_x, own_squares, *near_args), flops=dense
         )
         other_gated, sums = call(
             functools.partial(far_kernel_of_half, False),

time: 30.7 us -> 30.7 us (level)
  waiting for transfers between devices: 5.73 us -> 6.19 us
    ppermute x1, waiting for transfers between devices: 0.22 us -> 0.88 us  [on_device(): lax.ppermute(message, 'seq', CYCLE)]
    ppermute x11, waiting for transfers between devices: 3.85 us -> 3.49 us  [flip(): lax.ppermute(array, axis, [(i, i ^ mask) for i in range(lax.axis_size(axi...]
    ppermute x11, starting transfers between devices: 12.7 us -> 12.3 us  [flip(): lax.ppermute(array, axis, [(i, i ^ mask) for i in range(lax.axis_size(axi...]
  transfers between devices with their start and end apart: 15 -> 15, of which waited for: 6 -> 9; matrix products, arithmetic and copies ran while one was open for 0% -> 0% of each run, Pallas kernels for 17% -> 17%
where the time goes in v24:
time: 30.7 us; the launch traced here: 30.3 us
  starting transfers between devices  17.1 us (56%)
  Pallas kernels  6.85 us (22%)
  waiting for transfers between devices  6.19 us (20%)
    ppermute x11, starting transfers between devices, flip(): lax.ppermute(array, axis, [(i, i ^ mask) for i in range(lax.axis_size(axi...  12.3 us
    pallas_call x11, Pallas kernels, call(): pl.pallas_call(kernel, out_shape=out_shape, in_specs=specs, out_specs=jax...  6.85 us
    ppermute x3, starting transfers between devices, around(): received.append(lax.ppermute(array, ('seq', 'head'), pairs))  4.34 us
    ppermute x11, waiting for transfers between devices, flip(): lax.ppermute(array, axis, [(i, i ^ mask) for i in range(lax.axis_size(axi...  3.49 us
    ppermute x3, waiting for transfers between devices, around(): received.append(lax.ppermute(array, ('seq', 'head'), pairs))  1.81 us
    ppermute x1, waiting for transfers between devices, on_device(): lax.ppermute(message, 'seq', CYCLE)  0.88 us
  transfers between devices with their start and end apart: 15, of which 9 were waited for; matrix products, arithmetic and copies ran while one was open for 0% of the time, Pallas kernels for 17%

profile of v24, /device:TPU:0, one launch (start us, length us, event | category | flops | bytes accessed | tf_op | source)
XLA Modules:
  0.0 30.3 jit_solution(2369833045049583490)
XLA Ops:
  0.0 4.0 %collective-permute-start = (bf16[32,512]{1,0:T(8,128)(2,1)}, bf16[32,512]{1,0:T(8,128)(2,1)S(1)}, u32[]{:S(2)}, u32[]{:S(2)}) collective-permute-start(bf16[32,512]{1,0:T(8,128)(2,1)} %refs_6_.1), channel_id=1, source_target_pairs={{0,2},{1,3},{2,0},{3,1},{4,6},{5,7},{6,4},{7,5},{8,10},{9,11},{10,... | collective-permute-start | bytes 98312 | tf_op jit(solution)/shard_map/ppermute | solution.py:415
  4.0 1.3 %collective-permute-start.1 = (bf16[32,512]{1,0:T(8,128)(2,1)}, bf16[32,512]{1,0:T(8,128)(2,1)S(1)}, u32[]{:S(2)}, u32[]{:S(2)}) collective-permute-start(bf16[32,512]{1,0:T(8,128)(2,1)} %refs_6_.1), channel_id=1, source_target_pairs={{0,3},{1,2},{2,1},{3,0},{4,7},{5,6},{6,5},{7,4},{8,11},{9,10},{10,... | collective-permute-start | bytes 98312 | tf_op jit(solution)/shard_map/ppermute | solution.py:415
  5.4 0.2 collective-permute-start.2
  5.6 2.8 %collective-permute-start.3 = (bf16[32,512]{1,0:T(8,128)(2,1)}, bf16[32,512]{1,0:T(8,128)(2,1)S(1)}, u32[]{:S(2)}, u32[]{:S(2)}) collective-permute-start(bf16[32,512]{1,0:T(8,128)(2,1)} %refs_7_.1), channel_id=1, source_target_pairs={{0,2},{1,3},{2,0},{3,1},{4,6},{5,7},{6,4},{7,5},{8,10},{9,11},{10,... | collective-permute-start | bytes 98312 | tf_op jit(solution)/shard_map/ppermute | solution.py:415
  8.4 1.8 %shard_map.91 = (bf16[512,1024]{1,0:T(8,128)(2,1)S(1)}, f32[16,512]{1,0:T(8,128)S(1)}, bf16[512,1024]{1,0:T(8,128)(2,1)S(1)}, bf16[512,1024]{1,0:T(8,128)(2,1)S(...) custom-call(f32[16,512]{1,0:T(8,128)} %refs_0_.1, ...), custom_call_target="tpu_custom_call" | custom-call | flops 4294967296 | bytes 2097152 | tf_op jit(solution)/shard_map/pallas_call | solution.py:399
  10.3 0.3 %shard_map.92 = (bf16[136,512]{1,0:T(8,128)(2,1)S(1)}, bf16[136,512]{1,0:T(8,128)(2,1)S(1)}, bf16[128,1024]{1,0:T(8,128)(2,1)S(1)}) custom-call(bf16[32,512]{1,0:T(8,128)(2,1)S(1)} %get-tuple-element.36.refs_0_, bf16[32,512]{1,0:T(8,128)(2,1)S(1)} %collective-permute-done.refs_1_, bf16[32,512]{1,0:T(8,128)(2,1)S(1)} %collective-permute-done.1.refs_2_, ...), custom_call_target="tpu_custom_call" | custom-call | flops 268435456 | tf_op jit(solution)/shard_map/pallas_call | solution.py:399
  10.6 0.1 collective-permute-start.5
  10.7 1.3 %collective-permute-done.5.theirs_ref.refs_9_.refs_4_ = bf16[136,512]{1,0:T(8,128)(2,1)S(1)} collective-permute-done((bf16[136,512]{1,0:T(8,128)(2,1)S(1)}, bf16[136,512]{1,0:T(8,128)(2,1)S(1)}, u32[]{:S(2)}, u32[]{:S(2)}) %collective-permute-start.5) | collective-permute-done | bytes 139296 | tf_op jit(solution)/shard_map/ppermute | solution.py:415
  12.0 0.1 shard_map.94.refs_5_
  12.1 1.6 %collective-permute-start.6 = (bf16[136,512]{1,0:T(8,128)(2,1)S(1)}, bf16[136,512]{1,0:T(8,128)(2,1)S(1)}, u32[]{:S(2)}, u32[]{:S(2)}) collective-permute-start(bf16[136,512]{1,0:T(8,128)(2,1)S(1)} %shard_map.94.refs_5_), channel_id=1, source_target_pairs={{0,16},{4,20},{8,24},{12,28},{16,0},{20,4},{24,8},{28,12},{1,17},{... | collective-permute-start | bytes 417800 | tf_op jit(solution)/shard_map/ppermute | solution.py:415
  13.7 1.5 %collective-permute-start.7 = (bf16[136,512]{1,0:T(8,128)(2,1)S(1)}, bf16[136,512]{1,0:T(8,128)(2,1)S(1)}, u32[]{:S(2)}, u32[]{:S(2)}) collective-permute-start(bf16[136,512]{1,0:T(8,128)(2,1)S(1)} %shard_map.94.refs_5_), channel_id=1, source_target_pairs={{0,8},{4,12},{8,0},{12,4},{16,24},{20,28},{24,16},{28,20},{1,9},{5... | collective-permute-start | bytes 417800 | tf_op jit(solution)/shard_map/ppermute | solution.py:415
  15.2 0.7 %collective-permute-start.4 = (bf16[64,512]{1,0:T(8,128)(2,1)S(1)}, bf16[64,512]{1,0:T(8,128)(2,1)S(1)}, u32[]{:S(2)}, u32[]{:S(2)}) collective-permute-start(bf16[64,512]{1,0:T(8,128)(2,1)S(1)} %shard_map.93._.refs_4_), channel_id=1, source_target_pairs={{0,1},{1,0},{2,3},{3,2},{4,5},{5,4},{6,7},{7,6},{8,9},{9,8},{10,11... | collective-permute-start | bytes 196616 | tf_op jit(solution)/shard_map/ppermute | solution.py:415
  15.9 0.5 %collective-permute-start.9 = (bf16[136,512]{1,0:T(8,128)(2,1)S(1)}, bf16[136,512]{1,0:T(8,128)(2,1)S(1)}, u32[]{:S(2)}, u32[]{:S(2)}) collective-permute-start(bf16[136,512]{1,0:T(8,128)(2,1)S(1)} %shard_map.94.refs_5_), channel_id=1, source_target_pairs={{0,24},{4,28},{24,8},{28,12},{8,16},{12,20},{16,0},{20,4},{1,25},{... | collective-permute-start | bytes 417800 | tf_op jit(solution)/shard_map/ppermute | solution.py:531
  16.3 1.8 %shard_map.95 = (f32[512,1024]{1,0:T(8,128)S(1)}, f32[512,1024]{1,0:T(8,128)S(1)}, bf16[3,512,1024]{2,1,0:T(8,128)(2,1)S(1)}, bf16[1,256,1024]{2,1,0:T(8,128)(2,1)S(1)}) custom-call(bf16[512,1024]{1,0:T(8,128)(2,1)S(1)} %get-tuple-element.41.refs_0_, bf16[512,1024]{1,0:T(8,128)(2,1)S(1)} %get-tuple-element.42.refs_1_, ...), custom_call_target="tpu_custom_call" | custom-call | flops 1342177280 | tf_op jit(solution)/shard_map/pallas_call | solution.py:399
  18.1 1.3 %collective-permute-done.4.refs_5_ = bf16[64,512]{1,0:T(8,128)(2,1)S(1)} collective-permute-done((bf16[64,512]{1,0:T(8,128)(2,1)S(1)}, bf16[64,512]{1,0:T(8,128)(2,1)S(1)}, u32[]{:S(2)}, u32[]{:S(2)}) %collective-permute-start.4) | collective-permute-done | bytes 65568 | tf_op jit(solution)/shard_map/ppermute | solution.py:415
  19.5 0.7 %shard_map.96 = (f32[512,512]{1,0:T(8,128)S(1)}, bf16[512,128]{1,0:T(8,128)(2,1)S(1)}, bf16[512,256]{1,0:T(8,128)(2,1)S(1)}) custom-call(bf16[32,512]{1,0:T(8,128)(2,1)S(1)} %get-tuple-element.36.refs_0_, bf16[32,512]{1,0:T(8,128)(2,1)S(1)} %collective-permute-done.refs_1_, bf16[32,512]{1,0:T(8,128)(2,1)S(1)} %collective-permute-done.1.refs_2_, ...), custom_call_target="tpu_custom_call" | custom-call | tf_op jit(solution)/shard_map/pallas_call | solution.py:399
  20.1 0.1 collective-permute-done.7.x_ref.refs_5_
  20.3 0.9 %collective-permute-done.9.diagonal_ref = bf16[136,512]{1,0:T(8,128)(2,1)S(1)} collective-permute-done((bf16[136,512]{1,0:T(8,128)(2,1)S(1)}, bf16[136,512]{1,0:T(8,128)(2,1)S(1)}, u32[]{:S(2)}, u32[]{:S(2)}) %collective-permute-start.9) | collective-permute-done | bytes 139296 | tf_op jit(solution)/shard_map/ppermute | solution.py:531
  21.1 0.1 shard_map.97.refs_6_
  21.2 0.1 collective-permute-start.11
  21.3 0.2 shard_map.98
  21.5 0.1 collective-permute-done.8.x_ref.refs_5_
  21.6 0.4 %shard_map.99.refs_1_ = f32[512,512]{1,0:T(8,128)S(1)} custom-call(bf16[512,256]{1,0:T(8,128)(2,1)S(1)} %get-tuple-element.52.scores_ref, bf16[512,128]{1,0:T(8,128)(2,1)S(1)} %get-tuple-element.51.refs_0_.turned_ref, bf16[136,512]{1,0:T(8,128)(2,1)S(1)} %collective-permute-done.8.x_ref.refs_5_, f32[512,128]{1,0:T(8,128)S(1)} %get-tuple-element.62._.refs_7_, ...), custom_call_target="tpu_custom_call" | custom-call | flops 268435456 | tf_op jit(solution)/shard_map/pallas_call | solution.py:399
  22.0 0.6 %collective-permute-done.11.refs_6_ = bf16[128,512]{1,0:T(8,128)(2,1)S(1)} collective-permute-done((bf16[128,512]{1,0:T(8,128)(2,1)S(1)}, bf16[128,512]{1,0:T(8,128)(2,1)S(1)}, u32[]{:S(2)}, u32[]{:S(2)}) %collective-permute-start.11) | collective-permute-done | bytes 131104 | tf_op jit(solution)/shard_map/ppermute | solution.py:415
  22.7 0.3 shard_map.100
  22.9 1.1 %collective-permute-start.12 = (f32[1,512]{1,0:T(1,128)S(1)}, f32[1,512]{1,0:T(1,128)S(1)}, u32[]{:S(2)}, u32[]{:S(2)}) collective-permute-start(f32[1,512]{1,0:T(1,128)S(1)} %get-tuple-element.64.refs_0_), channel_id=1, source_target_pairs={{0,1},{1,2},{2,3},{3,0},{4,5},{5,6},{6,7},{7,4},{8,9},{9,10},{10,1... | collective-permute-start | bytes 6152 | tf_op jit(solution)/shard_map/ppermute | solution.py:430
  24.1 1.4 %collective-permute-start.13 = (f32[1,512]{1,0:T(1,128)S(1)}, f32[1,512]{1,0:T(1,128)S(1)}, u32[]{:S(2)}, u32[]{:S(2)}) collective-permute-start(f32[1,512]{1,0:T(1,128)S(1)} %get-tuple-element.64.refs_0_), channel_id=1, source_target_pairs={{0,2},{1,3},{2,0},{3,1},{4,6},{5,7},{6,4},{7,5},{8,10},{9,11},{10,... | collective-permute-start | bytes 6152 | tf_op jit(solution)/shard_map/ppermute | solution.py:430
  25.5 1.8 %collective-permute-start.14 = (f32[1,512]{1,0:T(1,128)S(1)}, f32[1,512]{1,0:T(1,128)S(1)}, u32[]{:S(2)}, u32[]{:S(2)}) collective-permute-start(f32[1,512]{1,0:T(1,128)S(1)} %get-tuple-element.64.refs_0_), channel_id=1, source_target_pairs={{0,3},{1,0},{2,1},{3,2},{4,7},{5,4},{6,5},{7,6},{8,11},{9,8},{10,9... | collective-permute-start | bytes 6152 | tf_op jit(solution)/shard_map/ppermute | solution.py:430
  27.3 1.1 %collective-permute-done.12.refs_1_ = f32[1,512]{1,0:T(1,128)S(1)} collective-permute-done((f32[1,512]{1,0:T(1,128)S(1)}, f32[1,512]{1,0:T(1,128)S(1)}, u32[]{:S(2)}, u32[]{:S(2)}) %collective-permute-start.12) | collective-permute-done | bytes 2080 | tf_op jit(solution)/shard_map/ppermute | solution.py:430
  28.3 0.2 collective-permute-done.13.refs_2_
  28.5 0.5 %collective-permute-done.14.refs_3_ = f32[1,512]{1,0:T(1,128)S(1)} collective-permute-done((f32[1,512]{1,0:T(1,128)S(1)}, f32[1,512]{1,0:T(1,128)S(1)}, u32[]{:S(2)}, u32[]{:S(2)}) %collective-permute-start.14) | collective-permute-done | bytes 2080 | tf_op jit(solution)/shard_map/ppermute | solution.py:430
  29.1 1.2 %shard_map.101 = bf16[512,1024]{1,0:T(8,128)(2,1)} custom-call(f32[1,512]{1,0:T(1,128)S(1)} %get-tuple-element.64.refs_0_, f32[1,512]{1,0:T(1,128)S(1)} %collective-permute-done.12.refs_1_, f32[1,512]{1,0:T(1,128)S(1)} %collective-permute-done.13.refs_2_, f32[1,512]{1,0:T(1,128)S(1)} %collective-permute-done.14.refs_3_, ...), custom_call_target="tpu_custom_call" | custom-call | flops 268435456 | bytes 3145728 | tf_op jit(solution)/shard_map/pallas_call | solution.py:399
  (9 shorter events, 0.0 us)
Async XLA Ops:
  0.0 10.2 %collective-permute-start = (bf16[32,512]{1,0:T(8,128)(2,1)}, bf16[32,512]{1,0:T(8,128)(2,1)S(1)}, u32[]{:S(2)}, u32[]{:S(2)}) collective-permute-start(bf16[32,512]{1,0:T(8,128)(2,1)} %refs_6_.1), channel_id=1, source_target_pairs={{0,2},{1,3},{2,0},{3,1},{4,6},{5,7},{6,4},{7,5},{8,10},{9,11},{10,... | collective-permute-start | bytes 98312 | tf_op jit(solution)/shard_map/ppermute | solution.py:415
  4.0 6.2 %collective-permute-start.1 = (bf16[32,512]{1,0:T(8,128)(2,1)}, bf16[32,512]{1,0:T(8,128)(2,1)S(1)}, u32[]{:S(2)}, u32[]{:S(2)}) collective-permute-start(bf16[32,512]{1,0:T(8,128)(2,1)} %refs_6_.1), channel_id=1, source_target_pairs={{0,3},{1,2},{2,1},{3,0},{4,7},{5,6},{6,5},{7,4},{8,11},{9,10},{10,... | collective-permute-start | bytes 98312 | tf_op jit(solution)/shard_map/ppermute | solution.py:415
  5.4 4.9 %collective-permute-start.2 = (bf16[32,512]{1,0:T(8,128)(2,1)}, bf16[32,512]{1,0:T(8,128)(2,1)S(1)}, u32[]{:S(2)}, u32[]{:S(2)}) collective-permute-start(bf16[32,512]{1,0:T(8,128)(2,1)} %refs_6_.1), channel_id=1, source_target_pairs={{0,1},{1,0},{2,3},{3,2},{4,5},{5,4},{6,7},{7,6},{8,9},{9,8},{10,11... | collective-permute-start | bytes 98312 | tf_op jit(solution)/shard_map/ppermute | solution.py:415
  5.6 5.1 %collective-permute-start.3 = (bf16[32,512]{1,0:T(8,128)(2,1)}, bf16[32,512]{1,0:T(8,128)(2,1)S(1)}, u32[]{:S(2)}, u32[]{:S(2)}) collective-permute-start(bf16[32,512]{1,0:T(8,128)(2,1)} %refs_7_.1), channel_id=1, source_target_pairs={{0,2},{1,3},{2,0},{3,1},{4,6},{5,7},{6,4},{7,5},{8,10},{9,11},{10,... | collective-permute-start | bytes 98312 | tf_op jit(solution)/shard_map/ppermute | solution.py:415
  10.6 1.4 %collective-permute-start.5 = (bf16[136,512]{1,0:T(8,128)(2,1)S(1)}, bf16[136,512]{1,0:T(8,128)(2,1)S(1)}, u32[]{:S(2)}, u32[]{:S(2)}) collective-permute-start(bf16[136,512]{1,0:T(8,128)(2,1)S(1)} %get-tuple-element.45), channel_id=1, source_target_pairs={{0,4},{4,0},{8,12},{12,8},{16,20},{20,16},{24,28},{28,24},{1,5},{5... | collective-permute-start | bytes 417800 | tf_op jit(solution)/shard_map/ppermute | solution.py:415
  12.1 8.0 %collective-permute-start.6 = (bf16[136,512]{1,0:T(8,128)(2,1)S(1)}, bf16[136,512]{1,0:T(8,128)(2,1)S(1)}, u32[]{:S(2)}, u32[]{:S(2)}) collective-permute-start(bf16[136,512]{1,0:T(8,128)(2,1)S(1)} %shard_map.94.refs_5_), channel_id=1, source_target_pairs={{0,16},{4,20},{8,24},{12,28},{16,0},{20,4},{24,8},{28,12},{1,17},{... | collective-permute-start | bytes 417800 | tf_op jit(solution)/shard_map/ppermute | solution.py:415
  13.7 6.6 %collective-permute-start.7 = (bf16[136,512]{1,0:T(8,128)(2,1)S(1)}, bf16[136,512]{1,0:T(8,128)(2,1)S(1)}, u32[]{:S(2)}, u32[]{:S(2)}) collective-permute-start(bf16[136,512]{1,0:T(8,128)(2,1)S(1)} %shard_map.94.refs_5_), channel_id=1, source_target_pairs={{0,8},{4,12},{8,0},{12,4},{16,24},{20,28},{24,16},{28,20},{1,9},{5... | collective-permute-start | bytes 417800 | tf_op jit(solution)/shard_map/ppermute | solution.py:415
  15.2 4.3 %collective-permute-start.4 = (bf16[64,512]{1,0:T(8,128)(2,1)S(1)}, bf16[64,512]{1,0:T(8,128)(2,1)S(1)}, u32[]{:S(2)}, u32[]{:S(2)}) collective-permute-start(bf16[64,512]{1,0:T(8,128)(2,1)S(1)} %shard_map.93._.refs_4_), channel_id=1, source_target_pairs={{0,1},{1,0},{2,3},{3,2},{4,5},{5,4},{6,7},{7,6},{8,9},{9,8},{10,11... | collective-permute-start | bytes 196616 | tf_op jit(solution)/shard_map/ppermute | solution.py:415
  15.9 5.3 %collective-permute-start.9 = (bf16[136,512]{1,0:T(8,128)(2,1)S(1)}, bf16[136,512]{1,0:T(8,128)(2,1)S(1)}, u32[]{:S(2)}, u32[]{:S(2)}) collective-permute-start(bf16[136,512]{1,0:T(8,128)(2,1)S(1)} %shard_map.94.refs_5_), channel_id=1, source_target_pairs={{0,24},{4,28},{24,8},{28,12},{8,16},{12,20},{16,0},{20,4},{1,25},{... | collective-permute-start | bytes 417800 | tf_op jit(solution)/shard_map/ppermute | solution.py:531
  16.3 3.9 %collective-permute-start.10 = (bf16[136,512]{1,0:T(8,128)(2,1)S(1)}, bf16[136,512]{1,0:T(8,128)(2,1)S(1)}, u32[]{:S(2)}, u32[]{:S(2)}) collective-permute-start(bf16[136,512]{1,0:T(8,128)(2,1)S(1)} %get-tuple-element.55._.mine_ref), channel_id=1, source_target_pairs={{0,4},{4,0},{8,12},{12,8},{16,20},{20,16},{24,28},{28,24},{1,5},{5... | collective-permute-start | bytes 417800 | tf_op jit(solution)/shard_map/ppermute | solution.py:415
  20.3 1.4 %collective-permute-start.8 = (bf16[136,512]{1,0:T(8,128)(2,1)S(1)}, bf16[136,512]{1,0:T(8,128)(2,1)S(1)}, u32[]{:S(2)}, u32[]{:S(2)}) collective-permute-start(bf16[136,512]{1,0:T(8,128)(2,1)S(1)} %collective-permute-done.7.x_ref.refs_5_), channel_id=1, source_target_pairs={{0,4},{4,0},{8,12},{12,8},{16,20},{20,16},{24,28},{28,24},{1,5},{5... | collective-permute-start | bytes 417800 | tf_op jit(solution)/shard_map/ppermute | solution.py:415
  21.2 1.4 %collective-permute-start.11 = (bf16[128,512]{1,0:T(8,128)(2,1)S(1)}, bf16[128,512]{1,0:T(8,128)(2,1)S(1)}, u32[]{:S(2)}, u32[]{:S(2)}) collective-permute-start(bf16[128,512]{1,0:T(8,128)(2,1)S(1)} %shard_map.97.refs_6_), channel_id=1, source_target_pairs={{0,4},{4,0},{8,12},{12,8},{16,20},{20,16},{24,28},{28,24},{1,5},{5... | collective-permute-start | bytes 393224 | tf_op jit(solution)/shard_map/ppermute | solution.py:415
  22.9 5.4 %collective-permute-start.12 = (f32[1,512]{1,0:T(1,128)S(1)}, f32[1,512]{1,0:T(1,128)S(1)}, u32[]{:S(2)}, u32[]{:S(2)}) collective-permute-start(f32[1,512]{1,0:T(1,128)S(1)} %get-tuple-element.64.refs_0_), channel_id=1, source_target_pairs={{0,1},{1,2},{2,3},{3,0},{4,5},{5,6},{6,7},{7,4},{8,9},{9,10},{10,1... | collective-permute-start | bytes 6152 | tf_op jit(solution)/shard_map/ppermute | solution.py:430
  24.1 4.5 %collective-permute-start.13 = (f32[1,512]{1,0:T(1,128)S(1)}, f32[1,512]{1,0:T(1,128)S(1)}, u32[]{:S(2)}, u32[]{:S(2)}) collective-permute-start(f32[1,512]{1,0:T(1,128)S(1)} %get-tuple-element.64.refs_0_), channel_id=1, source_target_pairs={{0,2},{1,3},{2,0},{3,1},{4,6},{5,7},{6,4},{7,5},{8,10},{9,11},{10,... | collective-permute-start | bytes 6152 | tf_op jit(solution)/shard_map/ppermute | solution.py:430
  25.5 3.6 %collective-permute-start.14 = (f32[1,512]{1,0:T(1,128)S(1)}, f32[1,512]{1,0:T(1,128)S(1)}, u32[]{:S(2)}, u32[]{:S(2)}) collective-permute-start(f32[1,512]{1,0:T(1,128)S(1)} %get-tuple-element.64.refs_0_), channel_id=1, source_target_pairs={{0,3},{1,0},{2,1},{3,2},{4,7},{5,4},{6,5},{7,6},{8,11},{9,8},{10,9... | collective-permute-start | bytes 6152 | tf_op jit(solution)/shard_map/ppermute | solution.py:430

commit v25 on v24

--- a/solution.py
+++ b/solution.py
@@ -531,7 +531,8 @@
         received = [flip(message, "seq", 4), flip(message, "seq", 2), lax.ppermute(message, "seq", CYCLE)]
         from_y, from_x, from_cycle = received
         from_y, from_x, near, far = lax.optimization_barrier((from_y, from_x, near, far))
-        from_cycle, other_theirs, near = lax.optimization_barrier((from_cycle, other_theirs, near))
+        from_cycle, near = lax.optimization_barrier((from_cycle, near))
+        from_cycle, other_theirs = lax.optimization_barrier((from_cycle, other_theirs))
         own = call(
             functools.partial(combine_kernel, size),
             shaped((size, width // 2), bf16),
@@ -550,7 +551,7 @@
         )
         near_args = base, own_factor, far, other_theirs, scaled, *span_states, *span_factors
         other_near = call(
-            functools.partial(other_near_kernel, spans), near_shape, (scores, turned, other_x, own_squares, *near_args), flops=dense
+            functools.partial(other_near_kernel, spans), near_shape, (scores, turned, other_x, own_squares, *near_args), flops=0
         )
         other_gated, sums = call(
             functools.partial(far_kernel_of_half, False),

time: 30.7 us -> 30.6 us (level)
  waiting for transfers between devices: 6.19 us -> 5.66 us
  starting transfers between devices: 17.1 us -> 17.5 us
    ppermute x1, waiting for transfers between devices: 0.88 us -> 0.2 us  [on_device(): lax.ppermute(message, 'seq', CYCLE)]
    ppermute x11, waiting for transfers between devices: 3.49 us -> 3.87 us  [flip(): lax.ppermute(array, axis, [(i, i ^ mask) for i in range(lax.axis_size(axi...]
    ppermute x11, starting transfers between devices: 12.3 us -> 12.7 us  [flip(): lax.ppermute(array, axis, [(i, i ^ mask) for i in range(lax.axis_size(axi...]
  transfers between devices with their start and end apart: 15 -> 15, of which waited for: 9 -> 6; matrix products, arithmetic and copies ran while one was open for 0% -> 0% of each run, Pallas kernels for 17% -> 17%
where the time goes in v25:
time: 30.6 us; the launch traced here: 30.2 us
  starting transfers between devices  17.5 us (57%)
  Pallas kernels  6.85 us (22%)
  waiting for transfers between devices  5.66 us (18%)
    ppermute x11, starting transfers between devices, flip(): lax.ppermute(array, axis, [(i, i ^ mask) for i in range(lax.axis_size(axi...  12.7 us
    pallas_call x11, Pallas kernels, call(): pl.pallas_call(kernel, out_shape=out_shape, in_specs=specs, out_specs=jax...  6.85 us
    ppermute x3, starting transfers between devices, around(): received.append(lax.ppermute(array, ('seq', 'head'), pairs))  4.36 us
    ppermute x11, waiting for transfers between devices, flip(): lax.ppermute(array, axis, [(i, i ^ mask) for i in range(lax.axis_size(axi...  3.87 us
    ppermute x3, waiting for transfers between devices, around(): received.append(lax.ppermute(array, ('seq', 'head'), pairs))  1.59 us
  transfers between devices with their start and end apart: 15, of which 6 were waited for; matrix products, arithmetic and copies ran while one was open for 0% of the time, Pallas kernels for 17%

profile of v25, /device:TPU:0, one launch (start us, length us, event | category | flops | bytes accessed | tf_op | source)
XLA Modules:
  0.0 30.2 jit_solution(15110012197165192679)
XLA Ops:
  0.0 4.0 %collective-permute-start = (bf16[32,512]{1,0:T(8,128)(2,1)}, bf16[32,512]{1,0:T(8,128)(2,1)S(1)}, u32[]{:S(2)}, u32[]{:S(2)}) collective-permute-start(bf16[32,512]{1,0:T(8,128)(2,1)} %refs_6_.1), channel_id=1, source_target_pairs={{0,2},{1,3},{2,0},{3,1},{4,6},{5,7},{6,4},{7,5},{8,10},{9,11},{10,... | collective-permute-start | bytes 98312 | tf_op jit(solution)/shard_map/ppermute | solution.py:415
  4.0 1.3 %collective-permute-start.1 = (bf16[32,512]{1,0:T(8,128)(2,1)}, bf16[32,512]{1,0:T(8,128)(2,1)S(1)}, u32[]{:S(2)}, u32[]{:S(2)}) collective-permute-start(bf16[32,512]{1,0:T(8,128)(2,1)} %refs_6_.1), channel_id=1, source_target_pairs={{0,3},{1,2},{2,1},{3,0},{4,7},{5,6},{6,5},{7,4},{8,11},{9,10},{10,... | collective-permute-start | bytes 98312 | tf_op jit(solution)/shard_map/ppermute | solution.py:415
  5.4 0.2 collective-permute-start.2
  5.6 2.8 %collective-permute-start.3 = (bf16[32,512]{1,0:T(8,128)(2,1)}, bf16[32,512]{1,0:T(8,128)(2,1)S(1)}, u32[]{:S(2)}, u32[]{:S(2)}) collective-permute-start(bf16[32,512]{1,0:T(8,128)(2,1)} %refs_7_.1), channel_id=1, source_target_pairs={{0,2},{1,3},{2,0},{3,1},{4,6},{5,7},{6,4},{7,5},{8,10},{9,11},{10,... | collective-permute-start | bytes 98312 | tf_op jit(solution)/shard_map/ppermute | solution.py:415
  8.4 1.8 %shard_map.91 = (bf16[512,1024]{1,0:T(8,128)(2,1)S(1)}, f32[16,512]{1,0:T(8,128)S(1)}, bf16[512,1024]{1,0:T(8,128)(2,1)S(1)}, bf16[512,1024]{1,0:T(8,128)(2,1)S(...) custom-call(f32[16,512]{1,0:T(8,128)} %refs_0_.1, ...), custom_call_target="tpu_custom_call" | custom-call | flops 4294967296 | bytes 2097152 | tf_op jit(solution)/shard_map/pallas_call | solution.py:399
  10.2 0.0 collective-permute-done.refs_1_
  10.3 0.0 collective-permute-done.2.refs_3_
  10.3 0.3 %shard_map.92 = (bf16[136,512]{1,0:T(8,128)(2,1)S(1)}, bf16[136,512]{1,0:T(8,128)(2,1)S(1)}, bf16[128,1024]{1,0:T(8,128)(2,1)S(1)}) custom-call(bf16[32,512]{1,0:T(8,128)(2,1)S(1)} %get-tuple-element.37.refs_0_, bf16[32,512]{1,0:T(8,128)(2,1)S(1)} %collective-permute-done.refs_1_, bf16[32,512]{1,0:T(8,128)(2,1)S(1)} %collective-permute-done.1.refs_2_, ...), custom_call_target="tpu_custom_call" | custom-call | flops 268435456 | tf_op jit(solution)/shard_map/pallas_call | solution.py:399
  10.6 0.1 collective-permute-start.5
  10.7 1.3 %collective-permute-done.5.theirs_ref.refs_9_.refs_4_ = bf16[136,512]{1,0:T(8,128)(2,1)S(1)} collective-permute-done((bf16[136,512]{1,0:T(8,128)(2,1)S(1)}, bf16[136,512]{1,0:T(8,128)(2,1)S(1)}, u32[]{:S(2)}, u32[]{:S(2)}) %collective-permute-start.5) | collective-permute-done | bytes 139296 | tf_op jit(solution)/shard_map/ppermute | solution.py:415
  12.0 0.1 shard_map.94.refs_5_
  12.1 1.6 %collective-permute-start.6 = (bf16[136,512]{1,0:T(8,128)(2,1)S(1)}, bf16[136,512]{1,0:T(8,128)(2,1)S(1)}, u32[]{:S(2)}, u32[]{:S(2)}) collective-permute-start(bf16[136,512]{1,0:T(8,128)(2,1)S(1)} %shard_map.94.refs_5_), channel_id=1, source_target_pairs={{0,16},{4,20},{8,24},{12,28},{16,0},{20,4},{24,8},{28,12},{1,17},{... | collective-permute-start | bytes 417800 | tf_op jit(solution)/shard_map/ppermute | solution.py:415
  13.7 1.5 %collective-permute-start.7 = (bf16[136,512]{1,0:T(8,128)(2,1)S(1)}, bf16[136,512]{1,0:T(8,128)(2,1)S(1)}, u32[]{:S(2)}, u32[]{:S(2)}) collective-permute-start(bf16[136,512]{1,0:T(8,128)(2,1)S(1)} %shard_map.94.refs_5_), channel_id=1, source_target_pairs={{0,8},{4,12},{8,0},{12,4},{16,24},{20,28},{24,16},{28,20},{1,9},{5... | collective-permute-start | bytes 417800 | tf_op jit(solution)/shard_map/ppermute | solution.py:415
  15.2 0.5 %collective-permute-start.9 = (bf16[136,512]{1,0:T(8,128)(2,1)S(1)}, bf16[136,512]{1,0:T(8,128)(2,1)S(1)}, u32[]{:S(2)}, u32[]{:S(2)}) collective-permute-start(bf16[136,512]{1,0:T(8,128)(2,1)S(1)} %shard_map.94.refs_5_), channel_id=1, source_target_pairs={{0,24},{4,28},{24,8},{28,12},{8,16},{12,20},{16,0},{20,4},{1,25},{... | collective-permute-start | bytes 417800 | tf_op jit(solution)/shard_map/ppermute | solution.py:531
  15.7 0.7 %collective-permute-start.4 = (bf16[64,512]{1,0:T(8,128)(2,1)S(1)}, bf16[64,512]{1,0:T(8,128)(2,1)S(1)}, u32[]{:S(2)}, u32[]{:S(2)}) collective-permute-start(bf16[64,512]{1,0:T(8,128)(2,1)S(1)} %shard_map.93._.refs_4_), channel_id=1, source_target_pairs={{0,1},{1,0},{2,3},{3,2},{4,5},{5,4},{6,7},{7,6},{8,9},{9,8},{10,11... | collective-permute-start | bytes 196616 | tf_op jit(solution)/shard_map/ppermute | solution.py:415
  16.3 1.8 %shard_map.95 = (f32[512,1024]{1,0:T(8,128)S(1)}, f32[512,1024]{1,0:T(8,128)S(1)}, bf16[3,512,1024]{2,1,0:T(8,128)(2,1)S(1)}, bf16[1,256,1024]{2,1,0:T(8,128)(2,1)S(1)}) custom-call(bf16[512,1024]{1,0:T(8,128)(2,1)S(1)} %get-tuple-element.42.refs_0_, bf16[512,1024]{1,0:T(8,128)(2,1)S(1)} %get-tuple-element.43.refs_1_, ...), custom_call_target="tpu_custom_call" | custom-call | flops 1342177280 | tf_op jit(solution)/shard_map/pallas_call | solution.py:399
  18.1 2.0 %collective-permute-done.4.refs_5_ = bf16[64,512]{1,0:T(8,128)(2,1)S(1)} collective-permute-done((bf16[64,512]{1,0:T(8,128)(2,1)S(1)}, bf16[64,512]{1,0:T(8,128)(2,1)S(1)}, u32[]{:S(2)}, u32[]{:S(2)}) %collective-permute-start.4) | collective-permute-done | bytes 65568 | tf_op jit(solution)/shard_map/ppermute | solution.py:415
  20.2 0.7 %shard_map.96 = (f32[512,512]{1,0:T(8,128)S(1)}, bf16[512,128]{1,0:T(8,128)(2,1)S(1)}, bf16[512,256]{1,0:T(8,128)(2,1)S(1)}) custom-call(bf16[32,512]{1,0:T(8,128)(2,1)S(1)} %get-tuple-element.37.refs_0_, bf16[32,512]{1,0:T(8,128)(2,1)S(1)} %collective-permute-done.refs_1_, bf16[32,512]{1,0:T(8,128)(2,1)S(1)} %collective-permute-done.1.refs_2_, ...), custom_call_target="tpu_custom_call" | custom-call | tf_op jit(solution)/shard_map/pallas_call | solution.py:399
  20.9 0.1 collective-permute-start.8
  20.9 0.2 collective-permute-done.9.diagonal_ref
  21.1 0.1 shard_map.97.refs_6_
  21.2 0.4 %collective-permute-start.11 = (bf16[128,512]{1,0:T(8,128)(2,1)S(1)}, bf16[128,512]{1,0:T(8,128)(2,1)S(1)}, u32[]{:S(2)}, u32[]{:S(2)}) collective-permute-start(bf16[128,512]{1,0:T(8,128)(2,1)S(1)} %shard_map.97.refs_6_), channel_id=1, source_target_pairs={{0,4},{4,0},{8,12},{12,8},{16,20},{20,16},{24,28},{28,24},{1,5},{5... | collective-permute-start | bytes 393224 | tf_op jit(solution)/shard_map/ppermute | solution.py:415
  21.6 0.2 shard_map.98
  21.8 0.5 %collective-permute-done.8.x_ref.refs_5_ = bf16[136,512]{1,0:T(8,128)(2,1)S(1)} collective-permute-done((bf16[136,512]{1,0:T(8,128)(2,1)S(1)}, bf16[136,512]{1,0:T(8,128)(2,1)S(1)}, u32[]{:S(2)}, u32[]{:S(2)}) %collective-permute-start.8) | collective-permute-done | bytes 139296 | tf_op jit(solution)/shard_map/ppermute | solution.py:415
  22.3 0.4 %shard_map.99.refs_1_ = f32[512,512]{1,0:T(8,128)S(1)} custom-call(bf16[512,256]{1,0:T(8,128)(2,1)S(1)} %get-tuple-element.53.scores_ref, bf16[512,128]{1,0:T(8,128)(2,1)S(1)} %get-tuple-element.52.refs_0_.turned_ref, bf16[136,512]{1,0:T(8,128)(2,1)S(1)} %collective-permute-done.8.x_ref.refs_5_, f32[512,128]{1,0:T(8,128)S(1)} %get-tuple-element.64._.refs_7_, ...), custom_call_target="tpu_custom_call" | custom-call | tf_op jit(solution)/shard_map/pallas_call | solution.py:399
  22.7 0.3 shard_map.100
  23.0 0.7 %collective-permute-start.12 = (f32[1,512]{1,0:T(1,128)S(1)}, f32[1,512]{1,0:T(1,128)S(1)}, u32[]{:S(2)}, u32[]{:S(2)}) collective-permute-start(f32[1,512]{1,0:T(1,128)S(1)} %get-tuple-element.66.refs_0_), channel_id=1, source_target_pairs={{0,1},{1,2},{2,3},{3,0},{4,5},{5,6},{6,7},{7,4},{8,9},{9,10},{10,1... | collective-permute-start | bytes 6152 | tf_op jit(solution)/shard_map/ppermute | solution.py:430
  23.7 1.6 %collective-permute-start.13 = (f32[1,512]{1,0:T(1,128)S(1)}, f32[1,512]{1,0:T(1,128)S(1)}, u32[]{:S(2)}, u32[]{:S(2)}) collective-permute-start(f32[1,512]{1,0:T(1,128)S(1)} %get-tuple-element.66.refs_0_), channel_id=1, source_target_pairs={{0,2},{1,3},{2,0},{3,1},{4,6},{5,7},{6,4},{7,5},{8,10},{9,11},{10,... | collective-permute-start | bytes 6152 | tf_op jit(solution)/shard_map/ppermute | solution.py:430
  25.3 2.0 %collective-permute-start.14 = (f32[1,512]{1,0:T(1,128)S(1)}, f32[1,512]{1,0:T(1,128)S(1)}, u32[]{:S(2)}, u32[]{:S(2)}) collective-permute-start(f32[1,512]{1,0:T(1,128)S(1)} %get-tuple-element.66.refs_0_), channel_id=1, source_target_pairs={{0,3},{1,0},{2,1},{3,2},{4,7},{5,4},{6,5},{7,6},{8,11},{9,8},{10,9... | collective-permute-start | bytes 6152 | tf_op jit(solution)/shard_map/ppermute | solution.py:430
  27.4 1.0 %collective-permute-done.12.refs_1_ = f32[1,512]{1,0:T(1,128)S(1)} collective-permute-done((f32[1,512]{1,0:T(1,128)S(1)}, f32[1,512]{1,0:T(1,128)S(1)}, u32[]{:S(2)}, u32[]{:S(2)}) %collective-permute-start.12) | collective-permute-done | bytes 2080 | tf_op jit(solution)/shard_map/ppermute | solution.py:430
  28.4 0.6 %collective-permute-done.14.refs_3_ = f32[1,512]{1,0:T(1,128)S(1)} collective-permute-done((f32[1,512]{1,0:T(1,128)S(1)}, f32[1,512]{1,0:T(1,128)S(1)}, u32[]{:S(2)}, u32[]{:S(2)}) %collective-permute-start.14) | collective-permute-done | bytes 2080 | tf_op jit(solution)/shard_map/ppermute | solution.py:430
  28.9 1.2 %shard_map.101 = bf16[512,1024]{1,0:T(8,128)(2,1)} custom-call(f32[1,512]{1,0:T(1,128)S(1)} %get-tuple-element.66.refs_0_, f32[1,512]{1,0:T(1,128)S(1)} %collective-permute-done.12.refs_1_, f32[1,512]{1,0:T(1,128)S(1)} %collective-permute-done.13.refs_2_, f32[1,512]{1,0:T(1,128)S(1)} %collective-permute-done.14.refs_3_, ...), custom_call_target="tpu_custom_call" | custom-call | flops 268435456 | bytes 3145728 | tf_op jit(solution)/shard_map/pallas_call | solution.py:399
  (9 shorter events, 0.0 us)
Async XLA Ops:
  0.0 10.2 %collective-permute-start = (bf16[32,512]{1,0:T(8,128)(2,1)}, bf16[32,512]{1,0:T(8,128)(2,1)S(1)}, u32[]{:S(2)}, u32[]{:S(2)}) collective-permute-start(bf16[32,512]{1,0:T(8,128)(2,1)} %refs_6_.1), channel_id=1, source_target_pairs={{0,2},{1,3},{2,0},{3,1},{4,6},{5,7},{6,4},{7,5},{8,10},{9,11},{10,... | collective-permute-start | bytes 98312 | tf_op jit(solution)/shard_map/ppermute | solution.py:415
  4.0 6.2 %collective-permute-start.1 = (bf16[32,512]{1,0:T(8,128)(2,1)}, bf16[32,512]{1,0:T(8,128)(2,1)S(1)}, u32[]{:S(2)}, u32[]{:S(2)}) collective-permute-start(bf16[32,512]{1,0:T(8,128)(2,1)} %refs_6_.1), channel_id=1, source_target_pairs={{0,3},{1,2},{2,1},{3,0},{4,7},{5,6},{6,5},{7,4},{8,11},{9,10},{10,... | collective-permute-start | bytes 98312 | tf_op jit(solution)/shard_map/ppermute | solution.py:415
  5.4 4.9 %collective-permute-start.2 = (bf16[32,512]{1,0:T(8,128)(2,1)}, bf16[32,512]{1,0:T(8,128)(2,1)S(1)}, u32[]{:S(2)}, u32[]{:S(2)}) collective-permute-start(bf16[32,512]{1,0:T(8,128)(2,1)} %refs_6_.1), channel_id=1, source_target_pairs={{0,1},{1,0},{2,3},{3,2},{4,5},{5,4},{6,7},{7,6},{8,9},{9,8},{10,11... | collective-permute-start | bytes 98312 | tf_op jit(solution)/shard_map/ppermute | solution.py:415
  5.6 5.1 %collective-permute-start.3 = (bf16[32,512]{1,0:T(8,128)(2,1)}, bf16[32,512]{1,0:T(8,128)(2,1)S(1)}, u32[]{:S(2)}, u32[]{:S(2)}) collective-permute-start(bf16[32,512]{1,0:T(8,128)(2,1)} %refs_7_.1), channel_id=1, source_target_pairs={{0,2},{1,3},{2,0},{3,1},{4,6},{5,7},{6,4},{7,5},{8,10},{9,11},{10,... | collective-permute-start | bytes 98312 | tf_op jit(solution)/shard_map/ppermute | solution.py:415
  10.6 1.4 %collective-permute-start.5 = (bf16[136,512]{1,0:T(8,128)(2,1)S(1)}, bf16[136,512]{1,0:T(8,128)(2,1)S(1)}, u32[]{:S(2)}, u32[]{:S(2)}) collective-permute-start(bf16[136,512]{1,0:T(8,128)(2,1)S(1)} %get-tuple-element.46), channel_id=1, source_target_pairs={{0,4},{4,0},{8,12},{12,8},{16,20},{20,16},{24,28},{28,24},{1,5},{5... | collective-permute-start | bytes 417800 | tf_op jit(solution)/shard_map/ppermute | solution.py:415
  12.1 8.7 %collective-permute-start.6 = (bf16[136,512]{1,0:T(8,128)(2,1)S(1)}, bf16[136,512]{1,0:T(8,128)(2,1)S(1)}, u32[]{:S(2)}, u32[]{:S(2)}) collective-permute-start(bf16[136,512]{1,0:T(8,128)(2,1)S(1)} %shard_map.94.refs_5_), channel_id=1, source_target_pairs={{0,16},{4,20},{8,24},{12,28},{16,0},{20,4},{24,8},{28,12},{1,17},{... | collective-permute-start | bytes 417800 | tf_op jit(solution)/shard_map/ppermute | solution.py:415
  13.7 7.2 %collective-permute-start.7 = (bf16[136,512]{1,0:T(8,128)(2,1)S(1)}, bf16[136,512]{1,0:T(8,128)(2,1)S(1)}, u32[]{:S(2)}, u32[]{:S(2)}) collective-permute-start(bf16[136,512]{1,0:T(8,128)(2,1)S(1)} %shard_map.94.refs_5_), channel_id=1, source_target_pairs={{0,8},{4,12},{8,0},{12,4},{16,24},{20,28},{24,16},{28,20},{1,9},{5... | collective-permute-start | bytes 417800 | tf_op jit(solution)/shard_map/ppermute | solution.py:415
  15.2 5.9 %collective-permute-start.9 = (bf16[136,512]{1,0:T(8,128)(2,1)S(1)}, bf16[136,512]{1,0:T(8,128)(2,1)S(1)}, u32[]{:S(2)}, u32[]{:S(2)}) collective-permute-start(bf16[136,512]{1,0:T(8,128)(2,1)S(1)} %shard_map.94.refs_5_), channel_id=1, source_target_pairs={{0,24},{4,28},{24,8},{28,12},{8,16},{12,20},{16,0},{20,4},{1,25},{... | collective-permute-start | bytes 417800 | tf_op jit(solution)/shard_map/ppermute | solution.py:531
  15.7 5.5 %collective-permute-start.10 = (bf16[136,512]{1,0:T(8,128)(2,1)S(1)}, bf16[136,512]{1,0:T(8,128)(2,1)S(1)}, u32[]{:S(2)}, u32[]{:S(2)}) collective-permute-start(bf16[136,512]{1,0:T(8,128)(2,1)S(1)} %get-tuple-element.62._.mine_ref), channel_id=1, source_target_pairs={{0,4},{4,0},{8,12},{12,8},{16,20},{20,16},{24,28},{28,24},{1,5},{5... | collective-permute-start | bytes 417800 | tf_op jit(solution)/shard_map/ppermute | solution.py:415
  15.7 4.5 %collective-permute-start.4 = (bf16[64,512]{1,0:T(8,128)(2,1)S(1)}, bf16[64,512]{1,0:T(8,128)(2,1)S(1)}, u32[]{:S(2)}, u32[]{:S(2)}) collective-permute-start(bf16[64,512]{1,0:T(8,128)(2,1)S(1)} %shard_map.93._.refs_4_), channel_id=1, source_target_pairs={{0,1},{1,0},{2,3},{3,2},{4,5},{5,4},{6,7},{7,6},{8,9},{9,8},{10,11... | collective-permute-start | bytes 196616 | tf_op jit(solution)/shard_map/ppermute | solution.py:415
  20.9 1.4 %collective-permute-start.8 = (bf16[136,512]{1,0:T(8,128)(2,1)S(1)}, bf16[136,512]{1,0:T(8,128)(2,1)S(1)}, u32[]{:S(2)}, u32[]{:S(2)}) collective-permute-start(bf16[136,512]{1,0:T(8,128)(2,1)S(1)} %collective-permute-done.7.x_ref.refs_5_), channel_id=1, source_target_pairs={{0,4},{4,0},{8,12},{12,8},{16,20},{20,16},{24,28},{28,24},{1,5},{5... | collective-permute-start | bytes 417800 | tf_op jit(solution)/shard_map/ppermute | solution.py:415
  21.2 1.4 %collective-permute-start.11 = (bf16[128,512]{1,0:T(8,128)(2,1)S(1)}, bf16[128,512]{1,0:T(8,128)(2,1)S(1)}, u32[]{:S(2)}, u32[]{:S(2)}) collective-permute-start(bf16[128,512]{1,0:T(8,128)(2,1)S(1)} %shard_map.97.refs_6_), channel_id=1, source_target_pairs={{0,4},{4,0},{8,12},{12,8},{16,20},{20,16},{24,28},{28,24},{1,5},{5... | collective-permute-start | bytes 393224 | tf_op jit(solution)/shard_map/ppermute | solution.py:415
  23.0 5.4 %collective-permute-start.12 = (f32[1,512]{1,0:T(1,128)S(1)}, f32[1,512]{1,0:T(1,128)S(1)}, u32[]{:S(2)}, u32[]{:S(2)}) collective-permute-start(f32[1,512]{1,0:T(1,128)S(1)} %get-tuple-element.66.refs_0_), channel_id=1, source_target_pairs={{0,1},{1,2},{2,3},{3,0},{4,5},{5,6},{6,7},{7,4},{8,9},{9,10},{10,1... | collective-permute-start | bytes 6152 | tf_op jit(solution)/shard_map/ppermute | solution.py:430
  23.7 4.7 %collective-permute-start.13 = (f32[1,512]{1,0:T(1,128)S(1)}, f32[1,512]{1,0:T(1,128)S(1)}, u32[]{:S(2)}, u32[]{:S(2)}) collective-permute-start(f32[1,512]{1,0:T(1,128)S(1)} %get-tuple-element.66.refs_0_), channel_id=1, source_target_pairs={{0,2},{1,3},{2,0},{3,1},{4,6},{5,7},{6,4},{7,5},{8,10},{9,11},{10,... | collective-permute-start | bytes 6152 | tf_op jit(solution)/shard_map/ppermute | solution.py:430
  25.3 3.6 %collective-permute-start.14 = (f32[1,512]{1,0:T(1,128)S(1)}, f32[1,512]{1,0:T(1,128)S(1)}, u32[]{:S(2)}, u32[]{:S(2)}) collective-permute-start(f32[1,512]{1,0:T(1,128)S(1)} %get-tuple-element.66.refs_0_), channel_id=1, source_target_pairs={{0,3},{1,0},{2,1},{3,2},{4,7},{5,4},{6,5},{7,6},{8,11},{9,8},{10,9... | collective-permute-start | bytes 6152 | tf_op jit(solution)/shard_map/ppermute | solution.py:430

commit v26 on v25

--- a/solution.py
+++ b/solution.py
@@ -11,7 +11,7 @@
 GROUP = 256
 DECAY_ROWS = 8
 BLOCK = 256
-NORM_CHUNKS = 4
+NORM_CHUNKS = 8
 FIRST_HOP = 2
 LATER_SHIFTS = (2, 1, 3)
 CYCLE = [(2 * chip + core, 2 * target + core) for chip, target in ((0, 3), (3, 1), (1, 2), (2, 0)) for core in (0, 1)]

time: 30.6 us -> 30.7 us (level)
  no operation moved by 1% of the time
where the time goes in v26:
time: 30.7 us; the launch traced here: 30.2 us
  starting transfers between devices  17.5 us (57%)
  Pallas kernels  6.91 us (23%)
  waiting for transfers between devices  5.66 us (18%)
    ppermute x11, starting transfers between devices, flip(): lax.ppermute(array, axis, [(i, i ^ mask) for i in range(lax.axis_size(axi...  12.7 us
    pallas_call x11, Pallas kernels, call(): pl.pallas_call(kernel, out_shape=out_shape, in_specs=specs, out_specs=jax...  6.91 us
    ppermute x3, starting transfers between devices, around(): received.append(lax.ppermute(array, ('seq', 'head'), pairs))  4.36 us
    ppermute x11, waiting for transfers between devices, flip(): lax.ppermute(array, axis, [(i, i ^ mask) for i in range(lax.axis_size(axi...  3.87 us
    ppermute x3, waiting for transfers between devices, around(): received.append(lax.ppermute(array, ('seq', 'head'), pairs))  1.59 us
  transfers between devices with their start and end apart: 15, of which 6 were waited for; matrix products, arithmetic and copies ran while one was open for 0% of the time, Pallas kernels for 17%

profile of v26, /device:TPU:0, one launch (start us, length us, event | category | flops | bytes accessed | tf_op | source)
XLA Modules:
  0.0 30.2 jit_solution(13183760166963462857)
XLA Ops:
  0.0 4.0 %collective-permute-start = (bf16[32,512]{1,0:T(8,128)(2,1)}, bf16[32,512]{1,0:T(8,128)(2,1)S(1)}, u32[]{:S(2)}, u32[]{:S(2)}) collective-permute-start(bf16[32,512]{1,0:T(8,128)(2,1)} %refs_6_.1), channel_id=1, source_target_pairs={{0,2},{1,3},{2,0},{3,1},{4,6},{5,7},{6,4},{7,5},{8,10},{9,11},{10,... | collective-permute-start | bytes 98312 | tf_op jit(solution)/shard_map/ppermute | solution.py:415
  4.0 1.3 %collective-permute-start.1 = (bf16[32,512]{1,0:T(8,128)(2,1)}, bf16[32,512]{1,0:T(8,128)(2,1)S(1)}, u32[]{:S(2)}, u32[]{:S(2)}) collective-permute-start(bf16[32,512]{1,0:T(8,128)(2,1)} %refs_6_.1), channel_id=1, source_target_pairs={{0,3},{1,2},{2,1},{3,0},{4,7},{5,6},{6,5},{7,4},{8,11},{9,10},{10,... | collective-permute-start | bytes 98312 | tf_op jit(solution)/shard_map/ppermute | solution.py:415
  5.4 0.2 collective-permute-start.2
  5.6 2.8 %collective-permute-start.3 = (bf16[32,512]{1,0:T(8,128)(2,1)}, bf16[32,512]{1,0:T(8,128)(2,1)S(1)}, u32[]{:S(2)}, u32[]{:S(2)}) collective-permute-start(bf16[32,512]{1,0:T(8,128)(2,1)} %refs_7_.1), channel_id=1, source_target_pairs={{0,2},{1,3},{2,0},{3,1},{4,6},{5,7},{6,4},{7,5},{8,10},{9,11},{10,... | collective-permute-start | bytes 98312 | tf_op jit(solution)/shard_map/ppermute | solution.py:415
  8.4 1.8 %shard_map.91 = (bf16[512,1024]{1,0:T(8,128)(2,1)S(1)}, f32[16,512]{1,0:T(8,128)S(1)}, bf16[512,1024]{1,0:T(8,128)(2,1)S(1)}, bf16[512,1024]{1,0:T(8,128)(2,1)S(...) custom-call(f32[16,512]{1,0:T(8,128)} %refs_0_.1, ...), custom_call_target="tpu_custom_call" | custom-call | flops 4294967296 | bytes 2097152 | tf_op jit(solution)/shard_map/pallas_call | solution.py:399
  10.2 0.0 collective-permute-done.refs_1_
  10.3 0.0 collective-permute-done.2.refs_3_
  10.3 0.3 %shard_map.92 = (bf16[136,512]{1,0:T(8,128)(2,1)S(1)}, bf16[136,512]{1,0:T(8,128)(2,1)S(1)}, bf16[128,1024]{1,0:T(8,128)(2,1)S(1)}) custom-call(bf16[32,512]{1,0:T(8,128)(2,1)S(1)} %get-tuple-element.37.refs_0_, bf16[32,512]{1,0:T(8,128)(2,1)S(1)} %collective-permute-done.refs_1_, bf16[32,512]{1,0:T(8,128)(2,1)S(1)} %collective-permute-done.1.refs_2_, ...), custom_call_target="tpu_custom_call" | custom-call | flops 268435456 | tf_op jit(solution)/shard_map/pallas_call | solution.py:399
  10.6 0.1 collective-permute-start.5
  10.7 1.3 %collective-permute-done.5.theirs_ref.refs_9_.refs_4_ = bf16[136,512]{1,0:T(8,128)(2,1)S(1)} collective-permute-done((bf16[136,512]{1,0:T(8,128)(2,1)S(1)}, bf16[136,512]{1,0:T(8,128)(2,1)S(1)}, u32[]{:S(2)}, u32[]{:S(2)}) %collective-permute-start.5) | collective-permute-done | bytes 139296 | tf_op jit(solution)/shard_map/ppermute | solution.py:415
  12.0 0.1 shard_map.94.refs_5_
  12.1 1.6 %collective-permute-start.6 = (bf16[136,512]{1,0:T(8,128)(2,1)S(1)}, bf16[136,512]{1,0:T(8,128)(2,1)S(1)}, u32[]{:S(2)}, u32[]{:S(2)}) collective-permute-start(bf16[136,512]{1,0:T(8,128)(2,1)S(1)} %shard_map.94.refs_5_), channel_id=1, source_target_pairs={{0,16},{4,20},{8,24},{12,28},{16,0},{20,4},{24,8},{28,12},{1,17},{... | collective-permute-start | bytes 417800 | tf_op jit(solution)/shard_map/ppermute | solution.py:415
  13.7 1.5 %collective-permute-start.7 = (bf16[136,512]{1,0:T(8,128)(2,1)S(1)}, bf16[136,512]{1,0:T(8,128)(2,1)S(1)}, u32[]{:S(2)}, u32[]{:S(2)}) collective-permute-start(bf16[136,512]{1,0:T(8,128)(2,1)S(1)} %shard_map.94.refs_5_), channel_id=1, source_target_pairs={{0,8},{4,12},{8,0},{12,4},{16,24},{20,28},{24,16},{28,20},{1,9},{5... | collective-permute-start | bytes 417800 | tf_op jit(solution)/shard_map/ppermute | solution.py:415
  15.2 0.5 %collective-permute-start.9 = (bf16[136,512]{1,0:T(8,128)(2,1)S(1)}, bf16[136,512]{1,0:T(8,128)(2,1)S(1)}, u32[]{:S(2)}, u32[]{:S(2)}) collective-permute-start(bf16[136,512]{1,0:T(8,128)(2,1)S(1)} %shard_map.94.refs_5_), channel_id=1, source_target_pairs={{0,24},{4,28},{24,8},{28,12},{8,16},{12,20},{16,0},{20,4},{1,25},{... | collective-permute-start | bytes 417800 | tf_op jit(solution)/shard_map/ppermute | solution.py:531
  15.7 0.7 %collective-permute-start.4 = (bf16[64,512]{1,0:T(8,128)(2,1)S(1)}, bf16[64,512]{1,0:T(8,128)(2,1)S(1)}, u32[]{:S(2)}, u32[]{:S(2)}) collective-permute-start(bf16[64,512]{1,0:T(8,128)(2,1)S(1)} %shard_map.93._.refs_4_), channel_id=1, source_target_pairs={{0,1},{1,0},{2,3},{3,2},{4,5},{5,4},{6,7},{7,6},{8,9},{9,8},{10,11... | collective-permute-start | bytes 196616 | tf_op jit(solution)/shard_map/ppermute | solution.py:415
  16.3 1.8 %shard_map.95 = (f32[512,1024]{1,0:T(8,128)S(1)}, f32[512,1024]{1,0:T(8,128)S(1)}, bf16[3,512,1024]{2,1,0:T(8,128)(2,1)S(1)}, bf16[1,256,1024]{2,1,0:T(8,128)(2,1)S(1)}) custom-call(bf16[512,1024]{1,0:T(8,128)(2,1)S(1)} %get-tuple-element.42.refs_0_, bf16[512,1024]{1,0:T(8,128)(2,1)S(1)} %get-tuple-element.43.refs_1_, ...), custom_call_target="tpu_custom_call" | custom-call | flops 1342177280 | tf_op jit(solution)/shard_map/pallas_call | solution.py:399
  18.1 2.0 %collective-permute-done.4.refs_5_ = bf16[64,512]{1,0:T(8,128)(2,1)S(1)} collective-permute-done((bf16[64,512]{1,0:T(8,128)(2,1)S(1)}, bf16[64,512]{1,0:T(8,128)(2,1)S(1)}, u32[]{:S(2)}, u32[]{:S(2)}) %collective-permute-start.4) | collective-permute-done | bytes 65568 | tf_op jit(solution)/shard_map/ppermute | solution.py:415
  20.2 0.7 %shard_map.96 = (f32[512,512]{1,0:T(8,128)S(1)}, bf16[512,128]{1,0:T(8,128)(2,1)S(1)}, bf16[512,256]{1,0:T(8,128)(2,1)S(1)}) custom-call(bf16[32,512]{1,0:T(8,128)(2,1)S(1)} %get-tuple-element.37.refs_0_, bf16[32,512]{1,0:T(8,128)(2,1)S(1)} %collective-permute-done.refs_1_, bf16[32,512]{1,0:T(8,128)(2,1)S(1)} %collective-permute-done.1.refs_2_, ...), custom_call_target="tpu_custom_call" | custom-call | tf_op jit(solution)/shard_map/pallas_call | solution.py:399
  20.9 0.1 collective-permute-start.8
  20.9 0.2 collective-permute-done.9.diagonal_ref
  21.1 0.1 shard_map.97.refs_6_
  21.2 0.4 %collective-permute-start.11 = (bf16[128,512]{1,0:T(8,128)(2,1)S(1)}, bf16[128,512]{1,0:T(8,128)(2,1)S(1)}, u32[]{:S(2)}, u32[]{:S(2)}) collective-permute-start(bf16[128,512]{1,0:T(8,128)(2,1)S(1)} %shard_map.97.refs_6_), channel_id=1, source_target_pairs={{0,4},{4,0},{8,12},{12,8},{16,20},{20,16},{24,28},{28,24},{1,5},{5... | collective-permute-start | bytes 393224 | tf_op jit(solution)/shard_map/ppermute | solution.py:415
  21.6 0.2 shard_map.98
  21.8 0.5 %collective-permute-done.8.x_ref.refs_5_ = bf16[136,512]{1,0:T(8,128)(2,1)S(1)} collective-permute-done((bf16[136,512]{1,0:T(8,128)(2,1)S(1)}, bf16[136,512]{1,0:T(8,128)(2,1)S(1)}, u32[]{:S(2)}, u32[]{:S(2)}) %collective-permute-start.8) | collective-permute-done | bytes 139296 | tf_op jit(solution)/shard_map/ppermute | solution.py:415
  22.3 0.4 %shard_map.99.refs_1_ = f32[512,512]{1,0:T(8,128)S(1)} custom-call(bf16[512,256]{1,0:T(8,128)(2,1)S(1)} %get-tuple-element.53.scores_ref, bf16[512,128]{1,0:T(8,128)(2,1)S(1)} %get-tuple-element.52.refs_0_.turned_ref, bf16[136,512]{1,0:T(8,128)(2,1)S(1)} %collective-permute-done.8.x_ref.refs_5_, f32[512,128]{1,0:T(8,128)S(1)} %get-tuple-element.64._.refs_7_, ...), custom_call_target="tpu_custom_call" | custom-call | tf_op jit(solution)/shard_map/pallas_call | solution.py:399
  22.7 0.3 shard_map.100
  23.0 0.7 %collective-permute-start.12 = (f32[1,512]{1,0:T(1,128)S(1)}, f32[1,512]{1,0:T(1,128)S(1)}, u32[]{:S(2)}, u32[]{:S(2)}) collective-permute-start(f32[1,512]{1,0:T(1,128)S(1)} %get-tuple-element.66.refs_0_), channel_id=1, source_target_pairs={{0,1},{1,2},{2,3},{3,0},{4,5},{5,6},{6,7},{7,4},{8,9},{9,10},{10,1... | collective-permute-start | bytes 6152 | tf_op jit(solution)/shard_map/ppermute | solution.py:430
  23.7 1.6 %collective-permute-start.13 = (f32[1,512]{1,0:T(1,128)S(1)}, f32[1,512]{1,0:T(1,128)S(1)}, u32[]{:S(2)}, u32[]{:S(2)}) collective-permute-start(f32[1,512]{1,0:T(1,128)S(1)} %get-tuple-element.66.refs_0_), channel_id=1, source_target_pairs={{0,2},{1,3},{2,0},{3,1},{4,6},{5,7},{6,4},{7,5},{8,10},{9,11},{10,... | collective-permute-start | bytes 6152 | tf_op jit(solution)/shard_map/ppermute | solution.py:430
  25.3 2.0 %collective-permute-start.14 = (f32[1,512]{1,0:T(1,128)S(1)}, f32[1,512]{1,0:T(1,128)S(1)}, u32[]{:S(2)}, u32[]{:S(2)}) collective-permute-start(f32[1,512]{1,0:T(1,128)S(1)} %get-tuple-element.66.refs_0_), channel_id=1, source_target_pairs={{0,3},{1,0},{2,1},{3,2},{4,7},{5,4},{6,5},{7,6},{8,11},{9,8},{10,9... | collective-permute-start | bytes 6152 | tf_op jit(solution)/shard_map/ppermute | solution.py:430
  27.4 1.0 %collective-permute-done.12.refs_1_ = f32[1,512]{1,0:T(1,128)S(1)} collective-permute-done((f32[1,512]{1,0:T(1,128)S(1)}, f32[1,512]{1,0:T(1,128)S(1)}, u32[]{:S(2)}, u32[]{:S(2)}) %collective-permute-start.12) | collective-permute-done | bytes 2080 | tf_op jit(solution)/shard_map/ppermute | solution.py:430
  28.4 0.6 %collective-permute-done.14.refs_3_ = f32[1,512]{1,0:T(1,128)S(1)} collective-permute-done((f32[1,512]{1,0:T(1,128)S(1)}, f32[1,512]{1,0:T(1,128)S(1)}, u32[]{:S(2)}, u32[]{:S(2)}) %collective-permute-start.14) | collective-permute-done | bytes 2080 | tf_op jit(solution)/shard_map/ppermute | solution.py:430
  28.9 1.3 %shard_map.101 = bf16[512,1024]{1,0:T(8,128)(2,1)} custom-call(f32[1,512]{1,0:T(1,128)S(1)} %get-tuple-element.66.refs_0_, f32[1,512]{1,0:T(1,128)S(1)} %collective-permute-done.12.refs_1_, f32[1,512]{1,0:T(1,128)S(1)} %collective-permute-done.13.refs_2_, f32[1,512]{1,0:T(1,128)S(1)} %collective-permute-done.14.refs_3_, ...), custom_call_target="tpu_custom_call" | custom-call | flops 268435456 | bytes 3145728 | tf_op jit(solution)/shard_map/pallas_call | solution.py:399
  (9 shorter events, 0.0 us)
Async XLA Ops:
  0.0 10.2 %collective-permute-start = (bf16[32,512]{1,0:T(8,128)(2,1)}, bf16[32,512]{1,0:T(8,128)(2,1)S(1)}, u32[]{:S(2)}, u32[]{:S(2)}) collective-permute-start(bf16[32,512]{1,0:T(8,128)(2,1)} %refs_6_.1), channel_id=1, source_target_pairs={{0,2},{1,3},{2,0},{3,1},{4,6},{5,7},{6,4},{7,5},{8,10},{9,11},{10,... | collective-permute-start | bytes 98312 | tf_op jit(solution)/shard_map/ppermute | solution.py:415
  4.0 6.2 %collective-permute-start.1 = (bf16[32,512]{1,0:T(8,128)(2,1)}, bf16[32,512]{1,0:T(8,128)(2,1)S(1)}, u32[]{:S(2)}, u32[]{:S(2)}) collective-permute-start(bf16[32,512]{1,0:T(8,128)(2,1)} %refs_6_.1), channel_id=1, source_target_pairs={{0,3},{1,2},{2,1},{3,0},{4,7},{5,6},{6,5},{7,4},{8,11},{9,10},{10,... | collective-permute-start | bytes 98312 | tf_op jit(solution)/shard_map/ppermute | solution.py:415
  5.4 4.9 %collective-permute-start.2 = (bf16[32,512]{1,0:T(8,128)(2,1)}, bf16[32,512]{1,0:T(8,128)(2,1)S(1)}, u32[]{:S(2)}, u32[]{:S(2)}) collective-permute-start(bf16[32,512]{1,0:T(8,128)(2,1)} %refs_6_.1), channel_id=1, source_target_pairs={{0,1},{1,0},{2,3},{3,2},{4,5},{5,4},{6,7},{7,6},{8,9},{9,8},{10,11... | collective-permute-start | bytes 98312 | tf_op jit(solution)/shard_map/ppermute | solution.py:415
  5.6 5.1 %collective-permute-start.3 = (bf16[32,512]{1,0:T(8,128)(2,1)}, bf16[32,512]{1,0:T(8,128)(2,1)S(1)}, u32[]{:S(2)}, u32[]{:S(2)}) collective-permute-start(bf16[32,512]{1,0:T(8,128)(2,1)} %refs_7_.1), channel_id=1, source_target_pairs={{0,2},{1,3},{2,0},{3,1},{4,6},{5,7},{6,4},{7,5},{8,10},{9,11},{10,... | collective-permute-start | bytes 98312 | tf_op jit(solution)/shard_map/ppermute | solution.py:415
  10.6 1.4 %collective-permute-start.5 = (bf16[136,512]{1,0:T(8,128)(2,1)S(1)}, bf16[136,512]{1,0:T(8,128)(2,1)S(1)}, u32[]{:S(2)}, u32[]{:S(2)}) collective-permute-start(bf16[136,512]{1,0:T(8,128)(2,1)S(1)} %get-tuple-element.46), channel_id=1, source_target_pairs={{0,4},{4,0},{8,12},{12,8},{16,20},{20,16},{24,28},{28,24},{1,5},{5... | collective-permute-start | bytes 417800 | tf_op jit(solution)/shard_map/ppermute | solution.py:415
  12.1 8.7 %collective-permute-start.6 = (bf16[136,512]{1,0:T(8,128)(2,1)S(1)}, bf16[136,512]{1,0:T(8,128)(2,1)S(1)}, u32[]{:S(2)}, u32[]{:S(2)}) collective-permute-start(bf16[136,512]{1,0:T(8,128)(2,1)S(1)} %shard_map.94.refs_5_), channel_id=1, source_target_pairs={{0,16},{4,20},{8,24},{12,28},{16,0},{20,4},{24,8},{28,12},{1,17},{... | collective-permute-start | bytes 417800 | tf_op jit(solution)/shard_map/ppermute | solution.py:415
  13.7 7.2 %collective-permute-start.7 = (bf16[136,512]{1,0:T(8,128)(2,1)S(1)}, bf16[136,512]{1,0:T(8,128)(2,1)S(1)}, u32[]{:S(2)}, u32[]{:S(2)}) collective-permute-start(bf16[136,512]{1,0:T(8,128)(2,1)S(1)} %shard_map.94.refs_5_), channel_id=1, source_target_pairs={{0,8},{4,12},{8,0},{12,4},{16,24},{20,28},{24,16},{28,20},{1,9},{5... | collective-permute-start | bytes 417800 | tf_op jit(solution)/shard_map/ppermute | solution.py:415
  15.2 5.9 %collective-permute-start.9 = (bf16[136,512]{1,0:T(8,128)(2,1)S(1)}, bf16[136,512]{1,0:T(8,128)(2,1)S(1)}, u32[]{:S(2)}, u32[]{:S(2)}) collective-permute-start(bf16[136,512]{1,0:T(8,128)(2,1)S(1)} %shard_map.94.refs_5_), channel_id=1, source_target_pairs={{0,24},{4,28},{24,8},{28,12},{8,16},{12,20},{16,0},{20,4},{1,25},{... | collective-permute-start | bytes 417800 | tf_op jit(solution)/shard_map/ppermute | solution.py:531
  15.7 5.5 %collective-permute-start.10 = (bf16[136,512]{1,0:T(8,128)(2,1)S(1)}, bf16[136,512]{1,0:T(8,128)(2,1)S(1)}, u32[]{:S(2)}, u32[]{:S(2)}) collective-permute-start(bf16[136,512]{1,0:T(8,128)(2,1)S(1)} %get-tuple-element.62._.mine_ref), channel_id=1, source_target_pairs={{0,4},{4,0},{8,12},{12,8},{16,20},{20,16},{24,28},{28,24},{1,5},{5... | collective-permute-start | bytes 417800 | tf_op jit(solution)/shard_map/ppermute | solution.py:415
  15.7 4.5 %collective-permute-start.4 = (bf16[64,512]{1,0:T(8,128)(2,1)S(1)}, bf16[64,512]{1,0:T(8,128)(2,1)S(1)}, u32[]{:S(2)}, u32[]{:S(2)}) collective-permute-start(bf16[64,512]{1,0:T(8,128)(2,1)S(1)} %shard_map.93._.refs_4_), channel_id=1, source_target_pairs={{0,1},{1,0},{2,3},{3,2},{4,5},{5,4},{6,7},{7,6},{8,9},{9,8},{10,11... | collective-permute-start | bytes 196616 | tf_op jit(solution)/shard_map/ppermute | solution.py:415
  20.9 1.4 %collective-permute-start.8 = (bf16[136,512]{1,0:T(8,128)(2,1)S(1)}, bf16[136,512]{1,0:T(8,128)(2,1)S(1)}, u32[]{:S(2)}, u32[]{:S(2)}) collective-permute-start(bf16[136,512]{1,0:T(8,128)(2,1)S(1)} %collective-permute-done.7.x_ref.refs_5_), channel_id=1, source_target_pairs={{0,4},{4,0},{8,12},{12,8},{16,20},{20,16},{24,28},{28,24},{1,5},{5... | collective-permute-start | bytes 417800 | tf_op jit(solution)/shard_map/ppermute | solution.py:415
  21.2 1.4 %collective-permute-start.11 = (bf16[128,512]{1,0:T(8,128)(2,1)S(1)}, bf16[128,512]{1,0:T(8,128)(2,1)S(1)}, u32[]{:S(2)}, u32[]{:S(2)}) collective-permute-start(bf16[128,512]{1,0:T(8,128)(2,1)S(1)} %shard_map.97.refs_6_), channel_id=1, source_target_pairs={{0,4},{4,0},{8,12},{12,8},{16,20},{20,16},{24,28},{28,24},{1,5},{5... | collective-permute-start | bytes 393224 | tf_op jit(solution)/shard_map/ppermute | solution.py:415
  23.0 5.4 %collective-permute-start.12 = (f32[1,512]{1,0:T(1,128)S(1)}, f32[1,512]{1,0:T(1,128)S(1)}, u32[]{:S(2)}, u32[]{:S(2)}) collective-permute-start(f32[1,512]{1,0:T(1,128)S(1)} %get-tuple-element.66.refs_0_), channel_id=1, source_target_pairs={{0,1},{1,2},{2,3},{3,0},{4,5},{5,6},{6,7},{7,4},{8,9},{9,10},{10,1... | collective-permute-start | bytes 6152 | tf_op jit(solution)/shard_map/ppermute | solution.py:430
  23.7 4.7 %collective-permute-start.13 = (f32[1,512]{1,0:T(1,128)S(1)}, f32[1,512]{1,0:T(1,128)S(1)}, u32[]{:S(2)}, u32[]{:S(2)}) collective-permute-start(f32[1,512]{1,0:T(1,128)S(1)} %get-tuple-element.66.refs_0_), channel_id=1, source_target_pairs={{0,2},{1,3},{2,0},{3,1},{4,6},{5,7},{6,4},{7,5},{8,10},{9,11},{10,... | collective-permute-start | bytes 6152 | tf_op jit(solution)/shard_map/ppermute | solution.py:430
  25.3 3.6 %collective-permute-start.14 = (f32[1,512]{1,0:T(1,128)S(1)}, f32[1,512]{1,0:T(1,128)S(1)}, u32[]{:S(2)}, u32[]{:S(2)}) collective-permute-start(f32[1,512]{1,0:T(1,128)S(1)} %get-tuple-element.66.refs_0_), channel_id=1, source_target_pairs={{0,3},{1,0},{2,1},{3,2},{4,7},{5,4},{6,5},{7,6},{8,11},{9,8},{10,9... | collective-permute-start | bytes 6152 | tf_op jit(solution)/shard_map/ppermute | solution.py:430

commit v27 on v25

--- a/solution.py
+++ b/solution.py
@@ -10,7 +10,7 @@
 P_SIZE = 64
 GROUP = 256
 DECAY_ROWS = 8
-BLOCK = 256
+BLOCK = 128
 NORM_CHUNKS = 4
 FIRST_HOP = 2
 LATER_SHIFTS = (2, 1, 3)

time: 30.6 us -> 30.8 us (level)
  Pallas kernels: 6.85 us -> 7.48 us
  waiting for transfers between devices: 5.66 us -> 5.2 us
    pallas_call x11, Pallas kernels: 6.85 us -> 7.48 us  [call(): pl.pallas_call(kernel, out_shape=out_shape, in_specs=specs, out_specs=jax...]
    ppermute x11, waiting for transfers between devices: 3.87 us -> 3.53 us  [flip(): lax.ppermute(array, axis, [(i, i ^ mask) for i in range(lax.axis_size(axi...]
  transfers between devices with their start and end apart: 15 -> 15, of which waited for: 6 -> 6; matrix products, arithmetic and copies ran while one was open for 0% -> 0% of each run, Pallas kernels for 17% -> 19%
where the time goes in v27:
time: 30.8 us; the launch traced here: 30.5 us
  starting transfers between devices  17.7 us (57%)
  Pallas kernels  7.48 us (24%)
  waiting for transfers between devices  5.2 us (17%)
    ppermute x11, starting transfers between devices, flip(): lax.ppermute(array, axis, [(i, i ^ mask) for i in range(lax.axis_size(axi...  12.8 us
    pallas_call x11, Pallas kernels, call(): pl.pallas_call(kernel, out_shape=out_shape, in_specs=specs, out_specs=jax...  7.48 us
    ppermute x3, starting transfers between devices, around(): received.append(lax.ppermute(array, ('seq', 'head'), pairs))  4.35 us
    ppermute x11, waiting for transfers between devices, flip(): lax.ppermute(array, axis, [(i, i ^ mask) for i in range(lax.axis_size(axi...  3.53 us
    ppermute x3, waiting for transfers between devices, around(): received.append(lax.ppermute(array, ('seq', 'head'), pairs))  1.61 us
  transfers between devices with their start and end apart: 15, of which 6 were waited for; matrix products, arithmetic and copies ran while one was open for 0% of the time, Pallas kernels for 19%

profile of v27, /device:TPU:0, one launch (start us, length us, event | category | flops | bytes accessed | tf_op | source)
XLA Modules:
  0.0 30.5 jit_solution(2628361406299796626)
XLA Ops:
  0.0 4.0 %collective-permute-start = (bf16[32,512]{1,0:T(8,128)(2,1)}, bf16[32,512]{1,0:T(8,128)(2,1)S(1)}, u32[]{:S(2)}, u32[]{:S(2)}) collective-permute-start(bf16[32,512]{1,0:T(8,128)(2,1)} %refs_6_.1), channel_id=1, source_target_pairs={{0,2},{1,3},{2,0},{3,1},{4,6},{5,7},{6,4},{7,5},{8,10},{9,11},{10,... | collective-permute-start | bytes 98312 | tf_op jit(solution)/shard_map/ppermute | solution.py:415
  4.0 1.3 %collective-permute-start.1 = (bf16[32,512]{1,0:T(8,128)(2,1)}, bf16[32,512]{1,0:T(8,128)(2,1)S(1)}, u32[]{:S(2)}, u32[]{:S(2)}) collective-permute-start(bf16[32,512]{1,0:T(8,128)(2,1)} %refs_6_.1), channel_id=1, source_target_pairs={{0,3},{1,2},{2,1},{3,0},{4,7},{5,6},{6,5},{7,4},{8,11},{9,10},{10,... | collective-permute-start | bytes 98312 | tf_op jit(solution)/shard_map/ppermute | solution.py:415
  5.4 0.2 collective-permute-start.2
  5.6 2.8 %collective-permute-start.3 = (bf16[32,512]{1,0:T(8,128)(2,1)}, bf16[32,512]{1,0:T(8,128)(2,1)S(1)}, u32[]{:S(2)}, u32[]{:S(2)}) collective-permute-start(bf16[32,512]{1,0:T(8,128)(2,1)} %refs_7_.1), channel_id=1, source_target_pairs={{0,2},{1,3},{2,0},{3,1},{4,6},{5,7},{6,4},{7,5},{8,10},{9,11},{10,... | collective-permute-start | bytes 98312 | tf_op jit(solution)/shard_map/ppermute | solution.py:415
  8.4 1.8 %shard_map.91 = (bf16[512,1024]{1,0:T(8,128)(2,1)S(1)}, f32[16,512]{1,0:T(8,128)S(1)}, bf16[512,1024]{1,0:T(8,128)(2,1)S(1)}, bf16[512,1024]{1,0:T(8,128)(2,1)S(...) custom-call(f32[16,512]{1,0:T(8,128)} %refs_0_.1, ...), custom_call_target="tpu_custom_call" | custom-call | flops 4294967296 | bytes 2097152 | tf_op jit(solution)/shard_map/pallas_call | solution.py:399
  10.2 0.0 collective-permute-done.refs_1_
  10.3 0.0 collective-permute-done.2.refs_3_
  10.3 0.3 %shard_map.92 = (bf16[136,512]{1,0:T(8,128)(2,1)S(1)}, bf16[136,512]{1,0:T(8,128)(2,1)S(1)}, bf16[128,1024]{1,0:T(8,128)(2,1)S(1)}) custom-call(bf16[32,512]{1,0:T(8,128)(2,1)S(1)} %get-tuple-element.37.refs_0_, bf16[32,512]{1,0:T(8,128)(2,1)S(1)} %collective-permute-done.refs_1_, bf16[32,512]{1,0:T(8,128)(2,1)S(1)} %collective-permute-done.1.refs_2_, ...), custom_call_target="tpu_custom_call" | custom-call | flops 268435456 | tf_op jit(solution)/shard_map/pallas_call | solution.py:399
  10.6 0.1 collective-permute-start.5
  10.7 1.3 %collective-permute-done.5.theirs_ref.refs_9_.refs_4_ = bf16[136,512]{1,0:T(8,128)(2,1)S(1)} collective-permute-done((bf16[136,512]{1,0:T(8,128)(2,1)S(1)}, bf16[136,512]{1,0:T(8,128)(2,1)S(1)}, u32[]{:S(2)}, u32[]{:S(2)}) %collective-permute-start.5) | collective-permute-done | bytes 139296 | tf_op jit(solution)/shard_map/ppermute | solution.py:415
  12.1 0.1 shard_map.94.refs_5_
  12.1 1.6 %collective-permute-start.6 = (bf16[136,512]{1,0:T(8,128)(2,1)S(1)}, bf16[136,512]{1,0:T(8,128)(2,1)S(1)}, u32[]{:S(2)}, u32[]{:S(2)}) collective-permute-start(bf16[136,512]{1,0:T(8,128)(2,1)S(1)} %shard_map.94.refs_5_), channel_id=1, source_target_pairs={{0,16},{4,20},{8,24},{12,28},{16,0},{20,4},{24,8},{28,12},{1,17},{... | collective-permute-start | bytes 417800 | tf_op jit(solution)/shard_map/ppermute | solution.py:415
  13.7 1.5 %collective-permute-start.7 = (bf16[136,512]{1,0:T(8,128)(2,1)S(1)}, bf16[136,512]{1,0:T(8,128)(2,1)S(1)}, u32[]{:S(2)}, u32[]{:S(2)}) collective-permute-start(bf16[136,512]{1,0:T(8,128)(2,1)S(1)} %shard_map.94.refs_5_), channel_id=1, source_target_pairs={{0,8},{4,12},{8,0},{12,4},{16,24},{20,28},{24,16},{28,20},{1,9},{5... | collective-permute-start | bytes 417800 | tf_op jit(solution)/shard_map/ppermute | solution.py:415
  15.2 0.5 %collective-permute-start.9 = (bf16[136,512]{1,0:T(8,128)(2,1)S(1)}, bf16[136,512]{1,0:T(8,128)(2,1)S(1)}, u32[]{:S(2)}, u32[]{:S(2)}) collective-permute-start(bf16[136,512]{1,0:T(8,128)(2,1)S(1)} %shard_map.94.refs_5_), channel_id=1, source_target_pairs={{0,24},{4,28},{24,8},{28,12},{8,16},{12,20},{16,0},{20,4},{1,25},{... | collective-permute-start | bytes 417800 | tf_op jit(solution)/shard_map/ppermute | solution.py:531
  15.7 0.7 %collective-permute-start.4 = (bf16[64,512]{1,0:T(8,128)(2,1)S(1)}, bf16[64,512]{1,0:T(8,128)(2,1)S(1)}, u32[]{:S(2)}, u32[]{:S(2)}) collective-permute-start(bf16[64,512]{1,0:T(8,128)(2,1)S(1)} %shard_map.93._.refs_4_), channel_id=1, source_target_pairs={{0,1},{1,0},{2,3},{3,2},{4,5},{5,4},{6,7},{7,6},{8,9},{9,8},{10,11... | collective-permute-start | bytes 196616 | tf_op jit(solution)/shard_map/ppermute | solution.py:415
  16.4 2.0 %shard_map.95 = (f32[512,1024]{1,0:T(8,128)S(1)}, f32[512,1024]{1,0:T(8,128)S(1)}, bf16[3,512,1024]{2,1,0:T(8,128)(2,1)S(1)}, bf16[1,256,1024]{2,1,0:T(8,128)(2,1)S(1)}) custom-call(bf16[512,1024]{1,0:T(8,128)(2,1)S(1)} %get-tuple-element.42.refs_0_, bf16[512,1024]{1,0:T(8,128)(2,1)S(1)} %get-tuple-element.43.refs_1_, ...), custom_call_target="tpu_custom_call" | custom-call | flops 1342177280 | tf_op jit(solution)/shard_map/pallas_call | solution.py:399
  18.4 1.8 %collective-permute-done.4.refs_5_ = bf16[64,512]{1,0:T(8,128)(2,1)S(1)} collective-permute-done((bf16[64,512]{1,0:T(8,128)(2,1)S(1)}, bf16[64,512]{1,0:T(8,128)(2,1)S(1)}, u32[]{:S(2)}, u32[]{:S(2)}) %collective-permute-start.4) | collective-permute-done | bytes 65568 | tf_op jit(solution)/shard_map/ppermute | solution.py:415
  20.2 0.8 %shard_map.96 = (f32[512,512]{1,0:T(8,128)S(1)}, bf16[512,128]{1,0:T(8,128)(2,1)S(1)}, bf16[512,256]{1,0:T(8,128)(2,1)S(1)}) custom-call(bf16[32,512]{1,0:T(8,128)(2,1)S(1)} %get-tuple-element.37.refs_0_, bf16[32,512]{1,0:T(8,128)(2,1)S(1)} %collective-permute-done.refs_1_, bf16[32,512]{1,0:T(8,128)(2,1)S(1)} %collective-permute-done.1.refs_2_, ...), custom_call_target="tpu_custom_call" | custom-call | tf_op jit(solution)/shard_map/pallas_call | solution.py:399
  21.0 0.1 collective-permute-start.8
  21.1 0.1 collective-permute-done.9.diagonal_ref
  21.1 0.1 shard_map.97.refs_6_
  21.2 0.5 %collective-permute-start.11 = (bf16[128,512]{1,0:T(8,128)(2,1)S(1)}, bf16[128,512]{1,0:T(8,128)(2,1)S(1)}, u32[]{:S(2)}, u32[]{:S(2)}) collective-permute-start(bf16[128,512]{1,0:T(8,128)(2,1)S(1)} %shard_map.97.refs_6_), channel_id=1, source_target_pairs={{0,4},{4,0},{8,12},{12,8},{16,20},{20,16},{24,28},{28,24},{1,5},{5... | collective-permute-start | bytes 393224 | tf_op jit(solution)/shard_map/ppermute | solution.py:415
  21.8 0.2 shard_map.98
  22.0 0.4 %collective-permute-done.8.x_ref.refs_5_ = bf16[136,512]{1,0:T(8,128)(2,1)S(1)} collective-permute-done((bf16[136,512]{1,0:T(8,128)(2,1)S(1)}, bf16[136,512]{1,0:T(8,128)(2,1)S(1)}, u32[]{:S(2)}, u32[]{:S(2)}) %collective-permute-start.8) | collective-permute-done | bytes 139296 | tf_op jit(solution)/shard_map/ppermute | solution.py:415
  22.4 0.6 %shard_map.99.refs_1_ = f32[512,512]{1,0:T(8,128)S(1)} custom-call(bf16[512,256]{1,0:T(8,128)(2,1)S(1)} %get-tuple-element.53.scores_ref, bf16[512,128]{1,0:T(8,128)(2,1)S(1)} %get-tuple-element.52.refs_0_.turned_ref, bf16[136,512]{1,0:T(8,128)(2,1)S(1)} %collective-permute-done.8.x_ref.refs_5_, f32[512,128]{1,0:T(8,128)S(1)} %get-tuple-element.64._.refs_7_, ...), custom_call_target="tpu_custom_call" | custom-call | tf_op jit(solution)/shard_map/pallas_call | solution.py:399
  23.0 0.3 shard_map.100
  23.3 0.7 %collective-permute-start.12 = (f32[1,512]{1,0:T(1,128)S(1)}, f32[1,512]{1,0:T(1,128)S(1)}, u32[]{:S(2)}, u32[]{:S(2)}) collective-permute-start(f32[1,512]{1,0:T(1,128)S(1)} %get-tuple-element.66.refs_0_), channel_id=1, source_target_pairs={{0,1},{1,2},{2,3},{3,0},{4,5},{5,6},{6,7},{7,4},{8,9},{9,10},{10,1... | collective-permute-start | bytes 6152 | tf_op jit(solution)/shard_map/ppermute | solution.py:430
  24.0 1.6 %collective-permute-start.13 = (f32[1,512]{1,0:T(1,128)S(1)}, f32[1,512]{1,0:T(1,128)S(1)}, u32[]{:S(2)}, u32[]{:S(2)}) collective-permute-start(f32[1,512]{1,0:T(1,128)S(1)} %get-tuple-element.66.refs_0_), channel_id=1, source_target_pairs={{0,2},{1,3},{2,0},{3,1},{4,6},{5,7},{6,4},{7,5},{8,10},{9,11},{10,... | collective-permute-start | bytes 6152 | tf_op jit(solution)/shard_map/ppermute | solution.py:430
  25.6 2.0 %collective-permute-start.14 = (f32[1,512]{1,0:T(1,128)S(1)}, f32[1,512]{1,0:T(1,128)S(1)}, u32[]{:S(2)}, u32[]{:S(2)}) collective-permute-start(f32[1,512]{1,0:T(1,128)S(1)} %get-tuple-element.66.refs_0_), channel_id=1, source_target_pairs={{0,3},{1,0},{2,1},{3,2},{4,7},{5,4},{6,5},{7,6},{8,11},{9,8},{10,9... | collective-permute-start | bytes 6152 | tf_op jit(solution)/shard_map/ppermute | solution.py:430
  27.6 1.0 %collective-permute-done.12.refs_1_ = f32[1,512]{1,0:T(1,128)S(1)} collective-permute-done((f32[1,512]{1,0:T(1,128)S(1)}, f32[1,512]{1,0:T(1,128)S(1)}, u32[]{:S(2)}, u32[]{:S(2)}) %collective-permute-start.12) | collective-permute-done | bytes 2080 | tf_op jit(solution)/shard_map/ppermute | solution.py:430
  28.7 0.6 %collective-permute-done.14.refs_3_ = f32[1,512]{1,0:T(1,128)S(1)} collective-permute-done((f32[1,512]{1,0:T(1,128)S(1)}, f32[1,512]{1,0:T(1,128)S(1)}, u32[]{:S(2)}, u32[]{:S(2)}) %collective-permute-start.14) | collective-permute-done | bytes 2080 | tf_op jit(solution)/shard_map/ppermute | solution.py:430
  29.3 1.2 %shard_map.101 = bf16[512,1024]{1,0:T(8,128)(2,1)} custom-call(f32[1,512]{1,0:T(1,128)S(1)} %get-tuple-element.66.refs_0_, f32[1,512]{1,0:T(1,128)S(1)} %collective-permute-done.12.refs_1_, f32[1,512]{1,0:T(1,128)S(1)} %collective-permute-done.13.refs_2_, f32[1,512]{1,0:T(1,128)S(1)} %collective-permute-done.14.refs_3_, ...), custom_call_target="tpu_custom_call" | custom-call | flops 268435456 | bytes 3145728 | tf_op jit(solution)/shard_map/pallas_call | solution.py:399
  (9 shorter events, 0.0 us)
Async XLA Ops:
  0.0 10.2 %collective-permute-start = (bf16[32,512]{1,0:T(8,128)(2,1)}, bf16[32,512]{1,0:T(8,128)(2,1)S(1)}, u32[]{:S(2)}, u32[]{:S(2)}) collective-permute-start(bf16[32,512]{1,0:T(8,128)(2,1)} %refs_6_.1), channel_id=1, source_target_pairs={{0,2},{1,3},{2,0},{3,1},{4,6},{5,7},{6,4},{7,5},{8,10},{9,11},{10,... | collective-permute-start | bytes 98312 | tf_op jit(solution)/shard_map/ppermute | solution.py:415
  4.0 6.2 %collective-permute-start.1 = (bf16[32,512]{1,0:T(8,128)(2,1)}, bf16[32,512]{1,0:T(8,128)(2,1)S(1)}, u32[]{:S(2)}, u32[]{:S(2)}) collective-permute-start(bf16[32,512]{1,0:T(8,128)(2,1)} %refs_6_.1), channel_id=1, source_target_pairs={{0,3},{1,2},{2,1},{3,0},{4,7},{5,6},{6,5},{7,4},{8,11},{9,10},{10,... | collective-permute-start | bytes 98312 | tf_op jit(solution)/shard_map/ppermute | solution.py:415
  5.4 4.9 %collective-permute-start.2 = (bf16[32,512]{1,0:T(8,128)(2,1)}, bf16[32,512]{1,0:T(8,128)(2,1)S(1)}, u32[]{:S(2)}, u32[]{:S(2)}) collective-permute-start(bf16[32,512]{1,0:T(8,128)(2,1)} %refs_6_.1), channel_id=1, source_target_pairs={{0,1},{1,0},{2,3},{3,2},{4,5},{5,4},{6,7},{7,6},{8,9},{9,8},{10,11... | collective-permute-start | bytes 98312 | tf_op jit(solution)/shard_map/ppermute | solution.py:415
  5.6 5.1 %collective-permute-start.3 = (bf16[32,512]{1,0:T(8,128)(2,1)}, bf16[32,512]{1,0:T(8,128)(2,1)S(1)}, u32[]{:S(2)}, u32[]{:S(2)}) collective-permute-start(bf16[32,512]{1,0:T(8,128)(2,1)} %refs_7_.1), channel_id=1, source_target_pairs={{0,2},{1,3},{2,0},{3,1},{4,6},{5,7},{6,4},{7,5},{8,10},{9,11},{10,... | collective-permute-start | bytes 98312 | tf_op jit(solution)/shard_map/ppermute | solution.py:415
  10.6 1.4 %collective-permute-start.5 = (bf16[136,512]{1,0:T(8,128)(2,1)S(1)}, bf16[136,512]{1,0:T(8,128)(2,1)S(1)}, u32[]{:S(2)}, u32[]{:S(2)}) collective-permute-start(bf16[136,512]{1,0:T(8,128)(2,1)S(1)} %get-tuple-element.46), channel_id=1, source_target_pairs={{0,4},{4,0},{8,12},{12,8},{16,20},{20,16},{24,28},{28,24},{1,5},{5... | collective-permute-start | bytes 417800 | tf_op jit(solution)/shard_map/ppermute | solution.py:415
  12.1 8.9 %collective-permute-start.6 = (bf16[136,512]{1,0:T(8,128)(2,1)S(1)}, bf16[136,512]{1,0:T(8,128)(2,1)S(1)}, u32[]{:S(2)}, u32[]{:S(2)}) collective-permute-start(bf16[136,512]{1,0:T(8,128)(2,1)S(1)} %shard_map.94.refs_5_), channel_id=1, source_target_pairs={{0,16},{4,20},{8,24},{12,28},{16,0},{20,4},{24,8},{28,12},{1,17},{... | collective-permute-start | bytes 417800 | tf_op jit(solution)/shard_map/ppermute | solution.py:415
  13.7 7.3 %collective-permute-start.7 = (bf16[136,512]{1,0:T(8,128)(2,1)S(1)}, bf16[136,512]{1,0:T(8,128)(2,1)S(1)}, u32[]{:S(2)}, u32[]{:S(2)}) collective-permute-start(bf16[136,512]{1,0:T(8,128)(2,1)S(1)} %shard_map.94.refs_5_), channel_id=1, source_target_pairs={{0,8},{4,12},{8,0},{12,4},{16,24},{20,28},{24,16},{28,20},{1,9},{5... | collective-permute-start | bytes 417800 | tf_op jit(solution)/shard_map/ppermute | solution.py:415
  15.2 5.9 %collective-permute-start.9 = (bf16[136,512]{1,0:T(8,128)(2,1)S(1)}, bf16[136,512]{1,0:T(8,128)(2,1)S(1)}, u32[]{:S(2)}, u32[]{:S(2)}) collective-permute-start(bf16[136,512]{1,0:T(8,128)(2,1)S(1)} %shard_map.94.refs_5_), channel_id=1, source_target_pairs={{0,24},{4,28},{24,8},{28,12},{8,16},{12,20},{16,0},{20,4},{1,25},{... | collective-permute-start | bytes 417800 | tf_op jit(solution)/shard_map/ppermute | solution.py:531
  15.7 5.5 %collective-permute-start.10 = (bf16[136,512]{1,0:T(8,128)(2,1)S(1)}, bf16[136,512]{1,0:T(8,128)(2,1)S(1)}, u32[]{:S(2)}, u32[]{:S(2)}) collective-permute-start(bf16[136,512]{1,0:T(8,128)(2,1)S(1)} %get-tuple-element.62._.mine_ref), channel_id=1, source_target_pairs={{0,4},{4,0},{8,12},{12,8},{16,20},{20,16},{24,28},{28,24},{1,5},{5... | collective-permute-start | bytes 417800 | tf_op jit(solution)/shard_map/ppermute | solution.py:415
  15.7 4.5 %collective-permute-start.4 = (bf16[64,512]{1,0:T(8,128)(2,1)S(1)}, bf16[64,512]{1,0:T(8,128)(2,1)S(1)}, u32[]{:S(2)}, u32[]{:S(2)}) collective-permute-start(bf16[64,512]{1,0:T(8,128)(2,1)S(1)} %shard_map.93._.refs_4_), channel_id=1, source_target_pairs={{0,1},{1,0},{2,3},{3,2},{4,5},{5,4},{6,7},{7,6},{8,9},{9,8},{10,11... | collective-permute-start | bytes 196616 | tf_op jit(solution)/shard_map/ppermute | solution.py:415
  21.0 1.4 %collective-permute-start.8 = (bf16[136,512]{1,0:T(8,128)(2,1)S(1)}, bf16[136,512]{1,0:T(8,128)(2,1)S(1)}, u32[]{:S(2)}, u32[]{:S(2)}) collective-permute-start(bf16[136,512]{1,0:T(8,128)(2,1)S(1)} %collective-permute-done.7.x_ref.refs_5_), channel_id=1, source_target_pairs={{0,4},{4,0},{8,12},{12,8},{16,20},{20,16},{24,28},{28,24},{1,5},{5... | collective-permute-start | bytes 417800 | tf_op jit(solution)/shard_map/ppermute | solution.py:415
  21.2 1.8 %collective-permute-start.11 = (bf16[128,512]{1,0:T(8,128)(2,1)S(1)}, bf16[128,512]{1,0:T(8,128)(2,1)S(1)}, u32[]{:S(2)}, u32[]{:S(2)}) collective-permute-start(bf16[128,512]{1,0:T(8,128)(2,1)S(1)} %shard_map.97.refs_6_), channel_id=1, source_target_pairs={{0,4},{4,0},{8,12},{12,8},{16,20},{20,16},{24,28},{28,24},{1,5},{5... | collective-permute-start | bytes 393224 | tf_op jit(solution)/shard_map/ppermute | solution.py:415
  23.3 5.4 %collective-permute-start.12 = (f32[1,512]{1,0:T(1,128)S(1)}, f32[1,512]{1,0:T(1,128)S(1)}, u32[]{:S(2)}, u32[]{:S(2)}) collective-permute-start(f32[1,512]{1,0:T(1,128)S(1)} %get-tuple-element.66.refs_0_), channel_id=1, source_target_pairs={{0,1},{1,2},{2,3},{3,0},{4,5},{5,6},{6,7},{7,4},{8,9},{9,10},{10,1... | collective-permute-start | bytes 6152 | tf_op jit(solution)/shard_map/ppermute | solution.py:430
  24.0 4.7 %collective-permute-start.13 = (f32[1,512]{1,0:T(1,128)S(1)}, f32[1,512]{1,0:T(1,128)S(1)}, u32[]{:S(2)}, u32[]{:S(2)}) collective-permute-start(f32[1,512]{1,0:T(1,128)S(1)} %get-tuple-element.66.refs_0_), channel_id=1, source_target_pairs={{0,2},{1,3},{2,0},{3,1},{4,6},{5,7},{6,4},{7,5},{8,10},{9,11},{10,... | collective-permute-start | bytes 6152 | tf_op jit(solution)/shard_map/ppermute | solution.py:430
  25.6 3.7 %collective-permute-start.14 = (f32[1,512]{1,0:T(1,128)S(1)}, f32[1,512]{1,0:T(1,128)S(1)}, u32[]{:S(2)}, u32[]{:S(2)}) collective-permute-start(f32[1,512]{1,0:T(1,128)S(1)} %get-tuple-element.66.refs_0_), channel_id=1, source_target_pairs={{0,3},{1,0},{2,1},{3,2},{4,7},{5,4},{6,5},{7,6},{8,11},{9,8},{10,9... | collective-permute-start | bytes 6152 | tf_op jit(solution)/shard_map/ppermute | solution.py:430
